TPU v7x, 32 devices: a whole 2x2x4 slice. The times are simulated.
32 devices in a mesh: groups: 2 (over y), ta: 4 (over z), gx: 4 (over x, core).
Axes of the slice: x: 2, y: 2, z: 4, core: 2. Of those that a mesh axis runs over, the one named last changes fastest.
Arguments:
- source: bfloat16 [4, 4, 3, 2, 16, 16, 128], P(None, None, None, None, ('groups', 'ta'), 'gx'), parts along dimension 4, may hold values from -6 to 6
- gauge_links: bfloat16 [4, 3, 3, 2, 2, 16, 16, 128], P(None, None, None, None, None, ('groups', 'ta'), 'gx'), parts along dimension 5, may hold values from -2.5 to 2.5
- clover_even: bfloat16 [2, 6, 6, 2, 16, 16, 128], P(None, None, None, None, ('groups', 'ta'), 'gx'), parts along dimension 4, may hold values from -0.5 to 1.5, as said below
- clover_odd_inv: bfloat16 [2, 6, 6, 2, 16, 16, 128], P(None, None, None, None, ('groups', 'ta'), 'gx'), parts along dimension 4, may hold values from -0.5 to 1.5, as said below
Outputs:
- result: bfloat16 [4, 4, 3, 2, 16, 16, 128], P(None, None, None, None, ('groups', 'ta'), 'gx'), parts along dimension 4
There are 2 independent parts, one for each index of `groups`. A program takes and returns all parts, laid end to end along the dimension named above; each array names one. Nothing has to cross between parts.
Inputs may be any that keep to these rules, and one draw needn't show every extreme that they name: `clover_even`: each 6 x 6 block of a site is Hermitian. `clover_odd_inv`: each 6 x 6 block of a site is Hermitian.
All inputs are finite; a program needn't handle non-finite values.
Results may differ from a plain program's by a relative error of at most 0.0055.
Values may be sent and summed in bfloat16 or wider, within the bound.
No kernel may reach another device: no remote copies, remote signals or barrier semaphores. Data moves between devices by JAX's collectives and lax.ppermute only.
A program may use at most 64 MiB of HBM per device.

v0:
```python
import functools

import jax
import jax.numpy as jnp
from jax import lax
from jax.experimental import pallas as pl
from jax.experimental.pallas import tpu as pltpu
from jax.sharding import PartitionSpec as P

HALF_DEPTH = 8
KAPPA2 = 0.14 * 0.14
RHS = 4
F32 = jnp.float32
BF16 = jnp.bfloat16

SPIN = (((0, 0), (1, 0)), ((1, 3), (0, 3)), ((1, 2), (0, 0)), ((0, 3), (1, 1)))
SPIN_INV = (((0, 0), (1, 0)), ((1, 1), (0, 1)), ((1, 0), (0, 2)), ((0, 1), (1, 3)))


def add_power(base, value, power):
    (br, bi), (vr, vi) = base, value
    if power == 0:
        return br + vr, bi + vi
    if power == 1:
        return br - vi, bi + vr
    if power == 2:
        return br - vr, bi - vi
    return br + vi, bi - vr


def project(field, mu, sign):
    shift = 0 if sign > 0 else 2
    half = []
    for row in range(2):
        col, power = SPIN[mu][row]
        for c in range(3):
            half.append(add_power(field[row * 3 + c], field[(2 + col) * 3 + c], (power + shift) % 4))
    return half


def rebuild(acc, half, mu, sign):
    shift = 0 if sign > 0 else 2
    out = list(acc)
    for j in range(6):
        out[j] = add_power(out[j], half[j], 0)
    for row in range(2):
        col, power = SPIN_INV[mu][row]
        for c in range(3):
            j = (2 + row) * 3 + c
            out[j] = add_power(out[j], half[col * 3 + c], (power + shift) % 4)
    return out


def color(links, half, adjoint):
    out = []
    for s in range(2):
        for a in range(3):
            re = im = None
            for b in range(3):
                lr, li = links[b][a] if adjoint else links[a][b]
                vr, vi = half[s * 3 + b]
                if adjoint:
                    tr, ti = lr * vr + li * vi, lr * vi - li * vr
                else:
                    tr, ti = lr * vr - li * vi, lr * vi + li * vr
                re = tr if re is None else re + tr
                im = ti if im is None else im + ti
            out.append((re, im))
    return out


def each(function, half):
    return [(function(re), function(im)) for re, im in half]


def load_pair(ref, index):
    block = ref[index * 16:(index + 1) * 16, :].astype(F32)
    return block[0:8], block[8:16]


def load_links(ref, mu, parity):
    links = []
    for a in range(3):
        row = []
        for b in range(3):
            k = ((mu * 3 + a) * 3 + b) * 2
            row.append((load_pair(ref, k)[parity], load_pair(ref, k + 1)[parity]))
        links.append(row)
    return links


def load_field(ref, r):
    return [load_pair(ref, r * 12 + j) for j in range(12)]


def store_pair(ref, index, pair):
    ref[index * 16:(index + 1) * 16, :] = jnp.concatenate(pair, axis=0).astype(ref.dtype)


def store_field(ref, r, field):
    for j in range(12):
        store_pair(ref, r * 12 + j, field[j])


def site_masks():
    rows = lax.broadcasted_iota(jnp.int32, (8, 128), 0)
    return rows // 4, rows % 4


def roll_rows(value, shift):
    shift %= 8
    return pltpu.roll(value, shift, 0) if shift else value


def select(mask, a, b):
    return jnp.where(mask, a, b)


def send_halos(f_ref, links_ref, parity, outs):
    t_back, t_ahead, x_back, x_ahead, kept = outs
    t_idx, x_idx = site_masks()
    first_t = t_idx == 0
    for mu in range(2):
        links = load_links(links_ref, mu, parity)
        ahead_all, carry_all = [], []
        for r in range(RHS):
            field = load_field(f_ref, r)
            ahead = project(field, mu, -1)
            carry = color(links, project(field, mu, 1), True)
            if mu == 0:
                moved = each(lambda v: roll_rows(v, 4), ahead)
                back = each(lambda v: roll_rows(v, 4), carry)
                for c in range(3):
                    store_pair(t_back, r * 3 + c, [select(first_t, ahead[c + 3][i], moved[c][i]) for i in range(2)])
                    store_pair(t_ahead, r * 3 + c, [select(first_t, back[c][i], carry[c + 3][i]) for i in range(2)])
            else:
                back = each(lambda v: roll_rows(v, 1), carry)
                ahead_all.append(ahead)
                carry_all.append(carry)
                if r % 2 == 1:
                    for c in range(3):
                        front, rear = [], []
                        for i in range(2):
                            group = [h[j][i] for h in ahead_all[-2:] for j in (c, c + 3)]
                            packed = group[0]
                            for k in range(1, 4):
                                packed = select(x_idx == k, roll_rows(group[k], k), packed)
                            front.append(packed)
                            group = [h[j][i] for h in carry_all[-2:] for j in (c, c + 3)]
                            packed = group[0]
                            for k in range(1, 4):
                                packed = select(x_idx == 3 - k, roll_rows(group[k], -k), packed)
                            rear.append(packed)
                        store_pair(x_back, (r // 2) * 3 + c, front)
                        store_pair(x_ahead, (r // 2) * 3 + c, rear)
            for j in range(6):
                store_pair(kept, (mu * RHS + r) * 6 + j, back[j])


def start_kernel(parity, f_ref, links_ref, *outs):
    send_halos(f_ref, links_ref, parity, outs)


def interior_kernel(parity, with_base, *refs):
    if with_base:
        f_ref, links_ref, base_ref, clover_ref, acc_ref = refs
        clover_to(clover_ref, lambda r: load_field(base_ref, r), acc_ref, 1.0)
    else:
        f_ref, links_ref, acc_ref = refs
    out_parity = 1 - parity
    t_idx, x_idx = site_masks()
    lane = lax.broadcasted_iota(jnp.int32, (8, 128), 1)
    odd = (t_idx + x_idx + lane // HALF_DEPTH + out_parity) % 2
    start = lane - lane % HALF_DEPTH
    up = jnp.where(odd == 1, start + (lane + 1) % HALF_DEPTH, lane)
    down = jnp.where(odd == 0, start + (lane + HALF_DEPTH - 1) % HALF_DEPTH, lane)

    def take(value, index):
        return jnp.take_along_axis(value, index, axis=1, mode="promise_in_bounds")

    for mu in (2, 3):
        if mu == 2:
            ahead_of = lambda v: pltpu.roll(v, 128 - HALF_DEPTH, 1)
            behind_of = lambda v: pltpu.roll(v, HALF_DEPTH, 1)
        else:
            ahead_of = lambda v: take(v, up)
            behind_of = lambda v: take(v, down)
        links_out = load_links(links_ref, mu, out_parity)
        links_in = load_links(links_ref, mu, parity)
        for r in range(RHS):
            field = load_field(f_ref, r)
            if mu == 2 and not with_base:
                zero = jnp.zeros((8, 128), F32)
                acc = [(zero, zero)] * 12
            else:
                acc = load_field(acc_ref, r)
            half = color(links_out, each(ahead_of, project(field, mu, -1)), False)
            acc = rebuild(acc, half, mu, -1)
            half = each(behind_of, color(links_in, project(field, mu, 1), True))
            acc = rebuild(acc, half, mu, 1)
            store_field(acc_ref, r, acc)


def clover_to(clover_ref, get_field, out_ref, scale):
    for chi in range(2):
        matrix = {}
        for i in range(6):
            for j in range(i, 6):
                k = (chi * 6 + i) * 6 + j
                block = clover_ref[k * 16:(k + 1) * 16, :].astype(F32)
                re, im = block[0:8], block[8:16]
                if scale != 1.0:
                    re, im = re * scale, im * scale
                matrix[i, j] = (re, im)
        for r in range(RHS):
            field = get_field(r)[chi * 6:chi * 6 + 6]
            for i in range(6):
                re = im = None
                for j in range(6):
                    vr, vi = field[j]
                    mr, mi = matrix[min(i, j), max(i, j)]
                    if i <= j:
                        tr, ti = mr * vr - mi * vi, mr * vi + mi * vr
                    else:
                        tr, ti = mr * vr + mi * vi, mr * vi - mi * vr
                    re = tr if re is None else re + tr
                    im = ti if im is None else im + ti
                store_pair(out_ref, r * 12 + chi * 6 + i, (re, im))


def join_halos(f_ref, links_ref, acc_ref, halos, parity, out_ref):
    from_next_t, from_last_t, from_next_x, from_last_x, kept = halos
    out_parity = 1 - parity
    t_idx, x_idx = site_masks()
    for mu in range(2):
        links = load_links(links_ref, mu, out_parity)
        for r in range(RHS):
            field = load_field(f_ref, r)
            ahead = project(field, mu, -1)
            behind = [load_pair(kept, (mu * RHS + r) * 6 + j) for j in range(6)]
            new_ahead, new_behind = [None] * 6, [None] * 6
            for c in range(3):
                if mu == 0:
                    nxt = load_pair(from_next_t, r * 3 + c)
                    last = load_pair(from_last_t, r * 3 + c)
                    for s in range(2):
                        j = s * 3 + c
                        new_ahead[j] = tuple(
                            select(t_idx == 1, roll_rows(nxt[i], 4 * s), roll_rows(ahead[j][i], 4)) for i in range(2)
                        )
                        new_behind[j] = tuple(
                            select(t_idx == 0, roll_rows(last[i], 4 * s), behind[j][i]) for i in range(2)
                        )
                else:
                    nxt = load_pair(from_next_x, (r // 2) * 3 + c)
                    last = load_pair(from_last_x, (r // 2) * 3 + c)
                    for s in range(2):
                        j = s * 3 + c
                        k = (r % 2) * 2 + s
                        new_ahead[j] = tuple(
                            select(x_idx == 3, roll_rows(nxt[i], 3 - k), roll_rows(ahead[j][i], 7)) for i in range(2)
                        )
                        new_behind[j] = tuple(
                            select(x_idx == 0, roll_rows(last[i], 5 + k), behind[j][i]) for i in range(2)
                        )
            acc = load_field(acc_ref if mu == 0 else out_ref, r)
            acc = rebuild(acc, color(links, new_ahead, False), mu, -1)
            acc = rebuild(acc, new_behind, mu, 1)
            store_field(out_ref, r, acc)


def odd_kernel(f_ref, links_ref, clover_ref, acc_ref, *refs):
    halos, out_ref, outs, summed = refs[:5], refs[5], refs[6:11], refs[11]
    join_halos(f_ref, links_ref, acc_ref, halos, 0, summed)
    clover_to(clover_ref, lambda r: load_field(summed, r), out_ref, -KAPPA2)
    send_halos(out_ref, links_ref, 1, outs)


def even_kernel(f_ref, links_ref, acc_ref, *refs):
    halos, out_ref, outs = refs[:5], refs[5], refs[6:11]
    join_halos(f_ref, links_ref, acc_ref, halos, 1, out_ref)
    send_halos(out_ref, links_ref, 0, outs)


def last_kernel(f_ref, links_ref, acc_ref, *refs):
    halos, out_ref, summed = refs[:5], refs[5], refs[6]
    join_halos(f_ref, links_ref, acc_ref, halos, 1, summed)
    for r in range(RHS):
        store_field(out_ref, r, load_field(summed, r))


ROWS = RHS * 24 * 8


def call(kernel, args, outs, flops, scratch=()):
    return pl.pallas_call(
        kernel,
        out_shape=tuple(jax.ShapeDtypeStruct(shape, dtype) for shape, dtype in outs),
        in_specs=[pl.BlockSpec(memory_space=pltpu.VMEM)] * len(args),
        out_specs=tuple([pl.BlockSpec(memory_space=pltpu.VMEM)] * len(outs)),
        scratch_shapes=list(scratch),
        compiler_params=pltpu.CompilerParams(vmem_limit_bytes=24 * 1024 * 1024),
        cost_estimate=pl.CostEstimate(flops=flops, bytes_accessed=2 * 1024 * 1024, transcendentals=0),
    )(*args)


HALO_OUTS = [((RHS * 3 * 16, 128), BF16)] * 2 + [((RHS * 3 * 8, 128), BF16)] * 2 + [((2 * RHS * 6 * 16, 128), F32)]
FIELD = [((ROWS, 128), F32)]


def exchange(parts):
    t_back, t_ahead, x_back, x_ahead, kept = parts

    def ring(axis, step):
        count = lax.axis_size(axis)
        return [(i, (i + step) % count) for i in range(count)]

    return (
        lax.ppermute(t_back, "ta", ring("ta", -1)),
        lax.ppermute(t_ahead, "ta", ring("ta", 1)),
        lax.ppermute(x_back, "gx", ring("gx", -1)),
        lax.ppermute(x_ahead, "gx", ring("gx", 1)),
        kept,
    )


def per_device(source, gauge_links, clover_even, clover_odd_inv):
    shape = source.shape
    f = source.reshape(-1, 128)
    links = gauge_links.reshape(-1, 128)
    even = clover_even.reshape(-1, 128)
    odd = clover_odd_inv.reshape(-1, 128)
    parts = call(functools.partial(start_kernel, 0), (f, links), HALO_OUTS, 3_000_000)
    field_scratch = [pltpu.VMEM((ROWS, 128), F32)]
    for step in range(2):
        halos = exchange(parts)
        acc, = call(functools.partial(interior_kernel, 0, False), (f, links), FIELD, 4_000_000)
        g, *parts = call(odd_kernel, (f, links, odd, acc, *halos), FIELD + HALO_OUTS, 6_000_000, field_scratch)
        halos = exchange(parts)
        acc, = call(functools.partial(interior_kernel, 1, True), (g, links, f, even), FIELD, 6_000_000)
        if step == 0:
            f, *parts = call(even_kernel, (g, links, acc, *halos), FIELD + HALO_OUTS, 4_000_000)
        else:
            out, = call(last_kernel, (g, links, acc, *halos), [((ROWS, 128), BF16)], 3_000_000, field_scratch)
    return out.reshape(shape)


def solution(mesh):
    field_spec = P(None, None, None, None, ("groups", "ta"), "gx", None)
    link_spec = P(None, None, None, None, None, ("groups", "ta"), "gx", None)
    return jax.shard_map(
        per_device,
        mesh=mesh,
        in_specs=(field_spec, link_spec, field_spec, field_spec),
        out_specs=field_spec,
        check_vma=False,
    )
```

profile of v0, /device:TPU:0, one launch (start us, length us, event | category | flops | bytes accessed | tf_op | source)
XLA Modules:
  0.0 38.2 jit_solution(8820369303778033916)
XLA Ops:
  0.0 0.0 copy-start
  0.0 1.0 %copy-done = bf16[4,3,3,2,2,2,4,128]{7,6,5,4,3,2,1,0:T(4,128)(2,1)S(1)} copy-done((bf16[4,3,3,2,2,2,4,128]{7,6,5,4,3,2,1,0:T(4,128)(2,1)S(1)}, bf16[4,3,3,2,2,2,4,128]{7,6,5,4,3,2,1,0:T(4,128)(2,1)}, u32[]{:S(2)}) %copy-start) | copy-done | bytes 294936
  1.0 0.0 copy-start.2
  1.0 0.9 %copy-done.2 = bf16[4,4,3,2,2,4,128]{6,5,4,3,2,1,0:T(4,128)(2,1)S(1)} copy-done((bf16[4,4,3,2,2,4,128]{6,5,4,3,2,1,0:T(4,128)(2,1)S(1)}, bf16[4,4,3,2,2,4,128]{6,5,4,3,2,1,0:T(4,128)(2,1)}, u32[]{:S(2)}) %copy-start.2) | copy-done | bytes 196632
  1.9 0.3 shard_map.47
  2.2 5.1 %collective-permute-start = (bf16[192,128]{1,0:T(8,128)(2,1)S(1)}, bf16[192,128]{1,0:T(8,128)(2,1)S(1)}, u32[]{:S(2)}, u32[]{:S(2)}) collective-permute-start(bf16[192,128]{1,0:T(8,128)(2,1)S(1)} %get-tuple-element.28), channel_id=1, source_target_pairs={{0,12},{4,0},{8,4},{12,8},{1,13},{5,1},{9,5},{13,9},{2,14},{6,2},{... | collective-permute-start | bytes 147464 | tf_op jit(solution)/shard_map/ppermute | solution.py:319
  7.3 0.0 collective-permute-start.1
  7.3 0.7 %collective-permute-start.2 = (bf16[96,128]{1,0:T(8,128)(2,1)S(1)}, bf16[96,128]{1,0:T(8,128)(2,1)S(1)}, u32[]{:S(2)}, u32[]{:S(2)}) collective-permute-start(bf16[96,128]{1,0:T(8,128)(2,1)S(1)} %get-tuple-element.30), channel_id=1, source_target_pairs={{0,3},{1,0},{2,1},{3,2},{4,7},{5,4},{6,5},{7,6},{8,11},{9,8},{10,9... | collective-permute-start | bytes 73736 | tf_op jit(solution)/shard_map/ppermute | solution.py:321
  7.9 0.0 collective-permute-start.3
  7.9 0.4 %shard_map.46.acc_ref = f32[768,128]{1,0:T(8,128)S(1)} custom-call(bf16[768,128]{1,0:T(8,128)(2,1)S(1)} %bitcast.15, bf16[1152,128]{1,0:T(8,128)(2,1)S(1)} %bitcast.6), custom_call_target="tpu_custom_call" | custom-call | flops 4000000 | bytes 2097152 | tf_op jit(solution)/shard_map/pallas_call | solution.py:296
  8.3 1.1 %collective-permute-done.2.refs_2_ = bf16[96,128]{1,0:T(8,128)(2,1)S(1)} collective-permute-done((bf16[96,128]{1,0:T(8,128)(2,1)S(1)}, bf16[96,128]{1,0:T(8,128)(2,1)S(1)}, u32[]{:S(2)}, u32[]{:S(2)}) %collective-permute-start.2) | collective-permute-done | bytes 24608 | tf_op jit(solution)/shard_map/ppermute | solution.py:321
  9.4 1.7 %collective-permute-done.3.refs_3_ = bf16[96,128]{1,0:T(8,128)(2,1)S(1)} collective-permute-done((bf16[96,128]{1,0:T(8,128)(2,1)S(1)}, bf16[96,128]{1,0:T(8,128)(2,1)S(1)}, u32[]{:S(2)}, u32[]{:S(2)}) %collective-permute-start.3) | collective-permute-done | bytes 24608 | tf_op jit(solution)/shard_map/ppermute | solution.py:322
  11.2 0.0 collective-permute-done.refs_0_
  11.2 2.0 %collective-permute-done.1.refs_1_ = bf16[192,128]{1,0:T(8,128)(2,1)S(1)} collective-permute-done((bf16[192,128]{1,0:T(8,128)(2,1)S(1)}, bf16[192,128]{1,0:T(8,128)(2,1)S(1)}, u32[]{:S(2)}, u32[]{:S(2)}) %collective-permute-start.1) | collective-permute-done | bytes 49184 | tf_op jit(solution)/shard_map/ppermute | solution.py:320
  13.1 0.0 copy-done.4
  13.1 0.8 %shard_map.48 = (f32[768,128]{1,0:T(8,128)S(1)}, bf16[192,128]{1,0:T(8,128)(2,1)S(1)}, bf16[192,128]{1,0:T(8,128)(2,1)S(1)}, bf16[96,128]{1,0:T(8,128)(2,1)S(1)}...) custom-call(bf16[768,128]{1,0:T(8,128)(2,1)S(1)} %bitcast.16, bf16[1152,128]{1,0:T(8,128)(2,1)S(1)} %bitcast.7, ...), custom_call_target="tpu_custom_call" | custom-call | flops 6000000 | bytes 2097152 | tf_op jit(solution)/shard_map/pallas_call | solution.py:296
  14.0 1.6 %collective-permute-start.4 = (bf16[192,128]{1,0:T(8,128)(2,1)S(1)}, bf16[192,128]{1,0:T(8,128)(2,1)S(1)}, u32[]{:S(2)}, u32[]{:S(2)}) collective-permute-start(bf16[192,128]{1,0:T(8,128)(2,1)S(1)} %get-tuple-element.34), channel_id=1, source_target_pairs={{0,12},{4,0},{8,4},{12,8},{1,13},{5,1},{9,5},{13,9},{2,14},{6,2},{... | collective-permute-start | bytes 147464 | tf_op jit(solution)/shard_map/ppermute | solution.py:319
  15.6 0.4 %collective-permute-start.5 = (bf16[192,128]{1,0:T(8,128)(2,1)S(1)}, bf16[192,128]{1,0:T(8,128)(2,1)S(1)}, u32[]{:S(2)}, u32[]{:S(2)}) collective-permute-start(bf16[192,128]{1,0:T(8,128)(2,1)S(1)} %get-tuple-element.35), channel_id=1, source_target_pairs={{0,4},{4,8},{8,12},{12,0},{1,5},{5,9},{9,13},{13,1},{2,6},{6,10},{... | collective-permute-start | bytes 147464 | tf_op jit(solution)/shard_map/ppermute | solution.py:320
  16.1 0.0 collective-permute-start.6
  16.1 0.5 %collective-permute-start.7 = (bf16[96,128]{1,0:T(8,128)(2,1)S(1)}, bf16[96,128]{1,0:T(8,128)(2,1)S(1)}, u32[]{:S(2)}, u32[]{:S(2)}) collective-permute-start(bf16[96,128]{1,0:T(8,128)(2,1)S(1)} %get-tuple-element.37), channel_id=1, source_target_pairs={{0,1},{1,2},{2,3},{3,0},{4,5},{5,6},{6,7},{7,4},{8,9},{9,10},{10,1... | collective-permute-start | bytes 73736 | tf_op jit(solution)/shard_map/ppermute | solution.py:322
  16.6 0.0 copy-done.3
  16.6 0.7 %shard_map.49.acc_ref = f32[768,128]{1,0:T(8,128)S(1)} custom-call(f32[768,128]{1,0:T(8,128)S(1)} %get-tuple-element.33.refs_0_.f_ref, bf16[1152,128]{1,0:T(8,128)(2,1)S(1)} %bitcast.8, bf16[768,128]{1,0:T(8,128)(2,1)S(1)} %bitcast.17, bf16[1152,128]{1,0:T(8,128)(2,1)S(1)} %bitcast.18), custom_call_target="tpu_custom_call" | custom-call | flops 6000000 | bytes 2097152 | tf_op jit(solution)/shard_map/pallas_call | solution.py:296
  17.3 0.3 collective-permute-done.6.refs_2_
  17.6 2.0 %collective-permute-done.7.refs_3_ = bf16[96,128]{1,0:T(8,128)(2,1)S(1)} collective-permute-done((bf16[96,128]{1,0:T(8,128)(2,1)S(1)}, bf16[96,128]{1,0:T(8,128)(2,1)S(1)}, u32[]{:S(2)}, u32[]{:S(2)}) %collective-permute-start.7) | collective-permute-done | bytes 24608 | tf_op jit(solution)/shard_map/ppermute | solution.py:322
  19.6 0.0 collective-permute-done.4.refs_0_
  19.6 2.0 %collective-permute-done.5.refs_1_ = bf16[192,128]{1,0:T(8,128)(2,1)S(1)} collective-permute-done((bf16[192,128]{1,0:T(8,128)(2,1)S(1)}, bf16[192,128]{1,0:T(8,128)(2,1)S(1)}, u32[]{:S(2)}, u32[]{:S(2)}) %collective-permute-start.5) | collective-permute-done | bytes 49184 | tf_op jit(solution)/shard_map/ppermute | solution.py:320
  21.5 0.0 copy-done.1
  21.5 0.5 %shard_map.50 = (f32[768,128]{1,0:T(8,128)S(1)}, bf16[192,128]{1,0:T(8,128)(2,1)S(1)}, bf16[192,128]{1,0:T(8,128)(2,1)S(1)}, bf16[96,128]{1,0:T(8,128)(2,1)S(1)}...) custom-call(f32[768,128]{1,0:T(8,128)S(1)} %get-tuple-element.33.refs_0_.f_ref, bf16[1152,128]{1,0:T(8,128)(2,1)S(1)} %bitcast.9, ...), custom_call_target="tpu_custom_call" | custom-call | flops 4000000 | bytes 2097152 | tf_op jit(solution)/shard_map/pallas_call | solution.py:296
  22.0 1.3 %collective-permute-start.8 = (bf16[192,128]{1,0:T(8,128)(2,1)S(1)}, bf16[192,128]{1,0:T(8,128)(2,1)S(1)}, u32[]{:S(2)}, u32[]{:S(2)}) collective-permute-start(bf16[192,128]{1,0:T(8,128)(2,1)S(1)} %get-tuple-element.40), channel_id=1, source_target_pairs={{0,12},{4,0},{8,4},{12,8},{1,13},{5,1},{9,5},{13,9},{2,14},{6,2},{... | collective-permute-start | bytes 147464 | tf_op jit(solution)/shard_map/ppermute | solution.py:319
  23.3 0.8 %collective-permute-start.9 = (bf16[192,128]{1,0:T(8,128)(2,1)S(1)}, bf16[192,128]{1,0:T(8,128)(2,1)S(1)}, u32[]{:S(2)}, u32[]{:S(2)}) collective-permute-start(bf16[192,128]{1,0:T(8,128)(2,1)S(1)} %get-tuple-element.41), channel_id=1, source_target_pairs={{0,4},{4,8},{8,12},{12,0},{1,5},{5,9},{9,13},{13,1},{2,6},{6,10},{... | collective-permute-start | bytes 147464 | tf_op jit(solution)/shard_map/ppermute | solution.py:320
  24.1 0.0 collective-permute-start.10
  24.1 0.5 %collective-permute-start.11 = (bf16[96,128]{1,0:T(8,128)(2,1)S(1)}, bf16[96,128]{1,0:T(8,128)(2,1)S(1)}, u32[]{:S(2)}, u32[]{:S(2)}) collective-permute-start(bf16[96,128]{1,0:T(8,128)(2,1)S(1)} %get-tuple-element.43), channel_id=1, source_target_pairs={{0,1},{1,2},{2,3},{3,0},{4,5},{5,6},{6,7},{7,4},{8,9},{9,10},{10,1... | collective-permute-start | bytes 73736 | tf_op jit(solution)/shard_map/ppermute | solution.py:322
  24.6 0.4 %shard_map.51.acc_ref = f32[768,128]{1,0:T(8,128)S(1)} custom-call(f32[768,128]{1,0:T(8,128)S(1)} %get-tuple-element.39.refs_0_.f_ref.refs_2_, bf16[1152,128]{1,0:T(8,128)(2,1)S(1)} %bitcast.10), custom_call_target="tpu_custom_call" | custom-call | flops 4000000 | bytes 2097152 | tf_op jit(solution)/shard_map/pallas_call | solution.py:296
  25.0 0.6 %collective-permute-done.10.refs_2_ = bf16[96,128]{1,0:T(8,128)(2,1)S(1)} collective-permute-done((bf16[96,128]{1,0:T(8,128)(2,1)S(1)}, bf16[96,128]{1,0:T(8,128)(2,1)S(1)}, u32[]{:S(2)}, u32[]{:S(2)}) %collective-permute-start.10) | collective-permute-done | bytes 24608 | tf_op jit(solution)/shard_map/ppermute | solution.py:321
  25.6 1.7 %collective-permute-done.11.refs_3_ = bf16[96,128]{1,0:T(8,128)(2,1)S(1)} collective-permute-done((bf16[96,128]{1,0:T(8,128)(2,1)S(1)}, bf16[96,128]{1,0:T(8,128)(2,1)S(1)}, u32[]{:S(2)}, u32[]{:S(2)}) %collective-permute-start.11) | collective-permute-done | bytes 24608 | tf_op jit(solution)/shard_map/ppermute | solution.py:322
  27.4 0.0 collective-permute-done.8.refs_0_
  27.4 1.8 %collective-permute-done.9.refs_1_ = bf16[192,128]{1,0:T(8,128)(2,1)S(1)} collective-permute-done((bf16[192,128]{1,0:T(8,128)(2,1)S(1)}, bf16[192,128]{1,0:T(8,128)(2,1)S(1)}, u32[]{:S(2)}, u32[]{:S(2)}) %collective-permute-start.9) | collective-permute-done | bytes 49184 | tf_op jit(solution)/shard_map/ppermute | solution.py:320
  29.2 0.8 %shard_map.52 = (f32[768,128]{1,0:T(8,128)S(1)}, bf16[192,128]{1,0:T(8,128)(2,1)S(1)}, bf16[192,128]{1,0:T(8,128)(2,1)S(1)}, bf16[96,128]{1,0:T(8,128)(2,1)S(1)}...) custom-call(f32[768,128]{1,0:T(8,128)S(1)} %get-tuple-element.39.refs_0_.f_ref.refs_2_, ...), custom_call_target="tpu_custom_call" | custom-call | flops 6000000 | bytes 2097152 | tf_op jit(solution)/shard_map/pallas_call | solution.py:296
  30.0 1.3 %collective-permute-start.12 = (bf16[192,128]{1,0:T(8,128)(2,1)S(1)}, bf16[192,128]{1,0:T(8,128)(2,1)S(1)}, u32[]{:S(2)}, u32[]{:S(2)}) collective-permute-start(bf16[192,128]{1,0:T(8,128)(2,1)S(1)} %get-tuple-element.46), channel_id=1, source_target_pairs={{0,12},{4,0},{8,4},{12,8},{1,13},{5,1},{9,5},{13,9},{2,14},{6,2},{... | collective-permute-start | bytes 147464 | tf_op jit(solution)/shard_map/ppermute | solution.py:319
  31.3 0.8 %collective-permute-start.13 = (bf16[192,128]{1,0:T(8,128)(2,1)S(1)}, bf16[192,128]{1,0:T(8,128)(2,1)S(1)}, u32[]{:S(2)}, u32[]{:S(2)}) collective-permute-start(bf16[192,128]{1,0:T(8,128)(2,1)S(1)} %get-tuple-element.47), channel_id=1, source_target_pairs={{0,4},{4,8},{8,12},{12,0},{1,5},{5,9},{9,13},{13,1},{2,6},{6,10},{... | collective-permute-start | bytes 147464 | tf_op jit(solution)/shard_map/ppermute | solution.py:320
  32.1 0.0 collective-permute-start.14
  32.1 0.5 %collective-permute-start.15 = (bf16[96,128]{1,0:T(8,128)(2,1)S(1)}, bf16[96,128]{1,0:T(8,128)(2,1)S(1)}, u32[]{:S(2)}, u32[]{:S(2)}) collective-permute-start(bf16[96,128]{1,0:T(8,128)(2,1)S(1)} %get-tuple-element.49), channel_id=1, source_target_pairs={{0,1},{1,2},{2,3},{3,0},{4,5},{5,6},{6,7},{7,4},{8,9},{9,10},{10,1... | collective-permute-start | bytes 73736 | tf_op jit(solution)/shard_map/ppermute | solution.py:322
  32.6 0.7 %shard_map.53.acc_ref = f32[768,128]{1,0:T(8,128)S(1)} custom-call(f32[768,128]{1,0:T(8,128)S(1)} %get-tuple-element.45.refs_0_.f_ref, bf16[1152,128]{1,0:T(8,128)(2,1)S(1)} %bitcast.12, f32[768,128]{1,0:T(8,128)S(1)} %get-tuple-element.39.refs_0_.f_ref.refs_2_, bf16[1152,128]{1,0:T(8,128)(2,1)S(1)} %bitcast.19), custom_call_target="tpu_custom_call" | custom-call | flops 6000000 | bytes 2097152 | tf_op jit(solution)/shard_map/pallas_call | solution.py:296
  33.3 0.3 collective-permute-done.14.refs_2_
  33.6 1.7 %collective-permute-done.15.refs_3_ = bf16[96,128]{1,0:T(8,128)(2,1)S(1)} collective-permute-done((bf16[96,128]{1,0:T(8,128)(2,1)S(1)}, bf16[96,128]{1,0:T(8,128)(2,1)S(1)}, u32[]{:S(2)}, u32[]{:S(2)}) %collective-permute-start.15) | collective-permute-done | bytes 24608 | tf_op jit(solution)/shard_map/ppermute | solution.py:322
  35.4 0.0 collective-permute-done.12.refs_0_
  35.4 1.8 %collective-permute-done.13.refs_1_ = bf16[192,128]{1,0:T(8,128)(2,1)S(1)} collective-permute-done((bf16[192,128]{1,0:T(8,128)(2,1)S(1)}, bf16[192,128]{1,0:T(8,128)(2,1)S(1)}, u32[]{:S(2)}, u32[]{:S(2)}) %collective-permute-start.13) | collective-permute-done | bytes 49184 | tf_op jit(solution)/shard_map/ppermute | solution.py:320
  37.2 1.0 %shard_map.54 = bf16[768,128]{1,0:T(8,128)(2,1)} custom-call(f32[768,128]{1,0:T(8,128)S(1)} %get-tuple-element.45.refs_0_.f_ref, bf16[1152,128]{1,0:T(8,128)(2,1)S(1)} %bitcast.13, f32[768,128]{1,0:T(8,128)S(1)} %shard_map.53.acc_ref, bf16[192,128]{1,0:T(8,128)(2,1)S(1)} %collective-permute-done.12.refs_0_, ...), custom_call_target="tpu_custom_call" | custom-call | flops 3000000 | bytes 2097152 | tf_op jit(solution)/shard_map/pallas_call | solution.py:296
  (3 shorter events, 0.0 us)
Async XLA Ops:
  0.0 1.0 %copy-start = (bf16[4,3,3,2,2,2,4,128]{7,6,5,4,3,2,1,0:T(4,128)(2,1)S(1)}, bf16[4,3,3,2,2,2,4,128]{7,6,5,4,3,2,1,0:T(4,128)(2,1)}, u32[]{:S(2)}) copy-start(bf16[4,3,3,2,2,2,4,128]{7,6,5,4,3,2,1,0:T(4,128)(2,1)} %param.5) | copy-start | bytes 884740
  1.0 0.9 %copy-start.2 = (bf16[4,4,3,2,2,4,128]{6,5,4,3,2,1,0:T(4,128)(2,1)S(1)}, bf16[4,4,3,2,2,4,128]{6,5,4,3,2,1,0:T(4,128)(2,1)}, u32[]{:S(2)}) copy-start(bf16[4,4,3,2,2,4,128]{6,5,4,3,2,1,0:T(4,128)(2,1)} %param.4) | copy-start | bytes 589828
  2.2 9.0 %collective-permute-start = (bf16[192,128]{1,0:T(8,128)(2,1)S(1)}, bf16[192,128]{1,0:T(8,128)(2,1)S(1)}, u32[]{:S(2)}, u32[]{:S(2)}) collective-permute-start(bf16[192,128]{1,0:T(8,128)(2,1)S(1)} %get-tuple-element.28), channel_id=1, source_target_pairs={{0,12},{4,0},{8,4},{12,8},{1,13},{5,1},{9,5},{13,9},{2,14},{6,2},{... | collective-permute-start | bytes 147464 | tf_op jit(solution)/shard_map/ppermute | solution.py:319
  7.3 5.9 %collective-permute-start.1 = (bf16[192,128]{1,0:T(8,128)(2,1)S(1)}, bf16[192,128]{1,0:T(8,128)(2,1)S(1)}, u32[]{:S(2)}, u32[]{:S(2)}) collective-permute-start(bf16[192,128]{1,0:T(8,128)(2,1)S(1)} %get-tuple-element.29), channel_id=1, source_target_pairs={{0,4},{4,8},{8,12},{12,0},{1,5},{5,9},{9,13},{13,1},{2,6},{6,10},{... | collective-permute-start | bytes 147464 | tf_op jit(solution)/shard_map/ppermute | solution.py:320
  7.3 2.2 %collective-permute-start.2 = (bf16[96,128]{1,0:T(8,128)(2,1)S(1)}, bf16[96,128]{1,0:T(8,128)(2,1)S(1)}, u32[]{:S(2)}, u32[]{:S(2)}) collective-permute-start(bf16[96,128]{1,0:T(8,128)(2,1)S(1)} %get-tuple-element.30), channel_id=1, source_target_pairs={{0,3},{1,0},{2,1},{3,2},{4,7},{5,4},{6,5},{7,6},{8,11},{9,8},{10,9... | collective-permute-start | bytes 73736 | tf_op jit(solution)/shard_map/ppermute | solution.py:321
  7.9 5.2 %copy-start.4 = (bf16[2,6,6,2,2,4,128]{6,5,4,3,2,1,0:T(4,128)(2,1)S(1)}, bf16[2,6,6,2,2,4,128]{6,5,4,3,2,1,0:T(4,128)(2,1)}, u32[]{:S(2)}) copy-start(bf16[2,6,6,2,2,4,128]{6,5,4,3,2,1,0:T(4,128)(2,1)} %param.7) | copy-start | bytes 884740
  7.9 3.3 %collective-permute-start.3 = (bf16[96,128]{1,0:T(8,128)(2,1)S(1)}, bf16[96,128]{1,0:T(8,128)(2,1)S(1)}, u32[]{:S(2)}, u32[]{:S(2)}) collective-permute-start(bf16[96,128]{1,0:T(8,128)(2,1)S(1)} %get-tuple-element.31), channel_id=1, source_target_pairs={{0,1},{1,2},{2,3},{3,0},{4,5},{5,6},{6,7},{7,4},{8,9},{9,10},{10,1... | collective-permute-start | bytes 73736 | tf_op jit(solution)/shard_map/ppermute | solution.py:322
  13.1 3.4 %copy-start.3 = (bf16[2,6,6,2,2,4,128]{6,5,4,3,2,1,0:T(4,128)(2,1)S(1)}, bf16[2,6,6,2,2,4,128]{6,5,4,3,2,1,0:T(4,128)(2,1)}, u32[]{:S(2)}) copy-start(bf16[2,6,6,2,2,4,128]{6,5,4,3,2,1,0:T(4,128)(2,1)} %param.6) | copy-start | bytes 884740
  14.0 5.6 %collective-permute-start.4 = (bf16[192,128]{1,0:T(8,128)(2,1)S(1)}, bf16[192,128]{1,0:T(8,128)(2,1)S(1)}, u32[]{:S(2)}, u32[]{:S(2)}) collective-permute-start(bf16[192,128]{1,0:T(8,128)(2,1)S(1)} %get-tuple-element.34), channel_id=1, source_target_pairs={{0,12},{4,0},{8,4},{12,8},{1,13},{5,1},{9,5},{13,9},{2,14},{6,2},{... | collective-permute-start | bytes 147464 | tf_op jit(solution)/shard_map/ppermute | solution.py:319
  15.6 5.9 %collective-permute-start.5 = (bf16[192,128]{1,0:T(8,128)(2,1)S(1)}, bf16[192,128]{1,0:T(8,128)(2,1)S(1)}, u32[]{:S(2)}, u32[]{:S(2)}) collective-permute-start(bf16[192,128]{1,0:T(8,128)(2,1)S(1)} %get-tuple-element.35), channel_id=1, source_target_pairs={{0,4},{4,8},{8,12},{12,0},{1,5},{5,9},{9,13},{13,1},{2,6},{6,10},{... | collective-permute-start | bytes 147464 | tf_op jit(solution)/shard_map/ppermute | solution.py:320
  16.1 1.5 %collective-permute-start.6 = (bf16[96,128]{1,0:T(8,128)(2,1)S(1)}, bf16[96,128]{1,0:T(8,128)(2,1)S(1)}, u32[]{:S(2)}, u32[]{:S(2)}) collective-permute-start(bf16[96,128]{1,0:T(8,128)(2,1)S(1)} %get-tuple-element.36), channel_id=1, source_target_pairs={{0,3},{1,0},{2,1},{3,2},{4,7},{5,4},{6,5},{7,6},{8,11},{9,8},{10,9... | collective-permute-start | bytes 73736 | tf_op jit(solution)/shard_map/ppermute | solution.py:321
  16.1 3.5 %collective-permute-start.7 = (bf16[96,128]{1,0:T(8,128)(2,1)S(1)}, bf16[96,128]{1,0:T(8,128)(2,1)S(1)}, u32[]{:S(2)}, u32[]{:S(2)}) collective-permute-start(bf16[96,128]{1,0:T(8,128)(2,1)S(1)} %get-tuple-element.37), channel_id=1, source_target_pairs={{0,1},{1,2},{2,3},{3,0},{4,5},{5,6},{6,7},{7,4},{8,9},{9,10},{10,1... | collective-permute-start | bytes 73736 | tf_op jit(solution)/shard_map/ppermute | solution.py:322
  16.6 4.9 %copy-start.1 = (bf16[4,3,3,2,2,2,4,128]{7,6,5,4,3,2,1,0:T(4,128)(2,1)S(1)}, bf16[4,3,3,2,2,2,4,128]{7,6,5,4,3,2,1,0:T(4,128)(2,1)}, u32[]{:S(2)}) copy-start(bf16[4,3,3,2,2,2,4,128]{7,6,5,4,3,2,1,0:T(4,128)(2,1)} %param.5) | copy-start | bytes 884740
  22.0 5.3 %collective-permute-start.8 = (bf16[192,128]{1,0:T(8,128)(2,1)S(1)}, bf16[192,128]{1,0:T(8,128)(2,1)S(1)}, u32[]{:S(2)}, u32[]{:S(2)}) collective-permute-start(bf16[192,128]{1,0:T(8,128)(2,1)S(1)} %get-tuple-element.40), channel_id=1, source_target_pairs={{0,12},{4,0},{8,4},{12,8},{1,13},{5,1},{9,5},{13,9},{2,14},{6,2},{... | collective-permute-start | bytes 147464 | tf_op jit(solution)/shard_map/ppermute | solution.py:319
  23.3 5.9 %collective-permute-start.9 = (bf16[192,128]{1,0:T(8,128)(2,1)S(1)}, bf16[192,128]{1,0:T(8,128)(2,1)S(1)}, u32[]{:S(2)}, u32[]{:S(2)}) collective-permute-start(bf16[192,128]{1,0:T(8,128)(2,1)S(1)} %get-tuple-element.41), channel_id=1, source_target_pairs={{0,4},{4,8},{8,12},{12,0},{1,5},{5,9},{9,13},{13,1},{2,6},{6,10},{... | collective-permute-start | bytes 147464 | tf_op jit(solution)/shard_map/ppermute | solution.py:320
  24.1 1.5 %collective-permute-start.10 = (bf16[96,128]{1,0:T(8,128)(2,1)S(1)}, bf16[96,128]{1,0:T(8,128)(2,1)S(1)}, u32[]{:S(2)}, u32[]{:S(2)}) collective-permute-start(bf16[96,128]{1,0:T(8,128)(2,1)S(1)} %get-tuple-element.42), channel_id=1, source_target_pairs={{0,3},{1,0},{2,1},{3,2},{4,7},{5,4},{6,5},{7,6},{8,11},{9,8},{10,9... | collective-permute-start | bytes 73736 | tf_op jit(solution)/shard_map/ppermute | solution.py:321
  24.1 3.3 %collective-permute-start.11 = (bf16[96,128]{1,0:T(8,128)(2,1)S(1)}, bf16[96,128]{1,0:T(8,128)(2,1)S(1)}, u32[]{:S(2)}, u32[]{:S(2)}) collective-permute-start(bf16[96,128]{1,0:T(8,128)(2,1)S(1)} %get-tuple-element.43), channel_id=1, source_target_pairs={{0,1},{1,2},{2,3},{3,0},{4,5},{5,6},{6,7},{7,4},{8,9},{9,10},{10,1... | collective-permute-start | bytes 73736 | tf_op jit(solution)/shard_map/ppermute | solution.py:322
  30.0 5.3 %collective-permute-start.12 = (bf16[192,128]{1,0:T(8,128)(2,1)S(1)}, bf16[192,128]{1,0:T(8,128)(2,1)S(1)}, u32[]{:S(2)}, u32[]{:S(2)}) collective-permute-start(bf16[192,128]{1,0:T(8,128)(2,1)S(1)} %get-tuple-element.46), channel_id=1, source_target_pairs={{0,12},{4,0},{8,4},{12,8},{1,13},{5,1},{9,5},{13,9},{2,14},{6,2},{... | collective-permute-start | bytes 147464 | tf_op jit(solution)/shard_map/ppermute | solution.py:319
  31.3 5.9 %collective-permute-start.13 = (bf16[192,128]{1,0:T(8,128)(2,1)S(1)}, bf16[192,128]{1,0:T(8,128)(2,1)S(1)}, u32[]{:S(2)}, u32[]{:S(2)}) collective-permute-start(bf16[192,128]{1,0:T(8,128)(2,1)S(1)} %get-tuple-element.47), channel_id=1, source_target_pairs={{0,4},{4,8},{8,12},{12,0},{1,5},{5,9},{9,13},{13,1},{2,6},{6,10},{... | collective-permute-start | bytes 147464 | tf_op jit(solution)/shard_map/ppermute | solution.py:320
  32.1 1.5 %collective-permute-start.14 = (bf16[96,128]{1,0:T(8,128)(2,1)S(1)}, bf16[96,128]{1,0:T(8,128)(2,1)S(1)}, u32[]{:S(2)}, u32[]{:S(2)}) collective-permute-start(bf16[96,128]{1,0:T(8,128)(2,1)S(1)} %get-tuple-element.48), channel_id=1, source_target_pairs={{0,3},{1,0},{2,1},{3,2},{4,7},{5,4},{6,5},{7,6},{8,11},{9,8},{10,9... | collective-permute-start | bytes 73736 | tf_op jit(solution)/shard_map/ppermute | solution.py:321
  32.1 3.3 %collective-permute-start.15 = (bf16[96,128]{1,0:T(8,128)(2,1)S(1)}, bf16[96,128]{1,0:T(8,128)(2,1)S(1)}, u32[]{:S(2)}, u32[]{:S(2)}) collective-permute-start(bf16[96,128]{1,0:T(8,128)(2,1)S(1)} %get-tuple-element.49), channel_id=1, source_target_pairs={{0,1},{1,2},{2,3},{3,0},{4,5},{5,6},{6,7},{7,4},{8,9},{9,10},{10,1... | collective-permute-start | bytes 73736 | tf_op jit(solution)/shard_map/ppermute | solution.py:322
where the time goes:
time: 38.3 us; the launch traced here: 38.2 us
  waiting for transfers between devices  17 us (44%)
  starting transfers between devices  13.5 us (35%)
  Pallas kernels  5.64 us (15%)
  local copies, waits for them, and re-layouts  1.9 us (5%)
    ppermute x4, starting transfers between devices, exchange(): lax.ppermute(t_back, 'ta', ring('ta', -1))  9.26 us
    ppermute x4, waiting for transfers between devices, exchange(): lax.ppermute(t_ahead, 'ta', ring('ta', 1))  7.56 us
    ppermute x4, waiting for transfers between devices, exchange(): lax.ppermute(x_ahead, 'gx', ring('gx', 1))  7.15 us
    pallas_call x9, Pallas kernels, call(): pl.pallas_call(kernel, out_shape=tuple((jax.ShapeDtypeStruct(shape, dtype...  5.64 us
    ppermute x4, waiting for transfers between devices, exchange(): lax.ppermute(x_back, 'gx', ring('gx', -1))  2.33 us
    ppermute x4, starting transfers between devices, exchange(): lax.ppermute(t_ahead, 'ta', ring('ta', 1))  2.08 us
    unnamed x10, local copies, waits for them, and re-layouts  1.9 us
    ppermute x4, starting transfers between devices, exchange(): lax.ppermute(x_ahead, 'gx', ring('gx', 1))  1.52 us
  transfers between devices with their start and end apart: 16, of which 12 were waited for; matrix products, arithmetic and copies ran while one was open for 0% of the time, Pallas kernels for 6%

commit v1 on v0

--- a/solution.py
+++ b/solution.py
@@ -107,6 +107,14 @@
     return rows // 4, rows % 4
 
 
+def even_device(axis):
+    return lax.broadcast(lax.axis_index(axis) % 2, (8, 128)) == 0
+
+
+def either(even, a, b):
+    return [select(even, a[i], b[i]) for i in range(2)]
+
+
 def roll_rows(value, shift):
     shift %= 8
     return pltpu.roll(value, shift, 0) if shift else value
@@ -117,7 +125,8 @@
 
 
 def send_halos(f_ref, links_ref, parity, outs):
-    t_back, t_ahead, x_back, x_ahead, kept = outs
+    t_far, t_near, x_far, x_near, kept = outs
+    even_t, even_x = even_device("ta"), even_device("gx")
     t_idx, x_idx = site_masks()
     first_t = t_idx == 0
     for mu in range(2):
@@ -131,8 +140,10 @@
                 moved = each(lambda v: roll_rows(v, 4), ahead)
                 back = each(lambda v: roll_rows(v, 4), carry)
                 for c in range(3):
-                    store_pair(t_back, r * 3 + c, [select(first_t, ahead[c + 3][i], moved[c][i]) for i in range(2)])
-                    store_pair(t_ahead, r * 3 + c, [select(first_t, back[c][i], carry[c + 3][i]) for i in range(2)])
+                    front = [select(first_t, ahead[c + 3][i], moved[c][i]) for i in range(2)]
+                    rear = [select(first_t, back[c][i], carry[c + 3][i]) for i in range(2)]
+                    store_pair(t_near, r * 3 + c, either(even_t, rear, front))
+                    store_pair(t_far, r * 3 + c, either(even_t, front, rear))
             else:
                 back = each(lambda v: roll_rows(v, 1), carry)
                 ahead_all.append(ahead)
@@ -151,14 +162,23 @@
                             for k in range(1, 4):
                                 packed = select(x_idx == 3 - k, roll_rows(group[k], -k), packed)
                             rear.append(packed)
-                        store_pair(x_back, (r // 2) * 3 + c, front)
-                        store_pair(x_ahead, (r // 2) * 3 + c, rear)
+                        store_pair(x_near, (r // 2) * 3 + c, either(even_x, rear, front))
+                        store_pair(x_far, (r // 2) * 3 + c, either(even_x, front, rear))
             for j in range(6):
                 store_pair(kept, (mu * RHS + r) * 6 + j, back[j])
 
 
-def start_kernel(parity, f_ref, links_ref, *outs):
-    send_halos(f_ref, links_ref, parity, outs)
+def start_kernel(f_hbm, links_hbm, *refs):
+    outs, (f_ref, links_ref, sems) = refs[:5], refs[5:]
+    copies = [
+        pltpu.make_async_copy(links_hbm.at[pl.ds(0, links_ref.shape[0])], links_ref, sems.at[0]),
+        pltpu.make_async_copy(f_hbm, f_ref, sems.at[1]),
+    ]
+    for copy in copies:
+        copy.start()
+    for copy in copies:
+        copy.wait()
+    send_halos(f_ref, links_ref, 0, outs)
 
 
 def interior_kernel(parity, with_base, *refs):
@@ -229,7 +249,8 @@
 
 
 def join_halos(f_ref, links_ref, acc_ref, halos, parity, out_ref):
-    from_next_t, from_last_t, from_next_x, from_last_x, kept = halos
+    t_far, t_near, x_far, x_near, kept = halos
+    even_t, even_x = even_device("ta"), even_device("gx")
     out_parity = 1 - parity
     t_idx, x_idx = site_masks()
     for mu in range(2):
@@ -241,8 +262,8 @@
             new_ahead, new_behind = [None] * 6, [None] * 6
             for c in range(3):
                 if mu == 0:
-                    nxt = load_pair(from_next_t, r * 3 + c)
-                    last = load_pair(from_last_t, r * 3 + c)
+                    near, far = load_pair(t_near, r * 3 + c), load_pair(t_far, r * 3 + c)
+                    nxt, last = either(even_t, near, far), either(even_t, far, near)
                     for s in range(2):
                         j = s * 3 + c
                         new_ahead[j] = tuple(
@@ -252,8 +273,8 @@
                             select(t_idx == 0, roll_rows(last[i], 4 * s), behind[j][i]) for i in range(2)
                         )
                 else:
-                    nxt = load_pair(from_next_x, (r // 2) * 3 + c)
-                    last = load_pair(from_last_x, (r // 2) * 3 + c)
+                    near, far = load_pair(x_near, (r // 2) * 3 + c), load_pair(x_far, (r // 2) * 3 + c)
+                    nxt, last = either(even_x, near, far), either(even_x, far, near)
                     for s in range(2):
                         j = s * 3 + c
                         k = (r % 2) * 2 + s
@@ -292,11 +313,11 @@
 ROWS = RHS * 24 * 8
 
 
-def call(kernel, args, outs, flops, scratch=()):
+def call(kernel, args, outs, flops, scratch=(), space=pltpu.VMEM):
     return pl.pallas_call(
         kernel,
         out_shape=tuple(jax.ShapeDtypeStruct(shape, dtype) for shape, dtype in outs),
-        in_specs=[pl.BlockSpec(memory_space=pltpu.VMEM)] * len(args),
+        in_specs=[pl.BlockSpec(memory_space=space)] * len(args),
         out_specs=tuple([pl.BlockSpec(memory_space=pltpu.VMEM)] * len(outs)),
         scratch_shapes=list(scratch),
         compiler_params=pltpu.CompilerParams(vmem_limit_bytes=24 * 1024 * 1024),
@@ -309,17 +330,18 @@
 
 
 def exchange(parts):
-    t_back, t_ahead, x_back, x_ahead, kept = parts
-
-    def ring(axis, step):
+    t_far, t_near, x_far, x_near, kept = parts
+
+    def pairs(axis, far):
         count = lax.axis_size(axis)
-        return [(i, (i + step) % count) for i in range(count)]
+        assert count % 2 == 0
+        return [(i, (i + (1 if (i % 2 == 0) != far else -1)) % count) for i in range(count)]
 
     return (
-        lax.ppermute(t_back, "ta", ring("ta", -1)),
-        lax.ppermute(t_ahead, "ta", ring("ta", 1)),
-        lax.ppermute(x_back, "gx", ring("gx", -1)),
-        lax.ppermute(x_ahead, "gx", ring("gx", 1)),
+        lax.ppermute(t_far, "ta", pairs("ta", True)),
+        lax.ppermute(t_near, "ta", pairs("ta", False)),
+        lax.ppermute(x_far, "gx", pairs("gx", True)),
+        lax.ppermute(x_near, "gx", pairs("gx", False)),
         kept,
     )
 
@@ -330,7 +352,13 @@
     links = gauge_links.reshape(-1, 128)
     even = clover_even.reshape(-1, 128)
     odd = clover_odd_inv.reshape(-1, 128)
-    parts = call(functools.partial(start_kernel, 0), (f, links), HALO_OUTS, 3_000_000)
+    start_scratch = [
+        pltpu.VMEM((ROWS, 128), BF16),
+        pltpu.VMEM((links.shape[0] // 2, 128), BF16),
+        pltpu.SemaphoreType.DMA((2,)),
+    ]
+    held = [pltpu.with_memory_space_constraint(v, pltpu.HBM) for v in (f, links)]
+    parts = call(start_kernel, held, HALO_OUTS, 3_000_000, start_scratch, pltpu.HBM)
     field_scratch = [pltpu.VMEM((ROWS, 128), F32)]
     for step in range(2):
         halos = exchange(parts)

time: 38.3 us -> 33.4 us (0.87)
  waiting for transfers between devices: 17 us -> 9.22 us
  starting transfers between devices: 13.5 us -> 17.2 us
  local copies, waits for them, and re-layouts: 1.9 us -> 0.01 us
  Pallas kernels: 5.64 us -> 6.79 us
    ppermute x16, waiting for transfers between devices: 17 us -> 9.22 us  [the longest x4 5.4 us: exchange(): lax.ppermute(x_far, 'gx', pairs('gx', True))]
    ppermute x16, starting transfers between devices: 13.5 us -> 17.2 us  [the longest x4 10.7 us: exchange(): lax.ppermute(t_far, 'ta', pairs('ta', True))]
    unnamed x10 -> x8, local copies, waits for them, and re-layouts: 1.9 us -> 0.01 us
    pallas_call x9, Pallas kernels: 5.64 us -> 6.79 us  [call(): pl.pallas_call(kernel, out_shape=tuple((jax.ShapeDtypeStruct(shape, dtype...]
  transfers between devices with their start and end apart: 16 -> 16, of which waited for: 12 -> 11; matrix products, arithmetic and copies ran while one was open for 0% -> 0% of each run, Pallas kernels for 6% -> 7%
where the time goes in v1:
time: 33.4 us; the launch traced here: 33.3 us
  starting transfers between devices  17.2 us (51%)
  waiting for transfers between devices  9.22 us (28%)
  Pallas kernels  6.79 us (20%)
    ppermute x4, starting transfers between devices, exchange(): lax.ppermute(t_far, 'ta', pairs('ta', True))  10.7 us
    pallas_call x9, Pallas kernels, call(): pl.pallas_call(kernel, out_shape=tuple((jax.ShapeDtypeStruct(shape, dtype...  6.79 us
    ppermute x4, waiting for transfers between devices, exchange(): lax.ppermute(x_far, 'gx', pairs('gx', True))  5.4 us
    ppermute x4, starting transfers between devices, exchange(): lax.ppermute(x_near, 'gx', pairs('gx', False))  5.33 us
    ppermute x4, waiting for transfers between devices, exchange(): lax.ppermute(t_near, 'ta', pairs('ta', False))  2.02 us
    ppermute x4, waiting for transfers between devices, exchange(): lax.ppermute(t_far, 'ta', pairs('ta', True))  1.79 us
  transfers between devices with their start and end apart: 16, of which 11 were waited for; matrix products, arithmetic and copies ran while one was open for 0% of the time, Pallas kernels for 7%

profile of v1, /device:TPU:0, one launch (start us, length us, event | category | flops | bytes accessed | tf_op | source)
XLA Modules:
  0.0 33.3 jit_solution(14884361132374398569)
XLA Ops:
  0.0 0.0 copy-start
  0.0 0.0 copy-start.1
  0.0 1.3 %shard_map.47 = (bf16[192,128]{1,0:T(8,128)(2,1)S(1)}, bf16[192,128]{1,0:T(8,128)(2,1)S(1)}, bf16[96,128]{1,0:T(8,128)(2,1)S(1)}, bf16[96,128]{1,0:T(8,128)(2,1)S(1)}, f32[768,128]{1,0:T(8,128)S(1)}) custom-call(bf16[768,128]{1,0:T(8,128)(2,1)} %bitcast.14, bf16[1152,128]{1,0:T(8,128)(2,1)} %bitcast.5), custom_call_target="tpu_custom_call" | custom-call | flops 3000000 | bytes 2097152 | tf_op jit(solution)/shard_map/pallas_call | solution.py:317
  1.4 5.1 %collective-permute-start = (bf16[192,128]{1,0:T(8,128)(2,1)S(1)}, bf16[192,128]{1,0:T(8,128)(2,1)S(1)}, u32[]{:S(2)}, u32[]{:S(2)}) collective-permute-start(bf16[192,128]{1,0:T(8,128)(2,1)S(1)} %get-tuple-element.28), channel_id=1, source_target_pairs={{0,12},{4,8},{8,4},{12,0},{1,13},{5,9},{9,5},{13,1},{2,14},{6,10},... | collective-permute-start | bytes 147464 | tf_op jit(solution)/shard_map/ppermute | solution.py:341
  6.5 0.0 collective-permute-start.1
  6.5 0.7 %collective-permute-start.2 = (bf16[96,128]{1,0:T(8,128)(2,1)S(1)}, bf16[96,128]{1,0:T(8,128)(2,1)S(1)}, u32[]{:S(2)}, u32[]{:S(2)}) collective-permute-start(bf16[96,128]{1,0:T(8,128)(2,1)S(1)} %get-tuple-element.30), channel_id=1, source_target_pairs={{0,3},{1,2},{2,1},{3,0},{4,7},{5,6},{6,5},{7,4},{8,11},{9,10},{10,... | collective-permute-start | bytes 73736 | tf_op jit(solution)/shard_map/ppermute | solution.py:343
  7.1 0.0 copy-start.3
  7.1 1.0 %collective-permute-start.3 = (bf16[96,128]{1,0:T(8,128)(2,1)S(1)}, bf16[96,128]{1,0:T(8,128)(2,1)S(1)}, u32[]{:S(2)}, u32[]{:S(2)}) collective-permute-start(bf16[96,128]{1,0:T(8,128)(2,1)S(1)} %get-tuple-element.31), channel_id=1, source_target_pairs={{0,1},{1,0},{2,3},{3,2},{4,5},{5,4},{6,7},{7,6},{8,9},{9,8},{10,11... | collective-permute-start | bytes 73736 | tf_op jit(solution)/shard_map/ppermute | solution.py:344
  8.1 0.0 copy-done
  8.1 0.0 copy-done.1
  8.1 0.4 %shard_map.46.acc_ref = f32[768,128]{1,0:T(8,128)S(1)} custom-call(bf16[768,128]{1,0:T(8,128)(2,1)S(1)} %bitcast.15, bf16[1152,128]{1,0:T(8,128)(2,1)S(1)} %bitcast.6), custom_call_target="tpu_custom_call" | custom-call | flops 4000000 | bytes 2097152 | tf_op jit(solution)/shard_map/pallas_call | solution.py:317
  8.5 1.4 %collective-permute-done.2.refs_2_ = bf16[96,128]{1,0:T(8,128)(2,1)S(1)} collective-permute-done((bf16[96,128]{1,0:T(8,128)(2,1)S(1)}, bf16[96,128]{1,0:T(8,128)(2,1)S(1)}, u32[]{:S(2)}, u32[]{:S(2)}) %collective-permute-start.2) | collective-permute-done | bytes 24608 | tf_op jit(solution)/shard_map/ppermute | solution.py:343
  9.9 0.0 collective-permute-done.3.refs_3_
  9.9 0.0 collective-permute-done.refs_0_
  9.9 0.6 %collective-permute-done.1.refs_1_ = bf16[192,128]{1,0:T(8,128)(2,1)S(1)} collective-permute-done((bf16[192,128]{1,0:T(8,128)(2,1)S(1)}, bf16[192,128]{1,0:T(8,128)(2,1)S(1)}, u32[]{:S(2)}, u32[]{:S(2)}) %collective-permute-start.1) | collective-permute-done | bytes 49184 | tf_op jit(solution)/shard_map/ppermute | solution.py:342
  10.6 0.0 copy-done.3
  10.6 0.9 %shard_map.48 = (f32[768,128]{1,0:T(8,128)S(1)}, bf16[192,128]{1,0:T(8,128)(2,1)S(1)}, bf16[192,128]{1,0:T(8,128)(2,1)S(1)}, bf16[96,128]{1,0:T(8,128)(2,1)S(1)}...) custom-call(bf16[768,128]{1,0:T(8,128)(2,1)S(1)} %bitcast.16, bf16[1152,128]{1,0:T(8,128)(2,1)S(1)} %bitcast.7, ...), custom_call_target="tpu_custom_call" | custom-call | flops 6000000 | bytes 2097152 | tf_op jit(solution)/shard_map/pallas_call | solution.py:317
  11.4 1.9 %collective-permute-start.4 = (bf16[192,128]{1,0:T(8,128)(2,1)S(1)}, bf16[192,128]{1,0:T(8,128)(2,1)S(1)}, u32[]{:S(2)}, u32[]{:S(2)}) collective-permute-start(bf16[192,128]{1,0:T(8,128)(2,1)S(1)} %get-tuple-element.34), channel_id=1, source_target_pairs={{0,12},{4,8},{8,4},{12,0},{1,13},{5,9},{9,5},{13,1},{2,14},{6,10},... | collective-permute-start | bytes 147464 | tf_op jit(solution)/shard_map/ppermute | solution.py:341
  13.3 0.0 collective-permute-start.5
  13.3 0.0 collective-permute-start.6
  13.3 1.6 %collective-permute-start.7 = (bf16[96,128]{1,0:T(8,128)(2,1)S(1)}, bf16[96,128]{1,0:T(8,128)(2,1)S(1)}, u32[]{:S(2)}, u32[]{:S(2)}) collective-permute-start(bf16[96,128]{1,0:T(8,128)(2,1)S(1)} %get-tuple-element.37), channel_id=1, source_target_pairs={{0,1},{1,0},{2,3},{3,2},{4,5},{5,4},{6,7},{7,6},{8,9},{9,8},{10,11... | collective-permute-start | bytes 73736 | tf_op jit(solution)/shard_map/ppermute | solution.py:344
  14.9 0.0 copy-done.2
  14.9 0.7 %shard_map.49.acc_ref = f32[768,128]{1,0:T(8,128)S(1)} custom-call(f32[768,128]{1,0:T(8,128)S(1)} %get-tuple-element.33.refs_0_.f_ref, bf16[1152,128]{1,0:T(8,128)(2,1)S(1)} %bitcast.8, bf16[768,128]{1,0:T(8,128)(2,1)S(1)} %bitcast.17, bf16[1152,128]{1,0:T(8,128)(2,1)S(1)} %bitcast.18), custom_call_target="tpu_custom_call" | custom-call | flops 6000000 | bytes 2097152 | tf_op jit(solution)/shard_map/pallas_call | solution.py:317
  15.6 1.1 %collective-permute-done.6.refs_2_ = bf16[96,128]{1,0:T(8,128)(2,1)S(1)} collective-permute-done((bf16[96,128]{1,0:T(8,128)(2,1)S(1)}, bf16[96,128]{1,0:T(8,128)(2,1)S(1)}, u32[]{:S(2)}, u32[]{:S(2)}) %collective-permute-start.6) | collective-permute-done | bytes 24608 | tf_op jit(solution)/shard_map/ppermute | solution.py:343
  16.8 0.0 collective-permute-done.7.refs_3_
  16.8 0.7 %collective-permute-done.4.refs_0_ = bf16[192,128]{1,0:T(8,128)(2,1)S(1)} collective-permute-done((bf16[192,128]{1,0:T(8,128)(2,1)S(1)}, bf16[192,128]{1,0:T(8,128)(2,1)S(1)}, u32[]{:S(2)}, u32[]{:S(2)}) %collective-permute-start.4) | collective-permute-done | bytes 49184 | tf_op jit(solution)/shard_map/ppermute | solution.py:341
  17.4 0.5 %collective-permute-done.5.refs_1_ = bf16[192,128]{1,0:T(8,128)(2,1)S(1)} collective-permute-done((bf16[192,128]{1,0:T(8,128)(2,1)S(1)}, bf16[192,128]{1,0:T(8,128)(2,1)S(1)}, u32[]{:S(2)}, u32[]{:S(2)}) %collective-permute-start.5) | collective-permute-done | bytes 49184 | tf_op jit(solution)/shard_map/ppermute | solution.py:342
  17.9 0.5 %shard_map.50 = (f32[768,128]{1,0:T(8,128)S(1)}, bf16[192,128]{1,0:T(8,128)(2,1)S(1)}, bf16[192,128]{1,0:T(8,128)(2,1)S(1)}, bf16[96,128]{1,0:T(8,128)(2,1)S(1)}...) custom-call(f32[768,128]{1,0:T(8,128)S(1)} %get-tuple-element.33.refs_0_.f_ref, bf16[1152,128]{1,0:T(8,128)(2,1)S(1)} %bitcast.9, ...), custom_call_target="tpu_custom_call" | custom-call | flops 4000000 | bytes 2097152 | tf_op jit(solution)/shard_map/pallas_call | solution.py:317
  18.5 1.9 %collective-permute-start.8 = (bf16[192,128]{1,0:T(8,128)(2,1)S(1)}, bf16[192,128]{1,0:T(8,128)(2,1)S(1)}, u32[]{:S(2)}, u32[]{:S(2)}) collective-permute-start(bf16[192,128]{1,0:T(8,128)(2,1)S(1)} %get-tuple-element.40), channel_id=1, source_target_pairs={{0,12},{4,8},{8,4},{12,0},{1,13},{5,9},{9,5},{13,1},{2,14},{6,10},... | collective-permute-start | bytes 147464 | tf_op jit(solution)/shard_map/ppermute | solution.py:341
  20.3 0.2 collective-permute-start.9
  20.5 0.0 collective-permute-start.10
  20.5 1.4 %collective-permute-start.11 = (bf16[96,128]{1,0:T(8,128)(2,1)S(1)}, bf16[96,128]{1,0:T(8,128)(2,1)S(1)}, u32[]{:S(2)}, u32[]{:S(2)}) collective-permute-start(bf16[96,128]{1,0:T(8,128)(2,1)S(1)} %get-tuple-element.43), channel_id=1, source_target_pairs={{0,1},{1,0},{2,3},{3,2},{4,5},{5,4},{6,7},{7,6},{8,9},{9,8},{10,11... | collective-permute-start | bytes 73736 | tf_op jit(solution)/shard_map/ppermute | solution.py:344
  21.9 0.4 %shard_map.51.acc_ref = f32[768,128]{1,0:T(8,128)S(1)} custom-call(f32[768,128]{1,0:T(8,128)S(1)} %get-tuple-element.39.refs_0_.f_ref.refs_2_, bf16[1152,128]{1,0:T(8,128)(2,1)S(1)} %bitcast.10), custom_call_target="tpu_custom_call" | custom-call | flops 4000000 | bytes 2097152 | tf_op jit(solution)/shard_map/pallas_call | solution.py:317
  22.3 1.6 %collective-permute-done.10.refs_2_ = bf16[96,128]{1,0:T(8,128)(2,1)S(1)} collective-permute-done((bf16[96,128]{1,0:T(8,128)(2,1)S(1)}, bf16[96,128]{1,0:T(8,128)(2,1)S(1)}, u32[]{:S(2)}, u32[]{:S(2)}) %collective-permute-start.10) | collective-permute-done | bytes 24608 | tf_op jit(solution)/shard_map/ppermute | solution.py:343
  23.9 0.0 collective-permute-done.11.refs_3_
  23.9 0.6 %collective-permute-done.8.refs_0_ = bf16[192,128]{1,0:T(8,128)(2,1)S(1)} collective-permute-done((bf16[192,128]{1,0:T(8,128)(2,1)S(1)}, bf16[192,128]{1,0:T(8,128)(2,1)S(1)}, u32[]{:S(2)}, u32[]{:S(2)}) %collective-permute-start.8) | collective-permute-done | bytes 49184 | tf_op jit(solution)/shard_map/ppermute | solution.py:341
  24.5 0.5 %collective-permute-done.9.refs_1_ = bf16[192,128]{1,0:T(8,128)(2,1)S(1)} collective-permute-done((bf16[192,128]{1,0:T(8,128)(2,1)S(1)}, bf16[192,128]{1,0:T(8,128)(2,1)S(1)}, u32[]{:S(2)}, u32[]{:S(2)}) %collective-permute-start.9) | collective-permute-done | bytes 49184 | tf_op jit(solution)/shard_map/ppermute | solution.py:342
  24.9 0.8 %shard_map.52 = (f32[768,128]{1,0:T(8,128)S(1)}, bf16[192,128]{1,0:T(8,128)(2,1)S(1)}, bf16[192,128]{1,0:T(8,128)(2,1)S(1)}, bf16[96,128]{1,0:T(8,128)(2,1)S(1)}...) custom-call(f32[768,128]{1,0:T(8,128)S(1)} %get-tuple-element.39.refs_0_.f_ref.refs_2_, ...), custom_call_target="tpu_custom_call" | custom-call | flops 6000000 | bytes 2097152 | tf_op jit(solution)/shard_map/pallas_call | solution.py:317
  25.8 1.9 %collective-permute-start.12 = (bf16[192,128]{1,0:T(8,128)(2,1)S(1)}, bf16[192,128]{1,0:T(8,128)(2,1)S(1)}, u32[]{:S(2)}, u32[]{:S(2)}) collective-permute-start(bf16[192,128]{1,0:T(8,128)(2,1)S(1)} %get-tuple-element.46), channel_id=1, source_target_pairs={{0,12},{4,8},{8,4},{12,0},{1,13},{5,9},{9,5},{13,1},{2,14},{6,10},... | collective-permute-start | bytes 147464 | tf_op jit(solution)/shard_map/ppermute | solution.py:341
  27.7 0.2 collective-permute-start.13
  27.9 0.0 collective-permute-start.14
  27.9 1.4 %collective-permute-start.15 = (bf16[96,128]{1,0:T(8,128)(2,1)S(1)}, bf16[96,128]{1,0:T(8,128)(2,1)S(1)}, u32[]{:S(2)}, u32[]{:S(2)}) collective-permute-start(bf16[96,128]{1,0:T(8,128)(2,1)S(1)} %get-tuple-element.49), channel_id=1, source_target_pairs={{0,1},{1,0},{2,3},{3,2},{4,5},{5,4},{6,7},{7,6},{8,9},{9,8},{10,11... | collective-permute-start | bytes 73736 | tf_op jit(solution)/shard_map/ppermute | solution.py:344
  29.3 0.7 %shard_map.53.acc_ref = f32[768,128]{1,0:T(8,128)S(1)} custom-call(f32[768,128]{1,0:T(8,128)S(1)} %get-tuple-element.45.refs_0_.f_ref, bf16[1152,128]{1,0:T(8,128)(2,1)S(1)} %bitcast.12, f32[768,128]{1,0:T(8,128)S(1)} %get-tuple-element.39.refs_0_.f_ref.refs_2_, bf16[1152,128]{1,0:T(8,128)(2,1)S(1)} %bitcast.19), custom_call_target="tpu_custom_call" | custom-call | flops 6000000 | bytes 2097152 | tf_op jit(solution)/shard_map/pallas_call | solution.py:317
  30.0 1.2 %collective-permute-done.14.refs_2_ = bf16[96,128]{1,0:T(8,128)(2,1)S(1)} collective-permute-done((bf16[96,128]{1,0:T(8,128)(2,1)S(1)}, bf16[96,128]{1,0:T(8,128)(2,1)S(1)}, u32[]{:S(2)}, u32[]{:S(2)}) %collective-permute-start.14) | collective-permute-done | bytes 24608 | tf_op jit(solution)/shard_map/ppermute | solution.py:343
  31.2 0.0 collective-permute-done.15.refs_3_
  31.2 0.6 %collective-permute-done.12.refs_0_ = bf16[192,128]{1,0:T(8,128)(2,1)S(1)} collective-permute-done((bf16[192,128]{1,0:T(8,128)(2,1)S(1)}, bf16[192,128]{1,0:T(8,128)(2,1)S(1)}, u32[]{:S(2)}, u32[]{:S(2)}) %collective-permute-start.12) | collective-permute-done | bytes 49184 | tf_op jit(solution)/shard_map/ppermute | solution.py:341
  31.8 0.5 %collective-permute-done.13.refs_1_ = bf16[192,128]{1,0:T(8,128)(2,1)S(1)} collective-permute-done((bf16[192,128]{1,0:T(8,128)(2,1)S(1)}, bf16[192,128]{1,0:T(8,128)(2,1)S(1)}, u32[]{:S(2)}, u32[]{:S(2)}) %collective-permute-start.13) | collective-permute-done | bytes 49184 | tf_op jit(solution)/shard_map/ppermute | solution.py:342
  32.3 1.0 %shard_map.54 = bf16[768,128]{1,0:T(8,128)(2,1)} custom-call(f32[768,128]{1,0:T(8,128)S(1)} %get-tuple-element.45.refs_0_.f_ref, bf16[1152,128]{1,0:T(8,128)(2,1)S(1)} %bitcast.13, f32[768,128]{1,0:T(8,128)S(1)} %shard_map.53.acc_ref, bf16[192,128]{1,0:T(8,128)(2,1)S(1)} %collective-permute-done.12.refs_0_, ...), custom_call_target="tpu_custom_call" | custom-call | flops 3000000 | bytes 2097152 | tf_op jit(solution)/shard_map/pallas_call | solution.py:317
  (1 shorter events, 0.0 us)
Async XLA Ops:
  0.0 8.1 %copy-start = (bf16[4,3,3,2,2,2,4,128]{7,6,5,4,3,2,1,0:T(4,128)(2,1)S(1)}, bf16[4,3,3,2,2,2,4,128]{7,6,5,4,3,2,1,0:T(4,128)(2,1)}, u32[]{:S(2)}) copy-start(bf16[4,3,3,2,2,2,4,128]{7,6,5,4,3,2,1,0:T(4,128)(2,1)} %param.5) | copy-start | bytes 884740
  0.0 8.1 %copy-start.1 = (bf16[4,4,3,2,2,4,128]{6,5,4,3,2,1,0:T(4,128)(2,1)S(1)}, bf16[4,4,3,2,2,4,128]{6,5,4,3,2,1,0:T(4,128)(2,1)}, u32[]{:S(2)}) copy-start(bf16[4,4,3,2,2,4,128]{6,5,4,3,2,1,0:T(4,128)(2,1)} %param.4) | copy-start | bytes 589828
  1.4 8.6 %collective-permute-start = (bf16[192,128]{1,0:T(8,128)(2,1)S(1)}, bf16[192,128]{1,0:T(8,128)(2,1)S(1)}, u32[]{:S(2)}, u32[]{:S(2)}) collective-permute-start(bf16[192,128]{1,0:T(8,128)(2,1)S(1)} %get-tuple-element.28), channel_id=1, source_target_pairs={{0,12},{4,8},{8,4},{12,0},{1,13},{5,9},{9,5},{13,1},{2,14},{6,10},... | collective-permute-start | bytes 147464 | tf_op jit(solution)/shard_map/ppermute | solution.py:341
  6.5 4.1 %collective-permute-start.1 = (bf16[192,128]{1,0:T(8,128)(2,1)S(1)}, bf16[192,128]{1,0:T(8,128)(2,1)S(1)}, u32[]{:S(2)}, u32[]{:S(2)}) collective-permute-start(bf16[192,128]{1,0:T(8,128)(2,1)S(1)} %get-tuple-element.29), channel_id=1, source_target_pairs={{0,4},{4,0},{8,12},{12,8},{1,5},{5,1},{9,13},{13,9},{2,6},{6,2},{1... | collective-permute-start | bytes 147464 | tf_op jit(solution)/shard_map/ppermute | solution.py:342
  6.5 3.5 %collective-permute-start.2 = (bf16[96,128]{1,0:T(8,128)(2,1)S(1)}, bf16[96,128]{1,0:T(8,128)(2,1)S(1)}, u32[]{:S(2)}, u32[]{:S(2)}) collective-permute-start(bf16[96,128]{1,0:T(8,128)(2,1)S(1)} %get-tuple-element.30), channel_id=1, source_target_pairs={{0,3},{1,2},{2,1},{3,0},{4,7},{5,6},{6,5},{7,4},{8,11},{9,10},{10,... | collective-permute-start | bytes 73736 | tf_op jit(solution)/shard_map/ppermute | solution.py:343
  7.1 3.4 %copy-start.3 = (bf16[2,6,6,2,2,4,128]{6,5,4,3,2,1,0:T(4,128)(2,1)S(1)}, bf16[2,6,6,2,2,4,128]{6,5,4,3,2,1,0:T(4,128)(2,1)}, u32[]{:S(2)}) copy-start(bf16[2,6,6,2,2,4,128]{6,5,4,3,2,1,0:T(4,128)(2,1)} %param.7) | copy-start | bytes 884740
  7.1 2.8 %collective-permute-start.3 = (bf16[96,128]{1,0:T(8,128)(2,1)S(1)}, bf16[96,128]{1,0:T(8,128)(2,1)S(1)}, u32[]{:S(2)}, u32[]{:S(2)}) collective-permute-start(bf16[96,128]{1,0:T(8,128)(2,1)S(1)} %get-tuple-element.31), channel_id=1, source_target_pairs={{0,1},{1,0},{2,3},{3,2},{4,5},{5,4},{6,7},{7,6},{8,9},{9,8},{10,11... | collective-permute-start | bytes 73736 | tf_op jit(solution)/shard_map/ppermute | solution.py:344
  10.6 4.4 %copy-start.2 = (bf16[2,6,6,2,2,4,128]{6,5,4,3,2,1,0:T(4,128)(2,1)S(1)}, bf16[2,6,6,2,2,4,128]{6,5,4,3,2,1,0:T(4,128)(2,1)}, u32[]{:S(2)}) copy-start(bf16[2,6,6,2,2,4,128]{6,5,4,3,2,1,0:T(4,128)(2,1)} %param.6) | copy-start | bytes 884740
  11.4 6.0 %collective-permute-start.4 = (bf16[192,128]{1,0:T(8,128)(2,1)S(1)}, bf16[192,128]{1,0:T(8,128)(2,1)S(1)}, u32[]{:S(2)}, u32[]{:S(2)}) collective-permute-start(bf16[192,128]{1,0:T(8,128)(2,1)S(1)} %get-tuple-element.34), channel_id=1, source_target_pairs={{0,12},{4,8},{8,4},{12,0},{1,13},{5,9},{9,5},{13,1},{2,14},{6,10},... | collective-permute-start | bytes 147464 | tf_op jit(solution)/shard_map/ppermute | solution.py:341
  13.3 4.6 %collective-permute-start.5 = (bf16[192,128]{1,0:T(8,128)(2,1)S(1)}, bf16[192,128]{1,0:T(8,128)(2,1)S(1)}, u32[]{:S(2)}, u32[]{:S(2)}) collective-permute-start(bf16[192,128]{1,0:T(8,128)(2,1)S(1)} %get-tuple-element.35), channel_id=1, source_target_pairs={{0,4},{4,0},{8,12},{12,8},{1,5},{5,1},{9,13},{13,9},{2,6},{6,2},{1... | collective-permute-start | bytes 147464 | tf_op jit(solution)/shard_map/ppermute | solution.py:342
  13.3 3.5 %collective-permute-start.6 = (bf16[96,128]{1,0:T(8,128)(2,1)S(1)}, bf16[96,128]{1,0:T(8,128)(2,1)S(1)}, u32[]{:S(2)}, u32[]{:S(2)}) collective-permute-start(bf16[96,128]{1,0:T(8,128)(2,1)S(1)} %get-tuple-element.36), channel_id=1, source_target_pairs={{0,3},{1,2},{2,1},{3,0},{4,7},{5,6},{6,5},{7,4},{8,11},{9,10},{10,... | collective-permute-start | bytes 73736 | tf_op jit(solution)/shard_map/ppermute | solution.py:343
  13.3 3.5 %collective-permute-start.7 = (bf16[96,128]{1,0:T(8,128)(2,1)S(1)}, bf16[96,128]{1,0:T(8,128)(2,1)S(1)}, u32[]{:S(2)}, u32[]{:S(2)}) collective-permute-start(bf16[96,128]{1,0:T(8,128)(2,1)S(1)} %get-tuple-element.37), channel_id=1, source_target_pairs={{0,1},{1,0},{2,3},{3,2},{4,5},{5,4},{6,7},{7,6},{8,9},{9,8},{10,11... | collective-permute-start | bytes 73736 | tf_op jit(solution)/shard_map/ppermute | solution.py:344
  18.5 6.0 %collective-permute-start.8 = (bf16[192,128]{1,0:T(8,128)(2,1)S(1)}, bf16[192,128]{1,0:T(8,128)(2,1)S(1)}, u32[]{:S(2)}, u32[]{:S(2)}) collective-permute-start(bf16[192,128]{1,0:T(8,128)(2,1)S(1)} %get-tuple-element.40), channel_id=1, source_target_pairs={{0,12},{4,8},{8,4},{12,0},{1,13},{5,9},{9,5},{13,1},{2,14},{6,10},... | collective-permute-start | bytes 147464 | tf_op jit(solution)/shard_map/ppermute | solution.py:341
  20.3 4.6 %collective-permute-start.9 = (bf16[192,128]{1,0:T(8,128)(2,1)S(1)}, bf16[192,128]{1,0:T(8,128)(2,1)S(1)}, u32[]{:S(2)}, u32[]{:S(2)}) collective-permute-start(bf16[192,128]{1,0:T(8,128)(2,1)S(1)} %get-tuple-element.41), channel_id=1, source_target_pairs={{0,4},{4,0},{8,12},{12,8},{1,5},{5,1},{9,13},{13,9},{2,6},{6,2},{1... | collective-permute-start | bytes 147464 | tf_op jit(solution)/shard_map/ppermute | solution.py:342
  20.5 3.3 %collective-permute-start.10 = (bf16[96,128]{1,0:T(8,128)(2,1)S(1)}, bf16[96,128]{1,0:T(8,128)(2,1)S(1)}, u32[]{:S(2)}, u32[]{:S(2)}) collective-permute-start(bf16[96,128]{1,0:T(8,128)(2,1)S(1)} %get-tuple-element.42), channel_id=1, source_target_pairs={{0,3},{1,2},{2,1},{3,0},{4,7},{5,6},{6,5},{7,4},{8,11},{9,10},{10,... | collective-permute-start | bytes 73736 | tf_op jit(solution)/shard_map/ppermute | solution.py:343
  20.5 3.3 %collective-permute-start.11 = (bf16[96,128]{1,0:T(8,128)(2,1)S(1)}, bf16[96,128]{1,0:T(8,128)(2,1)S(1)}, u32[]{:S(2)}, u32[]{:S(2)}) collective-permute-start(bf16[96,128]{1,0:T(8,128)(2,1)S(1)} %get-tuple-element.43), channel_id=1, source_target_pairs={{0,1},{1,0},{2,3},{3,2},{4,5},{5,4},{6,7},{7,6},{8,9},{9,8},{10,11... | collective-permute-start | bytes 73736 | tf_op jit(solution)/shard_map/ppermute | solution.py:344
  25.8 6.0 %collective-permute-start.12 = (bf16[192,128]{1,0:T(8,128)(2,1)S(1)}, bf16[192,128]{1,0:T(8,128)(2,1)S(1)}, u32[]{:S(2)}, u32[]{:S(2)}) collective-permute-start(bf16[192,128]{1,0:T(8,128)(2,1)S(1)} %get-tuple-element.46), channel_id=1, source_target_pairs={{0,12},{4,8},{8,4},{12,0},{1,13},{5,9},{9,5},{13,1},{2,14},{6,10},... | collective-permute-start | bytes 147464 | tf_op jit(solution)/shard_map/ppermute | solution.py:341
  27.7 4.6 %collective-permute-start.13 = (bf16[192,128]{1,0:T(8,128)(2,1)S(1)}, bf16[192,128]{1,0:T(8,128)(2,1)S(1)}, u32[]{:S(2)}, u32[]{:S(2)}) collective-permute-start(bf16[192,128]{1,0:T(8,128)(2,1)S(1)} %get-tuple-element.47), channel_id=1, source_target_pairs={{0,4},{4,0},{8,12},{12,8},{1,5},{5,1},{9,13},{13,9},{2,6},{6,2},{1... | collective-permute-start | bytes 147464 | tf_op jit(solution)/shard_map/ppermute | solution.py:342
  27.9 3.3 %collective-permute-start.14 = (bf16[96,128]{1,0:T(8,128)(2,1)S(1)}, bf16[96,128]{1,0:T(8,128)(2,1)S(1)}, u32[]{:S(2)}, u32[]{:S(2)}) collective-permute-start(bf16[96,128]{1,0:T(8,128)(2,1)S(1)} %get-tuple-element.48), channel_id=1, source_target_pairs={{0,3},{1,2},{2,1},{3,0},{4,7},{5,6},{6,5},{7,4},{8,11},{9,10},{10,... | collective-permute-start | bytes 73736 | tf_op jit(solution)/shard_map/ppermute | solution.py:343
  27.9 3.3 %collective-permute-start.15 = (bf16[96,128]{1,0:T(8,128)(2,1)S(1)}, bf16[96,128]{1,0:T(8,128)(2,1)S(1)}, u32[]{:S(2)}, u32[]{:S(2)}) collective-permute-start(bf16[96,128]{1,0:T(8,128)(2,1)S(1)} %get-tuple-element.49), channel_id=1, source_target_pairs={{0,1},{1,0},{2,3},{3,2},{4,5},{5,4},{6,7},{7,6},{8,9},{9,8},{10,11... | collective-permute-start | bytes 73736 | tf_op jit(solution)/shard_map/ppermute | solution.py:344

commit v2 on v1

v2 whole, which is shorter than its diff:
```python
import functools

import jax
import jax.numpy as jnp
from jax import lax
from jax.experimental import pallas as pl
from jax.experimental.pallas import tpu as pltpu
from jax.sharding import PartitionSpec as P

HALF_DEPTH = 8
KAPPA2 = 0.14 * 0.14
RHS = 4
F32 = jnp.float32
BF16 = jnp.bfloat16

SPIN = (((0, 0), (1, 0)), ((1, 3), (0, 3)), ((1, 2), (0, 0)), ((0, 3), (1, 1)))
SPIN_INV = (((0, 0), (1, 0)), ((1, 1), (0, 1)), ((1, 0), (0, 2)), ((0, 1), (1, 3)))


def add_power(base, value, power):
    (br, bi), (vr, vi) = base, value
    if power == 0:
        return br + vr, bi + vi
    if power == 1:
        return br - vi, bi + vr
    if power == 2:
        return br - vr, bi - vi
    return br + vi, bi - vr


def project(field, mu, sign):
    shift = 0 if sign > 0 else 2
    half = []
    for row in range(2):
        col, power = SPIN[mu][row]
        for c in range(3):
            half.append(add_power(field[row * 3 + c], field[(2 + col) * 3 + c], (power + shift) % 4))
    return half


def rebuild(acc, half, mu, sign):
    shift = 0 if sign > 0 else 2
    out = list(acc)
    for j in range(6):
        out[j] = add_power(out[j], half[j], 0)
    for row in range(2):
        col, power = SPIN_INV[mu][row]
        for c in range(3):
            j = (2 + row) * 3 + c
            out[j] = add_power(out[j], half[col * 3 + c], (power + shift) % 4)
    return out


def color(links, half, adjoint):
    out = []
    for s in range(2):
        for a in range(3):
            re = im = None
            for b in range(3):
                lr, li = links[b][a] if adjoint else links[a][b]
                vr, vi = half[s * 3 + b]
                if adjoint:
                    tr, ti = lr * vr + li * vi, lr * vi - li * vr
                else:
                    tr, ti = lr * vr - li * vi, lr * vi + li * vr
                re = tr if re is None else re + tr
                im = ti if im is None else im + ti
            out.append((re, im))
    return out


def each(function, half):
    return [(function(re), function(im)) for re, im in half]


def load_pair(ref, index):
    block = ref[index * 16:(index + 1) * 16, :].astype(F32)
    return block[0:8], block[8:16]


def load_links(ref, mu, parity):
    links = []
    for a in range(3):
        row = []
        for b in range(3):
            k = ((mu * 3 + a) * 3 + b) * 2
            row.append((load_pair(ref, k)[parity], load_pair(ref, k + 1)[parity]))
        links.append(row)
    return links


def load_field(ref, r):
    return [load_pair(ref, r * 12 + j) for j in range(12)]


def store_pair(ref, index, pair):
    ref[index * 16:(index + 1) * 16, :] = jnp.concatenate(pair, axis=0).astype(ref.dtype)


def store_field(ref, r, field):
    for j in range(12):
        store_pair(ref, r * 12 + j, field[j])


def site_masks():
    rows = lax.broadcasted_iota(jnp.int32, (8, 128), 0)
    return rows // 4, rows % 4


def even_device(axis):
    return lax.broadcast(lax.axis_index(axis) % 2, (8, 128)) == 0


def either(even, a, b):
    return [select(even, a[i], b[i]) for i in range(2)]


def roll_rows(value, shift):
    shift %= 8
    return pltpu.roll(value, shift, 0) if shift else value


def select(mask, a, b):
    return jnp.where(mask, a, b)


def send_t(f_ref, links_ref, parity, t_far, t_near, kept, ready=lambda r: None):
    even = even_device("ta")
    t_idx, _ = site_masks()
    first = t_idx == 0
    links = load_links(links_ref, 0, parity)
    for r in range(RHS):
        ready(r)
        field = load_field(f_ref, r)
        ahead = project(field, 0, -1)
        carry = color(links, project(field, 0, 1), True)
        moved = each(lambda v: roll_rows(v, 4), ahead)
        back = each(lambda v: roll_rows(v, 4), carry)
        for c in range(3):
            front = [select(first, ahead[c + 3][i], moved[c][i]) for i in range(2)]
            rear = [select(first, back[c][i], carry[c + 3][i]) for i in range(2)]
            store_pair(t_near, r * 3 + c, either(even, rear, front))
            store_pair(t_far, r * 3 + c, either(even, front, rear))
        for j in range(6):
            store_pair(kept, r * 6 + j, back[j])


def send_x_kernel(parity, f_ref, links_ref, x_far, x_near, kept):
    even = even_device("gx")
    _, x_idx = site_masks()
    links = load_links(links_ref, 1, parity)
    for q in range(RHS // 2):
        fronts, rears = [], []
        for r in (2 * q, 2 * q + 1):
            field = load_field(f_ref, r)
            fronts.append(project(field, 1, -1))
            rears.append(color(links, project(field, 1, 1), True))
            for j in range(6):
                store_pair(kept, r * 6 + j, [roll_rows(v, 1) for v in rears[-1][j]])
        for c in range(3):
            front, rear = [], []
            for i in range(2):
                group = [h[j][i] for h in fronts for j in (c, c + 3)]
                packed = group[0]
                for k in range(1, 4):
                    packed = select(x_idx == k, roll_rows(group[k], k), packed)
                front.append(packed)
                group = [h[j][i] for h in rears for j in (c, c + 3)]
                packed = group[0]
                for k in range(1, 4):
                    packed = select(x_idx == 3 - k, roll_rows(group[k], -k), packed)
                rear.append(packed)
            store_pair(x_near, q * 3 + c, either(even, rear, front))
            store_pair(x_far, q * 3 + c, either(even, front, rear))


def start_kernel(f_hbm, links_hbm, *refs):
    outs, (f_ref, links_ref, sems) = refs[:3], refs[3:]
    part = f_ref.shape[0] // RHS
    copies = [pltpu.make_async_copy(links_hbm.at[pl.ds(0, links_ref.shape[0])], links_ref, sems.at[RHS])]
    for r in range(RHS):
        rows = pl.ds(r * part, part)
        copies.append(pltpu.make_async_copy(f_hbm.at[rows], f_ref.at[rows], sems.at[r]))
    for copy in copies:
        copy.start()
    copies[0].wait()
    send_t(f_ref, links_ref, 0, *outs, ready=lambda r: copies[1 + r].wait())


def interior_kernel(parity, with_base, *refs):
    if with_base:
        f_ref, links_ref, kept_t, kept_x, base_ref, clover_ref, acc_ref = refs
        clover_to(clover_ref, lambda r: load_field(base_ref, r), acc_ref, 1.0)
    else:
        f_ref, links_ref, kept_t, kept_x, acc_ref = refs
    out_parity = 1 - parity
    t_idx, x_idx = site_masks()
    lane = lax.broadcasted_iota(jnp.int32, (8, 128), 1)
    odd = (t_idx + x_idx + lane // HALF_DEPTH + out_parity) % 2
    start = lane - lane % HALF_DEPTH
    up = jnp.where(odd == 1, start + (lane + 1) % HALF_DEPTH, lane)
    down = jnp.where(odd == 0, start + (lane + HALF_DEPTH - 1) % HALF_DEPTH, lane)
    zero = jnp.zeros((8, 128), F32)

    def take(value, index):
        return jnp.take_along_axis(value, index, axis=1, mode="promise_in_bounds")

    for mu in (2, 3, 0, 1):
        if mu == 2:
            ahead_of = lambda v: pltpu.roll(v, 128 - HALF_DEPTH, 1)
            behind_of = lambda v: pltpu.roll(v, HALF_DEPTH, 1)
        elif mu == 3:
            ahead_of = lambda v: take(v, up)
            behind_of = lambda v: take(v, down)
        elif mu == 0:
            ahead_of = lambda v: select(t_idx == 0, roll_rows(v, 4), 0.0)
            behind_of = lambda v: select(t_idx == 1, v, 0.0)
        else:
            ahead_of = lambda v: select(x_idx < 3, roll_rows(v, 7), 0.0)
            behind_of = lambda v: select(x_idx > 0, v, 0.0)
        links_out = load_links(links_ref, mu, out_parity)
        if mu >= 2:
            links_in = load_links(links_ref, mu, parity)
        for r in range(RHS):
            field = load_field(f_ref, r)
            if mu == 2 and not with_base:
                acc = [(zero, zero)] * 12
            else:
                acc = load_field(acc_ref, r)
            half = color(links_out, each(ahead_of, project(field, mu, -1)), False)
            acc = rebuild(acc, half, mu, -1)
            if mu >= 2:
                half = color(links_in, project(field, mu, 1), True)
            else:
                half = [load_pair(kept_t if mu == 0 else kept_x, r * 6 + j) for j in range(6)]
            acc = rebuild(acc, each(behind_of, half), mu, 1)
            store_field(acc_ref, r, acc)


def clover_to(clover_ref, get_field, out_ref, scale):
    for chi in range(2):
        matrix = {}
        for i in range(6):
            for j in range(i, 6):
                k = (chi * 6 + i) * 6 + j
                block = clover_ref[k * 16:(k + 1) * 16, :].astype(F32)
                re, im = block[0:8], block[8:16]
                if scale != 1.0:
                    re, im = re * scale, im * scale
                matrix[i, j] = (re, im)
        for r in range(RHS):
            field = get_field(r)[chi * 6:chi * 6 + 6]
            for i in range(6):
                re = im = None
                for j in range(6):
                    vr, vi = field[j]
                    mr, mi = matrix[min(i, j), max(i, j)]
                    if i <= j:
                        tr, ti = mr * vr - mi * vi, mr * vi + mi * vr
                    else:
                        tr, ti = mr * vr + mi * vi, mr * vi - mi * vr
                    re = tr if re is None else re + tr
                    im = ti if im is None else im + ti
                store_pair(out_ref, r * 12 + chi * 6 + i, (re, im))


def matvec(links, vector):
    out = []
    for a in range(3):
        re = im = None
        for b in range(3):
            (lr, li), (vr, vi) = links[a][b], vector[b]
            tr, ti = lr * vr - li * vi, lr * vi + li * vr
            re = tr if re is None else re + tr
            im = ti if im is None else im + ti
        out.append((re, im))
    return out


def rebuild_signed(acc, half, mu, sign):
    out = list(acc)
    for j in range(6):
        out[j] = add_power(out[j], half[j], 0)
    half = each(lambda v: v * sign, half)
    for row in range(2):
        col, power = SPIN_INV[mu][row]
        for c in range(3):
            j = (2 + row) * 3 + c
            out[j] = add_power(out[j], half[col * 3 + c], power)
    return out


def join_x_kernel(parity, links_ref, acc_ref, x_far, x_near, out_ref):
    even = even_device("gx")
    _, x_idx = site_masks()
    sign = jnp.where(x_idx == 3, -1.0, 1.0).astype(F32)
    links = load_links(links_ref, 1, 1 - parity)

    def edge(value):
        for k in range(3):
            value = select(x_idx == k, roll_rows(value, k - 3), value)
        return value

    links = [each(edge, row) for row in links]
    for q in range(RHS // 2):
        nxt, last = [], []
        for c in range(3):
            near, far = load_pair(x_near, q * 3 + c), load_pair(x_far, q * 3 + c)
            nxt.append(either(even, near, far))
            last.append(either(even, far, near))
        ahead = matvec(links, nxt)
        for r in (2 * q, 2 * q + 1):
            half = [None] * 6
            for s in range(2):
                k = (r % 2) * 2 + s
                for c in range(3):
                    half[s * 3 + c] = tuple(
                        select(
                            x_idx == 3,
                            roll_rows(ahead[c][i], 3 - k),
                            select(x_idx == 0, roll_rows(last[c][i], 5 + k), 0.0),
                        )
                        for i in range(2)
                    )
            store_field(out_ref, r, rebuild_signed(load_field(acc_ref, r), half, 1, sign))


def join_t(links_ref, acc_ref, t_far, t_near, parity, out_ref, done=lambda r: None):
    even = even_device("ta")
    t_idx, _ = site_masks()
    first = t_idx == 0
    sign = jnp.where(first, 1.0, -1.0).astype(F32)
    links = load_links(links_ref, 0, 1 - parity)
    links = [each(lambda v: select(first, roll_rows(v, 4), v), row) for row in links]
    for r in range(RHS):
        nxt, last = [], []
        for c in range(3):
            near, far = load_pair(t_near, r * 3 + c), load_pair(t_far, r * 3 + c)
            nxt.append(either(even, near, far))
            last.append(either(even, far, near))
        ahead = matvec(links, nxt)
        half = [tuple(select(first, last[c][i], ahead[c][i]) for i in range(2)) for c in range(3)]
        half += [
            tuple(roll_rows(select(first, ahead[c][i], last[c][i]), 4) for i in range(2)) for c in range(3)
        ]
        store_field(out_ref, r, rebuild_signed(load_field(acc_ref, r), half, 0, sign))
        done(r)


def odd_kernel(links_ref, clover_ref, acc_ref, t_far, t_near, out_ref, *refs):
    outs, summed = refs[:3], refs[3]
    join_t(links_ref, acc_ref, t_far, t_near, 0, summed)
    clover_to(clover_ref, lambda r: load_field(summed, r), out_ref, -KAPPA2)
    send_t(out_ref, links_ref, 1, *outs)


def even_kernel(links_ref, acc_ref, t_far, t_near, out_ref, *outs):
    join_t(links_ref, acc_ref, t_far, t_near, 1, out_ref)
    send_t(out_ref, links_ref, 0, *outs)


def last_kernel(links_ref, acc_ref, t_far, t_near, out_hbm, held, sems):
    part = held.shape[0] // RHS
    copies = []

    def done(r):
        rows = pl.ds(r * part, part)
        copies.append(pltpu.make_async_copy(held.at[rows], out_hbm.at[rows], sems.at[r]))
        copies[-1].start()

    join_t(links_ref, acc_ref, t_far, t_near, 1, held, done)
    for copy in copies:
        copy.wait()


ROWS = RHS * 24 * 8
FIELD = [((ROWS, 128), F32)]
KEPT = [((RHS * 12 * 8, 128), F32)]
T_HALOS = [((RHS * 3 * 16, 128), BF16)] * 2
X_HALOS = [((RHS * 3 * 8, 128), BF16)] * 2


def call(kernel, args, outs, flops, scratch=(), in_space=pltpu.VMEM, out_space=pltpu.VMEM):
    return pl.pallas_call(
        kernel,
        out_shape=tuple(jax.ShapeDtypeStruct(shape, dtype) for shape, dtype in outs),
        in_specs=[pl.BlockSpec(memory_space=in_space)] * len(args),
        out_specs=tuple([pl.BlockSpec(memory_space=out_space)] * len(outs)),
        scratch_shapes=list(scratch),
        compiler_params=pltpu.CompilerParams(vmem_limit_bytes=24 * 1024 * 1024),
        cost_estimate=pl.CostEstimate(flops=flops, bytes_accessed=2 * 1024 * 1024, transcendentals=0),
    )(*args)


def swap(value, axis, far):
    count = lax.axis_size(axis)
    assert count % 2 == 0
    pairs = [(i, (i + (1 if (i % 2 == 0) != far else -1)) % count) for i in range(count)]
    return lax.ppermute(value, axis, pairs)


def per_device(source, gauge_links, clover_even, clover_odd_inv):
    shape = source.shape
    f = source.reshape(-1, 128)
    links = gauge_links.reshape(-1, 128)
    even = clover_even.reshape(-1, 128)
    odd = clover_odd_inv.reshape(-1, 128)
    held = [pltpu.with_memory_space_constraint(v, pltpu.HBM) for v in (f, links)]
    start_scratch = [
        pltpu.VMEM((ROWS, 128), BF16),
        pltpu.VMEM((links.shape[0] // 4, 128), BF16),
        pltpu.SemaphoreType.DMA((RHS + 1,)),
    ]
    t_far, t_near, kept_t = call(start_kernel, held, T_HALOS + KEPT, 1_500_000, start_scratch, in_space=pltpu.HBM)
    for hop in range(4):
        parity = hop % 2
        t_far, t_near = swap(t_far, "ta", True), swap(t_near, "ta", False)
        x_far, x_near, kept_x = call(
            functools.partial(send_x_kernel, parity), (f, links), X_HALOS + KEPT, 1_500_000
        )
        x_far, x_near = swap(x_far, "gx", True), swap(x_near, "gx", False)
        base = (before, even) if parity else ()
        acc, = call(
            functools.partial(interior_kernel, parity, bool(parity)),
            (f, links, kept_t, kept_x, *base), FIELD, 8_000_000 if parity else 5_000_000,
        )
        acc, = call(functools.partial(join_x_kernel, parity), (links, acc, x_far, x_near), FIELD, 1_000_000)
        before = f
        if parity == 0:
            f, t_far, t_near, kept_t = call(
                odd_kernel, (links, odd, acc, t_far, t_near), FIELD + T_HALOS + KEPT, 4_000_000,
                [pltpu.VMEM((ROWS, 128), F32)],
            )
        elif hop == 1:
            f, t_far, t_near, kept_t = call(
                even_kernel, (links, acc, t_far, t_near), FIELD + T_HALOS + KEPT, 2_000_000
            )
        else:
            out, = call(
                last_kernel, (links, acc, t_far, t_near), [((ROWS, 128), BF16)], 1_000_000,
                [pltpu.VMEM((ROWS, 128), BF16), pltpu.SemaphoreType.DMA((RHS,))], out_space=pltpu.HBM,
            )
    return out.reshape(shape)


def solution(mesh):
    field_spec = P(None, None, None, None, ("groups", "ta"), "gx", None)
    link_spec = P(None, None, None, None, None, ("groups", "ta"), "gx", None)
    return jax.shard_map(
        per_device,
        mesh=mesh,
        in_specs=(field_spec, link_spec, field_spec, field_spec),
        out_specs=field_spec,
        check_vma=False,
    )
```

time: 33.4 us -> 32 us (0.958)
  waiting for transfers between devices: 9.22 us -> 6.45 us
  starting transfers between devices: 17.2 us -> 18 us
  Pallas kernels: 6.79 us -> 7.24 us
    ppermute x16, waiting for transfers between devices: 9.22 us -> 6.45 us  [swap(): return lax.ppermute(value, axis, pairs)]
    ppermute x16, starting transfers between devices: 17.2 us -> 18 us  [swap(): return lax.ppermute(value, axis, pairs)]
    pallas_call x9 -> x17, Pallas kernels: 6.79 us -> 7.24 us  [call(): pl.pallas_call(kernel, out_shape=tuple((jax.ShapeDtypeStruct(shape, dtype...]
  transfers between devices with their start and end apart: 16 -> 16, of which waited for: 11 -> 9; matrix products, arithmetic and copies ran while one was open for 0% -> 0% of each run, Pallas kernels for 7% -> 13%
where the time goes in v2:
time: 32 us; the launch traced here: 31.8 us
  starting transfers between devices  18 us (56%)
  Pallas kernels  7.24 us (23%)
  waiting for transfers between devices  6.45 us (20%)
    ppermute x16, starting transfers between devices, swap(): return lax.ppermute(value, axis, pairs)  18 us
    pallas_call x17, Pallas kernels, call(): pl.pallas_call(kernel, out_shape=tuple((jax.ShapeDtypeStruct(shape, dtype...  7.24 us
    ppermute x16, waiting for transfers between devices, swap(): return lax.ppermute(value, axis, pairs)  6.45 us
  transfers between devices with their start and end apart: 16, of which 9 were waited for; matrix products, arithmetic and copies ran while one was open for 0% of the time, Pallas kernels for 13%

profile of v2, /device:TPU:0, one launch (start us, length us, event | category | flops | bytes accessed | tf_op | source)
XLA Modules:
  0.0 31.8 jit_solution(6147336470264687494)
XLA Ops:
  0.0 1.1 %shard_map.46 = (bf16[192,128]{1,0:T(8,128)(2,1)S(1)}, bf16[192,128]{1,0:T(8,128)(2,1)S(1)}, f32[384,128]{1,0:T(8,128)S(1)}) custom-call(bf16[768,128]{1,0:T(8,128)(2,1)} %bitcast.22, bf16[1152,128]{1,0:T(8,128)(2,1)} %bitcast.5), custom_call_target="tpu_custom_call" | custom-call | flops 1500000 | bytes 2097152 | tf_op jit(solution)/shard_map/pallas_call | solution.py:384
  1.2 5.1 %collective-permute-start.2 = (bf16[192,128]{1,0:T(8,128)(2,1)S(1)}, bf16[192,128]{1,0:T(8,128)(2,1)S(1)}, u32[]{:S(2)}, u32[]{:S(2)}) collective-permute-start(bf16[192,128]{1,0:T(8,128)(2,1)S(1)} %get-tuple-element.36), channel_id=1, source_target_pairs={{0,12},{4,8},{8,4},{12,0},{1,13},{5,9},{9,5},{13,1},{2,14},{6,10},... | collective-permute-start | bytes 147464 | tf_op jit(solution)/shard_map/ppermute | solution.py:399
  6.3 0.0 collective-permute-start.3
  6.3 0.1 shard_map.47
  6.4 0.7 %collective-permute-start = (bf16[96,128]{1,0:T(8,128)(2,1)S(1)}, bf16[96,128]{1,0:T(8,128)(2,1)S(1)}, u32[]{:S(2)}, u32[]{:S(2)}) collective-permute-start(bf16[96,128]{1,0:T(8,128)(2,1)S(1)} %get-tuple-element.34), channel_id=1, source_target_pairs={{0,3},{1,2},{2,1},{3,0},{4,7},{5,6},{6,5},{7,4},{8,11},{9,10},{10,... | collective-permute-start | bytes 73736 | tf_op jit(solution)/shard_map/ppermute | solution.py:399
  7.2 1.0 %collective-permute-start.1 = (bf16[96,128]{1,0:T(8,128)(2,1)S(1)}, bf16[96,128]{1,0:T(8,128)(2,1)S(1)}, u32[]{:S(2)}, u32[]{:S(2)}) collective-permute-start(bf16[96,128]{1,0:T(8,128)(2,1)S(1)} %get-tuple-element.35), channel_id=1, source_target_pairs={{0,1},{1,0},{2,3},{3,2},{4,5},{5,4},{6,7},{7,6},{8,9},{9,8},{10,11... | collective-permute-start | bytes 73736 | tf_op jit(solution)/shard_map/ppermute | solution.py:399
  8.1 0.7 %shard_map.48.acc_ref = f32[768,128]{1,0:T(8,128)S(1)} custom-call(bf16[768,128]{1,0:T(8,128)(2,1)S(1)} %bitcast.24, bf16[1152,128]{1,0:T(8,128)(2,1)S(1)} %bitcast.7, f32[384,128]{1,0:T(8,128)S(1)} %get-tuple-element.32.refs_2_, f32[384,128]{1,0:T(8,128)S(1)} %get-tuple-element.33.refs_3_), custom_call_target="tpu_custom_call" | custom-call | flops 5000000 | bytes 2097152 | tf_op jit(solution)/shard_map/pallas_call | solution.py:384
  8.8 0.0 copy-start.2
  8.8 1.2 %collective-permute-done.x_far = bf16[96,128]{1,0:T(8,128)(2,1)S(1)} collective-permute-done((bf16[96,128]{1,0:T(8,128)(2,1)S(1)}, bf16[96,128]{1,0:T(8,128)(2,1)S(1)}, u32[]{:S(2)}, u32[]{:S(2)}) %collective-permute-start) | collective-permute-done | bytes 24608 | tf_op jit(solution)/shard_map/ppermute | solution.py:399
  10.0 0.0 collective-permute-done.1.x_near
  10.0 0.1 shard_map.49.acc_ref
  10.1 0.0 collective-permute-done.2.t_far
  10.1 0.3 collective-permute-done.3.t_near
  10.4 0.5 %shard_map.50 = (f32[768,128]{1,0:T(8,128)S(1)}, bf16[192,128]{1,0:T(8,128)(2,1)S(1)}, bf16[192,128]{1,0:T(8,128)(2,1)S(1)}, f32[384,128]{1,0:T(8,128)S(1)}) custom-call(bf16[1152,128]{1,0:T(8,128)(2,1)S(1)} %bitcast.9, bf16[1152,128]{1,0:T(8,128)(2,1)S(1)} %bitcast.26, f32[768,128]{1,0:T(8,128)S(1)} %shard_map.49.acc_ref, ...), custom_call_target="tpu_custom_call" | custom-call | flops 4000000 | bytes 2097152 | tf_op jit(solution)/shard_map/pallas_call | solution.py:384
  10.9 1.9 %collective-permute-start.6 = (bf16[192,128]{1,0:T(8,128)(2,1)S(1)}, bf16[192,128]{1,0:T(8,128)(2,1)S(1)}, u32[]{:S(2)}, u32[]{:S(2)}) collective-permute-start(bf16[192,128]{1,0:T(8,128)(2,1)S(1)} %get-tuple-element.43), channel_id=1, source_target_pairs={{0,12},{4,8},{8,4},{12,0},{1,13},{5,9},{9,5},{13,1},{2,14},{6,10},... | collective-permute-start | bytes 147464 | tf_op jit(solution)/shard_map/ppermute | solution.py:399
  12.8 0.0 collective-permute-start.7
  12.8 0.1 shard_map.51
  12.9 0.1 collective-permute-start.4
  13.0 1.6 %collective-permute-start.5 = (bf16[96,128]{1,0:T(8,128)(2,1)S(1)}, bf16[96,128]{1,0:T(8,128)(2,1)S(1)}, u32[]{:S(2)}, u32[]{:S(2)}) collective-permute-start(bf16[96,128]{1,0:T(8,128)(2,1)S(1)} %get-tuple-element.42), channel_id=1, source_target_pairs={{0,1},{1,0},{2,3},{3,2},{4,5},{5,4},{6,7},{7,6},{8,9},{9,8},{10,11... | collective-permute-start | bytes 73736 | tf_op jit(solution)/shard_map/ppermute | solution.py:399
  14.6 1.0 %shard_map.52.acc_ref = f32[768,128]{1,0:T(8,128)S(1)} custom-call(f32[768,128]{1,0:T(8,128)S(1)} %get-tuple-element.38.f_ref.refs_0_, bf16[1152,128]{1,0:T(8,128)(2,1)S(1)} %bitcast.11, f32[384,128]{1,0:T(8,128)S(1)} %get-tuple-element.39.refs_2_, f32[384,128]{1,0:T(8,128)S(1)} %get-tuple-element.40.refs_3_, bf16[768,128]{1,0:T(8,128)(2,1)S(1)} %bitcast.25, ...), custom_call_target="tpu_custom_call" | custom-call | flops 8000000 | bytes 2097152 | tf_op jit(solution)/shard_map/pallas_call | solution.py:384
  15.5 0.9 %collective-permute-done.4.x_far = bf16[96,128]{1,0:T(8,128)(2,1)S(1)} collective-permute-done((bf16[96,128]{1,0:T(8,128)(2,1)S(1)}, bf16[96,128]{1,0:T(8,128)(2,1)S(1)}, u32[]{:S(2)}, u32[]{:S(2)}) %collective-permute-start.4) | collective-permute-done | bytes 24608 | tf_op jit(solution)/shard_map/ppermute | solution.py:399
  16.5 0.0 collective-permute-done.5.x_near
  16.5 0.1 shard_map.53.acc_ref
  16.6 0.6 %collective-permute-done.6.t_far = bf16[192,128]{1,0:T(8,128)(2,1)S(1)} collective-permute-done((bf16[192,128]{1,0:T(8,128)(2,1)S(1)}, bf16[192,128]{1,0:T(8,128)(2,1)S(1)}, u32[]{:S(2)}, u32[]{:S(2)}) %collective-permute-start.6) | collective-permute-done | bytes 49184 | tf_op jit(solution)/shard_map/ppermute | solution.py:399
  17.2 0.2 collective-permute-done.7.t_near
  17.4 0.2 shard_map.54
  17.6 2.0 %collective-permute-start.10 = (bf16[192,128]{1,0:T(8,128)(2,1)S(1)}, bf16[192,128]{1,0:T(8,128)(2,1)S(1)}, u32[]{:S(2)}, u32[]{:S(2)}) collective-permute-start(bf16[192,128]{1,0:T(8,128)(2,1)S(1)} %get-tuple-element.50), channel_id=1, source_target_pairs={{0,12},{4,8},{8,4},{12,0},{1,13},{5,9},{9,5},{13,1},{2,14},{6,10},... | collective-permute-start | bytes 147464 | tf_op jit(solution)/shard_map/ppermute | solution.py:399
  19.6 0.4 %collective-permute-start.11 = (bf16[192,128]{1,0:T(8,128)(2,1)S(1)}, bf16[192,128]{1,0:T(8,128)(2,1)S(1)}, u32[]{:S(2)}, u32[]{:S(2)}) collective-permute-start(bf16[192,128]{1,0:T(8,128)(2,1)S(1)} %get-tuple-element.51), channel_id=1, source_target_pairs={{0,4},{4,0},{8,12},{12,8},{1,5},{5,1},{9,13},{13,9},{2,6},{6,2},{1... | collective-permute-start | bytes 147464 | tf_op jit(solution)/shard_map/ppermute | solution.py:399
  20.0 0.1 shard_map.55
  20.1 0.1 collective-permute-start.8
  20.2 1.4 %collective-permute-start.9 = (bf16[96,128]{1,0:T(8,128)(2,1)S(1)}, bf16[96,128]{1,0:T(8,128)(2,1)S(1)}, u32[]{:S(2)}, u32[]{:S(2)}) collective-permute-start(bf16[96,128]{1,0:T(8,128)(2,1)S(1)} %get-tuple-element.49), channel_id=1, source_target_pairs={{0,1},{1,0},{2,3},{3,2},{4,5},{5,4},{6,7},{7,6},{8,9},{9,8},{10,11... | collective-permute-start | bytes 73736 | tf_op jit(solution)/shard_map/ppermute | solution.py:399
  21.6 0.6 %shard_map.56.acc_ref = f32[768,128]{1,0:T(8,128)S(1)} custom-call(f32[768,128]{1,0:T(8,128)S(1)} %get-tuple-element.45.f_ref.refs_0_.refs_4_, bf16[1152,128]{1,0:T(8,128)(2,1)S(1)} %bitcast.15, f32[384,128]{1,0:T(8,128)S(1)} %get-tuple-element.46.refs_2_, f32[384,128]{1,0:T(8,128)S(1)} %get-tuple-element.47.refs_3_), custom_call_target="tpu_custom_call" | custom-call | flops 5000000 | bytes 2097152 | tf_op jit(solution)/shard_map/pallas_call | solution.py:384
  22.2 1.3 %collective-permute-done.8.x_far = bf16[96,128]{1,0:T(8,128)(2,1)S(1)} collective-permute-done((bf16[96,128]{1,0:T(8,128)(2,1)S(1)}, bf16[96,128]{1,0:T(8,128)(2,1)S(1)}, u32[]{:S(2)}, u32[]{:S(2)}) %collective-permute-start.8) | collective-permute-done | bytes 24608 | tf_op jit(solution)/shard_map/ppermute | solution.py:399
  23.5 0.0 collective-permute-done.9.x_near
  23.5 0.1 shard_map.57.acc_ref
  23.6 0.5 %collective-permute-done.11.t_near = bf16[192,128]{1,0:T(8,128)(2,1)S(1)} collective-permute-done((bf16[192,128]{1,0:T(8,128)(2,1)S(1)}, bf16[192,128]{1,0:T(8,128)(2,1)S(1)}, u32[]{:S(2)}, u32[]{:S(2)}) %collective-permute-start.11) | collective-permute-done | bytes 49184 | tf_op jit(solution)/shard_map/ppermute | solution.py:399
  24.1 0.5 %shard_map.58 = (f32[768,128]{1,0:T(8,128)S(1)}, bf16[192,128]{1,0:T(8,128)(2,1)S(1)}, bf16[192,128]{1,0:T(8,128)(2,1)S(1)}, f32[384,128]{1,0:T(8,128)S(1)}) custom-call(bf16[1152,128]{1,0:T(8,128)(2,1)S(1)} %bitcast.17, bf16[1152,128]{1,0:T(8,128)(2,1)S(1)} %bitcast.27, f32[768,128]{1,0:T(8,128)S(1)} %shard_map.57.acc_ref, ...), custom_call_target="tpu_custom_call" | custom-call | flops 4000000 | bytes 2097152 | tf_op jit(solution)/shard_map/pallas_call | solution.py:384
  24.6 2.0 %collective-permute-start.14 = (bf16[192,128]{1,0:T(8,128)(2,1)S(1)}, bf16[192,128]{1,0:T(8,128)(2,1)S(1)}, u32[]{:S(2)}, u32[]{:S(2)}) collective-permute-start(bf16[192,128]{1,0:T(8,128)(2,1)S(1)} %get-tuple-element.57), channel_id=1, source_target_pairs={{0,12},{4,8},{8,4},{12,0},{1,13},{5,9},{9,5},{13,1},{2,14},{6,10},... | collective-permute-start | bytes 147464 | tf_op jit(solution)/shard_map/ppermute | solution.py:399
  26.6 0.4 %collective-permute-start.15 = (bf16[192,128]{1,0:T(8,128)(2,1)S(1)}, bf16[192,128]{1,0:T(8,128)(2,1)S(1)}, u32[]{:S(2)}, u32[]{:S(2)}) collective-permute-start(bf16[192,128]{1,0:T(8,128)(2,1)S(1)} %get-tuple-element.58), channel_id=1, source_target_pairs={{0,4},{4,0},{8,12},{12,8},{1,5},{5,1},{9,13},{13,9},{2,6},{6,2},{1... | collective-permute-start | bytes 147464 | tf_op jit(solution)/shard_map/ppermute | solution.py:399
  27.0 0.1 shard_map.59
  27.1 0.1 collective-permute-start.12
  27.2 1.4 %collective-permute-start.13 = (bf16[96,128]{1,0:T(8,128)(2,1)S(1)}, bf16[96,128]{1,0:T(8,128)(2,1)S(1)}, u32[]{:S(2)}, u32[]{:S(2)}) collective-permute-start(bf16[96,128]{1,0:T(8,128)(2,1)S(1)} %get-tuple-element.56), channel_id=1, source_target_pairs={{0,1},{1,0},{2,3},{3,2},{4,5},{5,4},{6,7},{7,6},{8,9},{9,8},{10,11... | collective-permute-start | bytes 73736 | tf_op jit(solution)/shard_map/ppermute | solution.py:399
  28.6 1.0 %shard_map.60.acc_ref = f32[768,128]{1,0:T(8,128)S(1)} custom-call(f32[768,128]{1,0:T(8,128)S(1)} %get-tuple-element.52.f_ref.refs_0_, bf16[1152,128]{1,0:T(8,128)(2,1)S(1)} %bitcast.19, f32[384,128]{1,0:T(8,128)S(1)} %get-tuple-element.53.refs_2_, f32[384,128]{1,0:T(8,128)S(1)} %get-tuple-element.54.refs_3_, ...), custom_call_target="tpu_custom_call" | custom-call | flops 8000000 | bytes 2097152 | tf_op jit(solution)/shard_map/pallas_call | solution.py:384
  29.5 1.0 %collective-permute-done.12.x_far = bf16[96,128]{1,0:T(8,128)(2,1)S(1)} collective-permute-done((bf16[96,128]{1,0:T(8,128)(2,1)S(1)}, bf16[96,128]{1,0:T(8,128)(2,1)S(1)}, u32[]{:S(2)}, u32[]{:S(2)}) %collective-permute-start.12) | collective-permute-done | bytes 24608 | tf_op jit(solution)/shard_map/ppermute | solution.py:399
  30.5 0.1 shard_map.61.acc_ref
  30.6 0.0 collective-permute-done.14.t_far
  30.6 0.5 %collective-permute-done.15.t_near = bf16[192,128]{1,0:T(8,128)(2,1)S(1)} collective-permute-done((bf16[192,128]{1,0:T(8,128)(2,1)S(1)}, bf16[192,128]{1,0:T(8,128)(2,1)S(1)}, u32[]{:S(2)}, u32[]{:S(2)}) %collective-permute-start.15) | collective-permute-done | bytes 49184 | tf_op jit(solution)/shard_map/ppermute | solution.py:399
  31.1 0.8 %shard_map.62 = bf16[768,128]{1,0:T(8,128)(2,1)} custom-call(bf16[1152,128]{1,0:T(8,128)(2,1)S(1)} %bitcast.21, f32[768,128]{1,0:T(8,128)S(1)} %shard_map.61.acc_ref, bf16[192,128]{1,0:T(8,128)(2,1)S(1)} %collective-permute-done.14.t_far, bf16[192,128]{1,0:T(8,128)(2,1)S(1)} %collective-permute-done.15.t_near), custom_call_target="tpu_custom_call" | custom-call | flops 1000000 | bytes 2097152 | tf_op jit(solution)/shard_map/pallas_call | solution.py:384
  (9 shorter events, 0.0 us)
Async XLA Ops:
  0.0 6.3 %copy-start = (bf16[4,3,3,2,2,2,4,128]{7,6,5,4,3,2,1,0:T(4,128)(2,1)S(1)}, bf16[4,3,3,2,2,2,4,128]{7,6,5,4,3,2,1,0:T(4,128)(2,1)}, u32[]{:S(2)}) copy-start(bf16[4,3,3,2,2,2,4,128]{7,6,5,4,3,2,1,0:T(4,128)(2,1)} %param.5) | copy-start | bytes 884740
  0.0 6.3 %copy-start.1 = (bf16[4,4,3,2,2,4,128]{6,5,4,3,2,1,0:T(4,128)(2,1)S(1)}, bf16[4,4,3,2,2,4,128]{6,5,4,3,2,1,0:T(4,128)(2,1)}, u32[]{:S(2)}) copy-start(bf16[4,4,3,2,2,4,128]{6,5,4,3,2,1,0:T(4,128)(2,1)} %param.4) | copy-start | bytes 589828
  1.2 8.9 %collective-permute-start.2 = (bf16[192,128]{1,0:T(8,128)(2,1)S(1)}, bf16[192,128]{1,0:T(8,128)(2,1)S(1)}, u32[]{:S(2)}, u32[]{:S(2)}) collective-permute-start(bf16[192,128]{1,0:T(8,128)(2,1)S(1)} %get-tuple-element.36), channel_id=1, source_target_pairs={{0,12},{4,8},{8,4},{12,0},{1,13},{5,9},{9,5},{13,1},{2,14},{6,10},... | collective-permute-start | bytes 147464 | tf_op jit(solution)/shard_map/ppermute | solution.py:399
  6.3 4.1 %collective-permute-start.3 = (bf16[192,128]{1,0:T(8,128)(2,1)S(1)}, bf16[192,128]{1,0:T(8,128)(2,1)S(1)}, u32[]{:S(2)}, u32[]{:S(2)}) collective-permute-start(bf16[192,128]{1,0:T(8,128)(2,1)S(1)} %get-tuple-element.37), channel_id=1, source_target_pairs={{0,4},{4,0},{8,12},{12,8},{1,5},{5,1},{9,13},{13,9},{2,6},{6,2},{1... | collective-permute-start | bytes 147464 | tf_op jit(solution)/shard_map/ppermute | solution.py:399
  6.4 3.5 %collective-permute-start = (bf16[96,128]{1,0:T(8,128)(2,1)S(1)}, bf16[96,128]{1,0:T(8,128)(2,1)S(1)}, u32[]{:S(2)}, u32[]{:S(2)}) collective-permute-start(bf16[96,128]{1,0:T(8,128)(2,1)S(1)} %get-tuple-element.34), channel_id=1, source_target_pairs={{0,3},{1,2},{2,1},{3,0},{4,7},{5,6},{6,5},{7,4},{8,11},{9,10},{10,... | collective-permute-start | bytes 73736 | tf_op jit(solution)/shard_map/ppermute | solution.py:399
  7.2 2.8 %collective-permute-start.1 = (bf16[96,128]{1,0:T(8,128)(2,1)S(1)}, bf16[96,128]{1,0:T(8,128)(2,1)S(1)}, u32[]{:S(2)}, u32[]{:S(2)}) collective-permute-start(bf16[96,128]{1,0:T(8,128)(2,1)S(1)} %get-tuple-element.35), channel_id=1, source_target_pairs={{0,1},{1,0},{2,3},{3,2},{4,5},{5,4},{6,7},{7,6},{8,9},{9,8},{10,11... | collective-permute-start | bytes 73736 | tf_op jit(solution)/shard_map/ppermute | solution.py:399
  8.8 1.6 %copy-start.2 = (bf16[2,6,6,2,2,4,128]{6,5,4,3,2,1,0:T(4,128)(2,1)S(1)}, bf16[2,6,6,2,2,4,128]{6,5,4,3,2,1,0:T(4,128)(2,1)}, u32[]{:S(2)}) copy-start(bf16[2,6,6,2,2,4,128]{6,5,4,3,2,1,0:T(4,128)(2,1)} %param.7) | copy-start | bytes 884740
  10.9 6.3 %collective-permute-start.6 = (bf16[192,128]{1,0:T(8,128)(2,1)S(1)}, bf16[192,128]{1,0:T(8,128)(2,1)S(1)}, u32[]{:S(2)}, u32[]{:S(2)}) collective-permute-start(bf16[192,128]{1,0:T(8,128)(2,1)S(1)} %get-tuple-element.43), channel_id=1, source_target_pairs={{0,12},{4,8},{8,4},{12,0},{1,13},{5,9},{9,5},{13,1},{2,14},{6,10},... | collective-permute-start | bytes 147464 | tf_op jit(solution)/shard_map/ppermute | solution.py:399
  12.8 4.6 %collective-permute-start.7 = (bf16[192,128]{1,0:T(8,128)(2,1)S(1)}, bf16[192,128]{1,0:T(8,128)(2,1)S(1)}, u32[]{:S(2)}, u32[]{:S(2)}) collective-permute-start(bf16[192,128]{1,0:T(8,128)(2,1)S(1)} %get-tuple-element.44), channel_id=1, source_target_pairs={{0,4},{4,0},{8,12},{12,8},{1,5},{5,1},{9,13},{13,9},{2,6},{6,2},{1... | collective-permute-start | bytes 147464 | tf_op jit(solution)/shard_map/ppermute | solution.py:399
  12.8 1.8 %copy-start.3 = (bf16[2,6,6,2,2,4,128]{6,5,4,3,2,1,0:T(4,128)(2,1)S(1)}, bf16[2,6,6,2,2,4,128]{6,5,4,3,2,1,0:T(4,128)(2,1)}, u32[]{:S(2)}) copy-start(bf16[2,6,6,2,2,4,128]{6,5,4,3,2,1,0:T(4,128)(2,1)} %param.6) | copy-start | bytes 884740
  12.9 3.6 %collective-permute-start.4 = (bf16[96,128]{1,0:T(8,128)(2,1)S(1)}, bf16[96,128]{1,0:T(8,128)(2,1)S(1)}, u32[]{:S(2)}, u32[]{:S(2)}) collective-permute-start(bf16[96,128]{1,0:T(8,128)(2,1)S(1)} %get-tuple-element.41), channel_id=1, source_target_pairs={{0,3},{1,2},{2,1},{3,0},{4,7},{5,6},{6,5},{7,4},{8,11},{9,10},{10,... | collective-permute-start | bytes 73736 | tf_op jit(solution)/shard_map/ppermute | solution.py:399
  13.0 3.5 %collective-permute-start.5 = (bf16[96,128]{1,0:T(8,128)(2,1)S(1)}, bf16[96,128]{1,0:T(8,128)(2,1)S(1)}, u32[]{:S(2)}, u32[]{:S(2)}) collective-permute-start(bf16[96,128]{1,0:T(8,128)(2,1)S(1)} %get-tuple-element.42), channel_id=1, source_target_pairs={{0,1},{1,0},{2,3},{3,2},{4,5},{5,4},{6,7},{7,6},{8,9},{9,8},{10,11... | collective-permute-start | bytes 73736 | tf_op jit(solution)/shard_map/ppermute | solution.py:399
  17.6 6.0 %collective-permute-start.10 = (bf16[192,128]{1,0:T(8,128)(2,1)S(1)}, bf16[192,128]{1,0:T(8,128)(2,1)S(1)}, u32[]{:S(2)}, u32[]{:S(2)}) collective-permute-start(bf16[192,128]{1,0:T(8,128)(2,1)S(1)} %get-tuple-element.50), channel_id=1, source_target_pairs={{0,12},{4,8},{8,4},{12,0},{1,13},{5,9},{9,5},{13,1},{2,14},{6,10},... | collective-permute-start | bytes 147464 | tf_op jit(solution)/shard_map/ppermute | solution.py:399
  19.6 4.5 %collective-permute-start.11 = (bf16[192,128]{1,0:T(8,128)(2,1)S(1)}, bf16[192,128]{1,0:T(8,128)(2,1)S(1)}, u32[]{:S(2)}, u32[]{:S(2)}) collective-permute-start(bf16[192,128]{1,0:T(8,128)(2,1)S(1)} %get-tuple-element.51), channel_id=1, source_target_pairs={{0,4},{4,0},{8,12},{12,8},{1,5},{5,1},{9,13},{13,9},{2,6},{6,2},{1... | collective-permute-start | bytes 147464 | tf_op jit(solution)/shard_map/ppermute | solution.py:399
  20.1 3.4 %collective-permute-start.8 = (bf16[96,128]{1,0:T(8,128)(2,1)S(1)}, bf16[96,128]{1,0:T(8,128)(2,1)S(1)}, u32[]{:S(2)}, u32[]{:S(2)}) collective-permute-start(bf16[96,128]{1,0:T(8,128)(2,1)S(1)} %get-tuple-element.48), channel_id=1, source_target_pairs={{0,3},{1,2},{2,1},{3,0},{4,7},{5,6},{6,5},{7,4},{8,11},{9,10},{10,... | collective-permute-start | bytes 73736 | tf_op jit(solution)/shard_map/ppermute | solution.py:399
  20.2 3.3 %collective-permute-start.9 = (bf16[96,128]{1,0:T(8,128)(2,1)S(1)}, bf16[96,128]{1,0:T(8,128)(2,1)S(1)}, u32[]{:S(2)}, u32[]{:S(2)}) collective-permute-start(bf16[96,128]{1,0:T(8,128)(2,1)S(1)} %get-tuple-element.49), channel_id=1, source_target_pairs={{0,1},{1,0},{2,3},{3,2},{4,5},{5,4},{6,7},{7,6},{8,9},{9,8},{10,11... | collective-permute-start | bytes 73736 | tf_op jit(solution)/shard_map/ppermute | solution.py:399
  24.6 6.0 %collective-permute-start.14 = (bf16[192,128]{1,0:T(8,128)(2,1)S(1)}, bf16[192,128]{1,0:T(8,128)(2,1)S(1)}, u32[]{:S(2)}, u32[]{:S(2)}) collective-permute-start(bf16[192,128]{1,0:T(8,128)(2,1)S(1)} %get-tuple-element.57), channel_id=1, source_target_pairs={{0,12},{4,8},{8,4},{12,0},{1,13},{5,9},{9,5},{13,1},{2,14},{6,10},... | collective-permute-start | bytes 147464 | tf_op jit(solution)/shard_map/ppermute | solution.py:399
  26.6 4.5 %collective-permute-start.15 = (bf16[192,128]{1,0:T(8,128)(2,1)S(1)}, bf16[192,128]{1,0:T(8,128)(2,1)S(1)}, u32[]{:S(2)}, u32[]{:S(2)}) collective-permute-start(bf16[192,128]{1,0:T(8,128)(2,1)S(1)} %get-tuple-element.58), channel_id=1, source_target_pairs={{0,4},{4,0},{8,12},{12,8},{1,5},{5,1},{9,13},{13,9},{2,6},{6,2},{1... | collective-permute-start | bytes 147464 | tf_op jit(solution)/shard_map/ppermute | solution.py:399
  27.1 3.4 %collective-permute-start.12 = (bf16[96,128]{1,0:T(8,128)(2,1)S(1)}, bf16[96,128]{1,0:T(8,128)(2,1)S(1)}, u32[]{:S(2)}, u32[]{:S(2)}) collective-permute-start(bf16[96,128]{1,0:T(8,128)(2,1)S(1)} %get-tuple-element.55), channel_id=1, source_target_pairs={{0,3},{1,2},{2,1},{3,0},{4,7},{5,6},{6,5},{7,4},{8,11},{9,10},{10,... | collective-permute-start | bytes 73736 | tf_op jit(solution)/shard_map/ppermute | solution.py:399
  27.2 3.3 %collective-permute-start.13 = (bf16[96,128]{1,0:T(8,128)(2,1)S(1)}, bf16[96,128]{1,0:T(8,128)(2,1)S(1)}, u32[]{:S(2)}, u32[]{:S(2)}) collective-permute-start(bf16[96,128]{1,0:T(8,128)(2,1)S(1)} %get-tuple-element.56), channel_id=1, source_target_pairs={{0,1},{1,0},{2,3},{3,2},{4,5},{5,4},{6,7},{7,6},{8,9},{9,8},{10,11... | collective-permute-start | bytes 73736 | tf_op jit(solution)/shard_map/ppermute | solution.py:399

commit v3 on v2

--- a/solution.py
+++ b/solution.py
@@ -112,6 +112,8 @@
 
 
 def either(even, a, b):
+    if isinstance(even, bool):
+        return a if even else b
     return [select(even, a[i], b[i]) for i in range(2)]
 
 
@@ -124,8 +126,7 @@
     return jnp.where(mask, a, b)
 
 
-def send_t(f_ref, links_ref, parity, t_far, t_near, kept, ready=lambda r: None):
-    even = even_device("ta")
+def send_t(f_ref, links_ref, parity, even, t_far, t_near, kept, ready=lambda r: None):
     t_idx, _ = site_masks()
     first = t_idx == 0
     links = load_links(links_ref, 0, parity)
@@ -184,7 +185,7 @@
     for copy in copies:
         copy.start()
     copies[0].wait()
-    send_t(f_ref, links_ref, 0, *outs, ready=lambda r: copies[1 + r].wait())
+    send_t(f_ref, links_ref, 0, even_device("ta"), *outs, ready=lambda r: copies[1 + r].wait())
 
 
 def interior_kernel(parity, with_base, *refs):
@@ -302,6 +303,8 @@
         return value
 
     links = [each(edge, row) for row in links]
+    part = x_near.shape[0] // 2
+    x_near = x_near.at[pl.ds(pl.multiple_of((1 - lax.axis_index("gx") % 2) * part, part), part)]
     for q in range(RHS // 2):
         nxt, last = [], []
         for c in range(3):
@@ -325,8 +328,7 @@
             store_field(out_ref, r, rebuild_signed(load_field(acc_ref, r), half, 1, sign))
 
 
-def join_t(links_ref, acc_ref, t_far, t_near, parity, out_ref, done=lambda r: None):
-    even = even_device("ta")
+def join_t(links_ref, acc_ref, t_far, t_near, parity, even, out_ref, done=lambda r: None):
     t_idx, _ = site_masks()
     first = t_idx == 0
     sign = jnp.where(first, 1.0, -1.0).astype(F32)
@@ -347,30 +349,45 @@
         done(r)
 
 
-def odd_kernel(links_ref, clover_ref, acc_ref, t_far, t_near, out_ref, *refs):
-    outs, summed = refs[:3], refs[3]
-    join_t(links_ref, acc_ref, t_far, t_near, 0, summed)
-    clover_to(clover_ref, lambda r: load_field(summed, r), out_ref, -KAPPA2)
-    send_t(out_ref, links_ref, 1, *outs)
-
-
-def even_kernel(links_ref, acc_ref, t_far, t_near, out_ref, *outs):
-    join_t(links_ref, acc_ref, t_far, t_near, 1, out_ref)
-    send_t(out_ref, links_ref, 0, *outs)
-
-
-def last_kernel(links_ref, acc_ref, t_far, t_near, out_hbm, held, sems):
+def for_class(even, body):
+    pl.when(lax.axis_index("ta") % 2 == (0 if even else 1))(body)
+
+
+def odd_kernel(even, links_ref, clover_ref, acc_ref, t_far, t_near, *refs):
+    out_ref, kept, far_out, near_out, summed = refs[-5:]
+
+    @functools.partial(for_class, even)
+    def body():
+        join_t(links_ref, acc_ref, t_far, t_near, 0, even, summed)
+        clover_to(clover_ref, lambda r: load_field(summed, r), out_ref, -KAPPA2)
+        send_t(out_ref, links_ref, 1, even, far_out, near_out, kept)
+
+
+def even_kernel(even, links_ref, acc_ref, t_far, t_near, *refs):
+    out_ref, kept, far_out, near_out = refs[-4:]
+
+    @functools.partial(for_class, even)
+    def body():
+        join_t(links_ref, acc_ref, t_far, t_near, 1, even, out_ref)
+        send_t(out_ref, links_ref, 0, even, far_out, near_out, kept)
+
+
+def last_kernel(even, links_ref, acc_ref, t_far, t_near, *refs):
+    out_hbm, held, sems = refs[-3:]
     part = held.shape[0] // RHS
-    copies = []
-
-    def done(r):
-        rows = pl.ds(r * part, part)
-        copies.append(pltpu.make_async_copy(held.at[rows], out_hbm.at[rows], sems.at[r]))
-        copies[-1].start()
-
-    join_t(links_ref, acc_ref, t_far, t_near, 1, held, done)
-    for copy in copies:
-        copy.wait()
+
+    @functools.partial(for_class, even)
+    def body():
+        copies = []
+
+        def done(r):
+            rows = pl.ds(r * part, part)
+            copies.append(pltpu.make_async_copy(held.at[rows], out_hbm.at[rows], sems.at[r]))
+            copies[-1].start()
+
+        join_t(links_ref, acc_ref, t_far, t_near, 1, even, held, done)
+        for copy in copies:
+            copy.wait()
 
 
 ROWS = RHS * 24 * 8
@@ -380,23 +397,36 @@
 X_HALOS = [((RHS * 3 * 8, 128), BF16)] * 2
 
 
-def call(kernel, args, outs, flops, scratch=(), in_space=pltpu.VMEM, out_space=pltpu.VMEM):
+def call(kernel, args, outs, flops, scratch=(), in_space=pltpu.VMEM, out_space=pltpu.VMEM, kept=()):
     return pl.pallas_call(
         kernel,
         out_shape=tuple(jax.ShapeDtypeStruct(shape, dtype) for shape, dtype in outs),
-        in_specs=[pl.BlockSpec(memory_space=in_space)] * len(args),
+        in_specs=[pl.BlockSpec(memory_space=in_space)] * len(args) + [pl.BlockSpec(memory_space=pl.ANY)] * len(kept),
         out_specs=tuple([pl.BlockSpec(memory_space=out_space)] * len(outs)),
         scratch_shapes=list(scratch),
+        input_output_aliases={len(args) + i: i for i in range(len(kept))},
         compiler_params=pltpu.CompilerParams(vmem_limit_bytes=24 * 1024 * 1024),
-        cost_estimate=pl.CostEstimate(flops=flops, bytes_accessed=2 * 1024 * 1024, transcendentals=0),
-    )(*args)
-
-
-def swap(value, axis, far):
+        cost_estimate=pl.CostEstimate(flops=flops, bytes_accessed=flops // 1000, transcendentals=0),
+    )(*args, *kept)
+
+
+def ring_pairs(axis, far):
     count = lax.axis_size(axis)
     assert count % 2 == 0
-    pairs = [(i, (i + (1 if (i % 2 == 0) != far else -1)) % count) for i in range(count)]
-    return lax.ppermute(value, axis, pairs)
+    return [(i, (i + (1 if (i % 2 == 0) != far else -1)) % count) for i in range(count)]
+
+
+def swap(value, axis, far):
+    return lax.ppermute(value, axis, ring_pairs(axis, far))
+
+
+def both(value, axis):
+    pairs = [[i, i + 1] for i in range(0, lax.axis_size(axis), 2)]
+    return lax.all_gather(value, axis, axis_index_groups=pairs, axis=0, tiled=True)
+
+
+def send(value, axis, far, even):
+    return lax.ppermute(value, axis, [p for p in ring_pairs(axis, far) if (p[0] % 2 == 0) == even])
 
 
 def per_device(source, gauge_links, clover_even, clover_odd_inv):
@@ -412,34 +442,47 @@
         pltpu.SemaphoreType.DMA((RHS + 1,)),
     ]
     t_far, t_near, kept_t = call(start_kernel, held, T_HALOS + KEPT, 1_500_000, start_scratch, in_space=pltpu.HBM)
+    first = True
+    sent = {}
+    for who in (first, not first):
+        sent[who] = send(t_far, "ta", True, who), send(t_near, "ta", False, who)
     for hop in range(4):
         parity = hop % 2
-        t_far, t_near = swap(t_far, "ta", True), swap(t_near, "ta", False)
         x_far, x_near, kept_x = call(
-            functools.partial(send_x_kernel, parity), (f, links), X_HALOS + KEPT, 1_500_000
+            functools.partial(send_x_kernel, parity), (f, links), X_HALOS + KEPT, 10_000_000_000
         )
-        x_far, x_near = swap(x_far, "gx", True), swap(x_near, "gx", False)
+        x_far, x_near = swap(x_far, "gx", True), both(x_near, "gx")
         base = (before, even) if parity else ()
         acc, = call(
             functools.partial(interior_kernel, parity, bool(parity)),
-            (f, links, kept_t, kept_x, *base), FIELD, 8_000_000 if parity else 5_000_000,
+            (f, links, kept_t, kept_x, *base), FIELD, 1_000,
         )
-        acc, = call(functools.partial(join_x_kernel, parity), (links, acc, x_far, x_near), FIELD, 1_000_000)
+        acc, = call(functools.partial(join_x_kernel, parity), (links, acc, x_far, x_near), FIELD, 1_000)
         before = f
-        if parity == 0:
-            f, t_far, t_near, kept_t = call(
-                odd_kernel, (links, odd, acc, t_far, t_near), FIELD + T_HALOS + KEPT, 4_000_000,
-                [pltpu.VMEM((ROWS, 128), F32)],
-            )
-        elif hop == 1:
-            f, t_far, t_near, kept_t = call(
-                even_kernel, (links, acc, t_far, t_near), FIELD + T_HALOS + KEPT, 2_000_000
-            )
-        else:
-            out, = call(
-                last_kernel, (links, acc, t_far, t_near), [((ROWS, 128), BF16)], 1_000_000,
-                [pltpu.VMEM((ROWS, 128), BF16), pltpu.SemaphoreType.DMA((RHS,))], out_space=pltpu.HBM,
-            )
+        first = not first
+        arrived, sent, held = sent, {}, ()
+        for who in (first, not first):
+            halos = arrived[not who]
+            if hop == 3:
+                held = call(
+                    functools.partial(last_kernel, who), (links, acc, *halos), [((ROWS, 128), BF16)], 1_000_000,
+                    [pltpu.VMEM((ROWS, 128), BF16), pltpu.SemaphoreType.DMA((RHS,))], out_space=pltpu.HBM, kept=held,
+                )
+                continue
+            if parity == 0:
+                *held, t_far, t_near = call(
+                    functools.partial(odd_kernel, who), (links, odd, acc, *halos), FIELD + KEPT + T_HALOS, 10_000_000_000,
+                    [pltpu.VMEM((ROWS, 128), F32)], kept=held,
+                )
+            else:
+                *held, t_far, t_near = call(
+                    functools.partial(even_kernel, who), (links, acc, *halos), FIELD + KEPT + T_HALOS, 10_000_000_000,
+                    kept=held,
+                )
+            sent[who] = send(t_far, "ta", True, who), send(t_near, "ta", False, who)
+        if hop < 3:
+            f, kept_t = held
+    out, = held
     return out.reshape(shape)
 
 

time: 32 us -> 58.3 us (1.82)
  starting transfers between devices: 18 us -> 35.9 us
  blocking collectives: 0 us -> 8.25 us
  waiting for transfers between devices: 6.45 us -> 5.14 us
  local copies, waits for them, and re-layouts: 0.02 us -> 0.86 us
    ppermute x16 -> x20, starting transfers between devices: 18 us -> 35.9 us  [the longest x16 33.2 us: send(): lax.ppermute(value, axis, [p for p in ring_pairs(axis, far) if (p[0] % 2...]
    all_gather x0 -> x4, blocking collectives: none -> 8.25 us  [both(): lax.all_gather(value, axis, axis_index_groups=pairs, axis=0, tiled=True)]
    ppermute x16 -> x20, waiting for transfers between devices: 6.45 us -> 5.14 us  [the longest x16 4.78 us: send(): lax.ppermute(value, axis, [p for p in ring_pairs(axis, far) if (p[0] % 2...]
    unnamed x8, local copies, waits for them, and re-layouts: 0.02 us -> 0.86 us
    pallas_call x17 -> x21, Pallas kernels: 7.24 us -> 7.36 us  [call(): pl.pallas_call(kernel, out_shape=tuple((jax.ShapeDtypeStruct(shape, dtype...]
  transfers between devices with their start and end apart: 16 -> 20, of which waited for: 9 -> 4; matrix products, arithmetic and copies ran while one was open for 0% -> 0% of each run, Pallas kernels for 13% -> 10%
where the time goes in v3:
time: 58.3 us; the launch traced here: 57.8 us
  starting transfers between devices  35.9 us (62%)
  blocking collectives  8.25 us (14%)
  Pallas kernels  7.36 us (13%)
  waiting for transfers between devices  5.14 us (9%)
  local copies, waits for them, and re-layouts  0.86 us (1%)
    ppermute x16, starting transfers between devices, send(): lax.ppermute(value, axis, [p for p in ring_pairs(axis, far) if (p[0] % 2...  33.2 us
    all_gather x4, blocking collectives, both(): lax.all_gather(value, axis, axis_index_groups=pairs, axis=0, tiled=True)  8.25 us
    pallas_call x21, Pallas kernels, call(): pl.pallas_call(kernel, out_shape=tuple((jax.ShapeDtypeStruct(shape, dtype...  7.36 us
    ppermute x16, waiting for transfers between devices, send(): lax.ppermute(value, axis, [p for p in ring_pairs(axis, far) if (p[0] % 2...  4.78 us
    ppermute x4, starting transfers between devices, swap(): return lax.ppermute(value, axis, ring_pairs(axis, far))  2.68 us
  transfers between devices with their start and end apart: 20, of which 4 were waited for; matrix products, arithmetic and copies ran while one was open for 0% of the time, Pallas kernels for 10%

profile of v3, /device:TPU:0, one launch (start us, length us, event | category | flops | bytes accessed | tf_op | source)
XLA Modules:
  0.0 57.8 jit_solution(5528340403363337258)
XLA Ops:
  0.0 1.1 %shard_map.46 = (bf16[192,128]{1,0:T(8,128)(2,1)S(1)}, bf16[192,128]{1,0:T(8,128)(2,1)S(1)}, f32[384,128]{1,0:T(8,128)S(1)}) custom-call(bf16[768,128]{1,0:T(8,128)(2,1)} %bitcast.26, bf16[1152,128]{1,0:T(8,128)(2,1)} %bitcast.5), custom_call_target="tpu_custom_call" | custom-call | flops 1500000 | bytes 1500 | tf_op jit(solution)/shard_map/pallas_call | solution.py:401
  1.2 7.0 %collective-permute-start.3 = (bf16[192,128]{1,0:T(8,128)(2,1)S(1)}, bf16[192,128]{1,0:T(8,128)(2,1)S(1)}, u32[]{:S(2)}, u32[]{:S(2)}) collective-permute-start(bf16[192,128]{1,0:T(8,128)(2,1)S(1)} %get-tuple-element.48), channel_id=1, source_target_pairs={{0,12},{8,4},{1,13},{9,5},{2,14},{10,6},{3,15},{11,7},{16,28},{24,... | collective-permute-start | bytes 147464 | tf_op jit(solution)/shard_map/ppermute | solution.py:429
  8.1 1.3 %collective-permute-start.4 = (bf16[192,128]{1,0:T(8,128)(2,1)S(1)}, bf16[192,128]{1,0:T(8,128)(2,1)S(1)}, u32[]{:S(2)}, u32[]{:S(2)}) collective-permute-start(bf16[192,128]{1,0:T(8,128)(2,1)S(1)} %get-tuple-element.49), channel_id=1, source_target_pairs={{0,4},{8,12},{1,5},{9,13},{2,6},{10,14},{3,7},{11,15},{16,20},{24,... | collective-permute-start | bytes 147464 | tf_op jit(solution)/shard_map/ppermute | solution.py:429
  9.4 0.1 shard_map.47
  9.6 0.7 %collective-permute-start = (bf16[96,128]{1,0:T(8,128)(2,1)S(1)}, bf16[96,128]{1,0:T(8,128)(2,1)S(1)}, u32[]{:S(2)}, u32[]{:S(2)}) collective-permute-start(bf16[96,128]{1,0:T(8,128)(2,1)S(1)} %get-tuple-element.46), channel_id=1, source_target_pairs={{0,3},{1,2},{2,1},{3,0},{4,7},{5,6},{6,5},{7,4},{8,11},{9,10},{10,... | collective-permute-start | bytes 73736 | tf_op jit(solution)/shard_map/ppermute | solution.py:420
  10.3 1.3 %collective-permute-start.1 = (bf16[192,128]{1,0:T(8,128)(2,1)S(1)}, bf16[192,128]{1,0:T(8,128)(2,1)S(1)}, u32[]{:S(2)}, u32[]{:S(2)}) collective-permute-start(bf16[192,128]{1,0:T(8,128)(2,1)S(1)} %get-tuple-element.48), channel_id=1, source_target_pairs={{4,8},{12,0},{5,9},{13,1},{6,10},{14,2},{7,11},{15,3},{20,24},{28,... | collective-permute-start | bytes 147464 | tf_op jit(solution)/shard_map/ppermute | solution.py:429
  11.6 1.3 %collective-permute-start.2 = (bf16[192,128]{1,0:T(8,128)(2,1)S(1)}, bf16[192,128]{1,0:T(8,128)(2,1)S(1)}, u32[]{:S(2)}, u32[]{:S(2)}) collective-permute-start(bf16[192,128]{1,0:T(8,128)(2,1)S(1)} %get-tuple-element.49), channel_id=1, source_target_pairs={{4,0},{12,8},{5,1},{13,9},{6,2},{14,10},{7,3},{15,11},{20,16},{28,... | collective-permute-start | bytes 147464 | tf_op jit(solution)/shard_map/ppermute | solution.py:429
  12.9 0.7 %shard_map.48.acc_ref = f32[768,128]{1,0:T(8,128)S(1)} custom-call(bf16[768,128]{1,0:T(8,128)(2,1)S(1)} %bitcast.28, bf16[1152,128]{1,0:T(8,128)(2,1)S(1)} %bitcast.7, f32[384,128]{1,0:T(8,128)S(1)} %get-tuple-element.44.refs_2_, f32[384,128]{1,0:T(8,128)S(1)} %get-tuple-element.45.refs_3_), custom_call_target="tpu_custom_call" | custom-call | flops 1000 | bytes 1 | tf_op jit(solution)/shard_map/pallas_call | solution.py:401
  13.6 2.5 %all_gather.12.x_near = bf16[192,128]{1,0:T(8,128)(2,1)S(1)} all-gather(bf16[96,128]{1,0:T(8,128)(2,1)S(1)} %get-tuple-element.47), channel_id=1, replica_groups={{0,1},{2,3},{4,5},{6,7},{8,9},{10,11},{12,13},{14,15},{16,17},{18,19},{..., dimensions={0}, use_global_device_ids=true | all-gather | bytes 73728 | tf_op jit(solution)/shard_map/all_gather | solution.py:425
  16.0 0.1 shard_map.49.acc_ref
  16.2 0.8 %copy-done.3 = bf16[2,6,6,2,2,4,128]{6,5,4,3,2,1,0:T(4,128)(2,1)S(1)} copy-done((bf16[2,6,6,2,2,4,128]{6,5,4,3,2,1,0:T(4,128)(2,1)S(1)}, bf16[2,6,6,2,2,4,128]{6,5,4,3,2,1,0:T(4,128)(2,1)}, u32[]{:S(2)}) %copy-start.3) | copy-done | bytes 294936
  17.0 1.3 %collective-permute-start.8 = (bf16[192,128]{1,0:T(8,128)(2,1)S(1)}, bf16[192,128]{1,0:T(8,128)(2,1)S(1)}, u32[]{:S(2)}, u32[]{:S(2)}) collective-permute-start(bf16[192,128]{1,0:T(8,128)(2,1)S(1)} %get-tuple-element.59), channel_id=1, source_target_pairs={{4,8},{12,0},{5,9},{13,1},{6,10},{14,2},{7,11},{15,3},{20,24},{28,... | collective-permute-start | bytes 147464 | tf_op jit(solution)/shard_map/ppermute | solution.py:429
  18.3 1.3 %collective-permute-start.9 = (bf16[192,128]{1,0:T(8,128)(2,1)S(1)}, bf16[192,128]{1,0:T(8,128)(2,1)S(1)}, u32[]{:S(2)}, u32[]{:S(2)}) collective-permute-start(bf16[192,128]{1,0:T(8,128)(2,1)S(1)} %get-tuple-element.60), channel_id=1, source_target_pairs={{4,0},{12,8},{5,1},{13,9},{6,2},{14,10},{7,3},{15,11},{20,16},{28,... | collective-permute-start | bytes 147464 | tf_op jit(solution)/shard_map/ppermute | solution.py:429
  19.6 0.5 shard_map.51
  20.1 0.0 copy-start.2
  20.2 0.1 shard_map.52
  20.3 0.5 collective-permute-start.5
  20.8 6.1 %collective-permute-start.6 = (bf16[192,128]{1,0:T(8,128)(2,1)S(1)}, bf16[192,128]{1,0:T(8,128)(2,1)S(1)}, u32[]{:S(2)}, u32[]{:S(2)}) collective-permute-start(bf16[192,128]{1,0:T(8,128)(2,1)S(1)} %get-tuple-element.57), channel_id=1, source_target_pairs={{0,12},{8,4},{1,13},{9,5},{2,14},{10,6},{3,15},{11,7},{16,28},{24,... | collective-permute-start | bytes 147464 | tf_op jit(solution)/shard_map/ppermute | solution.py:429
  26.9 1.3 %collective-permute-start.7 = (bf16[192,128]{1,0:T(8,128)(2,1)S(1)}, bf16[192,128]{1,0:T(8,128)(2,1)S(1)}, u32[]{:S(2)}, u32[]{:S(2)}) collective-permute-start(bf16[192,128]{1,0:T(8,128)(2,1)S(1)} %get-tuple-element.58), channel_id=1, source_target_pairs={{0,4},{8,12},{1,5},{9,13},{2,6},{10,14},{3,7},{11,15},{16,20},{24,... | collective-permute-start | bytes 147464 | tf_op jit(solution)/shard_map/ppermute | solution.py:429
  28.2 1.0 %shard_map.53.acc_ref = f32[768,128]{1,0:T(8,128)S(1)} custom-call(f32[768,128]{1,0:T(8,128)S(1)} %get-tuple-element.52.f_ref.refs_0_, bf16[1152,128]{1,0:T(8,128)(2,1)S(1)} %bitcast.12, f32[384,128]{1,0:T(8,128)S(1)} %get-tuple-element.53.refs_2_, f32[384,128]{1,0:T(8,128)S(1)} %get-tuple-element.54.refs_3_, bf16[768,128]{1,0:T(8,128)(2,1)S(1)} %bitcast.29, ...), custom_call_target="tpu_custom_call" | custom-call | flops 1000 | bytes 1 | tf_op jit(solution)/shard_map/pallas_call | solution.py:401
  29.2 1.8 %all_gather.13.x_near = bf16[192,128]{1,0:T(8,128)(2,1)S(1)} all-gather(bf16[96,128]{1,0:T(8,128)(2,1)S(1)} %get-tuple-element.56), channel_id=1, replica_groups={{0,1},{2,3},{4,5},{6,7},{8,9},{10,11},{12,13},{14,15},{16,17},{18,19},{..., dimensions={0}, use_global_device_ids=true | all-gather | bytes 73728 | tf_op jit(solution)/shard_map/all_gather | solution.py:425
  31.0 0.1 shard_map.54.acc_ref
  31.2 0.2 shard_map.55
  31.4 1.3 %collective-permute-start.13 = (bf16[192,128]{1,0:T(8,128)(2,1)S(1)}, bf16[192,128]{1,0:T(8,128)(2,1)S(1)}, u32[]{:S(2)}, u32[]{:S(2)}) collective-permute-start(bf16[192,128]{1,0:T(8,128)(2,1)S(1)} %get-tuple-element.70), channel_id=1, source_target_pairs={{0,12},{8,4},{1,13},{9,5},{2,14},{10,6},{3,15},{11,7},{16,28},{24,... | collective-permute-start | bytes 147464 | tf_op jit(solution)/shard_map/ppermute | solution.py:429
  32.7 1.3 %collective-permute-start.14 = (bf16[192,128]{1,0:T(8,128)(2,1)S(1)}, bf16[192,128]{1,0:T(8,128)(2,1)S(1)}, u32[]{:S(2)}, u32[]{:S(2)}) collective-permute-start(bf16[192,128]{1,0:T(8,128)(2,1)S(1)} %get-tuple-element.71), channel_id=1, source_target_pairs={{0,4},{8,12},{1,5},{9,13},{2,6},{10,14},{3,7},{11,15},{16,20},{24,... | collective-permute-start | bytes 147464 | tf_op jit(solution)/shard_map/ppermute | solution.py:429
  34.0 0.1 shard_map.57
  34.2 1.3 %collective-permute-start.10 = (bf16[96,128]{1,0:T(8,128)(2,1)S(1)}, bf16[96,128]{1,0:T(8,128)(2,1)S(1)}, u32[]{:S(2)}, u32[]{:S(2)}) collective-permute-start(bf16[96,128]{1,0:T(8,128)(2,1)S(1)} %get-tuple-element.66), channel_id=1, source_target_pairs={{0,3},{1,2},{2,1},{3,0},{4,7},{5,6},{6,5},{7,4},{8,11},{9,10},{10,... | collective-permute-start | bytes 73736 | tf_op jit(solution)/shard_map/ppermute | solution.py:420
  35.5 1.3 %collective-permute-start.11 = (bf16[192,128]{1,0:T(8,128)(2,1)S(1)}, bf16[192,128]{1,0:T(8,128)(2,1)S(1)}, u32[]{:S(2)}, u32[]{:S(2)}) collective-permute-start(bf16[192,128]{1,0:T(8,128)(2,1)S(1)} %get-tuple-element.68), channel_id=1, source_target_pairs={{4,8},{12,0},{5,9},{13,1},{6,10},{14,2},{7,11},{15,3},{20,24},{28,... | collective-permute-start | bytes 147464 | tf_op jit(solution)/shard_map/ppermute | solution.py:429
  36.8 1.3 %collective-permute-start.12 = (bf16[192,128]{1,0:T(8,128)(2,1)S(1)}, bf16[192,128]{1,0:T(8,128)(2,1)S(1)}, u32[]{:S(2)}, u32[]{:S(2)}) collective-permute-start(bf16[192,128]{1,0:T(8,128)(2,1)S(1)} %get-tuple-element.69), channel_id=1, source_target_pairs={{4,0},{12,8},{5,1},{13,9},{6,2},{14,10},{7,3},{15,11},{20,16},{28,... | collective-permute-start | bytes 147464 | tf_op jit(solution)/shard_map/ppermute | solution.py:429
  38.1 0.7 %shard_map.58.acc_ref = f32[768,128]{1,0:T(8,128)S(1)} custom-call(f32[768,128]{1,0:T(8,128)S(1)} %get-tuple-element.63.f_ref.refs_0_.refs_4_, bf16[1152,128]{1,0:T(8,128)(2,1)S(1)} %bitcast.17, f32[384,128]{1,0:T(8,128)S(1)} %get-tuple-element.64.refs_2_, f32[384,128]{1,0:T(8,128)S(1)} %get-tuple-element.65.refs_3_), custom_call_target="tpu_custom_call" | custom-call | flops 1000 | bytes 1 | tf_op jit(solution)/shard_map/pallas_call | solution.py:401
  38.7 1.8 %all_gather.14.x_near = bf16[192,128]{1,0:T(8,128)(2,1)S(1)} all-gather(bf16[96,128]{1,0:T(8,128)(2,1)S(1)} %get-tuple-element.67), channel_id=1, replica_groups={{0,1},{2,3},{4,5},{6,7},{8,9},{10,11},{12,13},{14,15},{16,17},{18,19},{..., dimensions={0}, use_global_device_ids=true | all-gather | bytes 73728 | tf_op jit(solution)/shard_map/all_gather | solution.py:425
  40.6 0.1 shard_map.59.acc_ref
  40.7 2.6 %collective-permute-done.11.t_far = bf16[192,128]{1,0:T(8,128)(2,1)S(1)} collective-permute-done((bf16[192,128]{1,0:T(8,128)(2,1)S(1)}, bf16[192,128]{1,0:T(8,128)(2,1)S(1)}, u32[]{:S(2)}, u32[]{:S(2)}) %collective-permute-start.11) | collective-permute-done | bytes 49184 | tf_op jit(solution)/shard_map/ppermute | solution.py:429
  43.3 0.4 collective-permute-done.12.t_near
  43.7 0.5 shard_map.61
  44.2 3.4 %collective-permute-start.16 = (bf16[192,128]{1,0:T(8,128)(2,1)S(1)}, bf16[192,128]{1,0:T(8,128)(2,1)S(1)}, u32[]{:S(2)}, u32[]{:S(2)}) collective-permute-start(bf16[192,128]{1,0:T(8,128)(2,1)S(1)} %get-tuple-element.79), channel_id=1, source_target_pairs={{0,12},{8,4},{1,13},{9,5},{2,14},{10,6},{3,15},{11,7},{16,28},{24,... | collective-permute-start | bytes 147464 | tf_op jit(solution)/shard_map/ppermute | solution.py:429
  47.6 1.3 %collective-permute-start.17 = (bf16[192,128]{1,0:T(8,128)(2,1)S(1)}, bf16[192,128]{1,0:T(8,128)(2,1)S(1)}, u32[]{:S(2)}, u32[]{:S(2)}) collective-permute-start(bf16[192,128]{1,0:T(8,128)(2,1)S(1)} %get-tuple-element.80), channel_id=1, source_target_pairs={{0,4},{8,12},{1,5},{9,13},{2,6},{10,14},{3,7},{11,15},{16,20},{24,... | collective-permute-start | bytes 147464 | tf_op jit(solution)/shard_map/ppermute | solution.py:429
  48.9 1.3 %collective-permute-start.18 = (bf16[192,128]{1,0:T(8,128)(2,1)S(1)}, bf16[192,128]{1,0:T(8,128)(2,1)S(1)}, u32[]{:S(2)}, u32[]{:S(2)}) collective-permute-start(bf16[192,128]{1,0:T(8,128)(2,1)S(1)} %get-tuple-element.81), channel_id=1, source_target_pairs={{4,8},{12,0},{5,9},{13,1},{6,10},{14,2},{7,11},{15,3},{20,24},{28,... | collective-permute-start | bytes 147464 | tf_op jit(solution)/shard_map/ppermute | solution.py:429
  50.2 1.3 %collective-permute-start.19 = (bf16[192,128]{1,0:T(8,128)(2,1)S(1)}, bf16[192,128]{1,0:T(8,128)(2,1)S(1)}, u32[]{:S(2)}, u32[]{:S(2)}) collective-permute-start(bf16[192,128]{1,0:T(8,128)(2,1)S(1)} %get-tuple-element.82), channel_id=1, source_target_pairs={{4,0},{12,8},{5,1},{13,9},{6,2},{14,10},{7,3},{15,11},{20,16},{28,... | collective-permute-start | bytes 147464 | tf_op jit(solution)/shard_map/ppermute | solution.py:429
  51.5 0.1 shard_map.62
  51.6 0.1 collective-permute-start.15
  51.7 1.0 %shard_map.63.acc_ref = f32[768,128]{1,0:T(8,128)S(1)} custom-call(f32[768,128]{1,0:T(8,128)S(1)} %get-tuple-element.74.f_ref.refs_0_, bf16[1152,128]{1,0:T(8,128)(2,1)S(1)} %bitcast.22, f32[384,128]{1,0:T(8,128)S(1)} %get-tuple-element.75.refs_2_, f32[384,128]{1,0:T(8,128)S(1)} %get-tuple-element.76.refs_3_, ...), custom_call_target="tpu_custom_call" | custom-call | flops 1000 | bytes 1 | tf_op jit(solution)/shard_map/pallas_call | solution.py:401
  52.7 2.1 %all_gather.15.x_near = bf16[192,128]{1,0:T(8,128)(2,1)S(1)} all-gather(bf16[96,128]{1,0:T(8,128)(2,1)S(1)} %get-tuple-element.78), channel_id=1, replica_groups={{0,1},{2,3},{4,5},{6,7},{8,9},{10,11},{12,13},{14,15},{16,17},{18,19},{..., dimensions={0}, use_global_device_ids=true | all-gather | bytes 73728 | tf_op jit(solution)/shard_map/all_gather | solution.py:425
  54.8 0.3 collective-permute-done.15.x_far
  55.2 0.1 shard_map.64.acc_ref
  55.3 1.8 %collective-permute-done.18.t_far = bf16[192,128]{1,0:T(8,128)(2,1)S(1)} collective-permute-done((bf16[192,128]{1,0:T(8,128)(2,1)S(1)}, bf16[192,128]{1,0:T(8,128)(2,1)S(1)}, u32[]{:S(2)}, u32[]{:S(2)}) %collective-permute-start.18) | collective-permute-done | bytes 49184 | tf_op jit(solution)/shard_map/ppermute | solution.py:429
  57.0 0.7 %shard_map.65.refs_0_ = bf16[768,128]{1,0:T(8,128)(2,1)} custom-call(bf16[1152,128]{1,0:T(8,128)(2,1)S(1)} %bitcast.24, f32[768,128]{1,0:T(8,128)S(1)} %shard_map.64.acc_ref, bf16[192,128]{1,0:T(8,128)(2,1)S(1)} %collective-permute-done.18.t_far, bf16[192,128]{1,0:T(8,128)(2,1)S(1)} %collective-permute-done.19.t_near), custom_call_target="tpu_custom_call" | custom-call | flops 1000000 | bytes 1000 | tf_op jit(solution)/shard_map/pallas_call | solution.py:401
  57.8 0.1 shard_map.66
  (25 shorter events, 0.1 us)
Async XLA Ops:
  0.0 9.4 %copy-start = (bf16[4,3,3,2,2,2,4,128]{7,6,5,4,3,2,1,0:T(4,128)(2,1)S(1)}, bf16[4,3,3,2,2,2,4,128]{7,6,5,4,3,2,1,0:T(4,128)(2,1)}, u32[]{:S(2)}) copy-start(bf16[4,3,3,2,2,2,4,128]{7,6,5,4,3,2,1,0:T(4,128)(2,1)} %param.5) | copy-start | bytes 884740
  0.0 9.4 %copy-start.1 = (bf16[4,4,3,2,2,4,128]{6,5,4,3,2,1,0:T(4,128)(2,1)S(1)}, bf16[4,4,3,2,2,4,128]{6,5,4,3,2,1,0:T(4,128)(2,1)}, u32[]{:S(2)}) copy-start(bf16[4,4,3,2,2,4,128]{6,5,4,3,2,1,0:T(4,128)(2,1)} %param.4) | copy-start | bytes 589828
  1.2 15.0 %collective-permute-start.3 = (bf16[192,128]{1,0:T(8,128)(2,1)S(1)}, bf16[192,128]{1,0:T(8,128)(2,1)S(1)}, u32[]{:S(2)}, u32[]{:S(2)}) collective-permute-start(bf16[192,128]{1,0:T(8,128)(2,1)S(1)} %get-tuple-element.48), channel_id=1, source_target_pairs={{0,12},{8,4},{1,13},{9,5},{2,14},{10,6},{3,15},{11,7},{16,28},{24,... | collective-permute-start | bytes 147464 | tf_op jit(solution)/shard_map/ppermute | solution.py:429
  8.1 8.0 %collective-permute-start.4 = (bf16[192,128]{1,0:T(8,128)(2,1)S(1)}, bf16[192,128]{1,0:T(8,128)(2,1)S(1)}, u32[]{:S(2)}, u32[]{:S(2)}) collective-permute-start(bf16[192,128]{1,0:T(8,128)(2,1)S(1)} %get-tuple-element.49), channel_id=1, source_target_pairs={{0,4},{8,12},{1,5},{9,13},{2,6},{10,14},{3,7},{11,15},{16,20},{24,... | collective-permute-start | bytes 147464 | tf_op jit(solution)/shard_map/ppermute | solution.py:429
  9.6 6.4 %collective-permute-start = (bf16[96,128]{1,0:T(8,128)(2,1)S(1)}, bf16[96,128]{1,0:T(8,128)(2,1)S(1)}, u32[]{:S(2)}, u32[]{:S(2)}) collective-permute-start(bf16[96,128]{1,0:T(8,128)(2,1)S(1)} %get-tuple-element.46), channel_id=1, source_target_pairs={{0,3},{1,2},{2,1},{3,0},{4,7},{5,6},{6,5},{7,4},{8,11},{9,10},{10,... | collective-permute-start | bytes 73736 | tf_op jit(solution)/shard_map/ppermute | solution.py:420
  10.3 9.3 %collective-permute-start.1 = (bf16[192,128]{1,0:T(8,128)(2,1)S(1)}, bf16[192,128]{1,0:T(8,128)(2,1)S(1)}, u32[]{:S(2)}, u32[]{:S(2)}) collective-permute-start(bf16[192,128]{1,0:T(8,128)(2,1)S(1)} %get-tuple-element.48), channel_id=1, source_target_pairs={{4,8},{12,0},{5,9},{13,1},{6,10},{14,2},{7,11},{15,3},{20,24},{28,... | collective-permute-start | bytes 147464 | tf_op jit(solution)/shard_map/ppermute | solution.py:429
  11.6 8.0 %collective-permute-start.2 = (bf16[192,128]{1,0:T(8,128)(2,1)S(1)}, bf16[192,128]{1,0:T(8,128)(2,1)S(1)}, u32[]{:S(2)}, u32[]{:S(2)}) collective-permute-start(bf16[192,128]{1,0:T(8,128)(2,1)S(1)} %get-tuple-element.49), channel_id=1, source_target_pairs={{4,0},{12,8},{5,1},{13,9},{6,2},{14,10},{7,3},{15,11},{20,16},{28,... | collective-permute-start | bytes 147464 | tf_op jit(solution)/shard_map/ppermute | solution.py:429
  16.0 1.0 %copy-start.3 = (bf16[2,6,6,2,2,4,128]{6,5,4,3,2,1,0:T(4,128)(2,1)S(1)}, bf16[2,6,6,2,2,4,128]{6,5,4,3,2,1,0:T(4,128)(2,1)}, u32[]{:S(2)}) copy-start(bf16[2,6,6,2,2,4,128]{6,5,4,3,2,1,0:T(4,128)(2,1)} %param.7) | copy-start | bytes 884740
  17.0 14.1 %collective-permute-start.8 = (bf16[192,128]{1,0:T(8,128)(2,1)S(1)}, bf16[192,128]{1,0:T(8,128)(2,1)S(1)}, u32[]{:S(2)}, u32[]{:S(2)}) collective-permute-start(bf16[192,128]{1,0:T(8,128)(2,1)S(1)} %get-tuple-element.59), channel_id=1, source_target_pairs={{4,8},{12,0},{5,9},{13,1},{6,10},{14,2},{7,11},{15,3},{20,24},{28,... | collective-permute-start | bytes 147464 | tf_op jit(solution)/shard_map/ppermute | solution.py:429
  18.3 12.9 %collective-permute-start.9 = (bf16[192,128]{1,0:T(8,128)(2,1)S(1)}, bf16[192,128]{1,0:T(8,128)(2,1)S(1)}, u32[]{:S(2)}, u32[]{:S(2)}) collective-permute-start(bf16[192,128]{1,0:T(8,128)(2,1)S(1)} %get-tuple-element.60), channel_id=1, source_target_pairs={{4,0},{12,8},{5,1},{13,9},{6,2},{14,10},{7,3},{15,11},{20,16},{28,... | collective-permute-start | bytes 147464 | tf_op jit(solution)/shard_map/ppermute | solution.py:429
  20.1 8.1 %copy-start.2 = (bf16[2,6,6,2,2,4,128]{6,5,4,3,2,1,0:T(4,128)(2,1)S(1)}, bf16[2,6,6,2,2,4,128]{6,5,4,3,2,1,0:T(4,128)(2,1)}, u32[]{:S(2)}) copy-start(bf16[2,6,6,2,2,4,128]{6,5,4,3,2,1,0:T(4,128)(2,1)} %param.6) | copy-start | bytes 884740
  20.3 10.8 %collective-permute-start.5 = (bf16[96,128]{1,0:T(8,128)(2,1)S(1)}, bf16[96,128]{1,0:T(8,128)(2,1)S(1)}, u32[]{:S(2)}, u32[]{:S(2)}) collective-permute-start(bf16[96,128]{1,0:T(8,128)(2,1)S(1)} %get-tuple-element.55), channel_id=1, source_target_pairs={{0,3},{1,2},{2,1},{3,0},{4,7},{5,6},{6,5},{7,4},{8,11},{9,10},{10,... | collective-permute-start | bytes 73736 | tf_op jit(solution)/shard_map/ppermute | solution.py:420
  20.8 13.1 %collective-permute-start.6 = (bf16[192,128]{1,0:T(8,128)(2,1)S(1)}, bf16[192,128]{1,0:T(8,128)(2,1)S(1)}, u32[]{:S(2)}, u32[]{:S(2)}) collective-permute-start(bf16[192,128]{1,0:T(8,128)(2,1)S(1)} %get-tuple-element.57), channel_id=1, source_target_pairs={{0,12},{8,4},{1,13},{9,5},{2,14},{10,6},{3,15},{11,7},{16,28},{24,... | collective-permute-start | bytes 147464 | tf_op jit(solution)/shard_map/ppermute | solution.py:429
  26.9 7.1 %collective-permute-start.7 = (bf16[192,128]{1,0:T(8,128)(2,1)S(1)}, bf16[192,128]{1,0:T(8,128)(2,1)S(1)}, u32[]{:S(2)}, u32[]{:S(2)}) collective-permute-start(bf16[192,128]{1,0:T(8,128)(2,1)S(1)} %get-tuple-element.58), channel_id=1, source_target_pairs={{0,4},{8,12},{1,5},{9,13},{2,6},{10,14},{3,7},{11,15},{16,20},{24,... | collective-permute-start | bytes 147464 | tf_op jit(solution)/shard_map/ppermute | solution.py:429
  31.4 9.3 %collective-permute-start.13 = (bf16[192,128]{1,0:T(8,128)(2,1)S(1)}, bf16[192,128]{1,0:T(8,128)(2,1)S(1)}, u32[]{:S(2)}, u32[]{:S(2)}) collective-permute-start(bf16[192,128]{1,0:T(8,128)(2,1)S(1)} %get-tuple-element.70), channel_id=1, source_target_pairs={{0,12},{8,4},{1,13},{9,5},{2,14},{10,6},{3,15},{11,7},{16,28},{24,... | collective-permute-start | bytes 147464 | tf_op jit(solution)/shard_map/ppermute | solution.py:429
  32.7 8.0 %collective-permute-start.14 = (bf16[192,128]{1,0:T(8,128)(2,1)S(1)}, bf16[192,128]{1,0:T(8,128)(2,1)S(1)}, u32[]{:S(2)}, u32[]{:S(2)}) collective-permute-start(bf16[192,128]{1,0:T(8,128)(2,1)S(1)} %get-tuple-element.71), channel_id=1, source_target_pairs={{0,4},{8,12},{1,5},{9,13},{2,6},{10,14},{3,7},{11,15},{16,20},{24,... | collective-permute-start | bytes 147464 | tf_op jit(solution)/shard_map/ppermute | solution.py:429
  34.2 6.4 %collective-permute-start.10 = (bf16[96,128]{1,0:T(8,128)(2,1)S(1)}, bf16[96,128]{1,0:T(8,128)(2,1)S(1)}, u32[]{:S(2)}, u32[]{:S(2)}) collective-permute-start(bf16[96,128]{1,0:T(8,128)(2,1)S(1)} %get-tuple-element.66), channel_id=1, source_target_pairs={{0,3},{1,2},{2,1},{3,0},{4,7},{5,6},{6,5},{7,4},{8,11},{9,10},{10,... | collective-permute-start | bytes 73736 | tf_op jit(solution)/shard_map/ppermute | solution.py:420
  35.5 7.8 %collective-permute-start.11 = (bf16[192,128]{1,0:T(8,128)(2,1)S(1)}, bf16[192,128]{1,0:T(8,128)(2,1)S(1)}, u32[]{:S(2)}, u32[]{:S(2)}) collective-permute-start(bf16[192,128]{1,0:T(8,128)(2,1)S(1)} %get-tuple-element.68), channel_id=1, source_target_pairs={{4,8},{12,0},{5,9},{13,1},{6,10},{14,2},{7,11},{15,3},{20,24},{28,... | collective-permute-start | bytes 147464 | tf_op jit(solution)/shard_map/ppermute | solution.py:429
  36.8 6.9 %collective-permute-start.12 = (bf16[192,128]{1,0:T(8,128)(2,1)S(1)}, bf16[192,128]{1,0:T(8,128)(2,1)S(1)}, u32[]{:S(2)}, u32[]{:S(2)}) collective-permute-start(bf16[192,128]{1,0:T(8,128)(2,1)S(1)} %get-tuple-element.69), channel_id=1, source_target_pairs={{4,0},{12,8},{5,1},{13,9},{6,2},{14,10},{7,3},{15,11},{20,16},{28,... | collective-permute-start | bytes 147464 | tf_op jit(solution)/shard_map/ppermute | solution.py:429
  44.2 13.5 %collective-permute-start.16 = (bf16[192,128]{1,0:T(8,128)(2,1)S(1)}, bf16[192,128]{1,0:T(8,128)(2,1)S(1)}, u32[]{:S(2)}, u32[]{:S(2)}) collective-permute-start(bf16[192,128]{1,0:T(8,128)(2,1)S(1)} %get-tuple-element.79), channel_id=1, source_target_pairs={{0,12},{8,4},{1,13},{9,5},{2,14},{10,6},{3,15},{11,7},{16,28},{24,... | collective-permute-start | bytes 147464 | tf_op jit(solution)/shard_map/ppermute | solution.py:429
  47.6 10.2 %collective-permute-start.17 = (bf16[192,128]{1,0:T(8,128)(2,1)S(1)}, bf16[192,128]{1,0:T(8,128)(2,1)S(1)}, u32[]{:S(2)}, u32[]{:S(2)}) collective-permute-start(bf16[192,128]{1,0:T(8,128)(2,1)S(1)} %get-tuple-element.80), channel_id=1, source_target_pairs={{0,4},{8,12},{1,5},{9,13},{2,6},{10,14},{3,7},{11,15},{16,20},{24,... | collective-permute-start | bytes 147464 | tf_op jit(solution)/shard_map/ppermute | solution.py:429
  48.9 8.1 %collective-permute-start.18 = (bf16[192,128]{1,0:T(8,128)(2,1)S(1)}, bf16[192,128]{1,0:T(8,128)(2,1)S(1)}, u32[]{:S(2)}, u32[]{:S(2)}) collective-permute-start(bf16[192,128]{1,0:T(8,128)(2,1)S(1)} %get-tuple-element.81), channel_id=1, source_target_pairs={{4,8},{12,0},{5,9},{13,1},{6,10},{14,2},{7,11},{15,3},{20,24},{28,... | collective-permute-start | bytes 147464 | tf_op jit(solution)/shard_map/ppermute | solution.py:429
  50.2 6.8 %collective-permute-start.19 = (bf16[192,128]{1,0:T(8,128)(2,1)S(1)}, bf16[192,128]{1,0:T(8,128)(2,1)S(1)}, u32[]{:S(2)}, u32[]{:S(2)}) collective-permute-start(bf16[192,128]{1,0:T(8,128)(2,1)S(1)} %get-tuple-element.82), channel_id=1, source_target_pairs={{4,0},{12,8},{5,1},{13,9},{6,2},{14,10},{7,3},{15,11},{20,16},{28,... | collective-permute-start | bytes 147464 | tf_op jit(solution)/shard_map/ppermute | solution.py:429
  51.6 3.5 %collective-permute-start.15 = (bf16[96,128]{1,0:T(8,128)(2,1)S(1)}, bf16[96,128]{1,0:T(8,128)(2,1)S(1)}, u32[]{:S(2)}, u32[]{:S(2)}) collective-permute-start(bf16[96,128]{1,0:T(8,128)(2,1)S(1)} %get-tuple-element.77), channel_id=1, source_target_pairs={{0,3},{1,2},{2,1},{3,0},{4,7},{5,6},{6,5},{7,4},{8,11},{9,10},{10,... | collective-permute-start | bytes 73736 | tf_op jit(solution)/shard_map/ppermute | solution.py:420

commit v4 on v2

--- a/solution.py
+++ b/solution.py
@@ -124,7 +124,7 @@
     return jnp.where(mask, a, b)
 
 
-def send_t(f_ref, links_ref, parity, t_far, t_near, kept, ready=lambda r: None):
+def send_t(f_ref, links_ref, parity, t_near, t_far, kept, ready=lambda r: None):
     even = even_device("ta")
     t_idx, _ = site_masks()
     first = t_idx == 0
@@ -325,7 +325,7 @@
             store_field(out_ref, r, rebuild_signed(load_field(acc_ref, r), half, 1, sign))
 
 
-def join_t(links_ref, acc_ref, t_far, t_near, parity, out_ref, done=lambda r: None):
+def join_t(links_ref, acc_ref, t_near, t_far, parity, out_ref, done=lambda r: None):
     even = even_device("ta")
     t_idx, _ = site_masks()
     first = t_idx == 0
@@ -347,19 +347,19 @@
         done(r)
 
 
-def odd_kernel(links_ref, clover_ref, acc_ref, t_far, t_near, out_ref, *refs):
+def odd_kernel(links_ref, clover_ref, acc_ref, t_near, t_far, out_ref, *refs):
     outs, summed = refs[:3], refs[3]
-    join_t(links_ref, acc_ref, t_far, t_near, 0, summed)
+    join_t(links_ref, acc_ref, t_near, t_far, 0, summed)
     clover_to(clover_ref, lambda r: load_field(summed, r), out_ref, -KAPPA2)
     send_t(out_ref, links_ref, 1, *outs)
 
 
-def even_kernel(links_ref, acc_ref, t_far, t_near, out_ref, *outs):
-    join_t(links_ref, acc_ref, t_far, t_near, 1, out_ref)
+def even_kernel(links_ref, acc_ref, t_near, t_far, out_ref, *outs):
+    join_t(links_ref, acc_ref, t_near, t_far, 1, out_ref)
     send_t(out_ref, links_ref, 0, *outs)
 
 
-def last_kernel(links_ref, acc_ref, t_far, t_near, out_hbm, held, sems):
+def last_kernel(links_ref, acc_ref, t_near, t_far, out_hbm, held, sems):
     part = held.shape[0] // RHS
     copies = []
 
@@ -368,7 +368,7 @@
         copies.append(pltpu.make_async_copy(held.at[rows], out_hbm.at[rows], sems.at[r]))
         copies[-1].start()
 
-    join_t(links_ref, acc_ref, t_far, t_near, 1, held, done)
+    join_t(links_ref, acc_ref, t_near, t_far, 1, held, done)
     for copy in copies:
         copy.wait()
 
@@ -411,10 +411,10 @@
         pltpu.VMEM((links.shape[0] // 4, 128), BF16),
         pltpu.SemaphoreType.DMA((RHS + 1,)),
     ]
-    t_far, t_near, kept_t = call(start_kernel, held, T_HALOS + KEPT, 1_500_000, start_scratch, in_space=pltpu.HBM)
+    t_near, t_far, kept_t = call(start_kernel, held, T_HALOS + KEPT, 1_500_000, start_scratch, in_space=pltpu.HBM)
     for hop in range(4):
         parity = hop % 2
-        t_far, t_near = swap(t_far, "ta", True), swap(t_near, "ta", False)
+        t_near, t_far = swap(t_near, "ta", False), swap(t_far, "ta", True)
         x_far, x_near, kept_x = call(
             functools.partial(send_x_kernel, parity), (f, links), X_HALOS + KEPT, 1_500_000
         )
@@ -427,17 +427,17 @@
         acc, = call(functools.partial(join_x_kernel, parity), (links, acc, x_far, x_near), FIELD, 1_000_000)
         before = f
         if parity == 0:
-            f, t_far, t_near, kept_t = call(
-                odd_kernel, (links, odd, acc, t_far, t_near), FIELD + T_HALOS + KEPT, 4_000_000,
+            f, t_near, t_far, kept_t = call(
+                odd_kernel, (links, odd, acc, t_near, t_far), FIELD + T_HALOS + KEPT, 4_000_000,
                 [pltpu.VMEM((ROWS, 128), F32)],
             )
         elif hop == 1:
-            f, t_far, t_near, kept_t = call(
-                even_kernel, (links, acc, t_far, t_near), FIELD + T_HALOS + KEPT, 2_000_000
+            f, t_near, t_far, kept_t = call(
+                even_kernel, (links, acc, t_near, t_far), FIELD + T_HALOS + KEPT, 2_000_000
             )
         else:
             out, = call(
-                last_kernel, (links, acc, t_far, t_near), [((ROWS, 128), BF16)], 1_000_000,
+                last_kernel, (links, acc, t_near, t_far), [((ROWS, 128), BF16)], 1_000_000,
                 [pltpu.VMEM((ROWS, 128), BF16), pltpu.SemaphoreType.DMA((RHS,))], out_space=pltpu.HBM,
             )
     return out.reshape(shape)

time: 32 us -> 31.9 us (level)
  waiting for transfers between devices: 6.45 us -> 5.6 us
  starting transfers between devices: 18 us -> 18.7 us
    ppermute x16, waiting for transfers between devices: 6.45 us -> 5.6 us  [swap(): return lax.ppermute(value, axis, pairs)]
    ppermute x16, starting transfers between devices: 18 us -> 18.7 us  [swap(): return lax.ppermute(value, axis, pairs)]
  transfers between devices with their start and end apart: 16 -> 16, of which waited for: 9 -> 7; matrix products, arithmetic and copies ran while one was open for 0% -> 0% of each run, Pallas kernels for 13% -> 13%
where the time goes in v4:
time: 31.9 us; the launch traced here: 31.7 us
  starting transfers between devices  18.7 us (59%)
  Pallas kernels  7.25 us (23%)
  waiting for transfers between devices  5.6 us (18%)
    ppermute x16, starting transfers between devices, swap(): return lax.ppermute(value, axis, pairs)  18.7 us
    pallas_call x17, Pallas kernels, call(): pl.pallas_call(kernel, out_shape=tuple((jax.ShapeDtypeStruct(shape, dtype...  7.25 us
    ppermute x16, waiting for transfers between devices, swap(): return lax.ppermute(value, axis, pairs)  5.6 us
  transfers between devices with their start and end apart: 16, of which 7 were waited for; matrix products, arithmetic and copies ran while one was open for 0% of the time, Pallas kernels for 13%

profile of v4, /device:TPU:0, one launch (start us, length us, event | category | flops | bytes accessed | tf_op | source)
XLA Modules:
  0.0 31.7 jit_solution(11480028009549741521)
XLA Ops:
  0.0 1.1 %shard_map.46 = (bf16[192,128]{1,0:T(8,128)(2,1)S(1)}, bf16[192,128]{1,0:T(8,128)(2,1)S(1)}, f32[384,128]{1,0:T(8,128)S(1)}) custom-call(bf16[768,128]{1,0:T(8,128)(2,1)} %bitcast.22, bf16[1152,128]{1,0:T(8,128)(2,1)} %bitcast.5), custom_call_target="tpu_custom_call" | custom-call | flops 1500000 | bytes 2097152 | tf_op jit(solution)/shard_map/pallas_call | solution.py:384
  1.2 3.1 %collective-permute-start.2 = (bf16[192,128]{1,0:T(8,128)(2,1)S(1)}, bf16[192,128]{1,0:T(8,128)(2,1)S(1)}, u32[]{:S(2)}, u32[]{:S(2)}) collective-permute-start(bf16[192,128]{1,0:T(8,128)(2,1)S(1)} %get-tuple-element.36), channel_id=1, source_target_pairs={{0,4},{4,0},{8,12},{12,8},{1,5},{5,1},{9,13},{13,9},{2,6},{6,2},{1... | collective-permute-start | bytes 147464 | tf_op jit(solution)/shard_map/ppermute | solution.py:399
  4.2 2.5 %collective-permute-start.3 = (bf16[192,128]{1,0:T(8,128)(2,1)S(1)}, bf16[192,128]{1,0:T(8,128)(2,1)S(1)}, u32[]{:S(2)}, u32[]{:S(2)}) collective-permute-start(bf16[192,128]{1,0:T(8,128)(2,1)S(1)} %get-tuple-element.37), channel_id=1, source_target_pairs={{0,12},{4,8},{8,4},{12,0},{1,13},{5,9},{9,5},{13,1},{2,14},{6,10},... | collective-permute-start | bytes 147464 | tf_op jit(solution)/shard_map/ppermute | solution.py:399
  6.7 0.1 shard_map.47
  6.9 0.4 %collective-permute-start = (bf16[96,128]{1,0:T(8,128)(2,1)S(1)}, bf16[96,128]{1,0:T(8,128)(2,1)S(1)}, u32[]{:S(2)}, u32[]{:S(2)}) collective-permute-start(bf16[96,128]{1,0:T(8,128)(2,1)S(1)} %get-tuple-element.34), channel_id=1, source_target_pairs={{0,3},{1,2},{2,1},{3,0},{4,7},{5,6},{6,5},{7,4},{8,11},{9,10},{10,... | collective-permute-start | bytes 73736 | tf_op jit(solution)/shard_map/ppermute | solution.py:399
  7.3 1.2 %collective-permute-start.1 = (bf16[96,128]{1,0:T(8,128)(2,1)S(1)}, bf16[96,128]{1,0:T(8,128)(2,1)S(1)}, u32[]{:S(2)}, u32[]{:S(2)}) collective-permute-start(bf16[96,128]{1,0:T(8,128)(2,1)S(1)} %get-tuple-element.35), channel_id=1, source_target_pairs={{0,1},{1,0},{2,3},{3,2},{4,5},{5,4},{6,7},{7,6},{8,9},{9,8},{10,11... | collective-permute-start | bytes 73736 | tf_op jit(solution)/shard_map/ppermute | solution.py:399
  8.5 0.7 %shard_map.48.acc_ref = f32[768,128]{1,0:T(8,128)S(1)} custom-call(bf16[768,128]{1,0:T(8,128)(2,1)S(1)} %bitcast.24, bf16[1152,128]{1,0:T(8,128)(2,1)S(1)} %bitcast.7, f32[384,128]{1,0:T(8,128)S(1)} %get-tuple-element.32.refs_2_, f32[384,128]{1,0:T(8,128)S(1)} %get-tuple-element.33.refs_3_), custom_call_target="tpu_custom_call" | custom-call | flops 5000000 | bytes 2097152 | tf_op jit(solution)/shard_map/pallas_call | solution.py:384
  9.2 0.0 copy-start.2
  9.2 1.2 %collective-permute-done.x_far = bf16[96,128]{1,0:T(8,128)(2,1)S(1)} collective-permute-done((bf16[96,128]{1,0:T(8,128)(2,1)S(1)}, bf16[96,128]{1,0:T(8,128)(2,1)S(1)}, u32[]{:S(2)}, u32[]{:S(2)}) %collective-permute-start) | collective-permute-done | bytes 24608 | tf_op jit(solution)/shard_map/ppermute | solution.py:399
  10.4 0.0 collective-permute-done.1.x_near
  10.4 0.1 shard_map.49.acc_ref
  10.5 0.0 collective-permute-done.2.t_near
  10.5 0.0 collective-permute-done.3.t_far
  10.5 0.5 %shard_map.50 = (f32[768,128]{1,0:T(8,128)S(1)}, bf16[192,128]{1,0:T(8,128)(2,1)S(1)}, bf16[192,128]{1,0:T(8,128)(2,1)S(1)}, f32[384,128]{1,0:T(8,128)S(1)}) custom-call(bf16[1152,128]{1,0:T(8,128)(2,1)S(1)} %bitcast.9, bf16[1152,128]{1,0:T(8,128)(2,1)S(1)} %bitcast.26, f32[768,128]{1,0:T(8,128)S(1)} %shard_map.49.acc_ref, ...), custom_call_target="tpu_custom_call" | custom-call | flops 4000000 | bytes 2097152 | tf_op jit(solution)/shard_map/pallas_call | solution.py:384
  11.1 0.7 %collective-permute-start.6 = (bf16[192,128]{1,0:T(8,128)(2,1)S(1)}, bf16[192,128]{1,0:T(8,128)(2,1)S(1)}, u32[]{:S(2)}, u32[]{:S(2)}) collective-permute-start(bf16[192,128]{1,0:T(8,128)(2,1)S(1)} %get-tuple-element.43), channel_id=1, source_target_pairs={{0,4},{4,0},{8,12},{12,8},{1,5},{5,1},{9,13},{13,9},{2,6},{6,2},{1... | collective-permute-start | bytes 147464 | tf_op jit(solution)/shard_map/ppermute | solution.py:399
  11.8 1.5 %collective-permute-start.7 = (bf16[192,128]{1,0:T(8,128)(2,1)S(1)}, bf16[192,128]{1,0:T(8,128)(2,1)S(1)}, u32[]{:S(2)}, u32[]{:S(2)}) collective-permute-start(bf16[192,128]{1,0:T(8,128)(2,1)S(1)} %get-tuple-element.44), channel_id=1, source_target_pairs={{0,12},{4,8},{8,4},{12,0},{1,13},{5,9},{9,5},{13,1},{2,14},{6,10},... | collective-permute-start | bytes 147464 | tf_op jit(solution)/shard_map/ppermute | solution.py:399
  13.3 0.1 shard_map.51
  13.4 0.1 collective-permute-start.4
  13.5 1.6 %collective-permute-start.5 = (bf16[96,128]{1,0:T(8,128)(2,1)S(1)}, bf16[96,128]{1,0:T(8,128)(2,1)S(1)}, u32[]{:S(2)}, u32[]{:S(2)}) collective-permute-start(bf16[96,128]{1,0:T(8,128)(2,1)S(1)} %get-tuple-element.42), channel_id=1, source_target_pairs={{0,1},{1,0},{2,3},{3,2},{4,5},{5,4},{6,7},{7,6},{8,9},{9,8},{10,11... | collective-permute-start | bytes 73736 | tf_op jit(solution)/shard_map/ppermute | solution.py:399
  15.1 1.0 %shard_map.52.acc_ref = f32[768,128]{1,0:T(8,128)S(1)} custom-call(f32[768,128]{1,0:T(8,128)S(1)} %get-tuple-element.38.f_ref.refs_0_, bf16[1152,128]{1,0:T(8,128)(2,1)S(1)} %bitcast.11, f32[384,128]{1,0:T(8,128)S(1)} %get-tuple-element.39.refs_2_, f32[384,128]{1,0:T(8,128)S(1)} %get-tuple-element.40.refs_3_, bf16[768,128]{1,0:T(8,128)(2,1)S(1)} %bitcast.25, ...), custom_call_target="tpu_custom_call" | custom-call | flops 8000000 | bytes 2097152 | tf_op jit(solution)/shard_map/pallas_call | solution.py:384
  16.1 0.9 %collective-permute-done.4.x_far = bf16[96,128]{1,0:T(8,128)(2,1)S(1)} collective-permute-done((bf16[96,128]{1,0:T(8,128)(2,1)S(1)}, bf16[96,128]{1,0:T(8,128)(2,1)S(1)}, u32[]{:S(2)}, u32[]{:S(2)}) %collective-permute-start.4) | collective-permute-done | bytes 24608 | tf_op jit(solution)/shard_map/ppermute | solution.py:399
  16.9 0.0 collective-permute-done.5.x_near
  16.9 0.1 shard_map.53.acc_ref
  17.0 0.7 %collective-permute-done.7.t_far = bf16[192,128]{1,0:T(8,128)(2,1)S(1)} collective-permute-done((bf16[192,128]{1,0:T(8,128)(2,1)S(1)}, bf16[192,128]{1,0:T(8,128)(2,1)S(1)}, u32[]{:S(2)}, u32[]{:S(2)}) %collective-permute-start.7) | collective-permute-done | bytes 49184 | tf_op jit(solution)/shard_map/ppermute | solution.py:399
  17.7 0.2 shard_map.54
  17.9 0.5 %collective-permute-start.10 = (bf16[192,128]{1,0:T(8,128)(2,1)S(1)}, bf16[192,128]{1,0:T(8,128)(2,1)S(1)}, u32[]{:S(2)}, u32[]{:S(2)}) collective-permute-start(bf16[192,128]{1,0:T(8,128)(2,1)S(1)} %get-tuple-element.50), channel_id=1, source_target_pairs={{0,4},{4,0},{8,12},{12,8},{1,5},{5,1},{9,13},{13,9},{2,6},{6,2},{1... | collective-permute-start | bytes 147464 | tf_op jit(solution)/shard_map/ppermute | solution.py:399
  18.4 1.7 %collective-permute-start.11 = (bf16[192,128]{1,0:T(8,128)(2,1)S(1)}, bf16[192,128]{1,0:T(8,128)(2,1)S(1)}, u32[]{:S(2)}, u32[]{:S(2)}) collective-permute-start(bf16[192,128]{1,0:T(8,128)(2,1)S(1)} %get-tuple-element.51), channel_id=1, source_target_pairs={{0,12},{4,8},{8,4},{12,0},{1,13},{5,9},{9,5},{13,1},{2,14},{6,10},... | collective-permute-start | bytes 147464 | tf_op jit(solution)/shard_map/ppermute | solution.py:399
  20.1 0.1 shard_map.55
  20.2 0.1 collective-permute-start.8
  20.3 1.6 %collective-permute-start.9 = (bf16[96,128]{1,0:T(8,128)(2,1)S(1)}, bf16[96,128]{1,0:T(8,128)(2,1)S(1)}, u32[]{:S(2)}, u32[]{:S(2)}) collective-permute-start(bf16[96,128]{1,0:T(8,128)(2,1)S(1)} %get-tuple-element.49), channel_id=1, source_target_pairs={{0,1},{1,0},{2,3},{3,2},{4,5},{5,4},{6,7},{7,6},{8,9},{9,8},{10,11... | collective-permute-start | bytes 73736 | tf_op jit(solution)/shard_map/ppermute | solution.py:399
  21.9 0.6 %shard_map.56.acc_ref = f32[768,128]{1,0:T(8,128)S(1)} custom-call(f32[768,128]{1,0:T(8,128)S(1)} %get-tuple-element.45.f_ref.refs_0_.refs_4_, bf16[1152,128]{1,0:T(8,128)(2,1)S(1)} %bitcast.15, f32[384,128]{1,0:T(8,128)S(1)} %get-tuple-element.46.refs_2_, f32[384,128]{1,0:T(8,128)S(1)} %get-tuple-element.47.refs_3_), custom_call_target="tpu_custom_call" | custom-call | flops 5000000 | bytes 2097152 | tf_op jit(solution)/shard_map/pallas_call | solution.py:384
  22.6 1.2 %collective-permute-done.8.x_far = bf16[96,128]{1,0:T(8,128)(2,1)S(1)} collective-permute-done((bf16[96,128]{1,0:T(8,128)(2,1)S(1)}, bf16[96,128]{1,0:T(8,128)(2,1)S(1)}, u32[]{:S(2)}, u32[]{:S(2)}) %collective-permute-start.8) | collective-permute-done | bytes 24608 | tf_op jit(solution)/shard_map/ppermute | solution.py:399
  23.8 0.0 collective-permute-done.9.x_near
  23.8 0.1 shard_map.57.acc_ref
  23.9 0.0 collective-permute-done.10.t_near
  23.9 0.4 %collective-permute-done.11.t_far = bf16[192,128]{1,0:T(8,128)(2,1)S(1)} collective-permute-done((bf16[192,128]{1,0:T(8,128)(2,1)S(1)}, bf16[192,128]{1,0:T(8,128)(2,1)S(1)}, u32[]{:S(2)}, u32[]{:S(2)}) %collective-permute-start.11) | collective-permute-done | bytes 49184 | tf_op jit(solution)/shard_map/ppermute | solution.py:399
  24.3 0.5 %shard_map.58 = (f32[768,128]{1,0:T(8,128)S(1)}, bf16[192,128]{1,0:T(8,128)(2,1)S(1)}, bf16[192,128]{1,0:T(8,128)(2,1)S(1)}, f32[384,128]{1,0:T(8,128)S(1)}) custom-call(bf16[1152,128]{1,0:T(8,128)(2,1)S(1)} %bitcast.17, bf16[1152,128]{1,0:T(8,128)(2,1)S(1)} %bitcast.27, f32[768,128]{1,0:T(8,128)S(1)} %shard_map.57.acc_ref, ...), custom_call_target="tpu_custom_call" | custom-call | flops 4000000 | bytes 2097152 | tf_op jit(solution)/shard_map/pallas_call | solution.py:384
  24.8 0.3 collective-permute-start.14
  25.1 2.1 %collective-permute-start.15 = (bf16[192,128]{1,0:T(8,128)(2,1)S(1)}, bf16[192,128]{1,0:T(8,128)(2,1)S(1)}, u32[]{:S(2)}, u32[]{:S(2)}) collective-permute-start(bf16[192,128]{1,0:T(8,128)(2,1)S(1)} %get-tuple-element.58), channel_id=1, source_target_pairs={{0,12},{4,8},{8,4},{12,0},{1,13},{5,9},{9,5},{13,1},{2,14},{6,10},... | collective-permute-start | bytes 147464 | tf_op jit(solution)/shard_map/ppermute | solution.py:399
  27.2 0.1 shard_map.59
  27.3 0.1 collective-permute-start.12
  27.4 1.3 %collective-permute-start.13 = (bf16[96,128]{1,0:T(8,128)(2,1)S(1)}, bf16[96,128]{1,0:T(8,128)(2,1)S(1)}, u32[]{:S(2)}, u32[]{:S(2)}) collective-permute-start(bf16[96,128]{1,0:T(8,128)(2,1)S(1)} %get-tuple-element.56), channel_id=1, source_target_pairs={{0,1},{1,0},{2,3},{3,2},{4,5},{5,4},{6,7},{7,6},{8,9},{9,8},{10,11... | collective-permute-start | bytes 73736 | tf_op jit(solution)/shard_map/ppermute | solution.py:399
  28.7 1.0 %shard_map.60.acc_ref = f32[768,128]{1,0:T(8,128)S(1)} custom-call(f32[768,128]{1,0:T(8,128)S(1)} %get-tuple-element.52.f_ref.refs_0_, bf16[1152,128]{1,0:T(8,128)(2,1)S(1)} %bitcast.19, f32[384,128]{1,0:T(8,128)S(1)} %get-tuple-element.53.refs_2_, f32[384,128]{1,0:T(8,128)S(1)} %get-tuple-element.54.refs_3_, ...), custom_call_target="tpu_custom_call" | custom-call | flops 8000000 | bytes 2097152 | tf_op jit(solution)/shard_map/pallas_call | solution.py:384
  29.6 1.0 %collective-permute-done.12.x_far = bf16[96,128]{1,0:T(8,128)(2,1)S(1)} collective-permute-done((bf16[96,128]{1,0:T(8,128)(2,1)S(1)}, bf16[96,128]{1,0:T(8,128)(2,1)S(1)}, u32[]{:S(2)}, u32[]{:S(2)}) %collective-permute-start.12) | collective-permute-done | bytes 24608 | tf_op jit(solution)/shard_map/ppermute | solution.py:399
  30.6 0.1 shard_map.61.acc_ref
  30.7 0.0 collective-permute-done.14.t_near
  30.7 0.3 collective-permute-done.15.t_far
  31.0 0.8 %shard_map.62 = bf16[768,128]{1,0:T(8,128)(2,1)} custom-call(bf16[1152,128]{1,0:T(8,128)(2,1)S(1)} %bitcast.21, f32[768,128]{1,0:T(8,128)S(1)} %shard_map.61.acc_ref, bf16[192,128]{1,0:T(8,128)(2,1)S(1)} %collective-permute-done.14.t_near, bf16[192,128]{1,0:T(8,128)(2,1)S(1)} %collective-permute-done.15.t_far), custom_call_target="tpu_custom_call" | custom-call | flops 1000000 | bytes 2097152 | tf_op jit(solution)/shard_map/pallas_call | solution.py:384
  (9 shorter events, 0.0 us)
Async XLA Ops:
  0.0 6.7 %copy-start = (bf16[4,3,3,2,2,2,4,128]{7,6,5,4,3,2,1,0:T(4,128)(2,1)S(1)}, bf16[4,3,3,2,2,2,4,128]{7,6,5,4,3,2,1,0:T(4,128)(2,1)}, u32[]{:S(2)}) copy-start(bf16[4,3,3,2,2,2,4,128]{7,6,5,4,3,2,1,0:T(4,128)(2,1)} %param.5) | copy-start | bytes 884740
  0.0 6.7 %copy-start.1 = (bf16[4,4,3,2,2,4,128]{6,5,4,3,2,1,0:T(4,128)(2,1)S(1)}, bf16[4,4,3,2,2,4,128]{6,5,4,3,2,1,0:T(4,128)(2,1)}, u32[]{:S(2)}) copy-start(bf16[4,4,3,2,2,4,128]{6,5,4,3,2,1,0:T(4,128)(2,1)} %param.4) | copy-start | bytes 589828
  1.2 9.3 %collective-permute-start.2 = (bf16[192,128]{1,0:T(8,128)(2,1)S(1)}, bf16[192,128]{1,0:T(8,128)(2,1)S(1)}, u32[]{:S(2)}, u32[]{:S(2)}) collective-permute-start(bf16[192,128]{1,0:T(8,128)(2,1)S(1)} %get-tuple-element.36), channel_id=1, source_target_pairs={{0,4},{4,0},{8,12},{12,8},{1,5},{5,1},{9,13},{13,9},{2,6},{6,2},{1... | collective-permute-start | bytes 147464 | tf_op jit(solution)/shard_map/ppermute | solution.py:399
  4.2 6.3 %collective-permute-start.3 = (bf16[192,128]{1,0:T(8,128)(2,1)S(1)}, bf16[192,128]{1,0:T(8,128)(2,1)S(1)}, u32[]{:S(2)}, u32[]{:S(2)}) collective-permute-start(bf16[192,128]{1,0:T(8,128)(2,1)S(1)} %get-tuple-element.37), channel_id=1, source_target_pairs={{0,12},{4,8},{8,4},{12,0},{1,13},{5,9},{9,5},{13,1},{2,14},{6,10},... | collective-permute-start | bytes 147464 | tf_op jit(solution)/shard_map/ppermute | solution.py:399
  6.9 3.5 %collective-permute-start = (bf16[96,128]{1,0:T(8,128)(2,1)S(1)}, bf16[96,128]{1,0:T(8,128)(2,1)S(1)}, u32[]{:S(2)}, u32[]{:S(2)}) collective-permute-start(bf16[96,128]{1,0:T(8,128)(2,1)S(1)} %get-tuple-element.34), channel_id=1, source_target_pairs={{0,3},{1,2},{2,1},{3,0},{4,7},{5,6},{6,5},{7,4},{8,11},{9,10},{10,... | collective-permute-start | bytes 73736 | tf_op jit(solution)/shard_map/ppermute | solution.py:399
  7.3 3.1 %collective-permute-start.1 = (bf16[96,128]{1,0:T(8,128)(2,1)S(1)}, bf16[96,128]{1,0:T(8,128)(2,1)S(1)}, u32[]{:S(2)}, u32[]{:S(2)}) collective-permute-start(bf16[96,128]{1,0:T(8,128)(2,1)S(1)} %get-tuple-element.35), channel_id=1, source_target_pairs={{0,1},{1,0},{2,3},{3,2},{4,5},{5,4},{6,7},{7,6},{8,9},{9,8},{10,11... | collective-permute-start | bytes 73736 | tf_op jit(solution)/shard_map/ppermute | solution.py:399
  9.2 1.3 %copy-start.2 = (bf16[2,6,6,2,2,4,128]{6,5,4,3,2,1,0:T(4,128)(2,1)S(1)}, bf16[2,6,6,2,2,4,128]{6,5,4,3,2,1,0:T(4,128)(2,1)}, u32[]{:S(2)}) copy-start(bf16[2,6,6,2,2,4,128]{6,5,4,3,2,1,0:T(4,128)(2,1)} %param.7) | copy-start | bytes 884740
  11.1 6.0 %collective-permute-start.6 = (bf16[192,128]{1,0:T(8,128)(2,1)S(1)}, bf16[192,128]{1,0:T(8,128)(2,1)S(1)}, u32[]{:S(2)}, u32[]{:S(2)}) collective-permute-start(bf16[192,128]{1,0:T(8,128)(2,1)S(1)} %get-tuple-element.43), channel_id=1, source_target_pairs={{0,4},{4,0},{8,12},{12,8},{1,5},{5,1},{9,13},{13,9},{2,6},{6,2},{1... | collective-permute-start | bytes 147464 | tf_op jit(solution)/shard_map/ppermute | solution.py:399
  11.8 5.9 %collective-permute-start.7 = (bf16[192,128]{1,0:T(8,128)(2,1)S(1)}, bf16[192,128]{1,0:T(8,128)(2,1)S(1)}, u32[]{:S(2)}, u32[]{:S(2)}) collective-permute-start(bf16[192,128]{1,0:T(8,128)(2,1)S(1)} %get-tuple-element.44), channel_id=1, source_target_pairs={{0,12},{4,8},{8,4},{12,0},{1,13},{5,9},{9,5},{13,1},{2,14},{6,10},... | collective-permute-start | bytes 147464 | tf_op jit(solution)/shard_map/ppermute | solution.py:399
  13.3 1.8 %copy-start.3 = (bf16[2,6,6,2,2,4,128]{6,5,4,3,2,1,0:T(4,128)(2,1)S(1)}, bf16[2,6,6,2,2,4,128]{6,5,4,3,2,1,0:T(4,128)(2,1)}, u32[]{:S(2)}) copy-start(bf16[2,6,6,2,2,4,128]{6,5,4,3,2,1,0:T(4,128)(2,1)} %param.6) | copy-start | bytes 884740
  13.4 3.5 %collective-permute-start.4 = (bf16[96,128]{1,0:T(8,128)(2,1)S(1)}, bf16[96,128]{1,0:T(8,128)(2,1)S(1)}, u32[]{:S(2)}, u32[]{:S(2)}) collective-permute-start(bf16[96,128]{1,0:T(8,128)(2,1)S(1)} %get-tuple-element.41), channel_id=1, source_target_pairs={{0,3},{1,2},{2,1},{3,0},{4,7},{5,6},{6,5},{7,4},{8,11},{9,10},{10,... | collective-permute-start | bytes 73736 | tf_op jit(solution)/shard_map/ppermute | solution.py:399
  13.5 3.5 %collective-permute-start.5 = (bf16[96,128]{1,0:T(8,128)(2,1)S(1)}, bf16[96,128]{1,0:T(8,128)(2,1)S(1)}, u32[]{:S(2)}, u32[]{:S(2)}) collective-permute-start(bf16[96,128]{1,0:T(8,128)(2,1)S(1)} %get-tuple-element.42), channel_id=1, source_target_pairs={{0,1},{1,0},{2,3},{3,2},{4,5},{5,4},{6,7},{7,6},{8,9},{9,8},{10,11... | collective-permute-start | bytes 73736 | tf_op jit(solution)/shard_map/ppermute | solution.py:399
  17.9 6.0 %collective-permute-start.10 = (bf16[192,128]{1,0:T(8,128)(2,1)S(1)}, bf16[192,128]{1,0:T(8,128)(2,1)S(1)}, u32[]{:S(2)}, u32[]{:S(2)}) collective-permute-start(bf16[192,128]{1,0:T(8,128)(2,1)S(1)} %get-tuple-element.50), channel_id=1, source_target_pairs={{0,4},{4,0},{8,12},{12,8},{1,5},{5,1},{9,13},{13,9},{2,6},{6,2},{1... | collective-permute-start | bytes 147464 | tf_op jit(solution)/shard_map/ppermute | solution.py:399
  18.4 5.9 %collective-permute-start.11 = (bf16[192,128]{1,0:T(8,128)(2,1)S(1)}, bf16[192,128]{1,0:T(8,128)(2,1)S(1)}, u32[]{:S(2)}, u32[]{:S(2)}) collective-permute-start(bf16[192,128]{1,0:T(8,128)(2,1)S(1)} %get-tuple-element.51), channel_id=1, source_target_pairs={{0,12},{4,8},{8,4},{12,0},{1,13},{5,9},{9,5},{13,1},{2,14},{6,10},... | collective-permute-start | bytes 147464 | tf_op jit(solution)/shard_map/ppermute | solution.py:399
  20.2 3.5 %collective-permute-start.8 = (bf16[96,128]{1,0:T(8,128)(2,1)S(1)}, bf16[96,128]{1,0:T(8,128)(2,1)S(1)}, u32[]{:S(2)}, u32[]{:S(2)}) collective-permute-start(bf16[96,128]{1,0:T(8,128)(2,1)S(1)} %get-tuple-element.48), channel_id=1, source_target_pairs={{0,3},{1,2},{2,1},{3,0},{4,7},{5,6},{6,5},{7,4},{8,11},{9,10},{10,... | collective-permute-start | bytes 73736 | tf_op jit(solution)/shard_map/ppermute | solution.py:399
  20.3 3.5 %collective-permute-start.9 = (bf16[96,128]{1,0:T(8,128)(2,1)S(1)}, bf16[96,128]{1,0:T(8,128)(2,1)S(1)}, u32[]{:S(2)}, u32[]{:S(2)}) collective-permute-start(bf16[96,128]{1,0:T(8,128)(2,1)S(1)} %get-tuple-element.49), channel_id=1, source_target_pairs={{0,1},{1,0},{2,3},{3,2},{4,5},{5,4},{6,7},{7,6},{8,9},{9,8},{10,11... | collective-permute-start | bytes 73736 | tf_op jit(solution)/shard_map/ppermute | solution.py:399
  24.8 5.9 %collective-permute-start.14 = (bf16[192,128]{1,0:T(8,128)(2,1)S(1)}, bf16[192,128]{1,0:T(8,128)(2,1)S(1)}, u32[]{:S(2)}, u32[]{:S(2)}) collective-permute-start(bf16[192,128]{1,0:T(8,128)(2,1)S(1)} %get-tuple-element.57), channel_id=1, source_target_pairs={{0,4},{4,0},{8,12},{12,8},{1,5},{5,1},{9,13},{13,9},{2,6},{6,2},{1... | collective-permute-start | bytes 147464 | tf_op jit(solution)/shard_map/ppermute | solution.py:399
  25.1 5.9 %collective-permute-start.15 = (bf16[192,128]{1,0:T(8,128)(2,1)S(1)}, bf16[192,128]{1,0:T(8,128)(2,1)S(1)}, u32[]{:S(2)}, u32[]{:S(2)}) collective-permute-start(bf16[192,128]{1,0:T(8,128)(2,1)S(1)} %get-tuple-element.58), channel_id=1, source_target_pairs={{0,12},{4,8},{8,4},{12,0},{1,13},{5,9},{9,5},{13,1},{2,14},{6,10},... | collective-permute-start | bytes 147464 | tf_op jit(solution)/shard_map/ppermute | solution.py:399
  27.3 3.3 %collective-permute-start.12 = (bf16[96,128]{1,0:T(8,128)(2,1)S(1)}, bf16[96,128]{1,0:T(8,128)(2,1)S(1)}, u32[]{:S(2)}, u32[]{:S(2)}) collective-permute-start(bf16[96,128]{1,0:T(8,128)(2,1)S(1)} %get-tuple-element.55), channel_id=1, source_target_pairs={{0,3},{1,2},{2,1},{3,0},{4,7},{5,6},{6,5},{7,4},{8,11},{9,10},{10,... | collective-permute-start | bytes 73736 | tf_op jit(solution)/shard_map/ppermute | solution.py:399
  27.4 3.2 %collective-permute-start.13 = (bf16[96,128]{1,0:T(8,128)(2,1)S(1)}, bf16[96,128]{1,0:T(8,128)(2,1)S(1)}, u32[]{:S(2)}, u32[]{:S(2)}) collective-permute-start(bf16[96,128]{1,0:T(8,128)(2,1)S(1)} %get-tuple-element.56), channel_id=1, source_target_pairs={{0,1},{1,0},{2,3},{3,2},{4,5},{5,4},{6,7},{7,6},{8,9},{9,8},{10,11... | collective-permute-start | bytes 73736 | tf_op jit(solution)/shard_map/ppermute | solution.py:399

commit v5 on v4

--- a/solution.py
+++ b/solution.py
@@ -107,8 +107,9 @@
     return rows // 4, rows % 4
 
 
-def even_device(axis):
-    return lax.broadcast(lax.axis_index(axis) % 2, (8, 128)) == 0
+def even_device(*axes):
+    place = sum(lax.axis_index(axis) for axis in axes)
+    return lax.broadcast(place % 2, (8, 128)) == 0
 
 
 def either(even, a, b):
@@ -124,8 +125,8 @@
     return jnp.where(mask, a, b)
 
 
-def send_t(f_ref, links_ref, parity, t_near, t_far, kept, ready=lambda r: None):
-    even = even_device("ta")
+def send_t(f_ref, links_ref, parity, t_one, t_two, kept, ready=lambda r: None):
+    even = even_device("ta", "gx")
     t_idx, _ = site_masks()
     first = t_idx == 0
     links = load_links(links_ref, 0, parity)
@@ -139,8 +140,8 @@
         for c in range(3):
             front = [select(first, ahead[c + 3][i], moved[c][i]) for i in range(2)]
             rear = [select(first, back[c][i], carry[c + 3][i]) for i in range(2)]
-            store_pair(t_near, r * 3 + c, either(even, rear, front))
-            store_pair(t_far, r * 3 + c, either(even, front, rear))
+            store_pair(t_one, r * 3 + c, either(even, rear, front))
+            store_pair(t_two, r * 3 + c, either(even, front, rear))
         for j in range(6):
             store_pair(kept, r * 6 + j, back[j])
 
@@ -325,8 +326,8 @@
             store_field(out_ref, r, rebuild_signed(load_field(acc_ref, r), half, 1, sign))
 
 
-def join_t(links_ref, acc_ref, t_near, t_far, parity, out_ref, done=lambda r: None):
-    even = even_device("ta")
+def join_t(links_ref, acc_ref, t_one, t_two, parity, out_ref, done=lambda r: None):
+    even = even_device("ta", "gx")
     t_idx, _ = site_masks()
     first = t_idx == 0
     sign = jnp.where(first, 1.0, -1.0).astype(F32)
@@ -335,9 +336,9 @@
     for r in range(RHS):
         nxt, last = [], []
         for c in range(3):
-            near, far = load_pair(t_near, r * 3 + c), load_pair(t_far, r * 3 + c)
-            nxt.append(either(even, near, far))
-            last.append(either(even, far, near))
+            one, two = load_pair(t_one, r * 3 + c), load_pair(t_two, r * 3 + c)
+            nxt.append(either(even, one, two))
+            last.append(either(even, two, one))
         ahead = matvec(links, nxt)
         half = [tuple(select(first, last[c][i], ahead[c][i]) for i in range(2)) for c in range(3)]
         half += [
@@ -347,19 +348,19 @@
         done(r)
 
 
-def odd_kernel(links_ref, clover_ref, acc_ref, t_near, t_far, out_ref, *refs):
+def odd_kernel(links_ref, clover_ref, acc_ref, t_one, t_two, out_ref, *refs):
     outs, summed = refs[:3], refs[3]
-    join_t(links_ref, acc_ref, t_near, t_far, 0, summed)
+    join_t(links_ref, acc_ref, t_one, t_two, 0, summed)
     clover_to(clover_ref, lambda r: load_field(summed, r), out_ref, -KAPPA2)
     send_t(out_ref, links_ref, 1, *outs)
 
 
-def even_kernel(links_ref, acc_ref, t_near, t_far, out_ref, *outs):
-    join_t(links_ref, acc_ref, t_near, t_far, 1, out_ref)
+def even_kernel(links_ref, acc_ref, t_one, t_two, out_ref, *outs):
+    join_t(links_ref, acc_ref, t_one, t_two, 1, out_ref)
     send_t(out_ref, links_ref, 0, *outs)
 
 
-def last_kernel(links_ref, acc_ref, t_near, t_far, out_hbm, held, sems):
+def last_kernel(links_ref, acc_ref, t_one, t_two, out_hbm, held, sems):
     part = held.shape[0] // RHS
     copies = []
 
@@ -368,7 +369,7 @@
         copies.append(pltpu.make_async_copy(held.at[rows], out_hbm.at[rows], sems.at[r]))
         copies[-1].start()
 
-    join_t(links_ref, acc_ref, t_near, t_far, 1, held, done)
+    join_t(links_ref, acc_ref, t_one, t_two, 1, held, done)
     for copy in copies:
         copy.wait()
 
@@ -397,6 +398,17 @@
     assert count % 2 == 0
     pairs = [(i, (i + (1 if (i % 2 == 0) != far else -1)) % count) for i in range(count)]
     return lax.ppermute(value, axis, pairs)
+
+
+def swap_t(value, ahead):
+    count, across = lax.axis_size("ta"), lax.axis_size("gx")
+    assert count % 2 == 0 and across % 2 == 0
+    pairs = []
+    for i in range(count):
+        for j in range(across):
+            step = 1 if ((i + j) % 2 == 0) == ahead else -1
+            pairs.append((i * across + j, (i + step) % count * across + j))
+    return lax.ppermute(value, ("ta", "gx"), pairs)
 
 
 def per_device(source, gauge_links, clover_even, clover_odd_inv):
@@ -411,10 +423,10 @@
         pltpu.VMEM((links.shape[0] // 4, 128), BF16),
         pltpu.SemaphoreType.DMA((RHS + 1,)),
     ]
-    t_near, t_far, kept_t = call(start_kernel, held, T_HALOS + KEPT, 1_500_000, start_scratch, in_space=pltpu.HBM)
+    t_one, t_two, kept_t = call(start_kernel, held, T_HALOS + KEPT, 1_500_000, start_scratch, in_space=pltpu.HBM)
     for hop in range(4):
         parity = hop % 2
-        t_near, t_far = swap(t_near, "ta", False), swap(t_far, "ta", True)
+        t_one, t_two = swap_t(t_one, True), swap_t(t_two, False)
         x_far, x_near, kept_x = call(
             functools.partial(send_x_kernel, parity), (f, links), X_HALOS + KEPT, 1_500_000
         )
@@ -427,17 +439,17 @@
         acc, = call(functools.partial(join_x_kernel, parity), (links, acc, x_far, x_near), FIELD, 1_000_000)
         before = f
         if parity == 0:
-            f, t_near, t_far, kept_t = call(
-                odd_kernel, (links, odd, acc, t_near, t_far), FIELD + T_HALOS + KEPT, 4_000_000,
+            f, t_one, t_two, kept_t = call(
+                odd_kernel, (links, odd, acc, t_one, t_two), FIELD + T_HALOS + KEPT, 4_000_000,
                 [pltpu.VMEM((ROWS, 128), F32)],
             )
         elif hop == 1:
-            f, t_near, t_far, kept_t = call(
-                even_kernel, (links, acc, t_near, t_far), FIELD + T_HALOS + KEPT, 2_000_000
+            f, t_one, t_two, kept_t = call(
+                even_kernel, (links, acc, t_one, t_two), FIELD + T_HALOS + KEPT, 2_000_000
             )
         else:
             out, = call(
-                last_kernel, (links, acc, t_near, t_far), [((ROWS, 128), BF16)], 1_000_000,
+                last_kernel, (links, acc, t_one, t_two), [((ROWS, 128), BF16)], 1_000_000,
                 [pltpu.VMEM((ROWS, 128), BF16), pltpu.SemaphoreType.DMA((RHS,))], out_space=pltpu.HBM,
             )
     return out.reshape(shape)

time: 31.9 us -> 31.8 us (level)
    ppermute x0 -> x8, starting transfers between devices: none -> 12.3 us  [swap_t(): return lax.ppermute(value, ('ta', 'gx'), pairs)]
    ppermute x16 -> x8, starting transfers between devices: 18.7 us -> 6.66 us  [swap(): return lax.ppermute(value, axis, pairs)]
    ppermute x16 -> x8, waiting for transfers between devices: 5.6 us -> 4.19 us  [swap(): return lax.ppermute(value, axis, pairs)]
    ppermute x0 -> x8, waiting for transfers between devices: none -> 1.15 us  [swap_t(): return lax.ppermute(value, ('ta', 'gx'), pairs)]
where the time goes in v5:
time: 31.8 us; the launch traced here: 31.7 us
  starting transfers between devices  18.9 us (59%)
  Pallas kernels  7.25 us (23%)
  waiting for transfers between devices  5.34 us (17%)
    ppermute x8, starting transfers between devices, swap_t(): return lax.ppermute(value, ('ta', 'gx'), pairs)  12.3 us
    pallas_call x17, Pallas kernels, call(): pl.pallas_call(kernel, out_shape=tuple((jax.ShapeDtypeStruct(shape, dtype...  7.25 us
    ppermute x8, starting transfers between devices, swap(): return lax.ppermute(value, axis, pairs)  6.66 us
    ppermute x8, waiting for transfers between devices, swap(): return lax.ppermute(value, axis, pairs)  4.19 us
    ppermute x8, waiting for transfers between devices, swap_t(): return lax.ppermute(value, ('ta', 'gx'), pairs)  1.15 us
  transfers between devices with their start and end apart: 16, of which 7 were waited for; matrix products, arithmetic and copies ran while one was open for 0% of the time, Pallas kernels for 13%

profile of v5, /device:TPU:0, one launch (start us, length us, event | category | flops | bytes accessed | tf_op | source)
XLA Modules:
  0.0 31.7 jit_solution(12380891450789184574)
XLA Ops:
  0.0 1.1 %shard_map.46 = (bf16[192,128]{1,0:T(8,128)(2,1)S(1)}, bf16[192,128]{1,0:T(8,128)(2,1)S(1)}, f32[384,128]{1,0:T(8,128)S(1)}) custom-call(bf16[768,128]{1,0:T(8,128)(2,1)} %bitcast.22, bf16[1152,128]{1,0:T(8,128)(2,1)} %bitcast.5), custom_call_target="tpu_custom_call" | custom-call | flops 1500000 | bytes 2097152 | tf_op jit(solution)/shard_map/pallas_call | solution.py:385
  1.2 3.1 %collective-permute-start.2 = (bf16[192,128]{1,0:T(8,128)(2,1)S(1)}, bf16[192,128]{1,0:T(8,128)(2,1)S(1)}, u32[]{:S(2)}, u32[]{:S(2)}) collective-permute-start(bf16[192,128]{1,0:T(8,128)(2,1)S(1)} %get-tuple-element.36), channel_id=1, source_target_pairs={{0,4},{1,13},{2,6},{3,15},{4,0},{5,9},{6,2},{7,11},{8,12},{9,5},{1... | collective-permute-start | bytes 147464 | tf_op jit(solution)/shard_map/ppermute | solution.py:411
  4.2 2.5 %collective-permute-start.3 = (bf16[192,128]{1,0:T(8,128)(2,1)S(1)}, bf16[192,128]{1,0:T(8,128)(2,1)S(1)}, u32[]{:S(2)}, u32[]{:S(2)}) collective-permute-start(bf16[192,128]{1,0:T(8,128)(2,1)S(1)} %get-tuple-element.37), channel_id=1, source_target_pairs={{0,12},{1,5},{2,14},{3,7},{4,8},{5,1},{6,10},{7,3},{8,4},{9,13},{1... | collective-permute-start | bytes 147464 | tf_op jit(solution)/shard_map/ppermute | solution.py:411
  6.7 0.1 shard_map.47
  6.9 0.3 collective-permute-start
  7.2 1.4 %collective-permute-start.1 = (bf16[96,128]{1,0:T(8,128)(2,1)S(1)}, bf16[96,128]{1,0:T(8,128)(2,1)S(1)}, u32[]{:S(2)}, u32[]{:S(2)}) collective-permute-start(bf16[96,128]{1,0:T(8,128)(2,1)S(1)} %get-tuple-element.35), channel_id=1, source_target_pairs={{0,1},{1,0},{2,3},{3,2},{4,5},{5,4},{6,7},{7,6},{8,9},{9,8},{10,11... | collective-permute-start | bytes 73736 | tf_op jit(solution)/shard_map/ppermute | solution.py:400
  8.5 0.7 %shard_map.48.acc_ref = f32[768,128]{1,0:T(8,128)S(1)} custom-call(bf16[768,128]{1,0:T(8,128)(2,1)S(1)} %bitcast.24, bf16[1152,128]{1,0:T(8,128)(2,1)S(1)} %bitcast.7, f32[384,128]{1,0:T(8,128)S(1)} %get-tuple-element.32.refs_2_, f32[384,128]{1,0:T(8,128)S(1)} %get-tuple-element.33.refs_3_), custom_call_target="tpu_custom_call" | custom-call | flops 5000000 | bytes 2097152 | tf_op jit(solution)/shard_map/pallas_call | solution.py:385
  9.2 0.0 copy-start.2
  9.2 1.2 %collective-permute-done.x_far = bf16[96,128]{1,0:T(8,128)(2,1)S(1)} collective-permute-done((bf16[96,128]{1,0:T(8,128)(2,1)S(1)}, bf16[96,128]{1,0:T(8,128)(2,1)S(1)}, u32[]{:S(2)}, u32[]{:S(2)}) %collective-permute-start) | collective-permute-done | bytes 24608 | tf_op jit(solution)/shard_map/ppermute | solution.py:400
  10.4 0.0 collective-permute-done.1.x_near
  10.4 0.1 shard_map.49.acc_ref
  10.5 0.0 collective-permute-done.2.t_one
  10.5 0.0 collective-permute-done.3.t_two
  10.5 0.5 %shard_map.50 = (f32[768,128]{1,0:T(8,128)S(1)}, bf16[192,128]{1,0:T(8,128)(2,1)S(1)}, bf16[192,128]{1,0:T(8,128)(2,1)S(1)}, f32[384,128]{1,0:T(8,128)S(1)}) custom-call(bf16[1152,128]{1,0:T(8,128)(2,1)S(1)} %bitcast.9, bf16[1152,128]{1,0:T(8,128)(2,1)S(1)} %bitcast.26, f32[768,128]{1,0:T(8,128)S(1)} %shard_map.49.acc_ref, ...), custom_call_target="tpu_custom_call" | custom-call | flops 4000000 | bytes 2097152 | tf_op jit(solution)/shard_map/pallas_call | solution.py:385
  11.1 0.5 %collective-permute-start.6 = (bf16[192,128]{1,0:T(8,128)(2,1)S(1)}, bf16[192,128]{1,0:T(8,128)(2,1)S(1)}, u32[]{:S(2)}, u32[]{:S(2)}) collective-permute-start(bf16[192,128]{1,0:T(8,128)(2,1)S(1)} %get-tuple-element.43), channel_id=1, source_target_pairs={{0,4},{1,13},{2,6},{3,15},{4,0},{5,9},{6,2},{7,11},{8,12},{9,5},{1... | collective-permute-start | bytes 147464 | tf_op jit(solution)/shard_map/ppermute | solution.py:411
  11.6 1.7 %collective-permute-start.7 = (bf16[192,128]{1,0:T(8,128)(2,1)S(1)}, bf16[192,128]{1,0:T(8,128)(2,1)S(1)}, u32[]{:S(2)}, u32[]{:S(2)}) collective-permute-start(bf16[192,128]{1,0:T(8,128)(2,1)S(1)} %get-tuple-element.44), channel_id=1, source_target_pairs={{0,12},{1,5},{2,14},{3,7},{4,8},{5,1},{6,10},{7,3},{8,4},{9,13},{1... | collective-permute-start | bytes 147464 | tf_op jit(solution)/shard_map/ppermute | solution.py:411
  13.3 0.1 shard_map.51
  13.4 0.1 collective-permute-start.4
  13.5 1.6 %collective-permute-start.5 = (bf16[96,128]{1,0:T(8,128)(2,1)S(1)}, bf16[96,128]{1,0:T(8,128)(2,1)S(1)}, u32[]{:S(2)}, u32[]{:S(2)}) collective-permute-start(bf16[96,128]{1,0:T(8,128)(2,1)S(1)} %get-tuple-element.42), channel_id=1, source_target_pairs={{0,1},{1,0},{2,3},{3,2},{4,5},{5,4},{6,7},{7,6},{8,9},{9,8},{10,11... | collective-permute-start | bytes 73736 | tf_op jit(solution)/shard_map/ppermute | solution.py:400
  15.1 1.0 %shard_map.52.acc_ref = f32[768,128]{1,0:T(8,128)S(1)} custom-call(f32[768,128]{1,0:T(8,128)S(1)} %get-tuple-element.38.f_ref.refs_0_, bf16[1152,128]{1,0:T(8,128)(2,1)S(1)} %bitcast.11, f32[384,128]{1,0:T(8,128)S(1)} %get-tuple-element.39.refs_2_, f32[384,128]{1,0:T(8,128)S(1)} %get-tuple-element.40.refs_3_, bf16[768,128]{1,0:T(8,128)(2,1)S(1)} %bitcast.25, ...), custom_call_target="tpu_custom_call" | custom-call | flops 8000000 | bytes 2097152 | tf_op jit(solution)/shard_map/pallas_call | solution.py:385
  16.1 0.9 %collective-permute-done.4.x_far = bf16[96,128]{1,0:T(8,128)(2,1)S(1)} collective-permute-done((bf16[96,128]{1,0:T(8,128)(2,1)S(1)}, bf16[96,128]{1,0:T(8,128)(2,1)S(1)}, u32[]{:S(2)}, u32[]{:S(2)}) %collective-permute-start.4) | collective-permute-done | bytes 24608 | tf_op jit(solution)/shard_map/ppermute | solution.py:400
  16.9 0.0 collective-permute-done.5.x_near
  16.9 0.1 shard_map.53.acc_ref
  17.0 0.0 collective-permute-done.6.t_one
  17.0 0.4 %collective-permute-done.7.t_two = bf16[192,128]{1,0:T(8,128)(2,1)S(1)} collective-permute-done((bf16[192,128]{1,0:T(8,128)(2,1)S(1)}, bf16[192,128]{1,0:T(8,128)(2,1)S(1)}, u32[]{:S(2)}, u32[]{:S(2)}) %collective-permute-start.7) | collective-permute-done | bytes 49184 | tf_op jit(solution)/shard_map/ppermute | solution.py:411
  17.5 0.2 shard_map.54
  17.7 0.7 %collective-permute-start.10 = (bf16[192,128]{1,0:T(8,128)(2,1)S(1)}, bf16[192,128]{1,0:T(8,128)(2,1)S(1)}, u32[]{:S(2)}, u32[]{:S(2)}) collective-permute-start(bf16[192,128]{1,0:T(8,128)(2,1)S(1)} %get-tuple-element.50), channel_id=1, source_target_pairs={{0,4},{1,13},{2,6},{3,15},{4,0},{5,9},{6,2},{7,11},{8,12},{9,5},{1... | collective-permute-start | bytes 147464 | tf_op jit(solution)/shard_map/ppermute | solution.py:411
  18.4 1.7 %collective-permute-start.11 = (bf16[192,128]{1,0:T(8,128)(2,1)S(1)}, bf16[192,128]{1,0:T(8,128)(2,1)S(1)}, u32[]{:S(2)}, u32[]{:S(2)}) collective-permute-start(bf16[192,128]{1,0:T(8,128)(2,1)S(1)} %get-tuple-element.51), channel_id=1, source_target_pairs={{0,12},{1,5},{2,14},{3,7},{4,8},{5,1},{6,10},{7,3},{8,4},{9,13},{1... | collective-permute-start | bytes 147464 | tf_op jit(solution)/shard_map/ppermute | solution.py:411
  20.1 0.1 shard_map.55
  20.3 0.1 collective-permute-start.8
  20.3 1.6 %collective-permute-start.9 = (bf16[96,128]{1,0:T(8,128)(2,1)S(1)}, bf16[96,128]{1,0:T(8,128)(2,1)S(1)}, u32[]{:S(2)}, u32[]{:S(2)}) collective-permute-start(bf16[96,128]{1,0:T(8,128)(2,1)S(1)} %get-tuple-element.49), channel_id=1, source_target_pairs={{0,1},{1,0},{2,3},{3,2},{4,5},{5,4},{6,7},{7,6},{8,9},{9,8},{10,11... | collective-permute-start | bytes 73736 | tf_op jit(solution)/shard_map/ppermute | solution.py:400
  21.9 0.6 %shard_map.56.acc_ref = f32[768,128]{1,0:T(8,128)S(1)} custom-call(f32[768,128]{1,0:T(8,128)S(1)} %get-tuple-element.45.f_ref.refs_0_.refs_4_, bf16[1152,128]{1,0:T(8,128)(2,1)S(1)} %bitcast.15, f32[384,128]{1,0:T(8,128)S(1)} %get-tuple-element.46.refs_2_, f32[384,128]{1,0:T(8,128)S(1)} %get-tuple-element.47.refs_3_), custom_call_target="tpu_custom_call" | custom-call | flops 5000000 | bytes 2097152 | tf_op jit(solution)/shard_map/pallas_call | solution.py:385
  22.6 1.2 %collective-permute-done.8.x_far = bf16[96,128]{1,0:T(8,128)(2,1)S(1)} collective-permute-done((bf16[96,128]{1,0:T(8,128)(2,1)S(1)}, bf16[96,128]{1,0:T(8,128)(2,1)S(1)}, u32[]{:S(2)}, u32[]{:S(2)}) %collective-permute-start.8) | collective-permute-done | bytes 24608 | tf_op jit(solution)/shard_map/ppermute | solution.py:400
  23.8 0.0 collective-permute-done.9.x_near
  23.8 0.1 shard_map.57.acc_ref
  23.9 0.4 %collective-permute-done.11.t_two = bf16[192,128]{1,0:T(8,128)(2,1)S(1)} collective-permute-done((bf16[192,128]{1,0:T(8,128)(2,1)S(1)}, bf16[192,128]{1,0:T(8,128)(2,1)S(1)}, u32[]{:S(2)}, u32[]{:S(2)}) %collective-permute-start.11) | collective-permute-done | bytes 49184 | tf_op jit(solution)/shard_map/ppermute | solution.py:411
  24.3 0.5 %shard_map.58 = (f32[768,128]{1,0:T(8,128)S(1)}, bf16[192,128]{1,0:T(8,128)(2,1)S(1)}, bf16[192,128]{1,0:T(8,128)(2,1)S(1)}, f32[384,128]{1,0:T(8,128)S(1)}) custom-call(bf16[1152,128]{1,0:T(8,128)(2,1)S(1)} %bitcast.17, bf16[1152,128]{1,0:T(8,128)(2,1)S(1)} %bitcast.27, f32[768,128]{1,0:T(8,128)S(1)} %shard_map.57.acc_ref, ...), custom_call_target="tpu_custom_call" | custom-call | flops 4000000 | bytes 2097152 | tf_op jit(solution)/shard_map/pallas_call | solution.py:385
  24.8 0.1 collective-permute-start.14
  24.9 2.0 %collective-permute-start.15 = (bf16[192,128]{1,0:T(8,128)(2,1)S(1)}, bf16[192,128]{1,0:T(8,128)(2,1)S(1)}, u32[]{:S(2)}, u32[]{:S(2)}) collective-permute-start(bf16[192,128]{1,0:T(8,128)(2,1)S(1)} %get-tuple-element.58), channel_id=1, source_target_pairs={{0,12},{1,5},{2,14},{3,7},{4,8},{5,1},{6,10},{7,3},{8,4},{9,13},{1... | collective-permute-start | bytes 147464 | tf_op jit(solution)/shard_map/ppermute | solution.py:411
  26.9 0.1 shard_map.59
  27.0 0.1 collective-permute-start.12
  27.1 1.6 %collective-permute-start.13 = (bf16[96,128]{1,0:T(8,128)(2,1)S(1)}, bf16[96,128]{1,0:T(8,128)(2,1)S(1)}, u32[]{:S(2)}, u32[]{:S(2)}) collective-permute-start(bf16[96,128]{1,0:T(8,128)(2,1)S(1)} %get-tuple-element.56), channel_id=1, source_target_pairs={{0,1},{1,0},{2,3},{3,2},{4,5},{5,4},{6,7},{7,6},{8,9},{9,8},{10,11... | collective-permute-start | bytes 73736 | tf_op jit(solution)/shard_map/ppermute | solution.py:400
  28.7 1.0 %shard_map.60.acc_ref = f32[768,128]{1,0:T(8,128)S(1)} custom-call(f32[768,128]{1,0:T(8,128)S(1)} %get-tuple-element.52.f_ref.refs_0_, bf16[1152,128]{1,0:T(8,128)(2,1)S(1)} %bitcast.19, f32[384,128]{1,0:T(8,128)S(1)} %get-tuple-element.53.refs_2_, f32[384,128]{1,0:T(8,128)S(1)} %get-tuple-element.54.refs_3_, ...), custom_call_target="tpu_custom_call" | custom-call | flops 8000000 | bytes 2097152 | tf_op jit(solution)/shard_map/pallas_call | solution.py:385
  29.6 0.9 %collective-permute-done.12.x_far = bf16[96,128]{1,0:T(8,128)(2,1)S(1)} collective-permute-done((bf16[96,128]{1,0:T(8,128)(2,1)S(1)}, bf16[96,128]{1,0:T(8,128)(2,1)S(1)}, u32[]{:S(2)}, u32[]{:S(2)}) %collective-permute-start.12) | collective-permute-done | bytes 24608 | tf_op jit(solution)/shard_map/ppermute | solution.py:400
  30.5 0.1 shard_map.61.acc_ref
  30.6 0.0 collective-permute-done.14.t_one
  30.6 0.3 collective-permute-done.15.t_two
  30.9 0.8 %shard_map.62 = bf16[768,128]{1,0:T(8,128)(2,1)} custom-call(bf16[1152,128]{1,0:T(8,128)(2,1)S(1)} %bitcast.21, f32[768,128]{1,0:T(8,128)S(1)} %shard_map.61.acc_ref, bf16[192,128]{1,0:T(8,128)(2,1)S(1)} %collective-permute-done.14.t_one, bf16[192,128]{1,0:T(8,128)(2,1)S(1)} %collective-permute-done.15.t_two), custom_call_target="tpu_custom_call" | custom-call | flops 1000000 | bytes 2097152 | tf_op jit(solution)/shard_map/pallas_call | solution.py:385
  (9 shorter events, 0.0 us)
Async XLA Ops:
  0.0 6.7 %copy-start = (bf16[4,3,3,2,2,2,4,128]{7,6,5,4,3,2,1,0:T(4,128)(2,1)S(1)}, bf16[4,3,3,2,2,2,4,128]{7,6,5,4,3,2,1,0:T(4,128)(2,1)}, u32[]{:S(2)}) copy-start(bf16[4,3,3,2,2,2,4,128]{7,6,5,4,3,2,1,0:T(4,128)(2,1)} %param.5) | copy-start | bytes 884740
  0.0 6.7 %copy-start.1 = (bf16[4,4,3,2,2,4,128]{6,5,4,3,2,1,0:T(4,128)(2,1)S(1)}, bf16[4,4,3,2,2,4,128]{6,5,4,3,2,1,0:T(4,128)(2,1)}, u32[]{:S(2)}) copy-start(bf16[4,4,3,2,2,4,128]{6,5,4,3,2,1,0:T(4,128)(2,1)} %param.4) | copy-start | bytes 589828
  1.2 9.3 %collective-permute-start.2 = (bf16[192,128]{1,0:T(8,128)(2,1)S(1)}, bf16[192,128]{1,0:T(8,128)(2,1)S(1)}, u32[]{:S(2)}, u32[]{:S(2)}) collective-permute-start(bf16[192,128]{1,0:T(8,128)(2,1)S(1)} %get-tuple-element.36), channel_id=1, source_target_pairs={{0,4},{1,13},{2,6},{3,15},{4,0},{5,9},{6,2},{7,11},{8,12},{9,5},{1... | collective-permute-start | bytes 147464 | tf_op jit(solution)/shard_map/ppermute | solution.py:411
  4.2 6.3 %collective-permute-start.3 = (bf16[192,128]{1,0:T(8,128)(2,1)S(1)}, bf16[192,128]{1,0:T(8,128)(2,1)S(1)}, u32[]{:S(2)}, u32[]{:S(2)}) collective-permute-start(bf16[192,128]{1,0:T(8,128)(2,1)S(1)} %get-tuple-element.37), channel_id=1, source_target_pairs={{0,12},{1,5},{2,14},{3,7},{4,8},{5,1},{6,10},{7,3},{8,4},{9,13},{1... | collective-permute-start | bytes 147464 | tf_op jit(solution)/shard_map/ppermute | solution.py:411
  6.9 3.5 %collective-permute-start = (bf16[96,128]{1,0:T(8,128)(2,1)S(1)}, bf16[96,128]{1,0:T(8,128)(2,1)S(1)}, u32[]{:S(2)}, u32[]{:S(2)}) collective-permute-start(bf16[96,128]{1,0:T(8,128)(2,1)S(1)} %get-tuple-element.34), channel_id=1, source_target_pairs={{0,3},{1,2},{2,1},{3,0},{4,7},{5,6},{6,5},{7,4},{8,11},{9,10},{10,... | collective-permute-start | bytes 73736 | tf_op jit(solution)/shard_map/ppermute | solution.py:400
  7.2 3.3 %collective-permute-start.1 = (bf16[96,128]{1,0:T(8,128)(2,1)S(1)}, bf16[96,128]{1,0:T(8,128)(2,1)S(1)}, u32[]{:S(2)}, u32[]{:S(2)}) collective-permute-start(bf16[96,128]{1,0:T(8,128)(2,1)S(1)} %get-tuple-element.35), channel_id=1, source_target_pairs={{0,1},{1,0},{2,3},{3,2},{4,5},{5,4},{6,7},{7,6},{8,9},{9,8},{10,11... | collective-permute-start | bytes 73736 | tf_op jit(solution)/shard_map/ppermute | solution.py:400
  9.2 1.3 %copy-start.2 = (bf16[2,6,6,2,2,4,128]{6,5,4,3,2,1,0:T(4,128)(2,1)S(1)}, bf16[2,6,6,2,2,4,128]{6,5,4,3,2,1,0:T(4,128)(2,1)}, u32[]{:S(2)}) copy-start(bf16[2,6,6,2,2,4,128]{6,5,4,3,2,1,0:T(4,128)(2,1)} %param.7) | copy-start | bytes 884740
  11.1 6.0 %collective-permute-start.6 = (bf16[192,128]{1,0:T(8,128)(2,1)S(1)}, bf16[192,128]{1,0:T(8,128)(2,1)S(1)}, u32[]{:S(2)}, u32[]{:S(2)}) collective-permute-start(bf16[192,128]{1,0:T(8,128)(2,1)S(1)} %get-tuple-element.43), channel_id=1, source_target_pairs={{0,4},{1,13},{2,6},{3,15},{4,0},{5,9},{6,2},{7,11},{8,12},{9,5},{1... | collective-permute-start | bytes 147464 | tf_op jit(solution)/shard_map/ppermute | solution.py:411
  11.6 5.9 %collective-permute-start.7 = (bf16[192,128]{1,0:T(8,128)(2,1)S(1)}, bf16[192,128]{1,0:T(8,128)(2,1)S(1)}, u32[]{:S(2)}, u32[]{:S(2)}) collective-permute-start(bf16[192,128]{1,0:T(8,128)(2,1)S(1)} %get-tuple-element.44), channel_id=1, source_target_pairs={{0,12},{1,5},{2,14},{3,7},{4,8},{5,1},{6,10},{7,3},{8,4},{9,13},{1... | collective-permute-start | bytes 147464 | tf_op jit(solution)/shard_map/ppermute | solution.py:411
  13.3 1.8 %copy-start.3 = (bf16[2,6,6,2,2,4,128]{6,5,4,3,2,1,0:T(4,128)(2,1)S(1)}, bf16[2,6,6,2,2,4,128]{6,5,4,3,2,1,0:T(4,128)(2,1)}, u32[]{:S(2)}) copy-start(bf16[2,6,6,2,2,4,128]{6,5,4,3,2,1,0:T(4,128)(2,1)} %param.6) | copy-start | bytes 884740
  13.4 3.5 %collective-permute-start.4 = (bf16[96,128]{1,0:T(8,128)(2,1)S(1)}, bf16[96,128]{1,0:T(8,128)(2,1)S(1)}, u32[]{:S(2)}, u32[]{:S(2)}) collective-permute-start(bf16[96,128]{1,0:T(8,128)(2,1)S(1)} %get-tuple-element.41), channel_id=1, source_target_pairs={{0,3},{1,2},{2,1},{3,0},{4,7},{5,6},{6,5},{7,4},{8,11},{9,10},{10,... | collective-permute-start | bytes 73736 | tf_op jit(solution)/shard_map/ppermute | solution.py:400
  13.5 3.5 %collective-permute-start.5 = (bf16[96,128]{1,0:T(8,128)(2,1)S(1)}, bf16[96,128]{1,0:T(8,128)(2,1)S(1)}, u32[]{:S(2)}, u32[]{:S(2)}) collective-permute-start(bf16[96,128]{1,0:T(8,128)(2,1)S(1)} %get-tuple-element.42), channel_id=1, source_target_pairs={{0,1},{1,0},{2,3},{3,2},{4,5},{5,4},{6,7},{7,6},{8,9},{9,8},{10,11... | collective-permute-start | bytes 73736 | tf_op jit(solution)/shard_map/ppermute | solution.py:400
  17.7 6.2 %collective-permute-start.10 = (bf16[192,128]{1,0:T(8,128)(2,1)S(1)}, bf16[192,128]{1,0:T(8,128)(2,1)S(1)}, u32[]{:S(2)}, u32[]{:S(2)}) collective-permute-start(bf16[192,128]{1,0:T(8,128)(2,1)S(1)} %get-tuple-element.50), channel_id=1, source_target_pairs={{0,4},{1,13},{2,6},{3,15},{4,0},{5,9},{6,2},{7,11},{8,12},{9,5},{1... | collective-permute-start | bytes 147464 | tf_op jit(solution)/shard_map/ppermute | solution.py:411
  18.4 5.9 %collective-permute-start.11 = (bf16[192,128]{1,0:T(8,128)(2,1)S(1)}, bf16[192,128]{1,0:T(8,128)(2,1)S(1)}, u32[]{:S(2)}, u32[]{:S(2)}) collective-permute-start(bf16[192,128]{1,0:T(8,128)(2,1)S(1)} %get-tuple-element.51), channel_id=1, source_target_pairs={{0,12},{1,5},{2,14},{3,7},{4,8},{5,1},{6,10},{7,3},{8,4},{9,13},{1... | collective-permute-start | bytes 147464 | tf_op jit(solution)/shard_map/ppermute | solution.py:411
  20.3 3.5 %collective-permute-start.8 = (bf16[96,128]{1,0:T(8,128)(2,1)S(1)}, bf16[96,128]{1,0:T(8,128)(2,1)S(1)}, u32[]{:S(2)}, u32[]{:S(2)}) collective-permute-start(bf16[96,128]{1,0:T(8,128)(2,1)S(1)} %get-tuple-element.48), channel_id=1, source_target_pairs={{0,3},{1,2},{2,1},{3,0},{4,7},{5,6},{6,5},{7,4},{8,11},{9,10},{10,... | collective-permute-start | bytes 73736 | tf_op jit(solution)/shard_map/ppermute | solution.py:400
  20.3 3.5 %collective-permute-start.9 = (bf16[96,128]{1,0:T(8,128)(2,1)S(1)}, bf16[96,128]{1,0:T(8,128)(2,1)S(1)}, u32[]{:S(2)}, u32[]{:S(2)}) collective-permute-start(bf16[96,128]{1,0:T(8,128)(2,1)S(1)} %get-tuple-element.49), channel_id=1, source_target_pairs={{0,1},{1,0},{2,3},{3,2},{4,5},{5,4},{6,7},{7,6},{8,9},{9,8},{10,11... | collective-permute-start | bytes 73736 | tf_op jit(solution)/shard_map/ppermute | solution.py:400
  24.8 5.8 %collective-permute-start.14 = (bf16[192,128]{1,0:T(8,128)(2,1)S(1)}, bf16[192,128]{1,0:T(8,128)(2,1)S(1)}, u32[]{:S(2)}, u32[]{:S(2)}) collective-permute-start(bf16[192,128]{1,0:T(8,128)(2,1)S(1)} %get-tuple-element.57), channel_id=1, source_target_pairs={{0,4},{1,13},{2,6},{3,15},{4,0},{5,9},{6,2},{7,11},{8,12},{9,5},{1... | collective-permute-start | bytes 147464 | tf_op jit(solution)/shard_map/ppermute | solution.py:411
  24.9 6.1 %collective-permute-start.15 = (bf16[192,128]{1,0:T(8,128)(2,1)S(1)}, bf16[192,128]{1,0:T(8,128)(2,1)S(1)}, u32[]{:S(2)}, u32[]{:S(2)}) collective-permute-start(bf16[192,128]{1,0:T(8,128)(2,1)S(1)} %get-tuple-element.58), channel_id=1, source_target_pairs={{0,12},{1,5},{2,14},{3,7},{4,8},{5,1},{6,10},{7,3},{8,4},{9,13},{1... | collective-permute-start | bytes 147464 | tf_op jit(solution)/shard_map/ppermute | solution.py:411
  27.0 3.5 %collective-permute-start.12 = (bf16[96,128]{1,0:T(8,128)(2,1)S(1)}, bf16[96,128]{1,0:T(8,128)(2,1)S(1)}, u32[]{:S(2)}, u32[]{:S(2)}) collective-permute-start(bf16[96,128]{1,0:T(8,128)(2,1)S(1)} %get-tuple-element.55), channel_id=1, source_target_pairs={{0,3},{1,2},{2,1},{3,0},{4,7},{5,6},{6,5},{7,4},{8,11},{9,10},{10,... | collective-permute-start | bytes 73736 | tf_op jit(solution)/shard_map/ppermute | solution.py:400
  27.1 3.5 %collective-permute-start.13 = (bf16[96,128]{1,0:T(8,128)(2,1)S(1)}, bf16[96,128]{1,0:T(8,128)(2,1)S(1)}, u32[]{:S(2)}, u32[]{:S(2)}) collective-permute-start(bf16[96,128]{1,0:T(8,128)(2,1)S(1)} %get-tuple-element.56), channel_id=1, source_target_pairs={{0,1},{1,0},{2,3},{3,2},{4,5},{5,4},{6,7},{7,6},{8,9},{9,8},{10,11... | collective-permute-start | bytes 73736 | tf_op jit(solution)/shard_map/ppermute | solution.py:400

commit v6 on v5

--- a/solution.py
+++ b/solution.py
@@ -125,58 +125,69 @@
     return jnp.where(mask, a, b)
 
 
-def send_t(f_ref, links_ref, parity, t_one, t_two, kept, ready=lambda r: None):
+def t_edges(links):
+    t_idx, _ = site_masks()
+    return [each(lambda v: select(t_idx == 0, roll_rows(v, 4), v), row) for row in links]
+
+
+def x_edges(links):
+    _, x_idx = site_masks()
+
+    def edge(value):
+        out = value
+        for k in range(3):
+            out = select(x_idx == k, roll_rows(value, k - 3), out)
+        return out
+
+    return [each(edge, row) for row in links]
+
+
+def send_t(f_ref, links_ref, parity, t_one, t_two, ready=lambda r: None):
     even = even_device("ta", "gx")
     t_idx, _ = site_masks()
     first = t_idx == 0
-    links = load_links(links_ref, 0, parity)
+    links = t_edges(load_links(links_ref, 0, parity))
     for r in range(RHS):
         ready(r)
         field = load_field(f_ref, r)
-        ahead = project(field, 0, -1)
-        carry = color(links, project(field, 0, 1), True)
-        moved = each(lambda v: roll_rows(v, 4), ahead)
-        back = each(lambda v: roll_rows(v, 4), carry)
-        for c in range(3):
-            front = [select(first, ahead[c + 3][i], moved[c][i]) for i in range(2)]
-            rear = [select(first, back[c][i], carry[c + 3][i]) for i in range(2)]
-            store_pair(t_one, r * 3 + c, either(even, rear, front))
-            store_pair(t_two, r * 3 + c, either(even, front, rear))
-        for j in range(6):
-            store_pair(kept, r * 6 + j, back[j])
-
-
-def send_x_kernel(parity, f_ref, links_ref, x_far, x_near, kept):
+        ahead, behind = project(field, 0, -1), project(field, 0, 1)
+        rears = [
+            tuple(select(first, roll_rows(behind[c][i], 4), behind[c + 3][i]) for i in range(2)) for c in range(3)
+        ]
+        rears = matvec(links, rears, True)
+        for c in range(3):
+            front = [select(first, ahead[c + 3][i], roll_rows(ahead[c][i], 4)) for i in range(2)]
+            store_pair(t_one, r * 3 + c, either(even, rears[c], front))
+            store_pair(t_two, r * 3 + c, either(even, front, rears[c]))
+
+
+def send_x_kernel(parity, f_ref, links_ref, x_far, x_near):
     even = even_device("gx")
     _, x_idx = site_masks()
-    links = load_links(links_ref, 1, parity)
+    links = x_edges(load_links(links_ref, 1, parity))
+
+    def packed(values, row, step):
+        out = values[0]
+        for k in range(1, 4):
+            out = select(x_idx == row + step * k, roll_rows(values[k], step * k), out)
+        return out
+
     for q in range(RHS // 2):
+        fields = [load_field(f_ref, r) for r in (2 * q, 2 * q + 1)]
+        ahead = [project(field, 1, -1) for field in fields]
+        behind = [project(field, 1, 1) for field in fields]
         fronts, rears = [], []
-        for r in (2 * q, 2 * q + 1):
-            field = load_field(f_ref, r)
-            fronts.append(project(field, 1, -1))
-            rears.append(color(links, project(field, 1, 1), True))
-            for j in range(6):
-                store_pair(kept, r * 6 + j, [roll_rows(v, 1) for v in rears[-1][j]])
-        for c in range(3):
-            front, rear = [], []
-            for i in range(2):
-                group = [h[j][i] for h in fronts for j in (c, c + 3)]
-                packed = group[0]
-                for k in range(1, 4):
-                    packed = select(x_idx == k, roll_rows(group[k], k), packed)
-                front.append(packed)
-                group = [h[j][i] for h in rears for j in (c, c + 3)]
-                packed = group[0]
-                for k in range(1, 4):
-                    packed = select(x_idx == 3 - k, roll_rows(group[k], -k), packed)
-                rear.append(packed)
-            store_pair(x_near, q * 3 + c, either(even, rear, front))
-            store_pair(x_far, q * 3 + c, either(even, front, rear))
+        for c in range(3):
+            fronts.append([packed([h[j][i] for h in ahead for j in (c, c + 3)], 0, 1) for i in range(2)])
+            rears.append([packed([h[j][i] for h in behind for j in (c, c + 3)], 3, -1) for i in range(2)])
+        rears = matvec(links, rears, True)
+        for c in range(3):
+            store_pair(x_near, q * 3 + c, either(even, rears[c], fronts[c]))
+            store_pair(x_far, q * 3 + c, either(even, fronts[c], rears[c]))
 
 
 def start_kernel(f_hbm, links_hbm, *refs):
-    outs, (f_ref, links_ref, sems) = refs[:3], refs[3:]
+    outs, (f_ref, links_ref, sems) = refs[:2], refs[2:]
     part = f_ref.shape[0] // RHS
     copies = [pltpu.make_async_copy(links_hbm.at[pl.ds(0, links_ref.shape[0])], links_ref, sems.at[RHS])]
     for r in range(RHS):
@@ -190,10 +201,10 @@
 
 def interior_kernel(parity, with_base, *refs):
     if with_base:
-        f_ref, links_ref, kept_t, kept_x, base_ref, clover_ref, acc_ref = refs
+        f_ref, links_ref, base_ref, clover_ref, acc_ref = refs
         clover_to(clover_ref, lambda r: load_field(base_ref, r), acc_ref, 1.0)
     else:
-        f_ref, links_ref, kept_t, kept_x, acc_ref = refs
+        f_ref, links_ref, acc_ref = refs
     out_parity = 1 - parity
     t_idx, x_idx = site_masks()
     lane = lax.broadcasted_iota(jnp.int32, (8, 128), 1)
@@ -215,13 +226,12 @@
             behind_of = lambda v: take(v, down)
         elif mu == 0:
             ahead_of = lambda v: select(t_idx == 0, roll_rows(v, 4), 0.0)
-            behind_of = lambda v: select(t_idx == 1, v, 0.0)
+            behind_of = lambda v: select(t_idx == 1, roll_rows(v, 4), 0.0)
         else:
             ahead_of = lambda v: select(x_idx < 3, roll_rows(v, 7), 0.0)
-            behind_of = lambda v: select(x_idx > 0, v, 0.0)
+            behind_of = lambda v: select(x_idx > 0, roll_rows(v, 1), 0.0)
         links_out = load_links(links_ref, mu, out_parity)
-        if mu >= 2:
-            links_in = load_links(links_ref, mu, parity)
+        links_in = load_links(links_ref, mu, parity)
         for r in range(RHS):
             field = load_field(f_ref, r)
             if mu == 2 and not with_base:
@@ -230,10 +240,7 @@
                 acc = load_field(acc_ref, r)
             half = color(links_out, each(ahead_of, project(field, mu, -1)), False)
             acc = rebuild(acc, half, mu, -1)
-            if mu >= 2:
-                half = color(links_in, project(field, mu, 1), True)
-            else:
-                half = [load_pair(kept_t if mu == 0 else kept_x, r * 6 + j) for j in range(6)]
+            half = color(links_in, project(field, mu, 1), True)
             acc = rebuild(acc, each(behind_of, half), mu, 1)
             store_field(acc_ref, r, acc)
 
@@ -248,30 +255,37 @@
                 re, im = block[0:8], block[8:16]
                 if scale != 1.0:
                     re, im = re * scale, im * scale
-                matrix[i, j] = (re, im)
+                matrix[i, j] = (re, re + im, im - re)
         for r in range(RHS):
             field = get_field(r)[chi * 6:chi * 6 + 6]
+            both = [vr + vi for vr, vi in field]
             for i in range(6):
-                re = im = None
+                one = two = three = None
                 for j in range(6):
                     vr, vi = field[j]
-                    mr, mi = matrix[min(i, j), max(i, j)]
+                    m, plus, minus = matrix[min(i, j), max(i, j)]
+                    t_one = m * both[j]
                     if i <= j:
-                        tr, ti = mr * vr - mi * vi, mr * vi + mi * vr
+                        t_two, t_three = -(vi * plus), vr * minus
                     else:
-                        tr, ti = mr * vr + mi * vi, mr * vi - mi * vr
-                    re = tr if re is None else re + tr
-                    im = ti if im is None else im + ti
-                store_pair(out_ref, r * 12 + chi * 6 + i, (re, im))
-
-
-def matvec(links, vector):
+                        t_two, t_three = vi * minus, -(vr * plus)
+                    one = t_one if one is None else one + t_one
+                    two = t_two if two is None else two + t_two
+                    three = t_three if three is None else three + t_three
+                store_pair(out_ref, r * 12 + chi * 6 + i, (one + two, one + three))
+
+
+def matvec(links, vector, adjoint):
     out = []
     for a in range(3):
         re = im = None
         for b in range(3):
-            (lr, li), (vr, vi) = links[a][b], vector[b]
-            tr, ti = lr * vr - li * vi, lr * vi + li * vr
+            lr, li = links[b][a] if adjoint else links[a][b]
+            vr, vi = vector[b]
+            if adjoint:
+                tr, ti = lr * vr + li * vi, lr * vi - li * vr
+            else:
+                tr, ti = lr * vr - li * vi, lr * vi + li * vr
             re = tr if re is None else re + tr
             im = ti if im is None else im + ti
         out.append((re, im))
@@ -295,21 +309,14 @@
     even = even_device("gx")
     _, x_idx = site_masks()
     sign = jnp.where(x_idx == 3, -1.0, 1.0).astype(F32)
-    links = load_links(links_ref, 1, 1 - parity)
-
-    def edge(value):
-        for k in range(3):
-            value = select(x_idx == k, roll_rows(value, k - 3), value)
-        return value
-
-    links = [each(edge, row) for row in links]
+    links = x_edges(load_links(links_ref, 1, 1 - parity))
     for q in range(RHS // 2):
         nxt, last = [], []
         for c in range(3):
             near, far = load_pair(x_near, q * 3 + c), load_pair(x_far, q * 3 + c)
             nxt.append(either(even, near, far))
             last.append(either(even, far, near))
-        ahead = matvec(links, nxt)
+        ahead = matvec(links, nxt, False)
         for r in (2 * q, 2 * q + 1):
             half = [None] * 6
             for s in range(2):
@@ -331,15 +338,14 @@
     t_idx, _ = site_masks()
     first = t_idx == 0
     sign = jnp.where(first, 1.0, -1.0).astype(F32)
-    links = load_links(links_ref, 0, 1 - parity)
-    links = [each(lambda v: select(first, roll_rows(v, 4), v), row) for row in links]
+    links = t_edges(load_links(links_ref, 0, 1 - parity))
     for r in range(RHS):
         nxt, last = [], []
         for c in range(3):
             one, two = load_pair(t_one, r * 3 + c), load_pair(t_two, r * 3 + c)
             nxt.append(either(even, one, two))
             last.append(either(even, two, one))
-        ahead = matvec(links, nxt)
+        ahead = matvec(links, nxt, False)
         half = [tuple(select(first, last[c][i], ahead[c][i]) for i in range(2)) for c in range(3)]
         half += [
             tuple(roll_rows(select(first, ahead[c][i], last[c][i]), 4) for i in range(2)) for c in range(3)
@@ -349,7 +355,7 @@
 
 
 def odd_kernel(links_ref, clover_ref, acc_ref, t_one, t_two, out_ref, *refs):
-    outs, summed = refs[:3], refs[3]
+    outs, summed = refs[:2], refs[2]
     join_t(links_ref, acc_ref, t_one, t_two, 0, summed)
     clover_to(clover_ref, lambda r: load_field(summed, r), out_ref, -KAPPA2)
     send_t(out_ref, links_ref, 1, *outs)
@@ -376,7 +382,6 @@
 
 ROWS = RHS * 24 * 8
 FIELD = [((ROWS, 128), F32)]
-KEPT = [((RHS * 12 * 8, 128), F32)]
 T_HALOS = [((RHS * 3 * 16, 128), BF16)] * 2
 X_HALOS = [((RHS * 3 * 8, 128), BF16)] * 2
 
@@ -423,29 +428,30 @@
         pltpu.VMEM((links.shape[0] // 4, 128), BF16),
         pltpu.SemaphoreType.DMA((RHS + 1,)),
     ]
-    t_one, t_two, kept_t = call(start_kernel, held, T_HALOS + KEPT, 1_500_000, start_scratch, in_space=pltpu.HBM)
+    t_one, t_two = call(start_kernel, held, T_HALOS, 1_500_000, start_scratch, in_space=pltpu.HBM)
     for hop in range(4):
         parity = hop % 2
         t_one, t_two = swap_t(t_one, True), swap_t(t_two, False)
-        x_far, x_near, kept_x = call(
-            functools.partial(send_x_kernel, parity), (f, links), X_HALOS + KEPT, 1_500_000
+        x_far, x_near = call(
+            functools.partial(send_x_kernel, parity), (f, links), X_HALOS, 1_500_000
         )
+        here, x_far, x_near = lax.optimization_barrier((f, x_far, x_near))
         x_far, x_near = swap(x_far, "gx", True), swap(x_near, "gx", False)
         base = (before, even) if parity else ()
         acc, = call(
             functools.partial(interior_kernel, parity, bool(parity)),
-            (f, links, kept_t, kept_x, *base), FIELD, 8_000_000 if parity else 5_000_000,
+            (here, links, *base), FIELD, 8_000_000 if parity else 5_000_000,
         )
         acc, = call(functools.partial(join_x_kernel, parity), (links, acc, x_far, x_near), FIELD, 1_000_000)
         before = f
         if parity == 0:
-            f, t_one, t_two, kept_t = call(
-                odd_kernel, (links, odd, acc, t_one, t_two), FIELD + T_HALOS + KEPT, 4_000_000,
+            f, t_one, t_two = call(
+                odd_kernel, (links, odd, acc, t_one, t_two), FIELD + T_HALOS, 4_000_000,
                 [pltpu.VMEM((ROWS, 128), F32)],
             )
         elif hop == 1:
-            f, t_one, t_two, kept_t = call(
-                even_kernel, (links, acc, t_one, t_two), FIELD + T_HALOS + KEPT, 2_000_000
+            f, t_one, t_two = call(
+                even_kernel, (links, acc, t_one, t_two), FIELD + T_HALOS, 2_000_000
             )
         else:
             out, = call(

time: 31.8 us -> 31.6 us (level)
  waiting for transfers between devices: 5.34 us -> 4.79 us
  Pallas kernels: 7.25 us -> 7.58 us
    ppermute x8, waiting for transfers between devices: 4.19 us -> 3.6 us  [swap(): return lax.ppermute(value, axis, pairs)]
    pallas_call x17, Pallas kernels: 7.25 us -> 7.58 us  [call(): pl.pallas_call(kernel, out_shape=tuple((jax.ShapeDtypeStruct(shape, dtype...]
  transfers between devices with their start and end apart: 16 -> 16, of which waited for: 7 -> 7; matrix products, arithmetic and copies ran while one was open for 0% -> 0% of each run, Pallas kernels for 13% -> 15%
where the time goes in v6:
time: 31.6 us; the launch traced here: 31.5 us
  starting transfers between devices  18.9 us (60%)
  Pallas kernels  7.58 us (24%)
  waiting for transfers between devices  4.79 us (15%)
    ppermute x8, starting transfers between devices, swap_t(): return lax.ppermute(value, ('ta', 'gx'), pairs)  12.3 us
    pallas_call x17, Pallas kernels, call(): pl.pallas_call(kernel, out_shape=tuple((jax.ShapeDtypeStruct(shape, dtype...  7.58 us
    ppermute x8, starting transfers between devices, swap(): return lax.ppermute(value, axis, pairs)  6.59 us
    ppermute x8, waiting for transfers between devices, swap(): return lax.ppermute(value, axis, pairs)  3.6 us
    ppermute x8, waiting for transfers between devices, swap_t(): return lax.ppermute(value, ('ta', 'gx'), pairs)  1.18 us
  transfers between devices with their start and end apart: 16, of which 7 were waited for; matrix products, arithmetic and copies ran while one was open for 0% of the time, Pallas kernels for 15%

profile of v6, /device:TPU:0, one launch (start us, length us, event | category | flops | bytes accessed | tf_op | source)
XLA Modules:
  0.0 31.5 jit_solution(13666766230985588386)
XLA Ops:
  0.0 1.1 %shard_map.49 = (bf16[192,128]{1,0:T(8,128)(2,1)S(1)}, bf16[192,128]{1,0:T(8,128)(2,1)S(1)}) custom-call(bf16[768,128]{1,0:T(8,128)(2,1)} %bitcast.22, bf16[1152,128]{1,0:T(8,128)(2,1)} %bitcast.5), custom_call_target="tpu_custom_call" | custom-call | flops 1500000 | bytes 2097152 | tf_op jit(solution)/shard_map/pallas_call | solution.py:390
  1.1 3.1 %collective-permute-start.2 = (bf16[192,128]{1,0:T(8,128)(2,1)S(1)}, bf16[192,128]{1,0:T(8,128)(2,1)S(1)}, u32[]{:S(2)}, u32[]{:S(2)}) collective-permute-start(bf16[192,128]{1,0:T(8,128)(2,1)S(1)} %get-tuple-element.41), channel_id=1, source_target_pairs={{0,4},{1,13},{2,6},{3,15},{4,0},{5,9},{6,2},{7,11},{8,12},{9,5},{1... | collective-permute-start | bytes 147464 | tf_op jit(solution)/shard_map/ppermute | solution.py:416
  4.2 2.5 %collective-permute-start.3 = (bf16[192,128]{1,0:T(8,128)(2,1)S(1)}, bf16[192,128]{1,0:T(8,128)(2,1)S(1)}, u32[]{:S(2)}, u32[]{:S(2)}) collective-permute-start(bf16[192,128]{1,0:T(8,128)(2,1)S(1)} %get-tuple-element.42), channel_id=1, source_target_pairs={{0,12},{1,5},{2,14},{3,7},{4,8},{5,1},{6,10},{7,3},{8,4},{9,13},{1... | collective-permute-start | bytes 147464 | tf_op jit(solution)/shard_map/ppermute | solution.py:416
  6.7 0.1 shard_map.46
  6.8 0.3 collective-permute-start
  7.1 1.4 %collective-permute-start.1 = (bf16[96,128]{1,0:T(8,128)(2,1)S(1)}, bf16[96,128]{1,0:T(8,128)(2,1)S(1)}, u32[]{:S(2)}, u32[]{:S(2)}) collective-permute-start(bf16[96,128]{1,0:T(8,128)(2,1)S(1)} %get-tuple-element.40), channel_id=1, source_target_pairs={{0,1},{1,0},{2,3},{3,2},{4,5},{5,4},{6,7},{7,6},{8,9},{9,8},{10,11... | collective-permute-start | bytes 73736 | tf_op jit(solution)/shard_map/ppermute | solution.py:405
  8.5 0.9 %shard_map.47.acc_ref = f32[768,128]{1,0:T(8,128)S(1)} custom-call(bf16[768,128]{1,0:T(8,128)(2,1)S(1)} %bitcast.24, bf16[1152,128]{1,0:T(8,128)(2,1)S(1)} %bitcast.7), custom_call_target="tpu_custom_call" | custom-call | flops 5000000 | bytes 2097152 | tf_op jit(solution)/shard_map/pallas_call | solution.py:390
  9.3 0.0 copy-start.3
  9.3 1.0 %collective-permute-done.x_far = bf16[96,128]{1,0:T(8,128)(2,1)S(1)} collective-permute-done((bf16[96,128]{1,0:T(8,128)(2,1)S(1)}, bf16[96,128]{1,0:T(8,128)(2,1)S(1)}, u32[]{:S(2)}, u32[]{:S(2)}) %collective-permute-start) | collective-permute-done | bytes 24608 | tf_op jit(solution)/shard_map/ppermute | solution.py:405
  10.3 0.0 collective-permute-done.1.x_near
  10.3 0.1 shard_map.48.acc_ref
  10.4 0.0 collective-permute-done.2.t_one
  10.4 0.0 collective-permute-done.3.t_two
  10.5 0.5 %shard_map.50 = (f32[768,128]{1,0:T(8,128)S(1)}, bf16[192,128]{1,0:T(8,128)(2,1)S(1)}, bf16[192,128]{1,0:T(8,128)(2,1)S(1)}) custom-call(bf16[1152,128]{1,0:T(8,128)(2,1)S(1)} %bitcast.9, bf16[1152,128]{1,0:T(8,128)(2,1)S(1)} %bitcast.28, f32[768,128]{1,0:T(8,128)S(1)} %shard_map.48.acc_ref, bf16[192,128]{1,0:T(8,128)(2,1)S(1)} %collective-permute-done.2.t_one, ...), custom_call_target="tpu_custom_call" | custom-call | flops 4000000 | bytes 2097152 | tf_op jit(solution)/shard_map/pallas_call | solution.py:390
  10.9 0.6 %collective-permute-start.6 = (bf16[192,128]{1,0:T(8,128)(2,1)S(1)}, bf16[192,128]{1,0:T(8,128)(2,1)S(1)}, u32[]{:S(2)}, u32[]{:S(2)}) collective-permute-start(bf16[192,128]{1,0:T(8,128)(2,1)S(1)} %get-tuple-element.49), channel_id=1, source_target_pairs={{0,4},{1,13},{2,6},{3,15},{4,0},{5,9},{6,2},{7,11},{8,12},{9,5},{1... | collective-permute-start | bytes 147464 | tf_op jit(solution)/shard_map/ppermute | solution.py:416
  11.5 1.7 %collective-permute-start.7 = (bf16[192,128]{1,0:T(8,128)(2,1)S(1)}, bf16[192,128]{1,0:T(8,128)(2,1)S(1)}, u32[]{:S(2)}, u32[]{:S(2)}) collective-permute-start(bf16[192,128]{1,0:T(8,128)(2,1)S(1)} %get-tuple-element.50), channel_id=1, source_target_pairs={{0,12},{1,5},{2,14},{3,7},{4,8},{5,1},{6,10},{7,3},{8,4},{9,13},{1... | collective-permute-start | bytes 147464 | tf_op jit(solution)/shard_map/ppermute | solution.py:416
  13.2 0.1 shard_map.51
  13.3 0.1 collective-permute-start.4
  13.4 1.6 %collective-permute-start.5 = (bf16[96,128]{1,0:T(8,128)(2,1)S(1)}, bf16[96,128]{1,0:T(8,128)(2,1)S(1)}, u32[]{:S(2)}, u32[]{:S(2)}) collective-permute-start(bf16[96,128]{1,0:T(8,128)(2,1)S(1)} %get-tuple-element.48), channel_id=1, source_target_pairs={{0,1},{1,0},{2,3},{3,2},{4,5},{5,4},{6,7},{7,6},{8,9},{9,8},{10,11... | collective-permute-start | bytes 73736 | tf_op jit(solution)/shard_map/ppermute | solution.py:405
  15.0 1.1 %shard_map.52.acc_ref = f32[768,128]{1,0:T(8,128)S(1)} custom-call(f32[768,128]{1,0:T(8,128)S(1)} %get-tuple-element.46.f_ref.refs_0_, bf16[1152,128]{1,0:T(8,128)(2,1)S(1)} %bitcast.11, bf16[768,128]{1,0:T(8,128)(2,1)S(1)} %bitcast.25, bf16[1152,128]{1,0:T(8,128)(2,1)S(1)} %bitcast.26), custom_call_target="tpu_custom_call" | custom-call | flops 8000000 | bytes 2097152 | tf_op jit(solution)/shard_map/pallas_call | solution.py:390
  16.1 0.7 %collective-permute-done.4.x_far = bf16[96,128]{1,0:T(8,128)(2,1)S(1)} collective-permute-done((bf16[96,128]{1,0:T(8,128)(2,1)S(1)}, bf16[96,128]{1,0:T(8,128)(2,1)S(1)}, u32[]{:S(2)}, u32[]{:S(2)}) %collective-permute-start.4) | collective-permute-done | bytes 24608 | tf_op jit(solution)/shard_map/ppermute | solution.py:405
  16.8 0.0 collective-permute-done.5.x_near
  16.8 0.1 shard_map.53.acc_ref
  16.9 0.5 %collective-permute-done.7.t_two = bf16[192,128]{1,0:T(8,128)(2,1)S(1)} collective-permute-done((bf16[192,128]{1,0:T(8,128)(2,1)S(1)}, bf16[192,128]{1,0:T(8,128)(2,1)S(1)}, u32[]{:S(2)}, u32[]{:S(2)}) %collective-permute-start.7) | collective-permute-done | bytes 49184 | tf_op jit(solution)/shard_map/ppermute | solution.py:416
  17.4 0.2 shard_map.54
  17.6 0.7 %collective-permute-start.10 = (bf16[192,128]{1,0:T(8,128)(2,1)S(1)}, bf16[192,128]{1,0:T(8,128)(2,1)S(1)}, u32[]{:S(2)}, u32[]{:S(2)}) collective-permute-start(bf16[192,128]{1,0:T(8,128)(2,1)S(1)} %get-tuple-element.57), channel_id=1, source_target_pairs={{0,4},{1,13},{2,6},{3,15},{4,0},{5,9},{6,2},{7,11},{8,12},{9,5},{1... | collective-permute-start | bytes 147464 | tf_op jit(solution)/shard_map/ppermute | solution.py:416
  18.2 1.8 %collective-permute-start.11 = (bf16[192,128]{1,0:T(8,128)(2,1)S(1)}, bf16[192,128]{1,0:T(8,128)(2,1)S(1)}, u32[]{:S(2)}, u32[]{:S(2)}) collective-permute-start(bf16[192,128]{1,0:T(8,128)(2,1)S(1)} %get-tuple-element.58), channel_id=1, source_target_pairs={{0,12},{1,5},{2,14},{3,7},{4,8},{5,1},{6,10},{7,3},{8,4},{9,13},{1... | collective-permute-start | bytes 147464 | tf_op jit(solution)/shard_map/ppermute | solution.py:416
  20.0 0.1 shard_map.55
  20.1 0.1 collective-permute-start.8
  20.2 1.6 %collective-permute-start.9 = (bf16[96,128]{1,0:T(8,128)(2,1)S(1)}, bf16[96,128]{1,0:T(8,128)(2,1)S(1)}, u32[]{:S(2)}, u32[]{:S(2)}) collective-permute-start(bf16[96,128]{1,0:T(8,128)(2,1)S(1)} %get-tuple-element.56), channel_id=1, source_target_pairs={{0,1},{1,0},{2,3},{3,2},{4,5},{5,4},{6,7},{7,6},{8,9},{9,8},{10,11... | collective-permute-start | bytes 73736 | tf_op jit(solution)/shard_map/ppermute | solution.py:405
  21.8 0.8 %shard_map.56.acc_ref = f32[768,128]{1,0:T(8,128)S(1)} custom-call(f32[768,128]{1,0:T(8,128)S(1)} %get-tuple-element.54.f_ref.refs_0_.refs_2_, bf16[1152,128]{1,0:T(8,128)(2,1)S(1)} %bitcast.15), custom_call_target="tpu_custom_call" | custom-call | flops 5000000 | bytes 2097152 | tf_op jit(solution)/shard_map/pallas_call | solution.py:390
  22.6 1.1 %collective-permute-done.8.x_far = bf16[96,128]{1,0:T(8,128)(2,1)S(1)} collective-permute-done((bf16[96,128]{1,0:T(8,128)(2,1)S(1)}, bf16[96,128]{1,0:T(8,128)(2,1)S(1)}, u32[]{:S(2)}, u32[]{:S(2)}) %collective-permute-start.8) | collective-permute-done | bytes 24608 | tf_op jit(solution)/shard_map/ppermute | solution.py:405
  23.6 0.0 collective-permute-done.9.x_near
  23.6 0.1 shard_map.57.acc_ref
  23.7 0.0 collective-permute-done.10.t_one
  23.7 0.4 %collective-permute-done.11.t_two = bf16[192,128]{1,0:T(8,128)(2,1)S(1)} collective-permute-done((bf16[192,128]{1,0:T(8,128)(2,1)S(1)}, bf16[192,128]{1,0:T(8,128)(2,1)S(1)}, u32[]{:S(2)}, u32[]{:S(2)}) %collective-permute-start.11) | collective-permute-done | bytes 49184 | tf_op jit(solution)/shard_map/ppermute | solution.py:416
  24.1 0.5 %shard_map.58 = (f32[768,128]{1,0:T(8,128)S(1)}, bf16[192,128]{1,0:T(8,128)(2,1)S(1)}, bf16[192,128]{1,0:T(8,128)(2,1)S(1)}) custom-call(bf16[1152,128]{1,0:T(8,128)(2,1)S(1)} %bitcast.17, bf16[1152,128]{1,0:T(8,128)(2,1)S(1)} %bitcast.29, f32[768,128]{1,0:T(8,128)S(1)} %shard_map.57.acc_ref, bf16[192,128]{1,0:T(8,128)(2,1)S(1)} %collective-permute-done.10.t_one, ...), custom_call_target="tpu_custom_call" | custom-call | flops 4000000 | bytes 2097152 | tf_op jit(solution)/shard_map/pallas_call | solution.py:390
  24.6 0.1 collective-permute-start.14
  24.7 2.0 %collective-permute-start.15 = (bf16[192,128]{1,0:T(8,128)(2,1)S(1)}, bf16[192,128]{1,0:T(8,128)(2,1)S(1)}, u32[]{:S(2)}, u32[]{:S(2)}) collective-permute-start(bf16[192,128]{1,0:T(8,128)(2,1)S(1)} %get-tuple-element.66), channel_id=1, source_target_pairs={{0,12},{1,5},{2,14},{3,7},{4,8},{5,1},{6,10},{7,3},{8,4},{9,13},{1... | collective-permute-start | bytes 147464 | tf_op jit(solution)/shard_map/ppermute | solution.py:416
  26.7 0.1 shard_map.59
  26.8 0.1 collective-permute-start.12
  26.8 1.5 %collective-permute-start.13 = (bf16[96,128]{1,0:T(8,128)(2,1)S(1)}, bf16[96,128]{1,0:T(8,128)(2,1)S(1)}, u32[]{:S(2)}, u32[]{:S(2)}) collective-permute-start(bf16[96,128]{1,0:T(8,128)(2,1)S(1)} %get-tuple-element.64), channel_id=1, source_target_pairs={{0,1},{1,0},{2,3},{3,2},{4,5},{5,4},{6,7},{7,6},{8,9},{9,8},{10,11... | collective-permute-start | bytes 73736 | tf_op jit(solution)/shard_map/ppermute | solution.py:405
  28.4 1.1 %shard_map.60.acc_ref = f32[768,128]{1,0:T(8,128)S(1)} custom-call(f32[768,128]{1,0:T(8,128)S(1)} %get-tuple-element.62.f_ref.refs_0_, bf16[1152,128]{1,0:T(8,128)(2,1)S(1)} %bitcast.19, f32[768,128]{1,0:T(8,128)S(1)} %get-tuple-element.54.f_ref.refs_0_.refs_2_, bf16[1152,128]{1,0:T(8,128)(2,1)S(1)} %bitcast.27), custom_call_target="tpu_custom_call" | custom-call | flops 8000000 | bytes 2097152 | tf_op jit(solution)/shard_map/pallas_call | solution.py:390
  29.5 0.8 %collective-permute-done.12.x_far = bf16[96,128]{1,0:T(8,128)(2,1)S(1)} collective-permute-done((bf16[96,128]{1,0:T(8,128)(2,1)S(1)}, bf16[96,128]{1,0:T(8,128)(2,1)S(1)}, u32[]{:S(2)}, u32[]{:S(2)}) %collective-permute-start.12) | collective-permute-done | bytes 24608 | tf_op jit(solution)/shard_map/ppermute | solution.py:405
  30.3 0.1 shard_map.61.acc_ref
  30.4 0.0 collective-permute-done.14.t_one
  30.4 0.3 collective-permute-done.15.t_two
  30.7 0.8 %shard_map.62 = bf16[768,128]{1,0:T(8,128)(2,1)} custom-call(bf16[1152,128]{1,0:T(8,128)(2,1)S(1)} %bitcast.21, f32[768,128]{1,0:T(8,128)S(1)} %shard_map.61.acc_ref, bf16[192,128]{1,0:T(8,128)(2,1)S(1)} %collective-permute-done.14.t_one, bf16[192,128]{1,0:T(8,128)(2,1)S(1)} %collective-permute-done.15.t_two), custom_call_target="tpu_custom_call" | custom-call | flops 1000000 | bytes 2097152 | tf_op jit(solution)/shard_map/pallas_call | solution.py:390
  (9 shorter events, 0.0 us)
Async XLA Ops:
  0.0 6.7 %copy-start = (bf16[4,3,3,2,2,2,4,128]{7,6,5,4,3,2,1,0:T(4,128)(2,1)S(1)}, bf16[4,3,3,2,2,2,4,128]{7,6,5,4,3,2,1,0:T(4,128)(2,1)}, u32[]{:S(2)}) copy-start(bf16[4,3,3,2,2,2,4,128]{7,6,5,4,3,2,1,0:T(4,128)(2,1)} %param.5) | copy-start | bytes 884740
  0.0 6.7 %copy-start.1 = (bf16[4,4,3,2,2,4,128]{6,5,4,3,2,1,0:T(4,128)(2,1)S(1)}, bf16[4,4,3,2,2,4,128]{6,5,4,3,2,1,0:T(4,128)(2,1)}, u32[]{:S(2)}) copy-start(bf16[4,4,3,2,2,4,128]{6,5,4,3,2,1,0:T(4,128)(2,1)} %param.4) | copy-start | bytes 589828
  1.1 9.3 %collective-permute-start.2 = (bf16[192,128]{1,0:T(8,128)(2,1)S(1)}, bf16[192,128]{1,0:T(8,128)(2,1)S(1)}, u32[]{:S(2)}, u32[]{:S(2)}) collective-permute-start(bf16[192,128]{1,0:T(8,128)(2,1)S(1)} %get-tuple-element.41), channel_id=1, source_target_pairs={{0,4},{1,13},{2,6},{3,15},{4,0},{5,9},{6,2},{7,11},{8,12},{9,5},{1... | collective-permute-start | bytes 147464 | tf_op jit(solution)/shard_map/ppermute | solution.py:416
  4.2 6.2 %collective-permute-start.3 = (bf16[192,128]{1,0:T(8,128)(2,1)S(1)}, bf16[192,128]{1,0:T(8,128)(2,1)S(1)}, u32[]{:S(2)}, u32[]{:S(2)}) collective-permute-start(bf16[192,128]{1,0:T(8,128)(2,1)S(1)} %get-tuple-element.42), channel_id=1, source_target_pairs={{0,12},{1,5},{2,14},{3,7},{4,8},{5,1},{6,10},{7,3},{8,4},{9,13},{1... | collective-permute-start | bytes 147464 | tf_op jit(solution)/shard_map/ppermute | solution.py:416
  6.8 3.5 %collective-permute-start = (bf16[96,128]{1,0:T(8,128)(2,1)S(1)}, bf16[96,128]{1,0:T(8,128)(2,1)S(1)}, u32[]{:S(2)}, u32[]{:S(2)}) collective-permute-start(bf16[96,128]{1,0:T(8,128)(2,1)S(1)} %get-tuple-element.39), channel_id=1, source_target_pairs={{0,3},{1,2},{2,1},{3,0},{4,7},{5,6},{6,5},{7,4},{8,11},{9,10},{10,... | collective-permute-start | bytes 73736 | tf_op jit(solution)/shard_map/ppermute | solution.py:405
  7.1 3.3 %collective-permute-start.1 = (bf16[96,128]{1,0:T(8,128)(2,1)S(1)}, bf16[96,128]{1,0:T(8,128)(2,1)S(1)}, u32[]{:S(2)}, u32[]{:S(2)}) collective-permute-start(bf16[96,128]{1,0:T(8,128)(2,1)S(1)} %get-tuple-element.40), channel_id=1, source_target_pairs={{0,1},{1,0},{2,3},{3,2},{4,5},{5,4},{6,7},{7,6},{8,9},{9,8},{10,11... | collective-permute-start | bytes 73736 | tf_op jit(solution)/shard_map/ppermute | solution.py:405
  9.3 1.1 %copy-start.3 = (bf16[2,6,6,2,2,4,128]{6,5,4,3,2,1,0:T(4,128)(2,1)S(1)}, bf16[2,6,6,2,2,4,128]{6,5,4,3,2,1,0:T(4,128)(2,1)}, u32[]{:S(2)}) copy-start(bf16[2,6,6,2,2,4,128]{6,5,4,3,2,1,0:T(4,128)(2,1)} %param.7) | copy-start | bytes 884740
  10.9 6.0 %collective-permute-start.6 = (bf16[192,128]{1,0:T(8,128)(2,1)S(1)}, bf16[192,128]{1,0:T(8,128)(2,1)S(1)}, u32[]{:S(2)}, u32[]{:S(2)}) collective-permute-start(bf16[192,128]{1,0:T(8,128)(2,1)S(1)} %get-tuple-element.49), channel_id=1, source_target_pairs={{0,4},{1,13},{2,6},{3,15},{4,0},{5,9},{6,2},{7,11},{8,12},{9,5},{1... | collective-permute-start | bytes 147464 | tf_op jit(solution)/shard_map/ppermute | solution.py:416
  11.5 5.9 %collective-permute-start.7 = (bf16[192,128]{1,0:T(8,128)(2,1)S(1)}, bf16[192,128]{1,0:T(8,128)(2,1)S(1)}, u32[]{:S(2)}, u32[]{:S(2)}) collective-permute-start(bf16[192,128]{1,0:T(8,128)(2,1)S(1)} %get-tuple-element.50), channel_id=1, source_target_pairs={{0,12},{1,5},{2,14},{3,7},{4,8},{5,1},{6,10},{7,3},{8,4},{9,13},{1... | collective-permute-start | bytes 147464 | tf_op jit(solution)/shard_map/ppermute | solution.py:416
  13.2 1.8 %copy-start.2 = (bf16[2,6,6,2,2,4,128]{6,5,4,3,2,1,0:T(4,128)(2,1)S(1)}, bf16[2,6,6,2,2,4,128]{6,5,4,3,2,1,0:T(4,128)(2,1)}, u32[]{:S(2)}) copy-start(bf16[2,6,6,2,2,4,128]{6,5,4,3,2,1,0:T(4,128)(2,1)} %param.6) | copy-start | bytes 884740
  13.3 3.5 %collective-permute-start.4 = (bf16[96,128]{1,0:T(8,128)(2,1)S(1)}, bf16[96,128]{1,0:T(8,128)(2,1)S(1)}, u32[]{:S(2)}, u32[]{:S(2)}) collective-permute-start(bf16[96,128]{1,0:T(8,128)(2,1)S(1)} %get-tuple-element.47), channel_id=1, source_target_pairs={{0,3},{1,2},{2,1},{3,0},{4,7},{5,6},{6,5},{7,4},{8,11},{9,10},{10,... | collective-permute-start | bytes 73736 | tf_op jit(solution)/shard_map/ppermute | solution.py:405
  13.4 3.5 %collective-permute-start.5 = (bf16[96,128]{1,0:T(8,128)(2,1)S(1)}, bf16[96,128]{1,0:T(8,128)(2,1)S(1)}, u32[]{:S(2)}, u32[]{:S(2)}) collective-permute-start(bf16[96,128]{1,0:T(8,128)(2,1)S(1)} %get-tuple-element.48), channel_id=1, source_target_pairs={{0,1},{1,0},{2,3},{3,2},{4,5},{5,4},{6,7},{7,6},{8,9},{9,8},{10,11... | collective-permute-start | bytes 73736 | tf_op jit(solution)/shard_map/ppermute | solution.py:405
  17.6 6.1 %collective-permute-start.10 = (bf16[192,128]{1,0:T(8,128)(2,1)S(1)}, bf16[192,128]{1,0:T(8,128)(2,1)S(1)}, u32[]{:S(2)}, u32[]{:S(2)}) collective-permute-start(bf16[192,128]{1,0:T(8,128)(2,1)S(1)} %get-tuple-element.57), channel_id=1, source_target_pairs={{0,4},{1,13},{2,6},{3,15},{4,0},{5,9},{6,2},{7,11},{8,12},{9,5},{1... | collective-permute-start | bytes 147464 | tf_op jit(solution)/shard_map/ppermute | solution.py:416
  18.2 5.9 %collective-permute-start.11 = (bf16[192,128]{1,0:T(8,128)(2,1)S(1)}, bf16[192,128]{1,0:T(8,128)(2,1)S(1)}, u32[]{:S(2)}, u32[]{:S(2)}) collective-permute-start(bf16[192,128]{1,0:T(8,128)(2,1)S(1)} %get-tuple-element.58), channel_id=1, source_target_pairs={{0,12},{1,5},{2,14},{3,7},{4,8},{5,1},{6,10},{7,3},{8,4},{9,13},{1... | collective-permute-start | bytes 147464 | tf_op jit(solution)/shard_map/ppermute | solution.py:416
  20.1 3.5 %collective-permute-start.8 = (bf16[96,128]{1,0:T(8,128)(2,1)S(1)}, bf16[96,128]{1,0:T(8,128)(2,1)S(1)}, u32[]{:S(2)}, u32[]{:S(2)}) collective-permute-start(bf16[96,128]{1,0:T(8,128)(2,1)S(1)} %get-tuple-element.55), channel_id=1, source_target_pairs={{0,3},{1,2},{2,1},{3,0},{4,7},{5,6},{6,5},{7,4},{8,11},{9,10},{10,... | collective-permute-start | bytes 73736 | tf_op jit(solution)/shard_map/ppermute | solution.py:405
  20.2 3.5 %collective-permute-start.9 = (bf16[96,128]{1,0:T(8,128)(2,1)S(1)}, bf16[96,128]{1,0:T(8,128)(2,1)S(1)}, u32[]{:S(2)}, u32[]{:S(2)}) collective-permute-start(bf16[96,128]{1,0:T(8,128)(2,1)S(1)} %get-tuple-element.56), channel_id=1, source_target_pairs={{0,1},{1,0},{2,3},{3,2},{4,5},{5,4},{6,7},{7,6},{8,9},{9,8},{10,11... | collective-permute-start | bytes 73736 | tf_op jit(solution)/shard_map/ppermute | solution.py:405
  24.6 5.8 %collective-permute-start.14 = (bf16[192,128]{1,0:T(8,128)(2,1)S(1)}, bf16[192,128]{1,0:T(8,128)(2,1)S(1)}, u32[]{:S(2)}, u32[]{:S(2)}) collective-permute-start(bf16[192,128]{1,0:T(8,128)(2,1)S(1)} %get-tuple-element.65), channel_id=1, source_target_pairs={{0,4},{1,13},{2,6},{3,15},{4,0},{5,9},{6,2},{7,11},{8,12},{9,5},{1... | collective-permute-start | bytes 147464 | tf_op jit(solution)/shard_map/ppermute | solution.py:416
  24.7 6.1 %collective-permute-start.15 = (bf16[192,128]{1,0:T(8,128)(2,1)S(1)}, bf16[192,128]{1,0:T(8,128)(2,1)S(1)}, u32[]{:S(2)}, u32[]{:S(2)}) collective-permute-start(bf16[192,128]{1,0:T(8,128)(2,1)S(1)} %get-tuple-element.66), channel_id=1, source_target_pairs={{0,12},{1,5},{2,14},{3,7},{4,8},{5,1},{6,10},{7,3},{8,4},{9,13},{1... | collective-permute-start | bytes 147464 | tf_op jit(solution)/shard_map/ppermute | solution.py:416
  26.8 3.6 %collective-permute-start.12 = (bf16[96,128]{1,0:T(8,128)(2,1)S(1)}, bf16[96,128]{1,0:T(8,128)(2,1)S(1)}, u32[]{:S(2)}, u32[]{:S(2)}) collective-permute-start(bf16[96,128]{1,0:T(8,128)(2,1)S(1)} %get-tuple-element.63), channel_id=1, source_target_pairs={{0,3},{1,2},{2,1},{3,0},{4,7},{5,6},{6,5},{7,4},{8,11},{9,10},{10,... | collective-permute-start | bytes 73736 | tf_op jit(solution)/shard_map/ppermute | solution.py:405
  26.8 3.5 %collective-permute-start.13 = (bf16[96,128]{1,0:T(8,128)(2,1)S(1)}, bf16[96,128]{1,0:T(8,128)(2,1)S(1)}, u32[]{:S(2)}, u32[]{:S(2)}) collective-permute-start(bf16[96,128]{1,0:T(8,128)(2,1)S(1)} %get-tuple-element.64), channel_id=1, source_target_pairs={{0,1},{1,0},{2,3},{3,2},{4,5},{5,4},{6,7},{7,6},{8,9},{9,8},{10,11... | collective-permute-start | bytes 73736 | tf_op jit(solution)/shard_map/ppermute | solution.py:405

commit v7 on v6

--- a/solution.py
+++ b/solution.py
@@ -143,7 +143,7 @@
 
 
 def send_t(f_ref, links_ref, parity, t_one, t_two, ready=lambda r: None):
-    even = even_device("ta", "gx")
+    even = even_device("ta")
     t_idx, _ = site_masks()
     first = t_idx == 0
     links = t_edges(load_links(links_ref, 0, parity))
@@ -333,10 +333,19 @@
             store_field(out_ref, r, rebuild_signed(load_field(acc_ref, r), half, 1, sign))
 
 
-def join_t(links_ref, acc_ref, t_one, t_two, parity, out_ref, done=lambda r: None):
-    even = even_device("ta", "gx")
+def join_t(links_ref, acc_ref, one_hbm, two_hbm, parity, out_ref, t_one, t_two, sems, done=lambda r: None):
+    even = even_device("ta")
     t_idx, _ = site_masks()
     first = t_idx == 0
+    part = t_one.shape[0]
+    place = lax.axis_index("ta") % 2
+    copies = []
+    for i, (source, slot, held) in enumerate(((one_hbm, 1 - place, t_one), (two_hbm, place, t_two))):
+        rows = pl.ds(pl.multiple_of(slot * part, part), part)
+        copies.append(pltpu.make_async_copy(source.at[rows], held, sems.at[i]))
+        copies[i].start()
+    for copy in copies:
+        copy.wait()
     sign = jnp.where(first, 1.0, -1.0).astype(F32)
     links = t_edges(load_links(links_ref, 0, 1 - parity))
     for r in range(RHS):
@@ -355,18 +364,19 @@
 
 
 def odd_kernel(links_ref, clover_ref, acc_ref, t_one, t_two, out_ref, *refs):
-    outs, summed = refs[:2], refs[2]
-    join_t(links_ref, acc_ref, t_one, t_two, 0, summed)
+    outs, summed, held = refs[:2], refs[2], refs[3:]
+    join_t(links_ref, acc_ref, t_one, t_two, 0, summed, *held)
     clover_to(clover_ref, lambda r: load_field(summed, r), out_ref, -KAPPA2)
     send_t(out_ref, links_ref, 1, *outs)
 
 
-def even_kernel(links_ref, acc_ref, t_one, t_two, out_ref, *outs):
-    join_t(links_ref, acc_ref, t_one, t_two, 1, out_ref)
+def even_kernel(links_ref, acc_ref, t_one, t_two, out_ref, *refs):
+    outs, held = refs[:2], refs[2:]
+    join_t(links_ref, acc_ref, t_one, t_two, 1, out_ref, *held)
     send_t(out_ref, links_ref, 0, *outs)
 
 
-def last_kernel(links_ref, acc_ref, t_one, t_two, out_hbm, held, sems):
+def last_kernel(links_ref, acc_ref, t_one, t_two, out_hbm, held, sems, *halos):
     part = held.shape[0] // RHS
     copies = []
 
@@ -375,7 +385,7 @@
         copies.append(pltpu.make_async_copy(held.at[rows], out_hbm.at[rows], sems.at[r]))
         copies[-1].start()
 
-    join_t(links_ref, acc_ref, t_one, t_two, 1, held, done)
+    join_t(links_ref, acc_ref, t_one, t_two, 1, held, *halos, done=done)
     for copy in copies:
         copy.wait()
 
@@ -386,11 +396,15 @@
 X_HALOS = [((RHS * 3 * 8, 128), BF16)] * 2
 
 
-def call(kernel, args, outs, flops, scratch=(), in_space=pltpu.VMEM, out_space=pltpu.VMEM):
+HBM_SPEC = pl.BlockSpec(memory_space=pltpu.HBM)
+T_HELD = [pltpu.VMEM(T_HALOS[0][0], BF16)] * 2 + [pltpu.SemaphoreType.DMA((2,))]
+
+
+def call(kernel, args, outs, flops, scratch=(), in_space=pltpu.VMEM, out_space=pltpu.VMEM, in_hbm=0):
     return pl.pallas_call(
         kernel,
         out_shape=tuple(jax.ShapeDtypeStruct(shape, dtype) for shape, dtype in outs),
-        in_specs=[pl.BlockSpec(memory_space=in_space)] * len(args),
+        in_specs=[pl.BlockSpec(memory_space=in_space)] * (len(args) - in_hbm) + [HBM_SPEC] * in_hbm,
         out_specs=tuple([pl.BlockSpec(memory_space=out_space)] * len(outs)),
         scratch_shapes=list(scratch),
         compiler_params=pltpu.CompilerParams(vmem_limit_bytes=24 * 1024 * 1024),
@@ -405,15 +419,12 @@
     return lax.ppermute(value, axis, pairs)
 
 
-def swap_t(value, ahead):
-    count, across = lax.axis_size("ta"), lax.axis_size("gx")
-    assert count % 2 == 0 and across % 2 == 0
-    pairs = []
-    for i in range(count):
-        for j in range(across):
-            step = 1 if ((i + j) % 2 == 0) == ahead else -1
-            pairs.append((i * across + j, (i + step) % count * across + j))
-    return lax.ppermute(value, ("ta", "gx"), pairs)
+def both(value, axis, far):
+    count = lax.axis_size(axis)
+    assert count % 2 == 0
+    pairs = [[(i + far) % count, (i + far + 1) % count] for i in range(0, count, 2)]
+    value = lax.all_gather(value, axis, axis_index_groups=pairs, axis=0, tiled=True)
+    return pltpu.with_memory_space_constraint(value, pltpu.HBM)
 
 
 def per_device(source, gauge_links, clover_even, clover_odd_inv):
@@ -431,7 +442,7 @@
     t_one, t_two = call(start_kernel, held, T_HALOS, 1_500_000, start_scratch, in_space=pltpu.HBM)
     for hop in range(4):
         parity = hop % 2
-        t_one, t_two = swap_t(t_one, True), swap_t(t_two, False)
+        t_one, t_two = both(t_one, "ta", 0), both(t_two, "ta", 1)
         x_far, x_near = call(
             functools.partial(send_x_kernel, parity), (f, links), X_HALOS, 1_500_000
         )
@@ -447,16 +458,16 @@
         if parity == 0:
             f, t_one, t_two = call(
                 odd_kernel, (links, odd, acc, t_one, t_two), FIELD + T_HALOS, 4_000_000,
-                [pltpu.VMEM((ROWS, 128), F32)],
+                [pltpu.VMEM((ROWS, 128), F32)] + T_HELD, in_hbm=2,
             )
         elif hop == 1:
             f, t_one, t_two = call(
-                even_kernel, (links, acc, t_one, t_two), FIELD + T_HALOS, 2_000_000
+                even_kernel, (links, acc, t_one, t_two), FIELD + T_HALOS, 2_000_000, T_HELD, in_hbm=2
             )
         else:
             out, = call(
                 last_kernel, (links, acc, t_one, t_two), [((ROWS, 128), BF16)], 1_000_000,
-                [pltpu.VMEM((ROWS, 128), BF16), pltpu.SemaphoreType.DMA((RHS,))], out_space=pltpu.HBM,
+                [pltpu.VMEM((ROWS, 128), BF16), pltpu.SemaphoreType.DMA((RHS,))] + T_HELD, out_space=pltpu.HBM, in_hbm=2,
             )
     return out.reshape(shape)
 

time: 31.6 us -> 66.9 us (2.12)
  blocking collectives: 0 us -> 46.2 us
  starting transfers between devices: 18.9 us -> 5.96 us
  waiting for transfers between devices: 4.79 us -> 0.02 us
  Pallas kernels: 7.58 us -> 10.9 us
  local copies, waits for them, and re-layouts: 0.02 us -> 3.16 us
    all_gather x0 -> x8, blocking collectives: none -> 46.2 us  [both(): lax.all_gather(value, axis, axis_index_groups=pairs, axis=0, tiled=True)]
    ppermute x8 -> x0, starting transfers between devices: 12.3 us -> none  [swap_t(): return lax.ppermute(value, ('ta', 'gx'), pairs)]
    ppermute x8, waiting for transfers between devices: 3.6 us -> 0.02 us  [swap(): return lax.ppermute(value, axis, pairs)]
    pallas_call x17, Pallas kernels: 7.58 us -> 10.9 us  [call(): pl.pallas_call(kernel, out_shape=tuple((jax.ShapeDtypeStruct(shape, dtype...]
    unnamed x8 -> x12, local copies, waits for them, and re-layouts: 0.02 us -> 3.16 us
    ppermute x8 -> x0, waiting for transfers between devices: 1.18 us -> none  [swap_t(): return lax.ppermute(value, ('ta', 'gx'), pairs)]
  transfers between devices with their start and end apart: 16 -> 8, of which waited for: 7 -> 0; matrix products, arithmetic and copies ran while one was open for 0% -> 0% of each run, Pallas kernels for 15% -> 6%
where the time goes in v7:
time: 66.9 us; the launch traced here: 66.4 us
  blocking collectives  46.2 us (69%)
  Pallas kernels  10.9 us (16%)
  starting transfers between devices  5.96 us (9%)
  local copies, waits for them, and re-layouts  3.16 us (5%)
    all_gather x8, blocking collectives, both(): lax.all_gather(value, axis, axis_index_groups=pairs, axis=0, tiled=True)  46.2 us
    pallas_call x17, Pallas kernels, call(): pl.pallas_call(kernel, out_shape=tuple((jax.ShapeDtypeStruct(shape, dtype...  10.9 us
    ppermute x8, starting transfers between devices, swap(): return lax.ppermute(value, axis, pairs)  5.96 us
    unnamed x12, local copies, waits for them, and re-layouts  3.16 us
  transfers between devices with their start and end apart: 8, of which 0 were waited for; matrix products, arithmetic and copies ran while one was open for 0% of the time, Pallas kernels for 6%

profile of v7, /device:TPU:0, one launch (start us, length us, event | category | flops | bytes accessed | tf_op | source)
XLA Modules:
  0.0 66.4 jit_solution(16930557932483955219)
XLA Ops:
  0.0 1.0 %copy-done = bf16[4,3,3,2,2,2,4,128]{7,6,5,4,3,2,1,0:T(4,128)(2,1)S(1)} copy-done((bf16[4,3,3,2,2,2,4,128]{7,6,5,4,3,2,1,0:T(4,128)(2,1)S(1)}, bf16[4,3,3,2,2,2,4,128]{7,6,5,4,3,2,1,0:T(4,128)(2,1)}, u32[]{:S(2)}) %copy-start) | copy-done | bytes 294936
  1.0 0.9 %copy-done.2 = bf16[4,4,3,2,2,4,128]{6,5,4,3,2,1,0:T(4,128)(2,1)S(1)} copy-done((bf16[4,4,3,2,2,4,128]{6,5,4,3,2,1,0:T(4,128)(2,1)S(1)}, bf16[4,4,3,2,2,4,128]{6,5,4,3,2,1,0:T(4,128)(2,1)}, u32[]{:S(2)}) %copy-start.2) | copy-done | bytes 196632
  1.9 0.1 shard_map.46
  2.0 0.0 copy-start.1
  2.0 2.4 %collective-permute-start = (bf16[96,128]{1,0:T(8,128)(2,1)S(1)}, bf16[96,128]{1,0:T(8,128)(2,1)S(1)}, u32[]{:S(2)}, u32[]{:S(2)}) collective-permute-start(bf16[96,128]{1,0:T(8,128)(2,1)S(1)} %get-tuple-element.39), channel_id=1, source_target_pairs={{0,3},{1,2},{2,1},{3,0},{4,7},{5,6},{6,5},{7,4},{8,11},{9,10},{10,... | collective-permute-start | bytes 73736 | tf_op jit(solution)/shard_map/ppermute | solution.py:419
  4.4 0.7 %collective-permute-start.1 = (bf16[96,128]{1,0:T(8,128)(2,1)S(1)}, bf16[96,128]{1,0:T(8,128)(2,1)S(1)}, u32[]{:S(2)}, u32[]{:S(2)}) collective-permute-start(bf16[96,128]{1,0:T(8,128)(2,1)S(1)} %get-tuple-element.40), channel_id=1, source_target_pairs={{0,1},{1,0},{2,3},{3,2},{4,5},{5,4},{6,7},{7,6},{8,9},{9,8},{10,11... | collective-permute-start | bytes 73736 | tf_op jit(solution)/shard_map/ppermute | solution.py:419
  5.1 1.1 %shard_map.49 = (bf16[192,128]{1,0:T(8,128)(2,1)S(1)}, bf16[192,128]{1,0:T(8,128)(2,1)S(1)}) custom-call(bf16[768,128]{1,0:T(8,128)(2,1)} %bitcast.22, bf16[1152,128]{1,0:T(8,128)(2,1)} %bitcast.5), custom_call_target="tpu_custom_call" | custom-call | flops 1500000 | bytes 2097152 | tf_op jit(solution)/shard_map/pallas_call | solution.py:404
  6.2 4.9 %all_gather.24.t_one = bf16[384,128]{1,0:T(8,128)(2,1)} all-gather(bf16[192,128]{1,0:T(8,128)(2,1)S(1)} %get-tuple-element.41), channel_id=1, replica_groups={{0,4},{8,12},{1,5},{9,13},{2,6},{10,14},{3,7},{11,15},{16,20},{24,28},{..., dimensions={0}, use_global_device_ids=true | all-gather | bytes 147456 | tf_op jit(solution)/shard_map/all_gather | solution.py:426
  11.1 0.0 copy-done.1
  11.1 0.0 copy-done.3
  11.1 0.9 %shard_map.47.acc_ref = f32[768,128]{1,0:T(8,128)S(1)} custom-call(bf16[768,128]{1,0:T(8,128)(2,1)S(1)} %bitcast.24, bf16[1152,128]{1,0:T(8,128)(2,1)S(1)} %bitcast.7), custom_call_target="tpu_custom_call" | custom-call | flops 5000000 | bytes 2097152 | tf_op jit(solution)/shard_map/pallas_call | solution.py:404
  11.9 6.7 %all_gather.25.t_two = bf16[384,128]{1,0:T(8,128)(2,1)} all-gather(bf16[192,128]{1,0:T(8,128)(2,1)S(1)} %get-tuple-element.42), channel_id=1, replica_groups={{4,8},{12,0},{5,9},{13,1},{6,10},{14,2},{7,11},{15,3},{20,24},{28,16},{..., dimensions={0}, use_global_device_ids=true | all-gather | bytes 147456 | tf_op jit(solution)/shard_map/all_gather | solution.py:426
  18.6 0.0 collective-permute-done.x_far
  18.6 0.0 collective-permute-done.1.x_near
  18.6 0.1 shard_map.48.acc_ref
  18.7 0.9 %copy-done.5 = bf16[2,6,6,2,2,4,128]{6,5,4,3,2,1,0:T(4,128)(2,1)S(1)} copy-done((bf16[2,6,6,2,2,4,128]{6,5,4,3,2,1,0:T(4,128)(2,1)S(1)}, bf16[2,6,6,2,2,4,128]{6,5,4,3,2,1,0:T(4,128)(2,1)}, u32[]{:S(2)}) %copy-start.5) | copy-done | bytes 294936
  19.6 1.3 %shard_map.50 = (f32[768,128]{1,0:T(8,128)S(1)}, bf16[192,128]{1,0:T(8,128)(2,1)S(1)}, bf16[192,128]{1,0:T(8,128)(2,1)S(1)}) custom-call(bf16[1152,128]{1,0:T(8,128)(2,1)S(1)} %bitcast.9, bf16[1152,128]{1,0:T(8,128)(2,1)S(1)} %bitcast.28, f32[768,128]{1,0:T(8,128)S(1)} %shard_map.48.acc_ref, bf16[384,128]{1,0:T(8,128)(2,1)} %all_gather.24.t_one, ...), custom_call_target="tpu_custom_call" | custom-call | flops 4000000 | bytes 2097152 | tf_op jit(solution)/shard_map/pallas_call | solution.py:404
  20.9 4.9 %all_gather.26.t_one = bf16[384,128]{1,0:T(8,128)(2,1)} all-gather(bf16[192,128]{1,0:T(8,128)(2,1)S(1)} %get-tuple-element.49), channel_id=1, replica_groups={{0,4},{8,12},{1,5},{9,13},{2,6},{10,14},{3,7},{11,15},{16,20},{24,28},{..., dimensions={0}, use_global_device_ids=true | all-gather | bytes 147456 | tf_op jit(solution)/shard_map/all_gather | solution.py:426
  25.8 0.1 shard_map.51
  25.9 0.1 collective-permute-start.2
  25.9 0.4 collective-permute-start.3
  26.3 0.4 copy-done.4
  26.7 1.1 %shard_map.52.acc_ref = f32[768,128]{1,0:T(8,128)S(1)} custom-call(f32[768,128]{1,0:T(8,128)S(1)} %get-tuple-element.46.f_ref.refs_0_, bf16[1152,128]{1,0:T(8,128)(2,1)S(1)} %bitcast.11, bf16[768,128]{1,0:T(8,128)(2,1)S(1)} %bitcast.25, bf16[1152,128]{1,0:T(8,128)(2,1)S(1)} %bitcast.26), custom_call_target="tpu_custom_call" | custom-call | flops 8000000 | bytes 2097152 | tf_op jit(solution)/shard_map/pallas_call | solution.py:404
  27.9 6.7 %all_gather.27.t_two = bf16[384,128]{1,0:T(8,128)(2,1)} all-gather(bf16[192,128]{1,0:T(8,128)(2,1)S(1)} %get-tuple-element.50), channel_id=1, replica_groups={{4,8},{12,0},{5,9},{13,1},{6,10},{14,2},{7,11},{15,3},{20,24},{28,16},{..., dimensions={0}, use_global_device_ids=true | all-gather | bytes 147456 | tf_op jit(solution)/shard_map/all_gather | solution.py:426
  34.5 0.0 collective-permute-done.2.x_far
  34.5 0.0 collective-permute-done.3.x_near
  34.5 0.1 shard_map.53.acc_ref
  34.6 1.0 %shard_map.54 = (f32[768,128]{1,0:T(8,128)S(1)}, bf16[192,128]{1,0:T(8,128)(2,1)S(1)}, bf16[192,128]{1,0:T(8,128)(2,1)S(1)}) custom-call(bf16[1152,128]{1,0:T(8,128)(2,1)S(1)} %bitcast.13, f32[768,128]{1,0:T(8,128)S(1)} %shard_map.53.acc_ref, bf16[384,128]{1,0:T(8,128)(2,1)} %all_gather.26.t_one, bf16[384,128]{1,0:T(8,128)(2,1)} %all_gather.27.t_two), custom_call_target="tpu_custom_call" | custom-call | flops 2000000 | bytes 2097152 | tf_op jit(solution)/shard_map/pallas_call | solution.py:404
  35.7 4.9 %all_gather.28.t_one = bf16[384,128]{1,0:T(8,128)(2,1)} all-gather(bf16[192,128]{1,0:T(8,128)(2,1)S(1)} %get-tuple-element.57), channel_id=1, replica_groups={{0,4},{8,12},{1,5},{9,13},{2,6},{10,14},{3,7},{11,15},{16,20},{24,28},{..., dimensions={0}, use_global_device_ids=true | all-gather | bytes 147456 | tf_op jit(solution)/shard_map/all_gather | solution.py:426
  40.5 0.1 shard_map.55
  40.6 0.1 collective-permute-start.4
  40.7 1.4 %collective-permute-start.5 = (bf16[96,128]{1,0:T(8,128)(2,1)S(1)}, bf16[96,128]{1,0:T(8,128)(2,1)S(1)}, u32[]{:S(2)}, u32[]{:S(2)}) collective-permute-start(bf16[96,128]{1,0:T(8,128)(2,1)S(1)} %get-tuple-element.56), channel_id=1, source_target_pairs={{0,1},{1,0},{2,3},{3,2},{4,5},{5,4},{6,7},{7,6},{8,9},{9,8},{10,11... | collective-permute-start | bytes 73736 | tf_op jit(solution)/shard_map/ppermute | solution.py:419
  42.1 0.8 %shard_map.56.acc_ref = f32[768,128]{1,0:T(8,128)S(1)} custom-call(f32[768,128]{1,0:T(8,128)S(1)} %get-tuple-element.54.f_ref.refs_0_.refs_2_, bf16[1152,128]{1,0:T(8,128)(2,1)S(1)} %bitcast.15), custom_call_target="tpu_custom_call" | custom-call | flops 5000000 | bytes 2097152 | tf_op jit(solution)/shard_map/pallas_call | solution.py:404
  42.9 6.7 %all_gather.29.t_two = bf16[384,128]{1,0:T(8,128)(2,1)} all-gather(bf16[192,128]{1,0:T(8,128)(2,1)S(1)} %get-tuple-element.58), channel_id=1, replica_groups={{4,8},{12,0},{5,9},{13,1},{6,10},{14,2},{7,11},{15,3},{20,24},{28,16},{..., dimensions={0}, use_global_device_ids=true | all-gather | bytes 147456 | tf_op jit(solution)/shard_map/all_gather | solution.py:426
  49.6 0.0 collective-permute-done.4.x_far
  49.6 0.0 collective-permute-done.5.x_near
  49.6 0.1 shard_map.57.acc_ref
  49.7 1.3 %shard_map.58 = (f32[768,128]{1,0:T(8,128)S(1)}, bf16[192,128]{1,0:T(8,128)(2,1)S(1)}, bf16[192,128]{1,0:T(8,128)(2,1)S(1)}) custom-call(bf16[1152,128]{1,0:T(8,128)(2,1)S(1)} %bitcast.17, bf16[1152,128]{1,0:T(8,128)(2,1)S(1)} %bitcast.29, f32[768,128]{1,0:T(8,128)S(1)} %shard_map.57.acc_ref, bf16[384,128]{1,0:T(8,128)(2,1)} %all_gather.28.t_one, ...), custom_call_target="tpu_custom_call" | custom-call | flops 4000000 | bytes 2097152 | tf_op jit(solution)/shard_map/pallas_call | solution.py:404
  51.0 4.9 %all_gather.30.t_one = bf16[384,128]{1,0:T(8,128)(2,1)} all-gather(bf16[192,128]{1,0:T(8,128)(2,1)S(1)} %get-tuple-element.65), channel_id=1, replica_groups={{0,4},{8,12},{1,5},{9,13},{2,6},{10,14},{3,7},{11,15},{16,20},{24,28},{..., dimensions={0}, use_global_device_ids=true | all-gather | bytes 147456 | tf_op jit(solution)/shard_map/all_gather | solution.py:426
  55.9 0.1 shard_map.59
  56.0 1.1 %shard_map.60.acc_ref = f32[768,128]{1,0:T(8,128)S(1)} custom-call(f32[768,128]{1,0:T(8,128)S(1)} %get-tuple-element.62.f_ref.refs_0_, bf16[1152,128]{1,0:T(8,128)(2,1)S(1)} %bitcast.19, f32[768,128]{1,0:T(8,128)S(1)} %get-tuple-element.54.f_ref.refs_0_.refs_2_, bf16[1152,128]{1,0:T(8,128)(2,1)S(1)} %bitcast.27), custom_call_target="tpu_custom_call" | custom-call | flops 8000000 | bytes 2097152 | tf_op jit(solution)/shard_map/pallas_call | solution.py:404
  57.1 0.1 collective-permute-start.6
  57.2 0.8 %collective-permute-start.7 = (bf16[96,128]{1,0:T(8,128)(2,1)S(1)}, bf16[96,128]{1,0:T(8,128)(2,1)S(1)}, u32[]{:S(2)}, u32[]{:S(2)}) collective-permute-start(bf16[96,128]{1,0:T(8,128)(2,1)S(1)} %get-tuple-element.64), channel_id=1, source_target_pairs={{0,1},{1,0},{2,3},{3,2},{4,5},{5,4},{6,7},{7,6},{8,9},{9,8},{10,11... | collective-permute-start | bytes 73736 | tf_op jit(solution)/shard_map/ppermute | solution.py:419
  58.0 6.7 %all_gather.31.t_two = bf16[384,128]{1,0:T(8,128)(2,1)} all-gather(bf16[192,128]{1,0:T(8,128)(2,1)S(1)} %get-tuple-element.66), channel_id=1, replica_groups={{4,8},{12,0},{5,9},{13,1},{6,10},{14,2},{7,11},{15,3},{20,24},{28,16},{..., dimensions={0}, use_global_device_ids=true | all-gather | bytes 147456 | tf_op jit(solution)/shard_map/all_gather | solution.py:426
  64.7 0.0 collective-permute-done.6.x_far
  64.7 0.0 collective-permute-done.7.x_near
  64.7 0.1 shard_map.61.acc_ref
  64.8 1.6 %shard_map.62 = bf16[768,128]{1,0:T(8,128)(2,1)} custom-call(bf16[1152,128]{1,0:T(8,128)(2,1)S(1)} %bitcast.21, f32[768,128]{1,0:T(8,128)S(1)} %shard_map.61.acc_ref, bf16[384,128]{1,0:T(8,128)(2,1)} %all_gather.30.t_one, bf16[384,128]{1,0:T(8,128)(2,1)} %all_gather.31.t_two), custom_call_target="tpu_custom_call" | custom-call | flops 1000000 | bytes 2097152 | tf_op jit(solution)/shard_map/pallas_call | solution.py:404
  (5 shorter events, 0.0 us)
Async XLA Ops:
  0.0 1.0 %copy-start = (bf16[4,3,3,2,2,2,4,128]{7,6,5,4,3,2,1,0:T(4,128)(2,1)S(1)}, bf16[4,3,3,2,2,2,4,128]{7,6,5,4,3,2,1,0:T(4,128)(2,1)}, u32[]{:S(2)}) copy-start(bf16[4,3,3,2,2,2,4,128]{7,6,5,4,3,2,1,0:T(4,128)(2,1)} %param.5) | copy-start | bytes 884740
  1.0 0.9 %copy-start.2 = (bf16[4,4,3,2,2,4,128]{6,5,4,3,2,1,0:T(4,128)(2,1)S(1)}, bf16[4,4,3,2,2,4,128]{6,5,4,3,2,1,0:T(4,128)(2,1)}, u32[]{:S(2)}) copy-start(bf16[4,4,3,2,2,4,128]{6,5,4,3,2,1,0:T(4,128)(2,1)} %param.4) | copy-start | bytes 589828
  2.0 9.1 %copy-start.1 = (bf16[4,3,3,2,2,2,4,128]{7,6,5,4,3,2,1,0:T(4,128)(2,1)S(1)}, bf16[4,3,3,2,2,2,4,128]{7,6,5,4,3,2,1,0:T(4,128)(2,1)}, u32[]{:S(2)}) copy-start(bf16[4,3,3,2,2,2,4,128]{7,6,5,4,3,2,1,0:T(4,128)(2,1)} %param.5) | copy-start | bytes 884740
  2.0 16.6 %collective-permute-start = (bf16[96,128]{1,0:T(8,128)(2,1)S(1)}, bf16[96,128]{1,0:T(8,128)(2,1)S(1)}, u32[]{:S(2)}, u32[]{:S(2)}) collective-permute-start(bf16[96,128]{1,0:T(8,128)(2,1)S(1)} %get-tuple-element.39), channel_id=1, source_target_pairs={{0,3},{1,2},{2,1},{3,0},{4,7},{5,6},{6,5},{7,4},{8,11},{9,10},{10,... | collective-permute-start | bytes 73736 | tf_op jit(solution)/shard_map/ppermute | solution.py:419
  4.4 14.2 %collective-permute-start.1 = (bf16[96,128]{1,0:T(8,128)(2,1)S(1)}, bf16[96,128]{1,0:T(8,128)(2,1)S(1)}, u32[]{:S(2)}, u32[]{:S(2)}) collective-permute-start(bf16[96,128]{1,0:T(8,128)(2,1)S(1)} %get-tuple-element.40), channel_id=1, source_target_pairs={{0,1},{1,0},{2,3},{3,2},{4,5},{5,4},{6,7},{7,6},{8,9},{9,8},{10,11... | collective-permute-start | bytes 73736 | tf_op jit(solution)/shard_map/ppermute | solution.py:419
  5.1 6.0 %copy-start.3 = (bf16[4,4,3,2,2,4,128]{6,5,4,3,2,1,0:T(4,128)(2,1)S(1)}, bf16[4,4,3,2,2,4,128]{6,5,4,3,2,1,0:T(4,128)(2,1)}, u32[]{:S(2)}) copy-start(bf16[4,4,3,2,2,4,128]{6,5,4,3,2,1,0:T(4,128)(2,1)} %param.4) | copy-start | bytes 589828
  18.6 1.0 %copy-start.5 = (bf16[2,6,6,2,2,4,128]{6,5,4,3,2,1,0:T(4,128)(2,1)S(1)}, bf16[2,6,6,2,2,4,128]{6,5,4,3,2,1,0:T(4,128)(2,1)}, u32[]{:S(2)}) copy-start(bf16[2,6,6,2,2,4,128]{6,5,4,3,2,1,0:T(4,128)(2,1)} %param.7) | copy-start | bytes 884740
  25.8 1.0 %copy-start.4 = (bf16[2,6,6,2,2,4,128]{6,5,4,3,2,1,0:T(4,128)(2,1)S(1)}, bf16[2,6,6,2,2,4,128]{6,5,4,3,2,1,0:T(4,128)(2,1)}, u32[]{:S(2)}) copy-start(bf16[2,6,6,2,2,4,128]{6,5,4,3,2,1,0:T(4,128)(2,1)} %param.6) | copy-start | bytes 884740
  25.9 8.7 %collective-permute-start.2 = (bf16[96,128]{1,0:T(8,128)(2,1)S(1)}, bf16[96,128]{1,0:T(8,128)(2,1)S(1)}, u32[]{:S(2)}, u32[]{:S(2)}) collective-permute-start(bf16[96,128]{1,0:T(8,128)(2,1)S(1)} %get-tuple-element.47), channel_id=1, source_target_pairs={{0,3},{1,2},{2,1},{3,0},{4,7},{5,6},{6,5},{7,4},{8,11},{9,10},{10,... | collective-permute-start | bytes 73736 | tf_op jit(solution)/shard_map/ppermute | solution.py:419
  25.9 8.6 %collective-permute-start.3 = (bf16[96,128]{1,0:T(8,128)(2,1)S(1)}, bf16[96,128]{1,0:T(8,128)(2,1)S(1)}, u32[]{:S(2)}, u32[]{:S(2)}) collective-permute-start(bf16[96,128]{1,0:T(8,128)(2,1)S(1)} %get-tuple-element.48), channel_id=1, source_target_pairs={{0,1},{1,0},{2,3},{3,2},{4,5},{5,4},{6,7},{7,6},{8,9},{9,8},{10,11... | collective-permute-start | bytes 73736 | tf_op jit(solution)/shard_map/ppermute | solution.py:419
  40.6 9.0 %collective-permute-start.4 = (bf16[96,128]{1,0:T(8,128)(2,1)S(1)}, bf16[96,128]{1,0:T(8,128)(2,1)S(1)}, u32[]{:S(2)}, u32[]{:S(2)}) collective-permute-start(bf16[96,128]{1,0:T(8,128)(2,1)S(1)} %get-tuple-element.55), channel_id=1, source_target_pairs={{0,3},{1,2},{2,1},{3,0},{4,7},{5,6},{6,5},{7,4},{8,11},{9,10},{10,... | collective-permute-start | bytes 73736 | tf_op jit(solution)/shard_map/ppermute | solution.py:419
  40.7 8.9 %collective-permute-start.5 = (bf16[96,128]{1,0:T(8,128)(2,1)S(1)}, bf16[96,128]{1,0:T(8,128)(2,1)S(1)}, u32[]{:S(2)}, u32[]{:S(2)}) collective-permute-start(bf16[96,128]{1,0:T(8,128)(2,1)S(1)} %get-tuple-element.56), channel_id=1, source_target_pairs={{0,1},{1,0},{2,3},{3,2},{4,5},{5,4},{6,7},{7,6},{8,9},{9,8},{10,11... | collective-permute-start | bytes 73736 | tf_op jit(solution)/shard_map/ppermute | solution.py:419
  57.1 7.5 %collective-permute-start.6 = (bf16[96,128]{1,0:T(8,128)(2,1)S(1)}, bf16[96,128]{1,0:T(8,128)(2,1)S(1)}, u32[]{:S(2)}, u32[]{:S(2)}) collective-permute-start(bf16[96,128]{1,0:T(8,128)(2,1)S(1)} %get-tuple-element.63), channel_id=1, source_target_pairs={{0,3},{1,2},{2,1},{3,0},{4,7},{5,6},{6,5},{7,4},{8,11},{9,10},{10,... | collective-permute-start | bytes 73736 | tf_op jit(solution)/shard_map/ppermute | solution.py:419
  57.2 7.5 %collective-permute-start.7 = (bf16[96,128]{1,0:T(8,128)(2,1)S(1)}, bf16[96,128]{1,0:T(8,128)(2,1)S(1)}, u32[]{:S(2)}, u32[]{:S(2)}) collective-permute-start(bf16[96,128]{1,0:T(8,128)(2,1)S(1)} %get-tuple-element.64), channel_id=1, source_target_pairs={{0,1},{1,0},{2,3},{3,2},{4,5},{5,4},{6,7},{7,6},{8,9},{9,8},{10,11... | collective-permute-start | bytes 73736 | tf_op jit(solution)/shard_map/ppermute | solution.py:419

commit v8 on v6

--- a/solution.py
+++ b/solution.py
@@ -107,15 +107,6 @@
     return rows // 4, rows % 4
 
 
-def even_device(*axes):
-    place = sum(lax.axis_index(axis) for axis in axes)
-    return lax.broadcast(place % 2, (8, 128)) == 0
-
-
-def either(even, a, b):
-    return [select(even, a[i], b[i]) for i in range(2)]
-
-
 def roll_rows(value, shift):
     shift %= 8
     return pltpu.roll(value, shift, 0) if shift else value
@@ -142,8 +133,24 @@
     return [each(edge, row) for row in links]
 
 
-def send_t(f_ref, links_ref, parity, t_one, t_two, ready=lambda r: None):
-    even = even_device("ta", "gx")
+def slots(ref, axis, count):
+    rows = ref.shape[0] // count
+    me = lax.axis_index(axis)
+    return [pl.multiple_of(lax.rem(me + step, count) * rows, rows) for step in (1, count - 1)]
+
+
+def store_slot(ref, base, index, pair):
+    ref[pl.ds(base + index * 16, 16), :] = jnp.concatenate(pair, axis=0).astype(ref.dtype)
+
+
+def load_slot(ref, base, index):
+    block = ref[pl.ds(base + index * 16, 16), :].astype(F32)
+    return block[0:8], block[8:16]
+
+
+def send_t(f_ref, links_ref, parity, out_ref, count, ready=lambda r: None):
+    to_next, to_last = slots(out_ref, "ta", count)
+    out_ref[...] = jnp.zeros_like(out_ref)
     t_idx, _ = site_masks()
     first = t_idx == 0
     links = t_edges(load_links(links_ref, 0, parity))
@@ -157,12 +164,13 @@
         rears = matvec(links, rears, True)
         for c in range(3):
             front = [select(first, ahead[c + 3][i], roll_rows(ahead[c][i], 4)) for i in range(2)]
-            store_pair(t_one, r * 3 + c, either(even, rears[c], front))
-            store_pair(t_two, r * 3 + c, either(even, front, rears[c]))
-
-
-def send_x_kernel(parity, f_ref, links_ref, x_far, x_near):
-    even = even_device("gx")
+            store_slot(out_ref, to_next, r * 3 + c, rears[c])
+            store_slot(out_ref, to_last, r * 3 + c, front)
+
+
+def send_x_kernel(parity, count, f_ref, links_ref, out_ref):
+    to_next, to_last = slots(out_ref, "gx", count)
+    out_ref[...] = jnp.zeros_like(out_ref)
     _, x_idx = site_masks()
     links = x_edges(load_links(links_ref, 1, parity))
 
@@ -182,12 +190,12 @@
             rears.append([packed([h[j][i] for h in behind for j in (c, c + 3)], 3, -1) for i in range(2)])
         rears = matvec(links, rears, True)
         for c in range(3):
-            store_pair(x_near, q * 3 + c, either(even, rears[c], fronts[c]))
-            store_pair(x_far, q * 3 + c, either(even, fronts[c], rears[c]))
-
-
-def start_kernel(f_hbm, links_hbm, *refs):
-    outs, (f_ref, links_ref, sems) = refs[:2], refs[2:]
+            store_slot(out_ref, to_next, q * 3 + c, rears[c])
+            store_slot(out_ref, to_last, q * 3 + c, fronts[c])
+
+
+def start_kernel(count, f_hbm, links_hbm, *refs):
+    out_ref, f_ref, links_ref, sems = refs
     part = f_ref.shape[0] // RHS
     copies = [pltpu.make_async_copy(links_hbm.at[pl.ds(0, links_ref.shape[0])], links_ref, sems.at[RHS])]
     for r in range(RHS):
@@ -196,7 +204,7 @@
     for copy in copies:
         copy.start()
     copies[0].wait()
-    send_t(f_ref, links_ref, 0, *outs, ready=lambda r: copies[1 + r].wait())
+    send_t(f_ref, links_ref, 0, out_ref, count, ready=lambda r: copies[1 + r].wait())
 
 
 def interior_kernel(parity, with_base, *refs):
@@ -305,17 +313,16 @@
     return out
 
 
-def join_x_kernel(parity, links_ref, acc_ref, x_far, x_near, out_ref):
-    even = even_device("gx")
+def join_x_kernel(parity, count, links_ref, acc_ref, x_ref, out_ref):
+    from_next, from_last = slots(x_ref, "gx", count)
     _, x_idx = site_masks()
     sign = jnp.where(x_idx == 3, -1.0, 1.0).astype(F32)
     links = x_edges(load_links(links_ref, 1, 1 - parity))
     for q in range(RHS // 2):
         nxt, last = [], []
         for c in range(3):
-            near, far = load_pair(x_near, q * 3 + c), load_pair(x_far, q * 3 + c)
-            nxt.append(either(even, near, far))
-            last.append(either(even, far, near))
+            nxt.append(load_slot(x_ref, from_next, q * 3 + c))
+            last.append(load_slot(x_ref, from_last, q * 3 + c))
         ahead = matvec(links, nxt, False)
         for r in (2 * q, 2 * q + 1):
             half = [None] * 6
@@ -333,8 +340,8 @@
             store_field(out_ref, r, rebuild_signed(load_field(acc_ref, r), half, 1, sign))
 
 
-def join_t(links_ref, acc_ref, t_one, t_two, parity, out_ref, done=lambda r: None):
-    even = even_device("ta", "gx")
+def join_t(links_ref, acc_ref, t_ref, parity, out_ref, count, done=lambda r: None):
+    from_next, from_last = slots(t_ref, "ta", count)
     t_idx, _ = site_masks()
     first = t_idx == 0
     sign = jnp.where(first, 1.0, -1.0).astype(F32)
@@ -342,9 +349,8 @@
     for r in range(RHS):
         nxt, last = [], []
         for c in range(3):
-            one, two = load_pair(t_one, r * 3 + c), load_pair(t_two, r * 3 + c)
-            nxt.append(either(even, one, two))
-            last.append(either(even, two, one))
+            nxt.append(load_slot(t_ref, from_next, r * 3 + c))
+            last.append(load_slot(t_ref, from_last, r * 3 + c))
         ahead = matvec(links, nxt, False)
         half = [tuple(select(first, last[c][i], ahead[c][i]) for i in range(2)) for c in range(3)]
         half += [
@@ -354,19 +360,18 @@
         done(r)
 
 
-def odd_kernel(links_ref, clover_ref, acc_ref, t_one, t_two, out_ref, *refs):
-    outs, summed = refs[:2], refs[2]
-    join_t(links_ref, acc_ref, t_one, t_two, 0, summed)
+def odd_kernel(count, links_ref, clover_ref, acc_ref, t_ref, out_ref, halo_ref, summed):
+    join_t(links_ref, acc_ref, t_ref, 0, summed, count)
     clover_to(clover_ref, lambda r: load_field(summed, r), out_ref, -KAPPA2)
-    send_t(out_ref, links_ref, 1, *outs)
-
-
-def even_kernel(links_ref, acc_ref, t_one, t_two, out_ref, *outs):
-    join_t(links_ref, acc_ref, t_one, t_two, 1, out_ref)
-    send_t(out_ref, links_ref, 0, *outs)
-
-
-def last_kernel(links_ref, acc_ref, t_one, t_two, out_hbm, held, sems):
+    send_t(out_ref, links_ref, 1, halo_ref, count)
+
+
+def even_kernel(count, links_ref, acc_ref, t_ref, out_ref, halo_ref):
+    join_t(links_ref, acc_ref, t_ref, 1, out_ref, count)
+    send_t(out_ref, links_ref, 0, halo_ref, count)
+
+
+def last_kernel(count, links_ref, acc_ref, t_ref, out_hbm, held, sems):
     part = held.shape[0] // RHS
     copies = []
 
@@ -375,17 +380,13 @@
         copies.append(pltpu.make_async_copy(held.at[rows], out_hbm.at[rows], sems.at[r]))
         copies[-1].start()
 
-    join_t(links_ref, acc_ref, t_one, t_two, 1, held, done)
+    join_t(links_ref, acc_ref, t_ref, 1, held, count, done)
     for copy in copies:
         copy.wait()
 
 
 ROWS = RHS * 24 * 8
 FIELD = [((ROWS, 128), F32)]
-T_HALOS = [((RHS * 3 * 16, 128), BF16)] * 2
-X_HALOS = [((RHS * 3 * 8, 128), BF16)] * 2
-
-
 def call(kernel, args, outs, flops, scratch=(), in_space=pltpu.VMEM, out_space=pltpu.VMEM):
     return pl.pallas_call(
         kernel,
@@ -398,26 +399,14 @@
     )(*args)
 
 
-def swap(value, axis, far):
-    count = lax.axis_size(axis)
-    assert count % 2 == 0
-    pairs = [(i, (i + (1 if (i % 2 == 0) != far else -1)) % count) for i in range(count)]
-    return lax.ppermute(value, axis, pairs)
-
-
-def swap_t(value, ahead):
-    count, across = lax.axis_size("ta"), lax.axis_size("gx")
-    assert count % 2 == 0 and across % 2 == 0
-    pairs = []
-    for i in range(count):
-        for j in range(across):
-            step = 1 if ((i + j) % 2 == 0) == ahead else -1
-            pairs.append((i * across + j, (i + step) % count * across + j))
-    return lax.ppermute(value, ("ta", "gx"), pairs)
+def slot_shape(count, rows):
+    return [((count * rows, 128), BF16)]
 
 
 def per_device(source, gauge_links, clover_even, clover_odd_inv):
     shape = source.shape
+    across_t, across_x = lax.axis_size("ta"), lax.axis_size("gx")
+    t_shape, x_shape = slot_shape(across_t, RHS * 3 * 16), slot_shape(across_x, RHS * 3 * 8)
     f = source.reshape(-1, 128)
     links = gauge_links.reshape(-1, 128)
     even = clover_even.reshape(-1, 128)
@@ -428,34 +417,32 @@
         pltpu.VMEM((links.shape[0] // 4, 128), BF16),
         pltpu.SemaphoreType.DMA((RHS + 1,)),
     ]
-    t_one, t_two = call(start_kernel, held, T_HALOS, 1_500_000, start_scratch, in_space=pltpu.HBM)
+    t_halos, = call(functools.partial(start_kernel, across_t), held, t_shape, 1_500_000, start_scratch, in_space=pltpu.HBM)
     for hop in range(4):
         parity = hop % 2
-        t_one, t_two = swap_t(t_one, True), swap_t(t_two, False)
-        x_far, x_near = call(
-            functools.partial(send_x_kernel, parity), (f, links), X_HALOS, 1_500_000
-        )
-        here, x_far, x_near = lax.optimization_barrier((f, x_far, x_near))
-        x_far, x_near = swap(x_far, "gx", True), swap(x_near, "gx", False)
+        t_halos = lax.all_to_all(t_halos, "ta", 0, 0, tiled=True)
+        x_halos, = call(functools.partial(send_x_kernel, parity, across_x), (f, links), x_shape, 1_500_000)
+        here, x_halos = lax.optimization_barrier((f, x_halos))
+        x_halos = lax.all_to_all(x_halos, "gx", 0, 0, tiled=True)
         base = (before, even) if parity else ()
         acc, = call(
             functools.partial(interior_kernel, parity, bool(parity)),
             (here, links, *base), FIELD, 8_000_000 if parity else 5_000_000,
         )
-        acc, = call(functools.partial(join_x_kernel, parity), (links, acc, x_far, x_near), FIELD, 1_000_000)
+        acc, = call(functools.partial(join_x_kernel, parity, across_x), (links, acc, x_halos), FIELD, 1_000_000)
         before = f
         if parity == 0:
-            f, t_one, t_two = call(
-                odd_kernel, (links, odd, acc, t_one, t_two), FIELD + T_HALOS, 4_000_000,
+            f, t_halos = call(
+                functools.partial(odd_kernel, across_t), (links, odd, acc, t_halos), FIELD + t_shape, 4_000_000,
                 [pltpu.VMEM((ROWS, 128), F32)],
             )
         elif hop == 1:
-            f, t_one, t_two = call(
-                even_kernel, (links, acc, t_one, t_two), FIELD + T_HALOS, 2_000_000
+            f, t_halos = call(
+                functools.partial(even_kernel, across_t), (links, acc, t_halos), FIELD + t_shape, 2_000_000
             )
         else:
             out, = call(
-                last_kernel, (links, acc, t_one, t_two), [((ROWS, 128), BF16)], 1_000_000,
+                functools.partial(last_kernel, across_t), (links, acc, t_halos), [((ROWS, 128), BF16)], 1_000_000,
                 [pltpu.VMEM((ROWS, 128), BF16), pltpu.SemaphoreType.DMA((RHS,))], out_space=pltpu.HBM,
             )
     return out.reshape(shape)

time: 31.6 us -> 81.5 us (2.58)
  waiting for transfers between devices: 4.79 us -> 27.9 us
  blocking collectives: 0 us -> 20.1 us
  Pallas kernels: 7.58 us -> 10.9 us
  local copies, waits for them, and re-layouts: 0.02 us -> 1.91 us
    all_to_all x0 -> x5, waiting for transfers between devices: none -> 27.9 us  [the longest x4 25.4 us: per_device(): t_halos = lax.all_to_all(t_halos, 'ta', 0, 0, tiled=True)]
    all_to_all x0 -> x3, blocking collectives: none -> 20.1 us  [per_device(): x_halos = lax.all_to_all(x_halos, 'gx', 0, 0, tiled=True)]
    all_to_all x0 -> x5, starting transfers between devices: none -> 19.7 us  [the longest x4 15.5 us: per_device(): t_halos = lax.all_to_all(t_halos, 'ta', 0, 0, tiled=True)]
    ppermute x16 -> x0, starting transfers between devices: 18.9 us -> none  [the longest x8 12.3 us: swap_t(): return lax.ppermute(value, ('ta', 'gx'), pairs)]
    ppermute x16 -> x0, waiting for transfers between devices: 4.79 us -> none  [the longest x8 3.6 us: swap(): return lax.ppermute(value, axis, pairs)]
    pallas_call x17, Pallas kernels: 7.58 us -> 10.9 us  [call(): pl.pallas_call(kernel, out_shape=tuple((jax.ShapeDtypeStruct(shape, dtype...]
    unnamed x8 -> x12, local copies, waits for them, and re-layouts: 0.02 us -> 1.91 us
  transfers between devices with their start and end apart: 16 -> 5, of which waited for: 7 -> 5; matrix products, arithmetic and copies ran while one was open for 0% -> 0% of each run, Pallas kernels for 15% -> 7%
where the time goes in v8:
time: 81.5 us; the launch traced here: 80.7 us
  waiting for transfers between devices  27.9 us (34%)
  blocking collectives  20.1 us (25%)
  starting transfers between devices  19.7 us (24%)
  Pallas kernels  10.9 us (13%)
  local copies, waits for them, and re-layouts  1.91 us (2%)
    all_to_all x4, waiting for transfers between devices, per_device(): t_halos = lax.all_to_all(t_halos, 'ta', 0, 0, tiled=True)  25.4 us
    all_to_all x3, blocking collectives, per_device(): x_halos = lax.all_to_all(x_halos, 'gx', 0, 0, tiled=True)  20.1 us
    all_to_all x4, starting transfers between devices, per_device(): t_halos = lax.all_to_all(t_halos, 'ta', 0, 0, tiled=True)  15.5 us
    pallas_call x17, Pallas kernels, call(): pl.pallas_call(kernel, out_shape=tuple((jax.ShapeDtypeStruct(shape, dtype...  10.9 us
    all_to_all x1, starting transfers between devices, per_device(): x_halos = lax.all_to_all(x_halos, 'gx', 0, 0, tiled=True)  4.21 us
    all_to_all x1, waiting for transfers between devices, per_device(): x_halos = lax.all_to_all(x_halos, 'gx', 0, 0, tiled=True)  2.51 us
    unnamed x12, local copies, waits for them, and re-layouts  1.91 us
  transfers between devices with their start and end apart: 5, of which 5 were waited for; matrix products, arithmetic and copies ran while one was open for 0% of the time, Pallas kernels for 7%

profile of v8, /device:TPU:0, one launch (start us, length us, event | category | flops | bytes accessed | tf_op | source)
XLA Modules:
  0.0 80.7 jit_solution(6254832801665505380)
XLA Ops:
  0.0 0.0 copy-start
  0.0 1.0 %copy-done = bf16[4,3,3,2,2,2,4,128]{7,6,5,4,3,2,1,0:T(4,128)(2,1)S(1)} copy-done((bf16[4,3,3,2,2,2,4,128]{7,6,5,4,3,2,1,0:T(4,128)(2,1)S(1)}, bf16[4,3,3,2,2,2,4,128]{7,6,5,4,3,2,1,0:T(4,128)(2,1)}, u32[]{:S(2)}) %copy-start) | copy-done | bytes 294936
  1.0 0.0 copy-start.2
  1.0 0.9 %copy-done.2 = bf16[4,4,3,2,2,4,128]{6,5,4,3,2,1,0:T(4,128)(2,1)S(1)} copy-done((bf16[4,4,3,2,2,4,128]{6,5,4,3,2,1,0:T(4,128)(2,1)S(1)}, bf16[4,4,3,2,2,4,128]{6,5,4,3,2,1,0:T(4,128)(2,1)}, u32[]{:S(2)}) %copy-start.2) | copy-done | bytes 196632
  1.9 0.8 shard_map.46
  2.6 4.2 %all-to-all-start = ((bf16[4,96,128]{2,1,0:T(8,128)(2,1)}), bf16[4,96,128]{2,1,0:T(8,128)(2,1)S(1)}, u32[]{:S(2)}, u32[]{:S(2)}) async-start(bf16[4,96,128]{2,1,0:T(8,128)(2,1)} %bitcast.3), calls=%async_computation | async-start | bytes 196608 | tf_op jit(solution)/shard_map/all_to_all | solution.py:426
  6.8 0.0 copy-start.3
  6.9 1.8 %shard_map.49 = bf16[768,128]{1,0:T(8,128)(2,1)} custom-call(bf16[768,128]{1,0:T(8,128)(2,1)} %bitcast.38, bf16[1152,128]{1,0:T(8,128)(2,1)} %bitcast.21), custom_call_target="tpu_custom_call" | custom-call | flops 1500000 | bytes 2097152 | tf_op jit(solution)/shard_map/pallas_call | solution.py:391
  8.6 0.0 copy-start.1
  8.6 2.5 %all-to-all-done = bf16[4,96,128]{2,1,0:T(8,128)(2,1)S(1)} async-done(((bf16[4,96,128]{2,1,0:T(8,128)(2,1)}), bf16[4,96,128]{2,1,0:T(8,128)(2,1)S(1)}, u32[]{:S(2)}, u32[]{:S(2)}) %all-to-all-start) | async-done | bytes 98336 | tf_op jit(solution)/shard_map/all_to_all | solution.py:426
  11.1 5.4 %all-to-all-start.1 = ((bf16[4,192,128]{2,1,0:T(8,128)(2,1)}), bf16[4,192,128]{2,1,0:T(8,128)(2,1)S(1)}, u32[]{:S(2)}, u32[]{:S(2)}) async-start(bf16[4,192,128]{2,1,0:T(8,128)(2,1)} %bitcast.5), calls=%async_computation.1 | async-start | bytes 393216 | tf_op jit(solution)/shard_map/all_to_all | solution.py:423
  16.5 0.0 copy-done.3
  16.5 0.0 copy-done.1
  16.5 0.9 %shard_map.47.acc_ref = f32[768,128]{1,0:T(8,128)S(1)} custom-call(bf16[768,128]{1,0:T(8,128)(2,1)S(1)} %bitcast.40, bf16[1152,128]{1,0:T(8,128)(2,1)S(1)} %bitcast.23), custom_call_target="tpu_custom_call" | custom-call | flops 5000000 | bytes 2097152 | tf_op jit(solution)/shard_map/pallas_call | solution.py:391
  17.4 0.0 copy-start.5
  17.4 0.1 shard_map.48.acc_ref
  17.5 6.3 %all-to-all-done.1 = bf16[4,192,128]{2,1,0:T(8,128)(2,1)S(1)} async-done(((bf16[4,192,128]{2,1,0:T(8,128)(2,1)}), bf16[4,192,128]{2,1,0:T(8,128)(2,1)S(1)}, u32[]{:S(2)}, u32[]{:S(2)}) %all-to-all-start.1) | async-done | bytes 196640 | tf_op jit(solution)/shard_map/all_to_all | solution.py:423
  23.8 0.0 copy-done.5
  23.8 1.2 %shard_map.50 = (f32[768,128]{1,0:T(8,128)S(1)}, bf16[768,128]{1,0:T(8,128)(2,1)}) custom-call(bf16[1152,128]{1,0:T(8,128)(2,1)S(1)} %bitcast.25, bf16[1152,128]{1,0:T(8,128)(2,1)S(1)} %bitcast.44, f32[768,128]{1,0:T(8,128)S(1)} %shard_map.48.acc_ref, bf16[768,128]{1,0:T(8,128)(2,1)S(1)} %bitcast.47), custom_call_target="tpu_custom_call" | custom-call | flops 4000000 | bytes 2097152 | tf_op jit(solution)/shard_map/pallas_call | solution.py:391
  25.0 0.1 shard_map.51
  25.1 0.0 copy-start.4
  25.1 6.8 %all_to_all.88 = bf16[4,96,128]{2,1,0:T(8,128)(2,1)S(1)} all-to-all(bf16[4,96,128]{2,1,0:T(8,128)(2,1)S(1)} %bitcast.54), channel_id=1, replica_groups=mesh['groups'=2,'ta'=4,'gx'=4] {'gx'}, dimensions={0} | all-to-all | bytes 196608 | tf_op jit(solution)/shard_map/all_to_all | solution.py:426
  31.9 3.4 %all-to-all-start.3 = ((bf16[4,192,128]{2,1,0:T(8,128)(2,1)}), bf16[4,192,128]{2,1,0:T(8,128)(2,1)S(1)}, u32[]{:S(2)}, u32[]{:S(2)}) async-start(bf16[4,192,128]{2,1,0:T(8,128)(2,1)} %bitcast.10), calls=%async_computation.3 | async-start | bytes 393216 | tf_op jit(solution)/shard_map/all_to_all | solution.py:423
  35.3 0.0 copy-done.4
  35.3 1.1 %shard_map.52.acc_ref = f32[768,128]{1,0:T(8,128)S(1)} custom-call(f32[768,128]{1,0:T(8,128)S(1)} %get-tuple-element.22.f_ref.refs_0_, bf16[1152,128]{1,0:T(8,128)(2,1)S(1)} %bitcast.27, bf16[768,128]{1,0:T(8,128)(2,1)S(1)} %bitcast.41, bf16[1152,128]{1,0:T(8,128)(2,1)S(1)} %bitcast.42), custom_call_target="tpu_custom_call" | custom-call | flops 8000000 | bytes 2097152 | tf_op jit(solution)/shard_map/pallas_call | solution.py:391
  36.4 0.1 shard_map.53.acc_ref
  36.5 6.2 %all-to-all-done.3 = bf16[4,192,128]{2,1,0:T(8,128)(2,1)S(1)} async-done(((bf16[4,192,128]{2,1,0:T(8,128)(2,1)}), bf16[4,192,128]{2,1,0:T(8,128)(2,1)S(1)}, u32[]{:S(2)}, u32[]{:S(2)}) %all-to-all-start.3) | async-done | bytes 196640 | tf_op jit(solution)/shard_map/all_to_all | solution.py:423
  42.7 0.9 %shard_map.54 = (f32[768,128]{1,0:T(8,128)S(1)}, bf16[768,128]{1,0:T(8,128)(2,1)}) custom-call(bf16[1152,128]{1,0:T(8,128)(2,1)S(1)} %bitcast.29, f32[768,128]{1,0:T(8,128)S(1)} %shard_map.53.acc_ref, bf16[768,128]{1,0:T(8,128)(2,1)S(1)} %bitcast.46), custom_call_target="tpu_custom_call" | custom-call | flops 2000000 | bytes 2097152 | tf_op jit(solution)/shard_map/pallas_call | solution.py:391
  43.6 0.1 shard_map.55
  43.7 6.7 %all_to_all.89 = bf16[4,96,128]{2,1,0:T(8,128)(2,1)S(1)} all-to-all(bf16[4,96,128]{2,1,0:T(8,128)(2,1)S(1)} %bitcast.55), channel_id=1, replica_groups=mesh['groups'=2,'ta'=4,'gx'=4] {'gx'}, dimensions={0} | all-to-all | bytes 196608 | tf_op jit(solution)/shard_map/all_to_all | solution.py:426
  50.4 3.4 %all-to-all-start.5 = ((bf16[4,192,128]{2,1,0:T(8,128)(2,1)}), bf16[4,192,128]{2,1,0:T(8,128)(2,1)S(1)}, u32[]{:S(2)}, u32[]{:S(2)}) async-start(bf16[4,192,128]{2,1,0:T(8,128)(2,1)} %bitcast.14), calls=%async_computation.5 | async-start | bytes 393216 | tf_op jit(solution)/shard_map/all_to_all | solution.py:423
  53.7 0.8 %shard_map.56.acc_ref = f32[768,128]{1,0:T(8,128)S(1)} custom-call(f32[768,128]{1,0:T(8,128)S(1)} %get-tuple-element.26.f_ref.refs_0_.refs_2_, bf16[1152,128]{1,0:T(8,128)(2,1)S(1)} %bitcast.31), custom_call_target="tpu_custom_call" | custom-call | flops 5000000 | bytes 2097152 | tf_op jit(solution)/shard_map/pallas_call | solution.py:391
  54.5 0.1 shard_map.57.acc_ref
  54.6 6.6 %all-to-all-done.5 = bf16[4,192,128]{2,1,0:T(8,128)(2,1)S(1)} async-done(((bf16[4,192,128]{2,1,0:T(8,128)(2,1)}), bf16[4,192,128]{2,1,0:T(8,128)(2,1)S(1)}, u32[]{:S(2)}, u32[]{:S(2)}) %all-to-all-start.5) | async-done | bytes 196640 | tf_op jit(solution)/shard_map/all_to_all | solution.py:423
  61.2 1.2 %shard_map.58 = (f32[768,128]{1,0:T(8,128)S(1)}, bf16[768,128]{1,0:T(8,128)(2,1)}) custom-call(bf16[1152,128]{1,0:T(8,128)(2,1)S(1)} %bitcast.33, bf16[1152,128]{1,0:T(8,128)(2,1)S(1)} %bitcast.45, f32[768,128]{1,0:T(8,128)S(1)} %shard_map.57.acc_ref, bf16[768,128]{1,0:T(8,128)(2,1)S(1)} %bitcast.48), custom_call_target="tpu_custom_call" | custom-call | flops 4000000 | bytes 2097152 | tf_op jit(solution)/shard_map/pallas_call | solution.py:391
  62.4 0.1 shard_map.59
  62.4 6.7 %all_to_all.90 = bf16[4,96,128]{2,1,0:T(8,128)(2,1)S(1)} all-to-all(bf16[4,96,128]{2,1,0:T(8,128)(2,1)S(1)} %bitcast.56), channel_id=1, replica_groups=mesh['groups'=2,'ta'=4,'gx'=4] {'gx'}, dimensions={0} | all-to-all | bytes 196608 | tf_op jit(solution)/shard_map/all_to_all | solution.py:426
  69.1 3.4 %all-to-all-start.7 = ((bf16[4,192,128]{2,1,0:T(8,128)(2,1)}), bf16[4,192,128]{2,1,0:T(8,128)(2,1)S(1)}, u32[]{:S(2)}, u32[]{:S(2)}) async-start(bf16[4,192,128]{2,1,0:T(8,128)(2,1)} %bitcast.18), calls=%async_computation.7 | async-start | bytes 393216 | tf_op jit(solution)/shard_map/all_to_all | solution.py:423
  72.5 1.1 %shard_map.60.acc_ref = f32[768,128]{1,0:T(8,128)S(1)} custom-call(f32[768,128]{1,0:T(8,128)S(1)} %get-tuple-element.30.f_ref.refs_0_, bf16[1152,128]{1,0:T(8,128)(2,1)S(1)} %bitcast.35, f32[768,128]{1,0:T(8,128)S(1)} %get-tuple-element.26.f_ref.refs_0_.refs_2_, bf16[1152,128]{1,0:T(8,128)(2,1)S(1)} %bitcast.43), custom_call_target="tpu_custom_call" | custom-call | flops 8000000 | bytes 2097152 | tf_op jit(solution)/shard_map/pallas_call | solution.py:391
  73.6 0.1 shard_map.61.acc_ref
  73.7 6.3 %all-to-all-done.7 = bf16[4,192,128]{2,1,0:T(8,128)(2,1)S(1)} async-done(((bf16[4,192,128]{2,1,0:T(8,128)(2,1)}), bf16[4,192,128]{2,1,0:T(8,128)(2,1)S(1)}, u32[]{:S(2)}, u32[]{:S(2)}) %all-to-all-start.7) | async-done | bytes 196640 | tf_op jit(solution)/shard_map/all_to_all | solution.py:423
  80.0 0.7 shard_map.62
Async XLA Ops:
  0.0 1.0 %copy-start = (bf16[4,3,3,2,2,2,4,128]{7,6,5,4,3,2,1,0:T(4,128)(2,1)S(1)}, bf16[4,3,3,2,2,2,4,128]{7,6,5,4,3,2,1,0:T(4,128)(2,1)}, u32[]{:S(2)}) copy-start(bf16[4,3,3,2,2,2,4,128]{7,6,5,4,3,2,1,0:T(4,128)(2,1)} %param.5) | copy-start | bytes 884740
  1.0 0.9 %copy-start.2 = (bf16[4,4,3,2,2,4,128]{6,5,4,3,2,1,0:T(4,128)(2,1)S(1)}, bf16[4,4,3,2,2,4,128]{6,5,4,3,2,1,0:T(4,128)(2,1)}, u32[]{:S(2)}) copy-start(bf16[4,4,3,2,2,4,128]{6,5,4,3,2,1,0:T(4,128)(2,1)} %param.4) | copy-start | bytes 589828
  2.6 8.5 %all-to-all-start = ((bf16[4,96,128]{2,1,0:T(8,128)(2,1)}), bf16[4,96,128]{2,1,0:T(8,128)(2,1)S(1)}, u32[]{:S(2)}, u32[]{:S(2)}) async-start(bf16[4,96,128]{2,1,0:T(8,128)(2,1)} %bitcast.3), calls=%async_computation | async-start | bytes 196608 | tf_op jit(solution)/shard_map/all_to_all | solution.py:426
  6.8 9.7 %copy-start.3 = (bf16[4,4,3,2,2,4,128]{6,5,4,3,2,1,0:T(4,128)(2,1)S(1)}, bf16[4,4,3,2,2,4,128]{6,5,4,3,2,1,0:T(4,128)(2,1)}, u32[]{:S(2)}) copy-start(bf16[4,4,3,2,2,4,128]{6,5,4,3,2,1,0:T(4,128)(2,1)} %param.4) | copy-start | bytes 589828
  8.6 7.9 %copy-start.1 = (bf16[4,3,3,2,2,2,4,128]{7,6,5,4,3,2,1,0:T(4,128)(2,1)S(1)}, bf16[4,3,3,2,2,2,4,128]{7,6,5,4,3,2,1,0:T(4,128)(2,1)}, u32[]{:S(2)}) copy-start(bf16[4,3,3,2,2,2,4,128]{7,6,5,4,3,2,1,0:T(4,128)(2,1)} %param.5) | copy-start | bytes 884740
  11.1 12.7 %all-to-all-start.1 = ((bf16[4,192,128]{2,1,0:T(8,128)(2,1)}), bf16[4,192,128]{2,1,0:T(8,128)(2,1)S(1)}, u32[]{:S(2)}, u32[]{:S(2)}) async-start(bf16[4,192,128]{2,1,0:T(8,128)(2,1)} %bitcast.5), calls=%async_computation.1 | async-start | bytes 393216 | tf_op jit(solution)/shard_map/all_to_all | solution.py:423
  17.4 6.4 %copy-start.5 = (bf16[2,6,6,2,2,4,128]{6,5,4,3,2,1,0:T(4,128)(2,1)S(1)}, bf16[2,6,6,2,2,4,128]{6,5,4,3,2,1,0:T(4,128)(2,1)}, u32[]{:S(2)}) copy-start(bf16[2,6,6,2,2,4,128]{6,5,4,3,2,1,0:T(4,128)(2,1)} %param.7) | copy-start | bytes 884740
  25.1 10.2 %copy-start.4 = (bf16[2,6,6,2,2,4,128]{6,5,4,3,2,1,0:T(4,128)(2,1)S(1)}, bf16[2,6,6,2,2,4,128]{6,5,4,3,2,1,0:T(4,128)(2,1)}, u32[]{:S(2)}) copy-start(bf16[2,6,6,2,2,4,128]{6,5,4,3,2,1,0:T(4,128)(2,1)} %param.6) | copy-start | bytes 884740
  31.9 10.9 %all-to-all-start.3 = ((bf16[4,192,128]{2,1,0:T(8,128)(2,1)}), bf16[4,192,128]{2,1,0:T(8,128)(2,1)S(1)}, u32[]{:S(2)}, u32[]{:S(2)}) async-start(bf16[4,192,128]{2,1,0:T(8,128)(2,1)} %bitcast.10), calls=%async_computation.3 | async-start | bytes 393216 | tf_op jit(solution)/shard_map/all_to_all | solution.py:423
  50.4 10.9 %all-to-all-start.5 = ((bf16[4,192,128]{2,1,0:T(8,128)(2,1)}), bf16[4,192,128]{2,1,0:T(8,128)(2,1)S(1)}, u32[]{:S(2)}, u32[]{:S(2)}) async-start(bf16[4,192,128]{2,1,0:T(8,128)(2,1)} %bitcast.14), calls=%async_computation.5 | async-start | bytes 393216 | tf_op jit(solution)/shard_map/all_to_all | solution.py:423
  69.1 10.9 %all-to-all-start.7 = ((bf16[4,192,128]{2,1,0:T(8,128)(2,1)}), bf16[4,192,128]{2,1,0:T(8,128)(2,1)S(1)}, u32[]{:S(2)}, u32[]{:S(2)}) async-start(bf16[4,192,128]{2,1,0:T(8,128)(2,1)} %bitcast.18), calls=%async_computation.7 | async-start | bytes 393216 | tf_op jit(solution)/shard_map/all_to_all | solution.py:423

commit v9 on v6

--- a/solution.py
+++ b/solution.py
@@ -73,8 +73,18 @@
     return [(function(re), function(im)) for re, im in half]
 
 
+def block_rows(index):
+    if isinstance(index, int):
+        return slice(index * 16, (index + 1) * 16)
+    return pl.ds(pl.multiple_of(index * 16, 16), 16)
+
+
+def loop(count, body):
+    lax.fori_loop(0, count, lambda i, carry: (body(i), carry)[1], 0)
+
+
 def load_pair(ref, index):
-    block = ref[index * 16:(index + 1) * 16, :].astype(F32)
+    block = ref[block_rows(index), :].astype(F32)
     return block[0:8], block[8:16]
 
 
@@ -94,7 +104,7 @@
 
 
 def store_pair(ref, index, pair):
-    ref[index * 16:(index + 1) * 16, :] = jnp.concatenate(pair, axis=0).astype(ref.dtype)
+    ref[block_rows(index), :] = jnp.concatenate(pair, axis=0).astype(ref.dtype)
 
 
 def store_field(ref, r, field):
@@ -147,7 +157,8 @@
     t_idx, _ = site_masks()
     first = t_idx == 0
     links = t_edges(load_links(links_ref, 0, parity))
-    for r in range(RHS):
+    @functools.partial(loop, RHS)
+    def _(r):
         ready(r)
         field = load_field(f_ref, r)
         ahead, behind = project(field, 0, -1), project(field, 0, 1)
@@ -172,7 +183,8 @@
             out = select(x_idx == row + step * k, roll_rows(values[k], step * k), out)
         return out
 
-    for q in range(RHS // 2):
+    @functools.partial(loop, RHS // 2)
+    def _(q):
         fields = [load_field(f_ref, r) for r in (2 * q, 2 * q + 1)]
         ahead = [project(field, 1, -1) for field in fields]
         behind = [project(field, 1, 1) for field in fields]
@@ -189,14 +201,17 @@
 def start_kernel(f_hbm, links_hbm, *refs):
     outs, (f_ref, links_ref, sems) = refs[:2], refs[2:]
     part = f_ref.shape[0] // RHS
-    copies = [pltpu.make_async_copy(links_hbm.at[pl.ds(0, links_ref.shape[0])], links_ref, sems.at[RHS])]
+
+    def copy_of(r):
+        rows = pl.ds(pl.multiple_of(r * part, part), part)
+        return pltpu.make_async_copy(f_hbm.at[rows], f_ref.at[rows], sems.at[r])
+
+    link_copy = pltpu.make_async_copy(links_hbm.at[pl.ds(0, links_ref.shape[0])], links_ref, sems.at[RHS])
+    link_copy.start()
     for r in range(RHS):
-        rows = pl.ds(r * part, part)
-        copies.append(pltpu.make_async_copy(f_hbm.at[rows], f_ref.at[rows], sems.at[r]))
-    for copy in copies:
-        copy.start()
-    copies[0].wait()
-    send_t(f_ref, links_ref, 0, *outs, ready=lambda r: copies[1 + r].wait())
+        copy_of(r).start()
+    link_copy.wait()
+    send_t(f_ref, links_ref, 0, *outs, ready=lambda r: copy_of(r).wait())
 
 
 def interior_kernel(parity, with_base, *refs):
@@ -232,7 +247,8 @@
             behind_of = lambda v: select(x_idx > 0, roll_rows(v, 1), 0.0)
         links_out = load_links(links_ref, mu, out_parity)
         links_in = load_links(links_ref, mu, parity)
-        for r in range(RHS):
+        @functools.partial(loop, RHS)
+        def _(r):
             field = load_field(f_ref, r)
             if mu == 2 and not with_base:
                 acc = [(zero, zero)] * 12
@@ -256,7 +272,8 @@
                 if scale != 1.0:
                     re, im = re * scale, im * scale
                 matrix[i, j] = (re, re + im, im - re)
-        for r in range(RHS):
+        @functools.partial(loop, RHS)
+        def _(r):
             field = get_field(r)[chi * 6:chi * 6 + 6]
             both = [vr + vi for vr, vi in field]
             for i in range(6):
@@ -310,17 +327,18 @@
     _, x_idx = site_masks()
     sign = jnp.where(x_idx == 3, -1.0, 1.0).astype(F32)
     links = x_edges(load_links(links_ref, 1, 1 - parity))
-    for q in range(RHS // 2):
+    @functools.partial(loop, RHS // 2)
+    def _(q):
         nxt, last = [], []
         for c in range(3):
             near, far = load_pair(x_near, q * 3 + c), load_pair(x_far, q * 3 + c)
             nxt.append(either(even, near, far))
             last.append(either(even, far, near))
         ahead = matvec(links, nxt, False)
-        for r in (2 * q, 2 * q + 1):
+        for n, r in enumerate((2 * q, 2 * q + 1)):
             half = [None] * 6
             for s in range(2):
-                k = (r % 2) * 2 + s
+                k = n * 2 + s
                 for c in range(3):
                     half[s * 3 + c] = tuple(
                         select(
@@ -339,7 +357,8 @@
     first = t_idx == 0
     sign = jnp.where(first, 1.0, -1.0).astype(F32)
     links = t_edges(load_links(links_ref, 0, 1 - parity))
-    for r in range(RHS):
+    @functools.partial(loop, RHS)
+    def _(r):
         nxt, last = [], []
         for c in range(3):
             one, two = load_pair(t_one, r * 3 + c), load_pair(t_two, r * 3 + c)
@@ -368,16 +387,14 @@
 
 def last_kernel(links_ref, acc_ref, t_one, t_two, out_hbm, held, sems):
     part = held.shape[0] // RHS
-    copies = []
-
-    def done(r):
-        rows = pl.ds(r * part, part)
-        copies.append(pltpu.make_async_copy(held.at[rows], out_hbm.at[rows], sems.at[r]))
-        copies[-1].start()
-
-    join_t(links_ref, acc_ref, t_one, t_two, 1, held, done)
-    for copy in copies:
-        copy.wait()
+
+    def copy_of(r):
+        rows = pl.ds(pl.multiple_of(r * part, part), part)
+        return pltpu.make_async_copy(held.at[rows], out_hbm.at[rows], sems.at[r])
+
+    join_t(links_ref, acc_ref, t_one, t_two, 1, held, lambda r: copy_of(r).start())
+    for r in range(RHS):
+        copy_of(r).wait()
 
 
 ROWS = RHS * 24 * 8

time: 31.6 us -> 32.5 us (1.028)
  Pallas kernels: 7.58 us -> 10.1 us
  waiting for transfers between devices: 4.79 us -> 3.72 us
  starting transfers between devices: 18.9 us -> 18 us
  local copies, waits for them, and re-layouts: 0.02 us -> 0.36 us
    pallas_call x17, Pallas kernels: 7.58 us -> 10.1 us  [call(): pl.pallas_call(kernel, out_shape=tuple((jax.ShapeDtypeStruct(shape, dtype...]
    ppermute x8, waiting for transfers between devices: 3.6 us -> 1.82 us  [swap(): return lax.ppermute(value, axis, pairs)]
    ppermute x8, waiting for transfers between devices: 1.18 us -> 1.9 us  [swap_t(): return lax.ppermute(value, ('ta', 'gx'), pairs)]
    ppermute x8, starting transfers between devices: 6.59 us -> 6.03 us  [swap(): return lax.ppermute(value, axis, pairs)]
    ppermute x8, starting transfers between devices: 12.3 us -> 12 us  [swap_t(): return lax.ppermute(value, ('ta', 'gx'), pairs)]
    unnamed x8, local copies, waits for them, and re-layouts: 0.02 us -> 0.36 us
  transfers between devices with their start and end apart: 16 -> 16, of which waited for: 7 -> 7; matrix products, arithmetic and copies ran while one was open for 0% -> 0% of each run, Pallas kernels for 15% -> 21%
where the time goes in v9:
time: 32.5 us; the launch traced here: 32.3 us
  starting transfers between devices  18 us (55%)
  Pallas kernels  10.1 us (31%)
  waiting for transfers between devices  3.72 us (11%)
  local copies, waits for them, and re-layouts  0.36 us (1%)
    ppermute x8, starting transfers between devices, swap_t(): return lax.ppermute(value, ('ta', 'gx'), pairs)  12 us
    pallas_call x17, Pallas kernels, call(): pl.pallas_call(kernel, out_shape=tuple((jax.ShapeDtypeStruct(shape, dtype...  10.1 us
    ppermute x8, starting transfers between devices, swap(): return lax.ppermute(value, axis, pairs)  6.03 us
    ppermute x8, waiting for transfers between devices, swap_t(): return lax.ppermute(value, ('ta', 'gx'), pairs)  1.9 us
    ppermute x8, waiting for transfers between devices, swap(): return lax.ppermute(value, axis, pairs)  1.82 us
  transfers between devices with their start and end apart: 16, of which 7 were waited for; matrix products, arithmetic and copies ran while one was open for 0% of the time, Pallas kernels for 21%

profile of v9, /device:TPU:0, one launch (start us, length us, event | category | flops | bytes accessed | tf_op | source)
XLA Modules:
  0.0 32.3 jit_solution(14584168261046030649)
XLA Ops:
  0.0 1.1 %shard_map.49 = (bf16[192,128]{1,0:T(8,128)(2,1)S(1)}, bf16[192,128]{1,0:T(8,128)(2,1)S(1)}) custom-call(bf16[768,128]{1,0:T(8,128)(2,1)} %bitcast.22, bf16[1152,128]{1,0:T(8,128)(2,1)} %bitcast.5), custom_call_target="tpu_custom_call" | custom-call | flops 1500000 | bytes 2097152 | tf_op jit(solution)/shard_map/pallas_call | solution.py:407
  1.1 3.1 %collective-permute-start.2 = (bf16[192,128]{1,0:T(8,128)(2,1)S(1)}, bf16[192,128]{1,0:T(8,128)(2,1)S(1)}, u32[]{:S(2)}, u32[]{:S(2)}) collective-permute-start(bf16[192,128]{1,0:T(8,128)(2,1)S(1)} %get-tuple-element.41), channel_id=1, source_target_pairs={{0,4},{1,13},{2,6},{3,15},{4,0},{5,9},{6,2},{7,11},{8,12},{9,5},{1... | collective-permute-start | bytes 147464 | tf_op jit(solution)/shard_map/ppermute | solution.py:433
  4.2 2.5 %collective-permute-start.3 = (bf16[192,128]{1,0:T(8,128)(2,1)S(1)}, bf16[192,128]{1,0:T(8,128)(2,1)S(1)}, u32[]{:S(2)}, u32[]{:S(2)}) collective-permute-start(bf16[192,128]{1,0:T(8,128)(2,1)S(1)} %get-tuple-element.42), channel_id=1, source_target_pairs={{0,12},{1,5},{2,14},{3,7},{4,8},{5,1},{6,10},{7,3},{8,4},{9,13},{1... | collective-permute-start | bytes 147464 | tf_op jit(solution)/shard_map/ppermute | solution.py:433
  6.7 0.1 shard_map.46
  6.8 0.3 collective-permute-start
  7.1 1.4 %collective-permute-start.1 = (bf16[96,128]{1,0:T(8,128)(2,1)S(1)}, bf16[96,128]{1,0:T(8,128)(2,1)S(1)}, u32[]{:S(2)}, u32[]{:S(2)}) collective-permute-start(bf16[96,128]{1,0:T(8,128)(2,1)S(1)} %get-tuple-element.40), channel_id=1, source_target_pairs={{0,1},{1,0},{2,3},{3,2},{4,5},{5,4},{6,7},{7,6},{8,9},{9,8},{10,11... | collective-permute-start | bytes 73736 | tf_op jit(solution)/shard_map/ppermute | solution.py:422
  8.5 1.4 %shard_map.47.acc_ref = f32[768,128]{1,0:T(8,128)S(1)} custom-call(bf16[768,128]{1,0:T(8,128)(2,1)S(1)} %bitcast.24, bf16[1152,128]{1,0:T(8,128)(2,1)S(1)} %bitcast.7), custom_call_target="tpu_custom_call" | custom-call | flops 5000000 | bytes 2097152 | tf_op jit(solution)/shard_map/pallas_call | solution.py:407
  9.9 0.0 copy-start.3
  9.9 0.5 %collective-permute-done.x_far = bf16[96,128]{1,0:T(8,128)(2,1)S(1)} collective-permute-done((bf16[96,128]{1,0:T(8,128)(2,1)S(1)}, bf16[96,128]{1,0:T(8,128)(2,1)S(1)}, u32[]{:S(2)}, u32[]{:S(2)}) %collective-permute-start) | collective-permute-done | bytes 24608 | tf_op jit(solution)/shard_map/ppermute | solution.py:422
  10.4 0.0 collective-permute-done.1.x_near
  10.4 0.1 shard_map.48.acc_ref
  10.5 0.0 collective-permute-done.3.t_two
  10.5 0.3 %copy-done.3 = bf16[2,6,6,2,2,4,128]{6,5,4,3,2,1,0:T(4,128)(2,1)S(1)} copy-done((bf16[2,6,6,2,2,4,128]{6,5,4,3,2,1,0:T(4,128)(2,1)S(1)}, bf16[2,6,6,2,2,4,128]{6,5,4,3,2,1,0:T(4,128)(2,1)}, u32[]{:S(2)}) %copy-start.3) | copy-done | bytes 294936
  10.8 0.6 %shard_map.50 = (f32[768,128]{1,0:T(8,128)S(1)}, bf16[192,128]{1,0:T(8,128)(2,1)S(1)}, bf16[192,128]{1,0:T(8,128)(2,1)S(1)}) custom-call(bf16[1152,128]{1,0:T(8,128)(2,1)S(1)} %bitcast.9, bf16[1152,128]{1,0:T(8,128)(2,1)S(1)} %bitcast.28, f32[768,128]{1,0:T(8,128)S(1)} %shard_map.48.acc_ref, bf16[192,128]{1,0:T(8,128)(2,1)S(1)} %collective-permute-done.2.t_one, ...), custom_call_target="tpu_custom_call" | custom-call | flops 4000000 | bytes 2097152 | tf_op jit(solution)/shard_map/pallas_call | solution.py:407
  11.4 0.7 %collective-permute-start.6 = (bf16[192,128]{1,0:T(8,128)(2,1)S(1)}, bf16[192,128]{1,0:T(8,128)(2,1)S(1)}, u32[]{:S(2)}, u32[]{:S(2)}) collective-permute-start(bf16[192,128]{1,0:T(8,128)(2,1)S(1)} %get-tuple-element.49), channel_id=1, source_target_pairs={{0,4},{1,13},{2,6},{3,15},{4,0},{5,9},{6,2},{7,11},{8,12},{9,5},{1... | collective-permute-start | bytes 147464 | tf_op jit(solution)/shard_map/ppermute | solution.py:433
  12.2 1.2 %collective-permute-start.7 = (bf16[192,128]{1,0:T(8,128)(2,1)S(1)}, bf16[192,128]{1,0:T(8,128)(2,1)S(1)}, u32[]{:S(2)}, u32[]{:S(2)}) collective-permute-start(bf16[192,128]{1,0:T(8,128)(2,1)S(1)} %get-tuple-element.50), channel_id=1, source_target_pairs={{0,12},{1,5},{2,14},{3,7},{4,8},{5,1},{6,10},{7,3},{8,4},{9,13},{1... | collective-permute-start | bytes 147464 | tf_op jit(solution)/shard_map/ppermute | solution.py:433
  13.3 0.1 shard_map.51
  13.4 0.1 collective-permute-start.4
  13.5 1.6 %collective-permute-start.5 = (bf16[96,128]{1,0:T(8,128)(2,1)S(1)}, bf16[96,128]{1,0:T(8,128)(2,1)S(1)}, u32[]{:S(2)}, u32[]{:S(2)}) collective-permute-start(bf16[96,128]{1,0:T(8,128)(2,1)S(1)} %get-tuple-element.48), channel_id=1, source_target_pairs={{0,1},{1,0},{2,3},{3,2},{4,5},{5,4},{6,7},{7,6},{8,9},{9,8},{10,11... | collective-permute-start | bytes 73736 | tf_op jit(solution)/shard_map/ppermute | solution.py:422
  15.1 1.7 %shard_map.52.acc_ref = f32[768,128]{1,0:T(8,128)S(1)} custom-call(f32[768,128]{1,0:T(8,128)S(1)} %get-tuple-element.46.f_ref.refs_0_, bf16[1152,128]{1,0:T(8,128)(2,1)S(1)} %bitcast.11, bf16[768,128]{1,0:T(8,128)(2,1)S(1)} %bitcast.25, bf16[1152,128]{1,0:T(8,128)(2,1)S(1)} %bitcast.26), custom_call_target="tpu_custom_call" | custom-call | flops 8000000 | bytes 2097152 | tf_op jit(solution)/shard_map/pallas_call | solution.py:407
  16.8 0.2 collective-permute-done.4.x_far
  17.0 0.1 shard_map.53.acc_ref
  17.1 0.0 collective-permute-done.6.t_one
  17.1 1.0 %collective-permute-done.7.t_two = bf16[192,128]{1,0:T(8,128)(2,1)S(1)} collective-permute-done((bf16[192,128]{1,0:T(8,128)(2,1)S(1)}, bf16[192,128]{1,0:T(8,128)(2,1)S(1)}, u32[]{:S(2)}, u32[]{:S(2)}) %collective-permute-start.7) | collective-permute-done | bytes 49184 | tf_op jit(solution)/shard_map/ppermute | solution.py:433
  18.1 0.2 shard_map.54
  18.3 0.1 collective-permute-start.10
  18.4 1.9 %collective-permute-start.11 = (bf16[192,128]{1,0:T(8,128)(2,1)S(1)}, bf16[192,128]{1,0:T(8,128)(2,1)S(1)}, u32[]{:S(2)}, u32[]{:S(2)}) collective-permute-start(bf16[192,128]{1,0:T(8,128)(2,1)S(1)} %get-tuple-element.58), channel_id=1, source_target_pairs={{0,12},{1,5},{2,14},{3,7},{4,8},{5,1},{6,10},{7,3},{8,4},{9,13},{1... | collective-permute-start | bytes 147464 | tf_op jit(solution)/shard_map/ppermute | solution.py:433
  20.3 0.1 shard_map.55
  20.4 0.1 collective-permute-start.8
  20.5 1.5 %collective-permute-start.9 = (bf16[96,128]{1,0:T(8,128)(2,1)S(1)}, bf16[96,128]{1,0:T(8,128)(2,1)S(1)}, u32[]{:S(2)}, u32[]{:S(2)}) collective-permute-start(bf16[96,128]{1,0:T(8,128)(2,1)S(1)} %get-tuple-element.56), channel_id=1, source_target_pairs={{0,1},{1,0},{2,3},{3,2},{4,5},{5,4},{6,7},{7,6},{8,9},{9,8},{10,11... | collective-permute-start | bytes 73736 | tf_op jit(solution)/shard_map/ppermute | solution.py:422
  22.0 1.3 %shard_map.56.acc_ref = f32[768,128]{1,0:T(8,128)S(1)} custom-call(f32[768,128]{1,0:T(8,128)S(1)} %get-tuple-element.54.f_ref.refs_0_.refs_2_, bf16[1152,128]{1,0:T(8,128)(2,1)S(1)} %bitcast.15), custom_call_target="tpu_custom_call" | custom-call | flops 5000000 | bytes 2097152 | tf_op jit(solution)/shard_map/pallas_call | solution.py:407
  23.3 0.6 %collective-permute-done.8.x_far = bf16[96,128]{1,0:T(8,128)(2,1)S(1)} collective-permute-done((bf16[96,128]{1,0:T(8,128)(2,1)S(1)}, bf16[96,128]{1,0:T(8,128)(2,1)S(1)}, u32[]{:S(2)}, u32[]{:S(2)}) %collective-permute-start.8) | collective-permute-done | bytes 24608 | tf_op jit(solution)/shard_map/ppermute | solution.py:422
  23.9 0.0 collective-permute-done.9.x_near
  23.9 0.1 shard_map.57.acc_ref
  24.0 0.0 collective-permute-done.10.t_one
  24.0 0.4 %collective-permute-done.11.t_two = bf16[192,128]{1,0:T(8,128)(2,1)S(1)} collective-permute-done((bf16[192,128]{1,0:T(8,128)(2,1)S(1)}, bf16[192,128]{1,0:T(8,128)(2,1)S(1)}, u32[]{:S(2)}, u32[]{:S(2)}) %collective-permute-start.11) | collective-permute-done | bytes 49184 | tf_op jit(solution)/shard_map/ppermute | solution.py:433
  24.4 0.6 %shard_map.58 = (f32[768,128]{1,0:T(8,128)S(1)}, bf16[192,128]{1,0:T(8,128)(2,1)S(1)}, bf16[192,128]{1,0:T(8,128)(2,1)S(1)}) custom-call(bf16[1152,128]{1,0:T(8,128)(2,1)S(1)} %bitcast.17, bf16[1152,128]{1,0:T(8,128)(2,1)S(1)} %bitcast.29, f32[768,128]{1,0:T(8,128)S(1)} %shard_map.57.acc_ref, bf16[192,128]{1,0:T(8,128)(2,1)S(1)} %collective-permute-done.10.t_one, ...), custom_call_target="tpu_custom_call" | custom-call | flops 4000000 | bytes 2097152 | tf_op jit(solution)/shard_map/pallas_call | solution.py:407
  25.0 0.6 %collective-permute-start.14 = (bf16[192,128]{1,0:T(8,128)(2,1)S(1)}, bf16[192,128]{1,0:T(8,128)(2,1)S(1)}, u32[]{:S(2)}, u32[]{:S(2)}) collective-permute-start(bf16[192,128]{1,0:T(8,128)(2,1)S(1)} %get-tuple-element.65), channel_id=1, source_target_pairs={{0,4},{1,13},{2,6},{3,15},{4,0},{5,9},{6,2},{7,11},{8,12},{9,5},{1... | collective-permute-start | bytes 147464 | tf_op jit(solution)/shard_map/ppermute | solution.py:433
  25.7 1.9 %collective-permute-start.15 = (bf16[192,128]{1,0:T(8,128)(2,1)S(1)}, bf16[192,128]{1,0:T(8,128)(2,1)S(1)}, u32[]{:S(2)}, u32[]{:S(2)}) collective-permute-start(bf16[192,128]{1,0:T(8,128)(2,1)S(1)} %get-tuple-element.66), channel_id=1, source_target_pairs={{0,12},{1,5},{2,14},{3,7},{4,8},{5,1},{6,10},{7,3},{8,4},{9,13},{1... | collective-permute-start | bytes 147464 | tf_op jit(solution)/shard_map/ppermute | solution.py:433
  27.5 0.1 shard_map.59
  27.6 0.1 collective-permute-start.12
  27.7 1.1 %collective-permute-start.13 = (bf16[96,128]{1,0:T(8,128)(2,1)S(1)}, bf16[96,128]{1,0:T(8,128)(2,1)S(1)}, u32[]{:S(2)}, u32[]{:S(2)}) collective-permute-start(bf16[96,128]{1,0:T(8,128)(2,1)S(1)} %get-tuple-element.64), channel_id=1, source_target_pairs={{0,1},{1,0},{2,3},{3,2},{4,5},{5,4},{6,7},{7,6},{8,9},{9,8},{10,11... | collective-permute-start | bytes 73736 | tf_op jit(solution)/shard_map/ppermute | solution.py:422
  28.8 1.7 %shard_map.60.acc_ref = f32[768,128]{1,0:T(8,128)S(1)} custom-call(f32[768,128]{1,0:T(8,128)S(1)} %get-tuple-element.62.f_ref.refs_0_, bf16[1152,128]{1,0:T(8,128)(2,1)S(1)} %bitcast.19, f32[768,128]{1,0:T(8,128)S(1)} %get-tuple-element.54.f_ref.refs_0_.refs_2_, bf16[1152,128]{1,0:T(8,128)(2,1)S(1)} %bitcast.27), custom_call_target="tpu_custom_call" | custom-call | flops 8000000 | bytes 2097152 | tf_op jit(solution)/shard_map/pallas_call | solution.py:407
  30.4 0.5 %collective-permute-done.12.x_far = bf16[96,128]{1,0:T(8,128)(2,1)S(1)} collective-permute-done((bf16[96,128]{1,0:T(8,128)(2,1)S(1)}, bf16[96,128]{1,0:T(8,128)(2,1)S(1)}, u32[]{:S(2)}, u32[]{:S(2)}) %collective-permute-start.12) | collective-permute-done | bytes 24608 | tf_op jit(solution)/shard_map/ppermute | solution.py:422
  30.9 0.1 shard_map.61.acc_ref
  31.0 0.0 collective-permute-done.14.t_one
  31.1 0.5 %collective-permute-done.15.t_two = bf16[192,128]{1,0:T(8,128)(2,1)S(1)} collective-permute-done((bf16[192,128]{1,0:T(8,128)(2,1)S(1)}, bf16[192,128]{1,0:T(8,128)(2,1)S(1)}, u32[]{:S(2)}, u32[]{:S(2)}) %collective-permute-start.15) | collective-permute-done | bytes 49184 | tf_op jit(solution)/shard_map/ppermute | solution.py:433
  31.6 0.8 %shard_map.62 = bf16[768,128]{1,0:T(8,128)(2,1)} custom-call(bf16[1152,128]{1,0:T(8,128)(2,1)S(1)} %bitcast.21, f32[768,128]{1,0:T(8,128)S(1)} %shard_map.61.acc_ref, bf16[192,128]{1,0:T(8,128)(2,1)S(1)} %collective-permute-done.14.t_one, bf16[192,128]{1,0:T(8,128)(2,1)S(1)} %collective-permute-done.15.t_two), custom_call_target="tpu_custom_call" | custom-call | flops 1000000 | bytes 2097152 | tf_op jit(solution)/shard_map/pallas_call | solution.py:407
  (9 shorter events, 0.0 us)
Async XLA Ops:
  0.0 6.7 %copy-start = (bf16[4,3,3,2,2,2,4,128]{7,6,5,4,3,2,1,0:T(4,128)(2,1)S(1)}, bf16[4,3,3,2,2,2,4,128]{7,6,5,4,3,2,1,0:T(4,128)(2,1)}, u32[]{:S(2)}) copy-start(bf16[4,3,3,2,2,2,4,128]{7,6,5,4,3,2,1,0:T(4,128)(2,1)} %param.5) | copy-start | bytes 884740
  0.0 6.7 %copy-start.1 = (bf16[4,4,3,2,2,4,128]{6,5,4,3,2,1,0:T(4,128)(2,1)S(1)}, bf16[4,4,3,2,2,4,128]{6,5,4,3,2,1,0:T(4,128)(2,1)}, u32[]{:S(2)}) copy-start(bf16[4,4,3,2,2,4,128]{6,5,4,3,2,1,0:T(4,128)(2,1)} %param.4) | copy-start | bytes 589828
  1.1 9.3 %collective-permute-start.2 = (bf16[192,128]{1,0:T(8,128)(2,1)S(1)}, bf16[192,128]{1,0:T(8,128)(2,1)S(1)}, u32[]{:S(2)}, u32[]{:S(2)}) collective-permute-start(bf16[192,128]{1,0:T(8,128)(2,1)S(1)} %get-tuple-element.41), channel_id=1, source_target_pairs={{0,4},{1,13},{2,6},{3,15},{4,0},{5,9},{6,2},{7,11},{8,12},{9,5},{1... | collective-permute-start | bytes 147464 | tf_op jit(solution)/shard_map/ppermute | solution.py:433
  4.2 6.3 %collective-permute-start.3 = (bf16[192,128]{1,0:T(8,128)(2,1)S(1)}, bf16[192,128]{1,0:T(8,128)(2,1)S(1)}, u32[]{:S(2)}, u32[]{:S(2)}) collective-permute-start(bf16[192,128]{1,0:T(8,128)(2,1)S(1)} %get-tuple-element.42), channel_id=1, source_target_pairs={{0,12},{1,5},{2,14},{3,7},{4,8},{5,1},{6,10},{7,3},{8,4},{9,13},{1... | collective-permute-start | bytes 147464 | tf_op jit(solution)/shard_map/ppermute | solution.py:433
  6.8 3.5 %collective-permute-start = (bf16[96,128]{1,0:T(8,128)(2,1)S(1)}, bf16[96,128]{1,0:T(8,128)(2,1)S(1)}, u32[]{:S(2)}, u32[]{:S(2)}) collective-permute-start(bf16[96,128]{1,0:T(8,128)(2,1)S(1)} %get-tuple-element.39), channel_id=1, source_target_pairs={{0,3},{1,2},{2,1},{3,0},{4,7},{5,6},{6,5},{7,4},{8,11},{9,10},{10,... | collective-permute-start | bytes 73736 | tf_op jit(solution)/shard_map/ppermute | solution.py:422
  7.1 3.3 %collective-permute-start.1 = (bf16[96,128]{1,0:T(8,128)(2,1)S(1)}, bf16[96,128]{1,0:T(8,128)(2,1)S(1)}, u32[]{:S(2)}, u32[]{:S(2)}) collective-permute-start(bf16[96,128]{1,0:T(8,128)(2,1)S(1)} %get-tuple-element.40), channel_id=1, source_target_pairs={{0,1},{1,0},{2,3},{3,2},{4,5},{5,4},{6,7},{7,6},{8,9},{9,8},{10,11... | collective-permute-start | bytes 73736 | tf_op jit(solution)/shard_map/ppermute | solution.py:422
  9.9 1.0 %copy-start.3 = (bf16[2,6,6,2,2,4,128]{6,5,4,3,2,1,0:T(4,128)(2,1)S(1)}, bf16[2,6,6,2,2,4,128]{6,5,4,3,2,1,0:T(4,128)(2,1)}, u32[]{:S(2)}) copy-start(bf16[2,6,6,2,2,4,128]{6,5,4,3,2,1,0:T(4,128)(2,1)} %param.7) | copy-start | bytes 884740
  11.4 5.6 %collective-permute-start.6 = (bf16[192,128]{1,0:T(8,128)(2,1)S(1)}, bf16[192,128]{1,0:T(8,128)(2,1)S(1)}, u32[]{:S(2)}, u32[]{:S(2)}) collective-permute-start(bf16[192,128]{1,0:T(8,128)(2,1)S(1)} %get-tuple-element.49), channel_id=1, source_target_pairs={{0,4},{1,13},{2,6},{3,15},{4,0},{5,9},{6,2},{7,11},{8,12},{9,5},{1... | collective-permute-start | bytes 147464 | tf_op jit(solution)/shard_map/ppermute | solution.py:433
  12.2 5.9 %collective-permute-start.7 = (bf16[192,128]{1,0:T(8,128)(2,1)S(1)}, bf16[192,128]{1,0:T(8,128)(2,1)S(1)}, u32[]{:S(2)}, u32[]{:S(2)}) collective-permute-start(bf16[192,128]{1,0:T(8,128)(2,1)S(1)} %get-tuple-element.50), channel_id=1, source_target_pairs={{0,12},{1,5},{2,14},{3,7},{4,8},{5,1},{6,10},{7,3},{8,4},{9,13},{1... | collective-permute-start | bytes 147464 | tf_op jit(solution)/shard_map/ppermute | solution.py:433
  13.3 1.8 %copy-start.2 = (bf16[2,6,6,2,2,4,128]{6,5,4,3,2,1,0:T(4,128)(2,1)S(1)}, bf16[2,6,6,2,2,4,128]{6,5,4,3,2,1,0:T(4,128)(2,1)}, u32[]{:S(2)}) copy-start(bf16[2,6,6,2,2,4,128]{6,5,4,3,2,1,0:T(4,128)(2,1)} %param.6) | copy-start | bytes 884740
  13.4 3.5 %collective-permute-start.4 = (bf16[96,128]{1,0:T(8,128)(2,1)S(1)}, bf16[96,128]{1,0:T(8,128)(2,1)S(1)}, u32[]{:S(2)}, u32[]{:S(2)}) collective-permute-start(bf16[96,128]{1,0:T(8,128)(2,1)S(1)} %get-tuple-element.47), channel_id=1, source_target_pairs={{0,3},{1,2},{2,1},{3,0},{4,7},{5,6},{6,5},{7,4},{8,11},{9,10},{10,... | collective-permute-start | bytes 73736 | tf_op jit(solution)/shard_map/ppermute | solution.py:422
  13.5 3.5 %collective-permute-start.5 = (bf16[96,128]{1,0:T(8,128)(2,1)S(1)}, bf16[96,128]{1,0:T(8,128)(2,1)S(1)}, u32[]{:S(2)}, u32[]{:S(2)}) collective-permute-start(bf16[96,128]{1,0:T(8,128)(2,1)S(1)} %get-tuple-element.48), channel_id=1, source_target_pairs={{0,1},{1,0},{2,3},{3,2},{4,5},{5,4},{6,7},{7,6},{8,9},{9,8},{10,11... | collective-permute-start | bytes 73736 | tf_op jit(solution)/shard_map/ppermute | solution.py:422
  18.3 5.7 %collective-permute-start.10 = (bf16[192,128]{1,0:T(8,128)(2,1)S(1)}, bf16[192,128]{1,0:T(8,128)(2,1)S(1)}, u32[]{:S(2)}, u32[]{:S(2)}) collective-permute-start(bf16[192,128]{1,0:T(8,128)(2,1)S(1)} %get-tuple-element.57), channel_id=1, source_target_pairs={{0,4},{1,13},{2,6},{3,15},{4,0},{5,9},{6,2},{7,11},{8,12},{9,5},{1... | collective-permute-start | bytes 147464 | tf_op jit(solution)/shard_map/ppermute | solution.py:433
  18.4 6.0 %collective-permute-start.11 = (bf16[192,128]{1,0:T(8,128)(2,1)S(1)}, bf16[192,128]{1,0:T(8,128)(2,1)S(1)}, u32[]{:S(2)}, u32[]{:S(2)}) collective-permute-start(bf16[192,128]{1,0:T(8,128)(2,1)S(1)} %get-tuple-element.58), channel_id=1, source_target_pairs={{0,12},{1,5},{2,14},{3,7},{4,8},{5,1},{6,10},{7,3},{8,4},{9,13},{1... | collective-permute-start | bytes 147464 | tf_op jit(solution)/shard_map/ppermute | solution.py:433
  20.4 3.5 %collective-permute-start.8 = (bf16[96,128]{1,0:T(8,128)(2,1)S(1)}, bf16[96,128]{1,0:T(8,128)(2,1)S(1)}, u32[]{:S(2)}, u32[]{:S(2)}) collective-permute-start(bf16[96,128]{1,0:T(8,128)(2,1)S(1)} %get-tuple-element.55), channel_id=1, source_target_pairs={{0,3},{1,2},{2,1},{3,0},{4,7},{5,6},{6,5},{7,4},{8,11},{9,10},{10,... | collective-permute-start | bytes 73736 | tf_op jit(solution)/shard_map/ppermute | solution.py:422
  20.5 3.5 %collective-permute-start.9 = (bf16[96,128]{1,0:T(8,128)(2,1)S(1)}, bf16[96,128]{1,0:T(8,128)(2,1)S(1)}, u32[]{:S(2)}, u32[]{:S(2)}) collective-permute-start(bf16[96,128]{1,0:T(8,128)(2,1)S(1)} %get-tuple-element.56), channel_id=1, source_target_pairs={{0,1},{1,0},{2,3},{3,2},{4,5},{5,4},{6,7},{7,6},{8,9},{9,8},{10,11... | collective-permute-start | bytes 73736 | tf_op jit(solution)/shard_map/ppermute | solution.py:422
  25.0 6.0 %collective-permute-start.14 = (bf16[192,128]{1,0:T(8,128)(2,1)S(1)}, bf16[192,128]{1,0:T(8,128)(2,1)S(1)}, u32[]{:S(2)}, u32[]{:S(2)}) collective-permute-start(bf16[192,128]{1,0:T(8,128)(2,1)S(1)} %get-tuple-element.65), channel_id=1, source_target_pairs={{0,4},{1,13},{2,6},{3,15},{4,0},{5,9},{6,2},{7,11},{8,12},{9,5},{1... | collective-permute-start | bytes 147464 | tf_op jit(solution)/shard_map/ppermute | solution.py:433
  25.7 5.9 %collective-permute-start.15 = (bf16[192,128]{1,0:T(8,128)(2,1)S(1)}, bf16[192,128]{1,0:T(8,128)(2,1)S(1)}, u32[]{:S(2)}, u32[]{:S(2)}) collective-permute-start(bf16[192,128]{1,0:T(8,128)(2,1)S(1)} %get-tuple-element.66), channel_id=1, source_target_pairs={{0,12},{1,5},{2,14},{3,7},{4,8},{5,1},{6,10},{7,3},{8,4},{9,13},{1... | collective-permute-start | bytes 147464 | tf_op jit(solution)/shard_map/ppermute | solution.py:433
  27.6 3.3 %collective-permute-start.12 = (bf16[96,128]{1,0:T(8,128)(2,1)S(1)}, bf16[96,128]{1,0:T(8,128)(2,1)S(1)}, u32[]{:S(2)}, u32[]{:S(2)}) collective-permute-start(bf16[96,128]{1,0:T(8,128)(2,1)S(1)} %get-tuple-element.63), channel_id=1, source_target_pairs={{0,3},{1,2},{2,1},{3,0},{4,7},{5,6},{6,5},{7,4},{8,11},{9,10},{10,... | collective-permute-start | bytes 73736 | tf_op jit(solution)/shard_map/ppermute | solution.py:422
  27.7 3.2 %collective-permute-start.13 = (bf16[96,128]{1,0:T(8,128)(2,1)S(1)}, bf16[96,128]{1,0:T(8,128)(2,1)S(1)}, u32[]{:S(2)}, u32[]{:S(2)}) collective-permute-start(bf16[96,128]{1,0:T(8,128)(2,1)S(1)} %get-tuple-element.64), channel_id=1, source_target_pairs={{0,1},{1,0},{2,3},{3,2},{4,5},{5,4},{6,7},{7,6},{8,9},{9,8},{10,11... | collective-permute-start | bytes 73736 | tf_op jit(solution)/shard_map/ppermute | solution.py:422

commit v10 on v6

--- a/solution.py
+++ b/solution.py
@@ -186,17 +186,22 @@
             store_pair(x_far, q * 3 + c, either(even, fronts[c], rears[c]))
 
 
-def start_kernel(f_hbm, links_hbm, *refs):
-    outs, (f_ref, links_ref, sems) = refs[:2], refs[2:]
+def start_kernel(f_hbm, links_hbm, t_one, t_two, f_ref, links_ref, sems):
     part = f_ref.shape[0] // RHS
-    copies = [pltpu.make_async_copy(links_hbm.at[pl.ds(0, links_ref.shape[0])], links_ref, sems.at[RHS])]
-    for r in range(RHS):
-        rows = pl.ds(r * part, part)
-        copies.append(pltpu.make_async_copy(f_hbm.at[rows], f_ref.at[rows], sems.at[r]))
-    for copy in copies:
+    t_rows = links_ref.shape[0] // 4
+
+    def copy_rows(source, target, start, size, sem):
+        rows = pl.ds(start, size)
+        return pltpu.make_async_copy(source.at[rows], target.at[rows], sems.at[sem])
+
+    t_links = copy_rows(links_hbm, links_ref, 0, t_rows, RHS)
+    fields = [copy_rows(f_hbm, f_ref, r * part, part, r) for r in range(RHS)]
+    others = copy_rows(links_hbm, links_ref, t_rows, links_ref.shape[0] - t_rows, RHS + 1)
+    for copy in (t_links, *fields, others):
         copy.start()
-    copies[0].wait()
-    send_t(f_ref, links_ref, 0, *outs, ready=lambda r: copies[1 + r].wait())
+    t_links.wait()
+    send_t(f_ref, links_ref, 0, t_one, t_two, ready=lambda r: fields[r].wait())
+    others.wait()
 
 
 def interior_kernel(parity, with_base, *refs):
@@ -256,23 +261,26 @@
                 if scale != 1.0:
                     re, im = re * scale, im * scale
                 matrix[i, j] = (re, re + im, im - re)
-        for r in range(RHS):
-            field = get_field(r)[chi * 6:chi * 6 + 6]
-            both = [vr + vi for vr, vi in field]
+        for q in range(RHS // 2):
+            rhs = (2 * q, 2 * q + 1)
+            fields = [get_field(r)[chi * 6:chi * 6 + 6] for r in rhs]
+            sums = [[vr + vi for vr, vi in field] for field in fields]
             for i in range(6):
-                one = two = three = None
+                totals = [None, None]
                 for j in range(6):
-                    vr, vi = field[j]
                     m, plus, minus = matrix[min(i, j), max(i, j)]
-                    t_one = m * both[j]
-                    if i <= j:
-                        t_two, t_three = -(vi * plus), vr * minus
-                    else:
-                        t_two, t_three = vi * minus, -(vr * plus)
-                    one = t_one if one is None else one + t_one
-                    two = t_two if two is None else two + t_two
-                    three = t_three if three is None else three + t_three
-                store_pair(out_ref, r * 12 + chi * 6 + i, (one + two, one + three))
+                    for n in range(2):
+                        vr, vi = fields[n][j]
+                        one = m * sums[n][j]
+                        if i <= j:
+                            two, three = -(vi * plus), vr * minus
+                        else:
+                            two, three = vi * minus, -(vr * plus)
+                        old = totals[n]
+                        totals[n] = (one, two, three) if old is None else (old[0] + one, old[1] + two, old[2] + three)
+                for n, r in enumerate(rhs):
+                    one, two, three = totals[n]
+                    store_pair(out_ref, r * 12 + chi * 6 + i, (one + two, one + three))
 
 
 def matvec(links, vector, adjoint):
@@ -423,12 +431,10 @@
     even = clover_even.reshape(-1, 128)
     odd = clover_odd_inv.reshape(-1, 128)
     held = [pltpu.with_memory_space_constraint(v, pltpu.HBM) for v in (f, links)]
-    start_scratch = [
-        pltpu.VMEM((ROWS, 128), BF16),
-        pltpu.VMEM((links.shape[0] // 4, 128), BF16),
-        pltpu.SemaphoreType.DMA((RHS + 1,)),
-    ]
-    t_one, t_two = call(start_kernel, held, T_HALOS, 1_500_000, start_scratch, in_space=pltpu.HBM)
+    t_one, t_two, f, links = call(
+        start_kernel, held, T_HALOS + [(f.shape, BF16), (links.shape, BF16)], 1_500_000,
+        [pltpu.SemaphoreType.DMA((RHS + 2,))], in_space=pltpu.HBM,
+    )
     for hop in range(4):
         parity = hop % 2
         t_one, t_two = swap_t(t_one, True), swap_t(t_two, False)

time: 31.6 us -> 31.6 us (level)
  no operation moved by 1% of the time
where the time goes in v10:
time: 31.6 us; the launch traced here: 31.5 us
  starting transfers between devices  18.9 us (60%)
  Pallas kernels  7.6 us (24%)
  waiting for transfers between devices  4.79 us (15%)
    ppermute x8, starting transfers between devices, swap_t(): return lax.ppermute(value, ('ta', 'gx'), pairs)  12.3 us
    pallas_call x17, Pallas kernels, call(): pl.pallas_call(kernel, out_shape=tuple((jax.ShapeDtypeStruct(shape, dtype...  7.6 us
    ppermute x8, starting transfers between devices, swap(): return lax.ppermute(value, axis, pairs)  6.6 us
    ppermute x8, waiting for transfers between devices, swap(): return lax.ppermute(value, axis, pairs)  3.6 us
    ppermute x8, waiting for transfers between devices, swap_t(): return lax.ppermute(value, ('ta', 'gx'), pairs)  1.18 us
  transfers between devices with their start and end apart: 16, of which 7 were waited for; matrix products, arithmetic and copies ran while one was open for 0% of the time, Pallas kernels for 15%

profile of v10, /device:TPU:0, one launch (start us, length us, event | category | flops | bytes accessed | tf_op | source)
XLA Modules:
  0.0 31.5 jit_solution(11337101784034798932)
XLA Ops:
  0.0 1.1 %shard_map.46 = (bf16[192,128]{1,0:T(8,128)(2,1)S(1)}, bf16[192,128]{1,0:T(8,128)(2,1)S(1)}, bf16[768,128]{1,0:T(8,128)(2,1)S(1)}, bf16[1152,128]{1,0:T(8,128)(2,1)S(1)}) custom-call(bf16[768,128]{1,0:T(8,128)(2,1)} %bitcast.10, bf16[1152,128]{1,0:T(8,128)(2,1)} %bitcast.9), custom_call_target="tpu_custom_call" | custom-call | flops 1500000 | bytes 2097152 | tf_op jit(solution)/shard_map/pallas_call | solution.py:398
  1.1 3.1 %collective-permute-start.2 = (bf16[192,128]{1,0:T(8,128)(2,1)S(1)}, bf16[192,128]{1,0:T(8,128)(2,1)S(1)}, u32[]{:S(2)}, u32[]{:S(2)}) collective-permute-start(bf16[192,128]{1,0:T(8,128)(2,1)S(1)} %get-tuple-element.45), channel_id=1, source_target_pairs={{0,4},{1,13},{2,6},{3,15},{4,0},{5,9},{6,2},{7,11},{8,12},{9,5},{1... | collective-permute-start | bytes 147464 | tf_op jit(solution)/shard_map/ppermute | solution.py:424
  4.2 2.5 %collective-permute-start.3 = (bf16[192,128]{1,0:T(8,128)(2,1)S(1)}, bf16[192,128]{1,0:T(8,128)(2,1)S(1)}, u32[]{:S(2)}, u32[]{:S(2)}) collective-permute-start(bf16[192,128]{1,0:T(8,128)(2,1)S(1)} %get-tuple-element.46), channel_id=1, source_target_pairs={{0,12},{1,5},{2,14},{3,7},{4,8},{5,1},{6,10},{7,3},{8,4},{9,13},{1... | collective-permute-start | bytes 147464 | tf_op jit(solution)/shard_map/ppermute | solution.py:424
  6.7 0.1 shard_map.47
  6.8 0.3 collective-permute-start
  7.1 1.4 %collective-permute-start.1 = (bf16[96,128]{1,0:T(8,128)(2,1)S(1)}, bf16[96,128]{1,0:T(8,128)(2,1)S(1)}, u32[]{:S(2)}, u32[]{:S(2)}) collective-permute-start(bf16[96,128]{1,0:T(8,128)(2,1)S(1)} %get-tuple-element.44), channel_id=1, source_target_pairs={{0,1},{1,0},{2,3},{3,2},{4,5},{5,4},{6,7},{7,6},{8,9},{9,8},{10,11... | collective-permute-start | bytes 73736 | tf_op jit(solution)/shard_map/ppermute | solution.py:413
  8.5 0.9 %shard_map.48.acc_ref = f32[768,128]{1,0:T(8,128)S(1)} custom-call(bf16[768,128]{1,0:T(8,128)(2,1)S(1)} %get-tuple-element.42.f_ref.refs_0_.refs_2_, bf16[1152,128]{1,0:T(8,128)(2,1)S(1)} %get-tuple-element.38.links_ref.refs_1_), custom_call_target="tpu_custom_call" | custom-call | flops 5000000 | bytes 2097152 | tf_op jit(solution)/shard_map/pallas_call | solution.py:398
  9.3 0.0 copy-start.1
  9.3 1.0 %collective-permute-done.x_far = bf16[96,128]{1,0:T(8,128)(2,1)S(1)} collective-permute-done((bf16[96,128]{1,0:T(8,128)(2,1)S(1)}, bf16[96,128]{1,0:T(8,128)(2,1)S(1)}, u32[]{:S(2)}, u32[]{:S(2)}) %collective-permute-start) | collective-permute-done | bytes 24608 | tf_op jit(solution)/shard_map/ppermute | solution.py:413
  10.3 0.0 collective-permute-done.1.x_near
  10.3 0.1 shard_map.49.acc_ref
  10.4 0.0 collective-permute-done.2.t_one
  10.4 0.0 collective-permute-done.3.t_two
  10.5 0.5 %shard_map.50 = (f32[768,128]{1,0:T(8,128)S(1)}, bf16[192,128]{1,0:T(8,128)(2,1)S(1)}, bf16[192,128]{1,0:T(8,128)(2,1)S(1)}) custom-call(bf16[1152,128]{1,0:T(8,128)(2,1)S(1)} %get-tuple-element.38.links_ref.refs_1_, bf16[1152,128]{1,0:T(8,128)(2,1)S(1)} %bitcast.7, f32[768,128]{1,0:T(8,128)S(1)} %shard_map.49.acc_ref, ...), custom_call_target="tpu_custom_call" | custom-call | flops 4000000 | bytes 2097152 | tf_op jit(solution)/shard_map/pallas_call | solution.py:398
  10.9 0.6 %collective-permute-start.6 = (bf16[192,128]{1,0:T(8,128)(2,1)S(1)}, bf16[192,128]{1,0:T(8,128)(2,1)S(1)}, u32[]{:S(2)}, u32[]{:S(2)}) collective-permute-start(bf16[192,128]{1,0:T(8,128)(2,1)S(1)} %get-tuple-element.53), channel_id=1, source_target_pairs={{0,4},{1,13},{2,6},{3,15},{4,0},{5,9},{6,2},{7,11},{8,12},{9,5},{1... | collective-permute-start | bytes 147464 | tf_op jit(solution)/shard_map/ppermute | solution.py:424
  11.5 1.7 %collective-permute-start.7 = (bf16[192,128]{1,0:T(8,128)(2,1)S(1)}, bf16[192,128]{1,0:T(8,128)(2,1)S(1)}, u32[]{:S(2)}, u32[]{:S(2)}) collective-permute-start(bf16[192,128]{1,0:T(8,128)(2,1)S(1)} %get-tuple-element.54), channel_id=1, source_target_pairs={{0,12},{1,5},{2,14},{3,7},{4,8},{5,1},{6,10},{7,3},{8,4},{9,13},{1... | collective-permute-start | bytes 147464 | tf_op jit(solution)/shard_map/ppermute | solution.py:424
  13.2 0.1 shard_map.51
  13.3 0.1 collective-permute-start.4
  13.4 1.6 %collective-permute-start.5 = (bf16[96,128]{1,0:T(8,128)(2,1)S(1)}, bf16[96,128]{1,0:T(8,128)(2,1)S(1)}, u32[]{:S(2)}, u32[]{:S(2)}) collective-permute-start(bf16[96,128]{1,0:T(8,128)(2,1)S(1)} %get-tuple-element.52), channel_id=1, source_target_pairs={{0,1},{1,0},{2,3},{3,2},{4,5},{5,4},{6,7},{7,6},{8,9},{9,8},{10,11... | collective-permute-start | bytes 73736 | tf_op jit(solution)/shard_map/ppermute | solution.py:413
  15.0 1.1 %shard_map.52.acc_ref = f32[768,128]{1,0:T(8,128)S(1)} custom-call(f32[768,128]{1,0:T(8,128)S(1)} %get-tuple-element.50.f_ref.refs_0_, bf16[1152,128]{1,0:T(8,128)(2,1)S(1)} %get-tuple-element.38.links_ref.refs_1_, bf16[768,128]{1,0:T(8,128)(2,1)S(1)} %get-tuple-element.42.f_ref.refs_0_.refs_2_, bf16[1152,128]{1,0:T(8,128)(2,1)S(1)} %bitcast.5), custom_call_target="tpu_custom_call" | custom-call | flops 8000000 | bytes 2097152 | tf_op jit(solution)/shard_map/pallas_call | solution.py:398
  16.1 0.7 %collective-permute-done.4.x_far = bf16[96,128]{1,0:T(8,128)(2,1)S(1)} collective-permute-done((bf16[96,128]{1,0:T(8,128)(2,1)S(1)}, bf16[96,128]{1,0:T(8,128)(2,1)S(1)}, u32[]{:S(2)}, u32[]{:S(2)}) %collective-permute-start.4) | collective-permute-done | bytes 24608 | tf_op jit(solution)/shard_map/ppermute | solution.py:413
  16.8 0.0 collective-permute-done.5.x_near
  16.8 0.1 shard_map.53.acc_ref
  16.9 0.0 collective-permute-done.6.t_one
  16.9 0.5 %collective-permute-done.7.t_two = bf16[192,128]{1,0:T(8,128)(2,1)S(1)} collective-permute-done((bf16[192,128]{1,0:T(8,128)(2,1)S(1)}, bf16[192,128]{1,0:T(8,128)(2,1)S(1)}, u32[]{:S(2)}, u32[]{:S(2)}) %collective-permute-start.7) | collective-permute-done | bytes 49184 | tf_op jit(solution)/shard_map/ppermute | solution.py:424
  17.4 0.2 shard_map.54
  17.6 0.7 %collective-permute-start.10 = (bf16[192,128]{1,0:T(8,128)(2,1)S(1)}, bf16[192,128]{1,0:T(8,128)(2,1)S(1)}, u32[]{:S(2)}, u32[]{:S(2)}) collective-permute-start(bf16[192,128]{1,0:T(8,128)(2,1)S(1)} %get-tuple-element.61), channel_id=1, source_target_pairs={{0,4},{1,13},{2,6},{3,15},{4,0},{5,9},{6,2},{7,11},{8,12},{9,5},{1... | collective-permute-start | bytes 147464 | tf_op jit(solution)/shard_map/ppermute | solution.py:424
  18.2 1.8 %collective-permute-start.11 = (bf16[192,128]{1,0:T(8,128)(2,1)S(1)}, bf16[192,128]{1,0:T(8,128)(2,1)S(1)}, u32[]{:S(2)}, u32[]{:S(2)}) collective-permute-start(bf16[192,128]{1,0:T(8,128)(2,1)S(1)} %get-tuple-element.62), channel_id=1, source_target_pairs={{0,12},{1,5},{2,14},{3,7},{4,8},{5,1},{6,10},{7,3},{8,4},{9,13},{1... | collective-permute-start | bytes 147464 | tf_op jit(solution)/shard_map/ppermute | solution.py:424
  20.0 0.1 shard_map.55
  20.1 0.1 collective-permute-start.8
  20.2 1.6 %collective-permute-start.9 = (bf16[96,128]{1,0:T(8,128)(2,1)S(1)}, bf16[96,128]{1,0:T(8,128)(2,1)S(1)}, u32[]{:S(2)}, u32[]{:S(2)}) collective-permute-start(bf16[96,128]{1,0:T(8,128)(2,1)S(1)} %get-tuple-element.60), channel_id=1, source_target_pairs={{0,1},{1,0},{2,3},{3,2},{4,5},{5,4},{6,7},{7,6},{8,9},{9,8},{10,11... | collective-permute-start | bytes 73736 | tf_op jit(solution)/shard_map/ppermute | solution.py:413
  21.8 0.8 %shard_map.56.acc_ref = f32[768,128]{1,0:T(8,128)S(1)} custom-call(f32[768,128]{1,0:T(8,128)S(1)} %get-tuple-element.58.f_ref.refs_0_.refs_2_, bf16[1152,128]{1,0:T(8,128)(2,1)S(1)} %get-tuple-element.38.links_ref.refs_1_), custom_call_target="tpu_custom_call" | custom-call | flops 5000000 | bytes 2097152 | tf_op jit(solution)/shard_map/pallas_call | solution.py:398
  22.6 1.1 %collective-permute-done.8.x_far = bf16[96,128]{1,0:T(8,128)(2,1)S(1)} collective-permute-done((bf16[96,128]{1,0:T(8,128)(2,1)S(1)}, bf16[96,128]{1,0:T(8,128)(2,1)S(1)}, u32[]{:S(2)}, u32[]{:S(2)}) %collective-permute-start.8) | collective-permute-done | bytes 24608 | tf_op jit(solution)/shard_map/ppermute | solution.py:413
  23.6 0.1 shard_map.57.acc_ref
  23.7 0.0 collective-permute-done.10.t_one
  23.7 0.4 %collective-permute-done.11.t_two = bf16[192,128]{1,0:T(8,128)(2,1)S(1)} collective-permute-done((bf16[192,128]{1,0:T(8,128)(2,1)S(1)}, bf16[192,128]{1,0:T(8,128)(2,1)S(1)}, u32[]{:S(2)}, u32[]{:S(2)}) %collective-permute-start.11) | collective-permute-done | bytes 49184 | tf_op jit(solution)/shard_map/ppermute | solution.py:424
  24.1 0.5 %shard_map.58 = (f32[768,128]{1,0:T(8,128)S(1)}, bf16[192,128]{1,0:T(8,128)(2,1)S(1)}, bf16[192,128]{1,0:T(8,128)(2,1)S(1)}) custom-call(bf16[1152,128]{1,0:T(8,128)(2,1)S(1)} %get-tuple-element.38.links_ref.refs_1_, bf16[1152,128]{1,0:T(8,128)(2,1)S(1)} %bitcast.8, f32[768,128]{1,0:T(8,128)S(1)} %shard_map.57.acc_ref, ...), custom_call_target="tpu_custom_call" | custom-call | flops 4000000 | bytes 2097152 | tf_op jit(solution)/shard_map/pallas_call | solution.py:398
  24.6 0.1 collective-permute-start.14
  24.7 2.0 %collective-permute-start.15 = (bf16[192,128]{1,0:T(8,128)(2,1)S(1)}, bf16[192,128]{1,0:T(8,128)(2,1)S(1)}, u32[]{:S(2)}, u32[]{:S(2)}) collective-permute-start(bf16[192,128]{1,0:T(8,128)(2,1)S(1)} %get-tuple-element.70), channel_id=1, source_target_pairs={{0,12},{1,5},{2,14},{3,7},{4,8},{5,1},{6,10},{7,3},{8,4},{9,13},{1... | collective-permute-start | bytes 147464 | tf_op jit(solution)/shard_map/ppermute | solution.py:424
  26.7 0.1 shard_map.59
  26.8 0.1 collective-permute-start.12
  26.8 1.5 %collective-permute-start.13 = (bf16[96,128]{1,0:T(8,128)(2,1)S(1)}, bf16[96,128]{1,0:T(8,128)(2,1)S(1)}, u32[]{:S(2)}, u32[]{:S(2)}) collective-permute-start(bf16[96,128]{1,0:T(8,128)(2,1)S(1)} %get-tuple-element.68), channel_id=1, source_target_pairs={{0,1},{1,0},{2,3},{3,2},{4,5},{5,4},{6,7},{7,6},{8,9},{9,8},{10,11... | collective-permute-start | bytes 73736 | tf_op jit(solution)/shard_map/ppermute | solution.py:413
  28.4 1.1 %shard_map.60.acc_ref = f32[768,128]{1,0:T(8,128)S(1)} custom-call(f32[768,128]{1,0:T(8,128)S(1)} %get-tuple-element.66.f_ref.refs_0_, bf16[1152,128]{1,0:T(8,128)(2,1)S(1)} %get-tuple-element.38.links_ref.refs_1_, f32[768,128]{1,0:T(8,128)S(1)} %get-tuple-element.58.f_ref.refs_0_.refs_2_, bf16[1152,128]{1,0:T(8,128)(2,1)S(1)} %bitcast.6), custom_call_target="tpu_custom_call" | custom-call | flops 8000000 | bytes 2097152 | tf_op jit(solution)/shard_map/pallas_call | solution.py:398
  29.5 0.8 %collective-permute-done.12.x_far = bf16[96,128]{1,0:T(8,128)(2,1)S(1)} collective-permute-done((bf16[96,128]{1,0:T(8,128)(2,1)S(1)}, bf16[96,128]{1,0:T(8,128)(2,1)S(1)}, u32[]{:S(2)}, u32[]{:S(2)}) %collective-permute-start.12) | collective-permute-done | bytes 24608 | tf_op jit(solution)/shard_map/ppermute | solution.py:413
  30.3 0.1 shard_map.61.acc_ref
  30.4 0.0 collective-permute-done.14.t_one
  30.4 0.3 collective-permute-done.15.t_two
  30.7 0.8 %shard_map.62 = bf16[768,128]{1,0:T(8,128)(2,1)} custom-call(bf16[1152,128]{1,0:T(8,128)(2,1)S(1)} %get-tuple-element.38.links_ref.refs_1_, f32[768,128]{1,0:T(8,128)S(1)} %shard_map.61.acc_ref, bf16[192,128]{1,0:T(8,128)(2,1)S(1)} %collective-permute-done.14.t_one, bf16[192,128]{1,0:T(8,128)(2,1)S(1)} %collective-permute-done.15.t_two), custom_call_target="tpu_custom_call" | custom-call | flops 1000000 | bytes 2097152 | tf_op jit(solution)/shard_map/pallas_call | solution.py:398
  (5 shorter events, 0.0 us)
Async XLA Ops:
  1.1 9.3 %collective-permute-start.2 = (bf16[192,128]{1,0:T(8,128)(2,1)S(1)}, bf16[192,128]{1,0:T(8,128)(2,1)S(1)}, u32[]{:S(2)}, u32[]{:S(2)}) collective-permute-start(bf16[192,128]{1,0:T(8,128)(2,1)S(1)} %get-tuple-element.45), channel_id=1, source_target_pairs={{0,4},{1,13},{2,6},{3,15},{4,0},{5,9},{6,2},{7,11},{8,12},{9,5},{1... | collective-permute-start | bytes 147464 | tf_op jit(solution)/shard_map/ppermute | solution.py:424
  4.2 6.2 %collective-permute-start.3 = (bf16[192,128]{1,0:T(8,128)(2,1)S(1)}, bf16[192,128]{1,0:T(8,128)(2,1)S(1)}, u32[]{:S(2)}, u32[]{:S(2)}) collective-permute-start(bf16[192,128]{1,0:T(8,128)(2,1)S(1)} %get-tuple-element.46), channel_id=1, source_target_pairs={{0,12},{1,5},{2,14},{3,7},{4,8},{5,1},{6,10},{7,3},{8,4},{9,13},{1... | collective-permute-start | bytes 147464 | tf_op jit(solution)/shard_map/ppermute | solution.py:424
  6.8 3.5 %collective-permute-start = (bf16[96,128]{1,0:T(8,128)(2,1)S(1)}, bf16[96,128]{1,0:T(8,128)(2,1)S(1)}, u32[]{:S(2)}, u32[]{:S(2)}) collective-permute-start(bf16[96,128]{1,0:T(8,128)(2,1)S(1)} %get-tuple-element.43), channel_id=1, source_target_pairs={{0,3},{1,2},{2,1},{3,0},{4,7},{5,6},{6,5},{7,4},{8,11},{9,10},{10,... | collective-permute-start | bytes 73736 | tf_op jit(solution)/shard_map/ppermute | solution.py:413
  7.1 3.3 %collective-permute-start.1 = (bf16[96,128]{1,0:T(8,128)(2,1)S(1)}, bf16[96,128]{1,0:T(8,128)(2,1)S(1)}, u32[]{:S(2)}, u32[]{:S(2)}) collective-permute-start(bf16[96,128]{1,0:T(8,128)(2,1)S(1)} %get-tuple-element.44), channel_id=1, source_target_pairs={{0,1},{1,0},{2,3},{3,2},{4,5},{5,4},{6,7},{7,6},{8,9},{9,8},{10,11... | collective-permute-start | bytes 73736 | tf_op jit(solution)/shard_map/ppermute | solution.py:413
  9.3 1.1 %copy-start.1 = (bf16[2,6,6,2,2,4,128]{6,5,4,3,2,1,0:T(4,128)(2,1)S(1)}, bf16[2,6,6,2,2,4,128]{6,5,4,3,2,1,0:T(4,128)(2,1)}, u32[]{:S(2)}) copy-start(bf16[2,6,6,2,2,4,128]{6,5,4,3,2,1,0:T(4,128)(2,1)} %param.7) | copy-start | bytes 884740
  10.9 6.0 %collective-permute-start.6 = (bf16[192,128]{1,0:T(8,128)(2,1)S(1)}, bf16[192,128]{1,0:T(8,128)(2,1)S(1)}, u32[]{:S(2)}, u32[]{:S(2)}) collective-permute-start(bf16[192,128]{1,0:T(8,128)(2,1)S(1)} %get-tuple-element.53), channel_id=1, source_target_pairs={{0,4},{1,13},{2,6},{3,15},{4,0},{5,9},{6,2},{7,11},{8,12},{9,5},{1... | collective-permute-start | bytes 147464 | tf_op jit(solution)/shard_map/ppermute | solution.py:424
  11.5 5.9 %collective-permute-start.7 = (bf16[192,128]{1,0:T(8,128)(2,1)S(1)}, bf16[192,128]{1,0:T(8,128)(2,1)S(1)}, u32[]{:S(2)}, u32[]{:S(2)}) collective-permute-start(bf16[192,128]{1,0:T(8,128)(2,1)S(1)} %get-tuple-element.54), channel_id=1, source_target_pairs={{0,12},{1,5},{2,14},{3,7},{4,8},{5,1},{6,10},{7,3},{8,4},{9,13},{1... | collective-permute-start | bytes 147464 | tf_op jit(solution)/shard_map/ppermute | solution.py:424
  13.2 1.8 %copy-start = (bf16[2,6,6,2,2,4,128]{6,5,4,3,2,1,0:T(4,128)(2,1)S(1)}, bf16[2,6,6,2,2,4,128]{6,5,4,3,2,1,0:T(4,128)(2,1)}, u32[]{:S(2)}) copy-start(bf16[2,6,6,2,2,4,128]{6,5,4,3,2,1,0:T(4,128)(2,1)} %param.6) | copy-start | bytes 884740
  13.3 3.5 %collective-permute-start.4 = (bf16[96,128]{1,0:T(8,128)(2,1)S(1)}, bf16[96,128]{1,0:T(8,128)(2,1)S(1)}, u32[]{:S(2)}, u32[]{:S(2)}) collective-permute-start(bf16[96,128]{1,0:T(8,128)(2,1)S(1)} %get-tuple-element.51), channel_id=1, source_target_pairs={{0,3},{1,2},{2,1},{3,0},{4,7},{5,6},{6,5},{7,4},{8,11},{9,10},{10,... | collective-permute-start | bytes 73736 | tf_op jit(solution)/shard_map/ppermute | solution.py:413
  13.4 3.5 %collective-permute-start.5 = (bf16[96,128]{1,0:T(8,128)(2,1)S(1)}, bf16[96,128]{1,0:T(8,128)(2,1)S(1)}, u32[]{:S(2)}, u32[]{:S(2)}) collective-permute-start(bf16[96,128]{1,0:T(8,128)(2,1)S(1)} %get-tuple-element.52), channel_id=1, source_target_pairs={{0,1},{1,0},{2,3},{3,2},{4,5},{5,4},{6,7},{7,6},{8,9},{9,8},{10,11... | collective-permute-start | bytes 73736 | tf_op jit(solution)/shard_map/ppermute | solution.py:413
  17.6 6.2 %collective-permute-start.10 = (bf16[192,128]{1,0:T(8,128)(2,1)S(1)}, bf16[192,128]{1,0:T(8,128)(2,1)S(1)}, u32[]{:S(2)}, u32[]{:S(2)}) collective-permute-start(bf16[192,128]{1,0:T(8,128)(2,1)S(1)} %get-tuple-element.61), channel_id=1, source_target_pairs={{0,4},{1,13},{2,6},{3,15},{4,0},{5,9},{6,2},{7,11},{8,12},{9,5},{1... | collective-permute-start | bytes 147464 | tf_op jit(solution)/shard_map/ppermute | solution.py:424
  18.2 5.9 %collective-permute-start.11 = (bf16[192,128]{1,0:T(8,128)(2,1)S(1)}, bf16[192,128]{1,0:T(8,128)(2,1)S(1)}, u32[]{:S(2)}, u32[]{:S(2)}) collective-permute-start(bf16[192,128]{1,0:T(8,128)(2,1)S(1)} %get-tuple-element.62), channel_id=1, source_target_pairs={{0,12},{1,5},{2,14},{3,7},{4,8},{5,1},{6,10},{7,3},{8,4},{9,13},{1... | collective-permute-start | bytes 147464 | tf_op jit(solution)/shard_map/ppermute | solution.py:424
  20.1 3.5 %collective-permute-start.8 = (bf16[96,128]{1,0:T(8,128)(2,1)S(1)}, bf16[96,128]{1,0:T(8,128)(2,1)S(1)}, u32[]{:S(2)}, u32[]{:S(2)}) collective-permute-start(bf16[96,128]{1,0:T(8,128)(2,1)S(1)} %get-tuple-element.59), channel_id=1, source_target_pairs={{0,3},{1,2},{2,1},{3,0},{4,7},{5,6},{6,5},{7,4},{8,11},{9,10},{10,... | collective-permute-start | bytes 73736 | tf_op jit(solution)/shard_map/ppermute | solution.py:413
  20.2 3.5 %collective-permute-start.9 = (bf16[96,128]{1,0:T(8,128)(2,1)S(1)}, bf16[96,128]{1,0:T(8,128)(2,1)S(1)}, u32[]{:S(2)}, u32[]{:S(2)}) collective-permute-start(bf16[96,128]{1,0:T(8,128)(2,1)S(1)} %get-tuple-element.60), channel_id=1, source_target_pairs={{0,1},{1,0},{2,3},{3,2},{4,5},{5,4},{6,7},{7,6},{8,9},{9,8},{10,11... | collective-permute-start | bytes 73736 | tf_op jit(solution)/shard_map/ppermute | solution.py:413
  24.6 5.8 %collective-permute-start.14 = (bf16[192,128]{1,0:T(8,128)(2,1)S(1)}, bf16[192,128]{1,0:T(8,128)(2,1)S(1)}, u32[]{:S(2)}, u32[]{:S(2)}) collective-permute-start(bf16[192,128]{1,0:T(8,128)(2,1)S(1)} %get-tuple-element.69), channel_id=1, source_target_pairs={{0,4},{1,13},{2,6},{3,15},{4,0},{5,9},{6,2},{7,11},{8,12},{9,5},{1... | collective-permute-start | bytes 147464 | tf_op jit(solution)/shard_map/ppermute | solution.py:424
  24.7 6.1 %collective-permute-start.15 = (bf16[192,128]{1,0:T(8,128)(2,1)S(1)}, bf16[192,128]{1,0:T(8,128)(2,1)S(1)}, u32[]{:S(2)}, u32[]{:S(2)}) collective-permute-start(bf16[192,128]{1,0:T(8,128)(2,1)S(1)} %get-tuple-element.70), channel_id=1, source_target_pairs={{0,12},{1,5},{2,14},{3,7},{4,8},{5,1},{6,10},{7,3},{8,4},{9,13},{1... | collective-permute-start | bytes 147464 | tf_op jit(solution)/shard_map/ppermute | solution.py:424
  26.8 3.6 %collective-permute-start.12 = (bf16[96,128]{1,0:T(8,128)(2,1)S(1)}, bf16[96,128]{1,0:T(8,128)(2,1)S(1)}, u32[]{:S(2)}, u32[]{:S(2)}) collective-permute-start(bf16[96,128]{1,0:T(8,128)(2,1)S(1)} %get-tuple-element.67), channel_id=1, source_target_pairs={{0,3},{1,2},{2,1},{3,0},{4,7},{5,6},{6,5},{7,4},{8,11},{9,10},{10,... | collective-permute-start | bytes 73736 | tf_op jit(solution)/shard_map/ppermute | solution.py:413
  26.8 3.5 %collective-permute-start.13 = (bf16[96,128]{1,0:T(8,128)(2,1)S(1)}, bf16[96,128]{1,0:T(8,128)(2,1)S(1)}, u32[]{:S(2)}, u32[]{:S(2)}) collective-permute-start(bf16[96,128]{1,0:T(8,128)(2,1)S(1)} %get-tuple-element.68), channel_id=1, source_target_pairs={{0,1},{1,0},{2,3},{3,2},{4,5},{5,4},{6,7},{7,6},{8,9},{9,8},{10,11... | collective-permute-start | bytes 73736 | tf_op jit(solution)/shard_map/ppermute | solution.py:413

commit v11 on v6

--- a/solution.py
+++ b/solution.py
@@ -78,6 +78,14 @@
     return block[0:8], block[8:16]
 
 
+def rounded(half):
+    out = []
+    for pair in half:
+        block = jnp.concatenate(pair, axis=0).astype(BF16).astype(F32)
+        out.append((block[0:8], block[8:16]))
+    return out
+
+
 def load_links(ref, mu, parity):
     links = []
     for a in range(3):
@@ -154,7 +162,7 @@
         rears = [
             tuple(select(first, roll_rows(behind[c][i], 4), behind[c + 3][i]) for i in range(2)) for c in range(3)
         ]
-        rears = matvec(links, rears, True)
+        rears = matvec(links, rounded(rears), True)
         for c in range(3):
             front = [select(first, ahead[c + 3][i], roll_rows(ahead[c][i], 4)) for i in range(2)]
             store_pair(t_one, r * 3 + c, either(even, rears[c], front))
@@ -180,7 +188,7 @@
         for c in range(3):
             fronts.append([packed([h[j][i] for h in ahead for j in (c, c + 3)], 0, 1) for i in range(2)])
             rears.append([packed([h[j][i] for h in behind for j in (c, c + 3)], 3, -1) for i in range(2)])
-        rears = matvec(links, rears, True)
+        rears = matvec(links, rounded(rears), True)
         for c in range(3):
             store_pair(x_near, q * 3 + c, either(even, rears[c], fronts[c]))
             store_pair(x_far, q * 3 + c, either(even, fronts[c], rears[c]))
@@ -202,7 +210,7 @@
 def interior_kernel(parity, with_base, *refs):
     if with_base:
         f_ref, links_ref, base_ref, clover_ref, acc_ref = refs
-        clover_to(clover_ref, lambda r: load_field(base_ref, r), acc_ref, 1.0)
+        clover_to(clover_ref, lambda r: load_field(base_ref, r), acc_ref, -1.0 / KAPPA2)
     else:
         f_ref, links_ref, acc_ref = refs
     out_parity = 1 - parity
@@ -238,9 +246,9 @@
                 acc = [(zero, zero)] * 12
             else:
                 acc = load_field(acc_ref, r)
-            half = color(links_out, each(ahead_of, project(field, mu, -1)), False)
+            half = color(links_out, each(ahead_of, rounded(project(field, mu, -1))), False)
             acc = rebuild(acc, half, mu, -1)
-            half = color(links_in, project(field, mu, 1), True)
+            half = rounded(color(links_in, rounded(project(field, mu, 1)), True))
             acc = rebuild(acc, each(behind_of, half), mu, 1)
             store_field(acc_ref, r, acc)
 
@@ -333,7 +341,7 @@
             store_field(out_ref, r, rebuild_signed(load_field(acc_ref, r), half, 1, sign))
 
 
-def join_t(links_ref, acc_ref, t_one, t_two, parity, out_ref, done=lambda r: None):
+def join_t(links_ref, acc_ref, t_one, t_two, parity, out_ref, scale=None, done=lambda r: None):
     even = even_device("ta", "gx")
     t_idx, _ = site_masks()
     first = t_idx == 0
@@ -350,19 +358,22 @@
         half += [
             tuple(roll_rows(select(first, ahead[c][i], last[c][i]), 4) for i in range(2)) for c in range(3)
         ]
-        store_field(out_ref, r, rebuild_signed(load_field(acc_ref, r), half, 0, sign))
+        field = rebuild_signed(load_field(acc_ref, r), half, 0, sign)
+        if scale is not None:
+            field = each(lambda v: v * scale, field)
+        store_field(out_ref, r, field)
         done(r)
 
 
 def odd_kernel(links_ref, clover_ref, acc_ref, t_one, t_two, out_ref, *refs):
     outs, summed = refs[:2], refs[2]
     join_t(links_ref, acc_ref, t_one, t_two, 0, summed)
-    clover_to(clover_ref, lambda r: load_field(summed, r), out_ref, -KAPPA2)
+    clover_to(clover_ref, lambda r: load_field(summed, r), out_ref, 1.0)
     send_t(out_ref, links_ref, 1, *outs)
 
 
 def even_kernel(links_ref, acc_ref, t_one, t_two, out_ref, *outs):
-    join_t(links_ref, acc_ref, t_one, t_two, 1, out_ref)
+    join_t(links_ref, acc_ref, t_one, t_two, 1, out_ref, -KAPPA2)
     send_t(out_ref, links_ref, 0, *outs)
 
 
@@ -375,13 +386,14 @@
         copies.append(pltpu.make_async_copy(held.at[rows], out_hbm.at[rows], sems.at[r]))
         copies[-1].start()
 
-    join_t(links_ref, acc_ref, t_one, t_two, 1, held, done)
+    join_t(links_ref, acc_ref, t_one, t_two, 1, held, -KAPPA2, done)
     for copy in copies:
         copy.wait()
 
 
 ROWS = RHS * 24 * 8
-FIELD = [((ROWS, 128), F32)]
+FIELD = [((ROWS, 128), BF16)]
+SUM = [((ROWS, 128), F32)]
 T_HALOS = [((RHS * 3 * 16, 128), BF16)] * 2
 X_HALOS = [((RHS * 3 * 8, 128), BF16)] * 2
 
@@ -440,14 +452,14 @@
         base = (before, even) if parity else ()
         acc, = call(
             functools.partial(interior_kernel, parity, bool(parity)),
-            (here, links, *base), FIELD, 8_000_000 if parity else 5_000_000,
+            (here, links, *base), SUM, 8_000_000 if parity else 5_000_000,
         )
-        acc, = call(functools.partial(join_x_kernel, parity), (links, acc, x_far, x_near), FIELD, 1_000_000)
+        acc, = call(functools.partial(join_x_kernel, parity), (links, acc, x_far, x_near), SUM, 1_000_000)
         before = f
         if parity == 0:
             f, t_one, t_two = call(
                 odd_kernel, (links, odd, acc, t_one, t_two), FIELD + T_HALOS, 4_000_000,
-                [pltpu.VMEM((ROWS, 128), F32)],
+                [pltpu.VMEM((ROWS, 128), BF16)],
             )
         elif hop == 1:
             f, t_one, t_two = call(
@@ -455,7 +467,7 @@
             )
         else:
             out, = call(
-                last_kernel, (links, acc, t_one, t_two), [((ROWS, 128), BF16)], 1_000_000,
+                last_kernel, (links, acc, t_one, t_two), FIELD, 1_000_000,
                 [pltpu.VMEM((ROWS, 128), BF16), pltpu.SemaphoreType.DMA((RHS,))], out_space=pltpu.HBM,
             )
     return out.reshape(shape)

time: 31.6 us -> 31.8 us (level)
  Pallas kernels: 7.58 us -> 8.38 us
  waiting for transfers between devices: 4.79 us -> 4.25 us
    pallas_call x17, Pallas kernels: 7.58 us -> 8.38 us  [call(): pl.pallas_call(kernel, out_shape=tuple((jax.ShapeDtypeStruct(shape, dtype...]
    ppermute x8, waiting for transfers between devices: 3.6 us -> 3 us  [swap(): return lax.ppermute(value, axis, pairs)]
  transfers between devices with their start and end apart: 16 -> 16, of which waited for: 7 -> 7; matrix products, arithmetic and copies ran while one was open for 0% -> 0% of each run, Pallas kernels for 15% -> 17%
where the time goes in v11:
time: 31.8 us; the launch traced here: 31.6 us
  starting transfers between devices  18.8 us (59%)
  Pallas kernels  8.38 us (26%)
  waiting for transfers between devices  4.25 us (13%)
    ppermute x8, starting transfers between devices, swap_t(): return lax.ppermute(value, ('ta', 'gx'), pairs)  12.4 us
    pallas_call x17, Pallas kernels, call(): pl.pallas_call(kernel, out_shape=tuple((jax.ShapeDtypeStruct(shape, dtype...  8.38 us
    ppermute x8, starting transfers between devices, swap(): return lax.ppermute(value, axis, pairs)  6.38 us
    ppermute x8, waiting for transfers between devices, swap(): return lax.ppermute(value, axis, pairs)  3 us
    ppermute x8, waiting for transfers between devices, swap_t(): return lax.ppermute(value, ('ta', 'gx'), pairs)  1.26 us
  transfers between devices with their start and end apart: 16, of which 7 were waited for; matrix products, arithmetic and copies ran while one was open for 0% of the time, Pallas kernels for 17%

profile of v11, /device:TPU:0, one launch (start us, length us, event | category | flops | bytes accessed | tf_op | source)
XLA Modules:
  0.0 31.6 jit_solution(12334734584385242526)
XLA Ops:
  0.0 1.1 %shard_map.49 = (bf16[192,128]{1,0:T(8,128)(2,1)S(1)}, bf16[192,128]{1,0:T(8,128)(2,1)S(1)}) custom-call(bf16[768,128]{1,0:T(8,128)(2,1)} %bitcast.22, bf16[1152,128]{1,0:T(8,128)(2,1)} %bitcast.5), custom_call_target="tpu_custom_call" | custom-call | flops 1500000 | bytes 2097152 | tf_op jit(solution)/shard_map/pallas_call | solution.py:402
  1.1 3.1 %collective-permute-start.2 = (bf16[192,128]{1,0:T(8,128)(2,1)S(1)}, bf16[192,128]{1,0:T(8,128)(2,1)S(1)}, u32[]{:S(2)}, u32[]{:S(2)}) collective-permute-start(bf16[192,128]{1,0:T(8,128)(2,1)S(1)} %get-tuple-element.41), channel_id=1, source_target_pairs={{0,4},{1,13},{2,6},{3,15},{4,0},{5,9},{6,2},{7,11},{8,12},{9,5},{1... | collective-permute-start | bytes 147464 | tf_op jit(solution)/shard_map/ppermute | solution.py:428
  4.2 2.5 %collective-permute-start.3 = (bf16[192,128]{1,0:T(8,128)(2,1)S(1)}, bf16[192,128]{1,0:T(8,128)(2,1)S(1)}, u32[]{:S(2)}, u32[]{:S(2)}) collective-permute-start(bf16[192,128]{1,0:T(8,128)(2,1)S(1)} %get-tuple-element.42), channel_id=1, source_target_pairs={{0,12},{1,5},{2,14},{3,7},{4,8},{5,1},{6,10},{7,3},{8,4},{9,13},{1... | collective-permute-start | bytes 147464 | tf_op jit(solution)/shard_map/ppermute | solution.py:428
  6.7 0.1 shard_map.46
  6.8 0.3 collective-permute-start
  7.1 1.4 %collective-permute-start.1 = (bf16[96,128]{1,0:T(8,128)(2,1)S(1)}, bf16[96,128]{1,0:T(8,128)(2,1)S(1)}, u32[]{:S(2)}, u32[]{:S(2)}) collective-permute-start(bf16[96,128]{1,0:T(8,128)(2,1)S(1)} %get-tuple-element.40), channel_id=1, source_target_pairs={{0,1},{1,0},{2,3},{3,2},{4,5},{5,4},{6,7},{7,6},{8,9},{9,8},{10,11... | collective-permute-start | bytes 73736 | tf_op jit(solution)/shard_map/ppermute | solution.py:417
  8.5 1.0 %shard_map.47.acc_ref = f32[768,128]{1,0:T(8,128)S(1)} custom-call(bf16[768,128]{1,0:T(8,128)(2,1)S(1)} %bitcast.24, bf16[1152,128]{1,0:T(8,128)(2,1)S(1)} %bitcast.7), custom_call_target="tpu_custom_call" | custom-call | flops 5000000 | bytes 2097152 | tf_op jit(solution)/shard_map/pallas_call | solution.py:402
  9.4 0.0 copy-start.2
  9.5 0.9 %collective-permute-done.x_far = bf16[96,128]{1,0:T(8,128)(2,1)S(1)} collective-permute-done((bf16[96,128]{1,0:T(8,128)(2,1)S(1)}, bf16[96,128]{1,0:T(8,128)(2,1)S(1)}, u32[]{:S(2)}, u32[]{:S(2)}) %collective-permute-start) | collective-permute-done | bytes 24608 | tf_op jit(solution)/shard_map/ppermute | solution.py:417
  10.3 0.0 collective-permute-done.1.x_near
  10.3 0.1 shard_map.48.acc_ref
  10.4 0.0 collective-permute-done.2.t_one
  10.4 0.0 collective-permute-done.3.t_two
  10.5 0.5 %shard_map.50 = (bf16[768,128]{1,0:T(8,128)(2,1)S(1)}, bf16[192,128]{1,0:T(8,128)(2,1)S(1)}, bf16[192,128]{1,0:T(8,128)(2,1)S(1)}) custom-call(bf16[1152,128]{1,0:T(8,128)(2,1)S(1)} %bitcast.9, bf16[1152,128]{1,0:T(8,128)(2,1)S(1)} %bitcast.26, f32[768,128]{1,0:T(8,128)S(1)} %shard_map.48.acc_ref, bf16[192,128]{1,0:T(8,128)(2,1)S(1)} %collective-permute-done.2.t_one, ...), custom_call_target="tpu_custom_call" | custom-call | flops 4000000 | bytes 2097152 | tf_op jit(solution)/shard_map/pallas_call | solution.py:402
  11.0 0.0 copy-start.3
  11.0 0.7 %collective-permute-start.6 = (bf16[192,128]{1,0:T(8,128)(2,1)S(1)}, bf16[192,128]{1,0:T(8,128)(2,1)S(1)}, u32[]{:S(2)}, u32[]{:S(2)}) collective-permute-start(bf16[192,128]{1,0:T(8,128)(2,1)S(1)} %get-tuple-element.49), channel_id=1, source_target_pairs={{0,4},{1,13},{2,6},{3,15},{4,0},{5,9},{6,2},{7,11},{8,12},{9,5},{1... | collective-permute-start | bytes 147464 | tf_op jit(solution)/shard_map/ppermute | solution.py:428
  11.7 1.6 %collective-permute-start.7 = (bf16[192,128]{1,0:T(8,128)(2,1)S(1)}, bf16[192,128]{1,0:T(8,128)(2,1)S(1)}, u32[]{:S(2)}, u32[]{:S(2)}) collective-permute-start(bf16[192,128]{1,0:T(8,128)(2,1)S(1)} %get-tuple-element.50), channel_id=1, source_target_pairs={{0,12},{1,5},{2,14},{3,7},{4,8},{5,1},{6,10},{7,3},{8,4},{9,13},{1... | collective-permute-start | bytes 147464 | tf_op jit(solution)/shard_map/ppermute | solution.py:428
  13.3 0.1 shard_map.51
  13.4 0.1 collective-permute-start.4
  13.4 1.6 %collective-permute-start.5 = (bf16[96,128]{1,0:T(8,128)(2,1)S(1)}, bf16[96,128]{1,0:T(8,128)(2,1)S(1)}, u32[]{:S(2)}, u32[]{:S(2)}) collective-permute-start(bf16[96,128]{1,0:T(8,128)(2,1)S(1)} %get-tuple-element.48), channel_id=1, source_target_pairs={{0,1},{1,0},{2,3},{3,2},{4,5},{5,4},{6,7},{7,6},{8,9},{9,8},{10,11... | collective-permute-start | bytes 73736 | tf_op jit(solution)/shard_map/ppermute | solution.py:417
  15.0 1.3 %shard_map.52.acc_ref = f32[768,128]{1,0:T(8,128)S(1)} custom-call(bf16[768,128]{1,0:T(8,128)(2,1)S(1)} %get-tuple-element.46.f_ref.refs_0_, bf16[1152,128]{1,0:T(8,128)(2,1)S(1)} %bitcast.11, bf16[768,128]{1,0:T(8,128)(2,1)S(1)} %bitcast.25, bf16[1152,128]{1,0:T(8,128)(2,1)S(1)} %bitcast.28), custom_call_target="tpu_custom_call" | custom-call | flops 8000000 | bytes 2097152 | tf_op jit(solution)/shard_map/pallas_call | solution.py:402
  16.3 0.6 %collective-permute-done.4.x_far = bf16[96,128]{1,0:T(8,128)(2,1)S(1)} collective-permute-done((bf16[96,128]{1,0:T(8,128)(2,1)S(1)}, bf16[96,128]{1,0:T(8,128)(2,1)S(1)}, u32[]{:S(2)}, u32[]{:S(2)}) %collective-permute-start.4) | collective-permute-done | bytes 24608 | tf_op jit(solution)/shard_map/ppermute | solution.py:417
  16.9 0.1 shard_map.53.acc_ref
  17.0 0.0 collective-permute-done.6.t_one
  17.0 0.6 %collective-permute-done.7.t_two = bf16[192,128]{1,0:T(8,128)(2,1)S(1)} collective-permute-done((bf16[192,128]{1,0:T(8,128)(2,1)S(1)}, bf16[192,128]{1,0:T(8,128)(2,1)S(1)}, u32[]{:S(2)}, u32[]{:S(2)}) %collective-permute-start.7) | collective-permute-done | bytes 49184 | tf_op jit(solution)/shard_map/ppermute | solution.py:428
  17.6 0.2 shard_map.54
  17.8 0.6 %collective-permute-start.10 = (bf16[192,128]{1,0:T(8,128)(2,1)S(1)}, bf16[192,128]{1,0:T(8,128)(2,1)S(1)}, u32[]{:S(2)}, u32[]{:S(2)}) collective-permute-start(bf16[192,128]{1,0:T(8,128)(2,1)S(1)} %get-tuple-element.57), channel_id=1, source_target_pairs={{0,4},{1,13},{2,6},{3,15},{4,0},{5,9},{6,2},{7,11},{8,12},{9,5},{1... | collective-permute-start | bytes 147464 | tf_op jit(solution)/shard_map/ppermute | solution.py:428
  18.3 1.8 %collective-permute-start.11 = (bf16[192,128]{1,0:T(8,128)(2,1)S(1)}, bf16[192,128]{1,0:T(8,128)(2,1)S(1)}, u32[]{:S(2)}, u32[]{:S(2)}) collective-permute-start(bf16[192,128]{1,0:T(8,128)(2,1)S(1)} %get-tuple-element.58), channel_id=1, source_target_pairs={{0,12},{1,5},{2,14},{3,7},{4,8},{5,1},{6,10},{7,3},{8,4},{9,13},{1... | collective-permute-start | bytes 147464 | tf_op jit(solution)/shard_map/ppermute | solution.py:428
  20.1 0.1 shard_map.55
  20.2 0.1 collective-permute-start.8
  20.3 1.6 %collective-permute-start.9 = (bf16[96,128]{1,0:T(8,128)(2,1)S(1)}, bf16[96,128]{1,0:T(8,128)(2,1)S(1)}, u32[]{:S(2)}, u32[]{:S(2)}) collective-permute-start(bf16[96,128]{1,0:T(8,128)(2,1)S(1)} %get-tuple-element.56), channel_id=1, source_target_pairs={{0,1},{1,0},{2,3},{3,2},{4,5},{5,4},{6,7},{7,6},{8,9},{9,8},{10,11... | collective-permute-start | bytes 73736 | tf_op jit(solution)/shard_map/ppermute | solution.py:417
  21.9 1.0 %shard_map.56.acc_ref = f32[768,128]{1,0:T(8,128)S(1)} custom-call(bf16[768,128]{1,0:T(8,128)(2,1)S(1)} %get-tuple-element.54.f_ref.refs_0_.refs_2_, bf16[1152,128]{1,0:T(8,128)(2,1)S(1)} %bitcast.15), custom_call_target="tpu_custom_call" | custom-call | flops 5000000 | bytes 2097152 | tf_op jit(solution)/shard_map/pallas_call | solution.py:402
  22.8 0.9 %collective-permute-done.8.x_far = bf16[96,128]{1,0:T(8,128)(2,1)S(1)} collective-permute-done((bf16[96,128]{1,0:T(8,128)(2,1)S(1)}, bf16[96,128]{1,0:T(8,128)(2,1)S(1)}, u32[]{:S(2)}, u32[]{:S(2)}) %collective-permute-start.8) | collective-permute-done | bytes 24608 | tf_op jit(solution)/shard_map/ppermute | solution.py:417
  23.7 0.0 collective-permute-done.9.x_near
  23.7 0.1 shard_map.57.acc_ref
  23.8 0.0 collective-permute-done.10.t_one
  23.8 0.4 %collective-permute-done.11.t_two = bf16[192,128]{1,0:T(8,128)(2,1)S(1)} collective-permute-done((bf16[192,128]{1,0:T(8,128)(2,1)S(1)}, bf16[192,128]{1,0:T(8,128)(2,1)S(1)}, u32[]{:S(2)}, u32[]{:S(2)}) %collective-permute-start.11) | collective-permute-done | bytes 49184 | tf_op jit(solution)/shard_map/ppermute | solution.py:428
  24.2 0.5 %shard_map.58 = (bf16[768,128]{1,0:T(8,128)(2,1)S(1)}, bf16[192,128]{1,0:T(8,128)(2,1)S(1)}, bf16[192,128]{1,0:T(8,128)(2,1)S(1)}) custom-call(bf16[1152,128]{1,0:T(8,128)(2,1)S(1)} %bitcast.17, bf16[1152,128]{1,0:T(8,128)(2,1)S(1)} %bitcast.27, f32[768,128]{1,0:T(8,128)S(1)} %shard_map.57.acc_ref, bf16[192,128]{1,0:T(8,128)(2,1)S(1)} %collective-permute-done.10.t_one, ...), custom_call_target="tpu_custom_call" | custom-call | flops 4000000 | bytes 2097152 | tf_op jit(solution)/shard_map/pallas_call | solution.py:402
  24.7 0.1 collective-permute-start.14
  24.8 2.2 %collective-permute-start.15 = (bf16[192,128]{1,0:T(8,128)(2,1)S(1)}, bf16[192,128]{1,0:T(8,128)(2,1)S(1)}, u32[]{:S(2)}, u32[]{:S(2)}) collective-permute-start(bf16[192,128]{1,0:T(8,128)(2,1)S(1)} %get-tuple-element.66), channel_id=1, source_target_pairs={{0,12},{1,5},{2,14},{3,7},{4,8},{5,1},{6,10},{7,3},{8,4},{9,13},{1... | collective-permute-start | bytes 147464 | tf_op jit(solution)/shard_map/ppermute | solution.py:428
  27.0 0.1 shard_map.59
  27.1 0.1 collective-permute-start.12
  27.2 1.3 %collective-permute-start.13 = (bf16[96,128]{1,0:T(8,128)(2,1)S(1)}, bf16[96,128]{1,0:T(8,128)(2,1)S(1)}, u32[]{:S(2)}, u32[]{:S(2)}) collective-permute-start(bf16[96,128]{1,0:T(8,128)(2,1)S(1)} %get-tuple-element.64), channel_id=1, source_target_pairs={{0,1},{1,0},{2,3},{3,2},{4,5},{5,4},{6,7},{7,6},{8,9},{9,8},{10,11... | collective-permute-start | bytes 73736 | tf_op jit(solution)/shard_map/ppermute | solution.py:417
  28.5 1.3 %shard_map.60.acc_ref = f32[768,128]{1,0:T(8,128)S(1)} custom-call(bf16[768,128]{1,0:T(8,128)(2,1)S(1)} %get-tuple-element.62.f_ref.refs_0_, bf16[1152,128]{1,0:T(8,128)(2,1)S(1)} %bitcast.19, bf16[768,128]{1,0:T(8,128)(2,1)S(1)} %get-tuple-element.54.f_ref.refs_0_.refs_2_, bf16[1152,128]{1,0:T(8,128)(2,1)S(1)} %bitcast.29), custom_call_target="tpu_custom_call" | custom-call | flops 8000000 | bytes 2097152 | tf_op jit(solution)/shard_map/pallas_call | solution.py:402
  29.8 0.7 %collective-permute-done.12.x_far = bf16[96,128]{1,0:T(8,128)(2,1)S(1)} collective-permute-done((bf16[96,128]{1,0:T(8,128)(2,1)S(1)}, bf16[96,128]{1,0:T(8,128)(2,1)S(1)}, u32[]{:S(2)}, u32[]{:S(2)}) %collective-permute-start.12) | collective-permute-done | bytes 24608 | tf_op jit(solution)/shard_map/ppermute | solution.py:417
  30.5 0.1 shard_map.61.acc_ref
  30.6 0.3 collective-permute-done.15.t_two
  30.9 0.8 %shard_map.62 = bf16[768,128]{1,0:T(8,128)(2,1)} custom-call(bf16[1152,128]{1,0:T(8,128)(2,1)S(1)} %bitcast.21, f32[768,128]{1,0:T(8,128)S(1)} %shard_map.61.acc_ref, bf16[192,128]{1,0:T(8,128)(2,1)S(1)} %collective-permute-done.14.t_one, bf16[192,128]{1,0:T(8,128)(2,1)S(1)} %collective-permute-done.15.t_two), custom_call_target="tpu_custom_call" | custom-call | flops 1000000 | bytes 2097152 | tf_op jit(solution)/shard_map/pallas_call | solution.py:402
  (9 shorter events, 0.0 us)
Async XLA Ops:
  0.0 6.7 %copy-start = (bf16[4,3,3,2,2,2,4,128]{7,6,5,4,3,2,1,0:T(4,128)(2,1)S(1)}, bf16[4,3,3,2,2,2,4,128]{7,6,5,4,3,2,1,0:T(4,128)(2,1)}, u32[]{:S(2)}) copy-start(bf16[4,3,3,2,2,2,4,128]{7,6,5,4,3,2,1,0:T(4,128)(2,1)} %param.5) | copy-start | bytes 884740
  0.0 6.7 %copy-start.1 = (bf16[4,4,3,2,2,4,128]{6,5,4,3,2,1,0:T(4,128)(2,1)S(1)}, bf16[4,4,3,2,2,4,128]{6,5,4,3,2,1,0:T(4,128)(2,1)}, u32[]{:S(2)}) copy-start(bf16[4,4,3,2,2,4,128]{6,5,4,3,2,1,0:T(4,128)(2,1)} %param.4) | copy-start | bytes 589828
  1.1 9.3 %collective-permute-start.2 = (bf16[192,128]{1,0:T(8,128)(2,1)S(1)}, bf16[192,128]{1,0:T(8,128)(2,1)S(1)}, u32[]{:S(2)}, u32[]{:S(2)}) collective-permute-start(bf16[192,128]{1,0:T(8,128)(2,1)S(1)} %get-tuple-element.41), channel_id=1, source_target_pairs={{0,4},{1,13},{2,6},{3,15},{4,0},{5,9},{6,2},{7,11},{8,12},{9,5},{1... | collective-permute-start | bytes 147464 | tf_op jit(solution)/shard_map/ppermute | solution.py:428
  4.2 6.2 %collective-permute-start.3 = (bf16[192,128]{1,0:T(8,128)(2,1)S(1)}, bf16[192,128]{1,0:T(8,128)(2,1)S(1)}, u32[]{:S(2)}, u32[]{:S(2)}) collective-permute-start(bf16[192,128]{1,0:T(8,128)(2,1)S(1)} %get-tuple-element.42), channel_id=1, source_target_pairs={{0,12},{1,5},{2,14},{3,7},{4,8},{5,1},{6,10},{7,3},{8,4},{9,13},{1... | collective-permute-start | bytes 147464 | tf_op jit(solution)/shard_map/ppermute | solution.py:428
  6.8 3.5 %collective-permute-start = (bf16[96,128]{1,0:T(8,128)(2,1)S(1)}, bf16[96,128]{1,0:T(8,128)(2,1)S(1)}, u32[]{:S(2)}, u32[]{:S(2)}) collective-permute-start(bf16[96,128]{1,0:T(8,128)(2,1)S(1)} %get-tuple-element.39), channel_id=1, source_target_pairs={{0,3},{1,2},{2,1},{3,0},{4,7},{5,6},{6,5},{7,4},{8,11},{9,10},{10,... | collective-permute-start | bytes 73736 | tf_op jit(solution)/shard_map/ppermute | solution.py:417
  7.1 3.3 %collective-permute-start.1 = (bf16[96,128]{1,0:T(8,128)(2,1)S(1)}, bf16[96,128]{1,0:T(8,128)(2,1)S(1)}, u32[]{:S(2)}, u32[]{:S(2)}) collective-permute-start(bf16[96,128]{1,0:T(8,128)(2,1)S(1)} %get-tuple-element.40), channel_id=1, source_target_pairs={{0,1},{1,0},{2,3},{3,2},{4,5},{5,4},{6,7},{7,6},{8,9},{9,8},{10,11... | collective-permute-start | bytes 73736 | tf_op jit(solution)/shard_map/ppermute | solution.py:417
  9.4 1.0 %copy-start.2 = (bf16[2,6,6,2,2,4,128]{6,5,4,3,2,1,0:T(4,128)(2,1)S(1)}, bf16[2,6,6,2,2,4,128]{6,5,4,3,2,1,0:T(4,128)(2,1)}, u32[]{:S(2)}) copy-start(bf16[2,6,6,2,2,4,128]{6,5,4,3,2,1,0:T(4,128)(2,1)} %param.7) | copy-start | bytes 884740
  11.0 4.1 %copy-start.3 = (bf16[2,6,6,2,2,4,128]{6,5,4,3,2,1,0:T(4,128)(2,1)S(1)}, bf16[2,6,6,2,2,4,128]{6,5,4,3,2,1,0:T(4,128)(2,1)}, u32[]{:S(2)}) copy-start(bf16[2,6,6,2,2,4,128]{6,5,4,3,2,1,0:T(4,128)(2,1)} %param.6) | copy-start | bytes 884740
  11.0 6.0 %collective-permute-start.6 = (bf16[192,128]{1,0:T(8,128)(2,1)S(1)}, bf16[192,128]{1,0:T(8,128)(2,1)S(1)}, u32[]{:S(2)}, u32[]{:S(2)}) collective-permute-start(bf16[192,128]{1,0:T(8,128)(2,1)S(1)} %get-tuple-element.49), channel_id=1, source_target_pairs={{0,4},{1,13},{2,6},{3,15},{4,0},{5,9},{6,2},{7,11},{8,12},{9,5},{1... | collective-permute-start | bytes 147464 | tf_op jit(solution)/shard_map/ppermute | solution.py:428
  11.7 5.9 %collective-permute-start.7 = (bf16[192,128]{1,0:T(8,128)(2,1)S(1)}, bf16[192,128]{1,0:T(8,128)(2,1)S(1)}, u32[]{:S(2)}, u32[]{:S(2)}) collective-permute-start(bf16[192,128]{1,0:T(8,128)(2,1)S(1)} %get-tuple-element.50), channel_id=1, source_target_pairs={{0,12},{1,5},{2,14},{3,7},{4,8},{5,1},{6,10},{7,3},{8,4},{9,13},{1... | collective-permute-start | bytes 147464 | tf_op jit(solution)/shard_map/ppermute | solution.py:428
  13.4 3.5 %collective-permute-start.4 = (bf16[96,128]{1,0:T(8,128)(2,1)S(1)}, bf16[96,128]{1,0:T(8,128)(2,1)S(1)}, u32[]{:S(2)}, u32[]{:S(2)}) collective-permute-start(bf16[96,128]{1,0:T(8,128)(2,1)S(1)} %get-tuple-element.47), channel_id=1, source_target_pairs={{0,3},{1,2},{2,1},{3,0},{4,7},{5,6},{6,5},{7,4},{8,11},{9,10},{10,... | collective-permute-start | bytes 73736 | tf_op jit(solution)/shard_map/ppermute | solution.py:417
  13.4 3.5 %collective-permute-start.5 = (bf16[96,128]{1,0:T(8,128)(2,1)S(1)}, bf16[96,128]{1,0:T(8,128)(2,1)S(1)}, u32[]{:S(2)}, u32[]{:S(2)}) collective-permute-start(bf16[96,128]{1,0:T(8,128)(2,1)S(1)} %get-tuple-element.48), channel_id=1, source_target_pairs={{0,1},{1,0},{2,3},{3,2},{4,5},{5,4},{6,7},{7,6},{8,9},{9,8},{10,11... | collective-permute-start | bytes 73736 | tf_op jit(solution)/shard_map/ppermute | solution.py:417
  17.8 6.1 %collective-permute-start.10 = (bf16[192,128]{1,0:T(8,128)(2,1)S(1)}, bf16[192,128]{1,0:T(8,128)(2,1)S(1)}, u32[]{:S(2)}, u32[]{:S(2)}) collective-permute-start(bf16[192,128]{1,0:T(8,128)(2,1)S(1)} %get-tuple-element.57), channel_id=1, source_target_pairs={{0,4},{1,13},{2,6},{3,15},{4,0},{5,9},{6,2},{7,11},{8,12},{9,5},{1... | collective-permute-start | bytes 147464 | tf_op jit(solution)/shard_map/ppermute | solution.py:428
  18.3 5.9 %collective-permute-start.11 = (bf16[192,128]{1,0:T(8,128)(2,1)S(1)}, bf16[192,128]{1,0:T(8,128)(2,1)S(1)}, u32[]{:S(2)}, u32[]{:S(2)}) collective-permute-start(bf16[192,128]{1,0:T(8,128)(2,1)S(1)} %get-tuple-element.58), channel_id=1, source_target_pairs={{0,12},{1,5},{2,14},{3,7},{4,8},{5,1},{6,10},{7,3},{8,4},{9,13},{1... | collective-permute-start | bytes 147464 | tf_op jit(solution)/shard_map/ppermute | solution.py:428
  20.2 3.5 %collective-permute-start.8 = (bf16[96,128]{1,0:T(8,128)(2,1)S(1)}, bf16[96,128]{1,0:T(8,128)(2,1)S(1)}, u32[]{:S(2)}, u32[]{:S(2)}) collective-permute-start(bf16[96,128]{1,0:T(8,128)(2,1)S(1)} %get-tuple-element.55), channel_id=1, source_target_pairs={{0,3},{1,2},{2,1},{3,0},{4,7},{5,6},{6,5},{7,4},{8,11},{9,10},{10,... | collective-permute-start | bytes 73736 | tf_op jit(solution)/shard_map/ppermute | solution.py:417
  20.3 3.5 %collective-permute-start.9 = (bf16[96,128]{1,0:T(8,128)(2,1)S(1)}, bf16[96,128]{1,0:T(8,128)(2,1)S(1)}, u32[]{:S(2)}, u32[]{:S(2)}) collective-permute-start(bf16[96,128]{1,0:T(8,128)(2,1)S(1)} %get-tuple-element.56), channel_id=1, source_target_pairs={{0,1},{1,0},{2,3},{3,2},{4,5},{5,4},{6,7},{7,6},{8,9},{9,8},{10,11... | collective-permute-start | bytes 73736 | tf_op jit(solution)/shard_map/ppermute | solution.py:417
  24.7 5.8 %collective-permute-start.14 = (bf16[192,128]{1,0:T(8,128)(2,1)S(1)}, bf16[192,128]{1,0:T(8,128)(2,1)S(1)}, u32[]{:S(2)}, u32[]{:S(2)}) collective-permute-start(bf16[192,128]{1,0:T(8,128)(2,1)S(1)} %get-tuple-element.65), channel_id=1, source_target_pairs={{0,4},{1,13},{2,6},{3,15},{4,0},{5,9},{6,2},{7,11},{8,12},{9,5},{1... | collective-permute-start | bytes 147464 | tf_op jit(solution)/shard_map/ppermute | solution.py:428
  24.8 6.1 %collective-permute-start.15 = (bf16[192,128]{1,0:T(8,128)(2,1)S(1)}, bf16[192,128]{1,0:T(8,128)(2,1)S(1)}, u32[]{:S(2)}, u32[]{:S(2)}) collective-permute-start(bf16[192,128]{1,0:T(8,128)(2,1)S(1)} %get-tuple-element.66), channel_id=1, source_target_pairs={{0,12},{1,5},{2,14},{3,7},{4,8},{5,1},{6,10},{7,3},{8,4},{9,13},{1... | collective-permute-start | bytes 147464 | tf_op jit(solution)/shard_map/ppermute | solution.py:428
  27.1 3.3 %collective-permute-start.12 = (bf16[96,128]{1,0:T(8,128)(2,1)S(1)}, bf16[96,128]{1,0:T(8,128)(2,1)S(1)}, u32[]{:S(2)}, u32[]{:S(2)}) collective-permute-start(bf16[96,128]{1,0:T(8,128)(2,1)S(1)} %get-tuple-element.63), channel_id=1, source_target_pairs={{0,3},{1,2},{2,1},{3,0},{4,7},{5,6},{6,5},{7,4},{8,11},{9,10},{10,... | collective-permute-start | bytes 73736 | tf_op jit(solution)/shard_map/ppermute | solution.py:417
  27.2 3.3 %collective-permute-start.13 = (bf16[96,128]{1,0:T(8,128)(2,1)S(1)}, bf16[96,128]{1,0:T(8,128)(2,1)S(1)}, u32[]{:S(2)}, u32[]{:S(2)}) collective-permute-start(bf16[96,128]{1,0:T(8,128)(2,1)S(1)} %get-tuple-element.64), channel_id=1, source_target_pairs={{0,1},{1,0},{2,3},{3,2},{4,5},{5,4},{6,7},{7,6},{8,9},{9,8},{10,11... | collective-permute-start | bytes 73736 | tf_op jit(solution)/shard_map/ppermute | solution.py:417

commit v12 on v11

--- a/solution.py
+++ b/solution.py
@@ -169,7 +169,7 @@
             store_pair(t_two, r * 3 + c, either(even, front, rears[c]))
 
 
-def send_x_kernel(parity, f_ref, links_ref, x_far, x_near):
+def send_x(f_ref, links_ref, parity, x_far, x_near):
     even = even_device("gx")
     _, x_idx = site_masks()
     links = x_edges(load_links(links_ref, 1, parity))
@@ -195,7 +195,7 @@
 
 
 def start_kernel(f_hbm, links_hbm, *refs):
-    outs, (f_ref, links_ref, sems) = refs[:2], refs[2:]
+    outs, (f_ref, links_ref, sems) = refs[:4], refs[4:]
     part = f_ref.shape[0] // RHS
     copies = [pltpu.make_async_copy(links_hbm.at[pl.ds(0, links_ref.shape[0])], links_ref, sems.at[RHS])]
     for r in range(RHS):
@@ -204,7 +204,8 @@
     for copy in copies:
         copy.start()
     copies[0].wait()
-    send_t(f_ref, links_ref, 0, *outs, ready=lambda r: copies[1 + r].wait())
+    send_t(f_ref, links_ref, 0, *outs[:2], ready=lambda r: copies[1 + r].wait())
+    send_x(f_ref, links_ref, 0, *outs[2:])
 
 
 def interior_kernel(parity, with_base, *refs):
@@ -366,15 +367,17 @@
 
 
 def odd_kernel(links_ref, clover_ref, acc_ref, t_one, t_two, out_ref, *refs):
-    outs, summed = refs[:2], refs[2]
+    outs, summed = refs[:4], refs[4]
     join_t(links_ref, acc_ref, t_one, t_two, 0, summed)
     clover_to(clover_ref, lambda r: load_field(summed, r), out_ref, 1.0)
-    send_t(out_ref, links_ref, 1, *outs)
+    send_t(out_ref, links_ref, 1, *outs[:2])
+    send_x(out_ref, links_ref, 1, *outs[2:])
 
 
 def even_kernel(links_ref, acc_ref, t_one, t_two, out_ref, *outs):
     join_t(links_ref, acc_ref, t_one, t_two, 1, out_ref, -KAPPA2)
-    send_t(out_ref, links_ref, 0, *outs)
+    send_t(out_ref, links_ref, 0, *outs[:2])
+    send_x(out_ref, links_ref, 0, *outs[2:])
 
 
 def last_kernel(links_ref, acc_ref, t_one, t_two, out_hbm, held, sems):
@@ -395,7 +398,7 @@
 FIELD = [((ROWS, 128), BF16)]
 SUM = [((ROWS, 128), F32)]
 T_HALOS = [((RHS * 3 * 16, 128), BF16)] * 2
-X_HALOS = [((RHS * 3 * 8, 128), BF16)] * 2
+HALOS = T_HALOS + [((RHS * 3 * 8, 128), BF16)] * 2
 
 
 def call(kernel, args, outs, flops, scratch=(), in_space=pltpu.VMEM, out_space=pltpu.VMEM):
@@ -437,33 +440,29 @@
     held = [pltpu.with_memory_space_constraint(v, pltpu.HBM) for v in (f, links)]
     start_scratch = [
         pltpu.VMEM((ROWS, 128), BF16),
-        pltpu.VMEM((links.shape[0] // 4, 128), BF16),
+        pltpu.VMEM((links.shape[0] // 2, 128), BF16),
         pltpu.SemaphoreType.DMA((RHS + 1,)),
     ]
-    t_one, t_two = call(start_kernel, held, T_HALOS, 1_500_000, start_scratch, in_space=pltpu.HBM)
+    t_one, t_two, x_far, x_near = call(start_kernel, held, HALOS, 1_500_000, start_scratch, in_space=pltpu.HBM)
     for hop in range(4):
         parity = hop % 2
         t_one, t_two = swap_t(t_one, True), swap_t(t_two, False)
-        x_far, x_near = call(
-            functools.partial(send_x_kernel, parity), (f, links), X_HALOS, 1_500_000
-        )
-        here, x_far, x_near = lax.optimization_barrier((f, x_far, x_near))
         x_far, x_near = swap(x_far, "gx", True), swap(x_near, "gx", False)
         base = (before, even) if parity else ()
         acc, = call(
             functools.partial(interior_kernel, parity, bool(parity)),
-            (here, links, *base), SUM, 8_000_000 if parity else 5_000_000,
+            (f, links, *base), SUM, 8_000_000 if parity else 5_000_000,
         )
         acc, = call(functools.partial(join_x_kernel, parity), (links, acc, x_far, x_near), SUM, 1_000_000)
         before = f
         if parity == 0:
-            f, t_one, t_two = call(
-                odd_kernel, (links, odd, acc, t_one, t_two), FIELD + T_HALOS, 4_000_000,
+            f, t_one, t_two, x_far, x_near = call(
+                odd_kernel, (links, odd, acc, t_one, t_two), FIELD + HALOS, 4_000_000,
                 [pltpu.VMEM((ROWS, 128), BF16)],
             )
         elif hop == 1:
-            f, t_one, t_two = call(
-                even_kernel, (links, acc, t_one, t_two), FIELD + T_HALOS, 2_000_000
+            f, t_one, t_two, x_far, x_near = call(
+                even_kernel, (links, acc, t_one, t_two), FIELD + HALOS, 2_000_000
             )
         else:
             out, = call(

time: 31.8 us -> 32 us (level)
    pallas_call x17 -> x13, Pallas kernels: 8.38 us -> 8.38 us  [call(): pl.pallas_call(kernel, out_shape=tuple((jax.ShapeDtypeStruct(shape, dtype...]
  transfers between devices with their start and end apart: 16 -> 16, of which waited for: 7 -> 7; matrix products, arithmetic and copies ran while one was open for 0% -> 0% of each run, Pallas kernels for 17% -> 15%
where the time goes in v12:
time: 32 us; the launch traced here: 31.9 us
  starting transfers between devices  19 us (59%)
  Pallas kernels  8.38 us (26%)
  waiting for transfers between devices  4.39 us (14%)
    ppermute x8, starting transfers between devices, swap_t(): return lax.ppermute(value, ('ta', 'gx'), pairs)  12.6 us
    pallas_call x13, Pallas kernels, call(): pl.pallas_call(kernel, out_shape=tuple((jax.ShapeDtypeStruct(shape, dtype...  8.38 us
    ppermute x8, starting transfers between devices, swap(): return lax.ppermute(value, axis, pairs)  6.36 us
    ppermute x8, waiting for transfers between devices, swap(): return lax.ppermute(value, axis, pairs)  3.01 us
    ppermute x8, waiting for transfers between devices, swap_t(): return lax.ppermute(value, ('ta', 'gx'), pairs)  1.38 us
  transfers between devices with their start and end apart: 16, of which 7 were waited for; matrix products, arithmetic and copies ran while one was open for 0% of the time, Pallas kernels for 15%

profile of v12, /device:TPU:0, one launch (start us, length us, event | category | flops | bytes accessed | tf_op | source)
XLA Modules:
  0.0 31.9 jit_solution(9889669366703916034)
XLA Ops:
  0.0 1.2 %shard_map.47 = (bf16[192,128]{1,0:T(8,128)(2,1)S(1)}, bf16[192,128]{1,0:T(8,128)(2,1)S(1)}, bf16[96,128]{1,0:T(8,128)(2,1)S(1)}, bf16[96,128]{1,0:T(8,128)(2,1)S(1)}) custom-call(bf16[768,128]{1,0:T(8,128)(2,1)} %bitcast.18, bf16[1152,128]{1,0:T(8,128)(2,1)} %bitcast.5), custom_call_target="tpu_custom_call" | custom-call | flops 1500000 | bytes 2097152 | tf_op jit(solution)/shard_map/pallas_call | solution.py:405
  1.2 3.1 %collective-permute-start.2 = (bf16[192,128]{1,0:T(8,128)(2,1)S(1)}, bf16[192,128]{1,0:T(8,128)(2,1)S(1)}, u32[]{:S(2)}, u32[]{:S(2)}) collective-permute-start(bf16[192,128]{1,0:T(8,128)(2,1)S(1)} %get-tuple-element.26), channel_id=1, source_target_pairs={{0,4},{1,13},{2,6},{3,15},{4,0},{5,9},{6,2},{7,11},{8,12},{9,5},{1... | collective-permute-start | bytes 147464 | tf_op jit(solution)/shard_map/ppermute | solution.py:431
  4.3 2.5 %collective-permute-start.3 = (bf16[192,128]{1,0:T(8,128)(2,1)S(1)}, bf16[192,128]{1,0:T(8,128)(2,1)S(1)}, u32[]{:S(2)}, u32[]{:S(2)}) collective-permute-start(bf16[192,128]{1,0:T(8,128)(2,1)S(1)} %get-tuple-element.27), channel_id=1, source_target_pairs={{0,12},{1,5},{2,14},{3,7},{4,8},{5,1},{6,10},{7,3},{8,4},{9,13},{1... | collective-permute-start | bytes 147464 | tf_op jit(solution)/shard_map/ppermute | solution.py:431
  6.8 0.2 collective-permute-start
  7.0 1.4 %collective-permute-start.1 = (bf16[96,128]{1,0:T(8,128)(2,1)S(1)}, bf16[96,128]{1,0:T(8,128)(2,1)S(1)}, u32[]{:S(2)}, u32[]{:S(2)}) collective-permute-start(bf16[96,128]{1,0:T(8,128)(2,1)S(1)} %get-tuple-element.25), channel_id=1, source_target_pairs={{0,1},{1,0},{2,3},{3,2},{4,5},{5,4},{6,7},{7,6},{8,9},{9,8},{10,11... | collective-permute-start | bytes 73736 | tf_op jit(solution)/shard_map/ppermute | solution.py:420
  8.4 1.0 %shard_map.46.acc_ref = f32[768,128]{1,0:T(8,128)S(1)} custom-call(bf16[768,128]{1,0:T(8,128)(2,1)S(1)} %bitcast.19, bf16[1152,128]{1,0:T(8,128)(2,1)S(1)} %bitcast.6), custom_call_target="tpu_custom_call" | custom-call | flops 5000000 | bytes 2097152 | tf_op jit(solution)/shard_map/pallas_call | solution.py:405
  9.4 0.0 copy-start.2
  9.4 0.9 %collective-permute-done.x_far = bf16[96,128]{1,0:T(8,128)(2,1)S(1)} collective-permute-done((bf16[96,128]{1,0:T(8,128)(2,1)S(1)}, bf16[96,128]{1,0:T(8,128)(2,1)S(1)}, u32[]{:S(2)}, u32[]{:S(2)}) %collective-permute-start) | collective-permute-done | bytes 24608 | tf_op jit(solution)/shard_map/ppermute | solution.py:420
  10.3 0.0 collective-permute-done.1.x_near
  10.3 0.1 shard_map.48.acc_ref
  10.4 0.0 collective-permute-done.2.t_one
  10.4 0.0 collective-permute-done.3.t_two
  10.4 0.0 copy-start.3
  10.4 0.6 %shard_map.49 = (bf16[768,128]{1,0:T(8,128)(2,1)S(1)}, bf16[192,128]{1,0:T(8,128)(2,1)S(1)}, bf16[192,128]{1,0:T(8,128)(2,1)S(1)}, bf16[96,128]{1,0:T(8,128)(2,1)S(1)}, bf16[96,128]{1,0:T(8,128)(2,1)S(1)}) custom-call(bf16[1152,128]{1,0:T(8,128)(2,1)S(1)} %bitcast.8, bf16[1152,128]{1,0:T(8,128)(2,1)S(1)} %bitcast.21, f32[768,128]{1,0:T(8,128)S(1)} %shard_map.48.acc_ref, ...), custom_call_target="tpu_custom_call" | custom-call | flops 4000000 | bytes 2097152 | tf_op jit(solution)/shard_map/pallas_call | solution.py:405
  11.0 0.7 %collective-permute-start.6 = (bf16[192,128]{1,0:T(8,128)(2,1)S(1)}, bf16[192,128]{1,0:T(8,128)(2,1)S(1)}, u32[]{:S(2)}, u32[]{:S(2)}) collective-permute-start(bf16[192,128]{1,0:T(8,128)(2,1)S(1)} %get-tuple-element.31), channel_id=1, source_target_pairs={{0,4},{1,13},{2,6},{3,15},{4,0},{5,9},{6,2},{7,11},{8,12},{9,5},{1... | collective-permute-start | bytes 147464 | tf_op jit(solution)/shard_map/ppermute | solution.py:431
  11.7 1.7 %collective-permute-start.7 = (bf16[192,128]{1,0:T(8,128)(2,1)S(1)}, bf16[192,128]{1,0:T(8,128)(2,1)S(1)}, u32[]{:S(2)}, u32[]{:S(2)}) collective-permute-start(bf16[192,128]{1,0:T(8,128)(2,1)S(1)} %get-tuple-element.32), channel_id=1, source_target_pairs={{0,12},{1,5},{2,14},{3,7},{4,8},{5,1},{6,10},{7,3},{8,4},{9,13},{1... | collective-permute-start | bytes 147464 | tf_op jit(solution)/shard_map/ppermute | solution.py:431
  13.5 0.0 collective-permute-start.4
  13.5 1.6 %collective-permute-start.5 = (bf16[96,128]{1,0:T(8,128)(2,1)S(1)}, bf16[96,128]{1,0:T(8,128)(2,1)S(1)}, u32[]{:S(2)}, u32[]{:S(2)}) collective-permute-start(bf16[96,128]{1,0:T(8,128)(2,1)S(1)} %get-tuple-element.30), channel_id=1, source_target_pairs={{0,1},{1,0},{2,3},{3,2},{4,5},{5,4},{6,7},{7,6},{8,9},{9,8},{10,11... | collective-permute-start | bytes 73736 | tf_op jit(solution)/shard_map/ppermute | solution.py:420
  15.1 0.0 copy-done.3
  15.1 1.3 %shard_map.50.acc_ref = f32[768,128]{1,0:T(8,128)S(1)} custom-call(bf16[768,128]{1,0:T(8,128)(2,1)S(1)} %get-tuple-element.28.refs_0_, bf16[1152,128]{1,0:T(8,128)(2,1)S(1)} %bitcast.9, bf16[768,128]{1,0:T(8,128)(2,1)S(1)} %bitcast.20, bf16[1152,128]{1,0:T(8,128)(2,1)S(1)} %bitcast.23), custom_call_target="tpu_custom_call" | custom-call | flops 8000000 | bytes 2097152 | tf_op jit(solution)/shard_map/pallas_call | solution.py:405
  16.4 0.6 %collective-permute-done.4.x_far = bf16[96,128]{1,0:T(8,128)(2,1)S(1)} collective-permute-done((bf16[96,128]{1,0:T(8,128)(2,1)S(1)}, bf16[96,128]{1,0:T(8,128)(2,1)S(1)}, u32[]{:S(2)}, u32[]{:S(2)}) %collective-permute-start.4) | collective-permute-done | bytes 24608 | tf_op jit(solution)/shard_map/ppermute | solution.py:420
  16.9 0.0 collective-permute-done.5.x_near
  16.9 0.1 shard_map.51.acc_ref
  17.0 0.0 collective-permute-done.6.t_one
  17.0 0.6 %collective-permute-done.7.t_two = bf16[192,128]{1,0:T(8,128)(2,1)S(1)} collective-permute-done((bf16[192,128]{1,0:T(8,128)(2,1)S(1)}, bf16[192,128]{1,0:T(8,128)(2,1)S(1)}, u32[]{:S(2)}, u32[]{:S(2)}) %collective-permute-start.7) | collective-permute-done | bytes 49184 | tf_op jit(solution)/shard_map/ppermute | solution.py:431
  17.6 0.3 shard_map.52
  17.9 0.6 %collective-permute-start.10 = (bf16[192,128]{1,0:T(8,128)(2,1)S(1)}, bf16[192,128]{1,0:T(8,128)(2,1)S(1)}, u32[]{:S(2)}, u32[]{:S(2)}) collective-permute-start(bf16[192,128]{1,0:T(8,128)(2,1)S(1)} %get-tuple-element.36), channel_id=1, source_target_pairs={{0,4},{1,13},{2,6},{3,15},{4,0},{5,9},{6,2},{7,11},{8,12},{9,5},{1... | collective-permute-start | bytes 147464 | tf_op jit(solution)/shard_map/ppermute | solution.py:431
  18.5 1.9 %collective-permute-start.11 = (bf16[192,128]{1,0:T(8,128)(2,1)S(1)}, bf16[192,128]{1,0:T(8,128)(2,1)S(1)}, u32[]{:S(2)}, u32[]{:S(2)}) collective-permute-start(bf16[192,128]{1,0:T(8,128)(2,1)S(1)} %get-tuple-element.37), channel_id=1, source_target_pairs={{0,12},{1,5},{2,14},{3,7},{4,8},{5,1},{6,10},{7,3},{8,4},{9,13},{1... | collective-permute-start | bytes 147464 | tf_op jit(solution)/shard_map/ppermute | solution.py:431
  20.4 0.0 collective-permute-start.8
  20.4 1.6 %collective-permute-start.9 = (bf16[96,128]{1,0:T(8,128)(2,1)S(1)}, bf16[96,128]{1,0:T(8,128)(2,1)S(1)}, u32[]{:S(2)}, u32[]{:S(2)}) collective-permute-start(bf16[96,128]{1,0:T(8,128)(2,1)S(1)} %get-tuple-element.35), channel_id=1, source_target_pairs={{0,1},{1,0},{2,3},{3,2},{4,5},{5,4},{6,7},{7,6},{8,9},{9,8},{10,11... | collective-permute-start | bytes 73736 | tf_op jit(solution)/shard_map/ppermute | solution.py:420
  22.0 1.0 %shard_map.53.acc_ref = f32[768,128]{1,0:T(8,128)S(1)} custom-call(bf16[768,128]{1,0:T(8,128)(2,1)S(1)} %get-tuple-element.33.refs_0_.refs_2_, bf16[1152,128]{1,0:T(8,128)(2,1)S(1)} %bitcast.12), custom_call_target="tpu_custom_call" | custom-call | flops 5000000 | bytes 2097152 | tf_op jit(solution)/shard_map/pallas_call | solution.py:405
  23.0 0.9 %collective-permute-done.8.x_far = bf16[96,128]{1,0:T(8,128)(2,1)S(1)} collective-permute-done((bf16[96,128]{1,0:T(8,128)(2,1)S(1)}, bf16[96,128]{1,0:T(8,128)(2,1)S(1)}, u32[]{:S(2)}, u32[]{:S(2)}) %collective-permute-start.8) | collective-permute-done | bytes 24608 | tf_op jit(solution)/shard_map/ppermute | solution.py:420
  23.9 0.0 collective-permute-done.9.x_near
  23.9 0.1 shard_map.54.acc_ref
  24.0 0.0 collective-permute-done.10.t_one
  24.0 0.4 %collective-permute-done.11.t_two = bf16[192,128]{1,0:T(8,128)(2,1)S(1)} collective-permute-done((bf16[192,128]{1,0:T(8,128)(2,1)S(1)}, bf16[192,128]{1,0:T(8,128)(2,1)S(1)}, u32[]{:S(2)}, u32[]{:S(2)}) %collective-permute-start.11) | collective-permute-done | bytes 49184 | tf_op jit(solution)/shard_map/ppermute | solution.py:431
  24.4 0.6 %shard_map.55 = (bf16[768,128]{1,0:T(8,128)(2,1)S(1)}, bf16[192,128]{1,0:T(8,128)(2,1)S(1)}, bf16[192,128]{1,0:T(8,128)(2,1)S(1)}, bf16[96,128]{1,0:T(8,128)(2,1)S(1)}, bf16[96,128]{1,0:T(8,128)(2,1)S(1)}) custom-call(bf16[1152,128]{1,0:T(8,128)(2,1)S(1)} %bitcast.14, bf16[1152,128]{1,0:T(8,128)(2,1)S(1)} %bitcast.22, f32[768,128]{1,0:T(8,128)S(1)} %shard_map.54.acc_ref, ...), custom_call_target="tpu_custom_call" | custom-call | flops 4000000 | bytes 2097152 | tf_op jit(solution)/shard_map/pallas_call | solution.py:405
  25.0 0.2 collective-permute-start.14
  25.1 2.0 %collective-permute-start.15 = (bf16[192,128]{1,0:T(8,128)(2,1)S(1)}, bf16[192,128]{1,0:T(8,128)(2,1)S(1)}, u32[]{:S(2)}, u32[]{:S(2)}) collective-permute-start(bf16[192,128]{1,0:T(8,128)(2,1)S(1)} %get-tuple-element.42), channel_id=1, source_target_pairs={{0,12},{1,5},{2,14},{3,7},{4,8},{5,1},{6,10},{7,3},{8,4},{9,13},{1... | collective-permute-start | bytes 147464 | tf_op jit(solution)/shard_map/ppermute | solution.py:431
  27.1 0.0 collective-permute-start.12
  27.1 1.5 %collective-permute-start.13 = (bf16[96,128]{1,0:T(8,128)(2,1)S(1)}, bf16[96,128]{1,0:T(8,128)(2,1)S(1)}, u32[]{:S(2)}, u32[]{:S(2)}) collective-permute-start(bf16[96,128]{1,0:T(8,128)(2,1)S(1)} %get-tuple-element.40), channel_id=1, source_target_pairs={{0,1},{1,0},{2,3},{3,2},{4,5},{5,4},{6,7},{7,6},{8,9},{9,8},{10,11... | collective-permute-start | bytes 73736 | tf_op jit(solution)/shard_map/ppermute | solution.py:420
  28.6 1.3 %shard_map.56.acc_ref = f32[768,128]{1,0:T(8,128)S(1)} custom-call(bf16[768,128]{1,0:T(8,128)(2,1)S(1)} %get-tuple-element.38.refs_0_, bf16[1152,128]{1,0:T(8,128)(2,1)S(1)} %bitcast.15, bf16[768,128]{1,0:T(8,128)(2,1)S(1)} %get-tuple-element.33.refs_0_.refs_2_, bf16[1152,128]{1,0:T(8,128)(2,1)S(1)} %bitcast.24), custom_call_target="tpu_custom_call" | custom-call | flops 8000000 | bytes 2097152 | tf_op jit(solution)/shard_map/pallas_call | solution.py:405
  29.9 0.7 %collective-permute-done.12.x_far = bf16[96,128]{1,0:T(8,128)(2,1)S(1)} collective-permute-done((bf16[96,128]{1,0:T(8,128)(2,1)S(1)}, bf16[96,128]{1,0:T(8,128)(2,1)S(1)}, u32[]{:S(2)}, u32[]{:S(2)}) %collective-permute-start.12) | collective-permute-done | bytes 24608 | tf_op jit(solution)/shard_map/ppermute | solution.py:420
  30.6 0.0 collective-permute-done.13.x_near
  30.6 0.1 shard_map.57.acc_ref
  30.7 0.0 collective-permute-done.14.t_one
  30.7 0.4 %collective-permute-done.15.t_two = bf16[192,128]{1,0:T(8,128)(2,1)S(1)} collective-permute-done((bf16[192,128]{1,0:T(8,128)(2,1)S(1)}, bf16[192,128]{1,0:T(8,128)(2,1)S(1)}, u32[]{:S(2)}, u32[]{:S(2)}) %collective-permute-start.15) | collective-permute-done | bytes 49184 | tf_op jit(solution)/shard_map/ppermute | solution.py:431
  31.1 0.8 %shard_map.58 = bf16[768,128]{1,0:T(8,128)(2,1)} custom-call(bf16[1152,128]{1,0:T(8,128)(2,1)S(1)} %bitcast.17, f32[768,128]{1,0:T(8,128)S(1)} %shard_map.57.acc_ref, bf16[192,128]{1,0:T(8,128)(2,1)S(1)} %collective-permute-done.14.t_one, bf16[192,128]{1,0:T(8,128)(2,1)S(1)} %collective-permute-done.15.t_two), custom_call_target="tpu_custom_call" | custom-call | flops 1000000 | bytes 2097152 | tf_op jit(solution)/shard_map/pallas_call | solution.py:405
  (5 shorter events, 0.0 us)
Async XLA Ops:
  0.0 8.4 %copy-start = (bf16[4,3,3,2,2,2,4,128]{7,6,5,4,3,2,1,0:T(4,128)(2,1)S(1)}, bf16[4,3,3,2,2,2,4,128]{7,6,5,4,3,2,1,0:T(4,128)(2,1)}, u32[]{:S(2)}) copy-start(bf16[4,3,3,2,2,2,4,128]{7,6,5,4,3,2,1,0:T(4,128)(2,1)} %param.5) | copy-start | bytes 884740
  0.0 8.4 %copy-start.1 = (bf16[4,4,3,2,2,4,128]{6,5,4,3,2,1,0:T(4,128)(2,1)S(1)}, bf16[4,4,3,2,2,4,128]{6,5,4,3,2,1,0:T(4,128)(2,1)}, u32[]{:S(2)}) copy-start(bf16[4,4,3,2,2,4,128]{6,5,4,3,2,1,0:T(4,128)(2,1)} %param.4) | copy-start | bytes 589828
  1.2 9.1 %collective-permute-start.2 = (bf16[192,128]{1,0:T(8,128)(2,1)S(1)}, bf16[192,128]{1,0:T(8,128)(2,1)S(1)}, u32[]{:S(2)}, u32[]{:S(2)}) collective-permute-start(bf16[192,128]{1,0:T(8,128)(2,1)S(1)} %get-tuple-element.26), channel_id=1, source_target_pairs={{0,4},{1,13},{2,6},{3,15},{4,0},{5,9},{6,2},{7,11},{8,12},{9,5},{1... | collective-permute-start | bytes 147464 | tf_op jit(solution)/shard_map/ppermute | solution.py:431
  4.3 6.1 %collective-permute-start.3 = (bf16[192,128]{1,0:T(8,128)(2,1)S(1)}, bf16[192,128]{1,0:T(8,128)(2,1)S(1)}, u32[]{:S(2)}, u32[]{:S(2)}) collective-permute-start(bf16[192,128]{1,0:T(8,128)(2,1)S(1)} %get-tuple-element.27), channel_id=1, source_target_pairs={{0,12},{1,5},{2,14},{3,7},{4,8},{5,1},{6,10},{7,3},{8,4},{9,13},{1... | collective-permute-start | bytes 147464 | tf_op jit(solution)/shard_map/ppermute | solution.py:431
  6.8 3.5 %collective-permute-start = (bf16[96,128]{1,0:T(8,128)(2,1)S(1)}, bf16[96,128]{1,0:T(8,128)(2,1)S(1)}, u32[]{:S(2)}, u32[]{:S(2)}) collective-permute-start(bf16[96,128]{1,0:T(8,128)(2,1)S(1)} %get-tuple-element.24), channel_id=1, source_target_pairs={{0,3},{1,2},{2,1},{3,0},{4,7},{5,6},{6,5},{7,4},{8,11},{9,10},{10,... | collective-permute-start | bytes 73736 | tf_op jit(solution)/shard_map/ppermute | solution.py:420
  7.0 3.3 %collective-permute-start.1 = (bf16[96,128]{1,0:T(8,128)(2,1)S(1)}, bf16[96,128]{1,0:T(8,128)(2,1)S(1)}, u32[]{:S(2)}, u32[]{:S(2)}) collective-permute-start(bf16[96,128]{1,0:T(8,128)(2,1)S(1)} %get-tuple-element.25), channel_id=1, source_target_pairs={{0,1},{1,0},{2,3},{3,2},{4,5},{5,4},{6,7},{7,6},{8,9},{9,8},{10,11... | collective-permute-start | bytes 73736 | tf_op jit(solution)/shard_map/ppermute | solution.py:420
  9.4 1.0 %copy-start.2 = (bf16[2,6,6,2,2,4,128]{6,5,4,3,2,1,0:T(4,128)(2,1)S(1)}, bf16[2,6,6,2,2,4,128]{6,5,4,3,2,1,0:T(4,128)(2,1)}, u32[]{:S(2)}) copy-start(bf16[2,6,6,2,2,4,128]{6,5,4,3,2,1,0:T(4,128)(2,1)} %param.7) | copy-start | bytes 884740
  10.4 4.7 %copy-start.3 = (bf16[2,6,6,2,2,4,128]{6,5,4,3,2,1,0:T(4,128)(2,1)S(1)}, bf16[2,6,6,2,2,4,128]{6,5,4,3,2,1,0:T(4,128)(2,1)}, u32[]{:S(2)}) copy-start(bf16[2,6,6,2,2,4,128]{6,5,4,3,2,1,0:T(4,128)(2,1)} %param.6) | copy-start | bytes 884740
  11.0 6.0 %collective-permute-start.6 = (bf16[192,128]{1,0:T(8,128)(2,1)S(1)}, bf16[192,128]{1,0:T(8,128)(2,1)S(1)}, u32[]{:S(2)}, u32[]{:S(2)}) collective-permute-start(bf16[192,128]{1,0:T(8,128)(2,1)S(1)} %get-tuple-element.31), channel_id=1, source_target_pairs={{0,4},{1,13},{2,6},{3,15},{4,0},{5,9},{6,2},{7,11},{8,12},{9,5},{1... | collective-permute-start | bytes 147464 | tf_op jit(solution)/shard_map/ppermute | solution.py:431
  11.7 5.9 %collective-permute-start.7 = (bf16[192,128]{1,0:T(8,128)(2,1)S(1)}, bf16[192,128]{1,0:T(8,128)(2,1)S(1)}, u32[]{:S(2)}, u32[]{:S(2)}) collective-permute-start(bf16[192,128]{1,0:T(8,128)(2,1)S(1)} %get-tuple-element.32), channel_id=1, source_target_pairs={{0,12},{1,5},{2,14},{3,7},{4,8},{5,1},{6,10},{7,3},{8,4},{9,13},{1... | collective-permute-start | bytes 147464 | tf_op jit(solution)/shard_map/ppermute | solution.py:431
  13.5 3.5 %collective-permute-start.4 = (bf16[96,128]{1,0:T(8,128)(2,1)S(1)}, bf16[96,128]{1,0:T(8,128)(2,1)S(1)}, u32[]{:S(2)}, u32[]{:S(2)}) collective-permute-start(bf16[96,128]{1,0:T(8,128)(2,1)S(1)} %get-tuple-element.29), channel_id=1, source_target_pairs={{0,3},{1,2},{2,1},{3,0},{4,7},{5,6},{6,5},{7,4},{8,11},{9,10},{10,... | collective-permute-start | bytes 73736 | tf_op jit(solution)/shard_map/ppermute | solution.py:420
  13.5 3.5 %collective-permute-start.5 = (bf16[96,128]{1,0:T(8,128)(2,1)S(1)}, bf16[96,128]{1,0:T(8,128)(2,1)S(1)}, u32[]{:S(2)}, u32[]{:S(2)}) collective-permute-start(bf16[96,128]{1,0:T(8,128)(2,1)S(1)} %get-tuple-element.30), channel_id=1, source_target_pairs={{0,1},{1,0},{2,3},{3,2},{4,5},{5,4},{6,7},{7,6},{8,9},{9,8},{10,11... | collective-permute-start | bytes 73736 | tf_op jit(solution)/shard_map/ppermute | solution.py:420
  17.9 6.1 %collective-permute-start.10 = (bf16[192,128]{1,0:T(8,128)(2,1)S(1)}, bf16[192,128]{1,0:T(8,128)(2,1)S(1)}, u32[]{:S(2)}, u32[]{:S(2)}) collective-permute-start(bf16[192,128]{1,0:T(8,128)(2,1)S(1)} %get-tuple-element.36), channel_id=1, source_target_pairs={{0,4},{1,13},{2,6},{3,15},{4,0},{5,9},{6,2},{7,11},{8,12},{9,5},{1... | collective-permute-start | bytes 147464 | tf_op jit(solution)/shard_map/ppermute | solution.py:431
  18.5 5.9 %collective-permute-start.11 = (bf16[192,128]{1,0:T(8,128)(2,1)S(1)}, bf16[192,128]{1,0:T(8,128)(2,1)S(1)}, u32[]{:S(2)}, u32[]{:S(2)}) collective-permute-start(bf16[192,128]{1,0:T(8,128)(2,1)S(1)} %get-tuple-element.37), channel_id=1, source_target_pairs={{0,12},{1,5},{2,14},{3,7},{4,8},{5,1},{6,10},{7,3},{8,4},{9,13},{1... | collective-permute-start | bytes 147464 | tf_op jit(solution)/shard_map/ppermute | solution.py:431
  20.4 3.5 %collective-permute-start.8 = (bf16[96,128]{1,0:T(8,128)(2,1)S(1)}, bf16[96,128]{1,0:T(8,128)(2,1)S(1)}, u32[]{:S(2)}, u32[]{:S(2)}) collective-permute-start(bf16[96,128]{1,0:T(8,128)(2,1)S(1)} %get-tuple-element.34), channel_id=1, source_target_pairs={{0,3},{1,2},{2,1},{3,0},{4,7},{5,6},{6,5},{7,4},{8,11},{9,10},{10,... | collective-permute-start | bytes 73736 | tf_op jit(solution)/shard_map/ppermute | solution.py:420
  20.4 3.5 %collective-permute-start.9 = (bf16[96,128]{1,0:T(8,128)(2,1)S(1)}, bf16[96,128]{1,0:T(8,128)(2,1)S(1)}, u32[]{:S(2)}, u32[]{:S(2)}) collective-permute-start(bf16[96,128]{1,0:T(8,128)(2,1)S(1)} %get-tuple-element.35), channel_id=1, source_target_pairs={{0,1},{1,0},{2,3},{3,2},{4,5},{5,4},{6,7},{7,6},{8,9},{9,8},{10,11... | collective-permute-start | bytes 73736 | tf_op jit(solution)/shard_map/ppermute | solution.py:420
  25.0 5.7 %collective-permute-start.14 = (bf16[192,128]{1,0:T(8,128)(2,1)S(1)}, bf16[192,128]{1,0:T(8,128)(2,1)S(1)}, u32[]{:S(2)}, u32[]{:S(2)}) collective-permute-start(bf16[192,128]{1,0:T(8,128)(2,1)S(1)} %get-tuple-element.41), channel_id=1, source_target_pairs={{0,4},{1,13},{2,6},{3,15},{4,0},{5,9},{6,2},{7,11},{8,12},{9,5},{1... | collective-permute-start | bytes 147464 | tf_op jit(solution)/shard_map/ppermute | solution.py:431
  25.1 6.0 %collective-permute-start.15 = (bf16[192,128]{1,0:T(8,128)(2,1)S(1)}, bf16[192,128]{1,0:T(8,128)(2,1)S(1)}, u32[]{:S(2)}, u32[]{:S(2)}) collective-permute-start(bf16[192,128]{1,0:T(8,128)(2,1)S(1)} %get-tuple-element.42), channel_id=1, source_target_pairs={{0,12},{1,5},{2,14},{3,7},{4,8},{5,1},{6,10},{7,3},{8,4},{9,13},{1... | collective-permute-start | bytes 147464 | tf_op jit(solution)/shard_map/ppermute | solution.py:431
  27.1 3.5 %collective-permute-start.12 = (bf16[96,128]{1,0:T(8,128)(2,1)S(1)}, bf16[96,128]{1,0:T(8,128)(2,1)S(1)}, u32[]{:S(2)}, u32[]{:S(2)}) collective-permute-start(bf16[96,128]{1,0:T(8,128)(2,1)S(1)} %get-tuple-element.39), channel_id=1, source_target_pairs={{0,3},{1,2},{2,1},{3,0},{4,7},{5,6},{6,5},{7,4},{8,11},{9,10},{10,... | collective-permute-start | bytes 73736 | tf_op jit(solution)/shard_map/ppermute | solution.py:420
  27.1 3.5 %collective-permute-start.13 = (bf16[96,128]{1,0:T(8,128)(2,1)S(1)}, bf16[96,128]{1,0:T(8,128)(2,1)S(1)}, u32[]{:S(2)}, u32[]{:S(2)}) collective-permute-start(bf16[96,128]{1,0:T(8,128)(2,1)S(1)} %get-tuple-element.40), channel_id=1, source_target_pairs={{0,1},{1,0},{2,3},{3,2},{4,5},{5,4},{6,7},{7,6},{8,9},{9,8},{10,11... | collective-permute-start | bytes 73736 | tf_op jit(solution)/shard_map/ppermute | solution.py:420

commit v13 on v12

--- a/solution.py
+++ b/solution.py
@@ -314,7 +314,7 @@
     return out
 
 
-def join_x_kernel(parity, links_ref, acc_ref, x_far, x_near, out_ref):
+def join_x(links_ref, acc_ref, x_far, x_near, parity, out_ref, scale=None, done=lambda r: None):
     even = even_device("gx")
     _, x_idx = site_masks()
     sign = jnp.where(x_idx == 3, -1.0, 1.0).astype(F32)
@@ -339,10 +339,14 @@
                         )
                         for i in range(2)
                     )
-            store_field(out_ref, r, rebuild_signed(load_field(acc_ref, r), half, 1, sign))
-
-
-def join_t(links_ref, acc_ref, t_one, t_two, parity, out_ref, scale=None, done=lambda r: None):
+            field = rebuild_signed(load_field(acc_ref, r), half, 1, sign)
+            if scale is not None:
+                field = each(lambda v: v * scale, field)
+            store_field(out_ref, r, field)
+            done(r)
+
+
+def join_t_kernel(parity, links_ref, acc_ref, t_one, t_two, out_ref):
     even = even_device("ta", "gx")
     t_idx, _ = site_masks()
     first = t_idx == 0
@@ -359,28 +363,24 @@
         half += [
             tuple(roll_rows(select(first, ahead[c][i], last[c][i]), 4) for i in range(2)) for c in range(3)
         ]
-        field = rebuild_signed(load_field(acc_ref, r), half, 0, sign)
-        if scale is not None:
-            field = each(lambda v: v * scale, field)
-        store_field(out_ref, r, field)
-        done(r)
-
-
-def odd_kernel(links_ref, clover_ref, acc_ref, t_one, t_two, out_ref, *refs):
+        store_field(out_ref, r, rebuild_signed(load_field(acc_ref, r), half, 0, sign))
+
+
+def odd_kernel(links_ref, clover_ref, acc_ref, x_far, x_near, out_ref, *refs):
     outs, summed = refs[:4], refs[4]
-    join_t(links_ref, acc_ref, t_one, t_two, 0, summed)
+    join_x(links_ref, acc_ref, x_far, x_near, 0, summed)
     clover_to(clover_ref, lambda r: load_field(summed, r), out_ref, 1.0)
     send_t(out_ref, links_ref, 1, *outs[:2])
     send_x(out_ref, links_ref, 1, *outs[2:])
 
 
-def even_kernel(links_ref, acc_ref, t_one, t_two, out_ref, *outs):
-    join_t(links_ref, acc_ref, t_one, t_two, 1, out_ref, -KAPPA2)
+def even_kernel(links_ref, acc_ref, x_far, x_near, out_ref, *outs):
+    join_x(links_ref, acc_ref, x_far, x_near, 1, out_ref, -KAPPA2)
     send_t(out_ref, links_ref, 0, *outs[:2])
     send_x(out_ref, links_ref, 0, *outs[2:])
 
 
-def last_kernel(links_ref, acc_ref, t_one, t_two, out_hbm, held, sems):
+def last_kernel(links_ref, acc_ref, x_far, x_near, out_hbm, held, sems):
     part = held.shape[0] // RHS
     copies = []
 
@@ -389,7 +389,7 @@
         copies.append(pltpu.make_async_copy(held.at[rows], out_hbm.at[rows], sems.at[r]))
         copies[-1].start()
 
-    join_t(links_ref, acc_ref, t_one, t_two, 1, held, -KAPPA2, done)
+    join_x(links_ref, acc_ref, x_far, x_near, 1, held, -KAPPA2, done)
     for copy in copies:
         copy.wait()
 
@@ -453,20 +453,20 @@
             functools.partial(interior_kernel, parity, bool(parity)),
             (f, links, *base), SUM, 8_000_000 if parity else 5_000_000,
         )
-        acc, = call(functools.partial(join_x_kernel, parity), (links, acc, x_far, x_near), SUM, 1_000_000)
+        acc, = call(functools.partial(join_t_kernel, parity), (links, acc, t_one, t_two), SUM, 1_000_000)
         before = f
         if parity == 0:
             f, t_one, t_two, x_far, x_near = call(
-                odd_kernel, (links, odd, acc, t_one, t_two), FIELD + HALOS, 4_000_000,
+                odd_kernel, (links, odd, acc, x_far, x_near), FIELD + HALOS, 4_000_000,
                 [pltpu.VMEM((ROWS, 128), BF16)],
             )
         elif hop == 1:
             f, t_one, t_two, x_far, x_near = call(
-                even_kernel, (links, acc, t_one, t_two), FIELD + HALOS, 2_000_000
+                even_kernel, (links, acc, x_far, x_near), FIELD + HALOS, 2_000_000
             )
         else:
             out, = call(
-                last_kernel, (links, acc, t_one, t_two), FIELD, 1_000_000,
+                last_kernel, (links, acc, x_far, x_near), FIELD, 1_000_000,
                 [pltpu.VMEM((ROWS, 128), BF16), pltpu.SemaphoreType.DMA((RHS,))], out_space=pltpu.HBM,
             )
     return out.reshape(shape)

time: 32 us -> 32.3 us (level)
  starting transfers between devices: 19 us -> 19.6 us
  waiting for transfers between devices: 4.39 us -> 3.98 us
    ppermute x8, waiting for transfers between devices: 3.01 us -> 0.02 us  [swap(): return lax.ppermute(value, axis, pairs)]
    ppermute x8, waiting for transfers between devices: 1.38 us -> 3.95 us  [swap_t(): return lax.ppermute(value, ('ta', 'gx'), pairs)]
    ppermute x8, starting transfers between devices: 12.6 us -> 13.1 us  [swap_t(): return lax.ppermute(value, ('ta', 'gx'), pairs)]
  transfers between devices with their start and end apart: 16 -> 16, of which waited for: 7 -> 4; matrix products, arithmetic and copies ran while one was open for 0% -> 0% of each run, Pallas kernels for 15% -> 15%
where the time goes in v13:
time: 32.3 us; the launch traced here: 32.1 us
  starting transfers between devices  19.6 us (61%)
  Pallas kernels  8.39 us (26%)
  waiting for transfers between devices  3.98 us (12%)
    ppermute x8, starting transfers between devices, swap_t(): return lax.ppermute(value, ('ta', 'gx'), pairs)  13.1 us
    pallas_call x13, Pallas kernels, call(): pl.pallas_call(kernel, out_shape=tuple((jax.ShapeDtypeStruct(shape, dtype...  8.39 us
    ppermute x8, starting transfers between devices, swap(): return lax.ppermute(value, axis, pairs)  6.43 us
    ppermute x8, waiting for transfers between devices, swap_t(): return lax.ppermute(value, ('ta', 'gx'), pairs)  3.95 us
  transfers between devices with their start and end apart: 16, of which 4 were waited for; matrix products, arithmetic and copies ran while one was open for 0% of the time, Pallas kernels for 15%

profile of v13, /device:TPU:0, one launch (start us, length us, event | category | flops | bytes accessed | tf_op | source)
XLA Modules:
  0.0 32.1 jit_solution(13541284705245993710)
XLA Ops:
  0.0 1.2 %shard_map.47 = (bf16[192,128]{1,0:T(8,128)(2,1)S(1)}, bf16[192,128]{1,0:T(8,128)(2,1)S(1)}, bf16[96,128]{1,0:T(8,128)(2,1)S(1)}, bf16[96,128]{1,0:T(8,128)(2,1)S(1)}) custom-call(bf16[768,128]{1,0:T(8,128)(2,1)} %bitcast.18, bf16[1152,128]{1,0:T(8,128)(2,1)} %bitcast.5), custom_call_target="tpu_custom_call" | custom-call | flops 1500000 | bytes 2097152 | tf_op jit(solution)/shard_map/pallas_call | solution.py:405
  1.2 3.1 %collective-permute-start = (bf16[192,128]{1,0:T(8,128)(2,1)S(1)}, bf16[192,128]{1,0:T(8,128)(2,1)S(1)}, u32[]{:S(2)}, u32[]{:S(2)}) collective-permute-start(bf16[192,128]{1,0:T(8,128)(2,1)S(1)} %get-tuple-element.24), channel_id=1, source_target_pairs={{0,4},{1,13},{2,6},{3,15},{4,0},{5,9},{6,2},{7,11},{8,12},{9,5},{1... | collective-permute-start | bytes 147464 | tf_op jit(solution)/shard_map/ppermute | solution.py:431
  4.3 2.5 %collective-permute-start.1 = (bf16[192,128]{1,0:T(8,128)(2,1)S(1)}, bf16[192,128]{1,0:T(8,128)(2,1)S(1)}, u32[]{:S(2)}, u32[]{:S(2)}) collective-permute-start(bf16[192,128]{1,0:T(8,128)(2,1)S(1)} %get-tuple-element.25), channel_id=1, source_target_pairs={{0,12},{1,5},{2,14},{3,7},{4,8},{5,1},{6,10},{7,3},{8,4},{9,13},{1... | collective-permute-start | bytes 147464 | tf_op jit(solution)/shard_map/ppermute | solution.py:431
  6.8 0.2 collective-permute-start.2
  7.0 1.4 %collective-permute-start.3 = (bf16[96,128]{1,0:T(8,128)(2,1)S(1)}, bf16[96,128]{1,0:T(8,128)(2,1)S(1)}, u32[]{:S(2)}, u32[]{:S(2)}) collective-permute-start(bf16[96,128]{1,0:T(8,128)(2,1)S(1)} %get-tuple-element.27), channel_id=1, source_target_pairs={{0,1},{1,0},{2,3},{3,2},{4,5},{5,4},{6,7},{7,6},{8,9},{9,8},{10,11... | collective-permute-start | bytes 73736 | tf_op jit(solution)/shard_map/ppermute | solution.py:420
  8.4 1.0 %shard_map.46.acc_ref = f32[768,128]{1,0:T(8,128)S(1)} custom-call(bf16[768,128]{1,0:T(8,128)(2,1)S(1)} %bitcast.19, bf16[1152,128]{1,0:T(8,128)(2,1)S(1)} %bitcast.6), custom_call_target="tpu_custom_call" | custom-call | flops 5000000 | bytes 2097152 | tf_op jit(solution)/shard_map/pallas_call | solution.py:405
  9.4 0.0 copy-start.2
  9.4 0.0 collective-permute-done.t_one
  9.4 0.8 %collective-permute-done.1.t_two = bf16[192,128]{1,0:T(8,128)(2,1)S(1)} collective-permute-done((bf16[192,128]{1,0:T(8,128)(2,1)S(1)}, bf16[192,128]{1,0:T(8,128)(2,1)S(1)}, u32[]{:S(2)}, u32[]{:S(2)}) %collective-permute-start.1) | collective-permute-done | bytes 49184 | tf_op jit(solution)/shard_map/ppermute | solution.py:431
  10.2 0.1 shard_map.48.acc_ref
  10.3 0.0 collective-permute-done.2.x_far
  10.3 0.0 collective-permute-done.3.x_near
  10.3 0.0 copy-done.2
  10.3 0.0 copy-start.3
  10.4 0.6 %shard_map.49 = (bf16[768,128]{1,0:T(8,128)(2,1)S(1)}, bf16[192,128]{1,0:T(8,128)(2,1)S(1)}, bf16[192,128]{1,0:T(8,128)(2,1)S(1)}, bf16[96,128]{1,0:T(8,128)(2,1)S(1)}, bf16[96,128]{1,0:T(8,128)(2,1)S(1)}) custom-call(bf16[1152,128]{1,0:T(8,128)(2,1)S(1)} %bitcast.8, bf16[1152,128]{1,0:T(8,128)(2,1)S(1)} %bitcast.21, f32[768,128]{1,0:T(8,128)S(1)} %shard_map.48.acc_ref, ...), custom_call_target="tpu_custom_call" | custom-call | flops 4000000 | bytes 2097152 | tf_op jit(solution)/shard_map/pallas_call | solution.py:405
  11.0 0.7 %collective-permute-start.4 = (bf16[192,128]{1,0:T(8,128)(2,1)S(1)}, bf16[192,128]{1,0:T(8,128)(2,1)S(1)}, u32[]{:S(2)}, u32[]{:S(2)}) collective-permute-start(bf16[192,128]{1,0:T(8,128)(2,1)S(1)} %get-tuple-element.29), channel_id=1, source_target_pairs={{0,4},{1,13},{2,6},{3,15},{4,0},{5,9},{6,2},{7,11},{8,12},{9,5},{1... | collective-permute-start | bytes 147464 | tf_op jit(solution)/shard_map/ppermute | solution.py:431
  11.7 1.9 %collective-permute-start.5 = (bf16[192,128]{1,0:T(8,128)(2,1)S(1)}, bf16[192,128]{1,0:T(8,128)(2,1)S(1)}, u32[]{:S(2)}, u32[]{:S(2)}) collective-permute-start(bf16[192,128]{1,0:T(8,128)(2,1)S(1)} %get-tuple-element.30), channel_id=1, source_target_pairs={{0,12},{1,5},{2,14},{3,7},{4,8},{5,1},{6,10},{7,3},{8,4},{9,13},{1... | collective-permute-start | bytes 147464 | tf_op jit(solution)/shard_map/ppermute | solution.py:431
  13.6 0.0 collective-permute-start.6
  13.6 1.6 %collective-permute-start.7 = (bf16[96,128]{1,0:T(8,128)(2,1)S(1)}, bf16[96,128]{1,0:T(8,128)(2,1)S(1)}, u32[]{:S(2)}, u32[]{:S(2)}) collective-permute-start(bf16[96,128]{1,0:T(8,128)(2,1)S(1)} %get-tuple-element.32), channel_id=1, source_target_pairs={{0,1},{1,0},{2,3},{3,2},{4,5},{5,4},{6,7},{7,6},{8,9},{9,8},{10,11... | collective-permute-start | bytes 73736 | tf_op jit(solution)/shard_map/ppermute | solution.py:420
  15.2 1.3 %shard_map.50.acc_ref = f32[768,128]{1,0:T(8,128)S(1)} custom-call(bf16[768,128]{1,0:T(8,128)(2,1)S(1)} %get-tuple-element.28.refs_0_, bf16[1152,128]{1,0:T(8,128)(2,1)S(1)} %bitcast.9, bf16[768,128]{1,0:T(8,128)(2,1)S(1)} %bitcast.20, bf16[1152,128]{1,0:T(8,128)(2,1)S(1)} %bitcast.23), custom_call_target="tpu_custom_call" | custom-call | flops 8000000 | bytes 2097152 | tf_op jit(solution)/shard_map/pallas_call | solution.py:405
  16.5 0.0 collective-permute-done.4.t_one
  16.5 1.1 %collective-permute-done.5.t_two = bf16[192,128]{1,0:T(8,128)(2,1)S(1)} collective-permute-done((bf16[192,128]{1,0:T(8,128)(2,1)S(1)}, bf16[192,128]{1,0:T(8,128)(2,1)S(1)}, u32[]{:S(2)}, u32[]{:S(2)}) %collective-permute-start.5) | collective-permute-done | bytes 49184 | tf_op jit(solution)/shard_map/ppermute | solution.py:431
  17.6 0.1 shard_map.51.acc_ref
  17.7 0.0 collective-permute-done.6.x_far
  17.7 0.0 collective-permute-done.7.x_near
  17.7 0.3 shard_map.52
  18.0 0.5 %collective-permute-start.8 = (bf16[192,128]{1,0:T(8,128)(2,1)S(1)}, bf16[192,128]{1,0:T(8,128)(2,1)S(1)}, u32[]{:S(2)}, u32[]{:S(2)}) collective-permute-start(bf16[192,128]{1,0:T(8,128)(2,1)S(1)} %get-tuple-element.34), channel_id=1, source_target_pairs={{0,4},{1,13},{2,6},{3,15},{4,0},{5,9},{6,2},{7,11},{8,12},{9,5},{1... | collective-permute-start | bytes 147464 | tf_op jit(solution)/shard_map/ppermute | solution.py:431
  18.5 2.2 %collective-permute-start.9 = (bf16[192,128]{1,0:T(8,128)(2,1)S(1)}, bf16[192,128]{1,0:T(8,128)(2,1)S(1)}, u32[]{:S(2)}, u32[]{:S(2)}) collective-permute-start(bf16[192,128]{1,0:T(8,128)(2,1)S(1)} %get-tuple-element.35), channel_id=1, source_target_pairs={{0,12},{1,5},{2,14},{3,7},{4,8},{5,1},{6,10},{7,3},{8,4},{9,13},{1... | collective-permute-start | bytes 147464 | tf_op jit(solution)/shard_map/ppermute | solution.py:431
  20.6 0.0 collective-permute-start.10
  20.6 1.6 %collective-permute-start.11 = (bf16[96,128]{1,0:T(8,128)(2,1)S(1)}, bf16[96,128]{1,0:T(8,128)(2,1)S(1)}, u32[]{:S(2)}, u32[]{:S(2)}) collective-permute-start(bf16[96,128]{1,0:T(8,128)(2,1)S(1)} %get-tuple-element.37), channel_id=1, source_target_pairs={{0,1},{1,0},{2,3},{3,2},{4,5},{5,4},{6,7},{7,6},{8,9},{9,8},{10,11... | collective-permute-start | bytes 73736 | tf_op jit(solution)/shard_map/ppermute | solution.py:420
  22.3 1.0 %shard_map.53.acc_ref = f32[768,128]{1,0:T(8,128)S(1)} custom-call(bf16[768,128]{1,0:T(8,128)(2,1)S(1)} %get-tuple-element.33.refs_0_.refs_2_, bf16[1152,128]{1,0:T(8,128)(2,1)S(1)} %bitcast.12), custom_call_target="tpu_custom_call" | custom-call | flops 5000000 | bytes 2097152 | tf_op jit(solution)/shard_map/pallas_call | solution.py:405
  23.2 0.0 collective-permute-done.8.t_one
  23.2 1.1 %collective-permute-done.9.t_two = bf16[192,128]{1,0:T(8,128)(2,1)S(1)} collective-permute-done((bf16[192,128]{1,0:T(8,128)(2,1)S(1)}, bf16[192,128]{1,0:T(8,128)(2,1)S(1)}, u32[]{:S(2)}, u32[]{:S(2)}) %collective-permute-start.9) | collective-permute-done | bytes 49184 | tf_op jit(solution)/shard_map/ppermute | solution.py:431
  24.4 0.1 shard_map.54.acc_ref
  24.5 0.0 collective-permute-done.10.x_far
  24.5 0.0 collective-permute-done.11.x_near
  24.5 0.6 %shard_map.55 = (bf16[768,128]{1,0:T(8,128)(2,1)S(1)}, bf16[192,128]{1,0:T(8,128)(2,1)S(1)}, bf16[192,128]{1,0:T(8,128)(2,1)S(1)}, bf16[96,128]{1,0:T(8,128)(2,1)S(1)}, bf16[96,128]{1,0:T(8,128)(2,1)S(1)}) custom-call(bf16[1152,128]{1,0:T(8,128)(2,1)S(1)} %bitcast.14, bf16[1152,128]{1,0:T(8,128)(2,1)S(1)} %bitcast.22, f32[768,128]{1,0:T(8,128)S(1)} %shard_map.54.acc_ref, ...), custom_call_target="tpu_custom_call" | custom-call | flops 4000000 | bytes 2097152 | tf_op jit(solution)/shard_map/pallas_call | solution.py:405
  25.1 0.3 collective-permute-start.12
  25.3 2.1 %collective-permute-start.13 = (bf16[192,128]{1,0:T(8,128)(2,1)S(1)}, bf16[192,128]{1,0:T(8,128)(2,1)S(1)}, u32[]{:S(2)}, u32[]{:S(2)}) collective-permute-start(bf16[192,128]{1,0:T(8,128)(2,1)S(1)} %get-tuple-element.40), channel_id=1, source_target_pairs={{0,12},{1,5},{2,14},{3,7},{4,8},{5,1},{6,10},{7,3},{8,4},{9,13},{1... | collective-permute-start | bytes 147464 | tf_op jit(solution)/shard_map/ppermute | solution.py:431
  27.4 0.0 collective-permute-start.14
  27.4 1.6 %collective-permute-start.15 = (bf16[96,128]{1,0:T(8,128)(2,1)S(1)}, bf16[96,128]{1,0:T(8,128)(2,1)S(1)}, u32[]{:S(2)}, u32[]{:S(2)}) collective-permute-start(bf16[96,128]{1,0:T(8,128)(2,1)S(1)} %get-tuple-element.42), channel_id=1, source_target_pairs={{0,1},{1,0},{2,3},{3,2},{4,5},{5,4},{6,7},{7,6},{8,9},{9,8},{10,11... | collective-permute-start | bytes 73736 | tf_op jit(solution)/shard_map/ppermute | solution.py:420
  29.0 1.3 %shard_map.56.acc_ref = f32[768,128]{1,0:T(8,128)S(1)} custom-call(bf16[768,128]{1,0:T(8,128)(2,1)S(1)} %get-tuple-element.38.refs_0_, bf16[1152,128]{1,0:T(8,128)(2,1)S(1)} %bitcast.15, bf16[768,128]{1,0:T(8,128)(2,1)S(1)} %get-tuple-element.33.refs_0_.refs_2_, bf16[1152,128]{1,0:T(8,128)(2,1)S(1)} %bitcast.24), custom_call_target="tpu_custom_call" | custom-call | flops 8000000 | bytes 2097152 | tf_op jit(solution)/shard_map/pallas_call | solution.py:405
  30.3 0.0 collective-permute-done.12.t_one
  30.3 0.9 %collective-permute-done.13.t_two = bf16[192,128]{1,0:T(8,128)(2,1)S(1)} collective-permute-done((bf16[192,128]{1,0:T(8,128)(2,1)S(1)}, bf16[192,128]{1,0:T(8,128)(2,1)S(1)}, u32[]{:S(2)}, u32[]{:S(2)}) %collective-permute-start.13) | collective-permute-done | bytes 49184 | tf_op jit(solution)/shard_map/ppermute | solution.py:431
  31.2 0.1 shard_map.57.acc_ref
  31.3 0.0 collective-permute-done.14.x_far
  31.4 0.0 collective-permute-done.15.x_near
  31.4 0.8 %shard_map.58 = bf16[768,128]{1,0:T(8,128)(2,1)} custom-call(bf16[1152,128]{1,0:T(8,128)(2,1)S(1)} %bitcast.17, f32[768,128]{1,0:T(8,128)S(1)} %shard_map.57.acc_ref, bf16[96,128]{1,0:T(8,128)(2,1)S(1)} %collective-permute-done.14.x_far, bf16[96,128]{1,0:T(8,128)(2,1)S(1)} %collective-permute-done.15.x_near), custom_call_target="tpu_custom_call" | custom-call | flops 1000000 | bytes 2097152 | tf_op jit(solution)/shard_map/pallas_call | solution.py:405
  (5 shorter events, 0.0 us)
Async XLA Ops:
  0.0 8.4 %copy-start = (bf16[4,3,3,2,2,2,4,128]{7,6,5,4,3,2,1,0:T(4,128)(2,1)S(1)}, bf16[4,3,3,2,2,2,4,128]{7,6,5,4,3,2,1,0:T(4,128)(2,1)}, u32[]{:S(2)}) copy-start(bf16[4,3,3,2,2,2,4,128]{7,6,5,4,3,2,1,0:T(4,128)(2,1)} %param.5) | copy-start | bytes 884740
  0.0 8.4 %copy-start.1 = (bf16[4,4,3,2,2,4,128]{6,5,4,3,2,1,0:T(4,128)(2,1)S(1)}, bf16[4,4,3,2,2,4,128]{6,5,4,3,2,1,0:T(4,128)(2,1)}, u32[]{:S(2)}) copy-start(bf16[4,4,3,2,2,4,128]{6,5,4,3,2,1,0:T(4,128)(2,1)} %param.4) | copy-start | bytes 589828
  1.2 8.2 %collective-permute-start = (bf16[192,128]{1,0:T(8,128)(2,1)S(1)}, bf16[192,128]{1,0:T(8,128)(2,1)S(1)}, u32[]{:S(2)}, u32[]{:S(2)}) collective-permute-start(bf16[192,128]{1,0:T(8,128)(2,1)S(1)} %get-tuple-element.24), channel_id=1, source_target_pairs={{0,4},{1,13},{2,6},{3,15},{4,0},{5,9},{6,2},{7,11},{8,12},{9,5},{1... | collective-permute-start | bytes 147464 | tf_op jit(solution)/shard_map/ppermute | solution.py:431
  4.3 5.9 %collective-permute-start.1 = (bf16[192,128]{1,0:T(8,128)(2,1)S(1)}, bf16[192,128]{1,0:T(8,128)(2,1)S(1)}, u32[]{:S(2)}, u32[]{:S(2)}) collective-permute-start(bf16[192,128]{1,0:T(8,128)(2,1)S(1)} %get-tuple-element.25), channel_id=1, source_target_pairs={{0,12},{1,5},{2,14},{3,7},{4,8},{5,1},{6,10},{7,3},{8,4},{9,13},{1... | collective-permute-start | bytes 147464 | tf_op jit(solution)/shard_map/ppermute | solution.py:431
  6.8 3.5 %collective-permute-start.2 = (bf16[96,128]{1,0:T(8,128)(2,1)S(1)}, bf16[96,128]{1,0:T(8,128)(2,1)S(1)}, u32[]{:S(2)}, u32[]{:S(2)}) collective-permute-start(bf16[96,128]{1,0:T(8,128)(2,1)S(1)} %get-tuple-element.26), channel_id=1, source_target_pairs={{0,3},{1,2},{2,1},{3,0},{4,7},{5,6},{6,5},{7,4},{8,11},{9,10},{10,... | collective-permute-start | bytes 73736 | tf_op jit(solution)/shard_map/ppermute | solution.py:420
  7.0 3.3 %collective-permute-start.3 = (bf16[96,128]{1,0:T(8,128)(2,1)S(1)}, bf16[96,128]{1,0:T(8,128)(2,1)S(1)}, u32[]{:S(2)}, u32[]{:S(2)}) collective-permute-start(bf16[96,128]{1,0:T(8,128)(2,1)S(1)} %get-tuple-element.27), channel_id=1, source_target_pairs={{0,1},{1,0},{2,3},{3,2},{4,5},{5,4},{6,7},{7,6},{8,9},{9,8},{10,11... | collective-permute-start | bytes 73736 | tf_op jit(solution)/shard_map/ppermute | solution.py:420
  9.4 1.0 %copy-start.2 = (bf16[2,6,6,2,2,4,128]{6,5,4,3,2,1,0:T(4,128)(2,1)S(1)}, bf16[2,6,6,2,2,4,128]{6,5,4,3,2,1,0:T(4,128)(2,1)}, u32[]{:S(2)}) copy-start(bf16[2,6,6,2,2,4,128]{6,5,4,3,2,1,0:T(4,128)(2,1)} %param.7) | copy-start | bytes 884740
  10.3 4.8 %copy-start.3 = (bf16[2,6,6,2,2,4,128]{6,5,4,3,2,1,0:T(4,128)(2,1)S(1)}, bf16[2,6,6,2,2,4,128]{6,5,4,3,2,1,0:T(4,128)(2,1)}, u32[]{:S(2)}) copy-start(bf16[2,6,6,2,2,4,128]{6,5,4,3,2,1,0:T(4,128)(2,1)} %param.6) | copy-start | bytes 884740
  11.0 5.5 %collective-permute-start.4 = (bf16[192,128]{1,0:T(8,128)(2,1)S(1)}, bf16[192,128]{1,0:T(8,128)(2,1)S(1)}, u32[]{:S(2)}, u32[]{:S(2)}) collective-permute-start(bf16[192,128]{1,0:T(8,128)(2,1)S(1)} %get-tuple-element.29), channel_id=1, source_target_pairs={{0,4},{1,13},{2,6},{3,15},{4,0},{5,9},{6,2},{7,11},{8,12},{9,5},{1... | collective-permute-start | bytes 147464 | tf_op jit(solution)/shard_map/ppermute | solution.py:431
  11.7 5.9 %collective-permute-start.5 = (bf16[192,128]{1,0:T(8,128)(2,1)S(1)}, bf16[192,128]{1,0:T(8,128)(2,1)S(1)}, u32[]{:S(2)}, u32[]{:S(2)}) collective-permute-start(bf16[192,128]{1,0:T(8,128)(2,1)S(1)} %get-tuple-element.30), channel_id=1, source_target_pairs={{0,12},{1,5},{2,14},{3,7},{4,8},{5,1},{6,10},{7,3},{8,4},{9,13},{1... | collective-permute-start | bytes 147464 | tf_op jit(solution)/shard_map/ppermute | solution.py:431
  13.6 4.1 %collective-permute-start.6 = (bf16[96,128]{1,0:T(8,128)(2,1)S(1)}, bf16[96,128]{1,0:T(8,128)(2,1)S(1)}, u32[]{:S(2)}, u32[]{:S(2)}) collective-permute-start(bf16[96,128]{1,0:T(8,128)(2,1)S(1)} %get-tuple-element.31), channel_id=1, source_target_pairs={{0,3},{1,2},{2,1},{3,0},{4,7},{5,6},{6,5},{7,4},{8,11},{9,10},{10,... | collective-permute-start | bytes 73736 | tf_op jit(solution)/shard_map/ppermute | solution.py:420
  13.6 4.1 %collective-permute-start.7 = (bf16[96,128]{1,0:T(8,128)(2,1)S(1)}, bf16[96,128]{1,0:T(8,128)(2,1)S(1)}, u32[]{:S(2)}, u32[]{:S(2)}) collective-permute-start(bf16[96,128]{1,0:T(8,128)(2,1)S(1)} %get-tuple-element.32), channel_id=1, source_target_pairs={{0,1},{1,0},{2,3},{3,2},{4,5},{5,4},{6,7},{7,6},{8,9},{9,8},{10,11... | collective-permute-start | bytes 73736 | tf_op jit(solution)/shard_map/ppermute | solution.py:420
  18.0 5.2 %collective-permute-start.8 = (bf16[192,128]{1,0:T(8,128)(2,1)S(1)}, bf16[192,128]{1,0:T(8,128)(2,1)S(1)}, u32[]{:S(2)}, u32[]{:S(2)}) collective-permute-start(bf16[192,128]{1,0:T(8,128)(2,1)S(1)} %get-tuple-element.34), channel_id=1, source_target_pairs={{0,4},{1,13},{2,6},{3,15},{4,0},{5,9},{6,2},{7,11},{8,12},{9,5},{1... | collective-permute-start | bytes 147464 | tf_op jit(solution)/shard_map/ppermute | solution.py:431
  18.5 5.9 %collective-permute-start.9 = (bf16[192,128]{1,0:T(8,128)(2,1)S(1)}, bf16[192,128]{1,0:T(8,128)(2,1)S(1)}, u32[]{:S(2)}, u32[]{:S(2)}) collective-permute-start(bf16[192,128]{1,0:T(8,128)(2,1)S(1)} %get-tuple-element.35), channel_id=1, source_target_pairs={{0,12},{1,5},{2,14},{3,7},{4,8},{5,1},{6,10},{7,3},{8,4},{9,13},{1... | collective-permute-start | bytes 147464 | tf_op jit(solution)/shard_map/ppermute | solution.py:431
  20.6 3.8 %collective-permute-start.10 = (bf16[96,128]{1,0:T(8,128)(2,1)S(1)}, bf16[96,128]{1,0:T(8,128)(2,1)S(1)}, u32[]{:S(2)}, u32[]{:S(2)}) collective-permute-start(bf16[96,128]{1,0:T(8,128)(2,1)S(1)} %get-tuple-element.36), channel_id=1, source_target_pairs={{0,3},{1,2},{2,1},{3,0},{4,7},{5,6},{6,5},{7,4},{8,11},{9,10},{10,... | collective-permute-start | bytes 73736 | tf_op jit(solution)/shard_map/ppermute | solution.py:420
  20.6 3.8 %collective-permute-start.11 = (bf16[96,128]{1,0:T(8,128)(2,1)S(1)}, bf16[96,128]{1,0:T(8,128)(2,1)S(1)}, u32[]{:S(2)}, u32[]{:S(2)}) collective-permute-start(bf16[96,128]{1,0:T(8,128)(2,1)S(1)} %get-tuple-element.37), channel_id=1, source_target_pairs={{0,1},{1,0},{2,3},{3,2},{4,5},{5,4},{6,7},{7,6},{8,9},{9,8},{10,11... | collective-permute-start | bytes 73736 | tf_op jit(solution)/shard_map/ppermute | solution.py:420
  25.1 5.2 %collective-permute-start.12 = (bf16[192,128]{1,0:T(8,128)(2,1)S(1)}, bf16[192,128]{1,0:T(8,128)(2,1)S(1)}, u32[]{:S(2)}, u32[]{:S(2)}) collective-permute-start(bf16[192,128]{1,0:T(8,128)(2,1)S(1)} %get-tuple-element.39), channel_id=1, source_target_pairs={{0,4},{1,13},{2,6},{3,15},{4,0},{5,9},{6,2},{7,11},{8,12},{9,5},{1... | collective-permute-start | bytes 147464 | tf_op jit(solution)/shard_map/ppermute | solution.py:431
  25.3 5.9 %collective-permute-start.13 = (bf16[192,128]{1,0:T(8,128)(2,1)S(1)}, bf16[192,128]{1,0:T(8,128)(2,1)S(1)}, u32[]{:S(2)}, u32[]{:S(2)}) collective-permute-start(bf16[192,128]{1,0:T(8,128)(2,1)S(1)} %get-tuple-element.40), channel_id=1, source_target_pairs={{0,12},{1,5},{2,14},{3,7},{4,8},{5,1},{6,10},{7,3},{8,4},{9,13},{1... | collective-permute-start | bytes 147464 | tf_op jit(solution)/shard_map/ppermute | solution.py:431
  27.4 3.9 %collective-permute-start.14 = (bf16[96,128]{1,0:T(8,128)(2,1)S(1)}, bf16[96,128]{1,0:T(8,128)(2,1)S(1)}, u32[]{:S(2)}, u32[]{:S(2)}) collective-permute-start(bf16[96,128]{1,0:T(8,128)(2,1)S(1)} %get-tuple-element.41), channel_id=1, source_target_pairs={{0,3},{1,2},{2,1},{3,0},{4,7},{5,6},{6,5},{7,4},{8,11},{9,10},{10,... | collective-permute-start | bytes 73736 | tf_op jit(solution)/shard_map/ppermute | solution.py:420
  27.4 3.9 %collective-permute-start.15 = (bf16[96,128]{1,0:T(8,128)(2,1)S(1)}, bf16[96,128]{1,0:T(8,128)(2,1)S(1)}, u32[]{:S(2)}, u32[]{:S(2)}) collective-permute-start(bf16[96,128]{1,0:T(8,128)(2,1)S(1)} %get-tuple-element.42), channel_id=1, source_target_pairs={{0,1},{1,0},{2,3},{3,2},{4,5},{5,4},{6,7},{7,6},{8,9},{9,8},{10,11... | collective-permute-start | bytes 73736 | tf_op jit(solution)/shard_map/ppermute | solution.py:420

commit v14 on v11

--- a/solution.py
+++ b/solution.py
@@ -151,7 +151,7 @@
 
 
 def send_t(f_ref, links_ref, parity, t_one, t_two, ready=lambda r: None):
-    even = even_device("ta", "gx")
+    even = even_device("ta")
     t_idx, _ = site_masks()
     first = t_idx == 0
     links = t_edges(load_links(links_ref, 0, parity))
@@ -342,7 +342,7 @@
 
 
 def join_t(links_ref, acc_ref, t_one, t_two, parity, out_ref, scale=None, done=lambda r: None):
-    even = even_device("ta", "gx")
+    even = even_device("ta")
     t_idx, _ = site_masks()
     first = t_idx == 0
     sign = jnp.where(first, 1.0, -1.0).astype(F32)
@@ -415,17 +415,6 @@
     assert count % 2 == 0
     pairs = [(i, (i + (1 if (i % 2 == 0) != far else -1)) % count) for i in range(count)]
     return lax.ppermute(value, axis, pairs)
-
-
-def swap_t(value, ahead):
-    count, across = lax.axis_size("ta"), lax.axis_size("gx")
-    assert count % 2 == 0 and across % 2 == 0
-    pairs = []
-    for i in range(count):
-        for j in range(across):
-            step = 1 if ((i + j) % 2 == 0) == ahead else -1
-            pairs.append((i * across + j, (i + step) % count * across + j))
-    return lax.ppermute(value, ("ta", "gx"), pairs)
 
 
 def per_device(source, gauge_links, clover_even, clover_odd_inv):
@@ -443,7 +432,7 @@
     t_one, t_two = call(start_kernel, held, T_HALOS, 1_500_000, start_scratch, in_space=pltpu.HBM)
     for hop in range(4):
         parity = hop % 2
-        t_one, t_two = swap_t(t_one, True), swap_t(t_two, False)
+        t_one, t_two = swap(t_one, "ta", False), swap(t_two, "ta", True)
         x_far, x_near = call(
             functools.partial(send_x_kernel, parity), (f, links), X_HALOS, 1_500_000
         )

time: 31.8 us -> 31.8 us (level)
    ppermute x8 -> x0, starting transfers between devices: 12.4 us -> none  [swap_t(): return lax.ppermute(value, ('ta', 'gx'), pairs)]
    ppermute x8 -> x16, starting transfers between devices: 6.38 us -> 18.8 us  [swap(): return lax.ppermute(value, axis, pairs)]
    ppermute x8 -> x16, waiting for transfers between devices: 3 us -> 4.32 us  [swap(): return lax.ppermute(value, axis, pairs)]
    ppermute x8 -> x0, waiting for transfers between devices: 1.26 us -> none  [swap_t(): return lax.ppermute(value, ('ta', 'gx'), pairs)]
where the time goes in v14:
time: 31.8 us; the launch traced here: 31.7 us
  starting transfers between devices  18.8 us (59%)
  Pallas kernels  8.38 us (26%)
  waiting for transfers between devices  4.32 us (14%)
    ppermute x16, starting transfers between devices, swap(): return lax.ppermute(value, axis, pairs)  18.8 us
    pallas_call x17, Pallas kernels, call(): pl.pallas_call(kernel, out_shape=tuple((jax.ShapeDtypeStruct(shape, dtype...  8.38 us
    ppermute x16, waiting for transfers between devices, swap(): return lax.ppermute(value, axis, pairs)  4.32 us
  transfers between devices with their start and end apart: 16, of which 7 were waited for; matrix products, arithmetic and copies ran while one was open for 0% of the time, Pallas kernels for 17%

profile of v14, /device:TPU:0, one launch (start us, length us, event | category | flops | bytes accessed | tf_op | source)
XLA Modules:
  0.0 31.7 jit_solution(12204801432202146150)
XLA Ops:
  0.0 1.1 %shard_map.49 = (bf16[192,128]{1,0:T(8,128)(2,1)S(1)}, bf16[192,128]{1,0:T(8,128)(2,1)S(1)}) custom-call(bf16[768,128]{1,0:T(8,128)(2,1)} %bitcast.22, bf16[1152,128]{1,0:T(8,128)(2,1)} %bitcast.5), custom_call_target="tpu_custom_call" | custom-call | flops 1500000 | bytes 2097152 | tf_op jit(solution)/shard_map/pallas_call | solution.py:402
  1.1 3.1 %collective-permute-start.2 = (bf16[192,128]{1,0:T(8,128)(2,1)S(1)}, bf16[192,128]{1,0:T(8,128)(2,1)S(1)}, u32[]{:S(2)}, u32[]{:S(2)}) collective-permute-start(bf16[192,128]{1,0:T(8,128)(2,1)S(1)} %get-tuple-element.41), channel_id=1, source_target_pairs={{0,4},{4,0},{8,12},{12,8},{1,5},{5,1},{9,13},{13,9},{2,6},{6,2},{1... | collective-permute-start | bytes 147464 | tf_op jit(solution)/shard_map/ppermute | solution.py:417
  4.2 2.5 %collective-permute-start.3 = (bf16[192,128]{1,0:T(8,128)(2,1)S(1)}, bf16[192,128]{1,0:T(8,128)(2,1)S(1)}, u32[]{:S(2)}, u32[]{:S(2)}) collective-permute-start(bf16[192,128]{1,0:T(8,128)(2,1)S(1)} %get-tuple-element.42), channel_id=1, source_target_pairs={{0,12},{4,8},{8,4},{12,0},{1,13},{5,9},{9,5},{13,1},{2,14},{6,10},... | collective-permute-start | bytes 147464 | tf_op jit(solution)/shard_map/ppermute | solution.py:417
  6.7 0.1 shard_map.46
  6.8 0.4 %collective-permute-start = (bf16[96,128]{1,0:T(8,128)(2,1)S(1)}, bf16[96,128]{1,0:T(8,128)(2,1)S(1)}, u32[]{:S(2)}, u32[]{:S(2)}) collective-permute-start(bf16[96,128]{1,0:T(8,128)(2,1)S(1)} %get-tuple-element.39), channel_id=1, source_target_pairs={{0,3},{1,2},{2,1},{3,0},{4,7},{5,6},{6,5},{7,4},{8,11},{9,10},{10,... | collective-permute-start | bytes 73736 | tf_op jit(solution)/shard_map/ppermute | solution.py:417
  7.2 1.2 %collective-permute-start.1 = (bf16[96,128]{1,0:T(8,128)(2,1)S(1)}, bf16[96,128]{1,0:T(8,128)(2,1)S(1)}, u32[]{:S(2)}, u32[]{:S(2)}) collective-permute-start(bf16[96,128]{1,0:T(8,128)(2,1)S(1)} %get-tuple-element.40), channel_id=1, source_target_pairs={{0,1},{1,0},{2,3},{3,2},{4,5},{5,4},{6,7},{7,6},{8,9},{9,8},{10,11... | collective-permute-start | bytes 73736 | tf_op jit(solution)/shard_map/ppermute | solution.py:417
  8.5 1.0 %shard_map.47.acc_ref = f32[768,128]{1,0:T(8,128)S(1)} custom-call(bf16[768,128]{1,0:T(8,128)(2,1)S(1)} %bitcast.24, bf16[1152,128]{1,0:T(8,128)(2,1)S(1)} %bitcast.7), custom_call_target="tpu_custom_call" | custom-call | flops 5000000 | bytes 2097152 | tf_op jit(solution)/shard_map/pallas_call | solution.py:402
  9.4 0.0 copy-start.2
  9.5 0.9 %collective-permute-done.x_far = bf16[96,128]{1,0:T(8,128)(2,1)S(1)} collective-permute-done((bf16[96,128]{1,0:T(8,128)(2,1)S(1)}, bf16[96,128]{1,0:T(8,128)(2,1)S(1)}, u32[]{:S(2)}, u32[]{:S(2)}) %collective-permute-start) | collective-permute-done | bytes 24608 | tf_op jit(solution)/shard_map/ppermute | solution.py:417
  10.3 0.0 collective-permute-done.1.x_near
  10.3 0.1 shard_map.48.acc_ref
  10.4 0.0 collective-permute-done.2.t_one
  10.5 0.5 %shard_map.50 = (bf16[768,128]{1,0:T(8,128)(2,1)S(1)}, bf16[192,128]{1,0:T(8,128)(2,1)S(1)}, bf16[192,128]{1,0:T(8,128)(2,1)S(1)}) custom-call(bf16[1152,128]{1,0:T(8,128)(2,1)S(1)} %bitcast.9, bf16[1152,128]{1,0:T(8,128)(2,1)S(1)} %bitcast.26, f32[768,128]{1,0:T(8,128)S(1)} %shard_map.48.acc_ref, bf16[192,128]{1,0:T(8,128)(2,1)S(1)} %collective-permute-done.2.t_one, ...), custom_call_target="tpu_custom_call" | custom-call | flops 4000000 | bytes 2097152 | tf_op jit(solution)/shard_map/pallas_call | solution.py:402
  11.0 0.0 copy-start.3
  11.0 0.7 %collective-permute-start.6 = (bf16[192,128]{1,0:T(8,128)(2,1)S(1)}, bf16[192,128]{1,0:T(8,128)(2,1)S(1)}, u32[]{:S(2)}, u32[]{:S(2)}) collective-permute-start(bf16[192,128]{1,0:T(8,128)(2,1)S(1)} %get-tuple-element.49), channel_id=1, source_target_pairs={{0,4},{4,0},{8,12},{12,8},{1,5},{5,1},{9,13},{13,9},{2,6},{6,2},{1... | collective-permute-start | bytes 147464 | tf_op jit(solution)/shard_map/ppermute | solution.py:417
  11.7 1.5 %collective-permute-start.7 = (bf16[192,128]{1,0:T(8,128)(2,1)S(1)}, bf16[192,128]{1,0:T(8,128)(2,1)S(1)}, u32[]{:S(2)}, u32[]{:S(2)}) collective-permute-start(bf16[192,128]{1,0:T(8,128)(2,1)S(1)} %get-tuple-element.50), channel_id=1, source_target_pairs={{0,12},{4,8},{8,4},{12,0},{1,13},{5,9},{9,5},{13,1},{2,14},{6,10},... | collective-permute-start | bytes 147464 | tf_op jit(solution)/shard_map/ppermute | solution.py:417
  13.3 0.1 shard_map.51
  13.4 0.1 collective-permute-start.4
  13.4 1.6 %collective-permute-start.5 = (bf16[96,128]{1,0:T(8,128)(2,1)S(1)}, bf16[96,128]{1,0:T(8,128)(2,1)S(1)}, u32[]{:S(2)}, u32[]{:S(2)}) collective-permute-start(bf16[96,128]{1,0:T(8,128)(2,1)S(1)} %get-tuple-element.48), channel_id=1, source_target_pairs={{0,1},{1,0},{2,3},{3,2},{4,5},{5,4},{6,7},{7,6},{8,9},{9,8},{10,11... | collective-permute-start | bytes 73736 | tf_op jit(solution)/shard_map/ppermute | solution.py:417
  15.0 1.3 %shard_map.52.acc_ref = f32[768,128]{1,0:T(8,128)S(1)} custom-call(bf16[768,128]{1,0:T(8,128)(2,1)S(1)} %get-tuple-element.46.f_ref.refs_0_, bf16[1152,128]{1,0:T(8,128)(2,1)S(1)} %bitcast.11, bf16[768,128]{1,0:T(8,128)(2,1)S(1)} %bitcast.25, bf16[1152,128]{1,0:T(8,128)(2,1)S(1)} %bitcast.28), custom_call_target="tpu_custom_call" | custom-call | flops 8000000 | bytes 2097152 | tf_op jit(solution)/shard_map/pallas_call | solution.py:402
  16.3 0.6 %collective-permute-done.4.x_far = bf16[96,128]{1,0:T(8,128)(2,1)S(1)} collective-permute-done((bf16[96,128]{1,0:T(8,128)(2,1)S(1)}, bf16[96,128]{1,0:T(8,128)(2,1)S(1)}, u32[]{:S(2)}, u32[]{:S(2)}) %collective-permute-start.4) | collective-permute-done | bytes 24608 | tf_op jit(solution)/shard_map/ppermute | solution.py:417
  16.9 0.1 shard_map.53.acc_ref
  17.0 0.0 collective-permute-done.6.t_one
  17.0 0.6 %collective-permute-done.7.t_two = bf16[192,128]{1,0:T(8,128)(2,1)S(1)} collective-permute-done((bf16[192,128]{1,0:T(8,128)(2,1)S(1)}, bf16[192,128]{1,0:T(8,128)(2,1)S(1)}, u32[]{:S(2)}, u32[]{:S(2)}) %collective-permute-start.7) | collective-permute-done | bytes 49184 | tf_op jit(solution)/shard_map/ppermute | solution.py:417
  17.6 0.2 shard_map.54
  17.8 0.5 %collective-permute-start.10 = (bf16[192,128]{1,0:T(8,128)(2,1)S(1)}, bf16[192,128]{1,0:T(8,128)(2,1)S(1)}, u32[]{:S(2)}, u32[]{:S(2)}) collective-permute-start(bf16[192,128]{1,0:T(8,128)(2,1)S(1)} %get-tuple-element.57), channel_id=1, source_target_pairs={{0,4},{4,0},{8,12},{12,8},{1,5},{5,1},{9,13},{13,9},{2,6},{6,2},{1... | collective-permute-start | bytes 147464 | tf_op jit(solution)/shard_map/ppermute | solution.py:417
  18.3 1.8 %collective-permute-start.11 = (bf16[192,128]{1,0:T(8,128)(2,1)S(1)}, bf16[192,128]{1,0:T(8,128)(2,1)S(1)}, u32[]{:S(2)}, u32[]{:S(2)}) collective-permute-start(bf16[192,128]{1,0:T(8,128)(2,1)S(1)} %get-tuple-element.58), channel_id=1, source_target_pairs={{0,12},{4,8},{8,4},{12,0},{1,13},{5,9},{9,5},{13,1},{2,14},{6,10},... | collective-permute-start | bytes 147464 | tf_op jit(solution)/shard_map/ppermute | solution.py:417
  20.1 0.1 shard_map.55
  20.2 0.1 collective-permute-start.8
  20.3 1.6 %collective-permute-start.9 = (bf16[96,128]{1,0:T(8,128)(2,1)S(1)}, bf16[96,128]{1,0:T(8,128)(2,1)S(1)}, u32[]{:S(2)}, u32[]{:S(2)}) collective-permute-start(bf16[96,128]{1,0:T(8,128)(2,1)S(1)} %get-tuple-element.56), channel_id=1, source_target_pairs={{0,1},{1,0},{2,3},{3,2},{4,5},{5,4},{6,7},{7,6},{8,9},{9,8},{10,11... | collective-permute-start | bytes 73736 | tf_op jit(solution)/shard_map/ppermute | solution.py:417
  21.9 1.0 %shard_map.56.acc_ref = f32[768,128]{1,0:T(8,128)S(1)} custom-call(bf16[768,128]{1,0:T(8,128)(2,1)S(1)} %get-tuple-element.54.f_ref.refs_0_.refs_2_, bf16[1152,128]{1,0:T(8,128)(2,1)S(1)} %bitcast.15), custom_call_target="tpu_custom_call" | custom-call | flops 5000000 | bytes 2097152 | tf_op jit(solution)/shard_map/pallas_call | solution.py:402
  22.8 0.9 %collective-permute-done.8.x_far = bf16[96,128]{1,0:T(8,128)(2,1)S(1)} collective-permute-done((bf16[96,128]{1,0:T(8,128)(2,1)S(1)}, bf16[96,128]{1,0:T(8,128)(2,1)S(1)}, u32[]{:S(2)}, u32[]{:S(2)}) %collective-permute-start.8) | collective-permute-done | bytes 24608 | tf_op jit(solution)/shard_map/ppermute | solution.py:417
  23.7 0.0 collective-permute-done.9.x_near
  23.7 0.1 shard_map.57.acc_ref
  23.8 0.0 collective-permute-done.10.t_one
  23.8 0.4 %collective-permute-done.11.t_two = bf16[192,128]{1,0:T(8,128)(2,1)S(1)} collective-permute-done((bf16[192,128]{1,0:T(8,128)(2,1)S(1)}, bf16[192,128]{1,0:T(8,128)(2,1)S(1)}, u32[]{:S(2)}, u32[]{:S(2)}) %collective-permute-start.11) | collective-permute-done | bytes 49184 | tf_op jit(solution)/shard_map/ppermute | solution.py:417
  24.2 0.5 %shard_map.58 = (bf16[768,128]{1,0:T(8,128)(2,1)S(1)}, bf16[192,128]{1,0:T(8,128)(2,1)S(1)}, bf16[192,128]{1,0:T(8,128)(2,1)S(1)}) custom-call(bf16[1152,128]{1,0:T(8,128)(2,1)S(1)} %bitcast.17, bf16[1152,128]{1,0:T(8,128)(2,1)S(1)} %bitcast.27, f32[768,128]{1,0:T(8,128)S(1)} %shard_map.57.acc_ref, bf16[192,128]{1,0:T(8,128)(2,1)S(1)} %collective-permute-done.10.t_one, ...), custom_call_target="tpu_custom_call" | custom-call | flops 4000000 | bytes 2097152 | tf_op jit(solution)/shard_map/pallas_call | solution.py:402
  24.7 0.2 collective-permute-start.14
  25.0 2.1 %collective-permute-start.15 = (bf16[192,128]{1,0:T(8,128)(2,1)S(1)}, bf16[192,128]{1,0:T(8,128)(2,1)S(1)}, u32[]{:S(2)}, u32[]{:S(2)}) collective-permute-start(bf16[192,128]{1,0:T(8,128)(2,1)S(1)} %get-tuple-element.66), channel_id=1, source_target_pairs={{0,12},{4,8},{8,4},{12,0},{1,13},{5,9},{9,5},{13,1},{2,14},{6,10},... | collective-permute-start | bytes 147464 | tf_op jit(solution)/shard_map/ppermute | solution.py:417
  27.1 0.1 shard_map.59
  27.2 0.1 collective-permute-start.12
  27.2 1.3 %collective-permute-start.13 = (bf16[96,128]{1,0:T(8,128)(2,1)S(1)}, bf16[96,128]{1,0:T(8,128)(2,1)S(1)}, u32[]{:S(2)}, u32[]{:S(2)}) collective-permute-start(bf16[96,128]{1,0:T(8,128)(2,1)S(1)} %get-tuple-element.64), channel_id=1, source_target_pairs={{0,1},{1,0},{2,3},{3,2},{4,5},{5,4},{6,7},{7,6},{8,9},{9,8},{10,11... | collective-permute-start | bytes 73736 | tf_op jit(solution)/shard_map/ppermute | solution.py:417
  28.5 1.3 %shard_map.60.acc_ref = f32[768,128]{1,0:T(8,128)S(1)} custom-call(bf16[768,128]{1,0:T(8,128)(2,1)S(1)} %get-tuple-element.62.f_ref.refs_0_, bf16[1152,128]{1,0:T(8,128)(2,1)S(1)} %bitcast.19, bf16[768,128]{1,0:T(8,128)(2,1)S(1)} %get-tuple-element.54.f_ref.refs_0_.refs_2_, bf16[1152,128]{1,0:T(8,128)(2,1)S(1)} %bitcast.29), custom_call_target="tpu_custom_call" | custom-call | flops 8000000 | bytes 2097152 | tf_op jit(solution)/shard_map/pallas_call | solution.py:402
  29.8 0.7 %collective-permute-done.12.x_far = bf16[96,128]{1,0:T(8,128)(2,1)S(1)} collective-permute-done((bf16[96,128]{1,0:T(8,128)(2,1)S(1)}, bf16[96,128]{1,0:T(8,128)(2,1)S(1)}, u32[]{:S(2)}, u32[]{:S(2)}) %collective-permute-start.12) | collective-permute-done | bytes 24608 | tf_op jit(solution)/shard_map/ppermute | solution.py:417
  30.5 0.1 shard_map.61.acc_ref
  30.6 0.0 collective-permute-done.14.t_one
  30.6 0.3 collective-permute-done.15.t_two
  30.9 0.8 %shard_map.62 = bf16[768,128]{1,0:T(8,128)(2,1)} custom-call(bf16[1152,128]{1,0:T(8,128)(2,1)S(1)} %bitcast.21, f32[768,128]{1,0:T(8,128)S(1)} %shard_map.61.acc_ref, bf16[192,128]{1,0:T(8,128)(2,1)S(1)} %collective-permute-done.14.t_one, bf16[192,128]{1,0:T(8,128)(2,1)S(1)} %collective-permute-done.15.t_two), custom_call_target="tpu_custom_call" | custom-call | flops 1000000 | bytes 2097152 | tf_op jit(solution)/shard_map/pallas_call | solution.py:402
  (9 shorter events, 0.0 us)
Async XLA Ops:
  0.0 6.7 %copy-start = (bf16[4,3,3,2,2,2,4,128]{7,6,5,4,3,2,1,0:T(4,128)(2,1)S(1)}, bf16[4,3,3,2,2,2,4,128]{7,6,5,4,3,2,1,0:T(4,128)(2,1)}, u32[]{:S(2)}) copy-start(bf16[4,3,3,2,2,2,4,128]{7,6,5,4,3,2,1,0:T(4,128)(2,1)} %param.5) | copy-start | bytes 884740
  0.0 6.7 %copy-start.1 = (bf16[4,4,3,2,2,4,128]{6,5,4,3,2,1,0:T(4,128)(2,1)S(1)}, bf16[4,4,3,2,2,4,128]{6,5,4,3,2,1,0:T(4,128)(2,1)}, u32[]{:S(2)}) copy-start(bf16[4,4,3,2,2,4,128]{6,5,4,3,2,1,0:T(4,128)(2,1)} %param.4) | copy-start | bytes 589828
  1.1 9.3 %collective-permute-start.2 = (bf16[192,128]{1,0:T(8,128)(2,1)S(1)}, bf16[192,128]{1,0:T(8,128)(2,1)S(1)}, u32[]{:S(2)}, u32[]{:S(2)}) collective-permute-start(bf16[192,128]{1,0:T(8,128)(2,1)S(1)} %get-tuple-element.41), channel_id=1, source_target_pairs={{0,4},{4,0},{8,12},{12,8},{1,5},{5,1},{9,13},{13,9},{2,6},{6,2},{1... | collective-permute-start | bytes 147464 | tf_op jit(solution)/shard_map/ppermute | solution.py:417
  4.2 6.2 %collective-permute-start.3 = (bf16[192,128]{1,0:T(8,128)(2,1)S(1)}, bf16[192,128]{1,0:T(8,128)(2,1)S(1)}, u32[]{:S(2)}, u32[]{:S(2)}) collective-permute-start(bf16[192,128]{1,0:T(8,128)(2,1)S(1)} %get-tuple-element.42), channel_id=1, source_target_pairs={{0,12},{4,8},{8,4},{12,0},{1,13},{5,9},{9,5},{13,1},{2,14},{6,10},... | collective-permute-start | bytes 147464 | tf_op jit(solution)/shard_map/ppermute | solution.py:417
  6.8 3.5 %collective-permute-start = (bf16[96,128]{1,0:T(8,128)(2,1)S(1)}, bf16[96,128]{1,0:T(8,128)(2,1)S(1)}, u32[]{:S(2)}, u32[]{:S(2)}) collective-permute-start(bf16[96,128]{1,0:T(8,128)(2,1)S(1)} %get-tuple-element.39), channel_id=1, source_target_pairs={{0,3},{1,2},{2,1},{3,0},{4,7},{5,6},{6,5},{7,4},{8,11},{9,10},{10,... | collective-permute-start | bytes 73736 | tf_op jit(solution)/shard_map/ppermute | solution.py:417
  7.2 3.1 %collective-permute-start.1 = (bf16[96,128]{1,0:T(8,128)(2,1)S(1)}, bf16[96,128]{1,0:T(8,128)(2,1)S(1)}, u32[]{:S(2)}, u32[]{:S(2)}) collective-permute-start(bf16[96,128]{1,0:T(8,128)(2,1)S(1)} %get-tuple-element.40), channel_id=1, source_target_pairs={{0,1},{1,0},{2,3},{3,2},{4,5},{5,4},{6,7},{7,6},{8,9},{9,8},{10,11... | collective-permute-start | bytes 73736 | tf_op jit(solution)/shard_map/ppermute | solution.py:417
  9.4 1.0 %copy-start.2 = (bf16[2,6,6,2,2,4,128]{6,5,4,3,2,1,0:T(4,128)(2,1)S(1)}, bf16[2,6,6,2,2,4,128]{6,5,4,3,2,1,0:T(4,128)(2,1)}, u32[]{:S(2)}) copy-start(bf16[2,6,6,2,2,4,128]{6,5,4,3,2,1,0:T(4,128)(2,1)} %param.7) | copy-start | bytes 884740
  11.0 4.1 %copy-start.3 = (bf16[2,6,6,2,2,4,128]{6,5,4,3,2,1,0:T(4,128)(2,1)S(1)}, bf16[2,6,6,2,2,4,128]{6,5,4,3,2,1,0:T(4,128)(2,1)}, u32[]{:S(2)}) copy-start(bf16[2,6,6,2,2,4,128]{6,5,4,3,2,1,0:T(4,128)(2,1)} %param.6) | copy-start | bytes 884740
  11.0 6.0 %collective-permute-start.6 = (bf16[192,128]{1,0:T(8,128)(2,1)S(1)}, bf16[192,128]{1,0:T(8,128)(2,1)S(1)}, u32[]{:S(2)}, u32[]{:S(2)}) collective-permute-start(bf16[192,128]{1,0:T(8,128)(2,1)S(1)} %get-tuple-element.49), channel_id=1, source_target_pairs={{0,4},{4,0},{8,12},{12,8},{1,5},{5,1},{9,13},{13,9},{2,6},{6,2},{1... | collective-permute-start | bytes 147464 | tf_op jit(solution)/shard_map/ppermute | solution.py:417
  11.7 5.9 %collective-permute-start.7 = (bf16[192,128]{1,0:T(8,128)(2,1)S(1)}, bf16[192,128]{1,0:T(8,128)(2,1)S(1)}, u32[]{:S(2)}, u32[]{:S(2)}) collective-permute-start(bf16[192,128]{1,0:T(8,128)(2,1)S(1)} %get-tuple-element.50), channel_id=1, source_target_pairs={{0,12},{4,8},{8,4},{12,0},{1,13},{5,9},{9,5},{13,1},{2,14},{6,10},... | collective-permute-start | bytes 147464 | tf_op jit(solution)/shard_map/ppermute | solution.py:417
  13.4 3.5 %collective-permute-start.4 = (bf16[96,128]{1,0:T(8,128)(2,1)S(1)}, bf16[96,128]{1,0:T(8,128)(2,1)S(1)}, u32[]{:S(2)}, u32[]{:S(2)}) collective-permute-start(bf16[96,128]{1,0:T(8,128)(2,1)S(1)} %get-tuple-element.47), channel_id=1, source_target_pairs={{0,3},{1,2},{2,1},{3,0},{4,7},{5,6},{6,5},{7,4},{8,11},{9,10},{10,... | collective-permute-start | bytes 73736 | tf_op jit(solution)/shard_map/ppermute | solution.py:417
  13.4 3.5 %collective-permute-start.5 = (bf16[96,128]{1,0:T(8,128)(2,1)S(1)}, bf16[96,128]{1,0:T(8,128)(2,1)S(1)}, u32[]{:S(2)}, u32[]{:S(2)}) collective-permute-start(bf16[96,128]{1,0:T(8,128)(2,1)S(1)} %get-tuple-element.48), channel_id=1, source_target_pairs={{0,1},{1,0},{2,3},{3,2},{4,5},{5,4},{6,7},{7,6},{8,9},{9,8},{10,11... | collective-permute-start | bytes 73736 | tf_op jit(solution)/shard_map/ppermute | solution.py:417
  17.8 6.0 %collective-permute-start.10 = (bf16[192,128]{1,0:T(8,128)(2,1)S(1)}, bf16[192,128]{1,0:T(8,128)(2,1)S(1)}, u32[]{:S(2)}, u32[]{:S(2)}) collective-permute-start(bf16[192,128]{1,0:T(8,128)(2,1)S(1)} %get-tuple-element.57), channel_id=1, source_target_pairs={{0,4},{4,0},{8,12},{12,8},{1,5},{5,1},{9,13},{13,9},{2,6},{6,2},{1... | collective-permute-start | bytes 147464 | tf_op jit(solution)/shard_map/ppermute | solution.py:417
  18.3 5.9 %collective-permute-start.11 = (bf16[192,128]{1,0:T(8,128)(2,1)S(1)}, bf16[192,128]{1,0:T(8,128)(2,1)S(1)}, u32[]{:S(2)}, u32[]{:S(2)}) collective-permute-start(bf16[192,128]{1,0:T(8,128)(2,1)S(1)} %get-tuple-element.58), channel_id=1, source_target_pairs={{0,12},{4,8},{8,4},{12,0},{1,13},{5,9},{9,5},{13,1},{2,14},{6,10},... | collective-permute-start | bytes 147464 | tf_op jit(solution)/shard_map/ppermute | solution.py:417
  20.2 3.5 %collective-permute-start.8 = (bf16[96,128]{1,0:T(8,128)(2,1)S(1)}, bf16[96,128]{1,0:T(8,128)(2,1)S(1)}, u32[]{:S(2)}, u32[]{:S(2)}) collective-permute-start(bf16[96,128]{1,0:T(8,128)(2,1)S(1)} %get-tuple-element.55), channel_id=1, source_target_pairs={{0,3},{1,2},{2,1},{3,0},{4,7},{5,6},{6,5},{7,4},{8,11},{9,10},{10,... | collective-permute-start | bytes 73736 | tf_op jit(solution)/shard_map/ppermute | solution.py:417
  20.3 3.5 %collective-permute-start.9 = (bf16[96,128]{1,0:T(8,128)(2,1)S(1)}, bf16[96,128]{1,0:T(8,128)(2,1)S(1)}, u32[]{:S(2)}, u32[]{:S(2)}) collective-permute-start(bf16[96,128]{1,0:T(8,128)(2,1)S(1)} %get-tuple-element.56), channel_id=1, source_target_pairs={{0,1},{1,0},{2,3},{3,2},{4,5},{5,4},{6,7},{7,6},{8,9},{9,8},{10,11... | collective-permute-start | bytes 73736 | tf_op jit(solution)/shard_map/ppermute | solution.py:417
  24.7 5.8 %collective-permute-start.14 = (bf16[192,128]{1,0:T(8,128)(2,1)S(1)}, bf16[192,128]{1,0:T(8,128)(2,1)S(1)}, u32[]{:S(2)}, u32[]{:S(2)}) collective-permute-start(bf16[192,128]{1,0:T(8,128)(2,1)S(1)} %get-tuple-element.65), channel_id=1, source_target_pairs={{0,4},{4,0},{8,12},{12,8},{1,5},{5,1},{9,13},{13,9},{2,6},{6,2},{1... | collective-permute-start | bytes 147464 | tf_op jit(solution)/shard_map/ppermute | solution.py:417
  25.0 5.9 %collective-permute-start.15 = (bf16[192,128]{1,0:T(8,128)(2,1)S(1)}, bf16[192,128]{1,0:T(8,128)(2,1)S(1)}, u32[]{:S(2)}, u32[]{:S(2)}) collective-permute-start(bf16[192,128]{1,0:T(8,128)(2,1)S(1)} %get-tuple-element.66), channel_id=1, source_target_pairs={{0,12},{4,8},{8,4},{12,0},{1,13},{5,9},{9,5},{13,1},{2,14},{6,10},... | collective-permute-start | bytes 147464 | tf_op jit(solution)/shard_map/ppermute | solution.py:417
  27.2 3.3 %collective-permute-start.12 = (bf16[96,128]{1,0:T(8,128)(2,1)S(1)}, bf16[96,128]{1,0:T(8,128)(2,1)S(1)}, u32[]{:S(2)}, u32[]{:S(2)}) collective-permute-start(bf16[96,128]{1,0:T(8,128)(2,1)S(1)} %get-tuple-element.63), channel_id=1, source_target_pairs={{0,3},{1,2},{2,1},{3,0},{4,7},{5,6},{6,5},{7,4},{8,11},{9,10},{10,... | collective-permute-start | bytes 73736 | tf_op jit(solution)/shard_map/ppermute | solution.py:417
  27.2 3.2 %collective-permute-start.13 = (bf16[96,128]{1,0:T(8,128)(2,1)S(1)}, bf16[96,128]{1,0:T(8,128)(2,1)S(1)}, u32[]{:S(2)}, u32[]{:S(2)}) collective-permute-start(bf16[96,128]{1,0:T(8,128)(2,1)S(1)} %get-tuple-element.64), channel_id=1, source_target_pairs={{0,1},{1,0},{2,3},{3,2},{4,5},{5,4},{6,7},{7,6},{8,9},{9,8},{10,11... | collective-permute-start | bytes 73736 | tf_op jit(solution)/shard_map/ppermute | solution.py:417

commit v15 on v11

--- a/solution.py
+++ b/solution.py
@@ -169,7 +169,7 @@
             store_pair(t_two, r * 3 + c, either(even, front, rears[c]))
 
 
-def send_x_kernel(parity, f_ref, links_ref, x_far, x_near):
+def send_x_kernel(parity, f_ref, links_ref, x_near, x_far):
     even = even_device("gx")
     _, x_idx = site_masks()
     links = x_edges(load_links(links_ref, 1, parity))
@@ -313,7 +313,7 @@
     return out
 
 
-def join_x_kernel(parity, links_ref, acc_ref, x_far, x_near, out_ref):
+def join_x_kernel(parity, links_ref, acc_ref, x_near, x_far, out_ref):
     even = even_device("gx")
     _, x_idx = site_masks()
     sign = jnp.where(x_idx == 3, -1.0, 1.0).astype(F32)
@@ -444,17 +444,17 @@
     for hop in range(4):
         parity = hop % 2
         t_one, t_two = swap_t(t_one, True), swap_t(t_two, False)
-        x_far, x_near = call(
+        x_near, x_far = call(
             functools.partial(send_x_kernel, parity), (f, links), X_HALOS, 1_500_000
         )
-        here, x_far, x_near = lax.optimization_barrier((f, x_far, x_near))
-        x_far, x_near = swap(x_far, "gx", True), swap(x_near, "gx", False)
+        here, x_near, x_far = lax.optimization_barrier((f, x_near, x_far))
+        x_near, x_far = swap(x_near, "gx", False), swap(x_far, "gx", True)
         base = (before, even) if parity else ()
         acc, = call(
             functools.partial(interior_kernel, parity, bool(parity)),
             (here, links, *base), SUM, 8_000_000 if parity else 5_000_000,
         )
-        acc, = call(functools.partial(join_x_kernel, parity), (links, acc, x_far, x_near), SUM, 1_000_000)
+        acc, = call(functools.partial(join_x_kernel, parity), (links, acc, x_near, x_far), SUM, 1_000_000)
         before = f
         if parity == 0:
             f, t_one, t_two = call(

time: 31.8 us -> 32.3 us (1.016)
  starting transfers between devices: 18.8 us -> 19.9 us
  waiting for transfers between devices: 4.25 us -> 3.54 us
    ppermute x8, waiting for transfers between devices: 3 us -> 2.27 us  [swap(): return lax.ppermute(value, axis, pairs)]
    ppermute x8, starting transfers between devices: 12.4 us -> 13.2 us  [swap_t(): return lax.ppermute(value, ('ta', 'gx'), pairs)]
    ppermute x8, starting transfers between devices: 6.38 us -> 6.71 us  [swap(): return lax.ppermute(value, axis, pairs)]
  transfers between devices with their start and end apart: 16 -> 16, of which waited for: 7 -> 7; matrix products, arithmetic and copies ran while one was open for 0% -> 0% of each run, Pallas kernels for 17% -> 16%
where the time goes in v15:
time: 32.3 us; the launch traced here: 32.1 us
  starting transfers between devices  19.9 us (62%)
  Pallas kernels  8.37 us (26%)
  waiting for transfers between devices  3.54 us (11%)
    ppermute x8, starting transfers between devices, swap_t(): return lax.ppermute(value, ('ta', 'gx'), pairs)  13.2 us
    pallas_call x17, Pallas kernels, call(): pl.pallas_call(kernel, out_shape=tuple((jax.ShapeDtypeStruct(shape, dtype...  8.37 us
    ppermute x8, starting transfers between devices, swap(): return lax.ppermute(value, axis, pairs)  6.71 us
    ppermute x8, waiting for transfers between devices, swap(): return lax.ppermute(value, axis, pairs)  2.27 us
    ppermute x8, waiting for transfers between devices, swap_t(): return lax.ppermute(value, ('ta', 'gx'), pairs)  1.27 us
  transfers between devices with their start and end apart: 16, of which 7 were waited for; matrix products, arithmetic and copies ran while one was open for 0% of the time, Pallas kernels for 16%

profile of v15, /device:TPU:0, one launch (start us, length us, event | category | flops | bytes accessed | tf_op | source)
XLA Modules:
  0.0 32.1 jit_solution(6026469460921759960)
XLA Ops:
  0.0 1.1 %shard_map.49 = (bf16[192,128]{1,0:T(8,128)(2,1)S(1)}, bf16[192,128]{1,0:T(8,128)(2,1)S(1)}) custom-call(bf16[768,128]{1,0:T(8,128)(2,1)} %bitcast.22, bf16[1152,128]{1,0:T(8,128)(2,1)} %bitcast.5), custom_call_target="tpu_custom_call" | custom-call | flops 1500000 | bytes 2097152 | tf_op jit(solution)/shard_map/pallas_call | solution.py:402
  1.1 3.1 %collective-permute-start.2 = (bf16[192,128]{1,0:T(8,128)(2,1)S(1)}, bf16[192,128]{1,0:T(8,128)(2,1)S(1)}, u32[]{:S(2)}, u32[]{:S(2)}) collective-permute-start(bf16[192,128]{1,0:T(8,128)(2,1)S(1)} %get-tuple-element.41), channel_id=1, source_target_pairs={{0,4},{1,13},{2,6},{3,15},{4,0},{5,9},{6,2},{7,11},{8,12},{9,5},{1... | collective-permute-start | bytes 147464 | tf_op jit(solution)/shard_map/ppermute | solution.py:428
  4.2 2.5 %collective-permute-start.3 = (bf16[192,128]{1,0:T(8,128)(2,1)S(1)}, bf16[192,128]{1,0:T(8,128)(2,1)S(1)}, u32[]{:S(2)}, u32[]{:S(2)}) collective-permute-start(bf16[192,128]{1,0:T(8,128)(2,1)S(1)} %get-tuple-element.42), channel_id=1, source_target_pairs={{0,12},{1,5},{2,14},{3,7},{4,8},{5,1},{6,10},{7,3},{8,4},{9,13},{1... | collective-permute-start | bytes 147464 | tf_op jit(solution)/shard_map/ppermute | solution.py:428
  6.7 0.1 shard_map.46
  6.8 0.1 collective-permute-start
  6.9 1.6 %collective-permute-start.1 = (bf16[96,128]{1,0:T(8,128)(2,1)S(1)}, bf16[96,128]{1,0:T(8,128)(2,1)S(1)}, u32[]{:S(2)}, u32[]{:S(2)}) collective-permute-start(bf16[96,128]{1,0:T(8,128)(2,1)S(1)} %get-tuple-element.40), channel_id=1, source_target_pairs={{0,3},{1,2},{2,1},{3,0},{4,7},{5,6},{6,5},{7,4},{8,11},{9,10},{10,... | collective-permute-start | bytes 73736 | tf_op jit(solution)/shard_map/ppermute | solution.py:417
  8.5 1.0 %shard_map.47.acc_ref = f32[768,128]{1,0:T(8,128)S(1)} custom-call(bf16[768,128]{1,0:T(8,128)(2,1)S(1)} %bitcast.24, bf16[1152,128]{1,0:T(8,128)(2,1)S(1)} %bitcast.7), custom_call_target="tpu_custom_call" | custom-call | flops 5000000 | bytes 2097152 | tf_op jit(solution)/shard_map/pallas_call | solution.py:402
  9.5 0.0 copy-start.2
  9.5 0.0 collective-permute-done.x_near
  9.5 0.7 %collective-permute-done.1.x_far = bf16[96,128]{1,0:T(8,128)(2,1)S(1)} collective-permute-done((bf16[96,128]{1,0:T(8,128)(2,1)S(1)}, bf16[96,128]{1,0:T(8,128)(2,1)S(1)}, u32[]{:S(2)}, u32[]{:S(2)}) %collective-permute-start.1) | collective-permute-done | bytes 24608 | tf_op jit(solution)/shard_map/ppermute | solution.py:417
  10.2 0.1 shard_map.48.acc_ref
  10.3 0.0 collective-permute-done.2.t_one
  10.3 0.1 copy-done.2
  10.4 0.5 %shard_map.50 = (bf16[768,128]{1,0:T(8,128)(2,1)S(1)}, bf16[192,128]{1,0:T(8,128)(2,1)S(1)}, bf16[192,128]{1,0:T(8,128)(2,1)S(1)}) custom-call(bf16[1152,128]{1,0:T(8,128)(2,1)S(1)} %bitcast.9, bf16[1152,128]{1,0:T(8,128)(2,1)S(1)} %bitcast.26, f32[768,128]{1,0:T(8,128)S(1)} %shard_map.48.acc_ref, bf16[192,128]{1,0:T(8,128)(2,1)S(1)} %collective-permute-done.2.t_one, ...), custom_call_target="tpu_custom_call" | custom-call | flops 4000000 | bytes 2097152 | tf_op jit(solution)/shard_map/pallas_call | solution.py:402
  10.9 0.0 copy-start.3
  10.9 0.7 %collective-permute-start.6 = (bf16[192,128]{1,0:T(8,128)(2,1)S(1)}, bf16[192,128]{1,0:T(8,128)(2,1)S(1)}, u32[]{:S(2)}, u32[]{:S(2)}) collective-permute-start(bf16[192,128]{1,0:T(8,128)(2,1)S(1)} %get-tuple-element.49), channel_id=1, source_target_pairs={{0,4},{1,13},{2,6},{3,15},{4,0},{5,9},{6,2},{7,11},{8,12},{9,5},{1... | collective-permute-start | bytes 147464 | tf_op jit(solution)/shard_map/ppermute | solution.py:428
  11.7 1.6 %collective-permute-start.7 = (bf16[192,128]{1,0:T(8,128)(2,1)S(1)}, bf16[192,128]{1,0:T(8,128)(2,1)S(1)}, u32[]{:S(2)}, u32[]{:S(2)}) collective-permute-start(bf16[192,128]{1,0:T(8,128)(2,1)S(1)} %get-tuple-element.50), channel_id=1, source_target_pairs={{0,12},{1,5},{2,14},{3,7},{4,8},{5,1},{6,10},{7,3},{8,4},{9,13},{1... | collective-permute-start | bytes 147464 | tf_op jit(solution)/shard_map/ppermute | solution.py:428
  13.3 0.1 shard_map.51
  13.4 0.1 collective-permute-start.4
  13.4 1.6 %collective-permute-start.5 = (bf16[96,128]{1,0:T(8,128)(2,1)S(1)}, bf16[96,128]{1,0:T(8,128)(2,1)S(1)}, u32[]{:S(2)}, u32[]{:S(2)}) collective-permute-start(bf16[96,128]{1,0:T(8,128)(2,1)S(1)} %get-tuple-element.48), channel_id=1, source_target_pairs={{0,3},{1,2},{2,1},{3,0},{4,7},{5,6},{6,5},{7,4},{8,11},{9,10},{10,... | collective-permute-start | bytes 73736 | tf_op jit(solution)/shard_map/ppermute | solution.py:417
  15.0 1.3 %shard_map.52.acc_ref = f32[768,128]{1,0:T(8,128)S(1)} custom-call(bf16[768,128]{1,0:T(8,128)(2,1)S(1)} %get-tuple-element.46.f_ref.refs_0_, bf16[1152,128]{1,0:T(8,128)(2,1)S(1)} %bitcast.11, bf16[768,128]{1,0:T(8,128)(2,1)S(1)} %bitcast.25, bf16[1152,128]{1,0:T(8,128)(2,1)S(1)} %bitcast.28), custom_call_target="tpu_custom_call" | custom-call | flops 8000000 | bytes 2097152 | tf_op jit(solution)/shard_map/pallas_call | solution.py:402
  16.3 0.0 collective-permute-done.4.x_near
  16.4 0.4 %collective-permute-done.5.x_far = bf16[96,128]{1,0:T(8,128)(2,1)S(1)} collective-permute-done((bf16[96,128]{1,0:T(8,128)(2,1)S(1)}, bf16[96,128]{1,0:T(8,128)(2,1)S(1)}, u32[]{:S(2)}, u32[]{:S(2)}) %collective-permute-start.5) | collective-permute-done | bytes 24608 | tf_op jit(solution)/shard_map/ppermute | solution.py:417
  16.8 0.1 shard_map.53.acc_ref
  16.9 0.7 %collective-permute-done.7.t_two = bf16[192,128]{1,0:T(8,128)(2,1)S(1)} collective-permute-done((bf16[192,128]{1,0:T(8,128)(2,1)S(1)}, bf16[192,128]{1,0:T(8,128)(2,1)S(1)}, u32[]{:S(2)}, u32[]{:S(2)}) %collective-permute-start.7) | collective-permute-done | bytes 49184 | tf_op jit(solution)/shard_map/ppermute | solution.py:428
  17.6 0.2 shard_map.54
  17.8 0.5 %collective-permute-start.10 = (bf16[192,128]{1,0:T(8,128)(2,1)S(1)}, bf16[192,128]{1,0:T(8,128)(2,1)S(1)}, u32[]{:S(2)}, u32[]{:S(2)}) collective-permute-start(bf16[192,128]{1,0:T(8,128)(2,1)S(1)} %get-tuple-element.57), channel_id=1, source_target_pairs={{0,4},{1,13},{2,6},{3,15},{4,0},{5,9},{6,2},{7,11},{8,12},{9,5},{1... | collective-permute-start | bytes 147464 | tf_op jit(solution)/shard_map/ppermute | solution.py:428
  18.3 2.2 %collective-permute-start.11 = (bf16[192,128]{1,0:T(8,128)(2,1)S(1)}, bf16[192,128]{1,0:T(8,128)(2,1)S(1)}, u32[]{:S(2)}, u32[]{:S(2)}) collective-permute-start(bf16[192,128]{1,0:T(8,128)(2,1)S(1)} %get-tuple-element.58), channel_id=1, source_target_pairs={{0,12},{1,5},{2,14},{3,7},{4,8},{5,1},{6,10},{7,3},{8,4},{9,13},{1... | collective-permute-start | bytes 147464 | tf_op jit(solution)/shard_map/ppermute | solution.py:428
  20.5 0.1 shard_map.55
  20.6 0.1 collective-permute-start.8
  20.7 1.6 %collective-permute-start.9 = (bf16[96,128]{1,0:T(8,128)(2,1)S(1)}, bf16[96,128]{1,0:T(8,128)(2,1)S(1)}, u32[]{:S(2)}, u32[]{:S(2)}) collective-permute-start(bf16[96,128]{1,0:T(8,128)(2,1)S(1)} %get-tuple-element.56), channel_id=1, source_target_pairs={{0,3},{1,2},{2,1},{3,0},{4,7},{5,6},{6,5},{7,4},{8,11},{9,10},{10,... | collective-permute-start | bytes 73736 | tf_op jit(solution)/shard_map/ppermute | solution.py:417
  22.3 1.0 %shard_map.56.acc_ref = f32[768,128]{1,0:T(8,128)S(1)} custom-call(bf16[768,128]{1,0:T(8,128)(2,1)S(1)} %get-tuple-element.54.f_ref.refs_0_.refs_2_, bf16[1152,128]{1,0:T(8,128)(2,1)S(1)} %bitcast.15), custom_call_target="tpu_custom_call" | custom-call | flops 5000000 | bytes 2097152 | tf_op jit(solution)/shard_map/pallas_call | solution.py:402
  23.2 0.7 %collective-permute-done.9.x_far = bf16[96,128]{1,0:T(8,128)(2,1)S(1)} collective-permute-done((bf16[96,128]{1,0:T(8,128)(2,1)S(1)}, bf16[96,128]{1,0:T(8,128)(2,1)S(1)}, u32[]{:S(2)}, u32[]{:S(2)}) %collective-permute-start.9) | collective-permute-done | bytes 24608 | tf_op jit(solution)/shard_map/ppermute | solution.py:417
  24.0 0.1 shard_map.57.acc_ref
  24.1 0.0 collective-permute-done.10.t_one
  24.1 0.1 collective-permute-done.11.t_two
  24.2 0.5 %shard_map.58 = (bf16[768,128]{1,0:T(8,128)(2,1)S(1)}, bf16[192,128]{1,0:T(8,128)(2,1)S(1)}, bf16[192,128]{1,0:T(8,128)(2,1)S(1)}) custom-call(bf16[1152,128]{1,0:T(8,128)(2,1)S(1)} %bitcast.17, bf16[1152,128]{1,0:T(8,128)(2,1)S(1)} %bitcast.27, f32[768,128]{1,0:T(8,128)S(1)} %shard_map.57.acc_ref, bf16[192,128]{1,0:T(8,128)(2,1)S(1)} %collective-permute-done.10.t_one, ...), custom_call_target="tpu_custom_call" | custom-call | flops 4000000 | bytes 2097152 | tf_op jit(solution)/shard_map/pallas_call | solution.py:402
  24.7 0.7 %collective-permute-start.14 = (bf16[192,128]{1,0:T(8,128)(2,1)S(1)}, bf16[192,128]{1,0:T(8,128)(2,1)S(1)}, u32[]{:S(2)}, u32[]{:S(2)}) collective-permute-start(bf16[192,128]{1,0:T(8,128)(2,1)S(1)} %get-tuple-element.65), channel_id=1, source_target_pairs={{0,4},{1,13},{2,6},{3,15},{4,0},{5,9},{6,2},{7,11},{8,12},{9,5},{1... | collective-permute-start | bytes 147464 | tf_op jit(solution)/shard_map/ppermute | solution.py:428
  25.4 1.9 %collective-permute-start.15 = (bf16[192,128]{1,0:T(8,128)(2,1)S(1)}, bf16[192,128]{1,0:T(8,128)(2,1)S(1)}, u32[]{:S(2)}, u32[]{:S(2)}) collective-permute-start(bf16[192,128]{1,0:T(8,128)(2,1)S(1)} %get-tuple-element.66), channel_id=1, source_target_pairs={{0,12},{1,5},{2,14},{3,7},{4,8},{5,1},{6,10},{7,3},{8,4},{9,13},{1... | collective-permute-start | bytes 147464 | tf_op jit(solution)/shard_map/ppermute | solution.py:428
  27.3 0.1 shard_map.59
  27.4 0.1 collective-permute-start.12
  27.5 1.6 %collective-permute-start.13 = (bf16[96,128]{1,0:T(8,128)(2,1)S(1)}, bf16[96,128]{1,0:T(8,128)(2,1)S(1)}, u32[]{:S(2)}, u32[]{:S(2)}) collective-permute-start(bf16[96,128]{1,0:T(8,128)(2,1)S(1)} %get-tuple-element.64), channel_id=1, source_target_pairs={{0,3},{1,2},{2,1},{3,0},{4,7},{5,6},{6,5},{7,4},{8,11},{9,10},{10,... | collective-permute-start | bytes 73736 | tf_op jit(solution)/shard_map/ppermute | solution.py:417
  29.1 1.3 %shard_map.60.acc_ref = f32[768,128]{1,0:T(8,128)S(1)} custom-call(bf16[768,128]{1,0:T(8,128)(2,1)S(1)} %get-tuple-element.62.f_ref.refs_0_, bf16[1152,128]{1,0:T(8,128)(2,1)S(1)} %bitcast.19, bf16[768,128]{1,0:T(8,128)(2,1)S(1)} %get-tuple-element.54.f_ref.refs_0_.refs_2_, bf16[1152,128]{1,0:T(8,128)(2,1)S(1)} %bitcast.29), custom_call_target="tpu_custom_call" | custom-call | flops 8000000 | bytes 2097152 | tf_op jit(solution)/shard_map/pallas_call | solution.py:402
  30.4 0.0 collective-permute-done.12.x_near
  30.4 0.4 %collective-permute-done.13.x_far = bf16[96,128]{1,0:T(8,128)(2,1)S(1)} collective-permute-done((bf16[96,128]{1,0:T(8,128)(2,1)S(1)}, bf16[96,128]{1,0:T(8,128)(2,1)S(1)}, u32[]{:S(2)}, u32[]{:S(2)}) %collective-permute-start.13) | collective-permute-done | bytes 24608 | tf_op jit(solution)/shard_map/ppermute | solution.py:417
  30.8 0.1 shard_map.61.acc_ref
  30.9 0.4 %collective-permute-done.15.t_two = bf16[192,128]{1,0:T(8,128)(2,1)S(1)} collective-permute-done((bf16[192,128]{1,0:T(8,128)(2,1)S(1)}, bf16[192,128]{1,0:T(8,128)(2,1)S(1)}, u32[]{:S(2)}, u32[]{:S(2)}) %collective-permute-start.15) | collective-permute-done | bytes 49184 | tf_op jit(solution)/shard_map/ppermute | solution.py:428
  31.3 0.8 %shard_map.62 = bf16[768,128]{1,0:T(8,128)(2,1)} custom-call(bf16[1152,128]{1,0:T(8,128)(2,1)S(1)} %bitcast.21, f32[768,128]{1,0:T(8,128)S(1)} %shard_map.61.acc_ref, bf16[192,128]{1,0:T(8,128)(2,1)S(1)} %collective-permute-done.14.t_one, bf16[192,128]{1,0:T(8,128)(2,1)S(1)} %collective-permute-done.15.t_two), custom_call_target="tpu_custom_call" | custom-call | flops 1000000 | bytes 2097152 | tf_op jit(solution)/shard_map/pallas_call | solution.py:402
  (9 shorter events, 0.0 us)
Async XLA Ops:
  0.0 6.7 %copy-start = (bf16[4,3,3,2,2,2,4,128]{7,6,5,4,3,2,1,0:T(4,128)(2,1)S(1)}, bf16[4,3,3,2,2,2,4,128]{7,6,5,4,3,2,1,0:T(4,128)(2,1)}, u32[]{:S(2)}) copy-start(bf16[4,3,3,2,2,2,4,128]{7,6,5,4,3,2,1,0:T(4,128)(2,1)} %param.5) | copy-start | bytes 884740
  0.0 6.7 %copy-start.1 = (bf16[4,4,3,2,2,4,128]{6,5,4,3,2,1,0:T(4,128)(2,1)S(1)}, bf16[4,4,3,2,2,4,128]{6,5,4,3,2,1,0:T(4,128)(2,1)}, u32[]{:S(2)}) copy-start(bf16[4,4,3,2,2,4,128]{6,5,4,3,2,1,0:T(4,128)(2,1)} %param.4) | copy-start | bytes 589828
  1.1 9.2 %collective-permute-start.2 = (bf16[192,128]{1,0:T(8,128)(2,1)S(1)}, bf16[192,128]{1,0:T(8,128)(2,1)S(1)}, u32[]{:S(2)}, u32[]{:S(2)}) collective-permute-start(bf16[192,128]{1,0:T(8,128)(2,1)S(1)} %get-tuple-element.41), channel_id=1, source_target_pairs={{0,4},{1,13},{2,6},{3,15},{4,0},{5,9},{6,2},{7,11},{8,12},{9,5},{1... | collective-permute-start | bytes 147464 | tf_op jit(solution)/shard_map/ppermute | solution.py:428
  4.2 6.1 %collective-permute-start.3 = (bf16[192,128]{1,0:T(8,128)(2,1)S(1)}, bf16[192,128]{1,0:T(8,128)(2,1)S(1)}, u32[]{:S(2)}, u32[]{:S(2)}) collective-permute-start(bf16[192,128]{1,0:T(8,128)(2,1)S(1)} %get-tuple-element.42), channel_id=1, source_target_pairs={{0,12},{1,5},{2,14},{3,7},{4,8},{5,1},{6,10},{7,3},{8,4},{9,13},{1... | collective-permute-start | bytes 147464 | tf_op jit(solution)/shard_map/ppermute | solution.py:428
  6.8 2.7 %collective-permute-start = (bf16[96,128]{1,0:T(8,128)(2,1)S(1)}, bf16[96,128]{1,0:T(8,128)(2,1)S(1)}, u32[]{:S(2)}, u32[]{:S(2)}) collective-permute-start(bf16[96,128]{1,0:T(8,128)(2,1)S(1)} %get-tuple-element.39), channel_id=1, source_target_pairs={{0,1},{1,0},{2,3},{3,2},{4,5},{5,4},{6,7},{7,6},{8,9},{9,8},{10,11... | collective-permute-start | bytes 73736 | tf_op jit(solution)/shard_map/ppermute | solution.py:417
  6.9 3.3 %collective-permute-start.1 = (bf16[96,128]{1,0:T(8,128)(2,1)S(1)}, bf16[96,128]{1,0:T(8,128)(2,1)S(1)}, u32[]{:S(2)}, u32[]{:S(2)}) collective-permute-start(bf16[96,128]{1,0:T(8,128)(2,1)S(1)} %get-tuple-element.40), channel_id=1, source_target_pairs={{0,3},{1,2},{2,1},{3,0},{4,7},{5,6},{6,5},{7,4},{8,11},{9,10},{10,... | collective-permute-start | bytes 73736 | tf_op jit(solution)/shard_map/ppermute | solution.py:417
  9.5 1.0 %copy-start.2 = (bf16[2,6,6,2,2,4,128]{6,5,4,3,2,1,0:T(4,128)(2,1)S(1)}, bf16[2,6,6,2,2,4,128]{6,5,4,3,2,1,0:T(4,128)(2,1)}, u32[]{:S(2)}) copy-start(bf16[2,6,6,2,2,4,128]{6,5,4,3,2,1,0:T(4,128)(2,1)} %param.7) | copy-start | bytes 884740
  10.9 4.1 %copy-start.3 = (bf16[2,6,6,2,2,4,128]{6,5,4,3,2,1,0:T(4,128)(2,1)S(1)}, bf16[2,6,6,2,2,4,128]{6,5,4,3,2,1,0:T(4,128)(2,1)}, u32[]{:S(2)}) copy-start(bf16[2,6,6,2,2,4,128]{6,5,4,3,2,1,0:T(4,128)(2,1)} %param.6) | copy-start | bytes 884740
  10.9 5.9 %collective-permute-start.6 = (bf16[192,128]{1,0:T(8,128)(2,1)S(1)}, bf16[192,128]{1,0:T(8,128)(2,1)S(1)}, u32[]{:S(2)}, u32[]{:S(2)}) collective-permute-start(bf16[192,128]{1,0:T(8,128)(2,1)S(1)} %get-tuple-element.49), channel_id=1, source_target_pairs={{0,4},{1,13},{2,6},{3,15},{4,0},{5,9},{6,2},{7,11},{8,12},{9,5},{1... | collective-permute-start | bytes 147464 | tf_op jit(solution)/shard_map/ppermute | solution.py:428
  11.7 5.9 %collective-permute-start.7 = (bf16[192,128]{1,0:T(8,128)(2,1)S(1)}, bf16[192,128]{1,0:T(8,128)(2,1)S(1)}, u32[]{:S(2)}, u32[]{:S(2)}) collective-permute-start(bf16[192,128]{1,0:T(8,128)(2,1)S(1)} %get-tuple-element.50), channel_id=1, source_target_pairs={{0,12},{1,5},{2,14},{3,7},{4,8},{5,1},{6,10},{7,3},{8,4},{9,13},{1... | collective-permute-start | bytes 147464 | tf_op jit(solution)/shard_map/ppermute | solution.py:428
  13.4 3.0 %collective-permute-start.4 = (bf16[96,128]{1,0:T(8,128)(2,1)S(1)}, bf16[96,128]{1,0:T(8,128)(2,1)S(1)}, u32[]{:S(2)}, u32[]{:S(2)}) collective-permute-start(bf16[96,128]{1,0:T(8,128)(2,1)S(1)} %get-tuple-element.47), channel_id=1, source_target_pairs={{0,1},{1,0},{2,3},{3,2},{4,5},{5,4},{6,7},{7,6},{8,9},{9,8},{10,11... | collective-permute-start | bytes 73736 | tf_op jit(solution)/shard_map/ppermute | solution.py:417
  13.4 3.3 %collective-permute-start.5 = (bf16[96,128]{1,0:T(8,128)(2,1)S(1)}, bf16[96,128]{1,0:T(8,128)(2,1)S(1)}, u32[]{:S(2)}, u32[]{:S(2)}) collective-permute-start(bf16[96,128]{1,0:T(8,128)(2,1)S(1)} %get-tuple-element.48), channel_id=1, source_target_pairs={{0,3},{1,2},{2,1},{3,0},{4,7},{5,6},{6,5},{7,4},{8,11},{9,10},{10,... | collective-permute-start | bytes 73736 | tf_op jit(solution)/shard_map/ppermute | solution.py:417
  17.8 6.3 %collective-permute-start.10 = (bf16[192,128]{1,0:T(8,128)(2,1)S(1)}, bf16[192,128]{1,0:T(8,128)(2,1)S(1)}, u32[]{:S(2)}, u32[]{:S(2)}) collective-permute-start(bf16[192,128]{1,0:T(8,128)(2,1)S(1)} %get-tuple-element.57), channel_id=1, source_target_pairs={{0,4},{1,13},{2,6},{3,15},{4,0},{5,9},{6,2},{7,11},{8,12},{9,5},{1... | collective-permute-start | bytes 147464 | tf_op jit(solution)/shard_map/ppermute | solution.py:428
  18.3 5.9 %collective-permute-start.11 = (bf16[192,128]{1,0:T(8,128)(2,1)S(1)}, bf16[192,128]{1,0:T(8,128)(2,1)S(1)}, u32[]{:S(2)}, u32[]{:S(2)}) collective-permute-start(bf16[192,128]{1,0:T(8,128)(2,1)S(1)} %get-tuple-element.58), channel_id=1, source_target_pairs={{0,12},{1,5},{2,14},{3,7},{4,8},{5,1},{6,10},{7,3},{8,4},{9,13},{1... | collective-permute-start | bytes 147464 | tf_op jit(solution)/shard_map/ppermute | solution.py:428
  20.6 2.7 %collective-permute-start.8 = (bf16[96,128]{1,0:T(8,128)(2,1)S(1)}, bf16[96,128]{1,0:T(8,128)(2,1)S(1)}, u32[]{:S(2)}, u32[]{:S(2)}) collective-permute-start(bf16[96,128]{1,0:T(8,128)(2,1)S(1)} %get-tuple-element.55), channel_id=1, source_target_pairs={{0,1},{1,0},{2,3},{3,2},{4,5},{5,4},{6,7},{7,6},{8,9},{9,8},{10,11... | collective-permute-start | bytes 73736 | tf_op jit(solution)/shard_map/ppermute | solution.py:417
  20.7 3.3 %collective-permute-start.9 = (bf16[96,128]{1,0:T(8,128)(2,1)S(1)}, bf16[96,128]{1,0:T(8,128)(2,1)S(1)}, u32[]{:S(2)}, u32[]{:S(2)}) collective-permute-start(bf16[96,128]{1,0:T(8,128)(2,1)S(1)} %get-tuple-element.56), channel_id=1, source_target_pairs={{0,3},{1,2},{2,1},{3,0},{4,7},{5,6},{6,5},{7,4},{8,11},{9,10},{10,... | collective-permute-start | bytes 73736 | tf_op jit(solution)/shard_map/ppermute | solution.py:417
  24.7 6.2 %collective-permute-start.14 = (bf16[192,128]{1,0:T(8,128)(2,1)S(1)}, bf16[192,128]{1,0:T(8,128)(2,1)S(1)}, u32[]{:S(2)}, u32[]{:S(2)}) collective-permute-start(bf16[192,128]{1,0:T(8,128)(2,1)S(1)} %get-tuple-element.65), channel_id=1, source_target_pairs={{0,4},{1,13},{2,6},{3,15},{4,0},{5,9},{6,2},{7,11},{8,12},{9,5},{1... | collective-permute-start | bytes 147464 | tf_op jit(solution)/shard_map/ppermute | solution.py:428
  25.4 5.9 %collective-permute-start.15 = (bf16[192,128]{1,0:T(8,128)(2,1)S(1)}, bf16[192,128]{1,0:T(8,128)(2,1)S(1)}, u32[]{:S(2)}, u32[]{:S(2)}) collective-permute-start(bf16[192,128]{1,0:T(8,128)(2,1)S(1)} %get-tuple-element.66), channel_id=1, source_target_pairs={{0,12},{1,5},{2,14},{3,7},{4,8},{5,1},{6,10},{7,3},{8,4},{9,13},{1... | collective-permute-start | bytes 147464 | tf_op jit(solution)/shard_map/ppermute | solution.py:428
  27.4 3.0 %collective-permute-start.12 = (bf16[96,128]{1,0:T(8,128)(2,1)S(1)}, bf16[96,128]{1,0:T(8,128)(2,1)S(1)}, u32[]{:S(2)}, u32[]{:S(2)}) collective-permute-start(bf16[96,128]{1,0:T(8,128)(2,1)S(1)} %get-tuple-element.63), channel_id=1, source_target_pairs={{0,1},{1,0},{2,3},{3,2},{4,5},{5,4},{6,7},{7,6},{8,9},{9,8},{10,11... | collective-permute-start | bytes 73736 | tf_op jit(solution)/shard_map/ppermute | solution.py:417
  27.5 3.3 %collective-permute-start.13 = (bf16[96,128]{1,0:T(8,128)(2,1)S(1)}, bf16[96,128]{1,0:T(8,128)(2,1)S(1)}, u32[]{:S(2)}, u32[]{:S(2)}) collective-permute-start(bf16[96,128]{1,0:T(8,128)(2,1)S(1)} %get-tuple-element.64), channel_id=1, source_target_pairs={{0,3},{1,2},{2,1},{3,0},{4,7},{5,6},{6,5},{7,4},{8,11},{9,10},{10,... | collective-permute-start | bytes 73736 | tf_op jit(solution)/shard_map/ppermute | solution.py:417

commit v16 on v15

--- a/solution.py
+++ b/solution.py
@@ -169,8 +169,7 @@
             store_pair(t_two, r * 3 + c, either(even, front, rears[c]))
 
 
-def send_x_kernel(parity, f_ref, links_ref, x_near, x_far):
-    even = even_device("gx")
+def send_x_kernel(parity, f_ref, links_ref, x_back, x_ahead):
     _, x_idx = site_masks()
     links = x_edges(load_links(links_ref, 1, parity))
 
@@ -190,8 +189,8 @@
             rears.append([packed([h[j][i] for h in behind for j in (c, c + 3)], 3, -1) for i in range(2)])
         rears = matvec(links, rounded(rears), True)
         for c in range(3):
-            store_pair(x_near, q * 3 + c, either(even, rears[c], fronts[c]))
-            store_pair(x_far, q * 3 + c, either(even, fronts[c], rears[c]))
+            store_pair(x_back, q * 3 + c, fronts[c])
+            store_pair(x_ahead, q * 3 + c, rears[c])
 
 
 def start_kernel(f_hbm, links_hbm, *refs):
@@ -313,17 +312,15 @@
     return out
 
 
-def join_x_kernel(parity, links_ref, acc_ref, x_near, x_far, out_ref):
-    even = even_device("gx")
+def join_x_kernel(parity, links_ref, acc_ref, from_next, from_last, out_ref):
     _, x_idx = site_masks()
     sign = jnp.where(x_idx == 3, -1.0, 1.0).astype(F32)
     links = x_edges(load_links(links_ref, 1, 1 - parity))
     for q in range(RHS // 2):
         nxt, last = [], []
         for c in range(3):
-            near, far = load_pair(x_near, q * 3 + c), load_pair(x_far, q * 3 + c)
-            nxt.append(either(even, near, far))
-            last.append(either(even, far, near))
+            nxt.append(load_pair(from_next, q * 3 + c))
+            last.append(load_pair(from_last, q * 3 + c))
         ahead = matvec(links, nxt, False)
         for r in (2 * q, 2 * q + 1):
             half = [None] * 6
@@ -410,11 +407,9 @@
     )(*args)
 
 
-def swap(value, axis, far):
+def shift(value, axis, step):
     count = lax.axis_size(axis)
-    assert count % 2 == 0
-    pairs = [(i, (i + (1 if (i % 2 == 0) != far else -1)) % count) for i in range(count)]
-    return lax.ppermute(value, axis, pairs)
+    return lax.ppermute(value, axis, [(i, (i + step) % count) for i in range(count)])
 
 
 def swap_t(value, ahead):
@@ -444,17 +439,17 @@
     for hop in range(4):
         parity = hop % 2
         t_one, t_two = swap_t(t_one, True), swap_t(t_two, False)
-        x_near, x_far = call(
+        x_back, x_ahead = call(
             functools.partial(send_x_kernel, parity), (f, links), X_HALOS, 1_500_000
         )
-        here, x_near, x_far = lax.optimization_barrier((f, x_near, x_far))
-        x_near, x_far = swap(x_near, "gx", False), swap(x_far, "gx", True)
+        here, x_back, x_ahead = lax.optimization_barrier((f, x_back, x_ahead))
+        x_back, x_ahead = shift(x_back, "gx", -1), shift(x_ahead, "gx", 1)
         base = (before, even) if parity else ()
         acc, = call(
             functools.partial(interior_kernel, parity, bool(parity)),
             (here, links, *base), SUM, 8_000_000 if parity else 5_000_000,
         )
-        acc, = call(functools.partial(join_x_kernel, parity), (links, acc, x_near, x_far), SUM, 1_000_000)
+        acc, = call(functools.partial(join_x_kernel, parity), (links, acc, x_back, x_ahead), SUM, 1_000_000)
         before = f
         if parity == 0:
             f, t_one, t_two = call(

time: 32.3 us -> 33.1 us (1.025)
  waiting for transfers between devices: 3.54 us -> 10.1 us
  starting transfers between devices: 19.9 us -> 14.2 us
    ppermute x8, waiting for transfers between devices: 2.27 us -> 7.15 us  [shift(): lax.ppermute(value, axis, [(i, (i + step) % count) for i in range(count)])]
    ppermute x8, starting transfers between devices: 6.71 us -> 2.22 us  [shift(): lax.ppermute(value, axis, [(i, (i + step) % count) for i in range(count)])]
    ppermute x8, waiting for transfers between devices: 1.27 us -> 2.99 us  [swap_t(): return lax.ppermute(value, ('ta', 'gx'), pairs)]
    ppermute x8, starting transfers between devices: 13.2 us -> 12 us  [swap_t(): return lax.ppermute(value, ('ta', 'gx'), pairs)]
  transfers between devices with their start and end apart: 16 -> 16, of which waited for: 7 -> 8; matrix products, arithmetic and copies ran while one was open for 0% -> 0% of each run, Pallas kernels for 16% -> 16%
where the time goes in v16:
time: 33.1 us; the launch traced here: 32.9 us
  starting transfers between devices  14.2 us (43%)
  waiting for transfers between devices  10.1 us (31%)
  Pallas kernels  8.34 us (25%)
    ppermute x8, starting transfers between devices, swap_t(): return lax.ppermute(value, ('ta', 'gx'), pairs)  12 us
    pallas_call x17, Pallas kernels, call(): pl.pallas_call(kernel, out_shape=tuple((jax.ShapeDtypeStruct(shape, dtype...  8.34 us
    ppermute x8, waiting for transfers between devices, shift(): lax.ppermute(value, axis, [(i, (i + step) % count) for i in range(count)])  7.15 us
    ppermute x8, waiting for transfers between devices, swap_t(): return lax.ppermute(value, ('ta', 'gx'), pairs)  2.99 us
    ppermute x8, starting transfers between devices, shift(): lax.ppermute(value, axis, [(i, (i + step) % count) for i in range(count)])  2.22 us
  transfers between devices with their start and end apart: 16, of which 8 were waited for; matrix products, arithmetic and copies ran while one was open for 0% of the time, Pallas kernels for 16%

profile of v16, /device:TPU:0, one launch (start us, length us, event | category | flops | bytes accessed | tf_op | source)
XLA Modules:
  0.0 32.9 jit_solution(12813670376164283748)
XLA Ops:
  0.0 1.1 %shard_map.49 = (bf16[192,128]{1,0:T(8,128)(2,1)S(1)}, bf16[192,128]{1,0:T(8,128)(2,1)S(1)}) custom-call(bf16[768,128]{1,0:T(8,128)(2,1)} %bitcast.22, bf16[1152,128]{1,0:T(8,128)(2,1)} %bitcast.5), custom_call_target="tpu_custom_call" | custom-call | flops 1500000 | bytes 2097152 | tf_op jit(solution)/shard_map/pallas_call | solution.py:399
  1.1 3.1 %collective-permute-start.2 = (bf16[192,128]{1,0:T(8,128)(2,1)S(1)}, bf16[192,128]{1,0:T(8,128)(2,1)S(1)}, u32[]{:S(2)}, u32[]{:S(2)}) collective-permute-start(bf16[192,128]{1,0:T(8,128)(2,1)S(1)} %get-tuple-element.41), channel_id=1, source_target_pairs={{0,4},{1,13},{2,6},{3,15},{4,0},{5,9},{6,2},{7,11},{8,12},{9,5},{1... | collective-permute-start | bytes 147464 | tf_op jit(solution)/shard_map/ppermute | solution.py:423
  4.2 2.5 %collective-permute-start.3 = (bf16[192,128]{1,0:T(8,128)(2,1)S(1)}, bf16[192,128]{1,0:T(8,128)(2,1)S(1)}, u32[]{:S(2)}, u32[]{:S(2)}) collective-permute-start(bf16[192,128]{1,0:T(8,128)(2,1)S(1)} %get-tuple-element.42), channel_id=1, source_target_pairs={{0,12},{1,5},{2,14},{3,7},{4,8},{5,1},{6,10},{7,3},{8,4},{9,13},{1... | collective-permute-start | bytes 147464 | tf_op jit(solution)/shard_map/ppermute | solution.py:423
  6.7 0.1 shard_map.46
  6.8 0.3 collective-permute-start
  7.1 0.3 collective-permute-start.1
  7.4 1.0 %shard_map.47.acc_ref = f32[768,128]{1,0:T(8,128)S(1)} custom-call(bf16[768,128]{1,0:T(8,128)(2,1)S(1)} %bitcast.24, bf16[1152,128]{1,0:T(8,128)(2,1)S(1)} %bitcast.7), custom_call_target="tpu_custom_call" | custom-call | flops 5000000 | bytes 2097152 | tf_op jit(solution)/shard_map/pallas_call | solution.py:399
  8.3 0.0 copy-start.2
  8.3 0.2 collective-permute-done.from_next
  8.6 1.8 %collective-permute-done.1.from_last = bf16[96,128]{1,0:T(8,128)(2,1)S(1)} collective-permute-done((bf16[96,128]{1,0:T(8,128)(2,1)S(1)}, bf16[96,128]{1,0:T(8,128)(2,1)S(1)}, u32[]{:S(2)}, u32[]{:S(2)}) %collective-permute-start.1) | collective-permute-done | bytes 24608 | tf_op jit(solution)/shard_map/ppermute | solution.py:412
  10.4 0.1 shard_map.48.acc_ref
  10.5 0.0 collective-permute-done.2.t_one
  10.5 0.5 %shard_map.50 = (bf16[768,128]{1,0:T(8,128)(2,1)S(1)}, bf16[192,128]{1,0:T(8,128)(2,1)S(1)}, bf16[192,128]{1,0:T(8,128)(2,1)S(1)}) custom-call(bf16[1152,128]{1,0:T(8,128)(2,1)S(1)} %bitcast.9, bf16[1152,128]{1,0:T(8,128)(2,1)S(1)} %bitcast.26, f32[768,128]{1,0:T(8,128)S(1)} %shard_map.48.acc_ref, bf16[192,128]{1,0:T(8,128)(2,1)S(1)} %collective-permute-done.2.t_one, ...), custom_call_target="tpu_custom_call" | custom-call | flops 4000000 | bytes 2097152 | tf_op jit(solution)/shard_map/pallas_call | solution.py:399
  11.0 0.0 copy-start.3
  11.1 1.7 %collective-permute-start.6 = (bf16[192,128]{1,0:T(8,128)(2,1)S(1)}, bf16[192,128]{1,0:T(8,128)(2,1)S(1)}, u32[]{:S(2)}, u32[]{:S(2)}) collective-permute-start(bf16[192,128]{1,0:T(8,128)(2,1)S(1)} %get-tuple-element.49), channel_id=1, source_target_pairs={{0,4},{1,13},{2,6},{3,15},{4,0},{5,9},{6,2},{7,11},{8,12},{9,5},{1... | collective-permute-start | bytes 147464 | tf_op jit(solution)/shard_map/ppermute | solution.py:423
  12.8 0.5 %collective-permute-start.7 = (bf16[192,128]{1,0:T(8,128)(2,1)S(1)}, bf16[192,128]{1,0:T(8,128)(2,1)S(1)}, u32[]{:S(2)}, u32[]{:S(2)}) collective-permute-start(bf16[192,128]{1,0:T(8,128)(2,1)S(1)} %get-tuple-element.50), channel_id=1, source_target_pairs={{0,12},{1,5},{2,14},{3,7},{4,8},{5,1},{6,10},{7,3},{8,4},{9,13},{1... | collective-permute-start | bytes 147464 | tf_op jit(solution)/shard_map/ppermute | solution.py:423
  13.3 0.1 shard_map.51
  13.4 0.1 collective-permute-start.4
  13.4 0.5 %collective-permute-start.5 = (bf16[96,128]{1,0:T(8,128)(2,1)S(1)}, bf16[96,128]{1,0:T(8,128)(2,1)S(1)}, u32[]{:S(2)}, u32[]{:S(2)}) collective-permute-start(bf16[96,128]{1,0:T(8,128)(2,1)S(1)} %get-tuple-element.48), channel_id=1, source_target_pairs={{0,1},{1,2},{2,3},{3,0},{4,5},{5,6},{6,7},{7,4},{8,9},{9,10},{10,1... | collective-permute-start | bytes 73736 | tf_op jit(solution)/shard_map/ppermute | solution.py:412
  13.9 1.3 %shard_map.52.acc_ref = f32[768,128]{1,0:T(8,128)S(1)} custom-call(bf16[768,128]{1,0:T(8,128)(2,1)S(1)} %get-tuple-element.46.f_ref.refs_0_, bf16[1152,128]{1,0:T(8,128)(2,1)S(1)} %bitcast.11, bf16[768,128]{1,0:T(8,128)(2,1)S(1)} %bitcast.25, bf16[1152,128]{1,0:T(8,128)(2,1)S(1)} %bitcast.28), custom_call_target="tpu_custom_call" | custom-call | flops 8000000 | bytes 2097152 | tf_op jit(solution)/shard_map/pallas_call | solution.py:399
  15.2 0.0 collective-permute-done.4.from_next
  15.2 1.7 %collective-permute-done.5.from_last = bf16[96,128]{1,0:T(8,128)(2,1)S(1)} collective-permute-done((bf16[96,128]{1,0:T(8,128)(2,1)S(1)}, bf16[96,128]{1,0:T(8,128)(2,1)S(1)}, u32[]{:S(2)}, u32[]{:S(2)}) %collective-permute-start.5) | collective-permute-done | bytes 24608 | tf_op jit(solution)/shard_map/ppermute | solution.py:412
  17.0 0.1 shard_map.53.acc_ref
  17.1 1.6 %collective-permute-done.7.t_two = bf16[192,128]{1,0:T(8,128)(2,1)S(1)} collective-permute-done((bf16[192,128]{1,0:T(8,128)(2,1)S(1)}, bf16[192,128]{1,0:T(8,128)(2,1)S(1)}, u32[]{:S(2)}, u32[]{:S(2)}) %collective-permute-start.7) | collective-permute-done | bytes 49184 | tf_op jit(solution)/shard_map/ppermute | solution.py:423
  18.7 0.2 shard_map.54
  18.9 0.1 collective-permute-start.10
  18.9 1.7 %collective-permute-start.11 = (bf16[192,128]{1,0:T(8,128)(2,1)S(1)}, bf16[192,128]{1,0:T(8,128)(2,1)S(1)}, u32[]{:S(2)}, u32[]{:S(2)}) collective-permute-start(bf16[192,128]{1,0:T(8,128)(2,1)S(1)} %get-tuple-element.58), channel_id=1, source_target_pairs={{0,12},{1,5},{2,14},{3,7},{4,8},{5,1},{6,10},{7,3},{8,4},{9,13},{1... | collective-permute-start | bytes 147464 | tf_op jit(solution)/shard_map/ppermute | solution.py:423
  20.6 0.1 shard_map.55
  20.7 0.1 collective-permute-start.8
  20.8 0.5 %collective-permute-start.9 = (bf16[96,128]{1,0:T(8,128)(2,1)S(1)}, bf16[96,128]{1,0:T(8,128)(2,1)S(1)}, u32[]{:S(2)}, u32[]{:S(2)}) collective-permute-start(bf16[96,128]{1,0:T(8,128)(2,1)S(1)} %get-tuple-element.56), channel_id=1, source_target_pairs={{0,1},{1,2},{2,3},{3,0},{4,5},{5,6},{6,7},{7,4},{8,9},{9,10},{10,1... | collective-permute-start | bytes 73736 | tf_op jit(solution)/shard_map/ppermute | solution.py:412
  21.3 1.0 %shard_map.56.acc_ref = f32[768,128]{1,0:T(8,128)S(1)} custom-call(bf16[768,128]{1,0:T(8,128)(2,1)S(1)} %get-tuple-element.54.f_ref.refs_0_.refs_2_, bf16[1152,128]{1,0:T(8,128)(2,1)S(1)} %bitcast.15), custom_call_target="tpu_custom_call" | custom-call | flops 5000000 | bytes 2097152 | tf_op jit(solution)/shard_map/pallas_call | solution.py:399
  22.2 0.0 collective-permute-done.8.from_next
  22.3 1.8 %collective-permute-done.9.from_last = bf16[96,128]{1,0:T(8,128)(2,1)S(1)} collective-permute-done((bf16[96,128]{1,0:T(8,128)(2,1)S(1)}, bf16[96,128]{1,0:T(8,128)(2,1)S(1)}, u32[]{:S(2)}, u32[]{:S(2)}) %collective-permute-start.9) | collective-permute-done | bytes 24608 | tf_op jit(solution)/shard_map/ppermute | solution.py:412
  24.1 0.1 shard_map.57.acc_ref
  24.2 0.0 collective-permute-done.10.t_one
  24.2 0.8 %collective-permute-done.11.t_two = bf16[192,128]{1,0:T(8,128)(2,1)S(1)} collective-permute-done((bf16[192,128]{1,0:T(8,128)(2,1)S(1)}, bf16[192,128]{1,0:T(8,128)(2,1)S(1)}, u32[]{:S(2)}, u32[]{:S(2)}) %collective-permute-start.11) | collective-permute-done | bytes 49184 | tf_op jit(solution)/shard_map/ppermute | solution.py:423
  25.0 0.5 %shard_map.58 = (bf16[768,128]{1,0:T(8,128)(2,1)S(1)}, bf16[192,128]{1,0:T(8,128)(2,1)S(1)}, bf16[192,128]{1,0:T(8,128)(2,1)S(1)}) custom-call(bf16[1152,128]{1,0:T(8,128)(2,1)S(1)} %bitcast.17, bf16[1152,128]{1,0:T(8,128)(2,1)S(1)} %bitcast.27, f32[768,128]{1,0:T(8,128)S(1)} %shard_map.57.acc_ref, bf16[192,128]{1,0:T(8,128)(2,1)S(1)} %collective-permute-done.10.t_one, ...), custom_call_target="tpu_custom_call" | custom-call | flops 4000000 | bytes 2097152 | tf_op jit(solution)/shard_map/pallas_call | solution.py:399
  25.5 0.8 %collective-permute-start.14 = (bf16[192,128]{1,0:T(8,128)(2,1)S(1)}, bf16[192,128]{1,0:T(8,128)(2,1)S(1)}, u32[]{:S(2)}, u32[]{:S(2)}) collective-permute-start(bf16[192,128]{1,0:T(8,128)(2,1)S(1)} %get-tuple-element.65), channel_id=1, source_target_pairs={{0,4},{1,13},{2,6},{3,15},{4,0},{5,9},{6,2},{7,11},{8,12},{9,5},{1... | collective-permute-start | bytes 147464 | tf_op jit(solution)/shard_map/ppermute | solution.py:423
  26.3 1.8 %collective-permute-start.15 = (bf16[192,128]{1,0:T(8,128)(2,1)S(1)}, bf16[192,128]{1,0:T(8,128)(2,1)S(1)}, u32[]{:S(2)}, u32[]{:S(2)}) collective-permute-start(bf16[192,128]{1,0:T(8,128)(2,1)S(1)} %get-tuple-element.66), channel_id=1, source_target_pairs={{0,12},{1,5},{2,14},{3,7},{4,8},{5,1},{6,10},{7,3},{8,4},{9,13},{1... | collective-permute-start | bytes 147464 | tf_op jit(solution)/shard_map/ppermute | solution.py:423
  28.0 0.1 shard_map.59
  28.1 0.1 collective-permute-start.12
  28.2 0.5 %collective-permute-start.13 = (bf16[96,128]{1,0:T(8,128)(2,1)S(1)}, bf16[96,128]{1,0:T(8,128)(2,1)S(1)}, u32[]{:S(2)}, u32[]{:S(2)}) collective-permute-start(bf16[96,128]{1,0:T(8,128)(2,1)S(1)} %get-tuple-element.64), channel_id=1, source_target_pairs={{0,1},{1,2},{2,3},{3,0},{4,5},{5,6},{6,7},{7,4},{8,9},{9,10},{10,1... | collective-permute-start | bytes 73736 | tf_op jit(solution)/shard_map/ppermute | solution.py:412
  28.7 1.3 %shard_map.60.acc_ref = f32[768,128]{1,0:T(8,128)S(1)} custom-call(bf16[768,128]{1,0:T(8,128)(2,1)S(1)} %get-tuple-element.62.f_ref.refs_0_, bf16[1152,128]{1,0:T(8,128)(2,1)S(1)} %bitcast.19, bf16[768,128]{1,0:T(8,128)(2,1)S(1)} %get-tuple-element.54.f_ref.refs_0_.refs_2_, bf16[1152,128]{1,0:T(8,128)(2,1)S(1)} %bitcast.29), custom_call_target="tpu_custom_call" | custom-call | flops 8000000 | bytes 2097152 | tf_op jit(solution)/shard_map/pallas_call | solution.py:399
  30.0 0.0 collective-permute-done.12.from_next
  30.0 1.5 %collective-permute-done.13.from_last = bf16[96,128]{1,0:T(8,128)(2,1)S(1)} collective-permute-done((bf16[96,128]{1,0:T(8,128)(2,1)S(1)}, bf16[96,128]{1,0:T(8,128)(2,1)S(1)}, u32[]{:S(2)}, u32[]{:S(2)}) %collective-permute-start.13) | collective-permute-done | bytes 24608 | tf_op jit(solution)/shard_map/ppermute | solution.py:412
  31.5 0.1 shard_map.61.acc_ref
  31.6 0.6 %collective-permute-done.15.t_two = bf16[192,128]{1,0:T(8,128)(2,1)S(1)} collective-permute-done((bf16[192,128]{1,0:T(8,128)(2,1)S(1)}, bf16[192,128]{1,0:T(8,128)(2,1)S(1)}, u32[]{:S(2)}, u32[]{:S(2)}) %collective-permute-start.15) | collective-permute-done | bytes 49184 | tf_op jit(solution)/shard_map/ppermute | solution.py:423
  32.2 0.8 %shard_map.62 = bf16[768,128]{1,0:T(8,128)(2,1)} custom-call(bf16[1152,128]{1,0:T(8,128)(2,1)S(1)} %bitcast.21, f32[768,128]{1,0:T(8,128)S(1)} %shard_map.61.acc_ref, bf16[192,128]{1,0:T(8,128)(2,1)S(1)} %collective-permute-done.14.t_one, bf16[192,128]{1,0:T(8,128)(2,1)S(1)} %collective-permute-done.15.t_two), custom_call_target="tpu_custom_call" | custom-call | flops 1000000 | bytes 2097152 | tf_op jit(solution)/shard_map/pallas_call | solution.py:399
  (9 shorter events, 0.0 us)
Async XLA Ops:
  0.0 6.7 %copy-start = (bf16[4,3,3,2,2,2,4,128]{7,6,5,4,3,2,1,0:T(4,128)(2,1)S(1)}, bf16[4,3,3,2,2,2,4,128]{7,6,5,4,3,2,1,0:T(4,128)(2,1)}, u32[]{:S(2)}) copy-start(bf16[4,3,3,2,2,2,4,128]{7,6,5,4,3,2,1,0:T(4,128)(2,1)} %param.5) | copy-start | bytes 884740
  0.0 6.7 %copy-start.1 = (bf16[4,4,3,2,2,4,128]{6,5,4,3,2,1,0:T(4,128)(2,1)S(1)}, bf16[4,4,3,2,2,4,128]{6,5,4,3,2,1,0:T(4,128)(2,1)}, u32[]{:S(2)}) copy-start(bf16[4,4,3,2,2,4,128]{6,5,4,3,2,1,0:T(4,128)(2,1)} %param.4) | copy-start | bytes 589828
  1.1 9.4 %collective-permute-start.2 = (bf16[192,128]{1,0:T(8,128)(2,1)S(1)}, bf16[192,128]{1,0:T(8,128)(2,1)S(1)}, u32[]{:S(2)}, u32[]{:S(2)}) collective-permute-start(bf16[192,128]{1,0:T(8,128)(2,1)S(1)} %get-tuple-element.41), channel_id=1, source_target_pairs={{0,4},{1,13},{2,6},{3,15},{4,0},{5,9},{6,2},{7,11},{8,12},{9,5},{1... | collective-permute-start | bytes 147464 | tf_op jit(solution)/shard_map/ppermute | solution.py:423
  4.2 6.3 %collective-permute-start.3 = (bf16[192,128]{1,0:T(8,128)(2,1)S(1)}, bf16[192,128]{1,0:T(8,128)(2,1)S(1)}, u32[]{:S(2)}, u32[]{:S(2)}) collective-permute-start(bf16[192,128]{1,0:T(8,128)(2,1)S(1)} %get-tuple-element.42), channel_id=1, source_target_pairs={{0,12},{1,5},{2,14},{3,7},{4,8},{5,1},{6,10},{7,3},{8,4},{9,13},{1... | collective-permute-start | bytes 147464 | tf_op jit(solution)/shard_map/ppermute | solution.py:423
  6.8 1.8 %collective-permute-start = (bf16[96,128]{1,0:T(8,128)(2,1)S(1)}, bf16[96,128]{1,0:T(8,128)(2,1)S(1)}, u32[]{:S(2)}, u32[]{:S(2)}) collective-permute-start(bf16[96,128]{1,0:T(8,128)(2,1)S(1)} %get-tuple-element.39), channel_id=1, source_target_pairs={{0,3},{1,0},{2,1},{3,2},{4,7},{5,4},{6,5},{7,6},{8,11},{9,8},{10,9... | collective-permute-start | bytes 73736 | tf_op jit(solution)/shard_map/ppermute | solution.py:412
  7.1 3.3 %collective-permute-start.1 = (bf16[96,128]{1,0:T(8,128)(2,1)S(1)}, bf16[96,128]{1,0:T(8,128)(2,1)S(1)}, u32[]{:S(2)}, u32[]{:S(2)}) collective-permute-start(bf16[96,128]{1,0:T(8,128)(2,1)S(1)} %get-tuple-element.40), channel_id=1, source_target_pairs={{0,1},{1,2},{2,3},{3,0},{4,5},{5,6},{6,7},{7,4},{8,9},{9,10},{10,1... | collective-permute-start | bytes 73736 | tf_op jit(solution)/shard_map/ppermute | solution.py:412
  8.3 2.2 %copy-start.2 = (bf16[2,6,6,2,2,4,128]{6,5,4,3,2,1,0:T(4,128)(2,1)S(1)}, bf16[2,6,6,2,2,4,128]{6,5,4,3,2,1,0:T(4,128)(2,1)}, u32[]{:S(2)}) copy-start(bf16[2,6,6,2,2,4,128]{6,5,4,3,2,1,0:T(4,128)(2,1)} %param.7) | copy-start | bytes 884740
  11.0 2.9 %copy-start.3 = (bf16[2,6,6,2,2,4,128]{6,5,4,3,2,1,0:T(4,128)(2,1)S(1)}, bf16[2,6,6,2,2,4,128]{6,5,4,3,2,1,0:T(4,128)(2,1)}, u32[]{:S(2)}) copy-start(bf16[2,6,6,2,2,4,128]{6,5,4,3,2,1,0:T(4,128)(2,1)} %param.6) | copy-start | bytes 884740
  11.1 6.0 %collective-permute-start.6 = (bf16[192,128]{1,0:T(8,128)(2,1)S(1)}, bf16[192,128]{1,0:T(8,128)(2,1)S(1)}, u32[]{:S(2)}, u32[]{:S(2)}) collective-permute-start(bf16[192,128]{1,0:T(8,128)(2,1)S(1)} %get-tuple-element.49), channel_id=1, source_target_pairs={{0,4},{1,13},{2,6},{3,15},{4,0},{5,9},{6,2},{7,11},{8,12},{9,5},{1... | collective-permute-start | bytes 147464 | tf_op jit(solution)/shard_map/ppermute | solution.py:423
  12.8 5.9 %collective-permute-start.7 = (bf16[192,128]{1,0:T(8,128)(2,1)S(1)}, bf16[192,128]{1,0:T(8,128)(2,1)S(1)}, u32[]{:S(2)}, u32[]{:S(2)}) collective-permute-start(bf16[192,128]{1,0:T(8,128)(2,1)S(1)} %get-tuple-element.50), channel_id=1, source_target_pairs={{0,12},{1,5},{2,14},{3,7},{4,8},{5,1},{6,10},{7,3},{8,4},{9,13},{1... | collective-permute-start | bytes 147464 | tf_op jit(solution)/shard_map/ppermute | solution.py:423
  13.4 1.9 %collective-permute-start.4 = (bf16[96,128]{1,0:T(8,128)(2,1)S(1)}, bf16[96,128]{1,0:T(8,128)(2,1)S(1)}, u32[]{:S(2)}, u32[]{:S(2)}) collective-permute-start(bf16[96,128]{1,0:T(8,128)(2,1)S(1)} %get-tuple-element.47), channel_id=1, source_target_pairs={{0,3},{1,0},{2,1},{3,2},{4,7},{5,4},{6,5},{7,6},{8,11},{9,8},{10,9... | collective-permute-start | bytes 73736 | tf_op jit(solution)/shard_map/ppermute | solution.py:412
  13.4 3.5 %collective-permute-start.5 = (bf16[96,128]{1,0:T(8,128)(2,1)S(1)}, bf16[96,128]{1,0:T(8,128)(2,1)S(1)}, u32[]{:S(2)}, u32[]{:S(2)}) collective-permute-start(bf16[96,128]{1,0:T(8,128)(2,1)S(1)} %get-tuple-element.48), channel_id=1, source_target_pairs={{0,1},{1,2},{2,3},{3,0},{4,5},{5,6},{6,7},{7,4},{8,9},{9,10},{10,1... | collective-permute-start | bytes 73736 | tf_op jit(solution)/shard_map/ppermute | solution.py:412
  18.9 5.3 %collective-permute-start.10 = (bf16[192,128]{1,0:T(8,128)(2,1)S(1)}, bf16[192,128]{1,0:T(8,128)(2,1)S(1)}, u32[]{:S(2)}, u32[]{:S(2)}) collective-permute-start(bf16[192,128]{1,0:T(8,128)(2,1)S(1)} %get-tuple-element.57), channel_id=1, source_target_pairs={{0,4},{1,13},{2,6},{3,15},{4,0},{5,9},{6,2},{7,11},{8,12},{9,5},{1... | collective-permute-start | bytes 147464 | tf_op jit(solution)/shard_map/ppermute | solution.py:423
  18.9 6.1 %collective-permute-start.11 = (bf16[192,128]{1,0:T(8,128)(2,1)S(1)}, bf16[192,128]{1,0:T(8,128)(2,1)S(1)}, u32[]{:S(2)}, u32[]{:S(2)}) collective-permute-start(bf16[192,128]{1,0:T(8,128)(2,1)S(1)} %get-tuple-element.58), channel_id=1, source_target_pairs={{0,12},{1,5},{2,14},{3,7},{4,8},{5,1},{6,10},{7,3},{8,4},{9,13},{1... | collective-permute-start | bytes 147464 | tf_op jit(solution)/shard_map/ppermute | solution.py:423
  20.7 1.6 %collective-permute-start.8 = (bf16[96,128]{1,0:T(8,128)(2,1)S(1)}, bf16[96,128]{1,0:T(8,128)(2,1)S(1)}, u32[]{:S(2)}, u32[]{:S(2)}) collective-permute-start(bf16[96,128]{1,0:T(8,128)(2,1)S(1)} %get-tuple-element.55), channel_id=1, source_target_pairs={{0,3},{1,0},{2,1},{3,2},{4,7},{5,4},{6,5},{7,6},{8,11},{9,8},{10,9... | collective-permute-start | bytes 73736 | tf_op jit(solution)/shard_map/ppermute | solution.py:412
  20.8 3.3 %collective-permute-start.9 = (bf16[96,128]{1,0:T(8,128)(2,1)S(1)}, bf16[96,128]{1,0:T(8,128)(2,1)S(1)}, u32[]{:S(2)}, u32[]{:S(2)}) collective-permute-start(bf16[96,128]{1,0:T(8,128)(2,1)S(1)} %get-tuple-element.56), channel_id=1, source_target_pairs={{0,1},{1,2},{2,3},{3,0},{4,5},{5,6},{6,7},{7,4},{8,9},{9,10},{10,1... | collective-permute-start | bytes 73736 | tf_op jit(solution)/shard_map/ppermute | solution.py:412
  25.5 6.1 %collective-permute-start.14 = (bf16[192,128]{1,0:T(8,128)(2,1)S(1)}, bf16[192,128]{1,0:T(8,128)(2,1)S(1)}, u32[]{:S(2)}, u32[]{:S(2)}) collective-permute-start(bf16[192,128]{1,0:T(8,128)(2,1)S(1)} %get-tuple-element.65), channel_id=1, source_target_pairs={{0,4},{1,13},{2,6},{3,15},{4,0},{5,9},{6,2},{7,11},{8,12},{9,5},{1... | collective-permute-start | bytes 147464 | tf_op jit(solution)/shard_map/ppermute | solution.py:423
  26.3 5.9 %collective-permute-start.15 = (bf16[192,128]{1,0:T(8,128)(2,1)S(1)}, bf16[192,128]{1,0:T(8,128)(2,1)S(1)}, u32[]{:S(2)}, u32[]{:S(2)}) collective-permute-start(bf16[192,128]{1,0:T(8,128)(2,1)S(1)} %get-tuple-element.66), channel_id=1, source_target_pairs={{0,12},{1,5},{2,14},{3,7},{4,8},{5,1},{6,10},{7,3},{8,4},{9,13},{1... | collective-permute-start | bytes 147464 | tf_op jit(solution)/shard_map/ppermute | solution.py:423
  28.1 1.9 %collective-permute-start.12 = (bf16[96,128]{1,0:T(8,128)(2,1)S(1)}, bf16[96,128]{1,0:T(8,128)(2,1)S(1)}, u32[]{:S(2)}, u32[]{:S(2)}) collective-permute-start(bf16[96,128]{1,0:T(8,128)(2,1)S(1)} %get-tuple-element.63), channel_id=1, source_target_pairs={{0,3},{1,0},{2,1},{3,2},{4,7},{5,4},{6,5},{7,6},{8,11},{9,8},{10,9... | collective-permute-start | bytes 73736 | tf_op jit(solution)/shard_map/ppermute | solution.py:412
  28.2 3.3 %collective-permute-start.13 = (bf16[96,128]{1,0:T(8,128)(2,1)S(1)}, bf16[96,128]{1,0:T(8,128)(2,1)S(1)}, u32[]{:S(2)}, u32[]{:S(2)}) collective-permute-start(bf16[96,128]{1,0:T(8,128)(2,1)S(1)} %get-tuple-element.64), channel_id=1, source_target_pairs={{0,1},{1,2},{2,3},{3,0},{4,5},{5,6},{6,7},{7,4},{8,9},{9,10},{10,1... | collective-permute-start | bytes 73736 | tf_op jit(solution)/shard_map/ppermute | solution.py:412

commit v17 on v12

--- a/solution.py
+++ b/solution.py
@@ -171,6 +171,8 @@
 
 def send_x(f_ref, links_ref, parity, x_far, x_near):
     even = even_device("gx")
+    pad = x_far.shape[0] - x_near.shape[0]
+    x_far[x_near.shape[0]:, :] = jnp.zeros((pad, 128), BF16)
     _, x_idx = site_masks()
     links = x_edges(load_links(links_ref, 1, parity))
 
@@ -398,7 +400,8 @@
 FIELD = [((ROWS, 128), BF16)]
 SUM = [((ROWS, 128), F32)]
 T_HALOS = [((RHS * 3 * 16, 128), BF16)] * 2
-HALOS = T_HALOS + [((RHS * 3 * 8, 128), BF16)] * 2
+X_ROWS = RHS * 3 * 8
+HALOS = T_HALOS + [((RHS * 3 * 16 + 16, 128), BF16), ((X_ROWS, 128), BF16)]
 
 
 def call(kernel, args, outs, flops, scratch=(), in_space=pltpu.VMEM, out_space=pltpu.VMEM):

time: 32 us -> 34.9 us (1.091)
  waiting for transfers between devices: 4.39 us -> 11.3 us
  starting transfers between devices: 19 us -> 14.8 us
    ppermute x8, waiting for transfers between devices: 1.38 us -> 10.6 us  [swap_t(): return lax.ppermute(value, ('ta', 'gx'), pairs)]
    ppermute x8, starting transfers between devices: 6.36 us -> 3.62 us  [swap(): return lax.ppermute(value, axis, pairs)]
    ppermute x8, waiting for transfers between devices: 3.01 us -> 0.66 us  [swap(): return lax.ppermute(value, axis, pairs)]
    ppermute x8, starting transfers between devices: 12.6 us -> 11.2 us  [swap_t(): return lax.ppermute(value, ('ta', 'gx'), pairs)]
  transfers between devices with their start and end apart: 16 -> 16, of which waited for: 7 -> 9; matrix products, arithmetic and copies ran while one was open for 0% -> 0% of each run, Pallas kernels for 15% -> 14%
where the time goes in v17:
time: 34.9 us; the launch traced here: 34.7 us
  starting transfers between devices  14.8 us (42%)
  waiting for transfers between devices  11.3 us (32%)
  Pallas kernels  8.43 us (24%)
    ppermute x8, starting transfers between devices, swap_t(): return lax.ppermute(value, ('ta', 'gx'), pairs)  11.2 us
    ppermute x8, waiting for transfers between devices, swap_t(): return lax.ppermute(value, ('ta', 'gx'), pairs)  10.6 us
    pallas_call x13, Pallas kernels, call(): pl.pallas_call(kernel, out_shape=tuple((jax.ShapeDtypeStruct(shape, dtype...  8.43 us
    ppermute x8, starting transfers between devices, swap(): return lax.ppermute(value, axis, pairs)  3.62 us
  transfers between devices with their start and end apart: 16, of which 9 were waited for; matrix products, arithmetic and copies ran while one was open for 0% of the time, Pallas kernels for 14%

profile of v17, /device:TPU:0, one launch (start us, length us, event | category | flops | bytes accessed | tf_op | source)
XLA Modules:
  0.0 34.7 jit_solution(4529241047968243310)
XLA Ops:
  0.0 1.2 %shard_map.47 = (bf16[192,128]{1,0:T(8,128)(2,1)S(1)}, bf16[192,128]{1,0:T(8,128)(2,1)S(1)}, bf16[208,128]{1,0:T(8,128)(2,1)S(1)}, bf16[96,128]{1,0:T(8,128)(2,1)S(1)}) custom-call(bf16[768,128]{1,0:T(8,128)(2,1)} %bitcast.18, bf16[1152,128]{1,0:T(8,128)(2,1)} %bitcast.5), custom_call_target="tpu_custom_call" | custom-call | flops 1500000 | bytes 2097152 | tf_op jit(solution)/shard_map/pallas_call | solution.py:408
  1.2 2.4 %collective-permute-start = (bf16[208,128]{1,0:T(8,128)(2,1)S(1)}, bf16[208,128]{1,0:T(8,128)(2,1)S(1)}, u32[]{:S(2)}, u32[]{:S(2)}) collective-permute-start(bf16[208,128]{1,0:T(8,128)(2,1)S(1)} %get-tuple-element.24), channel_id=1, source_target_pairs={{0,3},{1,2},{2,1},{3,0},{4,7},{5,6},{6,5},{7,4},{8,11},{9,10},{10,... | collective-permute-start | bytes 159752 | tf_op jit(solution)/shard_map/ppermute | solution.py:423
  3.7 1.6 %collective-permute-start.2 = (bf16[192,128]{1,0:T(8,128)(2,1)S(1)}, bf16[192,128]{1,0:T(8,128)(2,1)S(1)}, u32[]{:S(2)}, u32[]{:S(2)}) collective-permute-start(bf16[192,128]{1,0:T(8,128)(2,1)S(1)} %get-tuple-element.26), channel_id=1, source_target_pairs={{0,4},{1,13},{2,6},{3,15},{4,0},{5,9},{6,2},{7,11},{8,12},{9,5},{1... | collective-permute-start | bytes 147464 | tf_op jit(solution)/shard_map/ppermute | solution.py:434
  5.3 2.5 %collective-permute-start.3 = (bf16[192,128]{1,0:T(8,128)(2,1)S(1)}, bf16[192,128]{1,0:T(8,128)(2,1)S(1)}, u32[]{:S(2)}, u32[]{:S(2)}) collective-permute-start(bf16[192,128]{1,0:T(8,128)(2,1)S(1)} %get-tuple-element.27), channel_id=1, source_target_pairs={{0,12},{1,5},{2,14},{3,7},{4,8},{5,1},{6,10},{7,3},{8,4},{9,13},{1... | collective-permute-start | bytes 147464 | tf_op jit(solution)/shard_map/ppermute | solution.py:434
  7.7 0.0 collective-permute-start.1
  7.7 0.0 copy-done
  7.7 1.0 %shard_map.46.acc_ref = f32[768,128]{1,0:T(8,128)S(1)} custom-call(bf16[768,128]{1,0:T(8,128)(2,1)S(1)} %bitcast.19, bf16[1152,128]{1,0:T(8,128)(2,1)S(1)} %bitcast.6), custom_call_target="tpu_custom_call" | custom-call | flops 5000000 | bytes 2097152 | tf_op jit(solution)/shard_map/pallas_call | solution.py:408
  8.7 0.0 copy-start.2
  8.7 0.2 collective-permute-done.1.x_near
  8.9 0.0 collective-permute-done.x_far
  8.9 0.1 shard_map.48.acc_ref
  9.0 0.0 collective-permute-done.2.t_one
  9.0 2.2 %collective-permute-done.3.t_two = bf16[192,128]{1,0:T(8,128)(2,1)S(1)} collective-permute-done((bf16[192,128]{1,0:T(8,128)(2,1)S(1)}, bf16[192,128]{1,0:T(8,128)(2,1)S(1)}, u32[]{:S(2)}, u32[]{:S(2)}) %collective-permute-start.3) | collective-permute-done | bytes 49184 | tf_op jit(solution)/shard_map/ppermute | solution.py:434
  11.3 0.6 %shard_map.49 = (bf16[768,128]{1,0:T(8,128)(2,1)S(1)}, bf16[192,128]{1,0:T(8,128)(2,1)S(1)}, bf16[192,128]{1,0:T(8,128)(2,1)S(1)}, bf16[208,128]{1,0:T(8,128)(2,1)S(1)}, bf16[96,128]{1,0:T(8,128)(2,1)S(1)}) custom-call(bf16[1152,128]{1,0:T(8,128)(2,1)S(1)} %bitcast.8, bf16[1152,128]{1,0:T(8,128)(2,1)S(1)} %bitcast.21, f32[768,128]{1,0:T(8,128)S(1)} %shard_map.48.acc_ref, ...), custom_call_target="tpu_custom_call" | custom-call | flops 4000000 | bytes 2097152 | tf_op jit(solution)/shard_map/pallas_call | solution.py:408
  11.9 0.1 collective-permute-start.4
  12.0 0.5 %collective-permute-start.6 = (bf16[192,128]{1,0:T(8,128)(2,1)S(1)}, bf16[192,128]{1,0:T(8,128)(2,1)S(1)}, u32[]{:S(2)}, u32[]{:S(2)}) collective-permute-start(bf16[192,128]{1,0:T(8,128)(2,1)S(1)} %get-tuple-element.31), channel_id=1, source_target_pairs={{0,4},{1,13},{2,6},{3,15},{4,0},{5,9},{6,2},{7,11},{8,12},{9,5},{1... | collective-permute-start | bytes 147464 | tf_op jit(solution)/shard_map/ppermute | solution.py:434
  12.5 2.5 %collective-permute-start.7 = (bf16[192,128]{1,0:T(8,128)(2,1)S(1)}, bf16[192,128]{1,0:T(8,128)(2,1)S(1)}, u32[]{:S(2)}, u32[]{:S(2)}) collective-permute-start(bf16[192,128]{1,0:T(8,128)(2,1)S(1)} %get-tuple-element.32), channel_id=1, source_target_pairs={{0,12},{1,5},{2,14},{3,7},{4,8},{5,1},{6,10},{7,3},{8,4},{9,13},{1... | collective-permute-start | bytes 147464 | tf_op jit(solution)/shard_map/ppermute | solution.py:434
  15.0 0.0 collective-permute-start.5
  15.0 0.0 copy-done.3
  15.0 1.3 %shard_map.50.acc_ref = f32[768,128]{1,0:T(8,128)S(1)} custom-call(bf16[768,128]{1,0:T(8,128)(2,1)S(1)} %get-tuple-element.28.refs_0_, bf16[1152,128]{1,0:T(8,128)(2,1)S(1)} %bitcast.9, bf16[768,128]{1,0:T(8,128)(2,1)S(1)} %bitcast.20, bf16[1152,128]{1,0:T(8,128)(2,1)S(1)} %bitcast.23), custom_call_target="tpu_custom_call" | custom-call | flops 8000000 | bytes 2097152 | tf_op jit(solution)/shard_map/pallas_call | solution.py:408
  16.3 0.0 collective-permute-done.5.x_near
  16.3 0.0 collective-permute-done.4.x_far
  16.3 0.1 shard_map.51.acc_ref
  16.4 0.0 collective-permute-done.6.t_one
  16.4 2.2 %collective-permute-done.7.t_two = bf16[192,128]{1,0:T(8,128)(2,1)S(1)} collective-permute-done((bf16[192,128]{1,0:T(8,128)(2,1)S(1)}, bf16[192,128]{1,0:T(8,128)(2,1)S(1)}, u32[]{:S(2)}, u32[]{:S(2)}) %collective-permute-start.7) | collective-permute-done | bytes 49184 | tf_op jit(solution)/shard_map/ppermute | solution.py:434
  18.7 0.3 shard_map.52
  19.0 0.8 %collective-permute-start.8 = (bf16[208,128]{1,0:T(8,128)(2,1)S(1)}, bf16[208,128]{1,0:T(8,128)(2,1)S(1)}, u32[]{:S(2)}, u32[]{:S(2)}) collective-permute-start(bf16[208,128]{1,0:T(8,128)(2,1)S(1)} %get-tuple-element.34), channel_id=1, source_target_pairs={{0,3},{1,2},{2,1},{3,0},{4,7},{5,6},{6,5},{7,4},{8,11},{9,10},{10,... | collective-permute-start | bytes 159752 | tf_op jit(solution)/shard_map/ppermute | solution.py:423
  19.8 0.7 %collective-permute-start.10 = (bf16[192,128]{1,0:T(8,128)(2,1)S(1)}, bf16[192,128]{1,0:T(8,128)(2,1)S(1)}, u32[]{:S(2)}, u32[]{:S(2)}) collective-permute-start(bf16[192,128]{1,0:T(8,128)(2,1)S(1)} %get-tuple-element.36), channel_id=1, source_target_pairs={{0,4},{1,13},{2,6},{3,15},{4,0},{5,9},{6,2},{7,11},{8,12},{9,5},{1... | collective-permute-start | bytes 147464 | tf_op jit(solution)/shard_map/ppermute | solution.py:434
  20.4 1.7 %collective-permute-start.11 = (bf16[192,128]{1,0:T(8,128)(2,1)S(1)}, bf16[192,128]{1,0:T(8,128)(2,1)S(1)}, u32[]{:S(2)}, u32[]{:S(2)}) collective-permute-start(bf16[192,128]{1,0:T(8,128)(2,1)S(1)} %get-tuple-element.37), channel_id=1, source_target_pairs={{0,12},{1,5},{2,14},{3,7},{4,8},{5,1},{6,10},{7,3},{8,4},{9,13},{1... | collective-permute-start | bytes 147464 | tf_op jit(solution)/shard_map/ppermute | solution.py:434
  22.1 0.0 collective-permute-start.9
  22.1 1.0 %shard_map.53.acc_ref = f32[768,128]{1,0:T(8,128)S(1)} custom-call(bf16[768,128]{1,0:T(8,128)(2,1)S(1)} %get-tuple-element.33.refs_0_.refs_2_, bf16[1152,128]{1,0:T(8,128)(2,1)S(1)} %bitcast.12), custom_call_target="tpu_custom_call" | custom-call | flops 5000000 | bytes 2097152 | tf_op jit(solution)/shard_map/pallas_call | solution.py:408
  23.1 0.2 collective-permute-done.9.x_near
  23.3 0.0 collective-permute-done.8.x_far
  23.3 0.1 shard_map.54.acc_ref
  23.4 0.4 %collective-permute-done.10.t_one = bf16[192,128]{1,0:T(8,128)(2,1)S(1)} collective-permute-done((bf16[192,128]{1,0:T(8,128)(2,1)S(1)}, bf16[192,128]{1,0:T(8,128)(2,1)S(1)}, u32[]{:S(2)}, u32[]{:S(2)}) %collective-permute-start.10) | collective-permute-done | bytes 49184 | tf_op jit(solution)/shard_map/ppermute | solution.py:434
  23.8 2.7 %collective-permute-done.11.t_two = bf16[192,128]{1,0:T(8,128)(2,1)S(1)} collective-permute-done((bf16[192,128]{1,0:T(8,128)(2,1)S(1)}, bf16[192,128]{1,0:T(8,128)(2,1)S(1)}, u32[]{:S(2)}, u32[]{:S(2)}) %collective-permute-start.11) | collective-permute-done | bytes 49184 | tf_op jit(solution)/shard_map/ppermute | solution.py:434
  26.6 0.6 %shard_map.55 = (bf16[768,128]{1,0:T(8,128)(2,1)S(1)}, bf16[192,128]{1,0:T(8,128)(2,1)S(1)}, bf16[192,128]{1,0:T(8,128)(2,1)S(1)}, bf16[208,128]{1,0:T(8,128)(2,1)S(1)}, bf16[96,128]{1,0:T(8,128)(2,1)S(1)}) custom-call(bf16[1152,128]{1,0:T(8,128)(2,1)S(1)} %bitcast.14, bf16[1152,128]{1,0:T(8,128)(2,1)S(1)} %bitcast.22, f32[768,128]{1,0:T(8,128)S(1)} %shard_map.54.acc_ref, ...), custom_call_target="tpu_custom_call" | custom-call | flops 4000000 | bytes 2097152 | tf_op jit(solution)/shard_map/pallas_call | solution.py:408
  27.2 0.2 collective-permute-start.12
  27.4 0.4 %collective-permute-start.14 = (bf16[192,128]{1,0:T(8,128)(2,1)S(1)}, bf16[192,128]{1,0:T(8,128)(2,1)S(1)}, u32[]{:S(2)}, u32[]{:S(2)}) collective-permute-start(bf16[192,128]{1,0:T(8,128)(2,1)S(1)} %get-tuple-element.41), channel_id=1, source_target_pairs={{0,4},{1,13},{2,6},{3,15},{4,0},{5,9},{6,2},{7,11},{8,12},{9,5},{1... | collective-permute-start | bytes 147464 | tf_op jit(solution)/shard_map/ppermute | solution.py:434
  27.8 1.4 %collective-permute-start.15 = (bf16[192,128]{1,0:T(8,128)(2,1)S(1)}, bf16[192,128]{1,0:T(8,128)(2,1)S(1)}, u32[]{:S(2)}, u32[]{:S(2)}) collective-permute-start(bf16[192,128]{1,0:T(8,128)(2,1)S(1)} %get-tuple-element.42), channel_id=1, source_target_pairs={{0,12},{1,5},{2,14},{3,7},{4,8},{5,1},{6,10},{7,3},{8,4},{9,13},{1... | collective-permute-start | bytes 147464 | tf_op jit(solution)/shard_map/ppermute | solution.py:434
  29.2 0.1 collective-permute-start.13
  29.3 1.3 %shard_map.56.acc_ref = f32[768,128]{1,0:T(8,128)S(1)} custom-call(bf16[768,128]{1,0:T(8,128)(2,1)S(1)} %get-tuple-element.38.refs_0_, bf16[1152,128]{1,0:T(8,128)(2,1)S(1)} %bitcast.15, bf16[768,128]{1,0:T(8,128)(2,1)S(1)} %get-tuple-element.33.refs_0_.refs_2_, bf16[1152,128]{1,0:T(8,128)(2,1)S(1)} %bitcast.24), custom_call_target="tpu_custom_call" | custom-call | flops 8000000 | bytes 2097152 | tf_op jit(solution)/shard_map/pallas_call | solution.py:408
  30.6 0.0 collective-permute-done.13.x_near
  30.6 0.2 collective-permute-done.12.x_far
  30.8 0.1 shard_map.57.acc_ref
  30.9 0.6 %collective-permute-done.14.t_one = bf16[192,128]{1,0:T(8,128)(2,1)S(1)} collective-permute-done((bf16[192,128]{1,0:T(8,128)(2,1)S(1)}, bf16[192,128]{1,0:T(8,128)(2,1)S(1)}, u32[]{:S(2)}, u32[]{:S(2)}) %collective-permute-start.14) | collective-permute-done | bytes 49184 | tf_op jit(solution)/shard_map/ppermute | solution.py:434
  31.5 2.4 %collective-permute-done.15.t_two = bf16[192,128]{1,0:T(8,128)(2,1)S(1)} collective-permute-done((bf16[192,128]{1,0:T(8,128)(2,1)S(1)}, bf16[192,128]{1,0:T(8,128)(2,1)S(1)}, u32[]{:S(2)}, u32[]{:S(2)}) %collective-permute-start.15) | collective-permute-done | bytes 49184 | tf_op jit(solution)/shard_map/ppermute | solution.py:434
  33.9 0.8 %shard_map.58 = bf16[768,128]{1,0:T(8,128)(2,1)} custom-call(bf16[1152,128]{1,0:T(8,128)(2,1)S(1)} %bitcast.17, f32[768,128]{1,0:T(8,128)S(1)} %shard_map.57.acc_ref, bf16[192,128]{1,0:T(8,128)(2,1)S(1)} %collective-permute-done.14.t_one, bf16[192,128]{1,0:T(8,128)(2,1)S(1)} %collective-permute-done.15.t_two), custom_call_target="tpu_custom_call" | custom-call | flops 1000000 | bytes 2097152 | tf_op jit(solution)/shard_map/pallas_call | solution.py:408
  (5 shorter events, 0.0 us)
Async XLA Ops:
  0.0 7.7 %copy-start = (bf16[4,3,3,2,2,2,4,128]{7,6,5,4,3,2,1,0:T(4,128)(2,1)S(1)}, bf16[4,3,3,2,2,2,4,128]{7,6,5,4,3,2,1,0:T(4,128)(2,1)}, u32[]{:S(2)}) copy-start(bf16[4,3,3,2,2,2,4,128]{7,6,5,4,3,2,1,0:T(4,128)(2,1)} %param.5) | copy-start | bytes 884740
  0.0 7.7 %copy-start.1 = (bf16[4,4,3,2,2,4,128]{6,5,4,3,2,1,0:T(4,128)(2,1)S(1)}, bf16[4,4,3,2,2,4,128]{6,5,4,3,2,1,0:T(4,128)(2,1)}, u32[]{:S(2)}) copy-start(bf16[4,4,3,2,2,4,128]{6,5,4,3,2,1,0:T(4,128)(2,1)} %param.4) | copy-start | bytes 589828
  1.2 7.7 %collective-permute-start = (bf16[208,128]{1,0:T(8,128)(2,1)S(1)}, bf16[208,128]{1,0:T(8,128)(2,1)S(1)}, u32[]{:S(2)}, u32[]{:S(2)}) collective-permute-start(bf16[208,128]{1,0:T(8,128)(2,1)S(1)} %get-tuple-element.24), channel_id=1, source_target_pairs={{0,3},{1,2},{2,1},{3,0},{4,7},{5,6},{6,5},{7,4},{8,11},{9,10},{10,... | collective-permute-start | bytes 159752 | tf_op jit(solution)/shard_map/ppermute | solution.py:423
  3.7 5.3 %collective-permute-start.2 = (bf16[192,128]{1,0:T(8,128)(2,1)S(1)}, bf16[192,128]{1,0:T(8,128)(2,1)S(1)}, u32[]{:S(2)}, u32[]{:S(2)}) collective-permute-start(bf16[192,128]{1,0:T(8,128)(2,1)S(1)} %get-tuple-element.26), channel_id=1, source_target_pairs={{0,4},{1,13},{2,6},{3,15},{4,0},{5,9},{6,2},{7,11},{8,12},{9,5},{1... | collective-permute-start | bytes 147464 | tf_op jit(solution)/shard_map/ppermute | solution.py:434
  5.3 6.0 %collective-permute-start.3 = (bf16[192,128]{1,0:T(8,128)(2,1)S(1)}, bf16[192,128]{1,0:T(8,128)(2,1)S(1)}, u32[]{:S(2)}, u32[]{:S(2)}) collective-permute-start(bf16[192,128]{1,0:T(8,128)(2,1)S(1)} %get-tuple-element.27), channel_id=1, source_target_pairs={{0,12},{1,5},{2,14},{3,7},{4,8},{5,1},{6,10},{7,3},{8,4},{9,13},{1... | collective-permute-start | bytes 147464 | tf_op jit(solution)/shard_map/ppermute | solution.py:434
  7.7 1.2 %collective-permute-start.1 = (bf16[96,128]{1,0:T(8,128)(2,1)S(1)}, bf16[96,128]{1,0:T(8,128)(2,1)S(1)}, u32[]{:S(2)}, u32[]{:S(2)}) collective-permute-start(bf16[96,128]{1,0:T(8,128)(2,1)S(1)} %get-tuple-element.25), channel_id=1, source_target_pairs={{0,1},{1,0},{2,3},{3,2},{4,5},{5,4},{6,7},{7,6},{8,9},{9,8},{10,11... | collective-permute-start | bytes 73736 | tf_op jit(solution)/shard_map/ppermute | solution.py:423
  8.7 2.5 %copy-start.2 = (bf16[2,6,6,2,2,4,128]{6,5,4,3,2,1,0:T(4,128)(2,1)S(1)}, bf16[2,6,6,2,2,4,128]{6,5,4,3,2,1,0:T(4,128)(2,1)}, u32[]{:S(2)}) copy-start(bf16[2,6,6,2,2,4,128]{6,5,4,3,2,1,0:T(4,128)(2,1)} %param.7) | copy-start | bytes 884740
  11.3 3.7 %copy-start.3 = (bf16[2,6,6,2,2,4,128]{6,5,4,3,2,1,0:T(4,128)(2,1)S(1)}, bf16[2,6,6,2,2,4,128]{6,5,4,3,2,1,0:T(4,128)(2,1)}, u32[]{:S(2)}) copy-start(bf16[2,6,6,2,2,4,128]{6,5,4,3,2,1,0:T(4,128)(2,1)} %param.6) | copy-start | bytes 884740
  11.9 4.5 %collective-permute-start.4 = (bf16[208,128]{1,0:T(8,128)(2,1)S(1)}, bf16[208,128]{1,0:T(8,128)(2,1)S(1)}, u32[]{:S(2)}, u32[]{:S(2)}) collective-permute-start(bf16[208,128]{1,0:T(8,128)(2,1)S(1)} %get-tuple-element.29), channel_id=1, source_target_pairs={{0,3},{1,2},{2,1},{3,0},{4,7},{5,6},{6,5},{7,4},{8,11},{9,10},{10,... | collective-permute-start | bytes 159752 | tf_op jit(solution)/shard_map/ppermute | solution.py:423
  12.0 4.5 %collective-permute-start.6 = (bf16[192,128]{1,0:T(8,128)(2,1)S(1)}, bf16[192,128]{1,0:T(8,128)(2,1)S(1)}, u32[]{:S(2)}, u32[]{:S(2)}) collective-permute-start(bf16[192,128]{1,0:T(8,128)(2,1)S(1)} %get-tuple-element.31), channel_id=1, source_target_pairs={{0,4},{1,13},{2,6},{3,15},{4,0},{5,9},{6,2},{7,11},{8,12},{9,5},{1... | collective-permute-start | bytes 147464 | tf_op jit(solution)/shard_map/ppermute | solution.py:434
  12.5 6.2 %collective-permute-start.7 = (bf16[192,128]{1,0:T(8,128)(2,1)S(1)}, bf16[192,128]{1,0:T(8,128)(2,1)S(1)}, u32[]{:S(2)}, u32[]{:S(2)}) collective-permute-start(bf16[192,128]{1,0:T(8,128)(2,1)S(1)} %get-tuple-element.32), channel_id=1, source_target_pairs={{0,12},{1,5},{2,14},{3,7},{4,8},{5,1},{6,10},{7,3},{8,4},{9,13},{1... | collective-permute-start | bytes 147464 | tf_op jit(solution)/shard_map/ppermute | solution.py:434
  15.0 1.3 %collective-permute-start.5 = (bf16[96,128]{1,0:T(8,128)(2,1)S(1)}, bf16[96,128]{1,0:T(8,128)(2,1)S(1)}, u32[]{:S(2)}, u32[]{:S(2)}) collective-permute-start(bf16[96,128]{1,0:T(8,128)(2,1)S(1)} %get-tuple-element.30), channel_id=1, source_target_pairs={{0,1},{1,0},{2,3},{3,2},{4,5},{5,4},{6,7},{7,6},{8,9},{9,8},{10,11... | collective-permute-start | bytes 73736 | tf_op jit(solution)/shard_map/ppermute | solution.py:423
  19.0 4.3 %collective-permute-start.8 = (bf16[208,128]{1,0:T(8,128)(2,1)S(1)}, bf16[208,128]{1,0:T(8,128)(2,1)S(1)}, u32[]{:S(2)}, u32[]{:S(2)}) collective-permute-start(bf16[208,128]{1,0:T(8,128)(2,1)S(1)} %get-tuple-element.34), channel_id=1, source_target_pairs={{0,3},{1,2},{2,1},{3,0},{4,7},{5,6},{6,5},{7,4},{8,11},{9,10},{10,... | collective-permute-start | bytes 159752 | tf_op jit(solution)/shard_map/ppermute | solution.py:423
  19.8 4.1 %collective-permute-start.10 = (bf16[192,128]{1,0:T(8,128)(2,1)S(1)}, bf16[192,128]{1,0:T(8,128)(2,1)S(1)}, u32[]{:S(2)}, u32[]{:S(2)}) collective-permute-start(bf16[192,128]{1,0:T(8,128)(2,1)S(1)} %get-tuple-element.36), channel_id=1, source_target_pairs={{0,4},{1,13},{2,6},{3,15},{4,0},{5,9},{6,2},{7,11},{8,12},{9,5},{1... | collective-permute-start | bytes 147464 | tf_op jit(solution)/shard_map/ppermute | solution.py:434
  20.4 6.2 %collective-permute-start.11 = (bf16[192,128]{1,0:T(8,128)(2,1)S(1)}, bf16[192,128]{1,0:T(8,128)(2,1)S(1)}, u32[]{:S(2)}, u32[]{:S(2)}) collective-permute-start(bf16[192,128]{1,0:T(8,128)(2,1)S(1)} %get-tuple-element.37), channel_id=1, source_target_pairs={{0,12},{1,5},{2,14},{3,7},{4,8},{5,1},{6,10},{7,3},{8,4},{9,13},{1... | collective-permute-start | bytes 147464 | tf_op jit(solution)/shard_map/ppermute | solution.py:434
  22.1 1.2 %collective-permute-start.9 = (bf16[96,128]{1,0:T(8,128)(2,1)S(1)}, bf16[96,128]{1,0:T(8,128)(2,1)S(1)}, u32[]{:S(2)}, u32[]{:S(2)}) collective-permute-start(bf16[96,128]{1,0:T(8,128)(2,1)S(1)} %get-tuple-element.35), channel_id=1, source_target_pairs={{0,1},{1,0},{2,3},{3,2},{4,5},{5,4},{6,7},{7,6},{8,9},{9,8},{10,11... | collective-permute-start | bytes 73736 | tf_op jit(solution)/shard_map/ppermute | solution.py:423
  27.2 3.6 %collective-permute-start.12 = (bf16[208,128]{1,0:T(8,128)(2,1)S(1)}, bf16[208,128]{1,0:T(8,128)(2,1)S(1)}, u32[]{:S(2)}, u32[]{:S(2)}) collective-permute-start(bf16[208,128]{1,0:T(8,128)(2,1)S(1)} %get-tuple-element.39), channel_id=1, source_target_pairs={{0,3},{1,2},{2,1},{3,0},{4,7},{5,6},{6,5},{7,4},{8,11},{9,10},{10,... | collective-permute-start | bytes 159752 | tf_op jit(solution)/shard_map/ppermute | solution.py:423
  27.4 4.1 %collective-permute-start.14 = (bf16[192,128]{1,0:T(8,128)(2,1)S(1)}, bf16[192,128]{1,0:T(8,128)(2,1)S(1)}, u32[]{:S(2)}, u32[]{:S(2)}) collective-permute-start(bf16[192,128]{1,0:T(8,128)(2,1)S(1)} %get-tuple-element.41), channel_id=1, source_target_pairs={{0,4},{1,13},{2,6},{3,15},{4,0},{5,9},{6,2},{7,11},{8,12},{9,5},{1... | collective-permute-start | bytes 147464 | tf_op jit(solution)/shard_map/ppermute | solution.py:434
  27.8 6.1 %collective-permute-start.15 = (bf16[192,128]{1,0:T(8,128)(2,1)S(1)}, bf16[192,128]{1,0:T(8,128)(2,1)S(1)}, u32[]{:S(2)}, u32[]{:S(2)}) collective-permute-start(bf16[192,128]{1,0:T(8,128)(2,1)S(1)} %get-tuple-element.42), channel_id=1, source_target_pairs={{0,12},{1,5},{2,14},{3,7},{4,8},{5,1},{6,10},{7,3},{8,4},{9,13},{1... | collective-permute-start | bytes 147464 | tf_op jit(solution)/shard_map/ppermute | solution.py:434
  29.2 1.4 %collective-permute-start.13 = (bf16[96,128]{1,0:T(8,128)(2,1)S(1)}, bf16[96,128]{1,0:T(8,128)(2,1)S(1)}, u32[]{:S(2)}, u32[]{:S(2)}) collective-permute-start(bf16[96,128]{1,0:T(8,128)(2,1)S(1)} %get-tuple-element.40), channel_id=1, source_target_pairs={{0,1},{1,0},{2,3},{3,2},{4,5},{5,4},{6,7},{7,6},{8,9},{9,8},{10,11... | collective-permute-start | bytes 73736 | tf_op jit(solution)/shard_map/ppermute | solution.py:423

commit v18 on v11

--- a/solution.py
+++ b/solution.py
@@ -207,7 +207,12 @@
     send_t(f_ref, links_ref, 0, *outs, ready=lambda r: copies[1 + r].wait())
 
 
-def interior_kernel(parity, with_base, *refs):
+def interior_kernel(parity, with_base, turn, count, *refs):
+    here = True if turn is None else lax.axis_index("gx") % 2 == turn
+    pl.when(here)(lambda: interior(parity, with_base, *refs[:count], refs[-1]))
+
+
+def interior(parity, with_base, *refs):
     if with_base:
         f_ref, links_ref, base_ref, clover_ref, acc_ref = refs
         clover_to(clover_ref, lambda r: load_field(base_ref, r), acc_ref, -1.0 / KAPPA2)
@@ -398,16 +403,17 @@
 X_HALOS = [((RHS * 3 * 8, 128), BF16)] * 2
 
 
-def call(kernel, args, outs, flops, scratch=(), in_space=pltpu.VMEM, out_space=pltpu.VMEM):
+def call(kernel, args, outs, flops, scratch=(), in_space=pltpu.VMEM, out_space=pltpu.VMEM, kept=()):
     return pl.pallas_call(
         kernel,
         out_shape=tuple(jax.ShapeDtypeStruct(shape, dtype) for shape, dtype in outs),
-        in_specs=[pl.BlockSpec(memory_space=in_space)] * len(args),
+        in_specs=[pl.BlockSpec(memory_space=in_space)] * len(args) + [pl.BlockSpec(memory_space=pl.ANY)] * len(kept),
         out_specs=tuple([pl.BlockSpec(memory_space=out_space)] * len(outs)),
         scratch_shapes=list(scratch),
+        input_output_aliases={len(args) + i: i for i in range(len(kept))},
         compiler_params=pltpu.CompilerParams(vmem_limit_bytes=24 * 1024 * 1024),
         cost_estimate=pl.CostEstimate(flops=flops, bytes_accessed=2 * 1024 * 1024, transcendentals=0),
-    )(*args)
+    )(*args, *kept)
 
 
 def swap(value, axis, far):
@@ -443,17 +449,21 @@
     t_one, t_two = call(start_kernel, held, T_HALOS, 1_500_000, start_scratch, in_space=pltpu.HBM)
     for hop in range(4):
         parity = hop % 2
+        base = (before, even) if parity else ()
+        part = functools.partial(interior_kernel, parity, bool(parity))
+        cost = 8_000_000 if parity else 5_000_000
+        count = 2 + len(base)
+        early = ()
+        if hop >= 2:
+            early = call(functools.partial(part, 1, count), (f, links, *base), SUM, cost)
+            t_one, t_two, *early = lax.optimization_barrier((t_one, t_two, *early))
         t_one, t_two = swap_t(t_one, True), swap_t(t_two, False)
         x_far, x_near = call(
             functools.partial(send_x_kernel, parity), (f, links), X_HALOS, 1_500_000
         )
         here, x_far, x_near = lax.optimization_barrier((f, x_far, x_near))
         x_far, x_near = swap(x_far, "gx", True), swap(x_near, "gx", False)
-        base = (before, even) if parity else ()
-        acc, = call(
-            functools.partial(interior_kernel, parity, bool(parity)),
-            (here, links, *base), SUM, 8_000_000 if parity else 5_000_000,
-        )
+        acc, = call(functools.partial(part, 0 if early else None, count), (here, links, *base), SUM, cost, kept=early)
         acc, = call(functools.partial(join_x_kernel, parity), (links, acc, x_far, x_near), SUM, 1_000_000)
         before = f
         if parity == 0:

time: 31.8 us -> 32.6 us (1.025)
  waiting for transfers between devices: 4.25 us -> 5.07 us
    ppermute x8, waiting for transfers between devices: 1.26 us -> 2.32 us  [swap_t(): return lax.ppermute(value, ('ta', 'gx'), pairs)]
    pallas_call x17 -> x19, Pallas kernels: 8.38 us -> 8.43 us  [call(): pl.pallas_call(kernel, out_shape=tuple((jax.ShapeDtypeStruct(shape, dtype...]
  transfers between devices with their start and end apart: 16 -> 16, of which waited for: 7 -> 7; matrix products, arithmetic and copies ran while one was open for 0% -> 0% of each run, Pallas kernels for 17% -> 16%
where the time goes in v18:
time: 32.6 us; the launch traced here: 32.4 us
  starting transfers between devices  18.7 us (57%)
  Pallas kernels  8.43 us (26%)
  waiting for transfers between devices  5.07 us (16%)
    ppermute x8, starting transfers between devices, swap_t(): return lax.ppermute(value, ('ta', 'gx'), pairs)  12.3 us
    pallas_call x19, Pallas kernels, call(): pl.pallas_call(kernel, out_shape=tuple((jax.ShapeDtypeStruct(shape, dtype...  8.43 us
    ppermute x8, starting transfers between devices, swap(): return lax.ppermute(value, axis, pairs)  6.41 us
    ppermute x8, waiting for transfers between devices, swap(): return lax.ppermute(value, axis, pairs)  2.75 us
    ppermute x8, waiting for transfers between devices, swap_t(): return lax.ppermute(value, ('ta', 'gx'), pairs)  2.32 us
  transfers between devices with their start and end apart: 16, of which 7 were waited for; matrix products, arithmetic and copies ran while one was open for 0% of the time, Pallas kernels for 16%

profile of v18, /device:TPU:0, one launch (start us, length us, event | category | flops | bytes accessed | tf_op | source)
XLA Modules:
  0.0 32.4 jit_solution(18295925048439295411)
XLA Ops:
  0.0 1.1 %shard_map.49 = (bf16[192,128]{1,0:T(8,128)(2,1)S(1)}, bf16[192,128]{1,0:T(8,128)(2,1)S(1)}) custom-call(bf16[768,128]{1,0:T(8,128)(2,1)} %bitcast.24, bf16[1152,128]{1,0:T(8,128)(2,1)} %bitcast.5), custom_call_target="tpu_custom_call" | custom-call | flops 1500000 | bytes 2097152 | tf_op jit(solution)/shard_map/pallas_call | solution.py:407
  1.1 3.1 %collective-permute-start.2 = (bf16[192,128]{1,0:T(8,128)(2,1)S(1)}, bf16[192,128]{1,0:T(8,128)(2,1)S(1)}, u32[]{:S(2)}, u32[]{:S(2)}) collective-permute-start(bf16[192,128]{1,0:T(8,128)(2,1)S(1)} %get-tuple-element.47), channel_id=1, source_target_pairs={{0,4},{1,13},{2,6},{3,15},{4,0},{5,9},{6,2},{7,11},{8,12},{9,5},{1... | collective-permute-start | bytes 147464 | tf_op jit(solution)/shard_map/ppermute | solution.py:434
  4.2 2.5 %collective-permute-start.3 = (bf16[192,128]{1,0:T(8,128)(2,1)S(1)}, bf16[192,128]{1,0:T(8,128)(2,1)S(1)}, u32[]{:S(2)}, u32[]{:S(2)}) collective-permute-start(bf16[192,128]{1,0:T(8,128)(2,1)S(1)} %get-tuple-element.48), channel_id=1, source_target_pairs={{0,12},{1,5},{2,14},{3,7},{4,8},{5,1},{6,10},{7,3},{8,4},{9,13},{1... | collective-permute-start | bytes 147464 | tf_op jit(solution)/shard_map/ppermute | solution.py:434
  6.7 0.1 shard_map.46
  6.8 0.3 collective-permute-start
  7.1 1.4 %collective-permute-start.1 = (bf16[96,128]{1,0:T(8,128)(2,1)S(1)}, bf16[96,128]{1,0:T(8,128)(2,1)S(1)}, u32[]{:S(2)}, u32[]{:S(2)}) collective-permute-start(bf16[96,128]{1,0:T(8,128)(2,1)S(1)} %get-tuple-element.46), channel_id=1, source_target_pairs={{0,1},{1,0},{2,3},{3,2},{4,5},{5,4},{6,7},{7,6},{8,9},{9,8},{10,11... | collective-permute-start | bytes 73736 | tf_op jit(solution)/shard_map/ppermute | solution.py:423
  8.5 1.0 %shard_map.47.acc_ref = f32[768,128]{1,0:T(8,128)S(1)} custom-call(bf16[768,128]{1,0:T(8,128)(2,1)S(1)} %bitcast.26, bf16[1152,128]{1,0:T(8,128)(2,1)S(1)} %bitcast.7), custom_call_target="tpu_custom_call" | custom-call | flops 5000000 | bytes 2097152 | tf_op jit(solution)/shard_map/pallas_call | solution.py:407
  9.4 0.0 copy-start.3
  9.5 0.9 %collective-permute-done.x_far = bf16[96,128]{1,0:T(8,128)(2,1)S(1)} collective-permute-done((bf16[96,128]{1,0:T(8,128)(2,1)S(1)}, bf16[96,128]{1,0:T(8,128)(2,1)S(1)}, u32[]{:S(2)}, u32[]{:S(2)}) %collective-permute-start) | collective-permute-done | bytes 24608 | tf_op jit(solution)/shard_map/ppermute | solution.py:423
  10.3 0.0 collective-permute-done.1.x_near
  10.3 0.1 shard_map.48.acc_ref
  10.4 0.0 collective-permute-done.2.t_one
  10.5 0.5 %shard_map.50 = (bf16[768,128]{1,0:T(8,128)(2,1)S(1)}, bf16[192,128]{1,0:T(8,128)(2,1)S(1)}, bf16[192,128]{1,0:T(8,128)(2,1)S(1)}) custom-call(bf16[1152,128]{1,0:T(8,128)(2,1)S(1)} %bitcast.9, bf16[1152,128]{1,0:T(8,128)(2,1)S(1)} %bitcast.31, f32[768,128]{1,0:T(8,128)S(1)} %shard_map.48.acc_ref, bf16[192,128]{1,0:T(8,128)(2,1)S(1)} %collective-permute-done.2.t_one, ...), custom_call_target="tpu_custom_call" | custom-call | flops 4000000 | bytes 2097152 | tf_op jit(solution)/shard_map/pallas_call | solution.py:407
  11.0 0.0 copy-start.2
  11.0 0.7 %collective-permute-start.6 = (bf16[192,128]{1,0:T(8,128)(2,1)S(1)}, bf16[192,128]{1,0:T(8,128)(2,1)S(1)}, u32[]{:S(2)}, u32[]{:S(2)}) collective-permute-start(bf16[192,128]{1,0:T(8,128)(2,1)S(1)} %get-tuple-element.55), channel_id=1, source_target_pairs={{0,4},{1,13},{2,6},{3,15},{4,0},{5,9},{6,2},{7,11},{8,12},{9,5},{1... | collective-permute-start | bytes 147464 | tf_op jit(solution)/shard_map/ppermute | solution.py:434
  11.7 1.6 %collective-permute-start.7 = (bf16[192,128]{1,0:T(8,128)(2,1)S(1)}, bf16[192,128]{1,0:T(8,128)(2,1)S(1)}, u32[]{:S(2)}, u32[]{:S(2)}) collective-permute-start(bf16[192,128]{1,0:T(8,128)(2,1)S(1)} %get-tuple-element.56), channel_id=1, source_target_pairs={{0,12},{1,5},{2,14},{3,7},{4,8},{5,1},{6,10},{7,3},{8,4},{9,13},{1... | collective-permute-start | bytes 147464 | tf_op jit(solution)/shard_map/ppermute | solution.py:434
  13.3 0.1 shard_map.51
  13.4 0.1 collective-permute-start.4
  13.4 1.6 %collective-permute-start.5 = (bf16[96,128]{1,0:T(8,128)(2,1)S(1)}, bf16[96,128]{1,0:T(8,128)(2,1)S(1)}, u32[]{:S(2)}, u32[]{:S(2)}) collective-permute-start(bf16[96,128]{1,0:T(8,128)(2,1)S(1)} %get-tuple-element.54), channel_id=1, source_target_pairs={{0,1},{1,0},{2,3},{3,2},{4,5},{5,4},{6,7},{7,6},{8,9},{9,8},{10,11... | collective-permute-start | bytes 73736 | tf_op jit(solution)/shard_map/ppermute | solution.py:423
  15.0 1.3 %shard_map.52.acc_ref = f32[768,128]{1,0:T(8,128)S(1)} custom-call(bf16[768,128]{1,0:T(8,128)(2,1)S(1)} %get-tuple-element.52.f_ref.refs_0_, bf16[1152,128]{1,0:T(8,128)(2,1)S(1)} %bitcast.11, bf16[768,128]{1,0:T(8,128)(2,1)S(1)} %bitcast.27, bf16[1152,128]{1,0:T(8,128)(2,1)S(1)} %bitcast.28), custom_call_target="tpu_custom_call" | custom-call | flops 8000000 | bytes 2097152 | tf_op jit(solution)/shard_map/pallas_call | solution.py:407
  16.3 0.6 %collective-permute-done.4.x_far = bf16[96,128]{1,0:T(8,128)(2,1)S(1)} collective-permute-done((bf16[96,128]{1,0:T(8,128)(2,1)S(1)}, bf16[96,128]{1,0:T(8,128)(2,1)S(1)}, u32[]{:S(2)}, u32[]{:S(2)}) %collective-permute-start.4) | collective-permute-done | bytes 24608 | tf_op jit(solution)/shard_map/ppermute | solution.py:423
  16.9 0.0 collective-permute-done.5.x_near
  16.9 0.1 shard_map.53.acc_ref
  17.0 0.6 %collective-permute-done.7.t_two = bf16[192,128]{1,0:T(8,128)(2,1)S(1)} collective-permute-done((bf16[192,128]{1,0:T(8,128)(2,1)S(1)}, bf16[192,128]{1,0:T(8,128)(2,1)S(1)}, u32[]{:S(2)}, u32[]{:S(2)}) %collective-permute-start.7) | collective-permute-done | bytes 49184 | tf_op jit(solution)/shard_map/ppermute | solution.py:434
  17.6 0.2 shard_map.54
  17.8 0.6 %collective-permute-start.10 = (bf16[192,128]{1,0:T(8,128)(2,1)S(1)}, bf16[192,128]{1,0:T(8,128)(2,1)S(1)}, u32[]{:S(2)}, u32[]{:S(2)}) collective-permute-start(bf16[192,128]{1,0:T(8,128)(2,1)S(1)} %get-tuple-element.66), channel_id=1, source_target_pairs={{0,4},{1,13},{2,6},{3,15},{4,0},{5,9},{6,2},{7,11},{8,12},{9,5},{1... | collective-permute-start | bytes 147464 | tf_op jit(solution)/shard_map/ppermute | solution.py:434
  18.4 1.8 %collective-permute-start.11 = (bf16[192,128]{1,0:T(8,128)(2,1)S(1)}, bf16[192,128]{1,0:T(8,128)(2,1)S(1)}, u32[]{:S(2)}, u32[]{:S(2)}) collective-permute-start(bf16[192,128]{1,0:T(8,128)(2,1)S(1)} %get-tuple-element.67), channel_id=1, source_target_pairs={{0,12},{1,5},{2,14},{3,7},{4,8},{5,1},{6,10},{7,3},{8,4},{9,13},{1... | collective-permute-start | bytes 147464 | tf_op jit(solution)/shard_map/ppermute | solution.py:434
  20.1 0.1 shard_map.55
  20.2 0.4 %collective-permute-start.8 = (bf16[96,128]{1,0:T(8,128)(2,1)S(1)}, bf16[96,128]{1,0:T(8,128)(2,1)S(1)}, u32[]{:S(2)}, u32[]{:S(2)}) collective-permute-start(bf16[96,128]{1,0:T(8,128)(2,1)S(1)} %get-tuple-element.64), channel_id=1, source_target_pairs={{0,3},{1,2},{2,1},{3,0},{4,7},{5,6},{6,5},{7,4},{8,11},{9,10},{10,... | collective-permute-start | bytes 73736 | tf_op jit(solution)/shard_map/ppermute | solution.py:423
  20.6 1.3 %collective-permute-start.9 = (bf16[96,128]{1,0:T(8,128)(2,1)S(1)}, bf16[96,128]{1,0:T(8,128)(2,1)S(1)}, u32[]{:S(2)}, u32[]{:S(2)}) collective-permute-start(bf16[96,128]{1,0:T(8,128)(2,1)S(1)} %get-tuple-element.65), channel_id=1, source_target_pairs={{0,1},{1,0},{2,3},{3,2},{4,5},{5,4},{6,7},{7,6},{8,9},{9,8},{10,11... | collective-permute-start | bytes 73736 | tf_op jit(solution)/shard_map/ppermute | solution.py:423
  21.9 1.0 %shard_map.57.acc_ref = f32[768,128]{1,0:T(8,128)S(1)} custom-call(bf16[768,128]{1,0:T(8,128)(2,1)S(1)} %get-tuple-element.60.f_ref.refs_0_.refs_2_, bf16[1152,128]{1,0:T(8,128)(2,1)S(1)} %bitcast.16, f32[768,128]{1,0:T(8,128)S(1)} %shard_map.56.refs_2_), custom_call_target="tpu_custom_call", output_to_operand_aliasing={{}: (2, {})} | custom-call | flops 5000000 | bytes 2097152 | tf_op jit(solution)/shard_map/pallas_call | solution.py:407
  22.9 0.7 %collective-permute-done.8.x_far = bf16[96,128]{1,0:T(8,128)(2,1)S(1)} collective-permute-done((bf16[96,128]{1,0:T(8,128)(2,1)S(1)}, bf16[96,128]{1,0:T(8,128)(2,1)S(1)}, u32[]{:S(2)}, u32[]{:S(2)}) %collective-permute-start.8) | collective-permute-done | bytes 24608 | tf_op jit(solution)/shard_map/ppermute | solution.py:423
  23.6 0.0 collective-permute-done.9.x_near
  23.6 0.1 shard_map.58.acc_ref
  23.6 0.0 collective-permute-done.10.t_one
  23.7 0.8 %collective-permute-done.11.t_two = bf16[192,128]{1,0:T(8,128)(2,1)S(1)} collective-permute-done((bf16[192,128]{1,0:T(8,128)(2,1)S(1)}, bf16[192,128]{1,0:T(8,128)(2,1)S(1)}, u32[]{:S(2)}, u32[]{:S(2)}) %collective-permute-start.11) | collective-permute-done | bytes 49184 | tf_op jit(solution)/shard_map/ppermute | solution.py:434
  24.4 0.5 %shard_map.59 = (bf16[768,128]{1,0:T(8,128)(2,1)S(1)}, bf16[192,128]{1,0:T(8,128)(2,1)S(1)}, bf16[192,128]{1,0:T(8,128)(2,1)S(1)}) custom-call(bf16[1152,128]{1,0:T(8,128)(2,1)S(1)} %bitcast.18, bf16[1152,128]{1,0:T(8,128)(2,1)S(1)} %bitcast.32, f32[768,128]{1,0:T(8,128)S(1)} %shard_map.58.acc_ref, bf16[192,128]{1,0:T(8,128)(2,1)S(1)} %collective-permute-done.10.t_one, ...), custom_call_target="tpu_custom_call" | custom-call | flops 4000000 | bytes 2097152 | tf_op jit(solution)/shard_map/pallas_call | solution.py:407
  25.0 0.3 collective-permute-start.14
  25.2 1.9 %collective-permute-start.15 = (bf16[192,128]{1,0:T(8,128)(2,1)S(1)}, bf16[192,128]{1,0:T(8,128)(2,1)S(1)}, u32[]{:S(2)}, u32[]{:S(2)}) collective-permute-start(bf16[192,128]{1,0:T(8,128)(2,1)S(1)} %get-tuple-element.78), channel_id=1, source_target_pairs={{0,12},{1,5},{2,14},{3,7},{4,8},{5,1},{6,10},{7,3},{8,4},{9,13},{1... | collective-permute-start | bytes 147464 | tf_op jit(solution)/shard_map/ppermute | solution.py:434
  27.1 0.1 shard_map.60
  27.2 0.6 %collective-permute-start.12 = (bf16[96,128]{1,0:T(8,128)(2,1)S(1)}, bf16[96,128]{1,0:T(8,128)(2,1)S(1)}, u32[]{:S(2)}, u32[]{:S(2)}) collective-permute-start(bf16[96,128]{1,0:T(8,128)(2,1)S(1)} %get-tuple-element.75), channel_id=1, source_target_pairs={{0,3},{1,2},{2,1},{3,0},{4,7},{5,6},{6,5},{7,4},{8,11},{9,10},{10,... | collective-permute-start | bytes 73736 | tf_op jit(solution)/shard_map/ppermute | solution.py:423
  27.8 0.8 %collective-permute-start.13 = (bf16[96,128]{1,0:T(8,128)(2,1)S(1)}, bf16[96,128]{1,0:T(8,128)(2,1)S(1)}, u32[]{:S(2)}, u32[]{:S(2)}) collective-permute-start(bf16[96,128]{1,0:T(8,128)(2,1)S(1)} %get-tuple-element.76), channel_id=1, source_target_pairs={{0,1},{1,0},{2,3},{3,2},{4,5},{5,4},{6,7},{7,6},{8,9},{9,8},{10,11... | collective-permute-start | bytes 73736 | tf_op jit(solution)/shard_map/ppermute | solution.py:423
  28.6 1.3 %shard_map.62.acc_ref = f32[768,128]{1,0:T(8,128)S(1)} custom-call(bf16[768,128]{1,0:T(8,128)(2,1)S(1)} %get-tuple-element.71.f_ref.refs_0_, bf16[1152,128]{1,0:T(8,128)(2,1)S(1)} %bitcast.21, bf16[768,128]{1,0:T(8,128)(2,1)S(1)} %get-tuple-element.60.f_ref.refs_0_.refs_2_, bf16[1152,128]{1,0:T(8,128)(2,1)S(1)} %bitcast.30, ...), custom_call_target="tpu_custom_call", output_to_operand_aliasing={{}: (4, {})} | custom-call | flops 8000000 | bytes 2097152 | tf_op jit(solution)/shard_map/pallas_call | solution.py:407
  29.9 0.6 %collective-permute-done.12.x_far = bf16[96,128]{1,0:T(8,128)(2,1)S(1)} collective-permute-done((bf16[96,128]{1,0:T(8,128)(2,1)S(1)}, bf16[96,128]{1,0:T(8,128)(2,1)S(1)}, u32[]{:S(2)}, u32[]{:S(2)}) %collective-permute-start.12) | collective-permute-done | bytes 24608 | tf_op jit(solution)/shard_map/ppermute | solution.py:423
  30.5 0.0 collective-permute-done.13.x_near
  30.5 0.1 shard_map.63.acc_ref
  30.7 1.0 %collective-permute-done.15.t_two = bf16[192,128]{1,0:T(8,128)(2,1)S(1)} collective-permute-done((bf16[192,128]{1,0:T(8,128)(2,1)S(1)}, bf16[192,128]{1,0:T(8,128)(2,1)S(1)}, u32[]{:S(2)}, u32[]{:S(2)}) %collective-permute-start.15) | collective-permute-done | bytes 49184 | tf_op jit(solution)/shard_map/ppermute | solution.py:434
  31.6 0.8 %shard_map.64 = bf16[768,128]{1,0:T(8,128)(2,1)} custom-call(bf16[1152,128]{1,0:T(8,128)(2,1)S(1)} %bitcast.23, f32[768,128]{1,0:T(8,128)S(1)} %shard_map.63.acc_ref, bf16[192,128]{1,0:T(8,128)(2,1)S(1)} %collective-permute-done.14.t_one, bf16[192,128]{1,0:T(8,128)(2,1)S(1)} %collective-permute-done.15.t_two), custom_call_target="tpu_custom_call" | custom-call | flops 1000000 | bytes 2097152 | tf_op jit(solution)/shard_map/pallas_call | solution.py:407
  (11 shorter events, 0.1 us)
Async XLA Ops:
  0.0 6.7 %copy-start = (bf16[4,3,3,2,2,2,4,128]{7,6,5,4,3,2,1,0:T(4,128)(2,1)S(1)}, bf16[4,3,3,2,2,2,4,128]{7,6,5,4,3,2,1,0:T(4,128)(2,1)}, u32[]{:S(2)}) copy-start(bf16[4,3,3,2,2,2,4,128]{7,6,5,4,3,2,1,0:T(4,128)(2,1)} %param.5) | copy-start | bytes 884740
  0.0 6.7 %copy-start.1 = (bf16[4,4,3,2,2,4,128]{6,5,4,3,2,1,0:T(4,128)(2,1)S(1)}, bf16[4,4,3,2,2,4,128]{6,5,4,3,2,1,0:T(4,128)(2,1)}, u32[]{:S(2)}) copy-start(bf16[4,4,3,2,2,4,128]{6,5,4,3,2,1,0:T(4,128)(2,1)} %param.4) | copy-start | bytes 589828
  1.1 9.3 %collective-permute-start.2 = (bf16[192,128]{1,0:T(8,128)(2,1)S(1)}, bf16[192,128]{1,0:T(8,128)(2,1)S(1)}, u32[]{:S(2)}, u32[]{:S(2)}) collective-permute-start(bf16[192,128]{1,0:T(8,128)(2,1)S(1)} %get-tuple-element.47), channel_id=1, source_target_pairs={{0,4},{1,13},{2,6},{3,15},{4,0},{5,9},{6,2},{7,11},{8,12},{9,5},{1... | collective-permute-start | bytes 147464 | tf_op jit(solution)/shard_map/ppermute | solution.py:434
  4.2 6.2 %collective-permute-start.3 = (bf16[192,128]{1,0:T(8,128)(2,1)S(1)}, bf16[192,128]{1,0:T(8,128)(2,1)S(1)}, u32[]{:S(2)}, u32[]{:S(2)}) collective-permute-start(bf16[192,128]{1,0:T(8,128)(2,1)S(1)} %get-tuple-element.48), channel_id=1, source_target_pairs={{0,12},{1,5},{2,14},{3,7},{4,8},{5,1},{6,10},{7,3},{8,4},{9,13},{1... | collective-permute-start | bytes 147464 | tf_op jit(solution)/shard_map/ppermute | solution.py:434
  6.8 3.5 %collective-permute-start = (bf16[96,128]{1,0:T(8,128)(2,1)S(1)}, bf16[96,128]{1,0:T(8,128)(2,1)S(1)}, u32[]{:S(2)}, u32[]{:S(2)}) collective-permute-start(bf16[96,128]{1,0:T(8,128)(2,1)S(1)} %get-tuple-element.45), channel_id=1, source_target_pairs={{0,3},{1,2},{2,1},{3,0},{4,7},{5,6},{6,5},{7,4},{8,11},{9,10},{10,... | collective-permute-start | bytes 73736 | tf_op jit(solution)/shard_map/ppermute | solution.py:423
  7.1 3.3 %collective-permute-start.1 = (bf16[96,128]{1,0:T(8,128)(2,1)S(1)}, bf16[96,128]{1,0:T(8,128)(2,1)S(1)}, u32[]{:S(2)}, u32[]{:S(2)}) collective-permute-start(bf16[96,128]{1,0:T(8,128)(2,1)S(1)} %get-tuple-element.46), channel_id=1, source_target_pairs={{0,1},{1,0},{2,3},{3,2},{4,5},{5,4},{6,7},{7,6},{8,9},{9,8},{10,11... | collective-permute-start | bytes 73736 | tf_op jit(solution)/shard_map/ppermute | solution.py:423
  9.4 1.0 %copy-start.3 = (bf16[2,6,6,2,2,4,128]{6,5,4,3,2,1,0:T(4,128)(2,1)S(1)}, bf16[2,6,6,2,2,4,128]{6,5,4,3,2,1,0:T(4,128)(2,1)}, u32[]{:S(2)}) copy-start(bf16[2,6,6,2,2,4,128]{6,5,4,3,2,1,0:T(4,128)(2,1)} %param.7) | copy-start | bytes 884740
  11.0 4.1 %copy-start.2 = (bf16[2,6,6,2,2,4,128]{6,5,4,3,2,1,0:T(4,128)(2,1)S(1)}, bf16[2,6,6,2,2,4,128]{6,5,4,3,2,1,0:T(4,128)(2,1)}, u32[]{:S(2)}) copy-start(bf16[2,6,6,2,2,4,128]{6,5,4,3,2,1,0:T(4,128)(2,1)} %param.6) | copy-start | bytes 884740
  11.0 6.0 %collective-permute-start.6 = (bf16[192,128]{1,0:T(8,128)(2,1)S(1)}, bf16[192,128]{1,0:T(8,128)(2,1)S(1)}, u32[]{:S(2)}, u32[]{:S(2)}) collective-permute-start(bf16[192,128]{1,0:T(8,128)(2,1)S(1)} %get-tuple-element.55), channel_id=1, source_target_pairs={{0,4},{1,13},{2,6},{3,15},{4,0},{5,9},{6,2},{7,11},{8,12},{9,5},{1... | collective-permute-start | bytes 147464 | tf_op jit(solution)/shard_map/ppermute | solution.py:434
  11.7 5.9 %collective-permute-start.7 = (bf16[192,128]{1,0:T(8,128)(2,1)S(1)}, bf16[192,128]{1,0:T(8,128)(2,1)S(1)}, u32[]{:S(2)}, u32[]{:S(2)}) collective-permute-start(bf16[192,128]{1,0:T(8,128)(2,1)S(1)} %get-tuple-element.56), channel_id=1, source_target_pairs={{0,12},{1,5},{2,14},{3,7},{4,8},{5,1},{6,10},{7,3},{8,4},{9,13},{1... | collective-permute-start | bytes 147464 | tf_op jit(solution)/shard_map/ppermute | solution.py:434
  13.4 3.5 %collective-permute-start.4 = (bf16[96,128]{1,0:T(8,128)(2,1)S(1)}, bf16[96,128]{1,0:T(8,128)(2,1)S(1)}, u32[]{:S(2)}, u32[]{:S(2)}) collective-permute-start(bf16[96,128]{1,0:T(8,128)(2,1)S(1)} %get-tuple-element.53), channel_id=1, source_target_pairs={{0,3},{1,2},{2,1},{3,0},{4,7},{5,6},{6,5},{7,4},{8,11},{9,10},{10,... | collective-permute-start | bytes 73736 | tf_op jit(solution)/shard_map/ppermute | solution.py:423
  13.4 3.5 %collective-permute-start.5 = (bf16[96,128]{1,0:T(8,128)(2,1)S(1)}, bf16[96,128]{1,0:T(8,128)(2,1)S(1)}, u32[]{:S(2)}, u32[]{:S(2)}) collective-permute-start(bf16[96,128]{1,0:T(8,128)(2,1)S(1)} %get-tuple-element.54), channel_id=1, source_target_pairs={{0,1},{1,0},{2,3},{3,2},{4,5},{5,4},{6,7},{7,6},{8,9},{9,8},{10,11... | collective-permute-start | bytes 73736 | tf_op jit(solution)/shard_map/ppermute | solution.py:423
  17.8 5.9 %collective-permute-start.10 = (bf16[192,128]{1,0:T(8,128)(2,1)S(1)}, bf16[192,128]{1,0:T(8,128)(2,1)S(1)}, u32[]{:S(2)}, u32[]{:S(2)}) collective-permute-start(bf16[192,128]{1,0:T(8,128)(2,1)S(1)} %get-tuple-element.66), channel_id=1, source_target_pairs={{0,4},{1,13},{2,6},{3,15},{4,0},{5,9},{6,2},{7,11},{8,12},{9,5},{1... | collective-permute-start | bytes 147464 | tf_op jit(solution)/shard_map/ppermute | solution.py:434
  18.4 6.0 %collective-permute-start.11 = (bf16[192,128]{1,0:T(8,128)(2,1)S(1)}, bf16[192,128]{1,0:T(8,128)(2,1)S(1)}, u32[]{:S(2)}, u32[]{:S(2)}) collective-permute-start(bf16[192,128]{1,0:T(8,128)(2,1)S(1)} %get-tuple-element.67), channel_id=1, source_target_pairs={{0,12},{1,5},{2,14},{3,7},{4,8},{5,1},{6,10},{7,3},{8,4},{9,13},{1... | collective-permute-start | bytes 147464 | tf_op jit(solution)/shard_map/ppermute | solution.py:434
  20.2 3.3 %collective-permute-start.8 = (bf16[96,128]{1,0:T(8,128)(2,1)S(1)}, bf16[96,128]{1,0:T(8,128)(2,1)S(1)}, u32[]{:S(2)}, u32[]{:S(2)}) collective-permute-start(bf16[96,128]{1,0:T(8,128)(2,1)S(1)} %get-tuple-element.64), channel_id=1, source_target_pairs={{0,3},{1,2},{2,1},{3,0},{4,7},{5,6},{6,5},{7,4},{8,11},{9,10},{10,... | collective-permute-start | bytes 73736 | tf_op jit(solution)/shard_map/ppermute | solution.py:423
  20.6 2.9 %collective-permute-start.9 = (bf16[96,128]{1,0:T(8,128)(2,1)S(1)}, bf16[96,128]{1,0:T(8,128)(2,1)S(1)}, u32[]{:S(2)}, u32[]{:S(2)}) collective-permute-start(bf16[96,128]{1,0:T(8,128)(2,1)S(1)} %get-tuple-element.65), channel_id=1, source_target_pairs={{0,1},{1,0},{2,3},{3,2},{4,5},{5,4},{6,7},{7,6},{8,9},{9,8},{10,11... | collective-permute-start | bytes 73736 | tf_op jit(solution)/shard_map/ppermute | solution.py:423
  25.0 5.7 %collective-permute-start.14 = (bf16[192,128]{1,0:T(8,128)(2,1)S(1)}, bf16[192,128]{1,0:T(8,128)(2,1)S(1)}, u32[]{:S(2)}, u32[]{:S(2)}) collective-permute-start(bf16[192,128]{1,0:T(8,128)(2,1)S(1)} %get-tuple-element.77), channel_id=1, source_target_pairs={{0,4},{1,13},{2,6},{3,15},{4,0},{5,9},{6,2},{7,11},{8,12},{9,5},{1... | collective-permute-start | bytes 147464 | tf_op jit(solution)/shard_map/ppermute | solution.py:434
  25.2 6.4 %collective-permute-start.15 = (bf16[192,128]{1,0:T(8,128)(2,1)S(1)}, bf16[192,128]{1,0:T(8,128)(2,1)S(1)}, u32[]{:S(2)}, u32[]{:S(2)}) collective-permute-start(bf16[192,128]{1,0:T(8,128)(2,1)S(1)} %get-tuple-element.78), channel_id=1, source_target_pairs={{0,12},{1,5},{2,14},{3,7},{4,8},{5,1},{6,10},{7,3},{8,4},{9,13},{1... | collective-permute-start | bytes 147464 | tf_op jit(solution)/shard_map/ppermute | solution.py:434
  27.2 3.3 %collective-permute-start.12 = (bf16[96,128]{1,0:T(8,128)(2,1)S(1)}, bf16[96,128]{1,0:T(8,128)(2,1)S(1)}, u32[]{:S(2)}, u32[]{:S(2)}) collective-permute-start(bf16[96,128]{1,0:T(8,128)(2,1)S(1)} %get-tuple-element.75), channel_id=1, source_target_pairs={{0,3},{1,2},{2,1},{3,0},{4,7},{5,6},{6,5},{7,4},{8,11},{9,10},{10,... | collective-permute-start | bytes 73736 | tf_op jit(solution)/shard_map/ppermute | solution.py:423
  27.8 2.7 %collective-permute-start.13 = (bf16[96,128]{1,0:T(8,128)(2,1)S(1)}, bf16[96,128]{1,0:T(8,128)(2,1)S(1)}, u32[]{:S(2)}, u32[]{:S(2)}) collective-permute-start(bf16[96,128]{1,0:T(8,128)(2,1)S(1)} %get-tuple-element.76), channel_id=1, source_target_pairs={{0,1},{1,0},{2,3},{3,2},{4,5},{5,4},{6,7},{7,6},{8,9},{9,8},{10,11... | collective-permute-start | bytes 73736 | tf_op jit(solution)/shard_map/ppermute | solution.py:423

commit v19 on v11

--- a/solution.py
+++ b/solution.py
@@ -115,8 +115,8 @@
     return rows // 4, rows % 4
 
 
-def even_device(*axes):
-    place = sum(lax.axis_index(axis) for axis in axes)
+def even_device(*axes, extra=0):
+    place = sum(lax.axis_index(axis) for axis in axes) + extra
     return lax.broadcast(place % 2, (8, 128)) == 0
 
 
@@ -151,7 +151,7 @@
 
 
 def send_t(f_ref, links_ref, parity, t_one, t_two, ready=lambda r: None):
-    even = even_device("ta", "gx")
+    even = even_device("ta", "gx", extra=parity)
     t_idx, _ = site_masks()
     first = t_idx == 0
     links = t_edges(load_links(links_ref, 0, parity))
@@ -342,7 +342,7 @@
 
 
 def join_t(links_ref, acc_ref, t_one, t_two, parity, out_ref, scale=None, done=lambda r: None):
-    even = even_device("ta", "gx")
+    even = even_device("ta", "gx", extra=parity)
     t_idx, _ = site_masks()
     first = t_idx == 0
     sign = jnp.where(first, 1.0, -1.0).astype(F32)
@@ -443,7 +443,7 @@
     t_one, t_two = call(start_kernel, held, T_HALOS, 1_500_000, start_scratch, in_space=pltpu.HBM)
     for hop in range(4):
         parity = hop % 2
-        t_one, t_two = swap_t(t_one, True), swap_t(t_two, False)
+        t_one, t_two = swap_t(t_one, parity == 0), swap_t(t_two, parity == 1)
         x_far, x_near = call(
             functools.partial(send_x_kernel, parity), (f, links), X_HALOS, 1_500_000
         )

time: 31.8 us -> 32.8 us (1.031)
  waiting for transfers between devices: 4.25 us -> 5.58 us
    ppermute x8, waiting for transfers between devices: 1.26 us -> 2.33 us  [swap_t(): return lax.ppermute(value, ('ta', 'gx'), pairs)]
  transfers between devices with their start and end apart: 16 -> 16, of which waited for: 7 -> 9; matrix products, arithmetic and copies ran while one was open for 0% -> 0% of each run, Pallas kernels for 17% -> 16%
where the time goes in v19:
time: 32.8 us; the launch traced here: 32.7 us
  starting transfers between devices  18.6 us (57%)
  Pallas kernels  8.38 us (26%)
  waiting for transfers between devices  5.58 us (17%)
    ppermute x8, starting transfers between devices, swap_t(): return lax.ppermute(value, ('ta', 'gx'), pairs)  12.5 us
    pallas_call x17, Pallas kernels, call(): pl.pallas_call(kernel, out_shape=tuple((jax.ShapeDtypeStruct(shape, dtype...  8.38 us
    ppermute x8, starting transfers between devices, swap(): return lax.ppermute(value, axis, pairs)  6.07 us
    ppermute x8, waiting for transfers between devices, swap(): return lax.ppermute(value, axis, pairs)  3.25 us
    ppermute x8, waiting for transfers between devices, swap_t(): return lax.ppermute(value, ('ta', 'gx'), pairs)  2.33 us
  transfers between devices with their start and end apart: 16, of which 9 were waited for; matrix products, arithmetic and copies ran while one was open for 0% of the time, Pallas kernels for 16%

profile of v19, /device:TPU:0, one launch (start us, length us, event | category | flops | bytes accessed | tf_op | source)
XLA Modules:
  0.0 32.7 jit_solution(3608445053414129515)
XLA Ops:
  0.0 1.1 %shard_map.49 = (bf16[192,128]{1,0:T(8,128)(2,1)S(1)}, bf16[192,128]{1,0:T(8,128)(2,1)S(1)}) custom-call(bf16[768,128]{1,0:T(8,128)(2,1)} %bitcast.22, bf16[1152,128]{1,0:T(8,128)(2,1)} %bitcast.5), custom_call_target="tpu_custom_call" | custom-call | flops 1500000 | bytes 2097152 | tf_op jit(solution)/shard_map/pallas_call | solution.py:402
  1.1 3.1 %collective-permute-start.2 = (bf16[192,128]{1,0:T(8,128)(2,1)S(1)}, bf16[192,128]{1,0:T(8,128)(2,1)S(1)}, u32[]{:S(2)}, u32[]{:S(2)}) collective-permute-start(bf16[192,128]{1,0:T(8,128)(2,1)S(1)} %get-tuple-element.41), channel_id=1, source_target_pairs={{0,4},{1,13},{2,6},{3,15},{4,0},{5,9},{6,2},{7,11},{8,12},{9,5},{1... | collective-permute-start | bytes 147464 | tf_op jit(solution)/shard_map/ppermute | solution.py:428
  4.2 2.5 %collective-permute-start.3 = (bf16[192,128]{1,0:T(8,128)(2,1)S(1)}, bf16[192,128]{1,0:T(8,128)(2,1)S(1)}, u32[]{:S(2)}, u32[]{:S(2)}) collective-permute-start(bf16[192,128]{1,0:T(8,128)(2,1)S(1)} %get-tuple-element.42), channel_id=1, source_target_pairs={{0,12},{1,5},{2,14},{3,7},{4,8},{5,1},{6,10},{7,3},{8,4},{9,13},{1... | collective-permute-start | bytes 147464 | tf_op jit(solution)/shard_map/ppermute | solution.py:428
  6.7 0.1 shard_map.46
  6.8 0.3 collective-permute-start
  7.1 1.4 %collective-permute-start.1 = (bf16[96,128]{1,0:T(8,128)(2,1)S(1)}, bf16[96,128]{1,0:T(8,128)(2,1)S(1)}, u32[]{:S(2)}, u32[]{:S(2)}) collective-permute-start(bf16[96,128]{1,0:T(8,128)(2,1)S(1)} %get-tuple-element.40), channel_id=1, source_target_pairs={{0,1},{1,0},{2,3},{3,2},{4,5},{5,4},{6,7},{7,6},{8,9},{9,8},{10,11... | collective-permute-start | bytes 73736 | tf_op jit(solution)/shard_map/ppermute | solution.py:417
  8.5 1.0 %shard_map.47.acc_ref = f32[768,128]{1,0:T(8,128)S(1)} custom-call(bf16[768,128]{1,0:T(8,128)(2,1)S(1)} %bitcast.24, bf16[1152,128]{1,0:T(8,128)(2,1)S(1)} %bitcast.7), custom_call_target="tpu_custom_call" | custom-call | flops 5000000 | bytes 2097152 | tf_op jit(solution)/shard_map/pallas_call | solution.py:402
  9.4 0.0 copy-start.2
  9.5 0.9 %collective-permute-done.x_far = bf16[96,128]{1,0:T(8,128)(2,1)S(1)} collective-permute-done((bf16[96,128]{1,0:T(8,128)(2,1)S(1)}, bf16[96,128]{1,0:T(8,128)(2,1)S(1)}, u32[]{:S(2)}, u32[]{:S(2)}) %collective-permute-start) | collective-permute-done | bytes 24608 | tf_op jit(solution)/shard_map/ppermute | solution.py:417
  10.3 0.1 shard_map.48.acc_ref
  10.4 0.0 collective-permute-done.2.t_one
  10.4 0.0 collective-permute-done.3.t_two
  10.5 0.5 %shard_map.50 = (bf16[768,128]{1,0:T(8,128)(2,1)S(1)}, bf16[192,128]{1,0:T(8,128)(2,1)S(1)}, bf16[192,128]{1,0:T(8,128)(2,1)S(1)}) custom-call(bf16[1152,128]{1,0:T(8,128)(2,1)S(1)} %bitcast.9, bf16[1152,128]{1,0:T(8,128)(2,1)S(1)} %bitcast.26, f32[768,128]{1,0:T(8,128)S(1)} %shard_map.48.acc_ref, bf16[192,128]{1,0:T(8,128)(2,1)S(1)} %collective-permute-done.2.t_one, ...), custom_call_target="tpu_custom_call" | custom-call | flops 4000000 | bytes 2097152 | tf_op jit(solution)/shard_map/pallas_call | solution.py:402
  11.0 0.0 copy-start.3
  11.0 2.2 %collective-permute-start.6 = (bf16[192,128]{1,0:T(8,128)(2,1)S(1)}, bf16[192,128]{1,0:T(8,128)(2,1)S(1)}, u32[]{:S(2)}, u32[]{:S(2)}) collective-permute-start(bf16[192,128]{1,0:T(8,128)(2,1)S(1)} %get-tuple-element.49), channel_id=1, source_target_pairs={{0,12},{1,5},{2,14},{3,7},{4,8},{5,1},{6,10},{7,3},{8,4},{9,13},{1... | collective-permute-start | bytes 147464 | tf_op jit(solution)/shard_map/ppermute | solution.py:428
  13.2 0.0 collective-permute-start.7
  13.2 0.1 shard_map.51
  13.3 0.1 collective-permute-start.4
  13.4 1.6 %collective-permute-start.5 = (bf16[96,128]{1,0:T(8,128)(2,1)S(1)}, bf16[96,128]{1,0:T(8,128)(2,1)S(1)}, u32[]{:S(2)}, u32[]{:S(2)}) collective-permute-start(bf16[96,128]{1,0:T(8,128)(2,1)S(1)} %get-tuple-element.48), channel_id=1, source_target_pairs={{0,1},{1,0},{2,3},{3,2},{4,5},{5,4},{6,7},{7,6},{8,9},{9,8},{10,11... | collective-permute-start | bytes 73736 | tf_op jit(solution)/shard_map/ppermute | solution.py:417
  15.0 1.3 %shard_map.52.acc_ref = f32[768,128]{1,0:T(8,128)S(1)} custom-call(bf16[768,128]{1,0:T(8,128)(2,1)S(1)} %get-tuple-element.46.f_ref.refs_0_, bf16[1152,128]{1,0:T(8,128)(2,1)S(1)} %bitcast.11, bf16[768,128]{1,0:T(8,128)(2,1)S(1)} %bitcast.25, bf16[1152,128]{1,0:T(8,128)(2,1)S(1)} %bitcast.28), custom_call_target="tpu_custom_call" | custom-call | flops 8000000 | bytes 2097152 | tf_op jit(solution)/shard_map/pallas_call | solution.py:402
  16.3 0.6 %collective-permute-done.4.x_far = bf16[96,128]{1,0:T(8,128)(2,1)S(1)} collective-permute-done((bf16[96,128]{1,0:T(8,128)(2,1)S(1)}, bf16[96,128]{1,0:T(8,128)(2,1)S(1)}, u32[]{:S(2)}, u32[]{:S(2)}) %collective-permute-start.4) | collective-permute-done | bytes 24608 | tf_op jit(solution)/shard_map/ppermute | solution.py:417
  16.8 0.0 collective-permute-done.5.x_near
  16.8 0.1 shard_map.53.acc_ref
  16.9 0.1 collective-permute-done.6.t_one
  17.0 0.5 %collective-permute-done.7.t_two = bf16[192,128]{1,0:T(8,128)(2,1)S(1)} collective-permute-done((bf16[192,128]{1,0:T(8,128)(2,1)S(1)}, bf16[192,128]{1,0:T(8,128)(2,1)S(1)}, u32[]{:S(2)}, u32[]{:S(2)}) %collective-permute-start.7) | collective-permute-done | bytes 49184 | tf_op jit(solution)/shard_map/ppermute | solution.py:428
  17.5 0.2 shard_map.54
  17.8 1.5 %collective-permute-start.10 = (bf16[192,128]{1,0:T(8,128)(2,1)S(1)}, bf16[192,128]{1,0:T(8,128)(2,1)S(1)}, u32[]{:S(2)}, u32[]{:S(2)}) collective-permute-start(bf16[192,128]{1,0:T(8,128)(2,1)S(1)} %get-tuple-element.57), channel_id=1, source_target_pairs={{0,4},{1,13},{2,6},{3,15},{4,0},{5,9},{6,2},{7,11},{8,12},{9,5},{1... | collective-permute-start | bytes 147464 | tf_op jit(solution)/shard_map/ppermute | solution.py:428
  19.2 1.6 %collective-permute-start.11 = (bf16[192,128]{1,0:T(8,128)(2,1)S(1)}, bf16[192,128]{1,0:T(8,128)(2,1)S(1)}, u32[]{:S(2)}, u32[]{:S(2)}) collective-permute-start(bf16[192,128]{1,0:T(8,128)(2,1)S(1)} %get-tuple-element.58), channel_id=1, source_target_pairs={{0,12},{1,5},{2,14},{3,7},{4,8},{5,1},{6,10},{7,3},{8,4},{9,13},{1... | collective-permute-start | bytes 147464 | tf_op jit(solution)/shard_map/ppermute | solution.py:428
  20.8 0.1 shard_map.55
  20.9 0.1 collective-permute-start.8
  21.0 1.3 %collective-permute-start.9 = (bf16[96,128]{1,0:T(8,128)(2,1)S(1)}, bf16[96,128]{1,0:T(8,128)(2,1)S(1)}, u32[]{:S(2)}, u32[]{:S(2)}) collective-permute-start(bf16[96,128]{1,0:T(8,128)(2,1)S(1)} %get-tuple-element.56), channel_id=1, source_target_pairs={{0,1},{1,0},{2,3},{3,2},{4,5},{5,4},{6,7},{7,6},{8,9},{9,8},{10,11... | collective-permute-start | bytes 73736 | tf_op jit(solution)/shard_map/ppermute | solution.py:417
  22.3 1.0 %shard_map.56.acc_ref = f32[768,128]{1,0:T(8,128)S(1)} custom-call(bf16[768,128]{1,0:T(8,128)(2,1)S(1)} %get-tuple-element.54.f_ref.refs_0_.refs_2_, bf16[1152,128]{1,0:T(8,128)(2,1)S(1)} %bitcast.15), custom_call_target="tpu_custom_call" | custom-call | flops 5000000 | bytes 2097152 | tf_op jit(solution)/shard_map/pallas_call | solution.py:402
  23.3 1.0 %collective-permute-done.8.x_far = bf16[96,128]{1,0:T(8,128)(2,1)S(1)} collective-permute-done((bf16[96,128]{1,0:T(8,128)(2,1)S(1)}, bf16[96,128]{1,0:T(8,128)(2,1)S(1)}, u32[]{:S(2)}, u32[]{:S(2)}) %collective-permute-start.8) | collective-permute-done | bytes 24608 | tf_op jit(solution)/shard_map/ppermute | solution.py:417
  24.3 0.0 collective-permute-done.9.x_near
  24.3 0.1 shard_map.57.acc_ref
  24.4 0.0 collective-permute-done.10.t_one
  24.4 0.8 %collective-permute-done.11.t_two = bf16[192,128]{1,0:T(8,128)(2,1)S(1)} collective-permute-done((bf16[192,128]{1,0:T(8,128)(2,1)S(1)}, bf16[192,128]{1,0:T(8,128)(2,1)S(1)}, u32[]{:S(2)}, u32[]{:S(2)}) %collective-permute-start.11) | collective-permute-done | bytes 49184 | tf_op jit(solution)/shard_map/ppermute | solution.py:428
  25.1 0.5 %shard_map.58 = (bf16[768,128]{1,0:T(8,128)(2,1)S(1)}, bf16[192,128]{1,0:T(8,128)(2,1)S(1)}, bf16[192,128]{1,0:T(8,128)(2,1)S(1)}) custom-call(bf16[1152,128]{1,0:T(8,128)(2,1)S(1)} %bitcast.17, bf16[1152,128]{1,0:T(8,128)(2,1)S(1)} %bitcast.27, f32[768,128]{1,0:T(8,128)S(1)} %shard_map.57.acc_ref, bf16[192,128]{1,0:T(8,128)(2,1)S(1)} %collective-permute-done.10.t_one, ...), custom_call_target="tpu_custom_call" | custom-call | flops 4000000 | bytes 2097152 | tf_op jit(solution)/shard_map/pallas_call | solution.py:402
  25.6 1.7 %collective-permute-start.14 = (bf16[192,128]{1,0:T(8,128)(2,1)S(1)}, bf16[192,128]{1,0:T(8,128)(2,1)S(1)}, u32[]{:S(2)}, u32[]{:S(2)}) collective-permute-start(bf16[192,128]{1,0:T(8,128)(2,1)S(1)} %get-tuple-element.65), channel_id=1, source_target_pairs={{0,12},{1,5},{2,14},{3,7},{4,8},{5,1},{6,10},{7,3},{8,4},{9,13},{1... | collective-permute-start | bytes 147464 | tf_op jit(solution)/shard_map/ppermute | solution.py:428
  27.3 0.1 shard_map.59
  27.4 0.1 collective-permute-start.12
  27.5 1.3 %collective-permute-start.13 = (bf16[96,128]{1,0:T(8,128)(2,1)S(1)}, bf16[96,128]{1,0:T(8,128)(2,1)S(1)}, u32[]{:S(2)}, u32[]{:S(2)}) collective-permute-start(bf16[96,128]{1,0:T(8,128)(2,1)S(1)} %get-tuple-element.64), channel_id=1, source_target_pairs={{0,1},{1,0},{2,3},{3,2},{4,5},{5,4},{6,7},{7,6},{8,9},{9,8},{10,11... | collective-permute-start | bytes 73736 | tf_op jit(solution)/shard_map/ppermute | solution.py:417
  28.8 1.3 %shard_map.60.acc_ref = f32[768,128]{1,0:T(8,128)S(1)} custom-call(bf16[768,128]{1,0:T(8,128)(2,1)S(1)} %get-tuple-element.62.f_ref.refs_0_, bf16[1152,128]{1,0:T(8,128)(2,1)S(1)} %bitcast.19, bf16[768,128]{1,0:T(8,128)(2,1)S(1)} %get-tuple-element.54.f_ref.refs_0_.refs_2_, bf16[1152,128]{1,0:T(8,128)(2,1)S(1)} %bitcast.29), custom_call_target="tpu_custom_call" | custom-call | flops 8000000 | bytes 2097152 | tf_op jit(solution)/shard_map/pallas_call | solution.py:402
  30.1 0.8 %collective-permute-done.12.x_far = bf16[96,128]{1,0:T(8,128)(2,1)S(1)} collective-permute-done((bf16[96,128]{1,0:T(8,128)(2,1)S(1)}, bf16[96,128]{1,0:T(8,128)(2,1)S(1)}, u32[]{:S(2)}, u32[]{:S(2)}) %collective-permute-start.12) | collective-permute-done | bytes 24608 | tf_op jit(solution)/shard_map/ppermute | solution.py:417
  30.9 0.1 shard_map.61.acc_ref
  31.0 0.7 %collective-permute-done.14.t_one = bf16[192,128]{1,0:T(8,128)(2,1)S(1)} collective-permute-done((bf16[192,128]{1,0:T(8,128)(2,1)S(1)}, bf16[192,128]{1,0:T(8,128)(2,1)S(1)}, u32[]{:S(2)}, u32[]{:S(2)}) %collective-permute-start.14) | collective-permute-done | bytes 49184 | tf_op jit(solution)/shard_map/ppermute | solution.py:428
  31.7 0.2 collective-permute-done.15.t_two
  31.9 0.8 %shard_map.62 = bf16[768,128]{1,0:T(8,128)(2,1)} custom-call(bf16[1152,128]{1,0:T(8,128)(2,1)S(1)} %bitcast.21, f32[768,128]{1,0:T(8,128)S(1)} %shard_map.61.acc_ref, bf16[192,128]{1,0:T(8,128)(2,1)S(1)} %collective-permute-done.14.t_one, bf16[192,128]{1,0:T(8,128)(2,1)S(1)} %collective-permute-done.15.t_two), custom_call_target="tpu_custom_call" | custom-call | flops 1000000 | bytes 2097152 | tf_op jit(solution)/shard_map/pallas_call | solution.py:402
  (9 shorter events, 0.0 us)
Async XLA Ops:
  0.0 6.7 %copy-start = (bf16[4,3,3,2,2,2,4,128]{7,6,5,4,3,2,1,0:T(4,128)(2,1)S(1)}, bf16[4,3,3,2,2,2,4,128]{7,6,5,4,3,2,1,0:T(4,128)(2,1)}, u32[]{:S(2)}) copy-start(bf16[4,3,3,2,2,2,4,128]{7,6,5,4,3,2,1,0:T(4,128)(2,1)} %param.5) | copy-start | bytes 884740
  0.0 6.7 %copy-start.1 = (bf16[4,4,3,2,2,4,128]{6,5,4,3,2,1,0:T(4,128)(2,1)S(1)}, bf16[4,4,3,2,2,4,128]{6,5,4,3,2,1,0:T(4,128)(2,1)}, u32[]{:S(2)}) copy-start(bf16[4,4,3,2,2,4,128]{6,5,4,3,2,1,0:T(4,128)(2,1)} %param.4) | copy-start | bytes 589828
  1.1 9.3 %collective-permute-start.2 = (bf16[192,128]{1,0:T(8,128)(2,1)S(1)}, bf16[192,128]{1,0:T(8,128)(2,1)S(1)}, u32[]{:S(2)}, u32[]{:S(2)}) collective-permute-start(bf16[192,128]{1,0:T(8,128)(2,1)S(1)} %get-tuple-element.41), channel_id=1, source_target_pairs={{0,4},{1,13},{2,6},{3,15},{4,0},{5,9},{6,2},{7,11},{8,12},{9,5},{1... | collective-permute-start | bytes 147464 | tf_op jit(solution)/shard_map/ppermute | solution.py:428
  4.2 6.2 %collective-permute-start.3 = (bf16[192,128]{1,0:T(8,128)(2,1)S(1)}, bf16[192,128]{1,0:T(8,128)(2,1)S(1)}, u32[]{:S(2)}, u32[]{:S(2)}) collective-permute-start(bf16[192,128]{1,0:T(8,128)(2,1)S(1)} %get-tuple-element.42), channel_id=1, source_target_pairs={{0,12},{1,5},{2,14},{3,7},{4,8},{5,1},{6,10},{7,3},{8,4},{9,13},{1... | collective-permute-start | bytes 147464 | tf_op jit(solution)/shard_map/ppermute | solution.py:428
  6.8 3.5 %collective-permute-start = (bf16[96,128]{1,0:T(8,128)(2,1)S(1)}, bf16[96,128]{1,0:T(8,128)(2,1)S(1)}, u32[]{:S(2)}, u32[]{:S(2)}) collective-permute-start(bf16[96,128]{1,0:T(8,128)(2,1)S(1)} %get-tuple-element.39), channel_id=1, source_target_pairs={{0,3},{1,2},{2,1},{3,0},{4,7},{5,6},{6,5},{7,4},{8,11},{9,10},{10,... | collective-permute-start | bytes 73736 | tf_op jit(solution)/shard_map/ppermute | solution.py:417
  7.1 3.3 %collective-permute-start.1 = (bf16[96,128]{1,0:T(8,128)(2,1)S(1)}, bf16[96,128]{1,0:T(8,128)(2,1)S(1)}, u32[]{:S(2)}, u32[]{:S(2)}) collective-permute-start(bf16[96,128]{1,0:T(8,128)(2,1)S(1)} %get-tuple-element.40), channel_id=1, source_target_pairs={{0,1},{1,0},{2,3},{3,2},{4,5},{5,4},{6,7},{7,6},{8,9},{9,8},{10,11... | collective-permute-start | bytes 73736 | tf_op jit(solution)/shard_map/ppermute | solution.py:417
  9.4 1.0 %copy-start.2 = (bf16[2,6,6,2,2,4,128]{6,5,4,3,2,1,0:T(4,128)(2,1)S(1)}, bf16[2,6,6,2,2,4,128]{6,5,4,3,2,1,0:T(4,128)(2,1)}, u32[]{:S(2)}) copy-start(bf16[2,6,6,2,2,4,128]{6,5,4,3,2,1,0:T(4,128)(2,1)} %param.7) | copy-start | bytes 884740
  11.0 4.0 %copy-start.3 = (bf16[2,6,6,2,2,4,128]{6,5,4,3,2,1,0:T(4,128)(2,1)S(1)}, bf16[2,6,6,2,2,4,128]{6,5,4,3,2,1,0:T(4,128)(2,1)}, u32[]{:S(2)}) copy-start(bf16[2,6,6,2,2,4,128]{6,5,4,3,2,1,0:T(4,128)(2,1)} %param.6) | copy-start | bytes 884740
  11.0 6.0 %collective-permute-start.6 = (bf16[192,128]{1,0:T(8,128)(2,1)S(1)}, bf16[192,128]{1,0:T(8,128)(2,1)S(1)}, u32[]{:S(2)}, u32[]{:S(2)}) collective-permute-start(bf16[192,128]{1,0:T(8,128)(2,1)S(1)} %get-tuple-element.49), channel_id=1, source_target_pairs={{0,12},{1,5},{2,14},{3,7},{4,8},{5,1},{6,10},{7,3},{8,4},{9,13},{1... | collective-permute-start | bytes 147464 | tf_op jit(solution)/shard_map/ppermute | solution.py:428
  13.2 4.4 %collective-permute-start.7 = (bf16[192,128]{1,0:T(8,128)(2,1)S(1)}, bf16[192,128]{1,0:T(8,128)(2,1)S(1)}, u32[]{:S(2)}, u32[]{:S(2)}) collective-permute-start(bf16[192,128]{1,0:T(8,128)(2,1)S(1)} %get-tuple-element.50), channel_id=1, source_target_pairs={{0,4},{1,13},{2,6},{3,15},{4,0},{5,9},{6,2},{7,11},{8,12},{9,5},{1... | collective-permute-start | bytes 147464 | tf_op jit(solution)/shard_map/ppermute | solution.py:428
  13.3 3.5 %collective-permute-start.4 = (bf16[96,128]{1,0:T(8,128)(2,1)S(1)}, bf16[96,128]{1,0:T(8,128)(2,1)S(1)}, u32[]{:S(2)}, u32[]{:S(2)}) collective-permute-start(bf16[96,128]{1,0:T(8,128)(2,1)S(1)} %get-tuple-element.47), channel_id=1, source_target_pairs={{0,3},{1,2},{2,1},{3,0},{4,7},{5,6},{6,5},{7,4},{8,11},{9,10},{10,... | collective-permute-start | bytes 73736 | tf_op jit(solution)/shard_map/ppermute | solution.py:417
  13.4 3.5 %collective-permute-start.5 = (bf16[96,128]{1,0:T(8,128)(2,1)S(1)}, bf16[96,128]{1,0:T(8,128)(2,1)S(1)}, u32[]{:S(2)}, u32[]{:S(2)}) collective-permute-start(bf16[96,128]{1,0:T(8,128)(2,1)S(1)} %get-tuple-element.48), channel_id=1, source_target_pairs={{0,1},{1,0},{2,3},{3,2},{4,5},{5,4},{6,7},{7,6},{8,9},{9,8},{10,11... | collective-permute-start | bytes 73736 | tf_op jit(solution)/shard_map/ppermute | solution.py:417
  17.8 6.6 %collective-permute-start.10 = (bf16[192,128]{1,0:T(8,128)(2,1)S(1)}, bf16[192,128]{1,0:T(8,128)(2,1)S(1)}, u32[]{:S(2)}, u32[]{:S(2)}) collective-permute-start(bf16[192,128]{1,0:T(8,128)(2,1)S(1)} %get-tuple-element.57), channel_id=1, source_target_pairs={{0,4},{1,13},{2,6},{3,15},{4,0},{5,9},{6,2},{7,11},{8,12},{9,5},{1... | collective-permute-start | bytes 147464 | tf_op jit(solution)/shard_map/ppermute | solution.py:428
  19.2 5.9 %collective-permute-start.11 = (bf16[192,128]{1,0:T(8,128)(2,1)S(1)}, bf16[192,128]{1,0:T(8,128)(2,1)S(1)}, u32[]{:S(2)}, u32[]{:S(2)}) collective-permute-start(bf16[192,128]{1,0:T(8,128)(2,1)S(1)} %get-tuple-element.58), channel_id=1, source_target_pairs={{0,12},{1,5},{2,14},{3,7},{4,8},{5,1},{6,10},{7,3},{8,4},{9,13},{1... | collective-permute-start | bytes 147464 | tf_op jit(solution)/shard_map/ppermute | solution.py:428
  20.9 3.3 %collective-permute-start.8 = (bf16[96,128]{1,0:T(8,128)(2,1)S(1)}, bf16[96,128]{1,0:T(8,128)(2,1)S(1)}, u32[]{:S(2)}, u32[]{:S(2)}) collective-permute-start(bf16[96,128]{1,0:T(8,128)(2,1)S(1)} %get-tuple-element.55), channel_id=1, source_target_pairs={{0,3},{1,2},{2,1},{3,0},{4,7},{5,6},{6,5},{7,4},{8,11},{9,10},{10,... | collective-permute-start | bytes 73736 | tf_op jit(solution)/shard_map/ppermute | solution.py:417
  21.0 3.3 %collective-permute-start.9 = (bf16[96,128]{1,0:T(8,128)(2,1)S(1)}, bf16[96,128]{1,0:T(8,128)(2,1)S(1)}, u32[]{:S(2)}, u32[]{:S(2)}) collective-permute-start(bf16[96,128]{1,0:T(8,128)(2,1)S(1)} %get-tuple-element.56), channel_id=1, source_target_pairs={{0,1},{1,0},{2,3},{3,2},{4,5},{5,4},{6,7},{7,6},{8,9},{9,8},{10,11... | collective-permute-start | bytes 73736 | tf_op jit(solution)/shard_map/ppermute | solution.py:417
  25.6 6.1 %collective-permute-start.14 = (bf16[192,128]{1,0:T(8,128)(2,1)S(1)}, bf16[192,128]{1,0:T(8,128)(2,1)S(1)}, u32[]{:S(2)}, u32[]{:S(2)}) collective-permute-start(bf16[192,128]{1,0:T(8,128)(2,1)S(1)} %get-tuple-element.65), channel_id=1, source_target_pairs={{0,12},{1,5},{2,14},{3,7},{4,8},{5,1},{6,10},{7,3},{8,4},{9,13},{1... | collective-permute-start | bytes 147464 | tf_op jit(solution)/shard_map/ppermute | solution.py:428
  27.3 4.6 %collective-permute-start.15 = (bf16[192,128]{1,0:T(8,128)(2,1)S(1)}, bf16[192,128]{1,0:T(8,128)(2,1)S(1)}, u32[]{:S(2)}, u32[]{:S(2)}) collective-permute-start(bf16[192,128]{1,0:T(8,128)(2,1)S(1)} %get-tuple-element.66), channel_id=1, source_target_pairs={{0,4},{1,13},{2,6},{3,15},{4,0},{5,9},{6,2},{7,11},{8,12},{9,5},{1... | collective-permute-start | bytes 147464 | tf_op jit(solution)/shard_map/ppermute | solution.py:428
  27.4 3.5 %collective-permute-start.12 = (bf16[96,128]{1,0:T(8,128)(2,1)S(1)}, bf16[96,128]{1,0:T(8,128)(2,1)S(1)}, u32[]{:S(2)}, u32[]{:S(2)}) collective-permute-start(bf16[96,128]{1,0:T(8,128)(2,1)S(1)} %get-tuple-element.63), channel_id=1, source_target_pairs={{0,3},{1,2},{2,1},{3,0},{4,7},{5,6},{6,5},{7,4},{8,11},{9,10},{10,... | collective-permute-start | bytes 73736 | tf_op jit(solution)/shard_map/ppermute | solution.py:417
  27.5 3.4 %collective-permute-start.13 = (bf16[96,128]{1,0:T(8,128)(2,1)S(1)}, bf16[96,128]{1,0:T(8,128)(2,1)S(1)}, u32[]{:S(2)}, u32[]{:S(2)}) collective-permute-start(bf16[96,128]{1,0:T(8,128)(2,1)S(1)} %get-tuple-element.64), channel_id=1, source_target_pairs={{0,1},{1,0},{2,3},{3,2},{4,5},{5,4},{6,7},{7,6},{8,9},{9,8},{10,11... | collective-permute-start | bytes 73736 | tf_op jit(solution)/shard_map/ppermute | solution.py:417

commit v20 on v11

--- a/solution.py
+++ b/solution.py
@@ -313,7 +313,7 @@
     return out
 
 
-def join_x_kernel(parity, links_ref, acc_ref, x_far, x_near, out_ref):
+def join_x(links_ref, acc_ref, x_far, x_near, parity, out_ref):
     even = even_device("gx")
     _, x_idx = site_masks()
     sign = jnp.where(x_idx == 3, -1.0, 1.0).astype(F32)
@@ -365,19 +365,22 @@
         done(r)
 
 
-def odd_kernel(links_ref, clover_ref, acc_ref, t_one, t_two, out_ref, *refs):
-    outs, summed = refs[:2], refs[2]
-    join_t(links_ref, acc_ref, t_one, t_two, 0, summed)
+def odd_kernel(links_ref, clover_ref, acc_ref, t_one, t_two, x_far, x_near, out_ref, *refs):
+    outs, summed, both = refs[:2], refs[2], refs[3]
+    join_x(links_ref, acc_ref, x_far, x_near, 0, both)
+    join_t(links_ref, both, t_one, t_two, 0, summed)
     clover_to(clover_ref, lambda r: load_field(summed, r), out_ref, 1.0)
     send_t(out_ref, links_ref, 1, *outs)
 
 
-def even_kernel(links_ref, acc_ref, t_one, t_two, out_ref, *outs):
-    join_t(links_ref, acc_ref, t_one, t_two, 1, out_ref, -KAPPA2)
+def even_kernel(links_ref, acc_ref, t_one, t_two, x_far, x_near, out_ref, *refs):
+    outs, both = refs[:2], refs[2]
+    join_x(links_ref, acc_ref, x_far, x_near, 1, both)
+    join_t(links_ref, both, t_one, t_two, 1, out_ref, -KAPPA2)
     send_t(out_ref, links_ref, 0, *outs)
 
 
-def last_kernel(links_ref, acc_ref, t_one, t_two, out_hbm, held, sems):
+def last_kernel(links_ref, acc_ref, t_one, t_two, x_far, x_near, out_hbm, held, sems, both):
     part = held.shape[0] // RHS
     copies = []
 
@@ -386,7 +389,8 @@
         copies.append(pltpu.make_async_copy(held.at[rows], out_hbm.at[rows], sems.at[r]))
         copies[-1].start()
 
-    join_t(links_ref, acc_ref, t_one, t_two, 1, held, -KAPPA2, done)
+    join_x(links_ref, acc_ref, x_far, x_near, 1, both)
+    join_t(links_ref, both, t_one, t_two, 1, held, -KAPPA2, done)
     for copy in copies:
         copy.wait()
 
@@ -454,21 +458,20 @@
             functools.partial(interior_kernel, parity, bool(parity)),
             (here, links, *base), SUM, 8_000_000 if parity else 5_000_000,
         )
-        acc, = call(functools.partial(join_x_kernel, parity), (links, acc, x_far, x_near), SUM, 1_000_000)
         before = f
         if parity == 0:
             f, t_one, t_two = call(
-                odd_kernel, (links, odd, acc, t_one, t_two), FIELD + T_HALOS, 4_000_000,
-                [pltpu.VMEM((ROWS, 128), BF16)],
+                odd_kernel, (links, odd, acc, t_one, t_two, x_far, x_near), FIELD + T_HALOS, 4_000_000,
+                [pltpu.VMEM((ROWS, 128), BF16), pltpu.VMEM((ROWS, 128), F32)],
             )
         elif hop == 1:
             f, t_one, t_two = call(
-                even_kernel, (links, acc, t_one, t_two), FIELD + T_HALOS, 2_000_000
+                even_kernel, (links, acc, t_one, t_two, x_far, x_near), FIELD + T_HALOS, 2_000_000, [pltpu.VMEM((ROWS, 128), F32)]
             )
         else:
             out, = call(
-                last_kernel, (links, acc, t_one, t_two), FIELD, 1_000_000,
-                [pltpu.VMEM((ROWS, 128), BF16), pltpu.SemaphoreType.DMA((RHS,))], out_space=pltpu.HBM,
+                last_kernel, (links, acc, t_one, t_two, x_far, x_near), FIELD, 1_000_000,
+                [pltpu.VMEM((ROWS, 128), BF16), pltpu.SemaphoreType.DMA((RHS,)), pltpu.VMEM((ROWS, 128), F32)], out_space=pltpu.HBM,
             )
     return out.reshape(shape)
 

time: 31.8 us -> 32 us (level)
    pallas_call x17 -> x13, Pallas kernels: 8.38 us -> 8.35 us  [call(): pl.pallas_call(kernel, out_shape=tuple((jax.ShapeDtypeStruct(shape, dtype...]
  transfers between devices with their start and end apart: 16 -> 16, of which waited for: 7 -> 7; matrix products, arithmetic and copies ran while one was open for 0% -> 0% of each run, Pallas kernels for 17% -> 15%
where the time goes in v20:
time: 32 us; the launch traced here: 31.9 us
  starting transfers between devices  19.1 us (60%)
  Pallas kernels  8.35 us (26%)
  waiting for transfers between devices  4.23 us (13%)
    ppermute x8, starting transfers between devices, swap_t(): return lax.ppermute(value, ('ta', 'gx'), pairs)  12.5 us
    pallas_call x13, Pallas kernels, call(): pl.pallas_call(kernel, out_shape=tuple((jax.ShapeDtypeStruct(shape, dtype...  8.35 us
    ppermute x8, starting transfers between devices, swap(): return lax.ppermute(value, axis, pairs)  6.66 us
    ppermute x8, waiting for transfers between devices, swap(): return lax.ppermute(value, axis, pairs)  2.92 us
    ppermute x8, waiting for transfers between devices, swap_t(): return lax.ppermute(value, ('ta', 'gx'), pairs)  1.31 us
  transfers between devices with their start and end apart: 16, of which 7 were waited for; matrix products, arithmetic and copies ran while one was open for 0% of the time, Pallas kernels for 15%

profile of v20, /device:TPU:0, one launch (start us, length us, event | category | flops | bytes accessed | tf_op | source)
XLA Modules:
  0.0 31.9 jit_solution(1327390379881375506)
XLA Ops:
  0.0 1.1 %shard_map.48 = (bf16[192,128]{1,0:T(8,128)(2,1)S(1)}, bf16[192,128]{1,0:T(8,128)(2,1)S(1)}) custom-call(bf16[768,128]{1,0:T(8,128)(2,1)} %bitcast.18, bf16[1152,128]{1,0:T(8,128)(2,1)} %bitcast.5), custom_call_target="tpu_custom_call" | custom-call | flops 1500000 | bytes 2097152 | tf_op jit(solution)/shard_map/pallas_call | solution.py:406
  1.1 3.1 %collective-permute-start = (bf16[192,128]{1,0:T(8,128)(2,1)S(1)}, bf16[192,128]{1,0:T(8,128)(2,1)S(1)}, u32[]{:S(2)}, u32[]{:S(2)}) collective-permute-start(bf16[192,128]{1,0:T(8,128)(2,1)S(1)} %get-tuple-element.39), channel_id=1, source_target_pairs={{0,4},{1,13},{2,6},{3,15},{4,0},{5,9},{6,2},{7,11},{8,12},{9,5},{1... | collective-permute-start | bytes 147464 | tf_op jit(solution)/shard_map/ppermute | solution.py:432
  4.2 2.5 %collective-permute-start.1 = (bf16[192,128]{1,0:T(8,128)(2,1)S(1)}, bf16[192,128]{1,0:T(8,128)(2,1)S(1)}, u32[]{:S(2)}, u32[]{:S(2)}) collective-permute-start(bf16[192,128]{1,0:T(8,128)(2,1)S(1)} %get-tuple-element.40), channel_id=1, source_target_pairs={{0,12},{1,5},{2,14},{3,7},{4,8},{5,1},{6,10},{7,3},{8,4},{9,13},{1... | collective-permute-start | bytes 147464 | tf_op jit(solution)/shard_map/ppermute | solution.py:432
  6.7 0.1 shard_map.46
  6.8 0.0 copy-start.2
  6.8 0.3 collective-permute-start.2
  7.1 1.4 %collective-permute-start.3 = (bf16[96,128]{1,0:T(8,128)(2,1)S(1)}, bf16[96,128]{1,0:T(8,128)(2,1)S(1)}, u32[]{:S(2)}, u32[]{:S(2)}) collective-permute-start(bf16[96,128]{1,0:T(8,128)(2,1)S(1)} %get-tuple-element.42), channel_id=1, source_target_pairs={{0,1},{1,0},{2,3},{3,2},{4,5},{5,4},{6,7},{7,6},{8,9},{9,8},{10,11... | collective-permute-start | bytes 73736 | tf_op jit(solution)/shard_map/ppermute | solution.py:421
  8.5 1.0 %shard_map.47.acc_ref = f32[768,128]{1,0:T(8,128)S(1)} custom-call(bf16[768,128]{1,0:T(8,128)(2,1)S(1)} %bitcast.20, bf16[1152,128]{1,0:T(8,128)(2,1)S(1)} %bitcast.7), custom_call_target="tpu_custom_call" | custom-call | flops 5000000 | bytes 2097152 | tf_op jit(solution)/shard_map/pallas_call | solution.py:406
  9.5 0.9 %collective-permute-done.2.x_far = bf16[96,128]{1,0:T(8,128)(2,1)S(1)} collective-permute-done((bf16[96,128]{1,0:T(8,128)(2,1)S(1)}, bf16[96,128]{1,0:T(8,128)(2,1)S(1)}, u32[]{:S(2)}, u32[]{:S(2)}) %collective-permute-start.2) | collective-permute-done | bytes 24608 | tf_op jit(solution)/shard_map/ppermute | solution.py:421
  10.3 0.0 collective-permute-done.3.x_near
  10.3 0.0 collective-permute-done.t_one
  10.3 0.0 collective-permute-done.1.t_two
  10.4 0.6 %shard_map.49 = (bf16[768,128]{1,0:T(8,128)(2,1)S(1)}, bf16[192,128]{1,0:T(8,128)(2,1)S(1)}, bf16[192,128]{1,0:T(8,128)(2,1)S(1)}) custom-call(bf16[1152,128]{1,0:T(8,128)(2,1)S(1)} %bitcast.8, bf16[1152,128]{1,0:T(8,128)(2,1)S(1)} %bitcast.22, f32[768,128]{1,0:T(8,128)S(1)} %shard_map.47.acc_ref, bf16[192,128]{1,0:T(8,128)(2,1)S(1)} %collective-permute-done.t_one, ...), custom_call_target="tpu_custom_call" | custom-call | flops 4000000 | bytes 2097152 | tf_op jit(solution)/shard_map/pallas_call | solution.py:406
  11.0 0.0 copy-start.3
  11.0 0.5 %collective-permute-start.4 = (bf16[192,128]{1,0:T(8,128)(2,1)S(1)}, bf16[192,128]{1,0:T(8,128)(2,1)S(1)}, u32[]{:S(2)}, u32[]{:S(2)}) collective-permute-start(bf16[192,128]{1,0:T(8,128)(2,1)S(1)} %get-tuple-element.47), channel_id=1, source_target_pairs={{0,4},{1,13},{2,6},{3,15},{4,0},{5,9},{6,2},{7,11},{8,12},{9,5},{1... | collective-permute-start | bytes 147464 | tf_op jit(solution)/shard_map/ppermute | solution.py:432
  11.5 1.8 %collective-permute-start.5 = (bf16[192,128]{1,0:T(8,128)(2,1)S(1)}, bf16[192,128]{1,0:T(8,128)(2,1)S(1)}, u32[]{:S(2)}, u32[]{:S(2)}) collective-permute-start(bf16[192,128]{1,0:T(8,128)(2,1)S(1)} %get-tuple-element.48), channel_id=1, source_target_pairs={{0,12},{1,5},{2,14},{3,7},{4,8},{5,1},{6,10},{7,3},{8,4},{9,13},{1... | collective-permute-start | bytes 147464 | tf_op jit(solution)/shard_map/ppermute | solution.py:432
  13.3 0.1 shard_map.50
  13.4 0.1 collective-permute-start.6
  13.5 1.6 %collective-permute-start.7 = (bf16[96,128]{1,0:T(8,128)(2,1)S(1)}, bf16[96,128]{1,0:T(8,128)(2,1)S(1)}, u32[]{:S(2)}, u32[]{:S(2)}) collective-permute-start(bf16[96,128]{1,0:T(8,128)(2,1)S(1)} %get-tuple-element.50), channel_id=1, source_target_pairs={{0,1},{1,0},{2,3},{3,2},{4,5},{5,4},{6,7},{7,6},{8,9},{9,8},{10,11... | collective-permute-start | bytes 73736 | tf_op jit(solution)/shard_map/ppermute | solution.py:421
  15.1 0.0 copy-done.3
  15.1 1.3 %shard_map.51.acc_ref = f32[768,128]{1,0:T(8,128)S(1)} custom-call(bf16[768,128]{1,0:T(8,128)(2,1)S(1)} %get-tuple-element.46.f_ref.refs_0_, bf16[1152,128]{1,0:T(8,128)(2,1)S(1)} %bitcast.10, bf16[768,128]{1,0:T(8,128)(2,1)S(1)} %bitcast.21, bf16[1152,128]{1,0:T(8,128)(2,1)S(1)} %bitcast.24), custom_call_target="tpu_custom_call" | custom-call | flops 8000000 | bytes 2097152 | tf_op jit(solution)/shard_map/pallas_call | solution.py:406
  16.4 0.6 %collective-permute-done.6.x_far = bf16[96,128]{1,0:T(8,128)(2,1)S(1)} collective-permute-done((bf16[96,128]{1,0:T(8,128)(2,1)S(1)}, bf16[96,128]{1,0:T(8,128)(2,1)S(1)}, u32[]{:S(2)}, u32[]{:S(2)}) %collective-permute-start.6) | collective-permute-done | bytes 24608 | tf_op jit(solution)/shard_map/ppermute | solution.py:421
  17.0 0.0 collective-permute-done.7.x_near
  17.0 0.0 collective-permute-done.4.t_one
  17.0 0.4 %collective-permute-done.5.t_two = bf16[192,128]{1,0:T(8,128)(2,1)S(1)} collective-permute-done((bf16[192,128]{1,0:T(8,128)(2,1)S(1)}, bf16[192,128]{1,0:T(8,128)(2,1)S(1)}, u32[]{:S(2)}, u32[]{:S(2)}) %collective-permute-start.5) | collective-permute-done | bytes 49184 | tf_op jit(solution)/shard_map/ppermute | solution.py:432
  17.4 0.3 shard_map.52
  17.7 0.7 %collective-permute-start.8 = (bf16[192,128]{1,0:T(8,128)(2,1)S(1)}, bf16[192,128]{1,0:T(8,128)(2,1)S(1)}, u32[]{:S(2)}, u32[]{:S(2)}) collective-permute-start(bf16[192,128]{1,0:T(8,128)(2,1)S(1)} %get-tuple-element.55), channel_id=1, source_target_pairs={{0,4},{1,13},{2,6},{3,15},{4,0},{5,9},{6,2},{7,11},{8,12},{9,5},{1... | collective-permute-start | bytes 147464 | tf_op jit(solution)/shard_map/ppermute | solution.py:432
  18.4 1.9 %collective-permute-start.9 = (bf16[192,128]{1,0:T(8,128)(2,1)S(1)}, bf16[192,128]{1,0:T(8,128)(2,1)S(1)}, u32[]{:S(2)}, u32[]{:S(2)}) collective-permute-start(bf16[192,128]{1,0:T(8,128)(2,1)S(1)} %get-tuple-element.56), channel_id=1, source_target_pairs={{0,12},{1,5},{2,14},{3,7},{4,8},{5,1},{6,10},{7,3},{8,4},{9,13},{1... | collective-permute-start | bytes 147464 | tf_op jit(solution)/shard_map/ppermute | solution.py:432
  20.3 0.1 shard_map.53
  20.4 0.1 collective-permute-start.10
  20.4 1.6 %collective-permute-start.11 = (bf16[96,128]{1,0:T(8,128)(2,1)S(1)}, bf16[96,128]{1,0:T(8,128)(2,1)S(1)}, u32[]{:S(2)}, u32[]{:S(2)}) collective-permute-start(bf16[96,128]{1,0:T(8,128)(2,1)S(1)} %get-tuple-element.58), channel_id=1, source_target_pairs={{0,1},{1,0},{2,3},{3,2},{4,5},{5,4},{6,7},{7,6},{8,9},{9,8},{10,11... | collective-permute-start | bytes 73736 | tf_op jit(solution)/shard_map/ppermute | solution.py:421
  22.0 1.0 %shard_map.54.acc_ref = f32[768,128]{1,0:T(8,128)S(1)} custom-call(bf16[768,128]{1,0:T(8,128)(2,1)S(1)} %get-tuple-element.54.f_ref.refs_0_.refs_2_, bf16[1152,128]{1,0:T(8,128)(2,1)S(1)} %bitcast.13), custom_call_target="tpu_custom_call" | custom-call | flops 5000000 | bytes 2097152 | tf_op jit(solution)/shard_map/pallas_call | solution.py:406
  23.0 0.9 %collective-permute-done.10.x_far = bf16[96,128]{1,0:T(8,128)(2,1)S(1)} collective-permute-done((bf16[96,128]{1,0:T(8,128)(2,1)S(1)}, bf16[96,128]{1,0:T(8,128)(2,1)S(1)}, u32[]{:S(2)}, u32[]{:S(2)}) %collective-permute-start.10) | collective-permute-done | bytes 24608 | tf_op jit(solution)/shard_map/ppermute | solution.py:421
  23.9 0.0 collective-permute-done.11.x_near
  23.9 0.0 collective-permute-done.8.t_one
  23.9 0.4 %collective-permute-done.9.t_two = bf16[192,128]{1,0:T(8,128)(2,1)S(1)} collective-permute-done((bf16[192,128]{1,0:T(8,128)(2,1)S(1)}, bf16[192,128]{1,0:T(8,128)(2,1)S(1)}, u32[]{:S(2)}, u32[]{:S(2)}) %collective-permute-start.9) | collective-permute-done | bytes 49184 | tf_op jit(solution)/shard_map/ppermute | solution.py:432
  24.3 0.6 %shard_map.55 = (bf16[768,128]{1,0:T(8,128)(2,1)S(1)}, bf16[192,128]{1,0:T(8,128)(2,1)S(1)}, bf16[192,128]{1,0:T(8,128)(2,1)S(1)}) custom-call(bf16[1152,128]{1,0:T(8,128)(2,1)S(1)} %bitcast.14, bf16[1152,128]{1,0:T(8,128)(2,1)S(1)} %bitcast.23, f32[768,128]{1,0:T(8,128)S(1)} %shard_map.54.acc_ref, bf16[192,128]{1,0:T(8,128)(2,1)S(1)} %collective-permute-done.8.t_one, ...), custom_call_target="tpu_custom_call" | custom-call | flops 4000000 | bytes 2097152 | tf_op jit(solution)/shard_map/pallas_call | solution.py:406
  24.9 0.1 collective-permute-start.12
  25.0 1.9 %collective-permute-start.13 = (bf16[192,128]{1,0:T(8,128)(2,1)S(1)}, bf16[192,128]{1,0:T(8,128)(2,1)S(1)}, u32[]{:S(2)}, u32[]{:S(2)}) collective-permute-start(bf16[192,128]{1,0:T(8,128)(2,1)S(1)} %get-tuple-element.64), channel_id=1, source_target_pairs={{0,12},{1,5},{2,14},{3,7},{4,8},{5,1},{6,10},{7,3},{8,4},{9,13},{1... | collective-permute-start | bytes 147464 | tf_op jit(solution)/shard_map/ppermute | solution.py:432
  26.9 0.1 shard_map.56
  27.0 0.1 collective-permute-start.14
  27.1 1.6 %collective-permute-start.15 = (bf16[96,128]{1,0:T(8,128)(2,1)S(1)}, bf16[96,128]{1,0:T(8,128)(2,1)S(1)}, u32[]{:S(2)}, u32[]{:S(2)}) collective-permute-start(bf16[96,128]{1,0:T(8,128)(2,1)S(1)} %get-tuple-element.66), channel_id=1, source_target_pairs={{0,1},{1,0},{2,3},{3,2},{4,5},{5,4},{6,7},{7,6},{8,9},{9,8},{10,11... | collective-permute-start | bytes 73736 | tf_op jit(solution)/shard_map/ppermute | solution.py:421
  28.7 1.3 %shard_map.57.acc_ref = f32[768,128]{1,0:T(8,128)S(1)} custom-call(bf16[768,128]{1,0:T(8,128)(2,1)S(1)} %get-tuple-element.62.f_ref.refs_0_, bf16[1152,128]{1,0:T(8,128)(2,1)S(1)} %bitcast.16, bf16[768,128]{1,0:T(8,128)(2,1)S(1)} %get-tuple-element.54.f_ref.refs_0_.refs_2_, bf16[1152,128]{1,0:T(8,128)(2,1)S(1)} %bitcast.25), custom_call_target="tpu_custom_call" | custom-call | flops 8000000 | bytes 2097152 | tf_op jit(solution)/shard_map/pallas_call | solution.py:406
  30.0 0.6 %collective-permute-done.14.x_far = bf16[96,128]{1,0:T(8,128)(2,1)S(1)} collective-permute-done((bf16[96,128]{1,0:T(8,128)(2,1)S(1)}, bf16[96,128]{1,0:T(8,128)(2,1)S(1)}, u32[]{:S(2)}, u32[]{:S(2)}) %collective-permute-start.14) | collective-permute-done | bytes 24608 | tf_op jit(solution)/shard_map/ppermute | solution.py:421
  30.5 0.0 collective-permute-done.15.x_near
  30.5 0.0 collective-permute-done.12.t_one
  30.5 0.5 %collective-permute-done.13.t_two = bf16[192,128]{1,0:T(8,128)(2,1)S(1)} collective-permute-done((bf16[192,128]{1,0:T(8,128)(2,1)S(1)}, bf16[192,128]{1,0:T(8,128)(2,1)S(1)}, u32[]{:S(2)}, u32[]{:S(2)}) %collective-permute-start.13) | collective-permute-done | bytes 49184 | tf_op jit(solution)/shard_map/ppermute | solution.py:432
  31.0 0.9 %shard_map.58 = bf16[768,128]{1,0:T(8,128)(2,1)} custom-call(bf16[1152,128]{1,0:T(8,128)(2,1)S(1)} %bitcast.17, f32[768,128]{1,0:T(8,128)S(1)} %shard_map.57.acc_ref, bf16[192,128]{1,0:T(8,128)(2,1)S(1)} %collective-permute-done.12.t_one, bf16[192,128]{1,0:T(8,128)(2,1)S(1)} %collective-permute-done.13.t_two, ...), custom_call_target="tpu_custom_call" | custom-call | flops 1000000 | bytes 2097152 | tf_op jit(solution)/shard_map/pallas_call | solution.py:406
  (5 shorter events, 0.0 us)
Async XLA Ops:
  0.0 6.7 %copy-start = (bf16[4,3,3,2,2,2,4,128]{7,6,5,4,3,2,1,0:T(4,128)(2,1)S(1)}, bf16[4,3,3,2,2,2,4,128]{7,6,5,4,3,2,1,0:T(4,128)(2,1)}, u32[]{:S(2)}) copy-start(bf16[4,3,3,2,2,2,4,128]{7,6,5,4,3,2,1,0:T(4,128)(2,1)} %param.5) | copy-start | bytes 884740
  0.0 6.7 %copy-start.1 = (bf16[4,4,3,2,2,4,128]{6,5,4,3,2,1,0:T(4,128)(2,1)S(1)}, bf16[4,4,3,2,2,4,128]{6,5,4,3,2,1,0:T(4,128)(2,1)}, u32[]{:S(2)}) copy-start(bf16[4,4,3,2,2,4,128]{6,5,4,3,2,1,0:T(4,128)(2,1)} %param.4) | copy-start | bytes 589828
  1.1 9.2 %collective-permute-start = (bf16[192,128]{1,0:T(8,128)(2,1)S(1)}, bf16[192,128]{1,0:T(8,128)(2,1)S(1)}, u32[]{:S(2)}, u32[]{:S(2)}) collective-permute-start(bf16[192,128]{1,0:T(8,128)(2,1)S(1)} %get-tuple-element.39), channel_id=1, source_target_pairs={{0,4},{1,13},{2,6},{3,15},{4,0},{5,9},{6,2},{7,11},{8,12},{9,5},{1... | collective-permute-start | bytes 147464 | tf_op jit(solution)/shard_map/ppermute | solution.py:432
  4.2 6.1 %collective-permute-start.1 = (bf16[192,128]{1,0:T(8,128)(2,1)S(1)}, bf16[192,128]{1,0:T(8,128)(2,1)S(1)}, u32[]{:S(2)}, u32[]{:S(2)}) collective-permute-start(bf16[192,128]{1,0:T(8,128)(2,1)S(1)} %get-tuple-element.40), channel_id=1, source_target_pairs={{0,12},{1,5},{2,14},{3,7},{4,8},{5,1},{6,10},{7,3},{8,4},{9,13},{1... | collective-permute-start | bytes 147464 | tf_op jit(solution)/shard_map/ppermute | solution.py:432
  6.8 3.6 %copy-start.2 = (bf16[2,6,6,2,2,4,128]{6,5,4,3,2,1,0:T(4,128)(2,1)S(1)}, bf16[2,6,6,2,2,4,128]{6,5,4,3,2,1,0:T(4,128)(2,1)}, u32[]{:S(2)}) copy-start(bf16[2,6,6,2,2,4,128]{6,5,4,3,2,1,0:T(4,128)(2,1)} %param.7) | copy-start | bytes 884740
  6.8 3.5 %collective-permute-start.2 = (bf16[96,128]{1,0:T(8,128)(2,1)S(1)}, bf16[96,128]{1,0:T(8,128)(2,1)S(1)}, u32[]{:S(2)}, u32[]{:S(2)}) collective-permute-start(bf16[96,128]{1,0:T(8,128)(2,1)S(1)} %get-tuple-element.41), channel_id=1, source_target_pairs={{0,3},{1,2},{2,1},{3,0},{4,7},{5,6},{6,5},{7,4},{8,11},{9,10},{10,... | collective-permute-start | bytes 73736 | tf_op jit(solution)/shard_map/ppermute | solution.py:421
  7.1 3.3 %collective-permute-start.3 = (bf16[96,128]{1,0:T(8,128)(2,1)S(1)}, bf16[96,128]{1,0:T(8,128)(2,1)S(1)}, u32[]{:S(2)}, u32[]{:S(2)}) collective-permute-start(bf16[96,128]{1,0:T(8,128)(2,1)S(1)} %get-tuple-element.42), channel_id=1, source_target_pairs={{0,1},{1,0},{2,3},{3,2},{4,5},{5,4},{6,7},{7,6},{8,9},{9,8},{10,11... | collective-permute-start | bytes 73736 | tf_op jit(solution)/shard_map/ppermute | solution.py:421
  11.0 4.1 %copy-start.3 = (bf16[2,6,6,2,2,4,128]{6,5,4,3,2,1,0:T(4,128)(2,1)S(1)}, bf16[2,6,6,2,2,4,128]{6,5,4,3,2,1,0:T(4,128)(2,1)}, u32[]{:S(2)}) copy-start(bf16[2,6,6,2,2,4,128]{6,5,4,3,2,1,0:T(4,128)(2,1)} %param.6) | copy-start | bytes 884740
  11.0 6.0 %collective-permute-start.4 = (bf16[192,128]{1,0:T(8,128)(2,1)S(1)}, bf16[192,128]{1,0:T(8,128)(2,1)S(1)}, u32[]{:S(2)}, u32[]{:S(2)}) collective-permute-start(bf16[192,128]{1,0:T(8,128)(2,1)S(1)} %get-tuple-element.47), channel_id=1, source_target_pairs={{0,4},{1,13},{2,6},{3,15},{4,0},{5,9},{6,2},{7,11},{8,12},{9,5},{1... | collective-permute-start | bytes 147464 | tf_op jit(solution)/shard_map/ppermute | solution.py:432
  11.5 5.9 %collective-permute-start.5 = (bf16[192,128]{1,0:T(8,128)(2,1)S(1)}, bf16[192,128]{1,0:T(8,128)(2,1)S(1)}, u32[]{:S(2)}, u32[]{:S(2)}) collective-permute-start(bf16[192,128]{1,0:T(8,128)(2,1)S(1)} %get-tuple-element.48), channel_id=1, source_target_pairs={{0,12},{1,5},{2,14},{3,7},{4,8},{5,1},{6,10},{7,3},{8,4},{9,13},{1... | collective-permute-start | bytes 147464 | tf_op jit(solution)/shard_map/ppermute | solution.py:432
  13.4 3.5 %collective-permute-start.6 = (bf16[96,128]{1,0:T(8,128)(2,1)S(1)}, bf16[96,128]{1,0:T(8,128)(2,1)S(1)}, u32[]{:S(2)}, u32[]{:S(2)}) collective-permute-start(bf16[96,128]{1,0:T(8,128)(2,1)S(1)} %get-tuple-element.49), channel_id=1, source_target_pairs={{0,3},{1,2},{2,1},{3,0},{4,7},{5,6},{6,5},{7,4},{8,11},{9,10},{10,... | collective-permute-start | bytes 73736 | tf_op jit(solution)/shard_map/ppermute | solution.py:421
  13.5 3.5 %collective-permute-start.7 = (bf16[96,128]{1,0:T(8,128)(2,1)S(1)}, bf16[96,128]{1,0:T(8,128)(2,1)S(1)}, u32[]{:S(2)}, u32[]{:S(2)}) collective-permute-start(bf16[96,128]{1,0:T(8,128)(2,1)S(1)} %get-tuple-element.50), channel_id=1, source_target_pairs={{0,1},{1,0},{2,3},{3,2},{4,5},{5,4},{6,7},{7,6},{8,9},{9,8},{10,11... | collective-permute-start | bytes 73736 | tf_op jit(solution)/shard_map/ppermute | solution.py:421
  17.7 6.2 %collective-permute-start.8 = (bf16[192,128]{1,0:T(8,128)(2,1)S(1)}, bf16[192,128]{1,0:T(8,128)(2,1)S(1)}, u32[]{:S(2)}, u32[]{:S(2)}) collective-permute-start(bf16[192,128]{1,0:T(8,128)(2,1)S(1)} %get-tuple-element.55), channel_id=1, source_target_pairs={{0,4},{1,13},{2,6},{3,15},{4,0},{5,9},{6,2},{7,11},{8,12},{9,5},{1... | collective-permute-start | bytes 147464 | tf_op jit(solution)/shard_map/ppermute | solution.py:432
  18.4 5.9 %collective-permute-start.9 = (bf16[192,128]{1,0:T(8,128)(2,1)S(1)}, bf16[192,128]{1,0:T(8,128)(2,1)S(1)}, u32[]{:S(2)}, u32[]{:S(2)}) collective-permute-start(bf16[192,128]{1,0:T(8,128)(2,1)S(1)} %get-tuple-element.56), channel_id=1, source_target_pairs={{0,12},{1,5},{2,14},{3,7},{4,8},{5,1},{6,10},{7,3},{8,4},{9,13},{1... | collective-permute-start | bytes 147464 | tf_op jit(solution)/shard_map/ppermute | solution.py:432
  20.4 3.5 %collective-permute-start.10 = (bf16[96,128]{1,0:T(8,128)(2,1)S(1)}, bf16[96,128]{1,0:T(8,128)(2,1)S(1)}, u32[]{:S(2)}, u32[]{:S(2)}) collective-permute-start(bf16[96,128]{1,0:T(8,128)(2,1)S(1)} %get-tuple-element.57), channel_id=1, source_target_pairs={{0,3},{1,2},{2,1},{3,0},{4,7},{5,6},{6,5},{7,4},{8,11},{9,10},{10,... | collective-permute-start | bytes 73736 | tf_op jit(solution)/shard_map/ppermute | solution.py:421
  20.4 3.5 %collective-permute-start.11 = (bf16[96,128]{1,0:T(8,128)(2,1)S(1)}, bf16[96,128]{1,0:T(8,128)(2,1)S(1)}, u32[]{:S(2)}, u32[]{:S(2)}) collective-permute-start(bf16[96,128]{1,0:T(8,128)(2,1)S(1)} %get-tuple-element.58), channel_id=1, source_target_pairs={{0,1},{1,0},{2,3},{3,2},{4,5},{5,4},{6,7},{7,6},{8,9},{9,8},{10,11... | collective-permute-start | bytes 73736 | tf_op jit(solution)/shard_map/ppermute | solution.py:421
  24.9 5.6 %collective-permute-start.12 = (bf16[192,128]{1,0:T(8,128)(2,1)S(1)}, bf16[192,128]{1,0:T(8,128)(2,1)S(1)}, u32[]{:S(2)}, u32[]{:S(2)}) collective-permute-start(bf16[192,128]{1,0:T(8,128)(2,1)S(1)} %get-tuple-element.63), channel_id=1, source_target_pairs={{0,4},{1,13},{2,6},{3,15},{4,0},{5,9},{6,2},{7,11},{8,12},{9,5},{1... | collective-permute-start | bytes 147464 | tf_op jit(solution)/shard_map/ppermute | solution.py:432
  25.0 6.1 %collective-permute-start.13 = (bf16[192,128]{1,0:T(8,128)(2,1)S(1)}, bf16[192,128]{1,0:T(8,128)(2,1)S(1)}, u32[]{:S(2)}, u32[]{:S(2)}) collective-permute-start(bf16[192,128]{1,0:T(8,128)(2,1)S(1)} %get-tuple-element.64), channel_id=1, source_target_pairs={{0,12},{1,5},{2,14},{3,7},{4,8},{5,1},{6,10},{7,3},{8,4},{9,13},{1... | collective-permute-start | bytes 147464 | tf_op jit(solution)/shard_map/ppermute | solution.py:432
  27.0 3.5 %collective-permute-start.14 = (bf16[96,128]{1,0:T(8,128)(2,1)S(1)}, bf16[96,128]{1,0:T(8,128)(2,1)S(1)}, u32[]{:S(2)}, u32[]{:S(2)}) collective-permute-start(bf16[96,128]{1,0:T(8,128)(2,1)S(1)} %get-tuple-element.65), channel_id=1, source_target_pairs={{0,3},{1,2},{2,1},{3,0},{4,7},{5,6},{6,5},{7,4},{8,11},{9,10},{10,... | collective-permute-start | bytes 73736 | tf_op jit(solution)/shard_map/ppermute | solution.py:421
  27.1 3.5 %collective-permute-start.15 = (bf16[96,128]{1,0:T(8,128)(2,1)S(1)}, bf16[96,128]{1,0:T(8,128)(2,1)S(1)}, u32[]{:S(2)}, u32[]{:S(2)}) collective-permute-start(bf16[96,128]{1,0:T(8,128)(2,1)S(1)} %get-tuple-element.66), channel_id=1, source_target_pairs={{0,1},{1,0},{2,3},{3,2},{4,5},{5,4},{6,7},{7,6},{8,9},{9,8},{10,11... | collective-permute-start | bytes 73736 | tf_op jit(solution)/shard_map/ppermute | solution.py:421

commit v21 on v11

--- a/solution.py
+++ b/solution.py
@@ -268,19 +268,20 @@
             field = get_field(r)[chi * 6:chi * 6 + 6]
             both = [vr + vi for vr, vi in field]
             for i in range(6):
-                one = two = three = None
+                re, im = matrix[i, i][0] * field[i][0], matrix[i, i][0] * field[i][1]
+                one = None
                 for j in range(6):
+                    if j == i:
+                        continue
                     vr, vi = field[j]
                     m, plus, minus = matrix[min(i, j), max(i, j)]
                     t_one = m * both[j]
-                    if i <= j:
-                        t_two, t_three = -(vi * plus), vr * minus
+                    one = t_one if one is None else one + t_one
+                    if i < j:
+                        re, im = re - vi * plus, im + vr * minus
                     else:
-                        t_two, t_three = vi * minus, -(vr * plus)
-                    one = t_one if one is None else one + t_one
-                    two = t_two if two is None else two + t_two
-                    three = t_three if three is None else three + t_three
-                store_pair(out_ref, r * 12 + chi * 6 + i, (one + two, one + three))
+                        re, im = re + vi * minus, im - vr * plus
+                store_pair(out_ref, r * 12 + chi * 6 + i, (re + one, im + one))
 
 
 def matvec(links, vector, adjoint):

time: 31.8 us -> 31.7 us (level)
  transfers between devices with their start and end apart: 16 -> 16, of which waited for: 7 -> 7; matrix products, arithmetic and copies ran while one was open for 0% -> 0% of each run, Pallas kernels for 17% -> 16%
where the time goes in v21:
time: 31.7 us; the launch traced here: 31.5 us
  starting transfers between devices  18.8 us (59%)
  Pallas kernels  8.14 us (26%)
  waiting for transfers between devices  4.37 us (14%)
    ppermute x8, starting transfers between devices, swap_t(): return lax.ppermute(value, ('ta', 'gx'), pairs)  12.4 us
    pallas_call x17, Pallas kernels, call(): pl.pallas_call(kernel, out_shape=tuple((jax.ShapeDtypeStruct(shape, dtype...  8.14 us
    ppermute x8, starting transfers between devices, swap(): return lax.ppermute(value, axis, pairs)  6.38 us
    ppermute x8, waiting for transfers between devices, swap(): return lax.ppermute(value, axis, pairs)  3.11 us
    ppermute x8, waiting for transfers between devices, swap_t(): return lax.ppermute(value, ('ta', 'gx'), pairs)  1.26 us
  transfers between devices with their start and end apart: 16, of which 7 were waited for; matrix products, arithmetic and copies ran while one was open for 0% of the time, Pallas kernels for 16%

profile of v21, /device:TPU:0, one launch (start us, length us, event | category | flops | bytes accessed | tf_op | source)
XLA Modules:
  0.0 31.5 jit_solution(11703006879592736183)
XLA Ops:
  0.0 1.1 %shard_map.49 = (bf16[192,128]{1,0:T(8,128)(2,1)S(1)}, bf16[192,128]{1,0:T(8,128)(2,1)S(1)}) custom-call(bf16[768,128]{1,0:T(8,128)(2,1)} %bitcast.22, bf16[1152,128]{1,0:T(8,128)(2,1)} %bitcast.5), custom_call_target="tpu_custom_call" | custom-call | flops 1500000 | bytes 2097152 | tf_op jit(solution)/shard_map/pallas_call | solution.py:403
  1.1 3.1 %collective-permute-start.2 = (bf16[192,128]{1,0:T(8,128)(2,1)S(1)}, bf16[192,128]{1,0:T(8,128)(2,1)S(1)}, u32[]{:S(2)}, u32[]{:S(2)}) collective-permute-start(bf16[192,128]{1,0:T(8,128)(2,1)S(1)} %get-tuple-element.41), channel_id=1, source_target_pairs={{0,4},{1,13},{2,6},{3,15},{4,0},{5,9},{6,2},{7,11},{8,12},{9,5},{1... | collective-permute-start | bytes 147464 | tf_op jit(solution)/shard_map/ppermute | solution.py:429
  4.2 2.5 %collective-permute-start.3 = (bf16[192,128]{1,0:T(8,128)(2,1)S(1)}, bf16[192,128]{1,0:T(8,128)(2,1)S(1)}, u32[]{:S(2)}, u32[]{:S(2)}) collective-permute-start(bf16[192,128]{1,0:T(8,128)(2,1)S(1)} %get-tuple-element.42), channel_id=1, source_target_pairs={{0,12},{1,5},{2,14},{3,7},{4,8},{5,1},{6,10},{7,3},{8,4},{9,13},{1... | collective-permute-start | bytes 147464 | tf_op jit(solution)/shard_map/ppermute | solution.py:429
  6.7 0.1 shard_map.46
  6.8 0.3 collective-permute-start
  7.1 1.4 %collective-permute-start.1 = (bf16[96,128]{1,0:T(8,128)(2,1)S(1)}, bf16[96,128]{1,0:T(8,128)(2,1)S(1)}, u32[]{:S(2)}, u32[]{:S(2)}) collective-permute-start(bf16[96,128]{1,0:T(8,128)(2,1)S(1)} %get-tuple-element.40), channel_id=1, source_target_pairs={{0,1},{1,0},{2,3},{3,2},{4,5},{5,4},{6,7},{7,6},{8,9},{9,8},{10,11... | collective-permute-start | bytes 73736 | tf_op jit(solution)/shard_map/ppermute | solution.py:418
  8.5 1.0 %shard_map.47.acc_ref = f32[768,128]{1,0:T(8,128)S(1)} custom-call(bf16[768,128]{1,0:T(8,128)(2,1)S(1)} %bitcast.24, bf16[1152,128]{1,0:T(8,128)(2,1)S(1)} %bitcast.7), custom_call_target="tpu_custom_call" | custom-call | flops 5000000 | bytes 2097152 | tf_op jit(solution)/shard_map/pallas_call | solution.py:403
  9.4 0.0 copy-start.2
  9.5 0.9 %collective-permute-done.x_far = bf16[96,128]{1,0:T(8,128)(2,1)S(1)} collective-permute-done((bf16[96,128]{1,0:T(8,128)(2,1)S(1)}, bf16[96,128]{1,0:T(8,128)(2,1)S(1)}, u32[]{:S(2)}, u32[]{:S(2)}) %collective-permute-start) | collective-permute-done | bytes 24608 | tf_op jit(solution)/shard_map/ppermute | solution.py:418
  10.3 0.0 collective-permute-done.1.x_near
  10.3 0.1 shard_map.48.acc_ref
  10.4 0.0 collective-permute-done.2.t_one
  10.4 0.0 collective-permute-done.3.t_two
  10.5 0.5 %shard_map.50 = (bf16[768,128]{1,0:T(8,128)(2,1)S(1)}, bf16[192,128]{1,0:T(8,128)(2,1)S(1)}, bf16[192,128]{1,0:T(8,128)(2,1)S(1)}) custom-call(bf16[1152,128]{1,0:T(8,128)(2,1)S(1)} %bitcast.9, bf16[1152,128]{1,0:T(8,128)(2,1)S(1)} %bitcast.26, f32[768,128]{1,0:T(8,128)S(1)} %shard_map.48.acc_ref, bf16[192,128]{1,0:T(8,128)(2,1)S(1)} %collective-permute-done.2.t_one, ...), custom_call_target="tpu_custom_call" | custom-call | flops 4000000 | bytes 2097152 | tf_op jit(solution)/shard_map/pallas_call | solution.py:403
  10.9 0.0 copy-start.3
  10.9 0.7 %collective-permute-start.6 = (bf16[192,128]{1,0:T(8,128)(2,1)S(1)}, bf16[192,128]{1,0:T(8,128)(2,1)S(1)}, u32[]{:S(2)}, u32[]{:S(2)}) collective-permute-start(bf16[192,128]{1,0:T(8,128)(2,1)S(1)} %get-tuple-element.49), channel_id=1, source_target_pairs={{0,4},{1,13},{2,6},{3,15},{4,0},{5,9},{6,2},{7,11},{8,12},{9,5},{1... | collective-permute-start | bytes 147464 | tf_op jit(solution)/shard_map/ppermute | solution.py:429
  11.6 1.6 %collective-permute-start.7 = (bf16[192,128]{1,0:T(8,128)(2,1)S(1)}, bf16[192,128]{1,0:T(8,128)(2,1)S(1)}, u32[]{:S(2)}, u32[]{:S(2)}) collective-permute-start(bf16[192,128]{1,0:T(8,128)(2,1)S(1)} %get-tuple-element.50), channel_id=1, source_target_pairs={{0,12},{1,5},{2,14},{3,7},{4,8},{5,1},{6,10},{7,3},{8,4},{9,13},{1... | collective-permute-start | bytes 147464 | tf_op jit(solution)/shard_map/ppermute | solution.py:429
  13.2 0.1 shard_map.51
  13.3 0.1 collective-permute-start.4
  13.4 1.6 %collective-permute-start.5 = (bf16[96,128]{1,0:T(8,128)(2,1)S(1)}, bf16[96,128]{1,0:T(8,128)(2,1)S(1)}, u32[]{:S(2)}, u32[]{:S(2)}) collective-permute-start(bf16[96,128]{1,0:T(8,128)(2,1)S(1)} %get-tuple-element.48), channel_id=1, source_target_pairs={{0,1},{1,0},{2,3},{3,2},{4,5},{5,4},{6,7},{7,6},{8,9},{9,8},{10,11... | collective-permute-start | bytes 73736 | tf_op jit(solution)/shard_map/ppermute | solution.py:418
  15.0 1.2 %shard_map.52.acc_ref = f32[768,128]{1,0:T(8,128)S(1)} custom-call(bf16[768,128]{1,0:T(8,128)(2,1)S(1)} %get-tuple-element.46.f_ref.refs_0_, bf16[1152,128]{1,0:T(8,128)(2,1)S(1)} %bitcast.11, bf16[768,128]{1,0:T(8,128)(2,1)S(1)} %bitcast.25, bf16[1152,128]{1,0:T(8,128)(2,1)S(1)} %bitcast.28), custom_call_target="tpu_custom_call" | custom-call | flops 8000000 | bytes 2097152 | tf_op jit(solution)/shard_map/pallas_call | solution.py:403
  16.2 0.6 %collective-permute-done.4.x_far = bf16[96,128]{1,0:T(8,128)(2,1)S(1)} collective-permute-done((bf16[96,128]{1,0:T(8,128)(2,1)S(1)}, bf16[96,128]{1,0:T(8,128)(2,1)S(1)}, u32[]{:S(2)}, u32[]{:S(2)}) %collective-permute-start.4) | collective-permute-done | bytes 24608 | tf_op jit(solution)/shard_map/ppermute | solution.py:418
  16.8 0.1 shard_map.53.acc_ref
  16.9 0.0 collective-permute-done.6.t_one
  16.9 0.6 %collective-permute-done.7.t_two = bf16[192,128]{1,0:T(8,128)(2,1)S(1)} collective-permute-done((bf16[192,128]{1,0:T(8,128)(2,1)S(1)}, bf16[192,128]{1,0:T(8,128)(2,1)S(1)}, u32[]{:S(2)}, u32[]{:S(2)}) %collective-permute-start.7) | collective-permute-done | bytes 49184 | tf_op jit(solution)/shard_map/ppermute | solution.py:429
  17.5 0.2 shard_map.54
  17.7 0.6 %collective-permute-start.10 = (bf16[192,128]{1,0:T(8,128)(2,1)S(1)}, bf16[192,128]{1,0:T(8,128)(2,1)S(1)}, u32[]{:S(2)}, u32[]{:S(2)}) collective-permute-start(bf16[192,128]{1,0:T(8,128)(2,1)S(1)} %get-tuple-element.57), channel_id=1, source_target_pairs={{0,4},{1,13},{2,6},{3,15},{4,0},{5,9},{6,2},{7,11},{8,12},{9,5},{1... | collective-permute-start | bytes 147464 | tf_op jit(solution)/shard_map/ppermute | solution.py:429
  18.3 1.8 %collective-permute-start.11 = (bf16[192,128]{1,0:T(8,128)(2,1)S(1)}, bf16[192,128]{1,0:T(8,128)(2,1)S(1)}, u32[]{:S(2)}, u32[]{:S(2)}) collective-permute-start(bf16[192,128]{1,0:T(8,128)(2,1)S(1)} %get-tuple-element.58), channel_id=1, source_target_pairs={{0,12},{1,5},{2,14},{3,7},{4,8},{5,1},{6,10},{7,3},{8,4},{9,13},{1... | collective-permute-start | bytes 147464 | tf_op jit(solution)/shard_map/ppermute | solution.py:429
  20.0 0.1 shard_map.55
  20.1 0.1 collective-permute-start.8
  20.2 1.6 %collective-permute-start.9 = (bf16[96,128]{1,0:T(8,128)(2,1)S(1)}, bf16[96,128]{1,0:T(8,128)(2,1)S(1)}, u32[]{:S(2)}, u32[]{:S(2)}) collective-permute-start(bf16[96,128]{1,0:T(8,128)(2,1)S(1)} %get-tuple-element.56), channel_id=1, source_target_pairs={{0,1},{1,0},{2,3},{3,2},{4,5},{5,4},{6,7},{7,6},{8,9},{9,8},{10,11... | collective-permute-start | bytes 73736 | tf_op jit(solution)/shard_map/ppermute | solution.py:418
  21.8 1.0 %shard_map.56.acc_ref = f32[768,128]{1,0:T(8,128)S(1)} custom-call(bf16[768,128]{1,0:T(8,128)(2,1)S(1)} %get-tuple-element.54.f_ref.refs_0_.refs_2_, bf16[1152,128]{1,0:T(8,128)(2,1)S(1)} %bitcast.15), custom_call_target="tpu_custom_call" | custom-call | flops 5000000 | bytes 2097152 | tf_op jit(solution)/shard_map/pallas_call | solution.py:403
  22.8 0.9 %collective-permute-done.8.x_far = bf16[96,128]{1,0:T(8,128)(2,1)S(1)} collective-permute-done((bf16[96,128]{1,0:T(8,128)(2,1)S(1)}, bf16[96,128]{1,0:T(8,128)(2,1)S(1)}, u32[]{:S(2)}, u32[]{:S(2)}) %collective-permute-start.8) | collective-permute-done | bytes 24608 | tf_op jit(solution)/shard_map/ppermute | solution.py:418
  23.7 0.1 shard_map.57.acc_ref
  23.8 0.0 collective-permute-done.10.t_one
  23.8 0.4 %collective-permute-done.11.t_two = bf16[192,128]{1,0:T(8,128)(2,1)S(1)} collective-permute-done((bf16[192,128]{1,0:T(8,128)(2,1)S(1)}, bf16[192,128]{1,0:T(8,128)(2,1)S(1)}, u32[]{:S(2)}, u32[]{:S(2)}) %collective-permute-start.11) | collective-permute-done | bytes 49184 | tf_op jit(solution)/shard_map/ppermute | solution.py:429
  24.2 0.5 %shard_map.58 = (bf16[768,128]{1,0:T(8,128)(2,1)S(1)}, bf16[192,128]{1,0:T(8,128)(2,1)S(1)}, bf16[192,128]{1,0:T(8,128)(2,1)S(1)}) custom-call(bf16[1152,128]{1,0:T(8,128)(2,1)S(1)} %bitcast.17, bf16[1152,128]{1,0:T(8,128)(2,1)S(1)} %bitcast.27, f32[768,128]{1,0:T(8,128)S(1)} %shard_map.57.acc_ref, bf16[192,128]{1,0:T(8,128)(2,1)S(1)} %collective-permute-done.10.t_one, ...), custom_call_target="tpu_custom_call" | custom-call | flops 4000000 | bytes 2097152 | tf_op jit(solution)/shard_map/pallas_call | solution.py:403
  24.6 0.1 collective-permute-start.14
  24.7 2.2 %collective-permute-start.15 = (bf16[192,128]{1,0:T(8,128)(2,1)S(1)}, bf16[192,128]{1,0:T(8,128)(2,1)S(1)}, u32[]{:S(2)}, u32[]{:S(2)}) collective-permute-start(bf16[192,128]{1,0:T(8,128)(2,1)S(1)} %get-tuple-element.66), channel_id=1, source_target_pairs={{0,12},{1,5},{2,14},{3,7},{4,8},{5,1},{6,10},{7,3},{8,4},{9,13},{1... | collective-permute-start | bytes 147464 | tf_op jit(solution)/shard_map/ppermute | solution.py:429
  26.9 0.1 shard_map.59
  27.0 0.1 collective-permute-start.12
  27.1 1.3 %collective-permute-start.13 = (bf16[96,128]{1,0:T(8,128)(2,1)S(1)}, bf16[96,128]{1,0:T(8,128)(2,1)S(1)}, u32[]{:S(2)}, u32[]{:S(2)}) collective-permute-start(bf16[96,128]{1,0:T(8,128)(2,1)S(1)} %get-tuple-element.64), channel_id=1, source_target_pairs={{0,1},{1,0},{2,3},{3,2},{4,5},{5,4},{6,7},{7,6},{8,9},{9,8},{10,11... | collective-permute-start | bytes 73736 | tf_op jit(solution)/shard_map/ppermute | solution.py:418
  28.4 1.2 %shard_map.60.acc_ref = f32[768,128]{1,0:T(8,128)S(1)} custom-call(bf16[768,128]{1,0:T(8,128)(2,1)S(1)} %get-tuple-element.62.f_ref.refs_0_, bf16[1152,128]{1,0:T(8,128)(2,1)S(1)} %bitcast.19, bf16[768,128]{1,0:T(8,128)(2,1)S(1)} %get-tuple-element.54.f_ref.refs_0_.refs_2_, bf16[1152,128]{1,0:T(8,128)(2,1)S(1)} %bitcast.29), custom_call_target="tpu_custom_call" | custom-call | flops 8000000 | bytes 2097152 | tf_op jit(solution)/shard_map/pallas_call | solution.py:403
  29.7 0.7 %collective-permute-done.12.x_far = bf16[96,128]{1,0:T(8,128)(2,1)S(1)} collective-permute-done((bf16[96,128]{1,0:T(8,128)(2,1)S(1)}, bf16[96,128]{1,0:T(8,128)(2,1)S(1)}, u32[]{:S(2)}, u32[]{:S(2)}) %collective-permute-start.12) | collective-permute-done | bytes 24608 | tf_op jit(solution)/shard_map/ppermute | solution.py:418
  30.4 0.0 collective-permute-done.13.x_near
  30.4 0.1 shard_map.61.acc_ref
  30.5 0.3 collective-permute-done.15.t_two
  30.8 0.8 %shard_map.62 = bf16[768,128]{1,0:T(8,128)(2,1)} custom-call(bf16[1152,128]{1,0:T(8,128)(2,1)S(1)} %bitcast.21, f32[768,128]{1,0:T(8,128)S(1)} %shard_map.61.acc_ref, bf16[192,128]{1,0:T(8,128)(2,1)S(1)} %collective-permute-done.14.t_one, bf16[192,128]{1,0:T(8,128)(2,1)S(1)} %collective-permute-done.15.t_two), custom_call_target="tpu_custom_call" | custom-call | flops 1000000 | bytes 2097152 | tf_op jit(solution)/shard_map/pallas_call | solution.py:403
  (9 shorter events, 0.0 us)
Async XLA Ops:
  0.0 6.7 %copy-start = (bf16[4,3,3,2,2,2,4,128]{7,6,5,4,3,2,1,0:T(4,128)(2,1)S(1)}, bf16[4,3,3,2,2,2,4,128]{7,6,5,4,3,2,1,0:T(4,128)(2,1)}, u32[]{:S(2)}) copy-start(bf16[4,3,3,2,2,2,4,128]{7,6,5,4,3,2,1,0:T(4,128)(2,1)} %param.5) | copy-start | bytes 884740
  0.0 6.7 %copy-start.1 = (bf16[4,4,3,2,2,4,128]{6,5,4,3,2,1,0:T(4,128)(2,1)S(1)}, bf16[4,4,3,2,2,4,128]{6,5,4,3,2,1,0:T(4,128)(2,1)}, u32[]{:S(2)}) copy-start(bf16[4,4,3,2,2,4,128]{6,5,4,3,2,1,0:T(4,128)(2,1)} %param.4) | copy-start | bytes 589828
  1.1 9.3 %collective-permute-start.2 = (bf16[192,128]{1,0:T(8,128)(2,1)S(1)}, bf16[192,128]{1,0:T(8,128)(2,1)S(1)}, u32[]{:S(2)}, u32[]{:S(2)}) collective-permute-start(bf16[192,128]{1,0:T(8,128)(2,1)S(1)} %get-tuple-element.41), channel_id=1, source_target_pairs={{0,4},{1,13},{2,6},{3,15},{4,0},{5,9},{6,2},{7,11},{8,12},{9,5},{1... | collective-permute-start | bytes 147464 | tf_op jit(solution)/shard_map/ppermute | solution.py:429
  4.2 6.2 %collective-permute-start.3 = (bf16[192,128]{1,0:T(8,128)(2,1)S(1)}, bf16[192,128]{1,0:T(8,128)(2,1)S(1)}, u32[]{:S(2)}, u32[]{:S(2)}) collective-permute-start(bf16[192,128]{1,0:T(8,128)(2,1)S(1)} %get-tuple-element.42), channel_id=1, source_target_pairs={{0,12},{1,5},{2,14},{3,7},{4,8},{5,1},{6,10},{7,3},{8,4},{9,13},{1... | collective-permute-start | bytes 147464 | tf_op jit(solution)/shard_map/ppermute | solution.py:429
  6.8 3.5 %collective-permute-start = (bf16[96,128]{1,0:T(8,128)(2,1)S(1)}, bf16[96,128]{1,0:T(8,128)(2,1)S(1)}, u32[]{:S(2)}, u32[]{:S(2)}) collective-permute-start(bf16[96,128]{1,0:T(8,128)(2,1)S(1)} %get-tuple-element.39), channel_id=1, source_target_pairs={{0,3},{1,2},{2,1},{3,0},{4,7},{5,6},{6,5},{7,4},{8,11},{9,10},{10,... | collective-permute-start | bytes 73736 | tf_op jit(solution)/shard_map/ppermute | solution.py:418
  7.1 3.3 %collective-permute-start.1 = (bf16[96,128]{1,0:T(8,128)(2,1)S(1)}, bf16[96,128]{1,0:T(8,128)(2,1)S(1)}, u32[]{:S(2)}, u32[]{:S(2)}) collective-permute-start(bf16[96,128]{1,0:T(8,128)(2,1)S(1)} %get-tuple-element.40), channel_id=1, source_target_pairs={{0,1},{1,0},{2,3},{3,2},{4,5},{5,4},{6,7},{7,6},{8,9},{9,8},{10,11... | collective-permute-start | bytes 73736 | tf_op jit(solution)/shard_map/ppermute | solution.py:418
  9.4 1.0 %copy-start.2 = (bf16[2,6,6,2,2,4,128]{6,5,4,3,2,1,0:T(4,128)(2,1)S(1)}, bf16[2,6,6,2,2,4,128]{6,5,4,3,2,1,0:T(4,128)(2,1)}, u32[]{:S(2)}) copy-start(bf16[2,6,6,2,2,4,128]{6,5,4,3,2,1,0:T(4,128)(2,1)} %param.7) | copy-start | bytes 884740
  10.9 4.1 %copy-start.3 = (bf16[2,6,6,2,2,4,128]{6,5,4,3,2,1,0:T(4,128)(2,1)S(1)}, bf16[2,6,6,2,2,4,128]{6,5,4,3,2,1,0:T(4,128)(2,1)}, u32[]{:S(2)}) copy-start(bf16[2,6,6,2,2,4,128]{6,5,4,3,2,1,0:T(4,128)(2,1)} %param.6) | copy-start | bytes 884740
  10.9 6.0 %collective-permute-start.6 = (bf16[192,128]{1,0:T(8,128)(2,1)S(1)}, bf16[192,128]{1,0:T(8,128)(2,1)S(1)}, u32[]{:S(2)}, u32[]{:S(2)}) collective-permute-start(bf16[192,128]{1,0:T(8,128)(2,1)S(1)} %get-tuple-element.49), channel_id=1, source_target_pairs={{0,4},{1,13},{2,6},{3,15},{4,0},{5,9},{6,2},{7,11},{8,12},{9,5},{1... | collective-permute-start | bytes 147464 | tf_op jit(solution)/shard_map/ppermute | solution.py:429
  11.6 5.9 %collective-permute-start.7 = (bf16[192,128]{1,0:T(8,128)(2,1)S(1)}, bf16[192,128]{1,0:T(8,128)(2,1)S(1)}, u32[]{:S(2)}, u32[]{:S(2)}) collective-permute-start(bf16[192,128]{1,0:T(8,128)(2,1)S(1)} %get-tuple-element.50), channel_id=1, source_target_pairs={{0,12},{1,5},{2,14},{3,7},{4,8},{5,1},{6,10},{7,3},{8,4},{9,13},{1... | collective-permute-start | bytes 147464 | tf_op jit(solution)/shard_map/ppermute | solution.py:429
  13.3 3.5 %collective-permute-start.4 = (bf16[96,128]{1,0:T(8,128)(2,1)S(1)}, bf16[96,128]{1,0:T(8,128)(2,1)S(1)}, u32[]{:S(2)}, u32[]{:S(2)}) collective-permute-start(bf16[96,128]{1,0:T(8,128)(2,1)S(1)} %get-tuple-element.47), channel_id=1, source_target_pairs={{0,3},{1,2},{2,1},{3,0},{4,7},{5,6},{6,5},{7,4},{8,11},{9,10},{10,... | collective-permute-start | bytes 73736 | tf_op jit(solution)/shard_map/ppermute | solution.py:418
  13.4 3.5 %collective-permute-start.5 = (bf16[96,128]{1,0:T(8,128)(2,1)S(1)}, bf16[96,128]{1,0:T(8,128)(2,1)S(1)}, u32[]{:S(2)}, u32[]{:S(2)}) collective-permute-start(bf16[96,128]{1,0:T(8,128)(2,1)S(1)} %get-tuple-element.48), channel_id=1, source_target_pairs={{0,1},{1,0},{2,3},{3,2},{4,5},{5,4},{6,7},{7,6},{8,9},{9,8},{10,11... | collective-permute-start | bytes 73736 | tf_op jit(solution)/shard_map/ppermute | solution.py:418
  17.7 6.1 %collective-permute-start.10 = (bf16[192,128]{1,0:T(8,128)(2,1)S(1)}, bf16[192,128]{1,0:T(8,128)(2,1)S(1)}, u32[]{:S(2)}, u32[]{:S(2)}) collective-permute-start(bf16[192,128]{1,0:T(8,128)(2,1)S(1)} %get-tuple-element.57), channel_id=1, source_target_pairs={{0,4},{1,13},{2,6},{3,15},{4,0},{5,9},{6,2},{7,11},{8,12},{9,5},{1... | collective-permute-start | bytes 147464 | tf_op jit(solution)/shard_map/ppermute | solution.py:429
  18.3 5.9 %collective-permute-start.11 = (bf16[192,128]{1,0:T(8,128)(2,1)S(1)}, bf16[192,128]{1,0:T(8,128)(2,1)S(1)}, u32[]{:S(2)}, u32[]{:S(2)}) collective-permute-start(bf16[192,128]{1,0:T(8,128)(2,1)S(1)} %get-tuple-element.58), channel_id=1, source_target_pairs={{0,12},{1,5},{2,14},{3,7},{4,8},{5,1},{6,10},{7,3},{8,4},{9,13},{1... | collective-permute-start | bytes 147464 | tf_op jit(solution)/shard_map/ppermute | solution.py:429
  20.1 3.5 %collective-permute-start.8 = (bf16[96,128]{1,0:T(8,128)(2,1)S(1)}, bf16[96,128]{1,0:T(8,128)(2,1)S(1)}, u32[]{:S(2)}, u32[]{:S(2)}) collective-permute-start(bf16[96,128]{1,0:T(8,128)(2,1)S(1)} %get-tuple-element.55), channel_id=1, source_target_pairs={{0,3},{1,2},{2,1},{3,0},{4,7},{5,6},{6,5},{7,4},{8,11},{9,10},{10,... | collective-permute-start | bytes 73736 | tf_op jit(solution)/shard_map/ppermute | solution.py:418
  20.2 3.5 %collective-permute-start.9 = (bf16[96,128]{1,0:T(8,128)(2,1)S(1)}, bf16[96,128]{1,0:T(8,128)(2,1)S(1)}, u32[]{:S(2)}, u32[]{:S(2)}) collective-permute-start(bf16[96,128]{1,0:T(8,128)(2,1)S(1)} %get-tuple-element.56), channel_id=1, source_target_pairs={{0,1},{1,0},{2,3},{3,2},{4,5},{5,4},{6,7},{7,6},{8,9},{9,8},{10,11... | collective-permute-start | bytes 73736 | tf_op jit(solution)/shard_map/ppermute | solution.py:418
  24.6 5.8 %collective-permute-start.14 = (bf16[192,128]{1,0:T(8,128)(2,1)S(1)}, bf16[192,128]{1,0:T(8,128)(2,1)S(1)}, u32[]{:S(2)}, u32[]{:S(2)}) collective-permute-start(bf16[192,128]{1,0:T(8,128)(2,1)S(1)} %get-tuple-element.65), channel_id=1, source_target_pairs={{0,4},{1,13},{2,6},{3,15},{4,0},{5,9},{6,2},{7,11},{8,12},{9,5},{1... | collective-permute-start | bytes 147464 | tf_op jit(solution)/shard_map/ppermute | solution.py:429
  24.7 6.1 %collective-permute-start.15 = (bf16[192,128]{1,0:T(8,128)(2,1)S(1)}, bf16[192,128]{1,0:T(8,128)(2,1)S(1)}, u32[]{:S(2)}, u32[]{:S(2)}) collective-permute-start(bf16[192,128]{1,0:T(8,128)(2,1)S(1)} %get-tuple-element.66), channel_id=1, source_target_pairs={{0,12},{1,5},{2,14},{3,7},{4,8},{5,1},{6,10},{7,3},{8,4},{9,13},{1... | collective-permute-start | bytes 147464 | tf_op jit(solution)/shard_map/ppermute | solution.py:429
  27.0 3.3 %collective-permute-start.12 = (bf16[96,128]{1,0:T(8,128)(2,1)S(1)}, bf16[96,128]{1,0:T(8,128)(2,1)S(1)}, u32[]{:S(2)}, u32[]{:S(2)}) collective-permute-start(bf16[96,128]{1,0:T(8,128)(2,1)S(1)} %get-tuple-element.63), channel_id=1, source_target_pairs={{0,3},{1,2},{2,1},{3,0},{4,7},{5,6},{6,5},{7,4},{8,11},{9,10},{10,... | collective-permute-start | bytes 73736 | tf_op jit(solution)/shard_map/ppermute | solution.py:418
  27.1 3.3 %collective-permute-start.13 = (bf16[96,128]{1,0:T(8,128)(2,1)S(1)}, bf16[96,128]{1,0:T(8,128)(2,1)S(1)}, u32[]{:S(2)}, u32[]{:S(2)}) collective-permute-start(bf16[96,128]{1,0:T(8,128)(2,1)S(1)} %get-tuple-element.64), channel_id=1, source_target_pairs={{0,1},{1,0},{2,3},{3,2},{4,5},{5,4},{6,7},{7,6},{8,9},{9,8},{10,11... | collective-permute-start | bytes 73736 | tf_op jit(solution)/shard_map/ppermute | solution.py:418

commit v22 on v21

--- a/solution.py
+++ b/solution.py
@@ -285,19 +285,20 @@
 
 
 def matvec(links, vector, adjoint):
+    both = [vr + vi for vr, vi in vector]
     out = []
     for a in range(3):
-        re = im = None
+        one = re = im = None
         for b in range(3):
             lr, li = links[b][a] if adjoint else links[a][b]
             vr, vi = vector[b]
-            if adjoint:
-                tr, ti = lr * vr + li * vi, lr * vi - li * vr
-            else:
-                tr, ti = lr * vr - li * vi, lr * vi + li * vr
-            re = tr if re is None else re + tr
-            im = ti if im is None else im + ti
-        out.append((re, im))
+            plus, minus = lr + li, li - lr
+            t_one = lr * both[b]
+            t_re, t_im = (vi * minus, vr * plus) if adjoint else (vi * plus, vr * minus)
+            one = t_one if one is None else one + t_one
+            re = t_re if re is None else re + t_re
+            im = t_im if im is None else im + t_im
+        out.append((one + re, one - im) if adjoint else (one - re, one + im))
     return out
 
 

time: 31.7 us -> 31.6 us (level)
  no operation moved by 1% of the time
where the time goes in v22:
time: 31.6 us; the launch traced here: 31.5 us
  starting transfers between devices  18.8 us (59%)
  Pallas kernels  8.11 us (26%)
  waiting for transfers between devices  4.37 us (14%)
    ppermute x8, starting transfers between devices, swap_t(): return lax.ppermute(value, ('ta', 'gx'), pairs)  12.4 us
    pallas_call x17, Pallas kernels, call(): pl.pallas_call(kernel, out_shape=tuple((jax.ShapeDtypeStruct(shape, dtype...  8.11 us
    ppermute x8, starting transfers between devices, swap(): return lax.ppermute(value, axis, pairs)  6.38 us
    ppermute x8, waiting for transfers between devices, swap(): return lax.ppermute(value, axis, pairs)  3.11 us
    ppermute x8, waiting for transfers between devices, swap_t(): return lax.ppermute(value, ('ta', 'gx'), pairs)  1.25 us
  transfers between devices with their start and end apart: 16, of which 7 were waited for; matrix products, arithmetic and copies ran while one was open for 0% of the time, Pallas kernels for 16%

profile of v22, /device:TPU:0, one launch (start us, length us, event | category | flops | bytes accessed | tf_op | source)
XLA Modules:
  0.0 31.5 jit_solution(13714568399185781613)
XLA Ops:
  0.0 1.1 %shard_map.49 = (bf16[192,128]{1,0:T(8,128)(2,1)S(1)}, bf16[192,128]{1,0:T(8,128)(2,1)S(1)}) custom-call(bf16[768,128]{1,0:T(8,128)(2,1)} %bitcast.22, bf16[1152,128]{1,0:T(8,128)(2,1)} %bitcast.5), custom_call_target="tpu_custom_call" | custom-call | flops 1500000 | bytes 2097152 | tf_op jit(solution)/shard_map/pallas_call | solution.py:404
  1.1 3.1 %collective-permute-start.2 = (bf16[192,128]{1,0:T(8,128)(2,1)S(1)}, bf16[192,128]{1,0:T(8,128)(2,1)S(1)}, u32[]{:S(2)}, u32[]{:S(2)}) collective-permute-start(bf16[192,128]{1,0:T(8,128)(2,1)S(1)} %get-tuple-element.41), channel_id=1, source_target_pairs={{0,4},{1,13},{2,6},{3,15},{4,0},{5,9},{6,2},{7,11},{8,12},{9,5},{1... | collective-permute-start | bytes 147464 | tf_op jit(solution)/shard_map/ppermute | solution.py:430
  4.2 2.5 %collective-permute-start.3 = (bf16[192,128]{1,0:T(8,128)(2,1)S(1)}, bf16[192,128]{1,0:T(8,128)(2,1)S(1)}, u32[]{:S(2)}, u32[]{:S(2)}) collective-permute-start(bf16[192,128]{1,0:T(8,128)(2,1)S(1)} %get-tuple-element.42), channel_id=1, source_target_pairs={{0,12},{1,5},{2,14},{3,7},{4,8},{5,1},{6,10},{7,3},{8,4},{9,13},{1... | collective-permute-start | bytes 147464 | tf_op jit(solution)/shard_map/ppermute | solution.py:430
  6.7 0.1 shard_map.46
  6.8 0.3 collective-permute-start
  7.1 1.4 %collective-permute-start.1 = (bf16[96,128]{1,0:T(8,128)(2,1)S(1)}, bf16[96,128]{1,0:T(8,128)(2,1)S(1)}, u32[]{:S(2)}, u32[]{:S(2)}) collective-permute-start(bf16[96,128]{1,0:T(8,128)(2,1)S(1)} %get-tuple-element.40), channel_id=1, source_target_pairs={{0,1},{1,0},{2,3},{3,2},{4,5},{5,4},{6,7},{7,6},{8,9},{9,8},{10,11... | collective-permute-start | bytes 73736 | tf_op jit(solution)/shard_map/ppermute | solution.py:419
  8.5 1.0 %shard_map.47.acc_ref = f32[768,128]{1,0:T(8,128)S(1)} custom-call(bf16[768,128]{1,0:T(8,128)(2,1)S(1)} %bitcast.24, bf16[1152,128]{1,0:T(8,128)(2,1)S(1)} %bitcast.7), custom_call_target="tpu_custom_call" | custom-call | flops 5000000 | bytes 2097152 | tf_op jit(solution)/shard_map/pallas_call | solution.py:404
  9.4 0.0 copy-start.2
  9.4 0.9 %collective-permute-done.x_far = bf16[96,128]{1,0:T(8,128)(2,1)S(1)} collective-permute-done((bf16[96,128]{1,0:T(8,128)(2,1)S(1)}, bf16[96,128]{1,0:T(8,128)(2,1)S(1)}, u32[]{:S(2)}, u32[]{:S(2)}) %collective-permute-start) | collective-permute-done | bytes 24608 | tf_op jit(solution)/shard_map/ppermute | solution.py:419
  10.3 0.0 collective-permute-done.1.x_near
  10.3 0.1 shard_map.48.acc_ref
  10.4 0.0 collective-permute-done.2.t_one
  10.4 0.0 collective-permute-done.3.t_two
  10.5 0.4 %shard_map.50 = (bf16[768,128]{1,0:T(8,128)(2,1)S(1)}, bf16[192,128]{1,0:T(8,128)(2,1)S(1)}, bf16[192,128]{1,0:T(8,128)(2,1)S(1)}) custom-call(bf16[1152,128]{1,0:T(8,128)(2,1)S(1)} %bitcast.9, bf16[1152,128]{1,0:T(8,128)(2,1)S(1)} %bitcast.26, f32[768,128]{1,0:T(8,128)S(1)} %shard_map.48.acc_ref, bf16[192,128]{1,0:T(8,128)(2,1)S(1)} %collective-permute-done.2.t_one, ...), custom_call_target="tpu_custom_call" | custom-call | flops 4000000 | bytes 2097152 | tf_op jit(solution)/shard_map/pallas_call | solution.py:404
  10.9 0.0 copy-start.3
  10.9 0.7 %collective-permute-start.6 = (bf16[192,128]{1,0:T(8,128)(2,1)S(1)}, bf16[192,128]{1,0:T(8,128)(2,1)S(1)}, u32[]{:S(2)}, u32[]{:S(2)}) collective-permute-start(bf16[192,128]{1,0:T(8,128)(2,1)S(1)} %get-tuple-element.49), channel_id=1, source_target_pairs={{0,4},{1,13},{2,6},{3,15},{4,0},{5,9},{6,2},{7,11},{8,12},{9,5},{1... | collective-permute-start | bytes 147464 | tf_op jit(solution)/shard_map/ppermute | solution.py:430
  11.6 1.6 %collective-permute-start.7 = (bf16[192,128]{1,0:T(8,128)(2,1)S(1)}, bf16[192,128]{1,0:T(8,128)(2,1)S(1)}, u32[]{:S(2)}, u32[]{:S(2)}) collective-permute-start(bf16[192,128]{1,0:T(8,128)(2,1)S(1)} %get-tuple-element.50), channel_id=1, source_target_pairs={{0,12},{1,5},{2,14},{3,7},{4,8},{5,1},{6,10},{7,3},{8,4},{9,13},{1... | collective-permute-start | bytes 147464 | tf_op jit(solution)/shard_map/ppermute | solution.py:430
  13.2 0.1 shard_map.51
  13.3 0.1 collective-permute-start.4
  13.4 1.6 %collective-permute-start.5 = (bf16[96,128]{1,0:T(8,128)(2,1)S(1)}, bf16[96,128]{1,0:T(8,128)(2,1)S(1)}, u32[]{:S(2)}, u32[]{:S(2)}) collective-permute-start(bf16[96,128]{1,0:T(8,128)(2,1)S(1)} %get-tuple-element.48), channel_id=1, source_target_pairs={{0,1},{1,0},{2,3},{3,2},{4,5},{5,4},{6,7},{7,6},{8,9},{9,8},{10,11... | collective-permute-start | bytes 73736 | tf_op jit(solution)/shard_map/ppermute | solution.py:419
  15.0 1.2 %shard_map.52.acc_ref = f32[768,128]{1,0:T(8,128)S(1)} custom-call(bf16[768,128]{1,0:T(8,128)(2,1)S(1)} %get-tuple-element.46.f_ref.refs_0_, bf16[1152,128]{1,0:T(8,128)(2,1)S(1)} %bitcast.11, bf16[768,128]{1,0:T(8,128)(2,1)S(1)} %bitcast.25, bf16[1152,128]{1,0:T(8,128)(2,1)S(1)} %bitcast.28), custom_call_target="tpu_custom_call" | custom-call | flops 8000000 | bytes 2097152 | tf_op jit(solution)/shard_map/pallas_call | solution.py:404
  16.2 0.6 %collective-permute-done.4.x_far = bf16[96,128]{1,0:T(8,128)(2,1)S(1)} collective-permute-done((bf16[96,128]{1,0:T(8,128)(2,1)S(1)}, bf16[96,128]{1,0:T(8,128)(2,1)S(1)}, u32[]{:S(2)}, u32[]{:S(2)}) %collective-permute-start.4) | collective-permute-done | bytes 24608 | tf_op jit(solution)/shard_map/ppermute | solution.py:419
  16.8 0.0 collective-permute-done.5.x_near
  16.8 0.1 shard_map.53.acc_ref
  16.9 0.6 %collective-permute-done.7.t_two = bf16[192,128]{1,0:T(8,128)(2,1)S(1)} collective-permute-done((bf16[192,128]{1,0:T(8,128)(2,1)S(1)}, bf16[192,128]{1,0:T(8,128)(2,1)S(1)}, u32[]{:S(2)}, u32[]{:S(2)}) %collective-permute-start.7) | collective-permute-done | bytes 49184 | tf_op jit(solution)/shard_map/ppermute | solution.py:430
  17.5 0.2 shard_map.54
  17.7 0.6 %collective-permute-start.10 = (bf16[192,128]{1,0:T(8,128)(2,1)S(1)}, bf16[192,128]{1,0:T(8,128)(2,1)S(1)}, u32[]{:S(2)}, u32[]{:S(2)}) collective-permute-start(bf16[192,128]{1,0:T(8,128)(2,1)S(1)} %get-tuple-element.57), channel_id=1, source_target_pairs={{0,4},{1,13},{2,6},{3,15},{4,0},{5,9},{6,2},{7,11},{8,12},{9,5},{1... | collective-permute-start | bytes 147464 | tf_op jit(solution)/shard_map/ppermute | solution.py:430
  18.3 1.8 %collective-permute-start.11 = (bf16[192,128]{1,0:T(8,128)(2,1)S(1)}, bf16[192,128]{1,0:T(8,128)(2,1)S(1)}, u32[]{:S(2)}, u32[]{:S(2)}) collective-permute-start(bf16[192,128]{1,0:T(8,128)(2,1)S(1)} %get-tuple-element.58), channel_id=1, source_target_pairs={{0,12},{1,5},{2,14},{3,7},{4,8},{5,1},{6,10},{7,3},{8,4},{9,13},{1... | collective-permute-start | bytes 147464 | tf_op jit(solution)/shard_map/ppermute | solution.py:430
  20.0 0.1 shard_map.55
  20.1 0.1 collective-permute-start.8
  20.2 1.6 %collective-permute-start.9 = (bf16[96,128]{1,0:T(8,128)(2,1)S(1)}, bf16[96,128]{1,0:T(8,128)(2,1)S(1)}, u32[]{:S(2)}, u32[]{:S(2)}) collective-permute-start(bf16[96,128]{1,0:T(8,128)(2,1)S(1)} %get-tuple-element.56), channel_id=1, source_target_pairs={{0,1},{1,0},{2,3},{3,2},{4,5},{5,4},{6,7},{7,6},{8,9},{9,8},{10,11... | collective-permute-start | bytes 73736 | tf_op jit(solution)/shard_map/ppermute | solution.py:419
  21.8 1.0 %shard_map.56.acc_ref = f32[768,128]{1,0:T(8,128)S(1)} custom-call(bf16[768,128]{1,0:T(8,128)(2,1)S(1)} %get-tuple-element.54.f_ref.refs_0_.refs_2_, bf16[1152,128]{1,0:T(8,128)(2,1)S(1)} %bitcast.15), custom_call_target="tpu_custom_call" | custom-call | flops 5000000 | bytes 2097152 | tf_op jit(solution)/shard_map/pallas_call | solution.py:404
  22.8 0.9 %collective-permute-done.8.x_far = bf16[96,128]{1,0:T(8,128)(2,1)S(1)} collective-permute-done((bf16[96,128]{1,0:T(8,128)(2,1)S(1)}, bf16[96,128]{1,0:T(8,128)(2,1)S(1)}, u32[]{:S(2)}, u32[]{:S(2)}) %collective-permute-start.8) | collective-permute-done | bytes 24608 | tf_op jit(solution)/shard_map/ppermute | solution.py:419
  23.7 0.1 shard_map.57.acc_ref
  23.7 0.0 collective-permute-done.10.t_one
  23.8 0.4 %collective-permute-done.11.t_two = bf16[192,128]{1,0:T(8,128)(2,1)S(1)} collective-permute-done((bf16[192,128]{1,0:T(8,128)(2,1)S(1)}, bf16[192,128]{1,0:T(8,128)(2,1)S(1)}, u32[]{:S(2)}, u32[]{:S(2)}) %collective-permute-start.11) | collective-permute-done | bytes 49184 | tf_op jit(solution)/shard_map/ppermute | solution.py:430
  24.1 0.4 %shard_map.58 = (bf16[768,128]{1,0:T(8,128)(2,1)S(1)}, bf16[192,128]{1,0:T(8,128)(2,1)S(1)}, bf16[192,128]{1,0:T(8,128)(2,1)S(1)}) custom-call(bf16[1152,128]{1,0:T(8,128)(2,1)S(1)} %bitcast.17, bf16[1152,128]{1,0:T(8,128)(2,1)S(1)} %bitcast.27, f32[768,128]{1,0:T(8,128)S(1)} %shard_map.57.acc_ref, bf16[192,128]{1,0:T(8,128)(2,1)S(1)} %collective-permute-done.10.t_one, ...), custom_call_target="tpu_custom_call" | custom-call | flops 4000000 | bytes 2097152 | tf_op jit(solution)/shard_map/pallas_call | solution.py:404
  24.6 0.1 collective-permute-start.14
  24.7 2.2 %collective-permute-start.15 = (bf16[192,128]{1,0:T(8,128)(2,1)S(1)}, bf16[192,128]{1,0:T(8,128)(2,1)S(1)}, u32[]{:S(2)}, u32[]{:S(2)}) collective-permute-start(bf16[192,128]{1,0:T(8,128)(2,1)S(1)} %get-tuple-element.66), channel_id=1, source_target_pairs={{0,12},{1,5},{2,14},{3,7},{4,8},{5,1},{6,10},{7,3},{8,4},{9,13},{1... | collective-permute-start | bytes 147464 | tf_op jit(solution)/shard_map/ppermute | solution.py:430
  26.9 0.1 shard_map.59
  27.0 0.1 collective-permute-start.12
  27.1 1.3 %collective-permute-start.13 = (bf16[96,128]{1,0:T(8,128)(2,1)S(1)}, bf16[96,128]{1,0:T(8,128)(2,1)S(1)}, u32[]{:S(2)}, u32[]{:S(2)}) collective-permute-start(bf16[96,128]{1,0:T(8,128)(2,1)S(1)} %get-tuple-element.64), channel_id=1, source_target_pairs={{0,1},{1,0},{2,3},{3,2},{4,5},{5,4},{6,7},{7,6},{8,9},{9,8},{10,11... | collective-permute-start | bytes 73736 | tf_op jit(solution)/shard_map/ppermute | solution.py:419
  28.4 1.2 %shard_map.60.acc_ref = f32[768,128]{1,0:T(8,128)S(1)} custom-call(bf16[768,128]{1,0:T(8,128)(2,1)S(1)} %get-tuple-element.62.f_ref.refs_0_, bf16[1152,128]{1,0:T(8,128)(2,1)S(1)} %bitcast.19, bf16[768,128]{1,0:T(8,128)(2,1)S(1)} %get-tuple-element.54.f_ref.refs_0_.refs_2_, bf16[1152,128]{1,0:T(8,128)(2,1)S(1)} %bitcast.29), custom_call_target="tpu_custom_call" | custom-call | flops 8000000 | bytes 2097152 | tf_op jit(solution)/shard_map/pallas_call | solution.py:404
  29.6 0.7 %collective-permute-done.12.x_far = bf16[96,128]{1,0:T(8,128)(2,1)S(1)} collective-permute-done((bf16[96,128]{1,0:T(8,128)(2,1)S(1)}, bf16[96,128]{1,0:T(8,128)(2,1)S(1)}, u32[]{:S(2)}, u32[]{:S(2)}) %collective-permute-start.12) | collective-permute-done | bytes 24608 | tf_op jit(solution)/shard_map/ppermute | solution.py:419
  30.3 0.1 shard_map.61.acc_ref
  30.4 0.0 collective-permute-done.14.t_one
  30.4 0.3 collective-permute-done.15.t_two
  30.7 0.8 %shard_map.62 = bf16[768,128]{1,0:T(8,128)(2,1)} custom-call(bf16[1152,128]{1,0:T(8,128)(2,1)S(1)} %bitcast.21, f32[768,128]{1,0:T(8,128)S(1)} %shard_map.61.acc_ref, bf16[192,128]{1,0:T(8,128)(2,1)S(1)} %collective-permute-done.14.t_one, bf16[192,128]{1,0:T(8,128)(2,1)S(1)} %collective-permute-done.15.t_two), custom_call_target="tpu_custom_call" | custom-call | flops 1000000 | bytes 2097152 | tf_op jit(solution)/shard_map/pallas_call | solution.py:404
  (9 shorter events, 0.0 us)
Async XLA Ops:
  0.0 6.7 %copy-start = (bf16[4,3,3,2,2,2,4,128]{7,6,5,4,3,2,1,0:T(4,128)(2,1)S(1)}, bf16[4,3,3,2,2,2,4,128]{7,6,5,4,3,2,1,0:T(4,128)(2,1)}, u32[]{:S(2)}) copy-start(bf16[4,3,3,2,2,2,4,128]{7,6,5,4,3,2,1,0:T(4,128)(2,1)} %param.5) | copy-start | bytes 884740
  0.0 6.7 %copy-start.1 = (bf16[4,4,3,2,2,4,128]{6,5,4,3,2,1,0:T(4,128)(2,1)S(1)}, bf16[4,4,3,2,2,4,128]{6,5,4,3,2,1,0:T(4,128)(2,1)}, u32[]{:S(2)}) copy-start(bf16[4,4,3,2,2,4,128]{6,5,4,3,2,1,0:T(4,128)(2,1)} %param.4) | copy-start | bytes 589828
  1.1 9.3 %collective-permute-start.2 = (bf16[192,128]{1,0:T(8,128)(2,1)S(1)}, bf16[192,128]{1,0:T(8,128)(2,1)S(1)}, u32[]{:S(2)}, u32[]{:S(2)}) collective-permute-start(bf16[192,128]{1,0:T(8,128)(2,1)S(1)} %get-tuple-element.41), channel_id=1, source_target_pairs={{0,4},{1,13},{2,6},{3,15},{4,0},{5,9},{6,2},{7,11},{8,12},{9,5},{1... | collective-permute-start | bytes 147464 | tf_op jit(solution)/shard_map/ppermute | solution.py:430
  4.2 6.2 %collective-permute-start.3 = (bf16[192,128]{1,0:T(8,128)(2,1)S(1)}, bf16[192,128]{1,0:T(8,128)(2,1)S(1)}, u32[]{:S(2)}, u32[]{:S(2)}) collective-permute-start(bf16[192,128]{1,0:T(8,128)(2,1)S(1)} %get-tuple-element.42), channel_id=1, source_target_pairs={{0,12},{1,5},{2,14},{3,7},{4,8},{5,1},{6,10},{7,3},{8,4},{9,13},{1... | collective-permute-start | bytes 147464 | tf_op jit(solution)/shard_map/ppermute | solution.py:430
  6.8 3.5 %collective-permute-start = (bf16[96,128]{1,0:T(8,128)(2,1)S(1)}, bf16[96,128]{1,0:T(8,128)(2,1)S(1)}, u32[]{:S(2)}, u32[]{:S(2)}) collective-permute-start(bf16[96,128]{1,0:T(8,128)(2,1)S(1)} %get-tuple-element.39), channel_id=1, source_target_pairs={{0,3},{1,2},{2,1},{3,0},{4,7},{5,6},{6,5},{7,4},{8,11},{9,10},{10,... | collective-permute-start | bytes 73736 | tf_op jit(solution)/shard_map/ppermute | solution.py:419
  7.1 3.3 %collective-permute-start.1 = (bf16[96,128]{1,0:T(8,128)(2,1)S(1)}, bf16[96,128]{1,0:T(8,128)(2,1)S(1)}, u32[]{:S(2)}, u32[]{:S(2)}) collective-permute-start(bf16[96,128]{1,0:T(8,128)(2,1)S(1)} %get-tuple-element.40), channel_id=1, source_target_pairs={{0,1},{1,0},{2,3},{3,2},{4,5},{5,4},{6,7},{7,6},{8,9},{9,8},{10,11... | collective-permute-start | bytes 73736 | tf_op jit(solution)/shard_map/ppermute | solution.py:419
  9.4 1.0 %copy-start.2 = (bf16[2,6,6,2,2,4,128]{6,5,4,3,2,1,0:T(4,128)(2,1)S(1)}, bf16[2,6,6,2,2,4,128]{6,5,4,3,2,1,0:T(4,128)(2,1)}, u32[]{:S(2)}) copy-start(bf16[2,6,6,2,2,4,128]{6,5,4,3,2,1,0:T(4,128)(2,1)} %param.7) | copy-start | bytes 884740
  10.9 4.1 %copy-start.3 = (bf16[2,6,6,2,2,4,128]{6,5,4,3,2,1,0:T(4,128)(2,1)S(1)}, bf16[2,6,6,2,2,4,128]{6,5,4,3,2,1,0:T(4,128)(2,1)}, u32[]{:S(2)}) copy-start(bf16[2,6,6,2,2,4,128]{6,5,4,3,2,1,0:T(4,128)(2,1)} %param.6) | copy-start | bytes 884740
  10.9 6.0 %collective-permute-start.6 = (bf16[192,128]{1,0:T(8,128)(2,1)S(1)}, bf16[192,128]{1,0:T(8,128)(2,1)S(1)}, u32[]{:S(2)}, u32[]{:S(2)}) collective-permute-start(bf16[192,128]{1,0:T(8,128)(2,1)S(1)} %get-tuple-element.49), channel_id=1, source_target_pairs={{0,4},{1,13},{2,6},{3,15},{4,0},{5,9},{6,2},{7,11},{8,12},{9,5},{1... | collective-permute-start | bytes 147464 | tf_op jit(solution)/shard_map/ppermute | solution.py:430
  11.6 5.9 %collective-permute-start.7 = (bf16[192,128]{1,0:T(8,128)(2,1)S(1)}, bf16[192,128]{1,0:T(8,128)(2,1)S(1)}, u32[]{:S(2)}, u32[]{:S(2)}) collective-permute-start(bf16[192,128]{1,0:T(8,128)(2,1)S(1)} %get-tuple-element.50), channel_id=1, source_target_pairs={{0,12},{1,5},{2,14},{3,7},{4,8},{5,1},{6,10},{7,3},{8,4},{9,13},{1... | collective-permute-start | bytes 147464 | tf_op jit(solution)/shard_map/ppermute | solution.py:430
  13.3 3.5 %collective-permute-start.4 = (bf16[96,128]{1,0:T(8,128)(2,1)S(1)}, bf16[96,128]{1,0:T(8,128)(2,1)S(1)}, u32[]{:S(2)}, u32[]{:S(2)}) collective-permute-start(bf16[96,128]{1,0:T(8,128)(2,1)S(1)} %get-tuple-element.47), channel_id=1, source_target_pairs={{0,3},{1,2},{2,1},{3,0},{4,7},{5,6},{6,5},{7,4},{8,11},{9,10},{10,... | collective-permute-start | bytes 73736 | tf_op jit(solution)/shard_map/ppermute | solution.py:419
  13.4 3.5 %collective-permute-start.5 = (bf16[96,128]{1,0:T(8,128)(2,1)S(1)}, bf16[96,128]{1,0:T(8,128)(2,1)S(1)}, u32[]{:S(2)}, u32[]{:S(2)}) collective-permute-start(bf16[96,128]{1,0:T(8,128)(2,1)S(1)} %get-tuple-element.48), channel_id=1, source_target_pairs={{0,1},{1,0},{2,3},{3,2},{4,5},{5,4},{6,7},{7,6},{8,9},{9,8},{10,11... | collective-permute-start | bytes 73736 | tf_op jit(solution)/shard_map/ppermute | solution.py:419
  17.7 6.1 %collective-permute-start.10 = (bf16[192,128]{1,0:T(8,128)(2,1)S(1)}, bf16[192,128]{1,0:T(8,128)(2,1)S(1)}, u32[]{:S(2)}, u32[]{:S(2)}) collective-permute-start(bf16[192,128]{1,0:T(8,128)(2,1)S(1)} %get-tuple-element.57), channel_id=1, source_target_pairs={{0,4},{1,13},{2,6},{3,15},{4,0},{5,9},{6,2},{7,11},{8,12},{9,5},{1... | collective-permute-start | bytes 147464 | tf_op jit(solution)/shard_map/ppermute | solution.py:430
  18.3 5.9 %collective-permute-start.11 = (bf16[192,128]{1,0:T(8,128)(2,1)S(1)}, bf16[192,128]{1,0:T(8,128)(2,1)S(1)}, u32[]{:S(2)}, u32[]{:S(2)}) collective-permute-start(bf16[192,128]{1,0:T(8,128)(2,1)S(1)} %get-tuple-element.58), channel_id=1, source_target_pairs={{0,12},{1,5},{2,14},{3,7},{4,8},{5,1},{6,10},{7,3},{8,4},{9,13},{1... | collective-permute-start | bytes 147464 | tf_op jit(solution)/shard_map/ppermute | solution.py:430
  20.1 3.5 %collective-permute-start.8 = (bf16[96,128]{1,0:T(8,128)(2,1)S(1)}, bf16[96,128]{1,0:T(8,128)(2,1)S(1)}, u32[]{:S(2)}, u32[]{:S(2)}) collective-permute-start(bf16[96,128]{1,0:T(8,128)(2,1)S(1)} %get-tuple-element.55), channel_id=1, source_target_pairs={{0,3},{1,2},{2,1},{3,0},{4,7},{5,6},{6,5},{7,4},{8,11},{9,10},{10,... | collective-permute-start | bytes 73736 | tf_op jit(solution)/shard_map/ppermute | solution.py:419
  20.2 3.5 %collective-permute-start.9 = (bf16[96,128]{1,0:T(8,128)(2,1)S(1)}, bf16[96,128]{1,0:T(8,128)(2,1)S(1)}, u32[]{:S(2)}, u32[]{:S(2)}) collective-permute-start(bf16[96,128]{1,0:T(8,128)(2,1)S(1)} %get-tuple-element.56), channel_id=1, source_target_pairs={{0,1},{1,0},{2,3},{3,2},{4,5},{5,4},{6,7},{7,6},{8,9},{9,8},{10,11... | collective-permute-start | bytes 73736 | tf_op jit(solution)/shard_map/ppermute | solution.py:419
  24.6 5.8 %collective-permute-start.14 = (bf16[192,128]{1,0:T(8,128)(2,1)S(1)}, bf16[192,128]{1,0:T(8,128)(2,1)S(1)}, u32[]{:S(2)}, u32[]{:S(2)}) collective-permute-start(bf16[192,128]{1,0:T(8,128)(2,1)S(1)} %get-tuple-element.65), channel_id=1, source_target_pairs={{0,4},{1,13},{2,6},{3,15},{4,0},{5,9},{6,2},{7,11},{8,12},{9,5},{1... | collective-permute-start | bytes 147464 | tf_op jit(solution)/shard_map/ppermute | solution.py:430
  24.7 6.1 %collective-permute-start.15 = (bf16[192,128]{1,0:T(8,128)(2,1)S(1)}, bf16[192,128]{1,0:T(8,128)(2,1)S(1)}, u32[]{:S(2)}, u32[]{:S(2)}) collective-permute-start(bf16[192,128]{1,0:T(8,128)(2,1)S(1)} %get-tuple-element.66), channel_id=1, source_target_pairs={{0,12},{1,5},{2,14},{3,7},{4,8},{5,1},{6,10},{7,3},{8,4},{9,13},{1... | collective-permute-start | bytes 147464 | tf_op jit(solution)/shard_map/ppermute | solution.py:430
  27.0 3.3 %collective-permute-start.12 = (bf16[96,128]{1,0:T(8,128)(2,1)S(1)}, bf16[96,128]{1,0:T(8,128)(2,1)S(1)}, u32[]{:S(2)}, u32[]{:S(2)}) collective-permute-start(bf16[96,128]{1,0:T(8,128)(2,1)S(1)} %get-tuple-element.63), channel_id=1, source_target_pairs={{0,3},{1,2},{2,1},{3,0},{4,7},{5,6},{6,5},{7,4},{8,11},{9,10},{10,... | collective-permute-start | bytes 73736 | tf_op jit(solution)/shard_map/ppermute | solution.py:419
  27.1 3.3 %collective-permute-start.13 = (bf16[96,128]{1,0:T(8,128)(2,1)S(1)}, bf16[96,128]{1,0:T(8,128)(2,1)S(1)}, u32[]{:S(2)}, u32[]{:S(2)}) collective-permute-start(bf16[96,128]{1,0:T(8,128)(2,1)S(1)} %get-tuple-element.64), channel_id=1, source_target_pairs={{0,1},{1,0},{2,3},{3,2},{4,5},{5,4},{6,7},{7,6},{8,9},{9,8},{10,11... | collective-permute-start | bytes 73736 | tf_op jit(solution)/shard_map/ppermute | solution.py:419
